TPU v7x, 32 devices: a whole 2x2x4 slice. The times are simulated.
32 devices in a mesh: grp: 2 (over x), seq: 16 (over z, y, core).
Axes of the slice: x: 2, y: 2, z: 4, core: 2. Of those that a mesh axis runs over, the one named last changes fastest.
Arguments:
- normed_token_features: bfloat16 [4, 1024, 5120], P('grp', 'seq'), parts along dimension 0, may hold values from -6 to 6
- queries: bfloat16 [4, 32, 1024, 128], P('grp', None, 'seq'), parts along dimension 0, may hold values from -8 to 8
- projected_keys: bfloat16 [4, 32, 1024, 128], P('grp', None, 'seq'), parts along dimension 0, may hold values from -8 to 8
- values: bfloat16 [4, 32, 1024, 128], P('grp', None, 'seq'), parts along dimension 0, may hold values from -6 to 6
- adapter_down_factors: bfloat16 [64, 64, 5120], P('seq'), may hold values from -0.078125 to 0.078125
- adapter_up_factors: bfloat16 [64, 64, 4096], P('seq'), may hold values from -1 to 1
- adapter_store_row: int32 [64], replicated, may hold values from 0 to 63, each once
- requests: int32 [4], P('grp'), parts along dimension 0, may hold values from 0 to 63
Outputs:
- attended: bfloat16 [4, 32, 1024, 128], P('grp', None, 'seq'), parts along dimension 0
There are 2 independent parts, one for each index of `grp`. A program takes and returns all parts, laid end to end along the dimension named above; an argument that names none is the same for every part. Nothing has to cross between parts.
Inputs may be any that keep to these rules, and one draw needn't show every extreme that they name: Adapter a's factors are row adapter_store_row[a] of the store, which device adapter_store_row[a] // 4 of seq holds. `requests`: several videos may request the same adapter.
All inputs are finite; a program needn't handle non-finite values.
Results may differ from a plain program's by a relative error of at most 0.0088.
Values may be sent and summed in bfloat16 or wider, within the bound.
No kernel may reach another device: no remote copies, remote signals or barrier semaphores. Data moves between devices by JAX's collectives and lax.ppermute only.
A program may use at most 64 MiB of HBM per device.

v0:
```python
import math

import jax
import jax.numpy as jnp
from jax import lax
from jax.sharding import PartitionSpec as P


def attend_rows(query_rows, keys_all, values_all):
    scores = jnp.dot(query_rows, keys_all.T, preferred_element_type=jnp.float32) / math.sqrt(
        query_rows.shape[-1]
    )
    row_max = jnp.max(scores, axis=1, keepdims=True)
    weights = jnp.exp(scores - row_max)
    weights = (weights / jnp.sum(weights, axis=1, keepdims=True)).astype(jnp.bfloat16)
    return jnp.dot(weights, values_all, preferred_element_type=jnp.float32).astype(jnp.bfloat16)


def attend_items(exchanged):
    query_in, keys_in, values_in = exchanged
    length = query_in.shape[2]
    head_width = query_in.shape[3]
    block_rows = math.gcd(length, 512)

    def one_pair(triple):
        q, k, v = triple
        blocks = q.reshape(length // block_rows, block_rows, head_width)
        outputs = lax.map(lambda query_block: attend_rows(query_block, k, v), blocks)
        return outputs.reshape(length, head_width)

    result = lax.map(one_pair, (query_in[0], keys_in[0], values_in[0]))
    return result[None]


def body(
    normed_token_features,
    queries,
    projected_keys,
    values,
    adapter_down_factors,
    adapter_up_factors,
    adapter_store_row,
    requests,
):
    seq_count, tok_local, model_width = normed_token_features.shape
    head_count = queries.shape[1]
    head_width = queries.shape[3]
    adapter_rank_size = adapter_down_factors.shape[1] // 2
    adapter_slots = adapter_down_factors.shape[0]
    devices_seq = lax.axis_size("seq")
    flat_store = jnp.concatenate(
        [
            adapter_down_factors.reshape(adapter_slots, -1),
            adapter_up_factors.reshape(adapter_slots, -1),
        ],
        axis=1,
    )
    flat_width = flat_store.shape[1]
    token_position = adapter_store_row[requests]
    owner_dev = token_position // adapter_slots
    local_slot = token_position % adapter_slots
    owned_here = owner_dev == lax.axis_index("seq")
    picked = jnp.take(flat_store, local_slot, axis=0)
    contribution = jnp.where(owned_here[:, None], picked, jnp.zeros_like(picked))
    contribution = contribution.reshape(seq_count, devices_seq, flat_width // devices_seq)
    received = lax.all_to_all(contribution, "seq", split_axis=1, concat_axis=1, tiled=True)
    shares = jnp.sum(received.astype(jnp.float32), axis=1).astype(jnp.bfloat16)
    factors = lax.all_gather(shares, "seq", axis=1, tiled=True)
    split_at = 2 * adapter_rank_size * model_width
    selected_down = factors[:, :split_at].reshape(seq_count, 2 * adapter_rank_size, model_width)
    selected_up = factors[:, split_at:].reshape(
        seq_count, 2 * adapter_rank_size, head_count * head_width
    )
    reduced_activation = jnp.einsum(
        "fiz,fpz->fip", normed_token_features, selected_down, preferred_element_type=jnp.float32
    ).astype(jnp.bfloat16)
    delta_q = jnp.einsum(
        "slr,srw->slw",
        reduced_activation[:, :, :adapter_rank_size],
        selected_up[:, :adapter_rank_size],
        preferred_element_type=jnp.float32,
    )
    delta_v = jnp.einsum(
        "slr,srw->slw",
        reduced_activation[:, :, adapter_rank_size:],
        selected_up[:, adapter_rank_size:],
        preferred_element_type=jnp.float32,
    )

    def to_heads(tensor):
        return tensor.reshape(seq_count, tok_local, head_count, head_width).transpose(0, 2, 1, 3)

    query_mix = (queries.astype(jnp.float32) + to_heads(delta_q)).astype(jnp.bfloat16)
    value_mix = (values.astype(jnp.float32) + to_heads(delta_v)).astype(jnp.bfloat16)
    pair_count = seq_count * head_count // devices_seq

    def to_pairs(tensor):
        return tensor.reshape(devices_seq, pair_count, tok_local, head_width)

    attended = attend_items(
        (
            lax.all_to_all(to_pairs(query_mix), "seq", split_axis=0, concat_axis=2, tiled=True),
            lax.all_to_all(
                to_pairs(projected_keys), "seq", split_axis=0, concat_axis=2, tiled=True
            ),
            lax.all_to_all(to_pairs(value_mix), "seq", split_axis=0, concat_axis=2, tiled=True),
        )
    )
    returned = lax.all_to_all(attended, "seq", split_axis=2, concat_axis=0, tiled=True)
    return returned.reshape(seq_count, head_count, tok_local, head_width)


def solution(mesh):
    in_specs = (
        P("grp", "seq", None),
        P("grp", None, "seq", None),
        P("grp", None, "seq", None),
        P("grp", None, "seq", None),
        P("seq", None, None),
        P("seq", None, None),
        P(),
        P("grp"),
    )
    out_specs = P("grp", None, "seq", None)
    return jax.shard_map(body, mesh=mesh, in_specs=in_specs, out_specs=out_specs, check_vma=False)
```

profile of v0, /device:TPU:1, one launch (start us, length us, event | category | flops | bytes accessed | tf_op | source)
XLA Modules:
  0.0 310.7 jit_solution(1577442832287453224)
XLA Ops:
  6.5 0.8 compare_select_fusion.2
  7.3 1.3 gather_fusion
  8.6 3.4 %copy.37 = bf16[1,4,64,4096]{3,1,2,0:T(4,128)(2,1)S(1)} copy(bf16[1,4,64,4096]{3,2,1,0:T(8,128)(2,1)} %bitcast.127) | data formatting | bytes 4194304
  12.0 2.0 copy.36
  14.0 1.3 mini-gather-slice.8
  15.3 5.8 %pad_maximum_fusion = (bf16[4,118016]{1,0:T(4,128)(2,1)S(1)}, bf16[4,118016]{1,0:T(4,128)(2,1)}, bf16[4,118016]{1,0:T(4,128)(2,1)}, bf16[4,118016]{1,0:T(4,128)(2,1)S(1)}) fusion(bf16[4,262144]{1,0:T(4,128)(2,1)S(1)} %bitcast.113, bf16[4,327680]{1,0:T(4,128)(2,1)S(1)} %bitcast.111), kind=kLoop, calls=%fused_computation.39 | loop fusion | flops 1888256 | bytes 11327488 | tf_op jit(solution)/shard_map/concatenate | solution.py:51
  21.1 14.2 %gather_fusion.1 = bf16[2,118016]{1,0:T(2,128)(2,1)} fusion(bf16[4,118016]{1,0:T(4,128)(2,1)} %get-tuple-element.86, s32[1024]{0:T(1024)S(1)} %pad_clamp_fusion), kind=kCustom, calls=%fused_computation.1 | custom fusion | bytes 944136 | tf_op jit(solution)/shard_map/jit(_take)/gather | solution.py:63
  35.3 2.1 constant_dynamic-update-slice_fusion.4
  37.5 14.2 %gather_fusion.2 = bf16[2,118016]{1,0:T(2,128)(2,1)} fusion(bf16[4,118016]{1,0:T(4,128)(2,1)} %get-tuple-element.85, s32[1024]{0:T(1024)S(1)} %pad_clamp_fusion), kind=kCustom, calls=%fused_computation.2 | custom fusion | bytes 944136 | tf_op jit(solution)/shard_map/jit(_take)/gather | solution.py:63
  51.7 1.9 gather_fusion.3
  53.6 1.9 gather_fusion.4
  55.5 1.9 gather_fusion.5
  57.5 1.1 constant_dynamic-update-slice_fusion.3
  58.6 2.1 constant_dynamic-update-slice_fusion.2
  60.7 1.1 constant_dynamic-update-slice_fusion.1
  61.8 1.1 constant_dynamic-update-slice_fusion
  62.9 4.0 %broadcast_select_fusion.1 = bf16[2,16,36864]{2,0,1:T(2,128)(2,1)S(1)} fusion(pred[2]{0:T(512)(128)(4,1)S(1)} %get-tuple-element.89, bf16[2,16,36864]{2,0,1:T(2,128)(2,1)} %bitcast.125, pred[2]{0:T(512)(128)(4,1)S(1)} %get-tuple-element.88), kind=kLoop, calls=%fused_computation.23 | loop fusion | flops 2359296 | bytes 4718596 | tf_op jit(solution)/shard_map/jit(_where)/select_n | solution.py:64
  66.9 61.6 %all_to_all.65 = bf16[2,16,36864]{2,0,1:T(2,128)(2,1)} all-to-all(bf16[2,16,36864]{2,0,1:T(2,128)(2,1)S(1)} %broadcast_select_fusion.1), channel_id=1, replica_groups=mesh['grp'=2,'seq'=16] {'seq'}, dimensions={1} | all-to-all | bytes 4718592 | tf_op jit(solution)/shard_map/all_to_all | solution.py:66
  128.5 4.4 %reduce_sum.21 = bf16[2,36864]{1,0:T(2,128)(2,1)} reduce(bf16[2,16,36864]{2,0,1:T(2,128)(2,1)} %all_to_all.65, bf16[]{:T(256)} %constant.77.clone.1), dimensions={1}, to_apply=%region_0.1 | reduce | flops 1105920 | bytes 2506754 | tf_op jit(solution)/shard_map/reduce_sum | solution.py:67
  132.9 3.7 %all-to-all-start.2 = ((bf16[16,4,64,128]{3,2,1,0:T(8,128)(2,1)}), bf16[16,4,64,128]{3,2,1,0:T(8,128)(2,1)S(1)}, u32[]{:S(2)}, u32[]{:S(2)}) async-start(bf16[16,4,64,128]{3,2,1,0:T(8,128)(2,1)} %bitcast.15), calls=%async_computation.2 | async-start | bytes 2097152 | tf_op jit(solution)/shard_map/all_to_all | solution.py:103
  136.7 47.2 %all-gather.2.cloned.1.call-done = bf16[2,589824]{1,0:T(2,128)(2,1)} async-done(((bf16[2,36864]{1,0:T(2,128)(2,1)}), bf16[2,589824]{1,0:T(2,128)(2,1)}) %all-gather.2.cloned.1.call-update) | async-done | bytes 2359312 | tf_op jit(solution)/shard_map/all_gather | solution.py:68
  183.8 1.2 slice-done
  187.6 1.3 fusion.9
  188.9 4.3 %all-to-all-start.3 = ((bf16[16,4,64,128]{3,2,1,0:T(8,128)(2,1)}), bf16[16,4,64,128]{3,2,1,0:T(8,128)(2,1)}, u32[]{:S(2)}, u32[]{:S(2)}) async-start(bf16[16,4,64,128]{3,2,1,0:T(8,128)(2,1)} %bitcast.124), calls=%async_computation.3 | async-start | bytes 2097152 | tf_op jit(solution)/shard_map/all_to_all | solution.py:106
  193.7 0.7 copy-done.7
  194.5 1.3 fusion.11
  195.7 20.8 %all-to-all-done.3 = bf16[16,4,64,128]{3,2,1,0:T(8,128)(2,1)} async-done(((bf16[16,4,64,128]{3,2,1,0:T(8,128)(2,1)}), bf16[16,4,64,128]{3,2,1,0:T(8,128)(2,1)}, u32[]{:S(2)}, u32[]{:S(2)}) %all-to-all-start.3) | async-done | bytes 1048608 | tf_op jit(solution)/shard_map/all_to_all | solution.py:106
  216.5 6.6 %all-to-all-start.1 = ((bf16[16,4,64,128]{3,2,1,0:T(8,128)(2,1)}), bf16[16,4,64,128]{3,2,1,0:T(8,128)(2,1)}, u32[]{:S(2)}, u32[]{:S(2)}) async-start(bf16[16,4,64,128]{3,2,1,0:T(8,128)(2,1)} %bitcast.11), calls=%async_computation.1 | async-start | bytes 2097152 | tf_op jit(solution)/shard_map/all_to_all | solution.py:102
  223.2 1.1 copy.29
  224.3 2.3 copy.31
  226.6 19.9 %all-to-all-done.1 = bf16[16,4,64,128]{3,2,1,0:T(8,128)(2,1)} async-done(((bf16[16,4,64,128]{3,2,1,0:T(8,128)(2,1)}), bf16[16,4,64,128]{3,2,1,0:T(8,128)(2,1)}, u32[]{:S(2)}, u32[]{:S(2)}) %all-to-all-start.1) | async-done | bytes 1048608 | tf_op jit(solution)/shard_map/all_to_all | solution.py:102
  246.4 1.3 copy.28
  247.7 21.2 %while.21 = (s32[]{:T(128)}, bf16[4,1024,128]{2,1,0:T(8,128)(2,1)}, bf16[4,1024,128]{2,1,0:T(8,128)(2,1)S(1)}, bf16[4,1024,128]{2,1,0:T(8,128)(2,1)}, bf16[4,102...) while((s32[]{:T(128)}, bf16[4,1024,128]{2,1,0:T(8,128)(2,1)}, ...), condition=%wide.region_6.7_spmd, body=%wide.region_1.6_spmd.sunk | while | flops 273218560 | bytes 9186018 | solution.py:31
  247.8 1.1 dynamic-slice_bitcast_fusion.3
  248.9 3.4 %while.22 = (s32[]{:T(128)}, bf16[2,512,128]{2,1,0:T(8,128)(2,1)S(1)}, bf16[2,512,128]{2,1,0:T(8,128)(2,1)S(1)}, bf16[1024,128]{1,0:T(8,128)(2,1)S(1)}, bf16[1024,128]{1,0:T(8,128)(2,1)S(1)}, /*index=5*/s32[]{:T(128)}) while((s32[]{:T(128)}, bf16[2,512,128]{2,1,0:T(8,128)(2,1)S(1)}, bf16[2,512,128]{2,1,0:T(8,128)(2,1)S(1)}, ...), condition=%wide.region_5.5_spmd, body=%wide.region_2.4_spmd.sunk | while | flops 273218560 | bytes 7088205 | solution.py:28
  252.3 0.7 bitcast_dynamic-update-slice_fusion.2
  253.0 1.1 dynamic-slice_bitcast_fusion.3
  254.2 3.4 %while.22 = (s32[]{:T(128)}, bf16[2,512,128]{2,1,0:T(8,128)(2,1)S(1)}, bf16[2,512,128]{2,1,0:T(8,128)(2,1)S(1)}, bf16[1024,128]{1,0:T(8,128)(2,1)S(1)}, bf16[1024,128]{1,0:T(8,128)(2,1)S(1)}, /*index=5*/s32[]{:T(128)}) while((s32[]{:T(128)}, bf16[2,512,128]{2,1,0:T(8,128)(2,1)S(1)}, bf16[2,512,128]{2,1,0:T(8,128)(2,1)S(1)}, ...), condition=%wide.region_5.5_spmd, body=%wide.region_2.4_spmd.sunk | while | flops 273218560 | bytes 7088205 | solution.py:28
  257.6 0.7 bitcast_dynamic-update-slice_fusion.2
  258.3 1.1 dynamic-slice_bitcast_fusion.3
  259.4 3.5 %while.22 = (s32[]{:T(128)}, bf16[2,512,128]{2,1,0:T(8,128)(2,1)S(1)}, bf16[2,512,128]{2,1,0:T(8,128)(2,1)S(1)}, bf16[1024,128]{1,0:T(8,128)(2,1)S(1)}, bf16[1024,128]{1,0:T(8,128)(2,1)S(1)}, /*index=5*/s32[]{:T(128)}) while((s32[]{:T(128)}, bf16[2,512,128]{2,1,0:T(8,128)(2,1)S(1)}, bf16[2,512,128]{2,1,0:T(8,128)(2,1)S(1)}, ...), condition=%wide.region_5.5_spmd, body=%wide.region_2.4_spmd.sunk | while | flops 273218560 | bytes 7088205 | solution.py:28
  262.9 0.7 bitcast_dynamic-update-slice_fusion.2
  263.6 1.1 dynamic-slice_bitcast_fusion.3
  264.7 3.4 %while.22 = (s32[]{:T(128)}, bf16[2,512,128]{2,1,0:T(8,128)(2,1)S(1)}, bf16[2,512,128]{2,1,0:T(8,128)(2,1)S(1)}, bf16[1024,128]{1,0:T(8,128)(2,1)S(1)}, bf16[1024,128]{1,0:T(8,128)(2,1)S(1)}, /*index=5*/s32[]{:T(128)}) while((s32[]{:T(128)}, bf16[2,512,128]{2,1,0:T(8,128)(2,1)S(1)}, bf16[2,512,128]{2,1,0:T(8,128)(2,1)S(1)}, ...), condition=%wide.region_5.5_spmd, body=%wide.region_2.4_spmd.sunk | while | flops 273218560 | bytes 7088205 | solution.py:28
  268.2 0.7 bitcast_dynamic-update-slice_fusion.2
  268.9 2.0 copy.53
  271.0 31.7 %all_to_all.66 = bf16[1,4,1024,128]{3,1,0,2:T(4,128)(2,1)S(1)} all-to-all(bf16[1,4,1024,128]{3,1,0,2:T(4,128)(2,1)S(1)} %bitcast.120), channel_id=1, replica_groups=mesh['grp'=2,'seq'=16] {'seq'}, dimensions={2} | all-to-all | bytes 2097152 | tf_op jit(solution)/shard_map/all_to_all | solution.py:109
  302.6 1.2 copy.33
  (62 shorter events, 16.9 us)
Async XLA Ops:
  6.5 179.1 %copy-start = (bf16[2,64,5120]{2,1,0:T(8,128)(2,1)S(1)}, bf16[2,64,5120]{2,1,0:T(8,128)(2,1)}, u32[]{:S(2)}) copy-start(bf16[2,64,5120]{2,1,0:T(8,128)(2,1)} %param.12) | copy-start | bytes 3932164
  6.5 177.3 %all-gather.2.cloned.1.call-start = ((), (), s32[]{:S(2)}) async-start(), calls=%async_computation.5 | async-start | bytes 2506752 | tf_op jit(solution)/shard_map/all_gather | solution.py:68
  8.6 3.4 %copy-start.2 = (bf16[4,64,5120]{2,1,0:T(8,128)(2,1)S(1)}, bf16[4,64,5120]{2,1,0:T(8,128)(2,1)}, u32[]{:S(2)}) copy-start(bf16[4,64,5120]{2,1,0:T(8,128)(2,1)} %param.16) | copy-start | bytes 7864324
  53.6 1.9 copy-start.1
  55.5 2.0 copy-start.3
  57.4 3.3 %copy-start.4 = (bf16[2,118016]{1,0:T(2,128)(2,1)S(1)}, bf16[2,118016]{1,0:T(2,128)(2,1)}, u32[]{:S(2)}) copy-start(bf16[2,118016]{1,0:T(2,128)(2,1)} %gather_fusion.4) | copy-start | bytes 1416196
  57.4 4.4 %copy-start.5 = (bf16[2,117760]{1,0:T(2,128)(2,1)S(1)}, bf16[2,117760]{1,0:T(2,128)(2,1)}, u32[]{:S(2)}) copy-start(bf16[2,117760]{1,0:T(2,128)(2,1)} %gather_fusion.5) | copy-start | bytes 1413124
  132.9 55.9 %all-to-all-start.2 = ((bf16[16,4,64,128]{3,2,1,0:T(8,128)(2,1)}), bf16[16,4,64,128]{3,2,1,0:T(8,128)(2,1)S(1)}, u32[]{:S(2)}, u32[]{:S(2)}) async-start(bf16[16,4,64,128]{3,2,1,0:T(8,128)(2,1)} %bitcast.15), calls=%async_computation.2 | async-start | bytes 2097152 | tf_op jit(solution)/shard_map/all_to_all | solution.py:103
  183.8 1.2 slice-start
  185.1 1.3 slice-start.1
  186.4 1.2 copy-start.6
  188.9 27.6 %all-to-all-start.3 = ((bf16[16,4,64,128]{3,2,1,0:T(8,128)(2,1)}), bf16[16,4,64,128]{3,2,1,0:T(8,128)(2,1)}, u32[]{:S(2)}, u32[]{:S(2)}) async-start(bf16[16,4,64,128]{3,2,1,0:T(8,128)(2,1)} %bitcast.124), calls=%async_computation.3 | async-start | bytes 2097152 | tf_op jit(solution)/shard_map/all_to_all | solution.py:106
  193.2 1.2 copy-start.7
  216.5 29.9 %all-to-all-start.1 = ((bf16[16,4,64,128]{3,2,1,0:T(8,128)(2,1)}), bf16[16,4,64,128]{3,2,1,0:T(8,128)(2,1)}, u32[]{:S(2)}, u32[]{:S(2)}) async-start(bf16[16,4,64,128]{3,2,1,0:T(8,128)(2,1)} %bitcast.11), calls=%async_computation.1 | async-start | bytes 2097152 | tf_op jit(solution)/shard_map/all_to_all | solution.py:102
Sparse Core Ops, SparseCore 0:
  133.1 50.7 all-gather.1
where the time goes:
time: 314 us; the launch traced here: 311 us
  blocking collectives  93.3 us (30%)
  waiting for transfers between devices  87.9 us (28%)
  local copies, waits for them, and re-layouts  68.5 us (22%)
  other arithmetic  21.8 us (7%)
  starting transfers between devices  14.7 us (5%)
  between operations  13.5 us (4%)
  matrix products  10.8 us (3%)
    all_to_all x1, blocking collectives, body(): lax.all_to_all(contribution, 'seq', split_axis=1, concat_axis=1, tiled=True)  61.6 us
    all_gather x1, waiting for transfers between devices, body(): factors = lax.all_gather(shares, 'seq', axis=1, tiled=True)  47.2 us
    gather x6, local copies, waits for them, and re-layouts, body(): picked = jnp.take(flat_store, local_slot, axis=0)  35.5 us
    all_to_all x1, blocking collectives, body(): lax.all_to_all(attended, 'seq', split_axis=2, concat_axis=0, tiled=True)  31.7 us
    all_to_all x1, waiting for transfers between devices, body(): lax.all_to_all(to_pairs(value_mix), 'seq', split_axis=0, concat_axis=2, t...  20.8 us
    all_to_all x1, waiting for transfers between devices, body(): lax.all_to_all(to_pairs(query_mix), 'seq', split_axis=0, concat_axis=2, t...  19.9 us
    unnamed x24, local copies, waits for them, and re-layouts  14.5 us
    all_to_all x1, starting transfers between devices, body(): lax.all_to_all(to_pairs(query_mix), 'seq', split_axis=0, concat_axis=2, t...  6.65 us
  transfers between devices with their start and end apart: 4, of which 3 were waited for; matrix products, arithmetic and copies ran while one was open for 3% of the time, Pallas kernels for 0%

commit v1 on v0

v1 whole, which is shorter than its diff:
```python
import functools
import math

import jax
import jax.numpy as jnp
from jax import lax
from jax.experimental import pallas as pl
from jax.experimental.pallas import tpu as pltpu
from jax.sharding import PartitionSpec as P

LANES = 128
CHUNKS = 2


def bit_count(n):
    bits = n.bit_length() - 1
    assert 1 << bits == n
    return bits


def reversed_bits(j, bits):
    out = 0
    for i in range(bits):
        out = out | (((j >> i) & 1) << (bits - 1 - i))
    return out


def pick_kernel(tiles, rows, heads, info, down_ref, up_ref, out_ref, *, dest, per_video, videos):
    video = dest(pl.program_id(0), info) // per_video
    owned = info[1 + videos + video] == 1

    @pl.when(owned)
    def _():
        for t in range(tiles):
            out_ref[0, t * rows : (t + 1) * rows, :] = down_ref[0, :, t * LANES : (t + 1) * LANES]
        base = tiles * rows
        ranks = up_ref.shape[1]
        for h in range(heads):
            out_ref[0, base + h * ranks : base + (h + 1) * ranks, :] = up_ref[
                0, :, h * LANES : (h + 1) * LANES
            ]

    @pl.when(jnp.logical_not(owned))
    def _():
        out_ref[...] = jnp.zeros_like(out_ref)


def low_rank_kernel(tiles, rows, col_split, per_video, bits, me_ref, x_ref, g_ref, out_ref, down):
    videos = x_ref.shape[0]
    for j in range(g_ref.shape[0]):
        dev = me_ref[0] ^ reversed_bits(j, bits)
        video = dev // per_video
        place = dev % per_video
        row = pl.multiple_of((place // col_split) * rows, rows)
        for t in range(tiles):
            col = pl.multiple_of(((place % col_split) * tiles + t) * LANES, LANES)
            down[video, pl.ds(row, rows), pl.ds(col, LANES)] = g_ref[j, t * rows : (t + 1) * rows, :]
    parts = [
        lax.dot_general(
            x_ref[s], down[s], (((1,), (1,)), ((), ())), preferred_element_type=jnp.float32
        )
        for s in range(videos)
    ]
    out_ref[...] = jnp.concatenate(parts, axis=1).astype(out_ref.dtype)


def attend_kernel(per_video, block_rows, me_ref, q_ref, k_ref, v_ref, low_ref, up_ref, out_ref, q_mix):
    devs, _, toks, width = q_ref.shape
    length = devs * toks
    ranks = up_ref.shape[0]
    videos = low_ref.shape[2] // ranks
    video = me_ref[0] // per_video
    up = jnp.concatenate([up_ref[...]] * videos, axis=0)
    row = lax.broadcasted_iota(jnp.int32, up.shape, 0)
    here = (row // ranks) == video
    for_q = (row % ranks) < (ranks // 2)
    zero = jnp.zeros_like(up)
    up_q = jnp.where(here & for_q, up, zero)
    up_v = jnp.where(here & jnp.logical_not(for_q), up, zero)
    low = low_ref[...].reshape(length, low_ref.shape[2])
    keys = k_ref[...].reshape(length, width)
    delta_v = jnp.dot(low, up_v, preferred_element_type=jnp.float32)
    vals = (v_ref[...].reshape(length, width).astype(jnp.float32) + delta_v).astype(jnp.bfloat16)
    delta_q = jnp.dot(low, up_q, preferred_element_type=jnp.float32)
    q_mix[...] = (q_ref[...].reshape(length, width).astype(jnp.float32) + delta_q).astype(
        jnp.bfloat16
    )
    scale = math.log2(math.e) / math.sqrt(width)
    devs_block = block_rows // toks
    for b in range(length // block_rows):
        q = q_mix[b * block_rows : (b + 1) * block_rows, :]
        scores = lax.dot_general(
            q, keys, (((1,), (1,)), ((), ())), preferred_element_type=jnp.float32
        )
        top = jnp.max(scores, axis=1, keepdims=True)
        weights = jnp.exp2((scores - top) * scale)
        total = jnp.sum(weights, axis=1, keepdims=True)
        mixed = jnp.dot(weights.astype(jnp.bfloat16), vals, preferred_element_type=jnp.float32)
        out = (mixed / total).astype(out_ref.dtype)
        out_ref[b * devs_block : (b + 1) * devs_block] = out.reshape(devs_block, 1, toks, width)


def body(
    normed_token_features,
    queries,
    projected_keys,
    values,
    adapter_down_factors,
    adapter_up_factors,
    adapter_store_row,
    requests,
):
    videos, toks, model_width = normed_token_features.shape
    heads = queries.shape[1]
    width = queries.shape[3]
    slots, ranks, _ = adapter_down_factors.shape
    devs = lax.axis_size("seq")
    bits = bit_count(devs)
    me = lax.axis_index("seq").astype(jnp.int32)
    pairs = videos * heads // devs
    per_video = devs // videos
    length = devs * toks
    chunks = math.gcd(pairs, CHUNKS)
    in_chunk = pairs // chunks

    def by_pairs(tensor):
        return tensor.reshape(devs, pairs, toks, width)

    sources = [by_pairs(t) for t in (queries, projected_keys, values)]
    arrived = []
    for c in range(chunks):
        packed = jnp.concatenate(
            [t[:, c * in_chunk : (c + 1) * in_chunk] for t in sources], axis=1
        )
        arrived.append(lax.all_to_all(packed, "seq", split_axis=0, concat_axis=0, tiled=True))

    col_split = math.gcd(per_video, model_width // LANES)
    row_split = per_video // col_split
    rows = ranks // row_split
    tiles = model_width // col_split // LANES
    down_rows = tiles * rows
    all_rows = down_rows + pairs * ranks

    store_row = adapter_store_row[requests]
    owned = (store_row // slots == me).astype(jnp.int32)
    info = jnp.concatenate([me[None], store_row % slots, owned]).astype(jnp.int32)

    def dest(j, info_ref):
        return info_ref[0] ^ reversed_bits(j, bits)

    def down_block(j, info_ref):
        dev = dest(j, info_ref)
        video = dev // per_video
        place = dev % per_video
        mine = info_ref[1 + videos + video]
        return (
            info_ref[1 + video] * mine,
            (place // col_split) * mine,
            (place % col_split) * mine,
        )

    def up_block(j, info_ref):
        dev = dest(j, info_ref)
        video = dev // per_video
        mine = info_ref[1 + videos + video]
        return (info_ref[1 + video] * mine, 0, (dev % per_video) * mine)

    picked = pl.pallas_call(
        functools.partial(
            pick_kernel, tiles, rows, pairs, dest=dest, per_video=per_video, videos=videos
        ),
        grid_spec=pltpu.PrefetchScalarGridSpec(
            num_scalar_prefetch=1,
            grid=(devs,),
            in_specs=[
                pl.BlockSpec((1, rows, tiles * LANES), down_block),
                pl.BlockSpec((1, ranks, pairs * LANES), up_block),
            ],
            out_specs=pl.BlockSpec((1, all_rows, LANES), lambda j, info_ref: (j, 0, 0)),
        ),
        out_shape=jax.ShapeDtypeStruct((devs, all_rows, LANES), jnp.bfloat16),
        cost_estimate=pl.CostEstimate(
            flops=0, bytes_accessed=devs * all_rows * LANES * 4, transcendentals=0
        ),
        name="pick_factors",
    )(info, adapter_down_factors, adapter_up_factors)

    def swap(tensor, bit):
        return lax.ppermute(tensor, "seq", [(i, i ^ (1 << bit)) for i in range(devs)])

    held = picked
    for bit in range(bits):
        half = held.shape[0] // 2
        held = held[:half] + swap(held[half:], bit)
    up_here = held[0, down_rows:].reshape(pairs, ranks, LANES)
    gathered = held[:, :down_rows]
    for bit in reversed(range(bits)):
        gathered = jnp.concatenate([gathered, swap(gathered, bit)], axis=0)

    low = pl.pallas_call(
        functools.partial(low_rank_kernel, tiles, rows, col_split, per_video, bits),
        grid_spec=pltpu.PrefetchScalarGridSpec(
            num_scalar_prefetch=1,
            grid=(1,),
            in_specs=[
                pl.BlockSpec((videos, toks, model_width), lambda i, m: (0, 0, 0)),
                pl.BlockSpec((devs, down_rows, LANES), lambda i, m: (0, 0, 0)),
            ],
            out_specs=pl.BlockSpec((toks, videos * ranks), lambda i, m: (0, 0)),
            scratch_shapes=[pltpu.VMEM((videos, ranks, model_width), jnp.bfloat16)],
        ),
        out_shape=jax.ShapeDtypeStruct((toks, videos * ranks), jnp.bfloat16),
        compiler_params=pltpu.CompilerParams(vmem_limit_bytes=24 << 20),
        cost_estimate=pl.CostEstimate(
            flops=2 * videos * toks * ranks * model_width,
            bytes_accessed=2 * videos * (toks + ranks) * model_width,
            transcendentals=0,
        ),
        name="low_rank",
    )(me[None], normed_token_features, gathered)
    low_all = lax.all_gather(low, "seq", axis=0)

    block_rows = math.gcd(length, 512)

    def attend(packed, up):
        count = packed.shape[1] // 3

        def part(which):
            return pl.BlockSpec(
                (devs, 1, toks, width), lambda p, m, w=which: (0, w * count + p, 0, 0)
            )

        return pl.pallas_call(
            functools.partial(attend_kernel, per_video, block_rows),
            grid_spec=pltpu.PrefetchScalarGridSpec(
                num_scalar_prefetch=1,
                grid=(count,),
                in_specs=[
                    part(0),
                    part(1),
                    part(2),
                    pl.BlockSpec((devs, toks, videos * ranks), lambda p, m: (0, 0, 0)),
                    pl.BlockSpec((pl.squeezed, ranks, LANES), lambda p, m: (p, 0, 0)),
                ],
                out_specs=pl.BlockSpec((devs, 1, toks, width), lambda p, m: (0, p, 0, 0)),
                scratch_shapes=[pltpu.VMEM((length, width), jnp.bfloat16)],
            ),
            out_shape=jax.ShapeDtypeStruct((devs, count, toks, width), jnp.bfloat16),
            compiler_params=pltpu.CompilerParams(vmem_limit_bytes=40 << 20),
            cost_estimate=pl.CostEstimate(
                flops=4 * count * length * length * width,
                bytes_accessed=8 * count * length * width,
                transcendentals=count * length * length,
            ),
            name="attend",
        )(me[None], packed, packed, packed, low_all, up)

    returned = []
    for c in range(chunks):
        mixed = attend(arrived[c], up_here[c * in_chunk : (c + 1) * in_chunk])
        returned.append(lax.all_to_all(mixed, "seq", split_axis=0, concat_axis=0, tiled=True))
    out = jnp.concatenate(returned, axis=1) if chunks > 1 else returned[0]
    return out.reshape(videos, heads, toks, width)


def solution(mesh):
    in_specs = (
        P("grp", "seq", None),
        P("grp", None, "seq", None),
        P("grp", None, "seq", None),
        P("grp", None, "seq", None),
        P("seq", None, None),
        P("seq", None, None),
        P(),
        P("grp"),
    )
    out_specs = P("grp", None, "seq", None)
    return jax.shard_map(body, mesh=mesh, in_specs=in_specs, out_specs=out_specs, check_vma=False)
```

time: 314 us -> 191 us (0.61)
  local copies, waits for them, and re-layouts: 68.5 us -> 6.81 us
  blocking collectives: 93.3 us -> 40.4 us
  Pallas kernels: 0 us -> 17.1 us
  other arithmetic: 21.8 us -> 5.7 us
  starting transfers between devices: 14.7 us -> 28.9 us
  between operations: 13.5 us -> 0.21 us
  matrix products: 10.8 us -> 0 us
    ppermute x0 -> x8, waiting for transfers between devices: none -> 80.5 us  [swap(): return lax.ppermute(tensor, 'seq', [(i, i ^ 1 << bit) for i in range(devs)])]
    all_to_all x2 -> x1, blocking collectives: 93.3 us -> 18.3 us  [body(): lax.all_to_all(mixed, 'seq', split_axis=0, concat_axis=0, tiled=True)]
    all_gather x1 -> x0, waiting for transfers between devices: 47.2 us -> none  [body(): factors = lax.all_gather(shares, 'seq', axis=1, tiled=True)]
    gather x7 -> x1, local copies, waits for them, and re-layouts: 36.8 us -> 0.64 us  [body(): store_row = adapter_store_row[requests]]
    all_to_all x3, waiting for transfers between devices: 40.6 us -> 9.6 us  [the longest x1 9.6 us: body(): lax.all_to_all(mixed, 'seq', split_axis=0, concat_axis=0, tiled=True)]
    all_gather x0 -> x1, blocking collectives: none -> 22.1 us  [body(): low_all = lax.all_gather(low, 'seq', axis=0)]
    pallas_call x0 -> x4, Pallas kernels: none -> 17.1 us  [the longest x2 9.08 us: attend(): pl.pallas_call(functools.partial(attend_kernel, per_video, block_rows), g...]
    unnamed x24 -> x19, local copies, waits for them, and re-layouts: 14.5 us -> 2.11 us
  transfers between devices with their start and end apart: 4 -> 11, of which waited for: 3 -> 8; matrix products, arithmetic and copies ran while one was open for 3% -> 3% of each run, Pallas kernels for 0% -> 9%
where the time goes in v1:
time: 191 us; the launch traced here: 189 us
  waiting for transfers between devices  90.1 us (47%)
  blocking collectives  40.4 us (21%)
  starting transfers between devices  28.9 us (15%)
  Pallas kernels  17.1 us (9%)
  local copies, waits for them, and re-layouts  6.81 us (4%)
  other arithmetic  5.7 us (3%)
    ppermute x8, waiting for transfers between devices, swap(): return lax.ppermute(tensor, 'seq', [(i, i ^ 1 << bit) for i in range(devs)])  80.5 us
    all_gather x1, blocking collectives, body(): low_all = lax.all_gather(low, 'seq', axis=0)  22.1 us
    all_to_all x1, blocking collectives, body(): lax.all_to_all(mixed, 'seq', split_axis=0, concat_axis=0, tiled=True)  18.3 us
    all_to_all x2, starting transfers between devices, body(): lax.all_to_all(packed, 'seq', split_axis=0, concat_axis=0, tiled=True)  14 us
    ppermute x8, starting transfers between devices, swap(): return lax.ppermute(tensor, 'seq', [(i, i ^ 1 << bit) for i in range(devs)])  11.4 us
    all_to_all x1, waiting for transfers between devices, body(): lax.all_to_all(mixed, 'seq', split_axis=0, concat_axis=0, tiled=True)  9.6 us
    pallas_call x2, Pallas kernels, attend(): pl.pallas_call(functools.partial(attend_kernel, per_video, block_rows), g...  9.08 us
    pallas_call x1, Pallas kernels, body(): pl.pallas_call(functools.partial(pick_kernel, tiles, rows, pairs, dest=de...  7.15 us
  transfers between devices with their start and end apart: 11, of which 8 were waited for; matrix products, arithmetic and copies ran while one was open for 3% of the time, Pallas kernels for 9%

profile of v1, /device:TPU:1, one launch (start us, length us, event | category | flops | bytes accessed | tf_op | source)
XLA Modules:
  0.0 189.2 jit_solution(7263464860765346016)
XLA Ops:
  0.0 1.4 fusion.2
  1.5 0.1 copy-done.5
  1.6 0.3 copy-done.6
  1.9 0.2 fusion
  2.1 1.3 pad_maximum_fusion
  3.4 7.5 %all-to-all-start = ((bf16[16,6,64,128]{3,2,1,0:T(8,128)(2,1)}), bf16[16,6,64,128]{3,2,1,0:T(8,128)(2,1)S(1)}, u32[]{:S(2)}, u32[]{:S(2)}) async-start(bf16[16,6,64,128]{3,2,1,0:T(8,128)(2,1)} %pad_maximum_fusion), calls=%async_computation | async-start | bytes 3145728 | tf_op jit(solution)/shard_map/all_to_all | solution.py:135
  10.9 0.6 gather_fusion
  11.6 0.6 pad_add_fusion.info
  12.2 7.1 %pick_factors.1 = bf16[16,576,128]{2,1,0:T(8,128)(2,1)} custom-call(s32[5]{0:T(128)} %pad_add_fusion.info, bf16[4,64,5120]{2,1,0:T(8,128)(2,1)} %down_ref.1, bf16[4,64,4096]{2,1,0:T(8,128)(2,1)} %up_ref.1), custom_call_target="tpu_custom_call" | custom-call | bytes 4718592 | tf_op jit(solution)/shard_map/pick_factors/pallas_call | solution.py:168
  19.3 1.5 slice.85
  20.9 0.2 collective-permute-start
  21.0 2.7 %collective-permute-done = bf16[8,576,128]{2,1,0:T(8,128)(2,1)S(1)} collective-permute-done((bf16[8,576,128]{2,1,0:T(8,128)(2,1)S(1)}, bf16[8,576,128]{2,1,0:T(8,128)(2,1)S(1)}, u32[]{:S(2)}, u32[]{:S(2)}) %collective-permute-start) | collective-permute-done | bytes 1179680 | tf_op jit(solution)/shard_map/ppermute | solution.py:189
  23.8 0.1 slice_add_fusion
  23.9 1.5 collective-permute-start.1
  25.4 20.8 %collective-permute-done.1 = bf16[4,576,128]{2,1,0:T(8,128)(2,1)S(1)} collective-permute-done((bf16[4,576,128]{2,1,0:T(8,128)(2,1)S(1)}, bf16[4,576,128]{2,1,0:T(8,128)(2,1)S(1)}, u32[]{:S(2)}, u32[]{:S(2)}) %collective-permute-start.1) | collective-permute-done | bytes 589856 | tf_op jit(solution)/shard_map/ppermute | solution.py:189
  46.2 0.1 slice_add_fusion.1
  46.3 0.0 copy-start.4
  46.3 0.8 copy-done.4
  47.1 0.7 slice.89
  47.8 2.3 %collective-permute-start.2 = (bf16[2,576,128]{2,1,0:T(8,128)(2,1)}, bf16[2,576,128]{2,1,0:T(8,128)(2,1)S(1)}, u32[]{:S(2)}, u32[]{:S(2)}) collective-permute-start(bf16[2,576,128]{2,1,0:T(8,128)(2,1)} %slice.89), channel_id=1, source_target_pairs={{0,4},{1,5},{2,6},{3,7},{4,0},{5,1},{6,2},{7,3},{8,12},{9,13},{10,... | collective-permute-start | bytes 884744 | tf_op jit(solution)/shard_map/ppermute | solution.py:189
  50.1 1.3 pad_maximum_fusion.1
  51.5 6.5 %all-to-all-start.2 = ((bf16[16,6,64,128]{3,2,1,0:T(8,128)(2,1)}), bf16[16,6,64,128]{3,2,1,0:T(8,128)(2,1)S(1)}, u32[]{:S(2)}, u32[]{:S(2)}) async-start(bf16[16,6,64,128]{3,2,1,0:T(8,128)(2,1)} %pad_maximum_fusion.1), calls=%async_computation.2 | async-start | bytes 3145728 | tf_op jit(solution)/shard_map/all_to_all | solution.py:135
  57.9 0.0 collective-permute-done.2
  57.9 1.0 slice_add_fusion.2
  59.0 3.4 %collective-permute-start.3 = (bf16[1,576,128]{2,1,0:T(8,128)(2,1)S(1)}, bf16[1,576,128]{2,1,0:T(8,128)(2,1)S(1)}, u32[]{:S(2)}, u32[]{:S(2)}) collective-permute-start(bf16[1,576,128]{2,1,0:T(8,128)(2,1)S(1)} %slice.91), channel_id=1, source_target_pairs={{0,8},{1,9},{2,10},{3,11},{4,12},{5,13},{6,14},{7,15},{8,0},{9,1},... | collective-permute-start | bytes 442376 | tf_op jit(solution)/shard_map/ppermute | solution.py:189
  62.4 38.9 %collective-permute-done.3 = bf16[1,576,128]{2,1,0:T(8,128)(2,1)S(1)} collective-permute-done((bf16[1,576,128]{2,1,0:T(8,128)(2,1)S(1)}, bf16[1,576,128]{2,1,0:T(8,128)(2,1)S(1)}, u32[]{:S(2)}, u32[]{:S(2)}) %collective-permute-start.3) | collective-permute-done | bytes 147488 | tf_op jit(solution)/shard_map/ppermute | solution.py:189
  101.4 0.1 collective-permute-start.4
  101.4 5.5 %collective-permute-done.4 = bf16[1,320,128]{2,1,0:T(8,128)(2,1)S(1)} collective-permute-done((bf16[1,320,128]{2,1,0:T(8,128)(2,1)S(1)}, bf16[1,320,128]{2,1,0:T(8,128)(2,1)S(1)}, u32[]{:S(2)}, u32[]{:S(2)}) %collective-permute-start.4) | collective-permute-done | bytes 81952 | tf_op jit(solution)/shard_map/ppermute | solution.py:189
  106.9 0.1 collective-permute-start.5
  107.0 4.7 %collective-permute-done.5 = bf16[2,320,128]{2,1,0:T(8,128)(2,1)S(1)} collective-permute-done((bf16[2,320,128]{2,1,0:T(8,128)(2,1)S(1)}, bf16[2,320,128]{2,1,0:T(8,128)(2,1)S(1)}, u32[]{:S(2)}, u32[]{:S(2)}) %collective-permute-start.5) | collective-permute-done | bytes 163872 | tf_op jit(solution)/shard_map/ppermute | solution.py:189
  111.7 1.0 collective-permute-start.6
  112.7 6.3 %collective-permute-done.6 = bf16[4,320,128]{2,1,0:T(8,128)(2,1)S(1)} collective-permute-done((bf16[4,320,128]{2,1,0:T(8,128)(2,1)S(1)}, bf16[4,320,128]{2,1,0:T(8,128)(2,1)S(1)}, u32[]{:S(2)}, u32[]{:S(2)}) %collective-permute-start.6) | collective-permute-done | bytes 327712 | tf_op jit(solution)/shard_map/ppermute | solution.py:189
  119.0 0.1 pad_maximum_fusion.3
  119.1 0.0 copy-start.2
  119.1 2.9 %collective-permute-start.7 = (bf16[8,320,128]{2,1,0:T(8,128)(2,1)S(1)}, bf16[8,320,128]{2,1,0:T(8,128)(2,1)S(1)}, u32[]{:S(2)}, u32[]{:S(2)}) collective-permute-start(bf16[8,320,128]{2,1,0:T(8,128)(2,1)S(1)} %pad_maximum_fusion.3), channel_id=1, source_target_pairs={{0,1},{1,0},{2,3},{3,2},{4,5},{5,4},{6,7},{7,6},{8,9},{9,8},{10,11... | collective-permute-start | bytes 1966088 | tf_op jit(solution)/shard_map/ppermute | solution.py:189
  122.1 1.6 collective-permute-done.7
  123.8 0.1 constant_dynamic-update-slice_fusion.g_ref
  123.9 0.9 low_rank.1
  124.7 22.1 %all-gather = bf16[1024,128]{1,0:T(8,128)(2,1)S(1)} all-gather(bf16[64,128]{1,0:T(8,128)(2,1)S(1)} %low_rank.1), channel_id=2, replica_groups=mesh['grp'=2,'seq'=16] {'seq'}, dimensions={0}, use_global_device_ids=true | all-gather | bytes 278528 | tf_op jit(solution)/shard_map/all_gather | solution.py:221
  146.9 4.5 %attend.2 = bf16[16,2,64,128]{3,2,1,0:T(8,128)(2,1)S(1)} custom-call(s32[1]{0:T(128)} %bitcast.me_ref, bf16[16,6,64,128]{3,2,1,0:T(8,128)(2,1)S(1)} %all-to-all-done.q_ref.k_ref.v_ref, bf16[16,6,64,128]{3,2,1,0:T(8,128)(2,1)S(1)} %all-to-all-done.q_ref.k_ref.v_ref, bf16[16,6,64,128]{3,2,1,0:T(8,128)(2,1)S(1)} %all-to-all-done.q_ref.k_ref.v_ref, ...), custom_call_target="tpu_custom_call" | custom-call | flops 1073741824 | bytes 2097152 | tf_op jit(solution)/shard_map/attend/pallas_call | solution.py:233
  151.4 0.0 copy-start.1
  151.4 0.8 copy-done.1
  152.2 0.0 all-to-all-done.2.q_ref.k_ref.v_ref
  152.2 3.5 %all-to-all-start.1 = ((bf16[16,2,64,128]{3,2,1,0:T(8,128)(2,1)}), bf16[16,2,64,128]{3,2,1,0:T(8,128)(2,1)S(1)}, u32[]{:S(2)}, u32[]{:S(2)}) async-start(bf16[16,2,64,128]{3,2,1,0:T(8,128)(2,1)} %copy-done.1), calls=%async_computation.1 | async-start | bytes 1048576 | tf_op jit(solution)/shard_map/all_to_all | solution.py:261
  155.7 4.5 %attend.3 = bf16[16,2,64,128]{3,2,1,0:T(8,128)(2,1)S(1)} custom-call(s32[1]{0:T(128)} %bitcast.me_ref, bf16[16,6,64,128]{3,2,1,0:T(8,128)(2,1)S(1)} %all-to-all-done.2.q_ref.k_ref.v_ref, bf16[16,6,64,128]{3,2,1,0:T(8,128)(2,1)S(1)} %all-to-all-done.2.q_ref.k_ref.v_ref, bf16[16,6,64,128]{3,2,1,0:T(8,128)(2,1)S(1)} %all-to-all-done.2.q_ref.k_ref.v_ref, ...), custom_call_target="tpu_custom_call" | custom-call | flops 1073741824 | bytes 2097152 | tf_op jit(solution)/shard_map/attend/pallas_call | solution.py:233
  160.3 9.6 %all-to-all-done.1 = bf16[16,2,64,128]{3,2,1,0:T(8,128)(2,1)S(1)} async-done(((bf16[16,2,64,128]{3,2,1,0:T(8,128)(2,1)}), bf16[16,2,64,128]{3,2,1,0:T(8,128)(2,1)S(1)}, u32[]{:S(2)}, u32[]{:S(2)}) %all-to-all-start.1) | async-done | bytes 524320 | tf_op jit(solution)/shard_map/all_to_all | solution.py:261
  169.9 18.3 %all_to_all.20 = bf16[16,2,64,128]{3,2,1,0:T(8,128)(2,1)S(1)} all-to-all(bf16[16,2,64,128]{3,2,1,0:T(8,128)(2,1)S(1)} %attend.3), channel_id=1, replica_groups=mesh['grp'=2,'seq'=16] {'seq'}, dimensions={0} | all-to-all | bytes 1048576 | tf_op jit(solution)/shard_map/all_to_all | solution.py:261
  188.2 1.1 pad_maximum_fusion.2
  (24 shorter events, 0.3 us)
Async XLA Ops:
  0.0 10.9 %copy-start = (s32[64]{0:T(128)S(1)}, s32[64]{0:T(128)}, u32[]{:S(2)}) copy-start(s32[64]{0:T(128)} %param.14) | copy-start | bytes 772
  0.0 1.6 copy-start.5
  0.0 1.9 copy-start.6
  3.4 7.5 %copy-start.7 = (s32[2]{0:T(128)S(1)}, s32[2]{0:T(128)}, u32[]{:S(2)}) copy-start(s32[2]{0:T(128)} %param.15) | copy-start | bytes 28
  3.4 48.1 %all-to-all-start = ((bf16[16,6,64,128]{3,2,1,0:T(8,128)(2,1)}), bf16[16,6,64,128]{3,2,1,0:T(8,128)(2,1)S(1)}, u32[]{:S(2)}, u32[]{:S(2)}) async-start(bf16[16,6,64,128]{3,2,1,0:T(8,128)(2,1)} %pad_maximum_fusion), calls=%async_computation | async-start | bytes 3145728 | tf_op jit(solution)/shard_map/all_to_all | solution.py:135
  19.3 4.4 %copy-start.3 = (bf16[16,576,128]{2,1,0:T(8,128)(2,1)S(1)}, bf16[16,576,128]{2,1,0:T(8,128)(2,1)}, u32[]{:S(2)}) copy-start(bf16[16,576,128]{2,1,0:T(8,128)(2,1)} %pick_factors.1) | copy-start | bytes 7077892
  20.9 2.9 %collective-permute-start = (bf16[8,576,128]{2,1,0:T(8,128)(2,1)S(1)}, bf16[8,576,128]{2,1,0:T(8,128)(2,1)S(1)}, u32[]{:S(2)}, u32[]{:S(2)}) collective-permute-start(bf16[8,576,128]{2,1,0:T(8,128)(2,1)S(1)} %slice.85), channel_id=1, source_target_pairs={{0,1},{1,0},{2,3},{3,2},{4,5},{5,4},{6,7},{7,6},{8,9},{9,8},{10,11... | collective-permute-start | bytes 3538952 | tf_op jit(solution)/shard_map/ppermute | solution.py:189
  23.9 22.3 %collective-permute-start.1 = (bf16[4,576,128]{2,1,0:T(8,128)(2,1)S(1)}, bf16[4,576,128]{2,1,0:T(8,128)(2,1)S(1)}, u32[]{:S(2)}, u32[]{:S(2)}) collective-permute-start(bf16[4,576,128]{2,1,0:T(8,128)(2,1)S(1)} %slice.87), channel_id=1, source_target_pairs={{0,2},{1,3},{2,0},{3,1},{4,6},{5,7},{6,4},{7,5},{8,10},{9,11},{10,... | collective-permute-start | bytes 1769480 | tf_op jit(solution)/shard_map/ppermute | solution.py:189
  46.3 0.8 copy-start.4
  47.8 10.1 %collective-permute-start.2 = (bf16[2,576,128]{2,1,0:T(8,128)(2,1)}, bf16[2,576,128]{2,1,0:T(8,128)(2,1)S(1)}, u32[]{:S(2)}, u32[]{:S(2)}) collective-permute-start(bf16[2,576,128]{2,1,0:T(8,128)(2,1)} %slice.89), channel_id=1, source_target_pairs={{0,4},{1,5},{2,6},{3,7},{4,0},{5,1},{6,2},{7,3},{8,12},{9,13},{10,... | collective-permute-start | bytes 884744 | tf_op jit(solution)/shard_map/ppermute | solution.py:189
  51.5 100.7 %all-to-all-start.2 = ((bf16[16,6,64,128]{3,2,1,0:T(8,128)(2,1)}), bf16[16,6,64,128]{3,2,1,0:T(8,128)(2,1)S(1)}, u32[]{:S(2)}, u32[]{:S(2)}) async-start(bf16[16,6,64,128]{3,2,1,0:T(8,128)(2,1)} %pad_maximum_fusion.1), calls=%async_computation.2 | async-start | bytes 3145728 | tf_op jit(solution)/shard_map/all_to_all | solution.py:135
  59.0 42.3 %collective-permute-start.3 = (bf16[1,576,128]{2,1,0:T(8,128)(2,1)S(1)}, bf16[1,576,128]{2,1,0:T(8,128)(2,1)S(1)}, u32[]{:S(2)}, u32[]{:S(2)}) collective-permute-start(bf16[1,576,128]{2,1,0:T(8,128)(2,1)S(1)} %slice.91), channel_id=1, source_target_pairs={{0,8},{1,9},{2,10},{3,11},{4,12},{5,13},{6,14},{7,15},{8,0},{9,1},... | collective-permute-start | bytes 442376 | tf_op jit(solution)/shard_map/ppermute | solution.py:189
  101.4 5.5 %collective-permute-start.4 = (bf16[1,320,128]{2,1,0:T(8,128)(2,1)S(1)}, bf16[1,320,128]{2,1,0:T(8,128)(2,1)S(1)}, u32[]{:S(2)}, u32[]{:S(2)}) collective-permute-start(bf16[1,320,128]{2,1,0:T(8,128)(2,1)S(1)} %get-tuple-element.13), channel_id=1, source_target_pairs={{0,8},{1,9},{2,10},{3,11},{4,12},{5,13},{6,14},{7,15},{8,0},{9,1},... | collective-permute-start | bytes 245768 | tf_op jit(solution)/shard_map/ppermute | solution.py:189
  106.9 4.7 %collective-permute-start.5 = (bf16[2,320,128]{2,1,0:T(8,128)(2,1)S(1)}, bf16[2,320,128]{2,1,0:T(8,128)(2,1)S(1)}, u32[]{:S(2)}, u32[]{:S(2)}) collective-permute-start(bf16[2,320,128]{2,1,0:T(8,128)(2,1)S(1)} %pad_maximum_fusion.5), channel_id=1, source_target_pairs={{0,4},{1,5},{2,6},{3,7},{4,0},{5,1},{6,2},{7,3},{8,12},{9,13},{10,... | collective-permute-start | bytes 491528 | tf_op jit(solution)/shard_map/ppermute | solution.py:189
  111.7 7.3 %collective-permute-start.6 = (bf16[4,320,128]{2,1,0:T(8,128)(2,1)S(1)}, bf16[4,320,128]{2,1,0:T(8,128)(2,1)S(1)}, u32[]{:S(2)}, u32[]{:S(2)}) collective-permute-start(bf16[4,320,128]{2,1,0:T(8,128)(2,1)S(1)} %pad_maximum_fusion.4), channel_id=1, source_target_pairs={{0,2},{1,3},{2,0},{3,1},{4,6},{5,7},{6,4},{7,5},{8,10},{9,11},{10,... | collective-permute-start | bytes 983048 | tf_op jit(solution)/shard_map/ppermute | solution.py:189
  119.1 4.8 %copy-start.2 = (bf16[2,64,5120]{2,1,0:T(8,128)(2,1)S(1)}, bf16[2,64,5120]{2,1,0:T(8,128)(2,1)}, u32[]{:S(2)}) copy-start(bf16[2,64,5120]{2,1,0:T(8,128)(2,1)} %x_ref.1) | copy-start | bytes 3932164
  119.1 4.7 %collective-permute-start.7 = (bf16[8,320,128]{2,1,0:T(8,128)(2,1)S(1)}, bf16[8,320,128]{2,1,0:T(8,128)(2,1)S(1)}, u32[]{:S(2)}, u32[]{:S(2)}) collective-permute-start(bf16[8,320,128]{2,1,0:T(8,128)(2,1)S(1)} %pad_maximum_fusion.3), channel_id=1, source_target_pairs={{0,1},{1,0},{2,3},{3,2},{4,5},{5,4},{6,7},{7,6},{8,9},{9,8},{10,11... | collective-permute-start | bytes 1966088 | tf_op jit(solution)/shard_map/ppermute | solution.py:189
  151.4 0.8 copy-start.1
  152.2 17.7 %all-to-all-start.1 = ((bf16[16,2,64,128]{3,2,1,0:T(8,128)(2,1)}), bf16[16,2,64,128]{3,2,1,0:T(8,128)(2,1)S(1)}, u32[]{:S(2)}, u32[]{:S(2)}) async-start(bf16[16,2,64,128]{3,2,1,0:T(8,128)(2,1)} %copy-done.1), calls=%async_computation.1 | async-start | bytes 1048576 | tf_op jit(solution)/shard_map/all_to_all | solution.py:261

commit v2 on v0

v2 whole, which is shorter than its diff:
```python
import functools
import math

import jax
import jax.numpy as jnp
from jax import lax
from jax.experimental import pallas as pl
from jax.experimental.pallas import tpu as pltpu
from jax.sharding import PartitionSpec as P

LANES = 128
LOW = 4
ANY = pl.BlockSpec(memory_space=pl.ANY)
VMEM = pl.BlockSpec(memory_space=pltpu.VMEM)
SMEM = pl.BlockSpec(memory_space=pltpu.SMEM)


def bit_count(n):
    bits = n.bit_length() - 1
    assert 1 << bits == n
    return bits


def reversed_bits(j, bits):
    out = 0
    for i in range(bits):
        out = out | (((j >> i) & 1) << (bits - 1 - i))
    return out


def after(arrays, *others):
    return lax.optimization_barrier((tuple(arrays), others))[0]


def run_copies(copies):
    for copy in copies:
        copy.start()
    for copy in copies:
        copy.wait()


def pack_kernel(devs, pairs, me_ref, q_ref, k_ref, v_ref, *refs):
    outs, sems = refs[:-1], refs[-1]
    copies = []
    for k in range(devs):
        first = (me_ref[0] ^ k) * pairs
        for i, (src, dst) in enumerate(
            ((k_ref, outs[k].at[0]), (v_ref, outs[k].at[1]), (q_ref, outs[devs + k]))
        ):
            copies.append(
                pltpu.make_async_copy(src.at[pl.ds(first, pairs)], dst, sems.at[3 * k + i])
            )
    run_copies(copies)


def unpack_kernel(devs, pairs, me_ref, *refs):
    ins, out, sems = refs[:devs], refs[devs], refs[devs + 1]
    run_copies(
        [
            pltpu.make_async_copy(
                ins[k], out.at[pl.ds((me_ref[0] ^ k) * pairs, pairs)], sems.at[k]
            )
            for k in range(devs)
        ]
    )


def pick_kernel(
    shape, me_ref, row_ref, req_ref, down_ref, up_ref, *refs
):
    devs, bits, per_video, pairs, col_split, rows, tiles = shape
    downs, ups = refs[: bits + 1], refs[bits + 1 : 2 * bits + 2]
    down, up, sems = refs[2 * bits + 2 :]
    slots, ranks, _ = down_ref.shape
    videos = down.shape[0]
    me = me_ref[0]
    for s in range(videos):
        place = row_ref[req_ref[s]]
        slot = place % slots
        owned = place // slots == me
        copies = [
            pltpu.make_async_copy(down_ref.at[slot], down.at[s], sems.at[2 * s]),
            pltpu.make_async_copy(up_ref.at[slot], up.at[s], sems.at[2 * s + 1]),
        ]

        @pl.when(owned)
        def _():
            run_copies(copies)

        @pl.when(jnp.logical_not(owned))
        def _():
            down[s] = jnp.zeros(down.shape[1:], down.dtype)
            up[s] = jnp.zeros(up.shape[1:], up.dtype)

    for j in range(devs):
        step = bits - j.bit_length()
        at = j - (1 << (j.bit_length() - 1)) if j else 0
        dev = me ^ reversed_bits(j, bits)
        video = dev // per_video
        place = dev % per_video
        row = pl.multiple_of((place // col_split) * rows, rows)
        for t in range(tiles):
            col = pl.multiple_of(((place % col_split) * tiles + t) * LANES, LANES)
            downs[step][at, t * rows : (t + 1) * rows, :] = down[
                video, pl.ds(row, rows), pl.ds(col, LANES)
            ]
        for p in range(pairs):
            col = pl.multiple_of((place * pairs + p) * LANES, LANES)
            ups[step][at, p * ranks : (p + 1) * ranks, :] = up[video, :, pl.ds(col, LANES)]


def low_rank_kernel(shape, me_ref, x_ref, g_ref, out_ref, down):
    devs, bits, per_video, _, col_split, rows, tiles = shape
    for j in range(devs):
        dev = me_ref[0] ^ reversed_bits(j, bits)
        video = dev // per_video
        place = dev % per_video
        row = pl.multiple_of((place // col_split) * rows, rows)
        for t in range(tiles):
            col = pl.multiple_of(((place % col_split) * tiles + t) * LANES, LANES)
            down[video, pl.ds(row, rows), pl.ds(col, LANES)] = g_ref[j, t * rows : (t + 1) * rows, :]
    parts = [
        lax.dot_general(
            x_ref[s], down[s], (((1,), (1,)), ((), ())), preferred_element_type=jnp.float32
        )
        for s in range(x_ref.shape[0])
    ]
    out_ref[...] = jnp.concatenate(parts, axis=1).astype(out_ref.dtype)


def up_part(up_ref, video, videos, second):
    up = jnp.concatenate([up_ref[...]] * videos, axis=0)
    ranks = up_ref.shape[0]
    row = lax.broadcasted_iota(jnp.int32, up.shape, 0)
    half = (row % ranks) // (ranks // 2)
    keep = (row // ranks == video) & (half == second)
    return jnp.where(keep, up, jnp.zeros_like(up))


def low_rows(low_refs, ks):
    return jnp.concatenate([low_refs[k % LOW][k // LOW] for k in ks], axis=0)


def prepare_kernel(devs, per_video, me_ref, up_ref, *refs):
    low_refs, kv_refs = refs[:LOW], refs[LOW : LOW + devs]
    k_ref, v_ref = refs[LOW + devs :]
    toks = kv_refs[0].shape[1]
    videos = low_refs[0].shape[2] // up_ref.shape[0]
    up = up_part(up_ref, me_ref[0] // per_video, videos, 1)
    delta = jnp.dot(
        low_rows(low_refs, range(devs)), up, preferred_element_type=jnp.float32
    )
    for k in range(devs):
        here = slice(k * toks, (k + 1) * toks)
        k_ref[here, :] = kv_refs[k][0]
        v_ref[here, :] = (kv_refs[k][1].astype(jnp.float32) + delta[here]).astype(v_ref.dtype)


def attend_kernel(ks, block, per_video, me_ref, up_ref, k_ref, v_ref, *refs):
    count = len(ks)
    low_refs, q_refs, out_refs = refs[:LOW], refs[LOW : LOW + count], refs[LOW + count :]
    width = k_ref.shape[1]
    toks = q_refs[0].shape[0]
    videos = low_refs[0].shape[2] // up_ref.shape[0]
    up = up_part(up_ref, me_ref[0] // per_video, videos, 0)
    keys, vals = k_ref[...], v_ref[...]
    scale = math.log2(math.e) / math.sqrt(width)
    for b in range(0, count, block):
        delta = jnp.dot(
            low_rows(low_refs, ks[b : b + block]), up, preferred_element_type=jnp.float32
        )
        q = jnp.concatenate([r[...] for r in q_refs[b : b + block]], axis=0)
        q = (q.astype(jnp.float32) + delta).astype(jnp.bfloat16)
        scores = lax.dot_general(
            q, keys, (((1,), (1,)), ((), ())), preferred_element_type=jnp.float32
        )
        top = jnp.max(scores, axis=1, keepdims=True)
        weights = jnp.exp2((scores - top) * scale)
        total = jnp.sum(weights, axis=1, keepdims=True)
        mixed = jnp.dot(weights.astype(jnp.bfloat16), vals, preferred_element_type=jnp.float32)
        out = (mixed / total).astype(jnp.bfloat16)
        for i in range(block):
            out_refs[b + i][...] = out[i * toks : (i + 1) * toks]


def body(
    normed_token_features,
    queries,
    projected_keys,
    values,
    adapter_down_factors,
    adapter_up_factors,
    adapter_store_row,
    requests,
):
    videos, toks, model_width = normed_token_features.shape
    heads = queries.shape[1]
    width = queries.shape[3]
    _, ranks, up_width = adapter_up_factors.shape
    devs = lax.axis_size("seq")
    bits = bit_count(devs)
    me = lax.axis_index("seq").astype(jnp.int32)[None]
    pairs = videos * heads // devs
    per_video = devs // videos
    length = devs * toks
    col_split = math.gcd(per_video, model_width // LANES)
    rows = ranks * col_split // per_video
    tiles = model_width // col_split // LANES
    shape = (devs, bits, per_video, pairs, col_split, rows, tiles)
    everyone = range(devs)

    def swap(tensor, k):
        return lax.ppermute(tensor, "seq", [(i, i ^ k) for i in everyone])

    def halve(pieces, gate=None):
        got = []
        for i in range(bits):
            h = devs >> (i + 1)
            send = sum((r[h : 2 * h] for r in got), pieces[i])
            if gate is not None:
                (send,) = after((send,), gate[i])
            got.append(swap(send, 1 << i))
        return sum((r[:1] for r in got), pieces[bits]), got

    sizes = [(2, pairs, toks, width)] * devs + [(pairs, toks, width)] * devs
    packed = pl.pallas_call(
        functools.partial(pack_kernel, devs, pairs),
        in_specs=[SMEM, ANY, ANY, ANY],
        out_specs=[ANY] * (2 * devs),
        out_shape=[jax.ShapeDtypeStruct(s, jnp.bfloat16) for s in sizes],
        scratch_shapes=[pltpu.SemaphoreType.DMA((3 * devs,))],
        cost_estimate=pl.CostEstimate(
            flops=0, bytes_accessed=12 * pairs * length * width, transcendentals=0
        ),
        name="pack",
    )(me, *(t.reshape(-1, toks, width) for t in (queries, projected_keys, values)))
    kv, q = list(packed[:devs]), list(packed[devs:])

    steps = [devs >> (i + 1) for i in range(bits)] + [1]
    piece_shapes = [(h, tiles * rows, LANES) for h in steps] + [
        (h, pairs * ranks, LANES) for h in steps
    ]
    pieces = pl.pallas_call(
        functools.partial(pick_kernel, shape),
        in_specs=[SMEM, SMEM, SMEM, ANY, ANY],
        out_specs=[VMEM] * (2 * bits + 2),
        out_shape=[jax.ShapeDtypeStruct(s, jnp.bfloat16) for s in piece_shapes],
        scratch_shapes=[
            pltpu.VMEM((videos, ranks, model_width), jnp.bfloat16),
            pltpu.VMEM((videos, ranks, up_width), jnp.bfloat16),
            pltpu.SemaphoreType.DMA((2 * videos,)),
        ],
        compiler_params=pltpu.CompilerParams(vmem_limit_bytes=24 << 20),
        cost_estimate=pl.CostEstimate(
            flops=0,
            bytes_accessed=4 * videos * ranks * (model_width + up_width),
            transcendentals=0,
        ),
        name="pick_factors",
    )(me, adapter_store_row, requests, adapter_down_factors, adapter_up_factors)

    shard, halved = halve(pieces[: bits + 1])
    gathered = [shard]
    for bit in reversed(range(bits)):
        gathered.append(jnp.concatenate([gathered[-1], swap(gathered[-1], 1 << bit)], axis=0))
    up_here = halve(pieces[bits + 1 :], halved)[0].reshape(pairs, ranks, LANES)

    low = pl.pallas_call(
        functools.partial(low_rank_kernel, shape),
        in_specs=[SMEM, VMEM, VMEM],
        out_specs=VMEM,
        scratch_shapes=[pltpu.VMEM((videos, ranks, model_width), jnp.bfloat16)],
        out_shape=jax.ShapeDtypeStruct((toks, videos * ranks), jnp.bfloat16),
        compiler_params=pltpu.CompilerParams(vmem_limit_bytes=24 << 20),
        cost_estimate=pl.CostEstimate(
            flops=2 * videos * toks * ranks * model_width,
            bytes_accessed=2 * videos * (toks + ranks) * model_width,
            transcendentals=0,
        ),
        name="low_rank",
    )(me, normed_token_features, gathered[-1])
    far = jnp.stack([low] + [swap(low, LOW * i) for i in range(1, devs // LOW)])
    lows = [far] + [swap(far, i) for i in range(1, LOW)]

    top = devs >> 1
    early = [k for k in everyone if k & top and not k & 2]
    middle = [k for k in everyone if k & top and k & 2]
    near = [k for k in range(1, top)]
    gates = {k: None for k in early}
    for i, k in enumerate(middle):
        gates[k] = shard if 2 * i < len(middle) else gathered[min(2, bits)]
    for k in near:
        gates[k] = halved[min(1, bits - 1)] if k < LOW else gathered[min(2, bits)]
    for k in everyone[1:]:
        if gates[k] is not None:
            (kv[k],) = after((kv[k],), gates[k])
        (q[k],) = after((q[k],), gathered[-1] if k & top else low)
    kv_here = [kv[0]] + [swap(kv[k], k) for k in everyone[1:]]
    q_here = [q[0]] + [swap(q[k], k) for k in everyone[1:]]

    low_specs = [pl.BlockSpec((devs // LOW, toks, videos * ranks), lambda p: (0, 0, 0))] * LOW
    up_spec = pl.BlockSpec((pl.squeezed, ranks, LANES), lambda p: (p, 0, 0))
    all_spec = pl.BlockSpec((pl.squeezed, length, width), lambda p: (p, 0, 0))
    part_spec = pl.BlockSpec((pl.squeezed, toks, width), lambda p: (p, 0, 0))
    keys, vals = pl.pallas_call(
        functools.partial(prepare_kernel, devs, per_video),
        grid=(pairs,),
        in_specs=[SMEM, up_spec, *low_specs]
        + [pl.BlockSpec((2, pl.squeezed, toks, width), lambda p: (0, p, 0, 0))] * devs,
        out_specs=[all_spec] * 2,
        out_shape=[jax.ShapeDtypeStruct((pairs, length, width), jnp.bfloat16)] * 2,
        compiler_params=pltpu.CompilerParams(vmem_limit_bytes=40 << 20),
        cost_estimate=pl.CostEstimate(
            flops=2 * pairs * length * width * videos * ranks,
            bytes_accessed=8 * pairs * length * width,
            transcendentals=0,
        ),
        name="prepare",
    )(me, up_here, *lows, *kv_here)

    def attend(ks):
        count = len(ks)
        return pl.pallas_call(
            functools.partial(
                attend_kernel, ks, math.gcd(count, max(1, 256 // toks)), per_video
            ),
            grid=(pairs,),
            in_specs=[SMEM, up_spec, all_spec, all_spec, *low_specs] + [part_spec] * count,
            out_specs=[part_spec] * count,
            out_shape=[jax.ShapeDtypeStruct((pairs, toks, width), jnp.bfloat16)] * count,
            compiler_params=pltpu.CompilerParams(vmem_limit_bytes=40 << 20),
            cost_estimate=pl.CostEstimate(
                flops=4 * pairs * count * toks * length * width,
                bytes_accessed=4 * pairs * (count * toks + length) * width,
                transcendentals=pairs * count * toks * length,
            ),
            name="attend",
        )(me, up_here, keys, vals, *lows, *(q_here[k] for k in ks))

    back = [None] * devs
    half = top // 2
    for ks in (early, middle, near[half - 1 :], [0] + near[: half - 1]):
        for k, out in zip(ks, attend(ks)):
            back[k] = swap(out, k) if k else out

    out = pl.pallas_call(
        functools.partial(unpack_kernel, devs, pairs),
        in_specs=[SMEM] + [ANY] * devs,
        out_specs=ANY,
        out_shape=jax.ShapeDtypeStruct((devs * pairs, toks, width), jnp.bfloat16),
        scratch_shapes=[pltpu.SemaphoreType.DMA((devs,))],
        cost_estimate=pl.CostEstimate(
            flops=0, bytes_accessed=4 * pairs * length * width, transcendentals=0
        ),
        name="unpack",
    )(me, *back)
    return out.reshape(videos, heads, toks, width)


def solution(mesh):
    in_specs = (
        P("grp", "seq", None),
        P("grp", None, "seq", None),
        P("grp", None, "seq", None),
        P("grp", None, "seq", None),
        P("seq", None, None),
        P("seq", None, None),
        P(),
        P("grp"),
    )
    out_specs = P("grp", None, "seq", None)
    return jax.shard_map(body, mesh=mesh, in_specs=in_specs, out_specs=out_specs, check_vma=False)
```

time: 314 us -> 308 us (0.981)
  Pallas kernels: 0 us -> 146 us
  blocking collectives: 93.3 us -> 0 us
  starting transfers between devices: 14.7 us -> 108 us
  local copies, waits for them, and re-layouts: 68.5 us -> 6.17 us
  waiting for transfers between devices: 87.9 us -> 42.7 us
  other arithmetic: 21.8 us -> 2.97 us
  between operations: 13.5 us -> 0.76 us
  matrix products: 10.8 us -> 0 us
    pallas_call x0 -> x9, Pallas kernels: none -> 146 us  [the longest x1 96.8 us: body(): pl.pallas_call(functools.partial(pack_kernel, devs, pairs), in_specs=[SME...]
    ppermute x0 -> x63, starting transfers between devices: none -> 108 us  [swap(): return lax.ppermute(tensor, 'seq', [(i, i ^ k) for i in everyone])]
    all_to_all x2 -> x0, blocking collectives: 93.3 us -> none  [the longest x1 61.6 us: body(): lax.all_to_all(contribution, 'seq', split_axis=1, concat_axis=1, tiled=True)]
    all_gather x1 -> x0, waiting for transfers between devices: 47.2 us -> none  [body(): factors = lax.all_gather(shares, 'seq', axis=1, tiled=True)]
    ppermute x0 -> x63, waiting for transfers between devices: none -> 42.7 us  [swap(): return lax.ppermute(tensor, 'seq', [(i, i ^ k) for i in everyone])]
    all_to_all x3 -> x0, waiting for transfers between devices: 40.6 us -> none  [the longest x1 20.8 us: body(): lax.all_to_all(to_pairs(value_mix), 'seq', split_axis=0, concat_axis=2, t...]
    gather x7 -> x0, local copies, waits for them, and re-layouts: 36.8 us -> none  [the longest x6 35.5 us: body(): picked = jnp.take(flat_store, local_slot, axis=0)]
    all_to_all x3 -> x0, starting transfers between devices: 14.7 us -> none  [the longest x1 6.65 us: body(): lax.all_to_all(to_pairs(query_mix), 'seq', split_axis=0, concat_axis=2, t...]
  transfers between devices with their start and end apart: 4 -> 63, of which waited for: 3 -> 14; matrix products, arithmetic and copies ran while one was open for 3% -> 1% of each run, Pallas kernels for 0% -> 36%
where the time goes in v2:
time: 308 us; the launch traced here: 306 us
  Pallas kernels  146 us (47%)
  starting transfers between devices  108 us (35%)
  waiting for transfers between devices  42.7 us (14%)
  local copies, waits for them, and re-layouts  6.17 us (2%)
    ppermute x63, starting transfers between devices, swap(): return lax.ppermute(tensor, 'seq', [(i, i ^ k) for i in everyone])  108 us
    pallas_call x1, Pallas kernels, body(): pl.pallas_call(functools.partial(pack_kernel, devs, pairs), in_specs=[SME...  96.8 us
    ppermute x63, waiting for transfers between devices, swap(): return lax.ppermute(tensor, 'seq', [(i, i ^ k) for i in everyone])  42.7 us
    pallas_call x1, Pallas kernels, body(): pl.pallas_call(functools.partial(unpack_kernel, devs, pairs), in_specs=[S...  33 us
    pallas_call x4, Pallas kernels, attend(): pl.pallas_call(functools.partial(attend_kernel, ks, math.gcd(count, max(1...  12.5 us
  transfers between devices with their start and end apart: 63, of which 14 were waited for; matrix products, arithmetic and copies ran while one was open for 1% of the time, Pallas kernels for 36%

profile of v2, /device:TPU:1, one launch (start us, length us, event | category | flops | bytes accessed | tf_op | source)
XLA Modules:
  0.0 306.4 jit_solution(358842714998044407)
XLA Ops:
  0.0 1.7 copy-done
  1.7 1.6 copy-done.1
  4.6 1.5 pick_factors.1
  6.3 2.0 collective-permute-done
  8.4 2.4 collective-permute-start.2
  10.8 7.8 %collective-permute-done.2 = bf16[4,320,128]{2,1,0:T(8,128)(2,1)S(1)} collective-permute-done((bf16[4,320,128]{2,1,0:T(8,128)(2,1)S(1)}, bf16[4,320,128]{2,1,0:T(8,128)(2,1)S(1)}, u32[]{:S(2)}, u32[]{:S(2)}) %collective-permute-start.2) | collective-permute-done | bytes 327712 | tf_op jit(solution)/shard_map/ppermute | solution.py:213
  19.9 3.6 %collective-permute-done.4 = bf16[2,320,128]{2,1,0:T(8,128)(2,1)S(1)} collective-permute-done((bf16[2,320,128]{2,1,0:T(8,128)(2,1)S(1)}, bf16[2,320,128]{2,1,0:T(8,128)(2,1)S(1)}, u32[]{:S(2)}, u32[]{:S(2)}) %collective-permute-start.4) | collective-permute-done | bytes 163872 | tf_op jit(solution)/shard_map/ppermute | solution.py:213
  23.6 1.9 collective-permute-start.6
  25.5 2.4 collective-permute-start.1
  29.9 4.0 %collective-permute-done.8 = bf16[1,320,128]{2,1,0:T(8,128)(2,1)S(1)} collective-permute-done((bf16[1,320,128]{2,1,0:T(8,128)(2,1)S(1)}, bf16[1,320,128]{2,1,0:T(8,128)(2,1)S(1)}, u32[]{:S(2)}, u32[]{:S(2)}) %collective-permute-start.8) | collective-permute-done | bytes 81952 | tf_op jit(solution)/shard_map/ppermute | solution.py:213
  34.0 4.2 %collective-permute-done.9 = bf16[2,320,128]{2,1,0:T(8,128)(2,1)S(1)} collective-permute-done((bf16[2,320,128]{2,1,0:T(8,128)(2,1)S(1)}, bf16[2,320,128]{2,1,0:T(8,128)(2,1)S(1)}, u32[]{:S(2)}, u32[]{:S(2)}) %collective-permute-start.9) | collective-permute-done | bytes 163872 | tf_op jit(solution)/shard_map/ppermute | solution.py:213
  39.8 96.8 %pack.1 = (bf16[2,4,64,128]{3,2,1,0:T(8,128)(2,1)}, bf16[2,4,64,128]{3,2,1,0:T(8,128)(2,1)}, bf16[2,4,64,128]{3,2,1,0:T(8,128)(2,1)}, bf16[2,4,64,128]{3,2,1,0:T...) custom-call(s32[1]{0:T(128)} %bitcast.me_ref, ...), custom_call_target="tpu_custom_call" | custom-call | bytes 6291456 | tf_op jit(solution)/shard_map/pack/pallas_call | solution.py:226
  138.0 5.8 %collective-permute-start.26 = (bf16[2,4,64,128]{3,2,1,0:T(8,128)(2,1)}, bf16[2,4,64,128]{3,2,1,0:T(8,128)(2,1)S(1)}, u32[]{:S(2)}, u32[]{:S(2)}) collective-permute-start(bf16[2,4,64,128]{3,2,1,0:T(8,128)(2,1)} %get-tuple-element.125), channel_id=1, source_target_pairs={{0,9},{1,8},{2,11},{3,10},{4,13},{5,12},{6,15},{7,14},{8,1},{9,0},... | collective-permute-start | bytes 393224 | tf_op jit(solution)/shard_map/ppermute | solution.py:213
  143.8 4.0 %collective-permute-start.29 = (bf16[2,4,64,128]{3,2,1,0:T(8,128)(2,1)}, bf16[2,4,64,128]{3,2,1,0:T(8,128)(2,1)S(1)}, u32[]{:S(2)}, u32[]{:S(2)}) collective-permute-start(bf16[2,4,64,128]{3,2,1,0:T(8,128)(2,1)} %get-tuple-element.130), channel_id=1, source_target_pairs={{0,12},{1,13},{2,14},{3,15},{4,8},{5,9},{6,10},{7,11},{8,4},{9,5},... | collective-permute-start | bytes 393224 | tf_op jit(solution)/shard_map/ppermute | solution.py:213
  150.7 8.5 %collective-permute-done.26.refs_13_ = bf16[2,4,64,128]{3,2,1,0:T(8,128)(2,1)S(1)} collective-permute-done((bf16[2,4,64,128]{3,2,1,0:T(8,128)(2,1)}, bf16[2,4,64,128]{3,2,1,0:T(8,128)(2,1)S(1)}, u32[]{:S(2)}, u32[]{:S(2)}) %collective-permute-start.26) | collective-permute-done | bytes 131104 | tf_op jit(solution)/shard_map/ppermute | solution.py:213
  161.7 3.5 %collective-permute-start.5 = (bf16[2,256,128]{2,1,0:T(8,128)(2,1)S(1)}, bf16[2,256,128]{2,1,0:T(8,128)(2,1)S(1)}, u32[]{:S(2)}, u32[]{:S(2)}) collective-permute-start(bf16[2,256,128]{2,1,0:T(8,128)(2,1)S(1)} %slice_add_fusion.4), channel_id=1, source_target_pairs={{0,4},{1,5},{2,6},{3,7},{4,0},{5,1},{6,2},{7,3},{8,12},{9,13},{10,... | collective-permute-start | bytes 393224 | tf_op jit(solution)/shard_map/ppermute | solution.py:213
  165.2 2.1 collective-permute-start.28
  167.4 2.0 collective-permute-start.27
  169.4 3.7 %collective-permute-start.32 = (bf16[2,4,64,128]{3,2,1,0:T(8,128)(2,1)S(1)}, bf16[2,4,64,128]{3,2,1,0:T(8,128)(2,1)S(1)}, u32[]{:S(2)}, u32[]{:S(2)}) collective-permute-start(bf16[2,4,64,128]{3,2,1,0:T(8,128)(2,1)S(1)} %copy-done.28), channel_id=1, source_target_pairs={{0,15},{1,14},{2,13},{3,12},{4,11},{5,10},{6,9},{7,8},{8,7},{9,6},... | collective-permute-start | bytes 393224 | tf_op jit(solution)/shard_map/ppermute | solution.py:213
  174.2 10.1 %collective-permute-start.24 = (bf16[2,4,64,128]{3,2,1,0:T(8,128)(2,1)S(1)}, bf16[2,4,64,128]{3,2,1,0:T(8,128)(2,1)S(1)}, u32[]{:S(2)}, u32[]{:S(2)}) collective-permute-start(bf16[2,4,64,128]{3,2,1,0:T(8,128)(2,1)S(1)} %copy-done.26), channel_id=1, source_target_pairs={{0,7},{1,6},{2,5},{3,4},{4,3},{5,2},{6,1},{7,0},{8,15},{9,14},{10,... | collective-permute-start | bytes 393224 | tf_op jit(solution)/shard_map/ppermute | solution.py:213
  184.4 2.9 collective-permute-done.27.refs_14_
  187.2 5.9 %collective-permute-start.22 = (bf16[2,4,64,128]{3,2,1,0:T(8,128)(2,1)S(1)}, bf16[2,4,64,128]{3,2,1,0:T(8,128)(2,1)S(1)}, u32[]{:S(2)}, u32[]{:S(2)}) collective-permute-start(bf16[2,4,64,128]{3,2,1,0:T(8,128)(2,1)S(1)} %copy-done.24), channel_id=1, source_target_pairs={{0,5},{1,4},{2,7},{3,6},{4,1},{5,0},{6,3},{7,2},{8,13},{9,12},{10,... | collective-permute-start | bytes 393224 | tf_op jit(solution)/shard_map/ppermute | solution.py:213
  193.1 5.0 %collective-permute-start.21 = (bf16[2,4,64,128]{3,2,1,0:T(8,128)(2,1)S(1)}, bf16[2,4,64,128]{3,2,1,0:T(8,128)(2,1)S(1)}, u32[]{:S(2)}, u32[]{:S(2)}) collective-permute-start(bf16[2,4,64,128]{3,2,1,0:T(8,128)(2,1)S(1)} %copy-done.23), channel_id=1, source_target_pairs={{0,4},{1,5},{2,6},{3,7},{4,0},{5,1},{6,2},{7,3},{8,12},{9,13},{10,... | collective-permute-start | bytes 393224 | tf_op jit(solution)/shard_map/ppermute | solution.py:213
  199.2 2.2 collective-permute-start.14
  202.8 4.4 %collective-permute-start.56 = (bf16[4,64,128]{2,1,0:T(8,128)(2,1)S(1)}, bf16[4,64,128]{2,1,0:T(8,128)(2,1)S(1)}, u32[]{:S(2)}, u32[]{:S(2)}) collective-permute-start(bf16[4,64,128]{2,1,0:T(8,128)(2,1)S(1)} %copy-done.48), channel_id=1, source_target_pairs={{0,15},{1,14},{2,13},{3,12},{4,11},{5,10},{6,9},{7,8},{8,7},{9,6},... | collective-permute-start | bytes 196616 | tf_op jit(solution)/shard_map/ppermute | solution.py:213
  207.3 2.1 collective-permute-start.55
  209.4 2.9 collective-permute-start.42
  212.3 1.4 collective-permute-start.17
  214.2 2.2 collective-permute-done.54.refs_5_
  223.5 1.4 prepare.1
  224.9 1.7 collective-permute-start.53
  227.9 2.2 collective-permute-start.49
  230.1 2.7 collective-permute-start.47
  232.8 3.1 %attend.5 = (bf16[4,64,128]{2,1,0:T(8,128)(2,1)S(1)}, bf16[4,64,128]{2,1,0:T(8,128)(2,1)S(1)}, bf16[4,64,128]{2,1,0:T(8,128)(2,1)S(1)}, bf16[4,64,128]{2,1,0:T(8,128)(2,1)S(1)}) custom-call(s32[1]{0:T(128)} %bitcast.me_ref, bf16[4,64,128]{2,1,0:T(8,128)(2,1)S(1)} %bitcast.11, bf16[4,1024,128]{2,1,0:T(8,128)(2,1)S(1)} %get-tuple-element.136.k_ref, ...), custom_call_target="tpu_custom_call" | custom-call | flops 536870912 | bytes 2621440 | tf_op jit(solution)/shard_map/attend/pallas_call | solution.py:323
  235.9 3.1 %attend.4 = (bf16[4,64,128]{2,1,0:T(8,128)(2,1)S(1)}, bf16[4,64,128]{2,1,0:T(8,128)(2,1)S(1)}, bf16[4,64,128]{2,1,0:T(8,128)(2,1)S(1)}, bf16[4,64,128]{2,1,0:T(8,128)(2,1)S(1)}) custom-call(s32[1]{0:T(128)} %bitcast.me_ref, bf16[4,64,128]{2,1,0:T(8,128)(2,1)S(1)} %bitcast.12, bf16[4,1024,128]{2,1,0:T(8,128)(2,1)S(1)} %get-tuple-element.136.k_ref, ...), custom_call_target="tpu_custom_call" | custom-call | flops 536870912 | bytes 2621440 | tf_op jit(solution)/shard_map/attend/pallas_call | solution.py:323
  239.7 1.9 collective-permute-start.44
  241.6 2.5 collective-permute-start.46
  244.4 3.1 %attend.6 = (bf16[4,64,128]{2,1,0:T(8,128)(2,1)S(1)}, bf16[4,64,128]{2,1,0:T(8,128)(2,1)S(1)}, bf16[4,64,128]{2,1,0:T(8,128)(2,1)S(1)}, bf16[4,64,128]{2,1,0:T(8,128)(2,1)S(1)}) custom-call(s32[1]{0:T(128)} %bitcast.me_ref, bf16[4,64,128]{2,1,0:T(8,128)(2,1)S(1)} %bitcast.13, bf16[4,1024,128]{2,1,0:T(8,128)(2,1)S(1)} %get-tuple-element.136.k_ref, ...), custom_call_target="tpu_custom_call" | custom-call | flops 536870912 | bytes 2621440 | tf_op jit(solution)/shard_map/attend/pallas_call | solution.py:323
  248.0 1.5 collective-permute-start.38
  249.7 2.3 collective-permute-start.52
  253.1 3.1 %attend.7 = (bf16[4,64,128]{2,1,0:T(8,128)(2,1)S(1)}, bf16[4,64,128]{2,1,0:T(8,128)(2,1)S(1)}, bf16[4,64,128]{2,1,0:T(8,128)(2,1)S(1)}, bf16[4,64,128]{2,1,0:T(8,128)(2,1)S(1)}) custom-call(s32[1]{0:T(128)} %bitcast.me_ref, bf16[4,64,128]{2,1,0:T(8,128)(2,1)S(1)} %bitcast.14, bf16[4,1024,128]{2,1,0:T(8,128)(2,1)S(1)} %get-tuple-element.136.k_ref, ...), custom_call_target="tpu_custom_call" | custom-call | flops 536870912 | bytes 2621440 | tf_op jit(solution)/shard_map/attend/pallas_call | solution.py:323
  256.3 2.6 collective-permute-start.60
  258.9 3.4 %collective-permute-start.58 = (bf16[4,64,128]{2,1,0:T(8,128)(2,1)S(1)}, bf16[4,64,128]{2,1,0:T(8,128)(2,1)S(1)}, u32[]{:S(2)}, u32[]{:S(2)}) collective-permute-start(bf16[4,64,128]{2,1,0:T(8,128)(2,1)S(1)} %get-tuple-element.180), channel_id=1, source_target_pairs={{0,11},{1,10},{2,9},{3,8},{4,15},{5,14},{6,13},{7,12},{8,3},{9,2},... | collective-permute-start | bytes 196616 | tf_op jit(solution)/shard_map/ppermute | solution.py:213
  262.3 1.7 collective-permute-start.61
  264.1 2.8 collective-permute-start.62
  266.9 3.0 collective-permute-done.57.refs_10_
  269.9 2.8 collective-permute-done.58.refs_11_
  273.4 33.0 %unpack.1 = bf16[64,64,128]{2,1,0:T(8,128)(2,1)} custom-call(s32[1]{0:T(128)} %bitcast.me_ref, bf16[4,64,128]{2,1,0:T(8,128)(2,1)} %copy-done.5, bf16[4,64,128]{2,1,0:T(8,128)(2,1)} %copy-done.12, bf16[4,64,128]{2,1,0:T(8,128)(2,1)} %copy-done.13, bf16[4,64,128]{2,1,0:T(8,128)(2,1)} %copy-done.14, bf16[4,64,128]{2,1,0:T(8,128)(2,1)} %copy-done.8, ...), custom_call_target="tpu_custom_call" | custom-call | bytes 2097152 | tf_op jit(solution)/shard_map/unpack/pallas_call | solution.py:346
  (201 shorter events, 29.0 us)
Async XLA Ops:
  8.4 10.2 %collective-permute-start.2 = (bf16[4,320,128]{2,1,0:T(8,128)(2,1)S(1)}, bf16[4,320,128]{2,1,0:T(8,128)(2,1)S(1)}, u32[]{:S(2)}, u32[]{:S(2)}) collective-permute-start(bf16[4,320,128]{2,1,0:T(8,128)(2,1)S(1)} %slice_add_fusion), channel_id=1, source_target_pairs={{0,2},{1,3},{2,0},{3,1},{4,6},{5,7},{6,4},{7,5},{8,10},{9,11},{10,... | collective-permute-start | bytes 983048 | tf_op jit(solution)/shard_map/ppermute | solution.py:213
  25.5 13.0 %collective-permute-start.1 = (bf16[8,256,128]{2,1,0:T(8,128)(2,1)S(1)}, bf16[8,256,128]{2,1,0:T(8,128)(2,1)S(1)}, u32[]{:S(2)}, u32[]{:S(2)}) collective-permute-start(bf16[8,256,128]{2,1,0:T(8,128)(2,1)S(1)} %get-tuple-element.98), channel_id=1, source_target_pairs={{0,1},{1,0},{2,3},{3,2},{4,5},{5,4},{6,7},{7,6},{8,9},{9,8},{10,11... | collective-permute-start | bytes 1572872 | tf_op jit(solution)/shard_map/ppermute | solution.py:213
  38.2 109.6 %collective-permute-start.10 = (bf16[4,320,128]{2,1,0:T(8,128)(2,1)S(1)}, bf16[4,320,128]{2,1,0:T(8,128)(2,1)S(1)}, u32[]{:S(2)}, u32[]{:S(2)}) collective-permute-start(bf16[4,320,128]{2,1,0:T(8,128)(2,1)S(1)} %pad_maximum_fusion.1), channel_id=1, source_target_pairs={{0,2},{1,3},{2,0},{3,1},{4,6},{5,7},{6,4},{7,5},{8,10},{9,11},{10,... | collective-permute-start | bytes 983048 | tf_op jit(solution)/shard_map/ppermute | solution.py:213
  38.6 109.3 %collective-permute-start.3 = (bf16[4,256,128]{2,1,0:T(8,128)(2,1)S(1)}, bf16[4,256,128]{2,1,0:T(8,128)(2,1)}, u32[]{:S(2)}, u32[]{:S(2)}) collective-permute-start(bf16[4,256,128]{2,1,0:T(8,128)(2,1)S(1)} %slice_add_fusion.1), channel_id=1, source_target_pairs={{0,2},{1,3},{2,0},{3,1},{4,6},{5,7},{6,4},{7,5},{8,10},{9,11},{10,... | collective-permute-start | bytes 786440 | tf_op jit(solution)/shard_map/ppermute | solution.py:213
  136.7 12.6 %collective-permute-start.25 = (bf16[2,4,64,128]{3,2,1,0:T(8,128)(2,1)}, bf16[2,4,64,128]{3,2,1,0:T(8,128)(2,1)S(1)}, u32[]{:S(2)}, u32[]{:S(2)}) collective-permute-start(bf16[2,4,64,128]{3,2,1,0:T(8,128)(2,1)} %get-tuple-element.124), channel_id=1, source_target_pairs={{0,8},{1,9},{2,10},{3,11},{4,12},{5,13},{6,14},{7,15},{8,0},{9,1},... | collective-permute-start | bytes 393224 | tf_op jit(solution)/shard_map/ppermute | solution.py:213
  138.0 21.3 %collective-permute-start.26 = (bf16[2,4,64,128]{3,2,1,0:T(8,128)(2,1)}, bf16[2,4,64,128]{3,2,1,0:T(8,128)(2,1)S(1)}, u32[]{:S(2)}, u32[]{:S(2)}) collective-permute-start(bf16[2,4,64,128]{3,2,1,0:T(8,128)(2,1)} %get-tuple-element.125), channel_id=1, source_target_pairs={{0,9},{1,8},{2,11},{3,10},{4,13},{5,12},{6,15},{7,14},{8,1},{9,0},... | collective-permute-start | bytes 393224 | tf_op jit(solution)/shard_map/ppermute | solution.py:213
  143.8 16.8 %collective-permute-start.29 = (bf16[2,4,64,128]{3,2,1,0:T(8,128)(2,1)}, bf16[2,4,64,128]{3,2,1,0:T(8,128)(2,1)S(1)}, u32[]{:S(2)}, u32[]{:S(2)}) collective-permute-start(bf16[2,4,64,128]{3,2,1,0:T(8,128)(2,1)} %get-tuple-element.130), channel_id=1, source_target_pairs={{0,12},{1,13},{2,14},{3,15},{4,8},{5,9},{6,10},{7,11},{8,4},{9,5},... | collective-permute-start | bytes 393224 | tf_op jit(solution)/shard_map/ppermute | solution.py:213
  147.8 13.9 %collective-permute-start.30 = (bf16[2,4,64,128]{3,2,1,0:T(8,128)(2,1)}, bf16[2,4,64,128]{3,2,1,0:T(8,128)(2,1)S(1)}, u32[]{:S(2)}, u32[]{:S(2)}) collective-permute-start(bf16[2,4,64,128]{3,2,1,0:T(8,128)(2,1)} %get-tuple-element.131), channel_id=1, source_target_pairs={{0,13},{1,12},{2,15},{3,14},{4,9},{5,8},{6,11},{7,10},{8,5},{9,4},... | collective-permute-start | bytes 393224 | tf_op jit(solution)/shard_map/ppermute | solution.py:213
  147.9 50.2 %collective-permute-start.11 = (bf16[8,320,128]{2,1,0:T(8,128)(2,1)S(1)}, bf16[8,320,128]{2,1,0:T(8,128)(2,1)S(1)}, u32[]{:S(2)}, u32[]{:S(2)}) collective-permute-start(bf16[8,320,128]{2,1,0:T(8,128)(2,1)S(1)} %pad_maximum_fusion), channel_id=1, source_target_pairs={{0,1},{1,0},{2,3},{3,2},{4,5},{5,4},{6,7},{7,6},{8,9},{9,8},{10,11... | collective-permute-start | bytes 1966088 | tf_op jit(solution)/shard_map/ppermute | solution.py:213
  149.4 15.9 %collective-permute-start.20 = (bf16[2,4,64,128]{3,2,1,0:T(8,128)(2,1)S(1)}, bf16[2,4,64,128]{3,2,1,0:T(8,128)(2,1)S(1)}, u32[]{:S(2)}, u32[]{:S(2)}) collective-permute-start(bf16[2,4,64,128]{3,2,1,0:T(8,128)(2,1)S(1)} %copy-done.33), channel_id=1, source_target_pairs={{0,3},{1,2},{2,1},{3,0},{4,7},{5,6},{6,5},{7,4},{8,11},{9,10},{10,... | collective-permute-start | bytes 393224 | tf_op jit(solution)/shard_map/ppermute | solution.py:213
  159.3 8.1 %collective-permute-start.19 = (bf16[2,4,64,128]{3,2,1,0:T(8,128)(2,1)S(1)}, bf16[2,4,64,128]{3,2,1,0:T(8,128)(2,1)S(1)}, u32[]{:S(2)}, u32[]{:S(2)}) collective-permute-start(bf16[2,4,64,128]{3,2,1,0:T(8,128)(2,1)S(1)} %copy-done.32), channel_id=1, source_target_pairs={{0,2},{1,3},{2,0},{3,1},{4,6},{5,7},{6,4},{7,5},{8,10},{9,11},{10,... | collective-permute-start | bytes 393224 | tf_op jit(solution)/shard_map/ppermute | solution.py:213
  160.6 8.8 %collective-permute-start.18 = (bf16[2,4,64,128]{3,2,1,0:T(8,128)(2,1)S(1)}, bf16[2,4,64,128]{3,2,1,0:T(8,128)(2,1)S(1)}, u32[]{:S(2)}, u32[]{:S(2)}) collective-permute-start(bf16[2,4,64,128]{3,2,1,0:T(8,128)(2,1)S(1)} %copy-done.31), channel_id=1, source_target_pairs={{0,1},{1,0},{2,3},{3,2},{4,5},{5,4},{6,7},{7,6},{8,9},{9,8},{10,11... | collective-permute-start | bytes 393224 | tf_op jit(solution)/shard_map/ppermute | solution.py:213
  161.7 11.4 %collective-permute-start.5 = (bf16[2,256,128]{2,1,0:T(8,128)(2,1)S(1)}, bf16[2,256,128]{2,1,0:T(8,128)(2,1)S(1)}, u32[]{:S(2)}, u32[]{:S(2)}) collective-permute-start(bf16[2,256,128]{2,1,0:T(8,128)(2,1)S(1)} %slice_add_fusion.4), channel_id=1, source_target_pairs={{0,4},{1,5},{2,6},{3,7},{4,0},{5,1},{6,2},{7,3},{8,12},{9,13},{10,... | collective-permute-start | bytes 393224 | tf_op jit(solution)/shard_map/ppermute | solution.py:213
  165.2 9.0 %collective-permute-start.28 = (bf16[2,4,64,128]{3,2,1,0:T(8,128)(2,1)S(1)}, bf16[2,4,64,128]{3,2,1,0:T(8,128)(2,1)S(1)}, u32[]{:S(2)}, u32[]{:S(2)}) collective-permute-start(bf16[2,4,64,128]{3,2,1,0:T(8,128)(2,1)S(1)} %copy-done.30), channel_id=1, source_target_pairs={{0,11},{1,10},{2,9},{3,8},{4,15},{5,14},{6,13},{7,12},{8,3},{9,2},... | collective-permute-start | bytes 393224 | tf_op jit(solution)/shard_map/ppermute | solution.py:213
  167.4 19.8 %collective-permute-start.27 = (bf16[2,4,64,128]{3,2,1,0:T(8,128)(2,1)S(1)}, bf16[2,4,64,128]{3,2,1,0:T(8,128)(2,1)S(1)}, u32[]{:S(2)}, u32[]{:S(2)}) collective-permute-start(bf16[2,4,64,128]{3,2,1,0:T(8,128)(2,1)S(1)} %copy-done.29), channel_id=1, source_target_pairs={{0,10},{1,11},{2,8},{3,9},{4,14},{5,15},{6,12},{7,13},{8,2},{9,3},... | collective-permute-start | bytes 393224 | tf_op jit(solution)/shard_map/ppermute | solution.py:213
  169.4 17.8 %collective-permute-start.32 = (bf16[2,4,64,128]{3,2,1,0:T(8,128)(2,1)S(1)}, bf16[2,4,64,128]{3,2,1,0:T(8,128)(2,1)S(1)}, u32[]{:S(2)}, u32[]{:S(2)}) collective-permute-start(bf16[2,4,64,128]{3,2,1,0:T(8,128)(2,1)S(1)} %copy-done.28), channel_id=1, source_target_pairs={{0,15},{1,14},{2,13},{3,12},{4,11},{5,10},{6,9},{7,8},{8,7},{9,6},... | collective-permute-start | bytes 393224 | tf_op jit(solution)/shard_map/ppermute | solution.py:213
  173.1 20.0 %collective-permute-start.31 = (bf16[2,4,64,128]{3,2,1,0:T(8,128)(2,1)S(1)}, bf16[2,4,64,128]{3,2,1,0:T(8,128)(2,1)S(1)}, u32[]{:S(2)}, u32[]{:S(2)}) collective-permute-start(bf16[2,4,64,128]{3,2,1,0:T(8,128)(2,1)S(1)} %copy-done.27), channel_id=1, source_target_pairs={{0,14},{1,15},{2,12},{3,13},{4,10},{5,11},{6,8},{7,9},{8,6},{9,7},... | collective-permute-start | bytes 393224 | tf_op jit(solution)/shard_map/ppermute | solution.py:213
  174.2 25.0 %collective-permute-start.24 = (bf16[2,4,64,128]{3,2,1,0:T(8,128)(2,1)S(1)}, bf16[2,4,64,128]{3,2,1,0:T(8,128)(2,1)S(1)}, u32[]{:S(2)}, u32[]{:S(2)}) collective-permute-start(bf16[2,4,64,128]{3,2,1,0:T(8,128)(2,1)S(1)} %copy-done.26), channel_id=1, source_target_pairs={{0,7},{1,6},{2,5},{3,4},{4,3},{5,2},{6,1},{7,0},{8,15},{9,14},{10,... | collective-permute-start | bytes 393224 | tf_op jit(solution)/shard_map/ppermute | solution.py:213
  187.2 14.2 %collective-permute-start.23 = (bf16[2,4,64,128]{3,2,1,0:T(8,128)(2,1)S(1)}, bf16[2,4,64,128]{3,2,1,0:T(8,128)(2,1)S(1)}, u32[]{:S(2)}, u32[]{:S(2)}) collective-permute-start(bf16[2,4,64,128]{3,2,1,0:T(8,128)(2,1)S(1)} %copy-done.25), channel_id=1, source_target_pairs={{0,6},{1,7},{2,4},{3,5},{4,2},{5,3},{6,0},{7,1},{8,14},{9,15},{10,... | collective-permute-start | bytes 393224 | tf_op jit(solution)/shard_map/ppermute | solution.py:213
  187.2 14.5 %collective-permute-start.22 = (bf16[2,4,64,128]{3,2,1,0:T(8,128)(2,1)S(1)}, bf16[2,4,64,128]{3,2,1,0:T(8,128)(2,1)S(1)}, u32[]{:S(2)}, u32[]{:S(2)}) collective-permute-start(bf16[2,4,64,128]{3,2,1,0:T(8,128)(2,1)S(1)} %copy-done.24), channel_id=1, source_target_pairs={{0,5},{1,4},{2,7},{3,6},{4,1},{5,0},{6,3},{7,2},{8,13},{9,12},{10,... | collective-permute-start | bytes 393224 | tf_op jit(solution)/shard_map/ppermute | solution.py:213
  193.1 9.7 %collective-permute-start.21 = (bf16[2,4,64,128]{3,2,1,0:T(8,128)(2,1)S(1)}, bf16[2,4,64,128]{3,2,1,0:T(8,128)(2,1)S(1)}, u32[]{:S(2)}, u32[]{:S(2)}) collective-permute-start(bf16[2,4,64,128]{3,2,1,0:T(8,128)(2,1)S(1)} %copy-done.23), channel_id=1, source_target_pairs={{0,4},{1,5},{2,6},{3,7},{4,0},{5,1},{6,2},{7,3},{8,12},{9,13},{10,... | collective-permute-start | bytes 393224 | tf_op jit(solution)/shard_map/ppermute | solution.py:213
  198.1 9.2 %collective-permute-start.7 = (bf16[1,256,128]{2,1,0:T(8,128)(2,1)S(1)}, bf16[1,256,128]{2,1,0:T(8,128)(2,1)S(1)}, u32[]{:S(2)}, u32[]{:S(2)}) collective-permute-start(bf16[1,256,128]{2,1,0:T(8,128)(2,1)S(1)} %slice_add_fusion.12), channel_id=1, source_target_pairs={{0,8},{1,9},{2,10},{3,11},{4,12},{5,13},{6,14},{7,15},{8,0},{9,1},... | collective-permute-start | bytes 196616 | tf_op jit(solution)/shard_map/ppermute | solution.py:213
  199.2 10.2 %collective-permute-start.14 = (bf16[64,128]{1,0:T(8,128)(2,1)S(1)}, bf16[64,128]{1,0:T(8,128)(2,1)S(1)}, u32[]{:S(2)}, u32[]{:S(2)}) collective-permute-start(bf16[64,128]{1,0:T(8,128)(2,1)S(1)} %low_rank.1), channel_id=1, source_target_pairs={{0,12},{1,13},{2,14},{3,15},{4,8},{5,9},{6,10},{7,11},{8,4},{9,5},... | collective-permute-start | bytes 49160 | tf_op jit(solution)/shard_map/ppermute | solution.py:213
  201.4 7.9 %collective-permute-start.13 = (bf16[64,128]{1,0:T(8,128)(2,1)S(1)}, bf16[64,128]{1,0:T(8,128)(2,1)S(1)}, u32[]{:S(2)}, u32[]{:S(2)}) collective-permute-start(bf16[64,128]{1,0:T(8,128)(2,1)S(1)} %low_rank.1), channel_id=1, source_target_pairs={{0,8},{1,9},{2,10},{3,11},{4,12},{5,13},{6,14},{7,15},{8,0},{9,1},... | collective-permute-start | bytes 49160 | tf_op jit(solution)/shard_map/ppermute | solution.py:213
  201.7 10.5 %collective-permute-start.12 = (bf16[64,128]{1,0:T(8,128)(2,1)S(1)}, bf16[64,128]{1,0:T(8,128)(2,1)S(1)}, u32[]{:S(2)}, u32[]{:S(2)}) collective-permute-start(bf16[64,128]{1,0:T(8,128)(2,1)S(1)} %low_rank.1), channel_id=1, source_target_pairs={{0,4},{1,5},{2,6},{3,7},{4,0},{5,1},{6,2},{7,3},{8,12},{9,13},{10,... | collective-permute-start | bytes 49160 | tf_op jit(solution)/shard_map/ppermute | solution.py:213
  202.8 9.5 %collective-permute-start.56 = (bf16[4,64,128]{2,1,0:T(8,128)(2,1)S(1)}, bf16[4,64,128]{2,1,0:T(8,128)(2,1)S(1)}, u32[]{:S(2)}, u32[]{:S(2)}) collective-permute-start(bf16[4,64,128]{2,1,0:T(8,128)(2,1)S(1)} %copy-done.48), channel_id=1, source_target_pairs={{0,15},{1,14},{2,13},{3,12},{4,11},{5,10},{6,9},{7,8},{8,7},{9,6},... | collective-permute-start | bytes 196616 | tf_op jit(solution)/shard_map/ppermute | solution.py:213
  209.4 8.0 %collective-permute-start.42 = (bf16[4,64,128]{2,1,0:T(8,128)(2,1)S(1)}, bf16[4,64,128]{2,1,0:T(8,128)(2,1)S(1)}, u32[]{:S(2)}, u32[]{:S(2)}) collective-permute-start(bf16[4,64,128]{2,1,0:T(8,128)(2,1)S(1)} %copy-done.45), channel_id=1, source_target_pairs={{0,7},{1,6},{2,5},{3,4},{4,3},{5,2},{6,1},{7,0},{8,15},{9,14},{10,... | collective-permute-start | bytes 196616 | tf_op jit(solution)/shard_map/ppermute | solution.py:213
  217.9 8.7 %collective-permute-start.39 = (bf16[4,64,128]{2,1,0:T(8,128)(2,1)S(1)}, bf16[4,64,128]{2,1,0:T(8,128)(2,1)S(1)}, u32[]{:S(2)}, u32[]{:S(2)}) collective-permute-start(bf16[4,64,128]{2,1,0:T(8,128)(2,1)S(1)} %copy-done.42), channel_id=1, source_target_pairs={{0,4},{1,5},{2,6},{3,7},{4,0},{5,1},{6,2},{7,3},{8,12},{9,13},{10,... | collective-permute-start | bytes 196616 | tf_op jit(solution)/shard_map/ppermute | solution.py:213
  219.4 8.5 %collective-permute-start.35 = (bf16[4,64,128]{2,1,0:T(8,128)(2,1)S(1)}, bf16[4,64,128]{2,1,0:T(8,128)(2,1)S(1)}, u32[]{:S(2)}, u32[]{:S(2)}) collective-permute-start(bf16[4,64,128]{2,1,0:T(8,128)(2,1)S(1)} %copy-done.41), channel_id=1, source_target_pairs={{0,3},{1,2},{2,1},{3,0},{4,7},{5,6},{6,5},{7,4},{8,11},{9,10},{10,... | collective-permute-start | bytes 196616 | tf_op jit(solution)/shard_map/ppermute | solution.py:213
  220.8 9.3 %collective-permute-start.34 = (bf16[4,64,128]{2,1,0:T(8,128)(2,1)S(1)}, bf16[4,64,128]{2,1,0:T(8,128)(2,1)S(1)}, u32[]{:S(2)}, u32[]{:S(2)}) collective-permute-start(bf16[4,64,128]{2,1,0:T(8,128)(2,1)S(1)} %copy-done.40), channel_id=1, source_target_pairs={{0,2},{1,3},{2,0},{3,1},{4,6},{5,7},{6,4},{7,5},{8,10},{9,11},{10,... | collective-permute-start | bytes 196616 | tf_op jit(solution)/shard_map/ppermute | solution.py:213
  221.7 8.3 %collective-permute-start.33 = (bf16[4,64,128]{2,1,0:T(8,128)(2,1)S(1)}, bf16[4,64,128]{2,1,0:T(8,128)(2,1)S(1)}, u32[]{:S(2)}, u32[]{:S(2)}) collective-permute-start(bf16[4,64,128]{2,1,0:T(8,128)(2,1)S(1)} %copy-done.39), channel_id=1, source_target_pairs={{0,1},{1,0},{2,3},{3,2},{4,5},{5,4},{6,7},{7,6},{8,9},{9,8},{10,11... | collective-permute-start | bytes 196616 | tf_op jit(solution)/shard_map/ppermute | solution.py:213
  224.9 14.8 %collective-permute-start.53 = (bf16[4,64,128]{2,1,0:T(8,128)(2,1)S(1)}, bf16[4,64,128]{2,1,0:T(8,128)(2,1)S(1)}, u32[]{:S(2)}, u32[]{:S(2)}) collective-permute-start(bf16[4,64,128]{2,1,0:T(8,128)(2,1)S(1)} %copy-done.38), channel_id=1, source_target_pairs={{0,10},{1,11},{2,8},{3,9},{4,14},{5,15},{6,12},{7,13},{8,2},{9,3},... | collective-permute-start | bytes 196616 | tf_op jit(solution)/shard_map/ppermute | solution.py:213
  226.6 13.1 %collective-permute-start.50 = (bf16[4,64,128]{2,1,0:T(8,128)(2,1)S(1)}, bf16[4,64,128]{2,1,0:T(8,128)(2,1)S(1)}, u32[]{:S(2)}, u32[]{:S(2)}) collective-permute-start(bf16[4,64,128]{2,1,0:T(8,128)(2,1)S(1)} %copy-done.37), channel_id=1, source_target_pairs={{0,13},{1,12},{2,15},{3,14},{4,9},{5,8},{6,11},{7,10},{8,5},{9,4},... | collective-permute-start | bytes 196616 | tf_op jit(solution)/shard_map/ppermute | solution.py:213
  227.9 13.7 %collective-permute-start.49 = (bf16[4,64,128]{2,1,0:T(8,128)(2,1)S(1)}, bf16[4,64,128]{2,1,0:T(8,128)(2,1)S(1)}, u32[]{:S(2)}, u32[]{:S(2)}) collective-permute-start(bf16[4,64,128]{2,1,0:T(8,128)(2,1)S(1)} %copy-done.36), channel_id=1, source_target_pairs={{0,12},{1,13},{2,14},{3,15},{4,8},{5,9},{6,10},{7,11},{8,4},{9,5},... | collective-permute-start | bytes 196616 | tf_op jit(solution)/shard_map/ppermute | solution.py:213
  230.0 11.6 %collective-permute-start.48 = (bf16[4,64,128]{2,1,0:T(8,128)(2,1)S(1)}, bf16[4,64,128]{2,1,0:T(8,128)(2,1)S(1)}, u32[]{:S(2)}, u32[]{:S(2)}) collective-permute-start(bf16[4,64,128]{2,1,0:T(8,128)(2,1)S(1)} %copy-done.35), channel_id=1, source_target_pairs={{0,9},{1,8},{2,11},{3,10},{4,13},{5,12},{6,15},{7,14},{8,1},{9,0},... | collective-permute-start | bytes 196616 | tf_op jit(solution)/shard_map/ppermute | solution.py:213
  230.1 14.0 %collective-permute-start.47 = (bf16[4,64,128]{2,1,0:T(8,128)(2,1)S(1)}, bf16[4,64,128]{2,1,0:T(8,128)(2,1)S(1)}, u32[]{:S(2)}, u32[]{:S(2)}) collective-permute-start(bf16[4,64,128]{2,1,0:T(8,128)(2,1)S(1)} %copy-done.34), channel_id=1, source_target_pairs={{0,8},{1,9},{2,10},{3,11},{4,12},{5,13},{6,14},{7,15},{8,0},{9,1},... | collective-permute-start | bytes 196616 | tf_op jit(solution)/shard_map/ppermute | solution.py:213
  239.7 8.3 %collective-permute-start.44 = (bf16[4,64,128]{2,1,0:T(8,128)(2,1)S(1)}, bf16[4,64,128]{2,1,0:T(8,128)(2,1)S(1)}, u32[]{:S(2)}, u32[]{:S(2)}) collective-permute-start(bf16[4,64,128]{2,1,0:T(8,128)(2,1)S(1)} %get-tuple-element.158), channel_id=1, source_target_pairs={{0,5},{1,4},{2,7},{3,6},{4,1},{5,0},{6,3},{7,2},{8,13},{9,12},{10,... | collective-permute-start | bytes 196616 | tf_op jit(solution)/shard_map/ppermute | solution.py:213
  241.6 8.1 %collective-permute-start.46 = (bf16[4,64,128]{2,1,0:T(8,128)(2,1)S(1)}, bf16[4,64,128]{2,1,0:T(8,128)(2,1)S(1)}, u32[]{:S(2)}, u32[]{:S(2)}) collective-permute-start(bf16[4,64,128]{2,1,0:T(8,128)(2,1)S(1)} %get-tuple-element.160), channel_id=1, source_target_pairs={{0,7},{1,6},{2,5},{3,4},{4,3},{5,2},{6,1},{7,0},{8,15},{9,14},{10,... | collective-permute-start | bytes 196616 | tf_op jit(solution)/shard_map/ppermute | solution.py:213
  247.5 8.8 %collective-permute-start.37 = (bf16[4,64,128]{2,1,0:T(8,128)(2,1)S(1)}, bf16[4,64,128]{2,1,0:T(8,128)(2,1)S(1)}, u32[]{:S(2)}, u32[]{:S(2)}) collective-permute-start(bf16[4,64,128]{2,1,0:T(8,128)(2,1)S(1)} %get-tuple-element.147), channel_id=1, source_target_pairs={{0,2},{1,3},{2,0},{3,1},{4,6},{5,7},{6,4},{7,5},{8,10},{9,11},{10,... | collective-permute-start | bytes 196616 | tf_op jit(solution)/shard_map/ppermute | solution.py:213
  248.0 10.9 %collective-permute-start.38 = (bf16[4,64,128]{2,1,0:T(8,128)(2,1)S(1)}, bf16[4,64,128]{2,1,0:T(8,128)(2,1)S(1)}, u32[]{:S(2)}, u32[]{:S(2)}) collective-permute-start(bf16[4,64,128]{2,1,0:T(8,128)(2,1)S(1)} %get-tuple-element.148), channel_id=1, source_target_pairs={{0,3},{1,2},{2,1},{3,0},{4,7},{5,6},{6,5},{7,4},{8,11},{9,10},{10,... | collective-permute-start | bytes 196616 | tf_op jit(solution)/shard_map/ppermute | solution.py:213
  249.4 9.5 %collective-permute-start.51 = (bf16[4,64,128]{2,1,0:T(8,128)(2,1)S(1)}, bf16[4,64,128]{2,1,0:T(8,128)(2,1)S(1)}, u32[]{:S(2)}, u32[]{:S(2)}) collective-permute-start(bf16[4,64,128]{2,1,0:T(8,128)(2,1)S(1)} %get-tuple-element.169), channel_id=1, source_target_pairs={{0,8},{1,9},{2,10},{3,11},{4,12},{5,13},{6,14},{7,15},{8,0},{9,1},... | collective-permute-start | bytes 196616 | tf_op jit(solution)/shard_map/ppermute | solution.py:213
  249.7 12.6 %collective-permute-start.52 = (bf16[4,64,128]{2,1,0:T(8,128)(2,1)S(1)}, bf16[4,64,128]{2,1,0:T(8,128)(2,1)S(1)}, u32[]{:S(2)}, u32[]{:S(2)}) collective-permute-start(bf16[4,64,128]{2,1,0:T(8,128)(2,1)S(1)} %get-tuple-element.170), channel_id=1, source_target_pairs={{0,9},{1,8},{2,11},{3,10},{4,13},{5,12},{6,15},{7,14},{8,1},{9,0},... | collective-permute-start | bytes 196616 | tf_op jit(solution)/shard_map/ppermute | solution.py:213
  252.0 12.1 %collective-permute-start.59 = (bf16[4,64,128]{2,1,0:T(8,128)(2,1)S(1)}, bf16[4,64,128]{2,1,0:T(8,128)(2,1)S(1)}, u32[]{:S(2)}, u32[]{:S(2)}) collective-permute-start(bf16[4,64,128]{2,1,0:T(8,128)(2,1)S(1)} %get-tuple-element.181), channel_id=1, source_target_pairs={{0,12},{1,13},{2,14},{3,15},{4,8},{5,9},{6,10},{7,11},{8,4},{9,5},... | collective-permute-start | bytes 196616 | tf_op jit(solution)/shard_map/ppermute | solution.py:213
  256.3 10.6 %collective-permute-start.60 = (bf16[4,64,128]{2,1,0:T(8,128)(2,1)S(1)}, bf16[4,64,128]{2,1,0:T(8,128)(2,1)S(1)}, u32[]{:S(2)}, u32[]{:S(2)}) collective-permute-start(bf16[4,64,128]{2,1,0:T(8,128)(2,1)S(1)} %get-tuple-element.182), channel_id=1, source_target_pairs={{0,13},{1,12},{2,15},{3,14},{4,9},{5,8},{6,11},{7,10},{8,5},{9,4},... | collective-permute-start | bytes 196616 | tf_op jit(solution)/shard_map/ppermute | solution.py:213
  258.9 11.0 %collective-permute-start.57 = (bf16[4,64,128]{2,1,0:T(8,128)(2,1)S(1)}, bf16[4,64,128]{2,1,0:T(8,128)(2,1)S(1)}, u32[]{:S(2)}, u32[]{:S(2)}) collective-permute-start(bf16[4,64,128]{2,1,0:T(8,128)(2,1)S(1)} %get-tuple-element.179), channel_id=1, source_target_pairs={{0,10},{1,11},{2,8},{3,9},{4,14},{5,15},{6,12},{7,13},{8,2},{9,3},... | collective-permute-start | bytes 196616 | tf_op jit(solution)/shard_map/ppermute | solution.py:213
  258.9 13.8 %collective-permute-start.58 = (bf16[4,64,128]{2,1,0:T(8,128)(2,1)S(1)}, bf16[4,64,128]{2,1,0:T(8,128)(2,1)S(1)}, u32[]{:S(2)}, u32[]{:S(2)}) collective-permute-start(bf16[4,64,128]{2,1,0:T(8,128)(2,1)S(1)} %get-tuple-element.180), channel_id=1, source_target_pairs={{0,11},{1,10},{2,9},{3,8},{4,15},{5,14},{6,13},{7,12},{8,3},{9,2},... | collective-permute-start | bytes 196616 | tf_op jit(solution)/shard_map/ppermute | solution.py:213
  262.3 10.4 %collective-permute-start.61 = (bf16[4,64,128]{2,1,0:T(8,128)(2,1)S(1)}, bf16[4,64,128]{2,1,0:T(8,128)(2,1)S(1)}, u32[]{:S(2)}, u32[]{:S(2)}) collective-permute-start(bf16[4,64,128]{2,1,0:T(8,128)(2,1)S(1)} %get-tuple-element.183), channel_id=1, source_target_pairs={{0,14},{1,15},{2,12},{3,13},{4,10},{5,11},{6,8},{7,9},{8,6},{9,7},... | collective-permute-start | bytes 196616 | tf_op jit(solution)/shard_map/ppermute | solution.py:213
  264.1 8.7 %collective-permute-start.62 = (bf16[4,64,128]{2,1,0:T(8,128)(2,1)S(1)}, bf16[4,64,128]{2,1,0:T(8,128)(2,1)S(1)}, u32[]{:S(2)}, u32[]{:S(2)}) collective-permute-start(bf16[4,64,128]{2,1,0:T(8,128)(2,1)S(1)} %get-tuple-element.184), channel_id=1, source_target_pairs={{0,15},{1,14},{2,13},{3,12},{4,11},{5,10},{6,9},{7,8},{8,7},{9,6},... | collective-permute-start | bytes 196616 | tf_op jit(solution)/shard_map/ppermute | solution.py:213
  (64 other events, 782.3 us)

commit v3 on v0

v3 whole, which is shorter than its diff:
```python
import functools
import math

import jax
import jax.numpy as jnp
from jax import lax
from jax.experimental import pallas as pl
from jax.experimental.pallas import tpu as pltpu
from jax.sharding import PartitionSpec as P

LANES = 128
LOW = 4
VMEM = pl.BlockSpec(memory_space=pltpu.VMEM)
SMEM = pl.BlockSpec(memory_space=pltpu.SMEM)
HBM = pl.BlockSpec(memory_space=pltpu.HBM)


def pick_kernel(per_video, pairs, me_ref, row_ref, req_ref, down_ref, up_ref, out_down, out_up, up, sems):
    slots, ranks, _ = down_ref.shape
    videos = out_down.shape[0]
    devs = out_up.shape[0]
    for s in range(videos):
        place = row_ref[req_ref[s]]
        slot = place % slots
        owned = place // slots == me_ref[0]
        copies = [
            pltpu.make_async_copy(down_ref.at[slot], out_down.at[s], sems.at[2 * s]),
            pltpu.make_async_copy(up_ref.at[slot], up.at[s], sems.at[2 * s + 1]),
        ]

        @pl.when(owned)
        def _():
            for copy in copies:
                copy.start()
            for copy in copies:
                copy.wait()

        @pl.when(jnp.logical_not(owned))
        def _():
            out_down[s] = jnp.zeros(out_down.shape[1:], out_down.dtype)
            up[s] = jnp.zeros(up.shape[1:], up.dtype)

    for d in range(devs):
        for p in range(pairs):
            col = ((d % per_video) * pairs + p) * LANES
            out_up[d, p * ranks : (p + 1) * ranks, :] = up[d // per_video, :, col : col + LANES]


def low_rank_kernel(x_ref, down_ref, out_ref):
    parts = [
        lax.dot_general(
            x_ref[s], down_ref[s], (((1,), (1,)), ((), ())), preferred_element_type=jnp.float32
        )
        for s in range(x_ref.shape[0])
    ]
    out_ref[...] = jnp.concatenate(parts, axis=1).astype(out_ref.dtype)


def up_part(up_ref, video, videos, second):
    up = jnp.concatenate([up_ref[...]] * videos, axis=0)
    ranks = up_ref.shape[0]
    row = lax.broadcasted_iota(jnp.int32, up.shape, 0)
    half = (row % ranks) // (ranks // 2)
    keep = (row // ranks == video) & (half == second)
    return jnp.where(keep, up, jnp.zeros_like(up))


def attend_kernel(per_video, block, me_ref, up_ref, q_ref, k_ref, v_ref, *refs):
    low_refs, out_ref, low, q_mix = refs[:LOW], refs[LOW], refs[LOW + 1], refs[LOW + 2]
    devs, toks, width = q_ref.shape
    length = devs * toks
    videos = low.shape[2] // up_ref.shape[0]
    me = me_ref[0]
    for k in range(devs):
        low[me ^ k] = low_refs[k % LOW][k // LOW]
    low_all = low[...].reshape(length, low.shape[2])
    up_q, up_v = (up_part(up_ref, me // per_video, videos, i) for i in range(2))
    keys = k_ref[...].reshape(length, width)
    delta_v = jnp.dot(low_all, up_v, preferred_element_type=jnp.float32)
    vals = (v_ref[...].reshape(length, width).astype(jnp.float32) + delta_v).astype(jnp.bfloat16)
    delta_q = jnp.dot(low_all, up_q, preferred_element_type=jnp.float32)
    q_mix[...] = (q_ref[...].reshape(length, width).astype(jnp.float32) + delta_q).astype(
        jnp.bfloat16
    )
    scale = math.log2(math.e) / math.sqrt(width)
    for b in range(0, devs, block):
        q = q_mix[b * toks : (b + block) * toks, :]
        scores = lax.dot_general(
            q, keys, (((1,), (1,)), ((), ())), preferred_element_type=jnp.float32
        )
        top = jnp.max(scores, axis=1, keepdims=True)
        weights = jnp.exp2((scores - top) * scale)
        total = jnp.sum(weights, axis=1, keepdims=True)
        mixed = jnp.dot(weights.astype(jnp.bfloat16), vals, preferred_element_type=jnp.float32)
        out_ref[b : b + block] = (mixed / total).astype(jnp.bfloat16).reshape(block, toks, width)


def body(
    normed_token_features,
    queries,
    projected_keys,
    values,
    adapter_down_factors,
    adapter_up_factors,
    adapter_store_row,
    requests,
):
    videos, toks, model_width = normed_token_features.shape
    heads = queries.shape[1]
    width = queries.shape[3]
    _, ranks, up_width = adapter_up_factors.shape
    devs = lax.axis_size("seq")
    me = lax.axis_index("seq").astype(jnp.int32)[None]
    pairs = videos * heads // devs
    per_video = devs // videos
    length = devs * toks

    def swap(tensor, k):
        return lax.ppermute(tensor, "seq", [(i, i ^ k) for i in range(devs)])

    def exchange(tensor):
        blocks = tensor.reshape(devs, pairs, toks, width)
        return lax.all_to_all(blocks, "seq", split_axis=0, concat_axis=0, tiled=True)

    down_part, up_parts = pl.pallas_call(
        functools.partial(pick_kernel, per_video, pairs),
        in_specs=[SMEM, SMEM, SMEM, HBM, HBM],
        out_specs=[VMEM, VMEM],
        out_shape=[
            jax.ShapeDtypeStruct((videos, ranks, model_width), jnp.bfloat16),
            jax.ShapeDtypeStruct((devs, pairs * ranks, LANES), jnp.bfloat16),
        ],
        scratch_shapes=[
            pltpu.VMEM((videos, ranks, up_width), jnp.bfloat16),
            pltpu.SemaphoreType.DMA((2 * videos,)),
        ],
        compiler_params=pltpu.CompilerParams(vmem_limit_bytes=24 << 20),
        cost_estimate=pl.CostEstimate(
            flops=0,
            bytes_accessed=4 * videos * ranks * (model_width + up_width),
            transcendentals=0,
        ),
        name="pick_factors",
    )(me, adapter_store_row, requests, adapter_down_factors, adapter_up_factors)
    down = lax.psum(down_part, "seq")
    up_here = lax.psum_scatter(up_parts, "seq", scatter_dimension=0, tiled=True)
    up_here = up_here.reshape(pairs, ranks, LANES)

    keys, vals, query = (exchange(t) for t in (projected_keys, values, queries))

    low = pl.pallas_call(
        low_rank_kernel,
        in_specs=[VMEM, VMEM],
        out_specs=VMEM,
        out_shape=jax.ShapeDtypeStruct((toks, videos * ranks), jnp.bfloat16),
        compiler_params=pltpu.CompilerParams(vmem_limit_bytes=24 << 20),
        cost_estimate=pl.CostEstimate(
            flops=2 * videos * toks * ranks * model_width,
            bytes_accessed=2 * videos * (toks + ranks) * model_width,
            transcendentals=0,
        ),
        name="low_rank",
    )(normed_token_features, down)
    far = jnp.stack([low] + [swap(low, LOW * i) for i in range(1, devs // LOW)])
    lows = [far] + [swap(far, i) for i in range(1, LOW)]

    low_spec = pl.BlockSpec((devs // LOW, toks, videos * ranks), lambda p: (0, 0, 0))
    part_spec = pl.BlockSpec((devs, pl.squeezed, toks, width), lambda p: (0, p, 0, 0))
    mixed = pl.pallas_call(
        functools.partial(attend_kernel, per_video, math.gcd(devs, max(1, 512 // toks))),
        grid=(pairs,),
        in_specs=[SMEM, pl.BlockSpec((pl.squeezed, ranks, LANES), lambda p: (p, 0, 0))]
        + [part_spec] * 3
        + [low_spec] * LOW,
        out_specs=part_spec,
        out_shape=jax.ShapeDtypeStruct((devs, pairs, toks, width), jnp.bfloat16),
        scratch_shapes=[
            pltpu.VMEM((devs, toks, videos * ranks), jnp.bfloat16),
            pltpu.VMEM((length, width), jnp.bfloat16),
        ],
        compiler_params=pltpu.CompilerParams(vmem_limit_bytes=48 << 20),
        cost_estimate=pl.CostEstimate(
            flops=4 * pairs * length * length * width,
            bytes_accessed=8 * pairs * length * width,
            transcendentals=pairs * length * length,
        ),
        name="attend",
    )(me, up_here, query, keys, vals, *lows)
    return exchange(mixed).reshape(videos, heads, toks, width)


def solution(mesh):
    in_specs = (
        P("grp", "seq", None),
        P("grp", None, "seq", None),
        P("grp", None, "seq", None),
        P("grp", None, "seq", None),
        P("seq", None, None),
        P("seq", None, None),
        P(),
        P("grp"),
    )
    out_specs = P("grp", None, "seq", None)
    return jax.shard_map(body, mesh=mesh, in_specs=in_specs, out_specs=out_specs, check_vma=False)
```

time: 314 us -> 266 us (0.85)
  local copies, waits for them, and re-layouts: 68.5 us -> 5.79 us
  waiting for transfers between devices: 87.9 us -> 146 us
  blocking collectives: 93.3 us -> 64.1 us
  other arithmetic: 21.8 us -> 0.01 us
  Pallas kernels: 0 us -> 12.4 us
  matrix products: 10.8 us -> 0 us
  starting transfers between devices: 14.7 us -> 23.9 us
    psum x0 -> x1, waiting for transfers between devices: none -> 76.6 us  [body(): down = lax.psum(down_part, 'seq')]
    all_gather x1 -> x0, waiting for transfers between devices: 47.2 us -> none  [body(): factors = lax.all_gather(shares, 'seq', axis=1, tiled=True)]
    reduce_scatter x0 -> x1, waiting for transfers between devices: none -> 41.9 us  [body(): up_here = lax.psum_scatter(up_parts, 'seq', scatter_dimension=0, tiled=True)]
    gather x7 -> x0, local copies, waits for them, and re-layouts: 36.8 us -> none  [the longest x6 35.5 us: body(): picked = jnp.take(flat_store, local_slot, axis=0)]
    all_to_all x2, blocking collectives: 93.3 us -> 64.1 us  [exchange(): lax.all_to_all(blocks, 'seq', split_axis=0, concat_axis=0, tiled=True)]
    all_to_all x3 -> x2, waiting for transfers between devices: 40.6 us -> 20.7 us  [exchange(): lax.all_to_all(blocks, 'seq', split_axis=0, concat_axis=0, tiled=True)]
    pallas_call x0 -> x3, Pallas kernels: none -> 12.4 us  [the longest x1 9.91 us: body(): pl.pallas_call(functools.partial(attend_kernel, per_video, math.gcd(devs,...]
    dot_general x19 -> x0, matrix products: 10.8 us -> none  [the longest x8 5.26 us: attend_rows(): jnp.dot(weights, values_all, preferred_element_type=jnp.float32)]
  transfers between devices with their start and end apart: 4 -> 10, of which waited for: 3 -> 7; matrix products, arithmetic and copies ran while one was open for 3% -> 0% of each run, Pallas kernels for 0% -> 1%
where the time goes in v3:
time: 266 us; the launch traced here: 265 us
  waiting for transfers between devices  146 us (55%)
  blocking collectives  64.1 us (24%)
  starting transfers between devices  23.9 us (9%)
  between operations  13.5 us (5%)
  Pallas kernels  12.4 us (5%)
  local copies, waits for them, and re-layouts  5.79 us (2%)
    psum x1, waiting for transfers between devices, body(): down = lax.psum(down_part, 'seq')  76.6 us
    all_to_all x2, blocking collectives, exchange(): lax.all_to_all(blocks, 'seq', split_axis=0, concat_axis=0, tiled=True)  64.1 us
    reduce_scatter x1, waiting for transfers between devices, body(): up_here = lax.psum_scatter(up_parts, 'seq', scatter_dimension=0, tiled=True)  41.9 us
    all_to_all x2, waiting for transfers between devices, exchange(): lax.all_to_all(blocks, 'seq', split_axis=0, concat_axis=0, tiled=True)  20.7 us
    all_to_all x2, starting transfers between devices, exchange(): lax.all_to_all(blocks, 'seq', split_axis=0, concat_axis=0, tiled=True)  14.3 us
    pallas_call x1, Pallas kernels, body(): pl.pallas_call(functools.partial(attend_kernel, per_video, math.gcd(devs,...  9.91 us
    ppermute x6, starting transfers between devices, swap(): return lax.ppermute(tensor, 'seq', [(i, i ^ k) for i in range(devs)])  9.51 us
    ppermute x6, waiting for transfers between devices, swap(): return lax.ppermute(tensor, 'seq', [(i, i ^ k) for i in range(devs)])  5.81 us
  transfers between devices with their start and end apart: 10, of which 7 were waited for; matrix products, arithmetic and copies ran while one was open for 0% of the time, Pallas kernels for 1%

profile of v3, /device:TPU:1, one launch (start us, length us, event | category | flops | bytes accessed | tf_op | source)
XLA Modules:
  0.0 265.4 jit_solution(8159864977917695471)
XLA Ops:
  6.5 0.0 copy-start
  6.5 32.9 %all_to_all.20.q_ref = bf16[16,4,64,128]{3,2,1,0:T(8,128)(2,1)} all-to-all(bf16[16,4,64,128]{3,2,1,0:T(8,128)(2,1)} %bitcast.13), channel_id=1, replica_groups=mesh['grp'=2,'seq'=16] {'seq'}, dimensions={0} | all-to-all | bytes 2097152 | tf_op jit(solution)/shard_map/all_to_all | solution.py:123
  39.5 0.0 copy-start.6
  39.5 0.0 copy-start.7
  39.5 4.8 %all-to-all-start.1 = ((bf16[16,4,64,128]{3,2,1,0:T(8,128)(2,1)}), bf16[16,4,64,128]{3,2,1,0:T(8,128)(2,1)}, u32[]{:S(2)}, u32[]{:S(2)}) async-start(bf16[16,4,64,128]{3,2,1,0:T(8,128)(2,1)} %bitcast.14), calls=%async_computation.2 | async-start | bytes 2097152 | tf_op jit(solution)/shard_map/all_to_all | solution.py:123
  44.2 0.0 all-reduce.2.cloned.1.call-start
  44.3 0.0 copy-done
  44.3 0.0 copy-done.6
  44.3 0.0 copy-done.7
  44.3 0.0 copy-start.1
  44.3 1.6 copy-done.1
  45.9 1.9 pick_factors.1
  47.8 0.0 copy-start.4
  47.8 1.1 copy-done.4
  48.9 0.0 all-reduce.2.cloned.1.call-update
  48.9 20.7 %all-to-all-done.1.k_ref = bf16[16,4,64,128]{3,2,1,0:T(8,128)(2,1)} async-done(((bf16[16,4,64,128]{3,2,1,0:T(8,128)(2,1)}), bf16[16,4,64,128]{3,2,1,0:T(8,128)(2,1)}, u32[]{:S(2)}, u32[]{:S(2)}) %all-to-all-start.1) | async-done | bytes 1048608 | tf_op jit(solution)/shard_map/all_to_all | solution.py:123
  69.6 0.0 copy-start.2
  69.7 9.5 %all-to-all-start.2 = ((bf16[16,4,64,128]{3,2,1,0:T(8,128)(2,1)}), bf16[16,4,64,128]{3,2,1,0:T(8,128)(2,1)S(1)}, u32[]{:S(2)}, u32[]{:S(2)}) async-start(bf16[16,4,64,128]{3,2,1,0:T(8,128)(2,1)} %bitcast.4), calls=%async_computation.3 | async-start | bytes 2097152 | tf_op jit(solution)/shard_map/all_to_all | solution.py:123
  79.2 0.0 reduce-scatter.2.cloned.1.call-start
  79.2 0.7 reduce-scatter.2.cloned.1.call-update
  79.9 76.6 %all-reduce.2.cloned.1.call-done.down_ref = bf16[2,64,5120]{2,1,0:T(8,128)(2,1)} async-done(((bf16[2,64,5120]{2,1,0:T(8,128)(2,1)}), bf16[2,64,5120]{2,1,0:T(8,128)(2,1)}) %all-reduce.2.cloned.1.call-update) | async-done | bytes 1310736 | tf_op jit(solution)/shard_map/psum | solution.py:145
  156.5 0.0 copy-done.2
  156.5 0.0 copy-start.3
  156.5 1.3 copy-done.3
  157.8 0.0 copy-start.5
  157.8 0.6 low_rank.1
  158.4 0.2 collective-permute-start
  158.6 1.3 collective-permute-start.1
  159.9 2.1 collective-permute-start.2
  162.0 0.0 collective-permute-done
  162.0 0.1 collective-permute-done.1
  162.1 2.2 collective-permute-done.2
  164.3 4.2 %collective-permute-start.3 = (bf16[4,64,128]{2,1,0:T(8,128)(2,1)S(1)}, bf16[4,64,128]{2,1,0:T(8,128)(2,1)S(1)}, u32[]{:S(2)}, u32[]{:S(2)}) collective-permute-start(bf16[4,64,128]{2,1,0:T(8,128)(2,1)S(1)} %pad_maximum_fusion.refs_0_), channel_id=1, source_target_pairs={{0,1},{1,0},{2,3},{3,2},{4,5},{5,4},{6,7},{7,6},{8,9},{9,8},{10,11... | collective-permute-start | bytes 196616 | tf_op jit(solution)/shard_map/ppermute | solution.py:119
  168.5 0.3 collective-permute-start.4
  168.8 1.4 collective-permute-start.5
  170.2 0.0 collective-permute-done.3.refs_1_
  170.2 2.0 collective-permute-done.4.refs_2_
  172.2 1.6 collective-permute-done.5.refs_3_
  173.7 41.9 %reduce-scatter.2.cloned.1.call-done = bf16[1,256,128]{2,1,0:T(8,128)(2,1)} async-done(((bf16[16,256,128]{2,1,0:T(8,128)(2,1)}), bf16[1,256,128]{2,1,0:T(8,128)(2,1)}) %reduce-scatter.2.cloned.1.call-update) | async-done | bytes 65552 | tf_op jit(solution)/shard_map/reduce_scatter | solution.py:146
  215.6 0.0 all-to-all-done.2.v_ref
  215.6 0.0 copy-done.5
  215.6 0.0 copy-start.8
  215.6 0.8 copy-done.8
  216.5 9.9 %attend.1 = bf16[16,4,64,128]{3,2,1,0:T(8,128)(2,1)S(1)} custom-call(s32[1]{0:T(128)} %bitcast.me_ref, bf16[4,64,128]{2,1,0:T(8,128)(2,1)S(1)} %bitcast.11, bf16[16,4,64,128]{3,2,1,0:T(8,128)(2,1)S(1)} %copy-done.5, bf16[16,4,64,128]{3,2,1,0:T(8,128)(2,1)} %all-to-all-done.1.k_ref, bf16[16,4,64,128]{3,2,1,0:T(8,128)(2,1)S(1)} %all-to-all-done.2.v_ref, ...), custom_call_target="tpu_custom_call" | custom-call | flops 2147483648 | bytes 4194304 | tf_op jit(solution)/shard_map/attend/pallas_call | solution.py:169
  226.4 31.1 %all_to_all.21 = bf16[16,4,64,128]{3,2,1,0:T(8,128)(2,1)S(1)} all-to-all(bf16[16,4,64,128]{3,2,1,0:T(8,128)(2,1)S(1)} %attend.1), channel_id=1, replica_groups=mesh['grp'=2,'seq'=16] {'seq'}, dimensions={0} | all-to-all | bytes 2097152 | tf_op jit(solution)/shard_map/all_to_all | solution.py:123
  257.5 1.0 copy.11
  (1 shorter events, 0.0 us)
Async XLA Ops:
  6.5 37.7 %copy-start = (bf16[4,64,5120]{2,1,0:T(8,128)(2,1)S(1)}, bf16[4,64,5120]{2,1,0:T(8,128)(2,1)}, u32[]{:S(2)}) copy-start(bf16[4,64,5120]{2,1,0:T(8,128)(2,1)} %down_ref.1) | copy-start | bytes 7864324
  39.5 4.8 %copy-start.6 = (s32[64]{0:T(128)S(1)}, s32[64]{0:T(128)}, u32[]{:S(2)}) copy-start(s32[64]{0:T(128)} %row_ref.1) | copy-start | bytes 772
  39.5 4.8 %copy-start.7 = (s32[2]{0:T(128)S(1)}, s32[2]{0:T(128)}, u32[]{:S(2)}) copy-start(s32[2]{0:T(128)} %req_ref.1) | copy-start | bytes 28
  39.5 30.2 %all-to-all-start.1 = ((bf16[16,4,64,128]{3,2,1,0:T(8,128)(2,1)}), bf16[16,4,64,128]{3,2,1,0:T(8,128)(2,1)}, u32[]{:S(2)}, u32[]{:S(2)}) async-start(bf16[16,4,64,128]{3,2,1,0:T(8,128)(2,1)} %bitcast.14), calls=%async_computation.2 | async-start | bytes 2097152 | tf_op jit(solution)/shard_map/all_to_all | solution.py:123
  44.2 112.3 %all-reduce.2.cloned.1.call-start = ((), (), s32[]{:S(2)}) async-start(), calls=%async_computation.6 | async-start | bytes 2621440 | tf_op jit(solution)/shard_map/psum | solution.py:145
  44.3 1.6 copy-start.1
  47.8 1.1 copy-start.4
  69.6 86.9 %copy-start.2 = (bf16[2,64,5120]{2,1,0:T(8,128)(2,1)S(1)}, bf16[2,64,5120]{2,1,0:T(8,128)(2,1)}, u32[]{:S(2)}) copy-start(bf16[2,64,5120]{2,1,0:T(8,128)(2,1)} %x_ref.1) | copy-start | bytes 3932164
  69.7 146.0 %all-to-all-start.2 = ((bf16[16,4,64,128]{3,2,1,0:T(8,128)(2,1)}), bf16[16,4,64,128]{3,2,1,0:T(8,128)(2,1)S(1)}, u32[]{:S(2)}, u32[]{:S(2)}) async-start(bf16[16,4,64,128]{3,2,1,0:T(8,128)(2,1)} %bitcast.4), calls=%async_computation.3 | async-start | bytes 2097152 | tf_op jit(solution)/shard_map/all_to_all | solution.py:123
  79.2 136.5 %reduce-scatter.2.cloned.1.call-start = ((), (), s32[]{:S(2)}) async-start(), calls=%async_computation.5 | async-start | bytes 1114112 | tf_op jit(solution)/shard_map/reduce_scatter | solution.py:146
  156.5 1.3 copy-start.3
  157.8 57.8 %copy-start.5 = (bf16[16,4,64,128]{3,2,1,0:T(8,128)(2,1)S(1)}, bf16[16,4,64,128]{3,2,1,0:T(8,128)(2,1)}, u32[]{:S(2)}) copy-start(bf16[16,4,64,128]{3,2,1,0:T(8,128)(2,1)} %all_to_all.20.q_ref) | copy-start | bytes 3145732
  158.4 3.6 %collective-permute-start = (bf16[64,128]{1,0:T(8,128)(2,1)S(1)}, bf16[64,128]{1,0:T(8,128)(2,1)S(1)}, u32[]{:S(2)}, u32[]{:S(2)}) collective-permute-start(bf16[64,128]{1,0:T(8,128)(2,1)S(1)} %low_rank.1), channel_id=1, source_target_pairs={{0,4},{1,5},{2,6},{3,7},{4,0},{5,1},{6,2},{7,3},{8,12},{9,13},{10,... | collective-permute-start | bytes 49160 | tf_op jit(solution)/shard_map/ppermute | solution.py:119
  158.6 3.5 %collective-permute-start.1 = (bf16[64,128]{1,0:T(8,128)(2,1)S(1)}, bf16[64,128]{1,0:T(8,128)(2,1)S(1)}, u32[]{:S(2)}, u32[]{:S(2)}) collective-permute-start(bf16[64,128]{1,0:T(8,128)(2,1)S(1)} %low_rank.1), channel_id=1, source_target_pairs={{0,8},{1,9},{2,10},{3,11},{4,12},{5,13},{6,14},{7,15},{8,0},{9,1},... | collective-permute-start | bytes 49160 | tf_op jit(solution)/shard_map/ppermute | solution.py:119
  159.9 4.4 %collective-permute-start.2 = (bf16[64,128]{1,0:T(8,128)(2,1)S(1)}, bf16[64,128]{1,0:T(8,128)(2,1)S(1)}, u32[]{:S(2)}, u32[]{:S(2)}) collective-permute-start(bf16[64,128]{1,0:T(8,128)(2,1)S(1)} %low_rank.1), channel_id=1, source_target_pairs={{0,12},{1,13},{2,14},{3,15},{4,8},{5,9},{6,10},{7,11},{8,4},{9,5},... | collective-permute-start | bytes 49160 | tf_op jit(solution)/shard_map/ppermute | solution.py:119
  164.3 5.9 %collective-permute-start.3 = (bf16[4,64,128]{2,1,0:T(8,128)(2,1)S(1)}, bf16[4,64,128]{2,1,0:T(8,128)(2,1)S(1)}, u32[]{:S(2)}, u32[]{:S(2)}) collective-permute-start(bf16[4,64,128]{2,1,0:T(8,128)(2,1)S(1)} %pad_maximum_fusion.refs_0_), channel_id=1, source_target_pairs={{0,1},{1,0},{2,3},{3,2},{4,5},{5,4},{6,7},{7,6},{8,9},{9,8},{10,11... | collective-permute-start | bytes 196616 | tf_op jit(solution)/shard_map/ppermute | solution.py:119
  168.5 3.7 %collective-permute-start.4 = (bf16[4,64,128]{2,1,0:T(8,128)(2,1)S(1)}, bf16[4,64,128]{2,1,0:T(8,128)(2,1)S(1)}, u32[]{:S(2)}, u32[]{:S(2)}) collective-permute-start(bf16[4,64,128]{2,1,0:T(8,128)(2,1)S(1)} %pad_maximum_fusion.refs_0_), channel_id=1, source_target_pairs={{0,2},{1,3},{2,0},{3,1},{4,6},{5,7},{6,4},{7,5},{8,10},{9,11},{10,... | collective-permute-start | bytes 196616 | tf_op jit(solution)/shard_map/ppermute | solution.py:119
  168.8 4.9 %collective-permute-start.5 = (bf16[4,64,128]{2,1,0:T(8,128)(2,1)S(1)}, bf16[4,64,128]{2,1,0:T(8,128)(2,1)S(1)}, u32[]{:S(2)}, u32[]{:S(2)}) collective-permute-start(bf16[4,64,128]{2,1,0:T(8,128)(2,1)S(1)} %pad_maximum_fusion.refs_0_), channel_id=1, source_target_pairs={{0,3},{1,2},{2,1},{3,0},{4,7},{5,6},{6,5},{7,4},{8,11},{9,10},{10,... | collective-permute-start | bytes 196616 | tf_op jit(solution)/shard_map/ppermute | solution.py:119
  215.6 0.8 copy-start.8
Sparse Core Ops, SparseCore 0:
  49.0 107.4 all-reduce.1
  160.1 55.4 reduce-scatter.1

commit v4 on v2

--- a/solution.py
+++ b/solution.py
@@ -28,10 +28,6 @@
     return out
 
 
-def after(arrays, *others):
-    return lax.optimization_barrier((tuple(arrays), others))[0]
-
-
 def run_copies(copies):
     for copy in copies:
         copy.start()
@@ -39,30 +35,21 @@
         copy.wait()
 
 
-def pack_kernel(devs, pairs, me_ref, q_ref, k_ref, v_ref, *refs):
-    outs, sems = refs[:-1], refs[-1]
-    copies = []
+def pack_kernel(devs, pairs, late, me_ref, k_ref, v_ref, q_ref, *outs):
     for k in range(devs):
-        first = (me_ref[0] ^ k) * pairs
-        for i, (src, dst) in enumerate(
-            ((k_ref, outs[k].at[0]), (v_ref, outs[k].at[1]), (q_ref, outs[devs + k]))
-        ):
-            copies.append(
-                pltpu.make_async_copy(src.at[pl.ds(first, pairs)], dst, sems.at[3 * k + i])
-            )
-    run_copies(copies)
+        here = pl.ds((me_ref[0] ^ k) * pairs, pairs)
+        outs[k][0] = k_ref[here]
+        outs[k][1] = v_ref[here]
+        if k in late:
+            outs[devs + late.index(k)][0] = q_ref[here]
+        else:
+            outs[k][2] = q_ref[here]
 
 
 def unpack_kernel(devs, pairs, me_ref, *refs):
-    ins, out, sems = refs[:devs], refs[devs], refs[devs + 1]
-    run_copies(
-        [
-            pltpu.make_async_copy(
-                ins[k], out.at[pl.ds((me_ref[0] ^ k) * pairs, pairs)], sems.at[k]
-            )
-            for k in range(devs)
-        ]
-    )
+    ins, out = refs[:devs], refs[devs]
+    for k in range(devs):
+        out[pl.ds((me_ref[0] ^ k) * pairs, pairs)] = ins[k][...]
 
 
 def pick_kernel(
@@ -212,29 +199,39 @@
     def swap(tensor, k):
         return lax.ppermute(tensor, "seq", [(i, i ^ k) for i in everyone])
 
-    def halve(pieces, gate=None):
-        got = []
-        for i in range(bits):
-            h = devs >> (i + 1)
-            send = sum((r[h : 2 * h] for r in got), pieces[i])
-            if gate is not None:
-                (send,) = after((send,), gate[i])
-            got.append(swap(send, 1 << i))
-        return sum((r[:1] for r in got), pieces[bits]), got
-
-    sizes = [(2, pairs, toks, width)] * devs + [(pairs, toks, width)] * devs
+    def after(array, *others):
+        return lax.optimization_barrier((array, others))[0]
+
+    top = devs >> 1
+    plain = [k for k in everyone if k & top and not k & 2]
+    crossed = [k for k in everyone if k & top and k & 2]
+    near = [k for k in range(1, top) if k < LOW]
+    side = [k for k in range(1, top) if k >= LOW]
+    ahead = plain[: 3 * len(plain) // 4]
+    behind = plain[3 * len(plain) // 4 :]
+
+    sizes = [(2 if k in crossed else 3, pairs, toks, width) for k in everyone]
+    sizes += [(1, pairs, toks, width) for k in crossed]
     packed = pl.pallas_call(
-        functools.partial(pack_kernel, devs, pairs),
-        in_specs=[SMEM, ANY, ANY, ANY],
-        out_specs=[ANY] * (2 * devs),
+        functools.partial(pack_kernel, devs, pairs, crossed),
+        in_specs=[SMEM, VMEM, VMEM, VMEM],
+        out_specs=[VMEM] * len(sizes),
         out_shape=[jax.ShapeDtypeStruct(s, jnp.bfloat16) for s in sizes],
-        scratch_shapes=[pltpu.SemaphoreType.DMA((3 * devs,))],
+        compiler_params=pltpu.CompilerParams(vmem_limit_bytes=40 << 20),
         cost_estimate=pl.CostEstimate(
             flops=0, bytes_accessed=12 * pairs * length * width, transcendentals=0
         ),
         name="pack",
-    )(me, *(t.reshape(-1, toks, width) for t in (queries, projected_keys, values)))
-    kv, q = list(packed[:devs]), list(packed[devs:])
+    )(me, *(t.reshape(-1, toks, width) for t in (projected_keys, values, queries)))
+    blocks = list(packed[:devs])
+    late = dict(zip(crossed, packed[devs:]))
+
+    def send(ks, *others):
+        for k in ks:
+            blocks[k] = swap(after(blocks[k], *others) if others else blocks[k], k)
+
+    def got(ks):
+        return [blocks[k] for k in ks]
 
     steps = [devs >> (i + 1) for i in range(bits)] + [1]
     piece_shapes = [(h, tiles * rows, LANES) for h in steps] + [
@@ -257,13 +254,40 @@
             transcendentals=0,
         ),
         name="pick_factors",
-    )(me, adapter_store_row, requests, adapter_down_factors, adapter_up_factors)
-
-    shard, halved = halve(pieces[: bits + 1])
-    gathered = [shard]
-    for bit in reversed(range(bits)):
-        gathered.append(jnp.concatenate([gathered[-1], swap(gathered[-1], 1 << bit)], axis=0))
-    up_here = halve(pieces[bits + 1 :], halved)[0].reshape(pairs, ranks, LANES)
+    )(after(me, blocks[top]), adapter_store_row, requests, adapter_down_factors, adapter_up_factors)
+    down_pieces, up_pieces = pieces[: bits + 1], pieces[bits + 1 :]
+
+    def halving(parts, received, i):
+        h = devs >> (i + 1) if i < bits else 0
+        size = max(h, 1)
+        return sum((r[h : h + size] for r in received), parts[i])
+
+    send(ahead)
+    down_got, up_got = [], []
+    for i in range(bits):
+        piece = halving(down_pieces, down_got, i)
+        if i == min(2, bits - 1):
+            piece = after(piece, *got(ahead[:-1]))
+            send(near, down_got[-1])
+        if i == bits - 1:
+            piece = after(piece, *got(ahead))
+        down_got.append(swap(piece, 1 << i))
+    gathered = halving(down_pieces, down_got, bits)
+    for i in range(2):
+        piece = after(halving(up_pieces, up_got, i), down_got[min(i + 1, bits - 1)])
+        up_got.append(swap(piece, 1 << i))
+    gathered = after(gathered, *got(near), *up_got)
+    for i in reversed(range(bits)):
+        if i == bits - 2:
+            send(behind, gathered)
+        if i == 1:
+            send(crossed[: len(crossed) // 2], gathered)
+        if i == 0:
+            gathered = after(gathered, *got(behind))
+            send(crossed[len(crossed) // 2 :], gathered)
+            send(side[: len(side) // 2], gathered)
+        gathered = jnp.concatenate([gathered, swap(gathered, 1 << i)], axis=0)
+    gathered = after(gathered, *got(crossed[: len(crossed) // 2]))
 
     low = pl.pallas_call(
         functools.partial(low_rank_kernel, shape),
@@ -278,25 +302,16 @@
             transcendentals=0,
         ),
         name="low_rank",
-    )(me, normed_token_features, gathered[-1])
+    )(me, normed_token_features, gathered)
+    send(side[len(side) // 2 :], low)
     far = jnp.stack([low] + [swap(low, LOW * i) for i in range(1, devs // LOW)])
+    for i in range(2, bits):
+        piece = after(halving(up_pieces, up_got, i), low)
+        up_got.append(swap(piece, 1 << i))
+    up_here = halving(up_pieces, up_got, bits).reshape(pairs, ranks, LANES)
+    far = after(far, *got(crossed[len(crossed) // 2 :]))
+    late = {k: swap(after(late[k], far), k) for k in crossed}
     lows = [far] + [swap(far, i) for i in range(1, LOW)]
-
-    top = devs >> 1
-    early = [k for k in everyone if k & top and not k & 2]
-    middle = [k for k in everyone if k & top and k & 2]
-    near = [k for k in range(1, top)]
-    gates = {k: None for k in early}
-    for i, k in enumerate(middle):
-        gates[k] = shard if 2 * i < len(middle) else gathered[min(2, bits)]
-    for k in near:
-        gates[k] = halved[min(1, bits - 1)] if k < LOW else gathered[min(2, bits)]
-    for k in everyone[1:]:
-        if gates[k] is not None:
-            (kv[k],) = after((kv[k],), gates[k])
-        (q[k],) = after((q[k],), gathered[-1] if k & top else low)
-    kv_here = [kv[0]] + [swap(kv[k], k) for k in everyone[1:]]
-    q_here = [q[0]] + [swap(q[k], k) for k in everyone[1:]]
 
     low_specs = [pl.BlockSpec((devs // LOW, toks, videos * ranks), lambda p: (0, 0, 0))] * LOW
     up_spec = pl.BlockSpec((pl.squeezed, ranks, LANES), lambda p: (p, 0, 0))
@@ -316,7 +331,11 @@
             transcendentals=0,
         ),
         name="prepare",
-    )(me, up_here, *lows, *kv_here)
+    )(me, up_here, *lows, *blocks)
+
+    def query_spec(k):
+        first = 0 if k in late else 2
+        return pl.BlockSpec((pl.squeezed, pl.squeezed, toks, width), lambda p: (first, p, 0, 0))
 
     def attend(ks):
         count = len(ks)
@@ -325,7 +344,7 @@
                 attend_kernel, ks, math.gcd(count, max(1, 256 // toks)), per_video
             ),
             grid=(pairs,),
-            in_specs=[SMEM, up_spec, all_spec, all_spec, *low_specs] + [part_spec] * count,
+            in_specs=[SMEM, up_spec, all_spec, all_spec, *low_specs] + [query_spec(k) for k in ks],
             out_specs=[part_spec] * count,
             out_shape=[jax.ShapeDtypeStruct((pairs, toks, width), jnp.bfloat16)] * count,
             compiler_params=pltpu.CompilerParams(vmem_limit_bytes=40 << 20),
@@ -335,20 +354,19 @@
                 transcendentals=pairs * count * toks * length,
             ),
             name="attend",
-        )(me, up_here, keys, vals, *lows, *(q_here[k] for k in ks))
+        )(me, up_here, keys, vals, *lows, *(late.get(k, blocks[k]) for k in ks))
 
     back = [None] * devs
-    half = top // 2
-    for ks in (early, middle, near[half - 1 :], [0] + near[: half - 1]):
+    for ks in (plain, crossed, side, [0] + near):
         for k, out in zip(ks, attend(ks)):
             back[k] = swap(out, k) if k else out
 
     out = pl.pallas_call(
         functools.partial(unpack_kernel, devs, pairs),
-        in_specs=[SMEM] + [ANY] * devs,
-        out_specs=ANY,
+        in_specs=[SMEM] + [VMEM] * devs,
+        out_specs=VMEM,
         out_shape=jax.ShapeDtypeStruct((devs * pairs, toks, width), jnp.bfloat16),
-        scratch_shapes=[pltpu.SemaphoreType.DMA((devs,))],
+        compiler_params=pltpu.CompilerParams(vmem_limit_bytes=24 << 20),
         cost_estimate=pl.CostEstimate(
             flops=0, bytes_accessed=4 * pairs * length * width, transcendentals=0
         ),

time: 308 us -> 190 us (0.62)
  Pallas kernels: 146 us -> 17.5 us
  waiting for transfers between devices: 42.7 us -> 94.5 us
  starting transfers between devices: 108 us -> 69 us
    pallas_call x1, Pallas kernels: 96.8 us -> 0.2 us  [body(): pl.pallas_call(functools.partial(pack_kernel, devs, pairs, crossed), in_s...]
    ppermute x63 -> x52, waiting for transfers between devices: 42.7 us -> 94.5 us  [swap(): return lax.ppermute(tensor, 'seq', [(i, i ^ k) for i in everyone])]
    ppermute x63 -> x52, starting transfers between devices: 108 us -> 69 us  [swap(): return lax.ppermute(tensor, 'seq', [(i, i ^ k) for i in everyone])]
    pallas_call x1, Pallas kernels: 33 us -> 1.04 us  [body(): pl.pallas_call(functools.partial(unpack_kernel, devs, pairs), in_specs=[S...]
    unnamed x101 -> x17, local copies, waits for them, and re-layouts: 6.09 us -> 6.82 us
  transfers between devices with their start and end apart: 63 -> 52, of which waited for: 14 -> 18; matrix products, arithmetic and copies ran while one was open for 1% -> 0% of each run, Pallas kernels for 36% -> 7%
where the time goes in v4:
time: 190 us; the launch traced here: 188 us
  waiting for transfers between devices  94.5 us (50%)
  starting transfers between devices  69 us (36%)
  Pallas kernels  17.5 us (9%)
  local copies, waits for them, and re-layouts  6.87 us (4%)
    ppermute x52, waiting for transfers between devices, swap(): return lax.ppermute(tensor, 'seq', [(i, i ^ k) for i in everyone])  94.5 us
    ppermute x52, starting transfers between devices, swap(): return lax.ppermute(tensor, 'seq', [(i, i ^ k) for i in everyone])  69 us
    pallas_call x4, Pallas kernels, attend(): pl.pallas_call(functools.partial(attend_kernel, ks, math.gcd(count, max(1...  12.5 us
    unnamed x17, local copies, waits for them, and re-layouts  6.82 us
  transfers between devices with their start and end apart: 52, of which 18 were waited for; matrix products, arithmetic and copies ran while one was open for 0% of the time, Pallas kernels for 7%

profile of v4, /device:TPU:1, one launch (start us, length us, event | category | flops | bytes accessed | tf_op | source)
XLA Modules:
  0.0 188.5 jit_solution(6191154091577010308)
XLA Ops:
  3.9 1.5 copy-done
  5.4 1.6 copy-done.1
  7.0 1.5 pick_factors.1
  8.7 2.0 %collective-permute-done = bf16[8,320,128]{2,1,0:T(8,128)(2,1)S(1)} collective-permute-done((bf16[8,320,128]{2,1,0:T(8,128)(2,1)S(1)}, bf16[8,320,128]{2,1,0:T(8,128)(2,1)S(1)}, u32[]{:S(2)}, u32[]{:S(2)}) %collective-permute-start) | collective-permute-done | bytes 655392 | tf_op jit(solution)/shard_map/ppermute | solution.py:200
  10.7 2.4 %collective-permute-start.1 = (bf16[4,320,128]{2,1,0:T(8,128)(2,1)S(1)}, bf16[4,320,128]{2,1,0:T(8,128)(2,1)S(1)}, u32[]{:S(2)}, u32[]{:S(2)}) collective-permute-start(bf16[4,320,128]{2,1,0:T(8,128)(2,1)S(1)} %slice_add_fusion), channel_id=1, source_target_pairs={{0,2},{1,3},{2,0},{3,1},{4,6},{5,7},{6,4},{7,5},{8,10},{9,11},{10,... | collective-permute-start | bytes 983048 | tf_op jit(solution)/shard_map/ppermute | solution.py:200
  13.2 2.3 %collective-permute-start.3 = (bf16[3,4,64,128]{3,2,1,0:T(8,128)(2,1)S(1)}, bf16[3,4,64,128]{3,2,1,0:T(8,128)(2,1)S(1)}, u32[]{:S(2)}, u32[]{:S(2)}) collective-permute-start(bf16[3,4,64,128]{3,2,1,0:T(8,128)(2,1)S(1)} %get-tuple-element.80), channel_id=1, source_target_pairs={{0,8},{1,9},{2,10},{3,11},{4,12},{5,13},{6,14},{7,15},{8,0},{9,1},... | collective-permute-start | bytes 589832 | tf_op jit(solution)/shard_map/ppermute | solution.py:200
  16.4 4.6 %collective-permute-done.1 = bf16[4,320,128]{2,1,0:T(8,128)(2,1)S(1)} collective-permute-done((bf16[4,320,128]{2,1,0:T(8,128)(2,1)S(1)}, bf16[4,320,128]{2,1,0:T(8,128)(2,1)S(1)}, u32[]{:S(2)}, u32[]{:S(2)}) %collective-permute-start.1) | collective-permute-done | bytes 327712 | tf_op jit(solution)/shard_map/ppermute | solution.py:200
  21.9 11.5 %collective-permute-done.4.refs_13_.refs_5_ = bf16[3,4,64,128]{3,2,1,0:T(8,128)(2,1)S(1)} collective-permute-done((bf16[3,4,64,128]{3,2,1,0:T(8,128)(2,1)S(1)}, bf16[3,4,64,128]{3,2,1,0:T(8,128)(2,1)S(1)}, u32[]{:S(2)}, u32[]{:S(2)}) %collective-permute-start.4) | collective-permute-done | bytes 196640 | tf_op jit(solution)/shard_map/ppermute | solution.py:200
  33.9 2.8 %collective-permute-start.7 = (bf16[3,4,64,128]{3,2,1,0:T(8,128)(2,1)S(1)}, bf16[3,4,64,128]{3,2,1,0:T(8,128)(2,1)S(1)}, u32[]{:S(2)}, u32[]{:S(2)}) collective-permute-start(bf16[3,4,64,128]{3,2,1,0:T(8,128)(2,1)S(1)} %get-tuple-element.95), channel_id=1, source_target_pairs={{0,12},{1,13},{2,14},{3,15},{4,8},{5,9},{6,10},{7,11},{8,4},{9,5},... | collective-permute-start | bytes 589832 | tf_op jit(solution)/shard_map/ppermute | solution.py:200
  36.8 2.8 %collective-permute-done.5 = bf16[2,320,128]{2,1,0:T(8,128)(2,1)S(1)} collective-permute-done((bf16[2,320,128]{2,1,0:T(8,128)(2,1)S(1)}, bf16[2,320,128]{2,1,0:T(8,128)(2,1)S(1)}, u32[]{:S(2)}, u32[]{:S(2)}) %collective-permute-start.5) | collective-permute-done | bytes 163872 | tf_op jit(solution)/shard_map/ppermute | solution.py:200
  39.6 5.7 %collective-permute-done.7.refs_16_.refs_6_ = bf16[3,4,64,128]{3,2,1,0:T(8,128)(2,1)S(1)} collective-permute-done((bf16[3,4,64,128]{3,2,1,0:T(8,128)(2,1)S(1)}, bf16[3,4,64,128]{3,2,1,0:T(8,128)(2,1)S(1)}, u32[]{:S(2)}, u32[]{:S(2)}) %collective-permute-start.7) | collective-permute-done | bytes 196640 | tf_op jit(solution)/shard_map/ppermute | solution.py:200
  45.3 2.0 %collective-permute-start.8 = (bf16[1,320,128]{2,1,0:T(8,128)(2,1)S(1)}, bf16[1,320,128]{2,1,0:T(8,128)(2,1)S(1)}, u32[]{:S(2)}, u32[]{:S(2)}) collective-permute-start(bf16[1,320,128]{2,1,0:T(8,128)(2,1)S(1)} %slice_add_fusion.6), channel_id=1, source_target_pairs={{0,8},{1,9},{2,10},{3,11},{4,12},{5,13},{6,14},{7,15},{8,0},{9,1},... | collective-permute-start | bytes 245768 | tf_op jit(solution)/shard_map/ppermute | solution.py:200
  47.6 1.9 collective-permute-start.9
  51.1 6.6 %collective-permute-done.10.refs_6_ = bf16[3,4,64,128]{3,2,1,0:T(8,128)(2,1)S(1)} collective-permute-done((bf16[3,4,64,128]{3,2,1,0:T(8,128)(2,1)S(1)}, bf16[3,4,64,128]{3,2,1,0:T(8,128)(2,1)S(1)}, u32[]{:S(2)}, u32[]{:S(2)}) %collective-permute-start.10) | collective-permute-done | bytes 196640 | tf_op jit(solution)/shard_map/ppermute | solution.py:200
  57.8 6.0 %collective-permute-done.11.refs_7_ = bf16[3,4,64,128]{3,2,1,0:T(8,128)(2,1)S(1)} collective-permute-done((bf16[3,4,64,128]{3,2,1,0:T(8,128)(2,1)S(1)}, bf16[3,4,64,128]{3,2,1,0:T(8,128)(2,1)S(1)}, u32[]{:S(2)}, u32[]{:S(2)}) %collective-permute-start.11) | collective-permute-done | bytes 196640 | tf_op jit(solution)/shard_map/ppermute | solution.py:200
  64.2 5.0 %collective-permute-done.12 = bf16[1,320,128]{2,1,0:T(8,128)(2,1)S(1)} collective-permute-done((bf16[1,320,128]{2,1,0:T(8,128)(2,1)S(1)}, bf16[1,320,128]{2,1,0:T(8,128)(2,1)S(1)}, u32[]{:S(2)}, u32[]{:S(2)}) %collective-permute-start.12) | collective-permute-done | bytes 81952 | tf_op jit(solution)/shard_map/ppermute | solution.py:200
  69.3 5.4 %collective-permute-done.13 = bf16[2,320,128]{2,1,0:T(8,128)(2,1)S(1)} collective-permute-done((bf16[2,320,128]{2,1,0:T(8,128)(2,1)S(1)}, bf16[2,320,128]{2,1,0:T(8,128)(2,1)S(1)}, u32[]{:S(2)}, u32[]{:S(2)}) %collective-permute-start.13) | collective-permute-done | bytes 163872 | tf_op jit(solution)/shard_map/ppermute | solution.py:200
  75.9 3.0 %collective-permute-start.15 = (bf16[3,4,64,128]{3,2,1,0:T(8,128)(2,1)S(1)}, bf16[3,4,64,128]{3,2,1,0:T(8,128)(2,1)S(1)}, u32[]{:S(2)}, u32[]{:S(2)}) collective-permute-start(bf16[3,4,64,128]{3,2,1,0:T(8,128)(2,1)S(1)} %get-tuple-element.105), channel_id=1, source_target_pairs={{0,13},{1,12},{2,15},{3,14},{4,9},{5,8},{6,11},{7,10},{8,5},{9,4},... | collective-permute-start | bytes 589832 | tf_op jit(solution)/shard_map/ppermute | solution.py:200
  78.9 3.8 %collective-permute-done.14 = bf16[4,320,128]{2,1,0:T(8,128)(2,1)S(1)} collective-permute-done((bf16[4,320,128]{2,1,0:T(8,128)(2,1)S(1)}, bf16[4,320,128]{2,1,0:T(8,128)(2,1)S(1)}, u32[]{:S(2)}, u32[]{:S(2)}) %collective-permute-start.14) | collective-permute-done | bytes 327712 | tf_op jit(solution)/shard_map/ppermute | solution.py:200
  82.9 1.6 collective-permute-done.15.refs_17_.refs_7_
  85.7 3.4 %collective-permute-start.17 = (bf16[2,4,64,128]{3,2,1,0:T(8,128)(2,1)S(1)}, bf16[2,4,64,128]{3,2,1,0:T(8,128)(2,1)S(1)}, u32[]{:S(2)}, u32[]{:S(2)}) collective-permute-start(bf16[2,4,64,128]{3,2,1,0:T(8,128)(2,1)S(1)} %get-tuple-element.108), channel_id=1, source_target_pairs={{0,10},{1,11},{2,8},{3,9},{4,14},{5,15},{6,12},{7,13},{8,2},{9,3},... | collective-permute-start | bytes 393224 | tf_op jit(solution)/shard_map/ppermute | solution.py:200
  89.4 3.5 %collective-permute-done.17.refs_14_ = bf16[2,4,64,128]{3,2,1,0:T(8,128)(2,1)S(1)} collective-permute-done((bf16[2,4,64,128]{3,2,1,0:T(8,128)(2,1)S(1)}, bf16[2,4,64,128]{3,2,1,0:T(8,128)(2,1)S(1)}, u32[]{:S(2)}, u32[]{:S(2)}) %collective-permute-start.17) | collective-permute-done | bytes 131104 | tf_op jit(solution)/shard_map/ppermute | solution.py:200
  92.8 8.5 %collective-permute-done.18.refs_15_ = bf16[2,4,64,128]{3,2,1,0:T(8,128)(2,1)S(1)} collective-permute-done((bf16[2,4,64,128]{3,2,1,0:T(8,128)(2,1)S(1)}, bf16[2,4,64,128]{3,2,1,0:T(8,128)(2,1)S(1)}, u32[]{:S(2)}, u32[]{:S(2)}) %collective-permute-start.18) | collective-permute-done | bytes 131104 | tf_op jit(solution)/shard_map/ppermute | solution.py:200
  102.3 1.7 collective-permute-start.23
  104.9 2.5 %collective-permute-start.24 = (bf16[2,4,64,128]{3,2,1,0:T(8,128)(2,1)S(1)}, bf16[2,4,64,128]{3,2,1,0:T(8,128)(2,1)S(1)}, u32[]{:S(2)}, u32[]{:S(2)}) collective-permute-start(bf16[2,4,64,128]{3,2,1,0:T(8,128)(2,1)S(1)} %get-tuple-element.116), channel_id=1, source_target_pairs={{0,14},{1,15},{2,12},{3,13},{4,10},{5,11},{6,8},{7,9},{8,6},{9,7},... | collective-permute-start | bytes 393224 | tf_op jit(solution)/shard_map/ppermute | solution.py:200
  107.4 3.1 %collective-permute-start.25 = (bf16[2,4,64,128]{3,2,1,0:T(8,128)(2,1)S(1)}, bf16[2,4,64,128]{3,2,1,0:T(8,128)(2,1)S(1)}, u32[]{:S(2)}, u32[]{:S(2)}) collective-permute-start(bf16[2,4,64,128]{3,2,1,0:T(8,128)(2,1)S(1)} %get-tuple-element.118), channel_id=1, source_target_pairs={{0,15},{1,14},{2,13},{3,12},{4,11},{5,10},{6,9},{7,8},{8,7},{9,6},... | collective-permute-start | bytes 393224 | tf_op jit(solution)/shard_map/ppermute | solution.py:200
  112.1 12.9 %collective-permute-done.21 = bf16[64,128]{1,0:T(8,128)(2,1)S(1)} collective-permute-done((bf16[64,128]{1,0:T(8,128)(2,1)S(1)}, bf16[64,128]{1,0:T(8,128)(2,1)S(1)}, u32[]{:S(2)}, u32[]{:S(2)}) %collective-permute-start.21) | collective-permute-done | bytes 16416 | tf_op jit(solution)/shard_map/ppermute | solution.py:200
  125.2 1.8 collective-permute-start.31
  127.0 1.5 collective-permute-start.32
  131.4 8.5 %collective-permute-done.28.refs_3_ = bf16[4,64,128]{2,1,0:T(8,128)(2,1)S(1)} collective-permute-done((bf16[4,64,128]{2,1,0:T(8,128)(2,1)S(1)}, bf16[4,64,128]{2,1,0:T(8,128)(2,1)S(1)}, u32[]{:S(2)}, u32[]{:S(2)}) %collective-permute-start.28) | collective-permute-done | bytes 65568 | tf_op jit(solution)/shard_map/ppermute | solution.py:200
  140.8 2.4 %collective-permute-start.43 = (bf16[1,4,64,128]{3,2,1,0:T(8,128)(2,1)S(1)}, bf16[1,4,64,128]{3,2,1,0:T(8,128)(2,1)S(1)}, u32[]{:S(2)}, u32[]{:S(2)}) collective-permute-start(bf16[1,4,64,128]{3,2,1,0:T(8,128)(2,1)S(1)} %get-tuple-element.144), channel_id=1, source_target_pairs={{0,11},{1,10},{2,9},{3,8},{4,15},{5,14},{6,13},{7,12},{8,3},{9,2},... | collective-permute-start | bytes 196616 | tf_op jit(solution)/shard_map/ppermute | solution.py:200
  143.2 1.8 collective-permute-start.44
  145.0 2.8 %collective-permute-start.45 = (bf16[1,4,64,128]{3,2,1,0:T(8,128)(2,1)S(1)}, bf16[1,4,64,128]{3,2,1,0:T(8,128)(2,1)S(1)}, u32[]{:S(2)}, u32[]{:S(2)}) collective-permute-start(bf16[1,4,64,128]{3,2,1,0:T(8,128)(2,1)S(1)} %get-tuple-element.148), channel_id=1, source_target_pairs={{0,15},{1,14},{2,13},{3,12},{4,11},{5,10},{6,9},{7,8},{8,7},{9,6},... | collective-permute-start | bytes 196616 | tf_op jit(solution)/shard_map/ppermute | solution.py:200
  147.9 1.4 prepare.1
  149.3 3.1 %attend.6 = (bf16[4,64,128]{2,1,0:T(8,128)(2,1)S(1)}, bf16[4,64,128]{2,1,0:T(8,128)(2,1)S(1)}, bf16[4,64,128]{2,1,0:T(8,128)(2,1)S(1)}, bf16[4,64,128]{2,1,0:T(8,128)(2,1)S(1)}) custom-call(s32[1]{0:T(128)} %bitcast.me_ref, bf16[4,64,128]{2,1,0:T(8,128)(2,1)S(1)} %bitcast.11, bf16[4,1024,128]{2,1,0:T(8,128)(2,1)S(1)} %get-tuple-element.129.k_ref, ...), custom_call_target="tpu_custom_call" | custom-call | flops 536870912 | bytes 2621440 | tf_op jit(solution)/shard_map/attend/pallas_call | solution.py:342
  152.5 3.1 %attend.5 = (bf16[4,64,128]{2,1,0:T(8,128)(2,1)S(1)}, bf16[4,64,128]{2,1,0:T(8,128)(2,1)S(1)}, bf16[4,64,128]{2,1,0:T(8,128)(2,1)S(1)}, bf16[4,64,128]{2,1,0:T(8,128)(2,1)S(1)}) custom-call(s32[1]{0:T(128)} %bitcast.me_ref, bf16[4,64,128]{2,1,0:T(8,128)(2,1)S(1)} %bitcast.12, bf16[4,1024,128]{2,1,0:T(8,128)(2,1)S(1)} %get-tuple-element.129.k_ref, ...), custom_call_target="tpu_custom_call" | custom-call | flops 536870912 | bytes 2621440 | tf_op jit(solution)/shard_map/attend/pallas_call | solution.py:342
  155.6 2.4 %collective-permute-start.41 = (bf16[4,64,128]{2,1,0:T(8,128)(2,1)S(1)}, bf16[4,64,128]{2,1,0:T(8,128)(2,1)S(1)}, u32[]{:S(2)}, u32[]{:S(2)}) collective-permute-start(bf16[4,64,128]{2,1,0:T(8,128)(2,1)S(1)} %get-tuple-element.140), channel_id=1, source_target_pairs={{0,9},{1,8},{2,11},{3,10},{4,13},{5,12},{6,15},{7,14},{8,1},{9,0},... | collective-permute-start | bytes 196616 | tf_op jit(solution)/shard_map/ppermute | solution.py:200
  158.1 1.6 collective-permute-start.48
  159.7 2.2 %collective-permute-start.49 = (bf16[4,64,128]{2,1,0:T(8,128)(2,1)S(1)}, bf16[4,64,128]{2,1,0:T(8,128)(2,1)S(1)}, u32[]{:S(2)}, u32[]{:S(2)}) collective-permute-start(bf16[4,64,128]{2,1,0:T(8,128)(2,1)S(1)} %get-tuple-element.152), channel_id=1, source_target_pairs={{0,13},{1,12},{2,15},{3,14},{4,9},{5,8},{6,11},{7,10},{8,5},{9,4},... | collective-permute-start | bytes 196616 | tf_op jit(solution)/shard_map/ppermute | solution.py:200
  161.9 3.1 %attend.4 = (bf16[4,64,128]{2,1,0:T(8,128)(2,1)S(1)}, bf16[4,64,128]{2,1,0:T(8,128)(2,1)S(1)}, bf16[4,64,128]{2,1,0:T(8,128)(2,1)S(1)}, bf16[4,64,128]{2,1,0:T(8,128)(2,1)S(1)}) custom-call(s32[1]{0:T(128)} %bitcast.me_ref, bf16[4,64,128]{2,1,0:T(8,128)(2,1)S(1)} %bitcast.13, bf16[4,1024,128]{2,1,0:T(8,128)(2,1)S(1)} %get-tuple-element.129.k_ref, ...), custom_call_target="tpu_custom_call" | custom-call | flops 536870912 | bytes 2621440 | tf_op jit(solution)/shard_map/attend/pallas_call | solution.py:342
  165.0 1.6 collective-permute-start.37
  166.6 2.8 %collective-permute-start.39 = (bf16[4,64,128]{2,1,0:T(8,128)(2,1)S(1)}, bf16[4,64,128]{2,1,0:T(8,128)(2,1)S(1)}, u32[]{:S(2)}, u32[]{:S(2)}) collective-permute-start(bf16[4,64,128]{2,1,0:T(8,128)(2,1)S(1)} %get-tuple-element.138), channel_id=1, source_target_pairs={{0,7},{1,6},{2,5},{3,4},{4,3},{5,2},{6,1},{7,0},{8,15},{9,14},{10,... | collective-permute-start | bytes 196616 | tf_op jit(solution)/shard_map/ppermute | solution.py:200
  169.8 3.1 %attend.7 = (bf16[4,64,128]{2,1,0:T(8,128)(2,1)S(1)}, bf16[4,64,128]{2,1,0:T(8,128)(2,1)S(1)}, bf16[4,64,128]{2,1,0:T(8,128)(2,1)S(1)}, bf16[4,64,128]{2,1,0:T(8,128)(2,1)S(1)}) custom-call(s32[1]{0:T(128)} %bitcast.me_ref, bf16[4,64,128]{2,1,0:T(8,128)(2,1)S(1)} %bitcast.14, bf16[4,1024,128]{2,1,0:T(8,128)(2,1)S(1)} %get-tuple-element.129.k_ref, ...), custom_call_target="tpu_custom_call" | custom-call | flops 536870912 | bytes 2621440 | tf_op jit(solution)/shard_map/attend/pallas_call | solution.py:342
  172.9 1.8 collective-permute-start.35
  175.3 2.7 %collective-permute-start.47 = (bf16[4,64,128]{2,1,0:T(8,128)(2,1)S(1)}, bf16[4,64,128]{2,1,0:T(8,128)(2,1)S(1)}, u32[]{:S(2)}, u32[]{:S(2)}) collective-permute-start(bf16[4,64,128]{2,1,0:T(8,128)(2,1)S(1)} %get-tuple-element.150), channel_id=1, source_target_pairs={{0,11},{1,10},{2,9},{3,8},{4,15},{5,14},{6,13},{7,12},{8,3},{9,2},... | collective-permute-start | bytes 196616 | tf_op jit(solution)/shard_map/ppermute | solution.py:200
  178.0 1.7 collective-permute-start.50
  179.8 3.0 %collective-permute-start.51 = (bf16[4,64,128]{2,1,0:T(8,128)(2,1)S(1)}, bf16[4,64,128]{2,1,0:T(8,128)(2,1)S(1)}, u32[]{:S(2)}, u32[]{:S(2)}) collective-permute-start(bf16[4,64,128]{2,1,0:T(8,128)(2,1)S(1)} %get-tuple-element.154), channel_id=1, source_target_pairs={{0,15},{1,14},{2,13},{3,12},{4,11},{5,10},{6,9},{7,8},{8,7},{9,6},... | collective-permute-start | bytes 196616 | tf_op jit(solution)/shard_map/ppermute | solution.py:200
  183.2 4.2 %collective-permute-done.47.refs_11_ = bf16[4,64,128]{2,1,0:T(8,128)(2,1)S(1)} collective-permute-done((bf16[4,64,128]{2,1,0:T(8,128)(2,1)S(1)}, bf16[4,64,128]{2,1,0:T(8,128)(2,1)S(1)}, u32[]{:S(2)}, u32[]{:S(2)}) %collective-permute-start.47) | collective-permute-done | bytes 65568 | tf_op jit(solution)/shard_map/ppermute | solution.py:200
  (95 shorter events, 21.7 us)
Async XLA Ops:
  10.7 10.2 %collective-permute-start.1 = (bf16[4,320,128]{2,1,0:T(8,128)(2,1)S(1)}, bf16[4,320,128]{2,1,0:T(8,128)(2,1)S(1)}, u32[]{:S(2)}, u32[]{:S(2)}) collective-permute-start(bf16[4,320,128]{2,1,0:T(8,128)(2,1)S(1)} %slice_add_fusion), channel_id=1, source_target_pairs={{0,2},{1,3},{2,0},{3,1},{4,6},{5,7},{6,4},{7,5},{8,10},{9,11},{10,... | collective-permute-start | bytes 983048 | tf_op jit(solution)/shard_map/ppermute | solution.py:200
  13.2 20.2 %collective-permute-start.3 = (bf16[3,4,64,128]{3,2,1,0:T(8,128)(2,1)S(1)}, bf16[3,4,64,128]{3,2,1,0:T(8,128)(2,1)S(1)}, u32[]{:S(2)}, u32[]{:S(2)}) collective-permute-start(bf16[3,4,64,128]{3,2,1,0:T(8,128)(2,1)S(1)} %get-tuple-element.80), channel_id=1, source_target_pairs={{0,8},{1,9},{2,10},{3,11},{4,12},{5,13},{6,14},{7,15},{8,0},{9,1},... | collective-permute-start | bytes 589832 | tf_op jit(solution)/shard_map/ppermute | solution.py:200
  15.5 17.9 %collective-permute-start.4 = (bf16[3,4,64,128]{3,2,1,0:T(8,128)(2,1)S(1)}, bf16[3,4,64,128]{3,2,1,0:T(8,128)(2,1)S(1)}, u32[]{:S(2)}, u32[]{:S(2)}) collective-permute-start(bf16[3,4,64,128]{3,2,1,0:T(8,128)(2,1)S(1)} %get-tuple-element.89), channel_id=1, source_target_pairs={{0,9},{1,8},{2,11},{3,10},{4,13},{5,12},{6,15},{7,14},{8,1},{9,0},... | collective-permute-start | bytes 589832 | tf_op jit(solution)/shard_map/ppermute | solution.py:200
  21.0 26.3 %collective-permute-start.2 = (bf16[8,256,128]{2,1,0:T(8,128)(2,1)S(1)}, bf16[8,256,128]{2,1,0:T(8,128)(2,1)S(1)}, u32[]{:S(2)}, u32[]{:S(2)}) collective-permute-start(bf16[8,256,128]{2,1,0:T(8,128)(2,1)S(1)} %get-tuple-element.86), channel_id=1, source_target_pairs={{0,1},{1,0},{2,3},{3,2},{4,5},{5,4},{6,7},{7,6},{8,9},{9,8},{10,11... | collective-permute-start | bytes 1572872 | tf_op jit(solution)/shard_map/ppermute | solution.py:200
  33.4 6.2 %collective-permute-start.5 = (bf16[2,320,128]{2,1,0:T(8,128)(2,1)S(1)}, bf16[2,320,128]{2,1,0:T(8,128)(2,1)S(1)}, u32[]{:S(2)}, u32[]{:S(2)}) collective-permute-start(bf16[2,320,128]{2,1,0:T(8,128)(2,1)S(1)} %slice_add_fusion.2), channel_id=1, source_target_pairs={{0,4},{1,5},{2,6},{3,7},{4,0},{5,1},{6,2},{7,3},{8,12},{9,13},{10,... | collective-permute-start | bytes 491528 | tf_op jit(solution)/shard_map/ppermute | solution.py:200
  33.9 11.3 %collective-permute-start.7 = (bf16[3,4,64,128]{3,2,1,0:T(8,128)(2,1)S(1)}, bf16[3,4,64,128]{3,2,1,0:T(8,128)(2,1)S(1)}, u32[]{:S(2)}, u32[]{:S(2)}) collective-permute-start(bf16[3,4,64,128]{3,2,1,0:T(8,128)(2,1)S(1)} %get-tuple-element.95), channel_id=1, source_target_pairs={{0,12},{1,13},{2,14},{3,15},{4,8},{5,9},{6,10},{7,11},{8,4},{9,5},... | collective-permute-start | bytes 589832 | tf_op jit(solution)/shard_map/ppermute | solution.py:200
  45.3 5.8 %collective-permute-start.8 = (bf16[1,320,128]{2,1,0:T(8,128)(2,1)S(1)}, bf16[1,320,128]{2,1,0:T(8,128)(2,1)S(1)}, u32[]{:S(2)}, u32[]{:S(2)}) collective-permute-start(bf16[1,320,128]{2,1,0:T(8,128)(2,1)S(1)} %slice_add_fusion.6), channel_id=1, source_target_pairs={{0,8},{1,9},{2,10},{3,11},{4,12},{5,13},{6,14},{7,15},{8,0},{9,1},... | collective-permute-start | bytes 245768 | tf_op jit(solution)/shard_map/ppermute | solution.py:200
  47.3 16.5 %collective-permute-start.6 = (bf16[4,256,128]{2,1,0:T(8,128)(2,1)S(1)}, bf16[4,256,128]{2,1,0:T(8,128)(2,1)S(1)}, u32[]{:S(2)}, u32[]{:S(2)}) collective-permute-start(bf16[4,256,128]{2,1,0:T(8,128)(2,1)S(1)} %slice_add_fusion.1), channel_id=1, source_target_pairs={{0,2},{1,3},{2,0},{3,1},{4,6},{5,7},{6,4},{7,5},{8,10},{9,11},{10,... | collective-permute-start | bytes 786440 | tf_op jit(solution)/shard_map/ppermute | solution.py:200
  49.5 8.3 %collective-permute-start.10 = (bf16[3,4,64,128]{3,2,1,0:T(8,128)(2,1)S(1)}, bf16[3,4,64,128]{3,2,1,0:T(8,128)(2,1)S(1)}, u32[]{:S(2)}, u32[]{:S(2)}) collective-permute-start(bf16[3,4,64,128]{3,2,1,0:T(8,128)(2,1)S(1)} %get-tuple-element.100), channel_id=1, source_target_pairs={{0,2},{1,3},{2,0},{3,1},{4,6},{5,7},{6,4},{7,5},{8,10},{9,11},{10,... | collective-permute-start | bytes 589832 | tf_op jit(solution)/shard_map/ppermute | solution.py:200
  50.7 13.1 %collective-permute-start.11 = (bf16[3,4,64,128]{3,2,1,0:T(8,128)(2,1)S(1)}, bf16[3,4,64,128]{3,2,1,0:T(8,128)(2,1)S(1)}, u32[]{:S(2)}, u32[]{:S(2)}) collective-permute-start(bf16[3,4,64,128]{3,2,1,0:T(8,128)(2,1)S(1)} %get-tuple-element.102), channel_id=1, source_target_pairs={{0,3},{1,2},{2,1},{3,0},{4,7},{5,6},{6,5},{7,4},{8,11},{9,10},{10,... | collective-permute-start | bytes 589832 | tf_op jit(solution)/shard_map/ppermute | solution.py:200
  69.3 5.5 %collective-permute-start.13 = (bf16[2,320,128]{2,1,0:T(8,128)(2,1)S(1)}, bf16[2,320,128]{2,1,0:T(8,128)(2,1)S(1)}, u32[]{:S(2)}, u32[]{:S(2)}) collective-permute-start(bf16[2,320,128]{2,1,0:T(8,128)(2,1)S(1)} %get-tuple-element.155), channel_id=1, source_target_pairs={{0,4},{1,5},{2,6},{3,7},{4,0},{5,1},{6,2},{7,3},{8,12},{9,13},{10,... | collective-permute-start | bytes 491528 | tf_op jit(solution)/shard_map/ppermute | solution.py:200
  74.7 8.0 %collective-permute-start.14 = (bf16[4,320,128]{2,1,0:T(8,128)(2,1)S(1)}, bf16[4,320,128]{2,1,0:T(8,128)(2,1)S(1)}, u32[]{:S(2)}, u32[]{:S(2)}) collective-permute-start(bf16[4,320,128]{2,1,0:T(8,128)(2,1)S(1)} %constant_dynamic-update-slice_fusion.2), channel_id=1, source_target_pairs={{0,2},{1,3},{2,0},{3,1},{4,6},{5,7},{6,4},{7,5},{8,10},{9,11},{10,... | collective-permute-start | bytes 983048 | tf_op jit(solution)/shard_map/ppermute | solution.py:200
  75.9 8.5 %collective-permute-start.15 = (bf16[3,4,64,128]{3,2,1,0:T(8,128)(2,1)S(1)}, bf16[3,4,64,128]{3,2,1,0:T(8,128)(2,1)S(1)}, u32[]{:S(2)}, u32[]{:S(2)}) collective-permute-start(bf16[3,4,64,128]{3,2,1,0:T(8,128)(2,1)S(1)} %get-tuple-element.105), channel_id=1, source_target_pairs={{0,13},{1,12},{2,15},{3,14},{4,9},{5,8},{6,11},{7,10},{8,5},{9,4},... | collective-permute-start | bytes 589832 | tf_op jit(solution)/shard_map/ppermute | solution.py:200
  85.7 7.1 %collective-permute-start.17 = (bf16[2,4,64,128]{3,2,1,0:T(8,128)(2,1)S(1)}, bf16[2,4,64,128]{3,2,1,0:T(8,128)(2,1)S(1)}, u32[]{:S(2)}, u32[]{:S(2)}) collective-permute-start(bf16[2,4,64,128]{3,2,1,0:T(8,128)(2,1)S(1)} %get-tuple-element.108), channel_id=1, source_target_pairs={{0,10},{1,11},{2,8},{3,9},{4,14},{5,15},{6,12},{7,13},{8,2},{9,3},... | collective-permute-start | bytes 393224 | tf_op jit(solution)/shard_map/ppermute | solution.py:200
  89.1 12.2 %collective-permute-start.18 = (bf16[2,4,64,128]{3,2,1,0:T(8,128)(2,1)S(1)}, bf16[2,4,64,128]{3,2,1,0:T(8,128)(2,1)S(1)}, u32[]{:S(2)}, u32[]{:S(2)}) collective-permute-start(bf16[2,4,64,128]{3,2,1,0:T(8,128)(2,1)S(1)} %get-tuple-element.110), channel_id=1, source_target_pairs={{0,11},{1,10},{2,9},{3,8},{4,15},{5,14},{6,13},{7,12},{8,3},{9,2},... | collective-permute-start | bytes 393224 | tf_op jit(solution)/shard_map/ppermute | solution.py:200
  102.2 8.9 %collective-permute-start.19 = (bf16[2,256,128]{2,1,0:T(8,128)(2,1)S(1)}, bf16[2,256,128]{2,1,0:T(8,128)(2,1)S(1)}, u32[]{:S(2)}, u32[]{:S(2)}) collective-permute-start(bf16[2,256,128]{2,1,0:T(8,128)(2,1)S(1)} %slice_add_fusion.4), channel_id=1, source_target_pairs={{0,4},{1,5},{2,6},{3,7},{4,0},{5,1},{6,2},{7,3},{8,12},{9,13},{10,... | collective-permute-start | bytes 393224 | tf_op jit(solution)/shard_map/ppermute | solution.py:200
  102.3 8.2 %collective-permute-start.23 = (bf16[64,128]{1,0:T(8,128)(2,1)S(1)}, bf16[64,128]{1,0:T(8,128)(2,1)S(1)}, u32[]{:S(2)}, u32[]{:S(2)}) collective-permute-start(bf16[64,128]{1,0:T(8,128)(2,1)S(1)} %low_rank.1), channel_id=1, source_target_pairs={{0,12},{1,13},{2,14},{3,15},{4,8},{5,9},{6,10},{7,11},{8,4},{9,5},... | collective-permute-start | bytes 49160 | tf_op jit(solution)/shard_map/ppermute | solution.py:200
  104.0 6.5 %collective-permute-start.22 = (bf16[64,128]{1,0:T(8,128)(2,1)S(1)}, bf16[64,128]{1,0:T(8,128)(2,1)S(1)}, u32[]{:S(2)}, u32[]{:S(2)}) collective-permute-start(bf16[64,128]{1,0:T(8,128)(2,1)S(1)} %low_rank.1), channel_id=1, source_target_pairs={{0,8},{1,9},{2,10},{3,11},{4,12},{5,13},{6,14},{7,15},{8,0},{9,1},... | collective-permute-start | bytes 49160 | tf_op jit(solution)/shard_map/ppermute | solution.py:200
  104.9 20.3 %collective-permute-start.24 = (bf16[2,4,64,128]{3,2,1,0:T(8,128)(2,1)S(1)}, bf16[2,4,64,128]{3,2,1,0:T(8,128)(2,1)S(1)}, u32[]{:S(2)}, u32[]{:S(2)}) collective-permute-start(bf16[2,4,64,128]{3,2,1,0:T(8,128)(2,1)S(1)} %get-tuple-element.116), channel_id=1, source_target_pairs={{0,14},{1,15},{2,12},{3,13},{4,10},{5,11},{6,8},{7,9},{8,6},{9,7},... | collective-permute-start | bytes 393224 | tf_op jit(solution)/shard_map/ppermute | solution.py:200
  107.4 19.6 %collective-permute-start.25 = (bf16[2,4,64,128]{3,2,1,0:T(8,128)(2,1)S(1)}, bf16[2,4,64,128]{3,2,1,0:T(8,128)(2,1)S(1)}, u32[]{:S(2)}, u32[]{:S(2)}) collective-permute-start(bf16[2,4,64,128]{3,2,1,0:T(8,128)(2,1)S(1)} %get-tuple-element.118), channel_id=1, source_target_pairs={{0,15},{1,14},{2,13},{3,12},{4,11},{5,10},{6,9},{7,8},{8,7},{9,6},... | collective-permute-start | bytes 393224 | tf_op jit(solution)/shard_map/ppermute | solution.py:200
  110.5 18.0 %collective-permute-start.29 = (bf16[3,4,64,128]{3,2,1,0:T(8,128)(2,1)S(1)}, bf16[3,4,64,128]{3,2,1,0:T(8,128)(2,1)S(1)}, u32[]{:S(2)}, u32[]{:S(2)}) collective-permute-start(bf16[3,4,64,128]{3,2,1,0:T(8,128)(2,1)S(1)} %get-tuple-element.122), channel_id=1, source_target_pairs={{0,4},{1,5},{2,6},{3,7},{4,0},{5,1},{6,2},{7,3},{8,12},{9,13},{10,... | collective-permute-start | bytes 589832 | tf_op jit(solution)/shard_map/ppermute | solution.py:200
  110.5 18.5 %collective-permute-start.30 = (bf16[3,4,64,128]{3,2,1,0:T(8,128)(2,1)S(1)}, bf16[3,4,64,128]{3,2,1,0:T(8,128)(2,1)S(1)}, u32[]{:S(2)}, u32[]{:S(2)}) collective-permute-start(bf16[3,4,64,128]{3,2,1,0:T(8,128)(2,1)S(1)} %get-tuple-element.124), channel_id=1, source_target_pairs={{0,5},{1,4},{2,7},{3,6},{4,1},{5,0},{6,3},{7,2},{8,13},{9,12},{10,... | collective-permute-start | bytes 589832 | tf_op jit(solution)/shard_map/ppermute | solution.py:200
  111.1 13.8 %collective-permute-start.21 = (bf16[64,128]{1,0:T(8,128)(2,1)S(1)}, bf16[64,128]{1,0:T(8,128)(2,1)S(1)}, u32[]{:S(2)}, u32[]{:S(2)}) collective-permute-start(bf16[64,128]{1,0:T(8,128)(2,1)S(1)} %low_rank.1), channel_id=1, source_target_pairs={{0,4},{1,5},{2,6},{3,7},{4,0},{5,1},{6,2},{7,3},{8,12},{9,13},{10,... | collective-permute-start | bytes 49160 | tf_op jit(solution)/shard_map/ppermute | solution.py:200
  124.9 5.8 %collective-permute-start.20 = (bf16[1,256,128]{2,1,0:T(8,128)(2,1)S(1)}, bf16[1,256,128]{2,1,0:T(8,128)(2,1)S(1)}, u32[]{:S(2)}, u32[]{:S(2)}) collective-permute-start(bf16[1,256,128]{2,1,0:T(8,128)(2,1)S(1)} %slice_add_fusion.12), channel_id=1, source_target_pairs={{0,8},{1,9},{2,10},{3,11},{4,12},{5,13},{6,14},{7,15},{8,0},{9,1},... | collective-permute-start | bytes 196616 | tf_op jit(solution)/shard_map/ppermute | solution.py:200
  125.2 19.9 %collective-permute-start.31 = (bf16[3,4,64,128]{3,2,1,0:T(8,128)(2,1)S(1)}, bf16[3,4,64,128]{3,2,1,0:T(8,128)(2,1)S(1)}, u32[]{:S(2)}, u32[]{:S(2)}) collective-permute-start(bf16[3,4,64,128]{3,2,1,0:T(8,128)(2,1)S(1)} %get-tuple-element.126), channel_id=1, source_target_pairs={{0,6},{1,7},{2,4},{3,5},{4,2},{5,3},{6,0},{7,1},{8,14},{9,15},{10,... | collective-permute-start | bytes 589832 | tf_op jit(solution)/shard_map/ppermute | solution.py:200
  127.0 20.9 %collective-permute-start.32 = (bf16[3,4,64,128]{3,2,1,0:T(8,128)(2,1)S(1)}, bf16[3,4,64,128]{3,2,1,0:T(8,128)(2,1)S(1)}, u32[]{:S(2)}, u32[]{:S(2)}) collective-permute-start(bf16[3,4,64,128]{3,2,1,0:T(8,128)(2,1)S(1)} %get-tuple-element.128), channel_id=1, source_target_pairs={{0,7},{1,6},{2,5},{3,4},{4,3},{5,2},{6,1},{7,0},{8,15},{9,14},{10,... | collective-permute-start | bytes 589832 | tf_op jit(solution)/shard_map/ppermute | solution.py:200
  128.5 11.4 %collective-permute-start.28 = (bf16[4,64,128]{2,1,0:T(8,128)(2,1)S(1)}, bf16[4,64,128]{2,1,0:T(8,128)(2,1)S(1)}, u32[]{:S(2)}, u32[]{:S(2)}) collective-permute-start(bf16[4,64,128]{2,1,0:T(8,128)(2,1)S(1)} %pad_maximum_fusion.2.refs_0_), channel_id=1, source_target_pairs={{0,3},{1,2},{2,1},{3,0},{4,7},{5,6},{6,5},{7,4},{8,11},{9,10},{10,... | collective-permute-start | bytes 196616 | tf_op jit(solution)/shard_map/ppermute | solution.py:200
  129.0 11.8 %collective-permute-start.27 = (bf16[4,64,128]{2,1,0:T(8,128)(2,1)S(1)}, bf16[4,64,128]{2,1,0:T(8,128)(2,1)S(1)}, u32[]{:S(2)}, u32[]{:S(2)}) collective-permute-start(bf16[4,64,128]{2,1,0:T(8,128)(2,1)S(1)} %pad_maximum_fusion.2.refs_0_), channel_id=1, source_target_pairs={{0,2},{1,3},{2,0},{3,1},{4,6},{5,7},{6,4},{7,5},{8,10},{9,11},{10,... | collective-permute-start | bytes 196616 | tf_op jit(solution)/shard_map/ppermute | solution.py:200
  130.7 12.5 %collective-permute-start.26 = (bf16[4,64,128]{2,1,0:T(8,128)(2,1)S(1)}, bf16[4,64,128]{2,1,0:T(8,128)(2,1)S(1)}, u32[]{:S(2)}, u32[]{:S(2)}) collective-permute-start(bf16[4,64,128]{2,1,0:T(8,128)(2,1)S(1)} %pad_maximum_fusion.2.refs_0_), channel_id=1, source_target_pairs={{0,1},{1,0},{2,3},{3,2},{4,5},{5,4},{6,7},{7,6},{8,9},{9,8},{10,11... | collective-permute-start | bytes 196616 | tf_op jit(solution)/shard_map/ppermute | solution.py:200
  139.9 15.7 %collective-permute-start.42 = (bf16[1,4,64,128]{3,2,1,0:T(8,128)(2,1)S(1)}, bf16[1,4,64,128]{3,2,1,0:T(8,128)(2,1)S(1)}, u32[]{:S(2)}, u32[]{:S(2)}) collective-permute-start(bf16[1,4,64,128]{3,2,1,0:T(8,128)(2,1)S(1)} %get-tuple-element.142), channel_id=1, source_target_pairs={{0,10},{1,11},{2,8},{3,9},{4,14},{5,15},{6,12},{7,13},{8,2},{9,3},... | collective-permute-start | bytes 196616 | tf_op jit(solution)/shard_map/ppermute | solution.py:200
  140.8 17.3 %collective-permute-start.43 = (bf16[1,4,64,128]{3,2,1,0:T(8,128)(2,1)S(1)}, bf16[1,4,64,128]{3,2,1,0:T(8,128)(2,1)S(1)}, u32[]{:S(2)}, u32[]{:S(2)}) collective-permute-start(bf16[1,4,64,128]{3,2,1,0:T(8,128)(2,1)S(1)} %get-tuple-element.144), channel_id=1, source_target_pairs={{0,11},{1,10},{2,9},{3,8},{4,15},{5,14},{6,13},{7,12},{8,3},{9,2},... | collective-permute-start | bytes 196616 | tf_op jit(solution)/shard_map/ppermute | solution.py:200
  143.2 16.5 %collective-permute-start.44 = (bf16[1,4,64,128]{3,2,1,0:T(8,128)(2,1)S(1)}, bf16[1,4,64,128]{3,2,1,0:T(8,128)(2,1)S(1)}, u32[]{:S(2)}, u32[]{:S(2)}) collective-permute-start(bf16[1,4,64,128]{3,2,1,0:T(8,128)(2,1)S(1)} %get-tuple-element.146), channel_id=1, source_target_pairs={{0,14},{1,15},{2,12},{3,13},{4,10},{5,11},{6,8},{7,9},{8,6},{9,7},... | collective-permute-start | bytes 196616 | tf_op jit(solution)/shard_map/ppermute | solution.py:200
  145.0 16.8 %collective-permute-start.45 = (bf16[1,4,64,128]{3,2,1,0:T(8,128)(2,1)S(1)}, bf16[1,4,64,128]{3,2,1,0:T(8,128)(2,1)S(1)}, u32[]{:S(2)}, u32[]{:S(2)}) collective-permute-start(bf16[1,4,64,128]{3,2,1,0:T(8,128)(2,1)S(1)} %get-tuple-element.148), channel_id=1, source_target_pairs={{0,15},{1,14},{2,13},{3,12},{4,11},{5,10},{6,9},{7,8},{8,7},{9,6},... | collective-permute-start | bytes 196616 | tf_op jit(solution)/shard_map/ppermute | solution.py:200
  152.4 12.6 %collective-permute-start.40 = (bf16[4,64,128]{2,1,0:T(8,128)(2,1)S(1)}, bf16[4,64,128]{2,1,0:T(8,128)(2,1)S(1)}, u32[]{:S(2)}, u32[]{:S(2)}) collective-permute-start(bf16[4,64,128]{2,1,0:T(8,128)(2,1)S(1)} %get-tuple-element.139), channel_id=1, source_target_pairs={{0,8},{1,9},{2,10},{3,11},{4,12},{5,13},{6,14},{7,15},{8,0},{9,1},... | collective-permute-start | bytes 196616 | tf_op jit(solution)/shard_map/ppermute | solution.py:200
  155.6 10.9 %collective-permute-start.41 = (bf16[4,64,128]{2,1,0:T(8,128)(2,1)S(1)}, bf16[4,64,128]{2,1,0:T(8,128)(2,1)S(1)}, u32[]{:S(2)}, u32[]{:S(2)}) collective-permute-start(bf16[4,64,128]{2,1,0:T(8,128)(2,1)S(1)} %get-tuple-element.140), channel_id=1, source_target_pairs={{0,9},{1,8},{2,11},{3,10},{4,13},{5,12},{6,15},{7,14},{8,1},{9,0},... | collective-permute-start | bytes 196616 | tf_op jit(solution)/shard_map/ppermute | solution.py:200
  158.1 8.5 %collective-permute-start.48 = (bf16[4,64,128]{2,1,0:T(8,128)(2,1)S(1)}, bf16[4,64,128]{2,1,0:T(8,128)(2,1)S(1)}, u32[]{:S(2)}, u32[]{:S(2)}) collective-permute-start(bf16[4,64,128]{2,1,0:T(8,128)(2,1)S(1)} %get-tuple-element.151), channel_id=1, source_target_pairs={{0,12},{1,13},{2,14},{3,15},{4,8},{5,9},{6,10},{7,11},{8,4},{9,5},... | collective-permute-start | bytes 196616 | tf_op jit(solution)/shard_map/ppermute | solution.py:200
  159.7 9.8 %collective-permute-start.49 = (bf16[4,64,128]{2,1,0:T(8,128)(2,1)S(1)}, bf16[4,64,128]{2,1,0:T(8,128)(2,1)S(1)}, u32[]{:S(2)}, u32[]{:S(2)}) collective-permute-start(bf16[4,64,128]{2,1,0:T(8,128)(2,1)S(1)} %get-tuple-element.152), channel_id=1, source_target_pairs={{0,13},{1,12},{2,15},{3,14},{4,9},{5,8},{6,11},{7,10},{8,5},{9,4},... | collective-permute-start | bytes 196616 | tf_op jit(solution)/shard_map/ppermute | solution.py:200
  161.9 7.6 %collective-permute-start.36 = (bf16[4,64,128]{2,1,0:T(8,128)(2,1)S(1)}, bf16[4,64,128]{2,1,0:T(8,128)(2,1)S(1)}, u32[]{:S(2)}, u32[]{:S(2)}) collective-permute-start(bf16[4,64,128]{2,1,0:T(8,128)(2,1)S(1)} %get-tuple-element.135), channel_id=1, source_target_pairs={{0,4},{1,5},{2,6},{3,7},{4,0},{5,1},{6,2},{7,3},{8,12},{9,13},{10,... | collective-permute-start | bytes 196616 | tf_op jit(solution)/shard_map/ppermute | solution.py:200
  165.0 8.0 %collective-permute-start.37 = (bf16[4,64,128]{2,1,0:T(8,128)(2,1)S(1)}, bf16[4,64,128]{2,1,0:T(8,128)(2,1)S(1)}, u32[]{:S(2)}, u32[]{:S(2)}) collective-permute-start(bf16[4,64,128]{2,1,0:T(8,128)(2,1)S(1)} %get-tuple-element.136), channel_id=1, source_target_pairs={{0,5},{1,4},{2,7},{3,6},{4,1},{5,0},{6,3},{7,2},{8,13},{9,12},{10,... | collective-permute-start | bytes 196616 | tf_op jit(solution)/shard_map/ppermute | solution.py:200
  166.6 8.2 %collective-permute-start.38 = (bf16[4,64,128]{2,1,0:T(8,128)(2,1)S(1)}, bf16[4,64,128]{2,1,0:T(8,128)(2,1)S(1)}, u32[]{:S(2)}, u32[]{:S(2)}) collective-permute-start(bf16[4,64,128]{2,1,0:T(8,128)(2,1)S(1)} %get-tuple-element.137), channel_id=1, source_target_pairs={{0,6},{1,7},{2,4},{3,5},{4,2},{5,3},{6,0},{7,1},{8,14},{9,15},{10,... | collective-permute-start | bytes 196616 | tf_op jit(solution)/shard_map/ppermute | solution.py:200
  166.6 8.7 %collective-permute-start.39 = (bf16[4,64,128]{2,1,0:T(8,128)(2,1)S(1)}, bf16[4,64,128]{2,1,0:T(8,128)(2,1)S(1)}, u32[]{:S(2)}, u32[]{:S(2)}) collective-permute-start(bf16[4,64,128]{2,1,0:T(8,128)(2,1)S(1)} %get-tuple-element.138), channel_id=1, source_target_pairs={{0,7},{1,6},{2,5},{3,4},{4,3},{5,2},{6,1},{7,0},{8,15},{9,14},{10,... | collective-permute-start | bytes 196616 | tf_op jit(solution)/shard_map/ppermute | solution.py:200
  169.5 8.6 %collective-permute-start.33 = (bf16[4,64,128]{2,1,0:T(8,128)(2,1)S(1)}, bf16[4,64,128]{2,1,0:T(8,128)(2,1)S(1)}, u32[]{:S(2)}, u32[]{:S(2)}) collective-permute-start(bf16[4,64,128]{2,1,0:T(8,128)(2,1)S(1)} %get-tuple-element.132), channel_id=1, source_target_pairs={{0,1},{1,0},{2,3},{3,2},{4,5},{5,4},{6,7},{7,6},{8,9},{9,8},{10,11... | collective-permute-start | bytes 196616 | tf_op jit(solution)/shard_map/ppermute | solution.py:200
  169.5 10.3 %collective-permute-start.34 = (bf16[4,64,128]{2,1,0:T(8,128)(2,1)S(1)}, bf16[4,64,128]{2,1,0:T(8,128)(2,1)S(1)}, u32[]{:S(2)}, u32[]{:S(2)}) collective-permute-start(bf16[4,64,128]{2,1,0:T(8,128)(2,1)S(1)} %get-tuple-element.133), channel_id=1, source_target_pairs={{0,2},{1,3},{2,0},{3,1},{4,6},{5,7},{6,4},{7,5},{8,10},{9,11},{10,... | collective-permute-start | bytes 196616 | tf_op jit(solution)/shard_map/ppermute | solution.py:200
  172.9 9.9 %collective-permute-start.35 = (bf16[4,64,128]{2,1,0:T(8,128)(2,1)S(1)}, bf16[4,64,128]{2,1,0:T(8,128)(2,1)S(1)}, u32[]{:S(2)}, u32[]{:S(2)}) collective-permute-start(bf16[4,64,128]{2,1,0:T(8,128)(2,1)S(1)} %get-tuple-element.134), channel_id=1, source_target_pairs={{0,3},{1,2},{2,1},{3,0},{4,7},{5,6},{6,5},{7,4},{8,11},{9,10},{10,... | collective-permute-start | bytes 196616 | tf_op jit(solution)/shard_map/ppermute | solution.py:200
  174.8 8.4 %collective-permute-start.46 = (bf16[4,64,128]{2,1,0:T(8,128)(2,1)S(1)}, bf16[4,64,128]{2,1,0:T(8,128)(2,1)S(1)}, u32[]{:S(2)}, u32[]{:S(2)}) collective-permute-start(bf16[4,64,128]{2,1,0:T(8,128)(2,1)S(1)} %get-tuple-element.149), channel_id=1, source_target_pairs={{0,10},{1,11},{2,8},{3,9},{4,14},{5,15},{6,12},{7,13},{8,2},{9,3},... | collective-permute-start | bytes 196616 | tf_op jit(solution)/shard_map/ppermute | solution.py:200
  175.3 12.1 %collective-permute-start.47 = (bf16[4,64,128]{2,1,0:T(8,128)(2,1)S(1)}, bf16[4,64,128]{2,1,0:T(8,128)(2,1)S(1)}, u32[]{:S(2)}, u32[]{:S(2)}) collective-permute-start(bf16[4,64,128]{2,1,0:T(8,128)(2,1)S(1)} %get-tuple-element.150), channel_id=1, source_target_pairs={{0,11},{1,10},{2,9},{3,8},{4,15},{5,14},{6,13},{7,12},{8,3},{9,2},... | collective-permute-start | bytes 196616 | tf_op jit(solution)/shard_map/ppermute | solution.py:200
  178.0 9.4 %collective-permute-start.50 = (bf16[4,64,128]{2,1,0:T(8,128)(2,1)S(1)}, bf16[4,64,128]{2,1,0:T(8,128)(2,1)S(1)}, u32[]{:S(2)}, u32[]{:S(2)}) collective-permute-start(bf16[4,64,128]{2,1,0:T(8,128)(2,1)S(1)} %get-tuple-element.153), channel_id=1, source_target_pairs={{0,14},{1,15},{2,12},{3,13},{4,10},{5,11},{6,8},{7,9},{8,6},{9,7},... | collective-permute-start | bytes 196616 | tf_op jit(solution)/shard_map/ppermute | solution.py:200
  179.8 7.7 %collective-permute-start.51 = (bf16[4,64,128]{2,1,0:T(8,128)(2,1)S(1)}, bf16[4,64,128]{2,1,0:T(8,128)(2,1)S(1)}, u32[]{:S(2)}, u32[]{:S(2)}) collective-permute-start(bf16[4,64,128]{2,1,0:T(8,128)(2,1)S(1)} %get-tuple-element.154), channel_id=1, source_target_pairs={{0,15},{1,14},{2,13},{3,12},{4,11},{5,10},{6,9},{7,8},{8,7},{9,6},... | collective-permute-start | bytes 196616 | tf_op jit(solution)/shard_map/ppermute | solution.py:200
  (12 other events, 42.0 us)

commit v5 on v4

--- a/solution.py
+++ b/solution.py
@@ -46,10 +46,12 @@
             outs[k][2] = q_ref[here]
 
 
-def unpack_kernel(devs, pairs, me_ref, *refs):
-    ins, out = refs[:devs], refs[devs]
-    for k in range(devs):
-        out[pl.ds((me_ref[0] ^ k) * pairs, pairs)] = ins[k][...]
+def unpack_kernel(devs, pairs, order, me_ref, *refs):
+    ins, crossed, out = refs[: len(order)], refs[len(order) : -1], refs[-1]
+    for i, k in enumerate(order):
+        out[pl.ds((me_ref[0] ^ k) * pairs, pairs)] = ins[i][0]
+        size = crossed[0].shape[0]
+        out[pl.ds((me_ref[0] ^ 1 ^ k) * pairs, pairs)] = crossed[i // size][i % size]
 
 
 def pick_kernel(
@@ -166,8 +168,8 @@
         total = jnp.sum(weights, axis=1, keepdims=True)
         mixed = jnp.dot(weights.astype(jnp.bfloat16), vals, preferred_element_type=jnp.float32)
         out = (mixed / total).astype(jnp.bfloat16)
-        for i in range(block):
-            out_refs[b + i][...] = out[i * toks : (i + 1) * toks]
+        for i in range(b, b + block):
+            out_refs[i // 2][i % 2] = out[(i - b) * toks : (i - b + 1) * toks]
 
 
 def body(
@@ -210,29 +212,6 @@
     ahead = plain[: 3 * len(plain) // 4]
     behind = plain[3 * len(plain) // 4 :]
 
-    sizes = [(2 if k in crossed else 3, pairs, toks, width) for k in everyone]
-    sizes += [(1, pairs, toks, width) for k in crossed]
-    packed = pl.pallas_call(
-        functools.partial(pack_kernel, devs, pairs, crossed),
-        in_specs=[SMEM, VMEM, VMEM, VMEM],
-        out_specs=[VMEM] * len(sizes),
-        out_shape=[jax.ShapeDtypeStruct(s, jnp.bfloat16) for s in sizes],
-        compiler_params=pltpu.CompilerParams(vmem_limit_bytes=40 << 20),
-        cost_estimate=pl.CostEstimate(
-            flops=0, bytes_accessed=12 * pairs * length * width, transcendentals=0
-        ),
-        name="pack",
-    )(me, *(t.reshape(-1, toks, width) for t in (projected_keys, values, queries)))
-    blocks = list(packed[:devs])
-    late = dict(zip(crossed, packed[devs:]))
-
-    def send(ks, *others):
-        for k in ks:
-            blocks[k] = swap(after(blocks[k], *others) if others else blocks[k], k)
-
-    def got(ks):
-        return [blocks[k] for k in ks]
-
     steps = [devs >> (i + 1) for i in range(bits)] + [1]
     piece_shapes = [(h, tiles * rows, LANES) for h in steps] + [
         (h, pairs * ranks, LANES) for h in steps
@@ -254,40 +233,66 @@
             transcendentals=0,
         ),
         name="pick_factors",
-    )(after(me, blocks[top]), adapter_store_row, requests, adapter_down_factors, adapter_up_factors)
+    )(me, adapter_store_row, requests, adapter_down_factors, adapter_up_factors)
     down_pieces, up_pieces = pieces[: bits + 1], pieces[bits + 1 :]
+
+    sizes = [(2 if k in crossed else 3, pairs, toks, width) for k in everyone]
+    sizes += [(1, pairs, toks, width) for k in crossed]
+    packed = pl.pallas_call(
+        functools.partial(pack_kernel, devs, pairs, crossed),
+        in_specs=[SMEM, VMEM, VMEM, VMEM],
+        out_specs=[VMEM] * len(sizes),
+        out_shape=[jax.ShapeDtypeStruct(s, jnp.bfloat16) for s in sizes],
+        compiler_params=pltpu.CompilerParams(vmem_limit_bytes=40 << 20),
+        cost_estimate=pl.CostEstimate(
+            flops=0, bytes_accessed=12 * pairs * length * width, transcendentals=0
+        ),
+        name="pack",
+    )(after(me, pieces[0]), *(t.reshape(-1, toks, width) for t in (projected_keys, values, queries)))
+    blocks = list(packed[:devs])
+    late = dict(zip(crossed, packed[devs:]))
+
+    def send(ks, *others):
+        for k in ks:
+            blocks[k] = swap(after(blocks[k], *others) if others else blocks[k], k)
+
+    def got(ks):
+        return [blocks[k] for k in ks]
 
     def halving(parts, received, i):
         h = devs >> (i + 1) if i < bits else 0
         size = max(h, 1)
         return sum((r[h : h + size] for r in received), parts[i])
 
-    send(ahead)
+    ahead, behind = plain[: len(plain) // 2], plain[len(plain) // 2 :]
     down_got, up_got = [], []
     for i in range(bits):
         piece = halving(down_pieces, down_got, i)
-        if i == min(2, bits - 1):
-            piece = after(piece, *got(ahead[:-1]))
-            send(near, down_got[-1])
+        if i == 1:
+            send(ahead)
+        if i == bits - 2:
+            piece = after(piece, *got(ahead[: len(ahead) // 2]))
         if i == bits - 1:
             piece = after(piece, *got(ahead))
+            send(near, down_got[-1])
+            for j in range(2):
+                part = after(halving(up_pieces, up_got, j), down_got[-1])
+                up_got.append(swap(part, 1 << j))
         down_got.append(swap(piece, 1 << i))
     gathered = halving(down_pieces, down_got, bits)
-    for i in range(2):
-        piece = after(halving(up_pieces, up_got, i), down_got[min(i + 1, bits - 1)])
-        up_got.append(swap(piece, 1 << i))
-    gathered = after(gathered, *got(near), *up_got)
     for i in reversed(range(bits)):
         if i == bits - 2:
-            send(behind, gathered)
+            gathered = after(gathered, *got(near[:2]))
+            send(behind[: len(behind) // 2], gathered)
         if i == 1:
-            send(crossed[: len(crossed) // 2], gathered)
+            gathered = after(gathered, *got(near), *up_got)
+            send(behind[len(behind) // 2 :], gathered)
+            send(side[: len(side) // 4], gathered)
         if i == 0:
-            gathered = after(gathered, *got(behind))
-            send(crossed[len(crossed) // 2 :], gathered)
-            send(side[: len(side) // 2], gathered)
+            gathered = after(gathered, *got(behind[: len(behind) // 2]))
+            send(crossed[: len(crossed) // 4], gathered)
         gathered = jnp.concatenate([gathered, swap(gathered, 1 << i)], axis=0)
-    gathered = after(gathered, *got(crossed[: len(crossed) // 2]))
+    gathered = after(gathered, *got(behind))
 
     low = pl.pallas_call(
         functools.partial(low_rank_kernel, shape),
@@ -303,20 +308,22 @@
         ),
         name="low_rank",
     )(me, normed_token_features, gathered)
-    send(side[len(side) // 2 :], low)
+    send(crossed[len(crossed) // 4 : len(crossed) // 2], low)
     far = jnp.stack([low] + [swap(low, LOW * i) for i in range(1, devs // LOW)])
+    far = after(far, *got(crossed[: len(crossed) // 4]), *got(side[: len(side) // 4]))
+    send(crossed[len(crossed) // 2 :], far)
+    send(side[len(side) // 4 :], far)
     for i in range(2, bits):
         piece = after(halving(up_pieces, up_got, i), low)
         up_got.append(swap(piece, 1 << i))
     up_here = halving(up_pieces, up_got, bits).reshape(pairs, ranks, LANES)
-    far = after(far, *got(crossed[len(crossed) // 2 :]))
+    lows = [far] + [swap(far, i) for i in range(1, LOW)]
     late = {k: swap(after(late[k], far), k) for k in crossed}
-    lows = [far] + [swap(far, i) for i in range(1, LOW)]
 
     low_specs = [pl.BlockSpec((devs // LOW, toks, videos * ranks), lambda p: (0, 0, 0))] * LOW
     up_spec = pl.BlockSpec((pl.squeezed, ranks, LANES), lambda p: (p, 0, 0))
     all_spec = pl.BlockSpec((pl.squeezed, length, width), lambda p: (p, 0, 0))
-    part_spec = pl.BlockSpec((pl.squeezed, toks, width), lambda p: (p, 0, 0))
+    pair_spec = pl.BlockSpec((2, pl.squeezed, toks, width), lambda p: (0, p, 0, 0))
     keys, vals = pl.pallas_call(
         functools.partial(prepare_kernel, devs, per_video),
         grid=(pairs,),
@@ -337,7 +344,7 @@
         first = 0 if k in late else 2
         return pl.BlockSpec((pl.squeezed, pl.squeezed, toks, width), lambda p: (first, p, 0, 0))
 
-    def attend(ks):
+    def attend(ks, me):
         count = len(ks)
         return pl.pallas_call(
             functools.partial(
@@ -345,8 +352,8 @@
             ),
             grid=(pairs,),
             in_specs=[SMEM, up_spec, all_spec, all_spec, *low_specs] + [query_spec(k) for k in ks],
-            out_specs=[part_spec] * count,
-            out_shape=[jax.ShapeDtypeStruct((pairs, toks, width), jnp.bfloat16)] * count,
+            out_specs=[pair_spec] * (count // 2),
+            out_shape=[jax.ShapeDtypeStruct((2, pairs, toks, width), jnp.bfloat16)] * (count // 2),
             compiler_params=pltpu.CompilerParams(vmem_limit_bytes=40 << 20),
             cost_estimate=pl.CostEstimate(
                 flops=4 * pairs * count * toks * length * width,
@@ -356,14 +363,21 @@
             name="attend",
         )(me, up_here, keys, vals, *lows, *(late.get(k, blocks[k]) for k in ks))
 
-    back = [None] * devs
+    order, back, across = [], [], []
+    turn = me
     for ks in (plain, crossed, side, [0] + near):
-        for k, out in zip(ks, attend(ks)):
-            back[k] = swap(out, k) if k else out
+        outs = attend(ks, turn)
+        turn = after(me, outs[0])
+        for k, out in zip(ks[::2], outs):
+            order.append(k)
+            back.append(swap(out, k) if k else out)
+    half = len(order) // 2
+    for part in (back[:half], back[half:]):
+        across.append(swap(jnp.stack([t[1] for t in part]), 1))
 
     out = pl.pallas_call(
-        functools.partial(unpack_kernel, devs, pairs),
-        in_specs=[SMEM] + [VMEM] * devs,
+        functools.partial(unpack_kernel, devs, pairs, order),
+        in_specs=[SMEM] + [VMEM] * (len(back) + len(across)),
         out_specs=VMEM,
         out_shape=jax.ShapeDtypeStruct((devs * pairs, toks, width), jnp.bfloat16),
         compiler_params=pltpu.CompilerParams(vmem_limit_bytes=24 << 20),
@@ -371,7 +385,7 @@
             flops=0, bytes_accessed=4 * pairs * length * width, transcendentals=0
         ),
         name="unpack",
-    )(me, *back)
+    )(me, *back, *across)
     return out.reshape(videos, heads, toks, width)
 
 

time: 190 us -> 177 us (0.932)
  waiting for transfers between devices: 94.5 us -> 78 us
  starting transfers between devices: 69 us -> 75.1 us
  local copies, waits for them, and re-layouts: 6.87 us -> 4.7 us
    ppermute x52 -> x46, waiting for transfers between devices: 94.5 us -> 78 us  [swap(): return lax.ppermute(tensor, 'seq', [(i, i ^ k) for i in everyone])]
    ppermute x52 -> x46, starting transfers between devices: 69 us -> 75.1 us  [swap(): return lax.ppermute(tensor, 'seq', [(i, i ^ k) for i in everyone])]
    unnamed x17 -> x16, local copies, waits for them, and re-layouts: 6.82 us -> 4.65 us
  transfers between devices with their start and end apart: 52 -> 46, of which waited for: 18 -> 22; matrix products, arithmetic and copies ran while one was open for 0% -> 0% of each run, Pallas kernels for 7% -> 7%
where the time goes in v5:
time: 177 us; the launch traced here: 176 us
  waiting for transfers between devices  78 us (44%)
  starting transfers between devices  75.1 us (42%)
  Pallas kernels  17.6 us (10%)
  local copies, waits for them, and re-layouts  4.7 us (3%)
    ppermute x46, waiting for transfers between devices, swap(): return lax.ppermute(tensor, 'seq', [(i, i ^ k) for i in everyone])  78 us
    ppermute x46, starting transfers between devices, swap(): return lax.ppermute(tensor, 'seq', [(i, i ^ k) for i in everyone])  75.1 us
    pallas_call x4, Pallas kernels, attend(): pl.pallas_call(functools.partial(attend_kernel, ks, math.gcd(count, max(1...  12.6 us
    unnamed x16, local copies, waits for them, and re-layouts  4.65 us
  transfers between devices with their start and end apart: 46, of which 22 were waited for; matrix products, arithmetic and copies ran while one was open for 0% of the time, Pallas kernels for 7%

profile of v5, /device:TPU:1, one launch (start us, length us, event | category | flops | bytes accessed | tf_op | source)
XLA Modules:
  0.0 176.3 jit_solution(7850658240791732613)
XLA Ops:
  0.0 1.7 copy-done
  1.7 1.6 copy-done.1
  4.7 1.5 pick_factors.1
  6.3 2.0 %collective-permute-done = bf16[8,320,128]{2,1,0:T(8,128)(2,1)S(1)} collective-permute-done((bf16[8,320,128]{2,1,0:T(8,128)(2,1)S(1)}, bf16[8,320,128]{2,1,0:T(8,128)(2,1)S(1)}, u32[]{:S(2)}, u32[]{:S(2)}) %collective-permute-start) | collective-permute-done | bytes 655392 | tf_op jit(solution)/shard_map/ppermute | solution.py:202
  8.4 2.6 %collective-permute-start.1 = (bf16[4,320,128]{2,1,0:T(8,128)(2,1)S(1)}, bf16[4,320,128]{2,1,0:T(8,128)(2,1)S(1)}, u32[]{:S(2)}, u32[]{:S(2)}) collective-permute-start(bf16[4,320,128]{2,1,0:T(8,128)(2,1)S(1)} %slice_add_fusion), channel_id=1, source_target_pairs={{0,2},{1,3},{2,0},{3,1},{4,6},{5,7},{6,4},{7,5},{8,10},{9,11},{10,... | collective-permute-start | bytes 983048 | tf_op jit(solution)/shard_map/ppermute | solution.py:202
  11.2 2.2 %collective-permute-start.2 = (bf16[3,4,64,128]{3,2,1,0:T(8,128)(2,1)S(1)}, bf16[3,4,64,128]{3,2,1,0:T(8,128)(2,1)S(1)}, u32[]{:S(2)}, u32[]{:S(2)}) collective-permute-start(bf16[3,4,64,128]{3,2,1,0:T(8,128)(2,1)S(1)} %get-tuple-element.83), channel_id=1, source_target_pairs={{0,8},{1,9},{2,10},{3,11},{4,12},{5,13},{6,14},{7,15},{8,0},{9,1},... | collective-permute-start | bytes 589832 | tf_op jit(solution)/shard_map/ppermute | solution.py:202
  13.4 5.3 %collective-permute-done.1 = bf16[4,320,128]{2,1,0:T(8,128)(2,1)S(1)} collective-permute-done((bf16[4,320,128]{2,1,0:T(8,128)(2,1)S(1)}, bf16[4,320,128]{2,1,0:T(8,128)(2,1)S(1)}, u32[]{:S(2)}, u32[]{:S(2)}) %collective-permute-start.1) | collective-permute-done | bytes 327712 | tf_op jit(solution)/shard_map/ppermute | solution.py:202
  18.8 3.6 %collective-permute-done.2.refs_12_.refs_4_ = bf16[3,4,64,128]{3,2,1,0:T(8,128)(2,1)S(1)} collective-permute-done((bf16[3,4,64,128]{3,2,1,0:T(8,128)(2,1)S(1)}, bf16[3,4,64,128]{3,2,1,0:T(8,128)(2,1)S(1)}, u32[]{:S(2)}, u32[]{:S(2)}) %collective-permute-start.2) | collective-permute-done | bytes 196640 | tf_op jit(solution)/shard_map/ppermute | solution.py:202
  22.4 1.1 collective-permute-start.3
  23.4 3.8 %collective-permute-start.6 = (bf16[3,4,64,128]{3,2,1,0:T(8,128)(2,1)S(1)}, bf16[3,4,64,128]{3,2,1,0:T(8,128)(2,1)S(1)}, u32[]{:S(2)}, u32[]{:S(2)}) collective-permute-start(bf16[3,4,64,128]{3,2,1,0:T(8,128)(2,1)S(1)} %get-tuple-element.91), channel_id=1, source_target_pairs={{0,9},{1,8},{2,11},{3,10},{4,13},{5,12},{6,15},{7,14},{8,1},{9,0},... | collective-permute-start | bytes 589832 | tf_op jit(solution)/shard_map/ppermute | solution.py:202
  27.2 5.1 %collective-permute-start.4 = (bf16[8,256,128]{2,1,0:T(8,128)(2,1)S(1)}, bf16[8,256,128]{2,1,0:T(8,128)(2,1)S(1)}, u32[]{:S(2)}, u32[]{:S(2)}) collective-permute-start(bf16[8,256,128]{2,1,0:T(8,128)(2,1)S(1)} %get-tuple-element.85), channel_id=1, source_target_pairs={{0,1},{1,0},{2,3},{3,2},{4,5},{5,4},{6,7},{7,6},{8,9},{9,8},{10,11... | collective-permute-start | bytes 1572872 | tf_op jit(solution)/shard_map/ppermute | solution.py:202
  32.3 3.6 %collective-permute-done.6.refs_13_.refs_5_ = bf16[3,4,64,128]{3,2,1,0:T(8,128)(2,1)S(1)} collective-permute-done((bf16[3,4,64,128]{3,2,1,0:T(8,128)(2,1)S(1)}, bf16[3,4,64,128]{3,2,1,0:T(8,128)(2,1)S(1)}, u32[]{:S(2)}, u32[]{:S(2)}) %collective-permute-start.6) | collective-permute-done | bytes 196640 | tf_op jit(solution)/shard_map/ppermute | solution.py:202
  36.0 5.9 %collective-permute-done.7 = bf16[1,320,128]{2,1,0:T(8,128)(2,1)S(1)} collective-permute-done((bf16[1,320,128]{2,1,0:T(8,128)(2,1)S(1)}, bf16[1,320,128]{2,1,0:T(8,128)(2,1)S(1)}, u32[]{:S(2)}, u32[]{:S(2)}) %collective-permute-start.7) | collective-permute-done | bytes 81952 | tf_op jit(solution)/shard_map/ppermute | solution.py:202
  42.4 4.7 %collective-permute-done.8 = bf16[1,320,128]{2,1,0:T(8,128)(2,1)S(1)} collective-permute-done((bf16[1,320,128]{2,1,0:T(8,128)(2,1)S(1)}, bf16[1,320,128]{2,1,0:T(8,128)(2,1)S(1)}, u32[]{:S(2)}, u32[]{:S(2)}) %collective-permute-start.8) | collective-permute-done | bytes 81952 | tf_op jit(solution)/shard_map/ppermute | solution.py:202
  47.1 1.1 collective-permute-done.10.refs_6_
  48.2 3.4 %collective-permute-start.11 = (bf16[2,320,128]{2,1,0:T(8,128)(2,1)S(1)}, bf16[2,320,128]{2,1,0:T(8,128)(2,1)S(1)}, u32[]{:S(2)}, u32[]{:S(2)}) collective-permute-start(bf16[2,320,128]{2,1,0:T(8,128)(2,1)S(1)} %pad_maximum_fusion.5), channel_id=1, source_target_pairs={{0,4},{1,5},{2,6},{3,7},{4,0},{5,1},{6,2},{7,3},{8,12},{9,13},{10,... | collective-permute-start | bytes 491528 | tf_op jit(solution)/shard_map/ppermute | solution.py:202
  51.9 2.5 %collective-permute-start.12 = (bf16[3,4,64,128]{3,2,1,0:T(8,128)(2,1)S(1)}, bf16[3,4,64,128]{3,2,1,0:T(8,128)(2,1)S(1)}, u32[]{:S(2)}, u32[]{:S(2)}) collective-permute-start(bf16[3,4,64,128]{3,2,1,0:T(8,128)(2,1)S(1)} %get-tuple-element.99), channel_id=1, source_target_pairs={{0,3},{1,2},{2,1},{3,0},{4,7},{5,6},{6,5},{7,4},{8,11},{9,10},{10,... | collective-permute-start | bytes 589832 | tf_op jit(solution)/shard_map/ppermute | solution.py:202
  55.4 8.5 %collective-permute-done.12.refs_7_ = bf16[3,4,64,128]{3,2,1,0:T(8,128)(2,1)S(1)} collective-permute-done((bf16[3,4,64,128]{3,2,1,0:T(8,128)(2,1)S(1)}, bf16[3,4,64,128]{3,2,1,0:T(8,128)(2,1)S(1)}, u32[]{:S(2)}, u32[]{:S(2)}) %collective-permute-start.12) | collective-permute-done | bytes 196640 | tf_op jit(solution)/shard_map/ppermute | solution.py:202
  64.2 8.8 %collective-permute-done.13 = bf16[4,320,128]{2,1,0:T(8,128)(2,1)S(1)} collective-permute-done((bf16[4,320,128]{2,1,0:T(8,128)(2,1)S(1)}, bf16[4,320,128]{2,1,0:T(8,128)(2,1)S(1)}, u32[]{:S(2)}, u32[]{:S(2)}) %collective-permute-start.13) | collective-permute-done | bytes 327712 | tf_op jit(solution)/shard_map/ppermute | solution.py:202
  73.4 2.5 %collective-permute-start.23 = (bf16[3,4,64,128]{3,2,1,0:T(8,128)(2,1)S(1)}, bf16[3,4,64,128]{3,2,1,0:T(8,128)(2,1)S(1)}, u32[]{:S(2)}, u32[]{:S(2)}) collective-permute-start(bf16[3,4,64,128]{3,2,1,0:T(8,128)(2,1)S(1)} %get-tuple-element.113), channel_id=1, source_target_pairs={{0,4},{1,5},{2,6},{3,7},{4,0},{5,1},{6,2},{7,3},{8,12},{9,13},{10,... | collective-permute-start | bytes 589832 | tf_op jit(solution)/shard_map/ppermute | solution.py:202
  75.9 1.9 %collective-permute-start.22 = (bf16[2,4,64,128]{3,2,1,0:T(8,128)(2,1)S(1)}, bf16[2,4,64,128]{3,2,1,0:T(8,128)(2,1)S(1)}, u32[]{:S(2)}, u32[]{:S(2)}) collective-permute-start(bf16[2,4,64,128]{3,2,1,0:T(8,128)(2,1)S(1)} %get-tuple-element.111), channel_id=1, source_target_pairs={{0,10},{1,11},{2,8},{3,9},{4,14},{5,15},{6,12},{7,13},{8,2},{9,3},... | collective-permute-start | bytes 393224 | tf_op jit(solution)/shard_map/ppermute | solution.py:202
  77.8 4.5 %collective-permute-done.16.refs_17_.refs_7_ = bf16[3,4,64,128]{3,2,1,0:T(8,128)(2,1)S(1)} collective-permute-done((bf16[3,4,64,128]{3,2,1,0:T(8,128)(2,1)S(1)}, bf16[3,4,64,128]{3,2,1,0:T(8,128)(2,1)S(1)}, u32[]{:S(2)}, u32[]{:S(2)}) %collective-permute-start.16) | collective-permute-done | bytes 196640 | tf_op jit(solution)/shard_map/ppermute | solution.py:202
  83.3 5.7 %collective-permute-start.20 = (bf16[64,128]{1,0:T(8,128)(2,1)S(1)}, bf16[64,128]{1,0:T(8,128)(2,1)S(1)}, u32[]{:S(2)}, u32[]{:S(2)}) collective-permute-start(bf16[64,128]{1,0:T(8,128)(2,1)S(1)} %low_rank.1), channel_id=1, source_target_pairs={{0,8},{1,9},{2,10},{3,11},{4,12},{5,13},{6,14},{7,15},{8,0},{9,1},... | collective-permute-start | bytes 49160 | tf_op jit(solution)/shard_map/ppermute | solution.py:202
  89.2 4.1 %collective-permute-start.17 = (bf16[2,256,128]{2,1,0:T(8,128)(2,1)S(1)}, bf16[2,256,128]{2,1,0:T(8,128)(2,1)S(1)}, u32[]{:S(2)}, u32[]{:S(2)}) collective-permute-start(bf16[2,256,128]{2,1,0:T(8,128)(2,1)S(1)} %slice_add_fusion.4), channel_id=1, source_target_pairs={{0,4},{1,5},{2,6},{3,7},{4,0},{5,1},{6,2},{7,3},{8,12},{9,13},{10,... | collective-permute-start | bytes 393224 | tf_op jit(solution)/shard_map/ppermute | solution.py:202
  93.4 1.6 collective-permute-start.26
  95.6 1.4 collective-permute-start.30
  97.0 1.1 collective-permute-done.26.refs_3_
  99.5 3.4 %collective-permute-start.32 = (bf16[2,4,64,128]{3,2,1,0:T(8,128)(2,1)S(1)}, bf16[2,4,64,128]{3,2,1,0:T(8,128)(2,1)S(1)}, u32[]{:S(2)}, u32[]{:S(2)}) collective-permute-start(bf16[2,4,64,128]{3,2,1,0:T(8,128)(2,1)S(1)} %get-tuple-element.127), channel_id=1, source_target_pairs={{0,15},{1,14},{2,13},{3,12},{4,11},{5,10},{6,9},{7,8},{8,7},{9,6},... | collective-permute-start | bytes 393224 | tf_op jit(solution)/shard_map/ppermute | solution.py:202
  102.9 1.7 collective-permute-start.28
  104.7 6.5 %collective-permute-done.30.refs_15_ = bf16[2,4,64,128]{3,2,1,0:T(8,128)(2,1)S(1)} collective-permute-done((bf16[2,4,64,128]{3,2,1,0:T(8,128)(2,1)S(1)}, bf16[2,4,64,128]{3,2,1,0:T(8,128)(2,1)S(1)}, u32[]{:S(2)}, u32[]{:S(2)}) %collective-permute-start.30) | collective-permute-done | bytes 131104 | tf_op jit(solution)/shard_map/ppermute | solution.py:202
  111.1 3.8 %collective-permute-start.35 = (bf16[1,4,64,128]{3,2,1,0:T(8,128)(2,1)S(1)}, bf16[1,4,64,128]{3,2,1,0:T(8,128)(2,1)S(1)}, u32[]{:S(2)}, u32[]{:S(2)}) collective-permute-start(bf16[1,4,64,128]{3,2,1,0:T(8,128)(2,1)S(1)} %get-tuple-element.134), channel_id=1, source_target_pairs={{0,10},{1,11},{2,8},{3,9},{4,14},{5,15},{6,12},{7,13},{8,2},{9,3},... | collective-permute-start | bytes 196616 | tf_op jit(solution)/shard_map/ppermute | solution.py:202
  114.9 6.2 %collective-permute-start.36 = (bf16[1,4,64,128]{3,2,1,0:T(8,128)(2,1)S(1)}, bf16[1,4,64,128]{3,2,1,0:T(8,128)(2,1)S(1)}, u32[]{:S(2)}, u32[]{:S(2)}) collective-permute-start(bf16[1,4,64,128]{3,2,1,0:T(8,128)(2,1)S(1)} %get-tuple-element.136), channel_id=1, source_target_pairs={{0,11},{1,10},{2,9},{3,8},{4,15},{5,14},{6,13},{7,12},{8,3},{9,2},... | collective-permute-start | bytes 196616 | tf_op jit(solution)/shard_map/ppermute | solution.py:202
  121.1 2.2 %collective-permute-done.18 = bf16[1,256,128]{2,1,0:T(8,128)(2,1)S(1)} collective-permute-done((bf16[1,256,128]{2,1,0:T(8,128)(2,1)S(1)}, bf16[1,256,128]{2,1,0:T(8,128)(2,1)S(1)}, u32[]{:S(2)}, u32[]{:S(2)}) %collective-permute-start.18) | collective-permute-done | bytes 65568 | tf_op jit(solution)/shard_map/ppermute | solution.py:202
  124.1 4.0 %collective-permute-start.38 = (bf16[1,4,64,128]{3,2,1,0:T(8,128)(2,1)S(1)}, bf16[1,4,64,128]{3,2,1,0:T(8,128)(2,1)S(1)}, u32[]{:S(2)}, u32[]{:S(2)}) collective-permute-start(bf16[1,4,64,128]{3,2,1,0:T(8,128)(2,1)S(1)} %get-tuple-element.140), channel_id=1, source_target_pairs={{0,15},{1,14},{2,13},{3,12},{4,11},{5,10},{6,9},{7,8},{8,7},{9,6},... | collective-permute-start | bytes 196616 | tf_op jit(solution)/shard_map/ppermute | solution.py:202
  128.1 7.7 %collective-permute-done.29.refs_11_.refs_7_ = bf16[3,4,64,128]{3,2,1,0:T(8,128)(2,1)S(1)} collective-permute-done((bf16[3,4,64,128]{3,2,1,0:T(8,128)(2,1)S(1)}, bf16[3,4,64,128]{3,2,1,0:T(8,128)(2,1)S(1)}, u32[]{:S(2)}, u32[]{:S(2)}) %collective-permute-start.29) | collective-permute-done | bytes 196640 | tf_op jit(solution)/shard_map/ppermute | solution.py:202
  135.8 1.4 prepare.1
  137.2 3.2 %attend.4 = (bf16[2,4,64,128]{3,2,1,0:T(8,128)(2,1)S(1)}, bf16[2,4,64,128]{3,2,1,0:T(8,128)(2,1)S(1)}) custom-call(s32[1]{0:T(128)} %bitcast.me_ref, bf16[4,64,128]{2,1,0:T(8,128)(2,1)S(1)} %bitcast.11, bf16[4,1024,128]{2,1,0:T(8,128)(2,1)S(1)} %get-tuple-element.128.k_ref, bf16[4,1024,128]{2,1,0:T(8,128)(2,1)S(1)} %get-tuple-element.129.v_ref, ...), custom_call_target="tpu_custom_call" | custom-call | flops 536870912 | bytes 2621440 | tf_op jit(solution)/shard_map/attend/pallas_call | solution.py:349
  140.4 3.2 %attend.5 = (bf16[2,4,64,128]{3,2,1,0:T(8,128)(2,1)S(1)}, bf16[2,4,64,128]{3,2,1,0:T(8,128)(2,1)S(1)}) custom-call(s32[1]{0:T(128)} %bitcast.me_ref, bf16[4,64,128]{2,1,0:T(8,128)(2,1)S(1)} %bitcast.12, bf16[4,1024,128]{2,1,0:T(8,128)(2,1)S(1)} %get-tuple-element.128.k_ref, bf16[4,1024,128]{2,1,0:T(8,128)(2,1)S(1)} %get-tuple-element.129.v_ref, ...), custom_call_target="tpu_custom_call" | custom-call | flops 536870912 | bytes 2621440 | tf_op jit(solution)/shard_map/attend/pallas_call | solution.py:349
  143.6 1.7 collective-permute-start.40
  145.3 1.9 %collective-permute-start.39 = (bf16[2,4,64,128]{3,2,1,0:T(8,128)(2,1)S(1)}, bf16[2,4,64,128]{3,2,1,0:T(8,128)(2,1)S(1)}, u32[]{:S(2)}, u32[]{:S(2)}) collective-permute-start(bf16[2,4,64,128]{3,2,1,0:T(8,128)(2,1)S(1)} %get-tuple-element.141), channel_id=1, source_target_pairs={{0,10},{1,11},{2,8},{3,9},{4,14},{5,15},{6,12},{7,13},{8,2},{9,3},... | collective-permute-start | bytes 393224 | tf_op jit(solution)/shard_map/ppermute | solution.py:202
  147.2 1.3 collective-permute-start.34
  149.3 3.1 %attend.6 = (bf16[2,4,64,128]{3,2,1,0:T(8,128)(2,1)S(1)}, bf16[2,4,64,128]{3,2,1,0:T(8,128)(2,1)S(1)}) custom-call(s32[1]{0:T(128)} %bitcast.me_ref, bf16[4,64,128]{2,1,0:T(8,128)(2,1)S(1)} %bitcast.13, bf16[4,1024,128]{2,1,0:T(8,128)(2,1)S(1)} %get-tuple-element.128.k_ref, bf16[4,1024,128]{2,1,0:T(8,128)(2,1)S(1)} %get-tuple-element.129.v_ref, ...), custom_call_target="tpu_custom_call" | custom-call | flops 536870912 | bytes 2621440 | tf_op jit(solution)/shard_map/attend/pallas_call | solution.py:349
  152.4 3.2 %attend.7 = (bf16[2,4,64,128]{3,2,1,0:T(8,128)(2,1)S(1)}, bf16[2,4,64,128]{3,2,1,0:T(8,128)(2,1)S(1)}) custom-call(s32[1]{0:T(128)} %bitcast.me_ref, bf16[4,64,128]{2,1,0:T(8,128)(2,1)S(1)} %bitcast.14, bf16[4,1024,128]{2,1,0:T(8,128)(2,1)S(1)} %get-tuple-element.128.k_ref, bf16[4,1024,128]{2,1,0:T(8,128)(2,1)S(1)} %get-tuple-element.129.v_ref, ...), custom_call_target="tpu_custom_call" | custom-call | flops 536870912 | bytes 2621440 | tf_op jit(solution)/shard_map/attend/pallas_call | solution.py:349
  156.1 7.4 %collective-permute-start.42 = (bf16[2,4,64,128]{3,2,1,0:T(8,128)(2,1)S(1)}, bf16[2,4,64,128]{3,2,1,0:T(8,128)(2,1)S(1)}, u32[]{:S(2)}, u32[]{:S(2)}) collective-permute-start(bf16[2,4,64,128]{3,2,1,0:T(8,128)(2,1)S(1)} %get-tuple-element.145), channel_id=1, source_target_pairs={{0,6},{1,7},{2,4},{3,5},{4,2},{5,3},{6,0},{7,1},{8,14},{9,15},{10,... | collective-permute-start | bytes 393224 | tf_op jit(solution)/shard_map/ppermute | solution.py:202
  163.4 1.2 collective-permute-done.39.refs_2_
  164.7 6.1 %collective-permute-done.33.refs_0_ = bf16[2,4,64,128]{3,2,1,0:T(8,128)(2,1)S(1)} collective-permute-done((bf16[2,4,64,128]{3,2,1,0:T(8,128)(2,1)S(1)}, bf16[2,4,64,128]{3,2,1,0:T(8,128)(2,1)S(1)}, u32[]{:S(2)}, u32[]{:S(2)}) %collective-permute-start.33) | collective-permute-done | bytes 131104 | tf_op jit(solution)/shard_map/ppermute | solution.py:202
  171.4 2.0 %collective-permute-done.41.refs_4_ = bf16[2,4,64,128]{3,2,1,0:T(8,128)(2,1)S(1)} collective-permute-done((bf16[2,4,64,128]{3,2,1,0:T(8,128)(2,1)S(1)}, bf16[2,4,64,128]{3,2,1,0:T(8,128)(2,1)S(1)}, u32[]{:S(2)}, u32[]{:S(2)}) %collective-permute-start.41) | collective-permute-done | bytes 131104 | tf_op jit(solution)/shard_map/ppermute | solution.py:202
  174.1 1.2 collective-permute-done.45.refs_9_
  (92 shorter events, 12.1 us)
Async XLA Ops:
  4.6 6.3 %copy-start.5 = (bf16[2,32,64,128]{3,2,1,0:T(8,128)(2,1)S(1)}, bf16[2,32,64,128]{3,2,1,0:T(8,128)(2,1)}, u32[]{:S(2)}) copy-start(bf16[2,32,64,128]{3,2,1,0:T(8,128)(2,1)} %param.9) | copy-start | bytes 3145732
  6.2 2.2 %collective-permute-start = (bf16[8,320,128]{2,1,0:T(8,128)(2,1)S(1)}, bf16[8,320,128]{2,1,0:T(8,128)(2,1)S(1)}, u32[]{:S(2)}, u32[]{:S(2)}) collective-permute-start(bf16[8,320,128]{2,1,0:T(8,128)(2,1)S(1)} %get-tuple-element.80), channel_id=1, source_target_pairs={{0,1},{1,0},{2,3},{3,2},{4,5},{5,4},{6,7},{7,6},{8,9},{9,8},{10,11... | collective-permute-start | bytes 1966088 | tf_op jit(solution)/shard_map/ppermute | solution.py:202
  8.4 10.4 %collective-permute-start.1 = (bf16[4,320,128]{2,1,0:T(8,128)(2,1)S(1)}, bf16[4,320,128]{2,1,0:T(8,128)(2,1)S(1)}, u32[]{:S(2)}, u32[]{:S(2)}) collective-permute-start(bf16[4,320,128]{2,1,0:T(8,128)(2,1)S(1)} %slice_add_fusion), channel_id=1, source_target_pairs={{0,2},{1,3},{2,0},{3,1},{4,6},{5,7},{6,4},{7,5},{8,10},{9,11},{10,... | collective-permute-start | bytes 983048 | tf_op jit(solution)/shard_map/ppermute | solution.py:202
  11.2 11.1 %collective-permute-start.2 = (bf16[3,4,64,128]{3,2,1,0:T(8,128)(2,1)S(1)}, bf16[3,4,64,128]{3,2,1,0:T(8,128)(2,1)S(1)}, u32[]{:S(2)}, u32[]{:S(2)}) collective-permute-start(bf16[3,4,64,128]{3,2,1,0:T(8,128)(2,1)S(1)} %get-tuple-element.83), channel_id=1, source_target_pairs={{0,8},{1,9},{2,10},{3,11},{4,12},{5,13},{6,14},{7,15},{8,0},{9,1},... | collective-permute-start | bytes 589832 | tf_op jit(solution)/shard_map/ppermute | solution.py:202
  22.4 4.8 %collective-permute-start.3 = (bf16[2,320,128]{2,1,0:T(8,128)(2,1)S(1)}, bf16[2,320,128]{2,1,0:T(8,128)(2,1)S(1)}, u32[]{:S(2)}, u32[]{:S(2)}) collective-permute-start(bf16[2,320,128]{2,1,0:T(8,128)(2,1)S(1)} %slice_add_fusion.2), channel_id=1, source_target_pairs={{0,4},{1,5},{2,6},{3,7},{4,0},{5,1},{6,2},{7,3},{8,12},{9,13},{10,... | collective-permute-start | bytes 491528 | tf_op jit(solution)/shard_map/ppermute | solution.py:202
  23.4 12.5 %collective-permute-start.6 = (bf16[3,4,64,128]{3,2,1,0:T(8,128)(2,1)S(1)}, bf16[3,4,64,128]{3,2,1,0:T(8,128)(2,1)S(1)}, u32[]{:S(2)}, u32[]{:S(2)}) collective-permute-start(bf16[3,4,64,128]{3,2,1,0:T(8,128)(2,1)S(1)} %get-tuple-element.91), channel_id=1, source_target_pairs={{0,9},{1,8},{2,11},{3,10},{4,13},{5,12},{6,15},{7,14},{8,1},{9,0},... | collective-permute-start | bytes 589832 | tf_op jit(solution)/shard_map/ppermute | solution.py:202
  27.2 24.4 %collective-permute-start.4 = (bf16[8,256,128]{2,1,0:T(8,128)(2,1)S(1)}, bf16[8,256,128]{2,1,0:T(8,128)(2,1)S(1)}, u32[]{:S(2)}, u32[]{:S(2)}) collective-permute-start(bf16[8,256,128]{2,1,0:T(8,128)(2,1)S(1)} %get-tuple-element.85), channel_id=1, source_target_pairs={{0,1},{1,0},{2,3},{3,2},{4,5},{5,4},{6,7},{7,6},{8,9},{9,8},{10,11... | collective-permute-start | bytes 1572872 | tf_op jit(solution)/shard_map/ppermute | solution.py:202
  36.0 5.9 %collective-permute-start.7 = (bf16[1,320,128]{2,1,0:T(8,128)(2,1)S(1)}, bf16[1,320,128]{2,1,0:T(8,128)(2,1)S(1)}, u32[]{:S(2)}, u32[]{:S(2)}) collective-permute-start(bf16[1,320,128]{2,1,0:T(8,128)(2,1)S(1)} %slice_add_fusion.6), channel_id=1, source_target_pairs={{0,8},{1,9},{2,10},{3,11},{4,12},{5,13},{6,14},{7,15},{8,0},{9,1},... | collective-permute-start | bytes 245768 | tf_op jit(solution)/shard_map/ppermute | solution.py:202
  41.9 5.2 %collective-permute-start.8 = (bf16[1,320,128]{2,1,0:T(8,128)(2,1)S(1)}, bf16[1,320,128]{2,1,0:T(8,128)(2,1)S(1)}, u32[]{:S(2)}, u32[]{:S(2)}) collective-permute-start(bf16[1,320,128]{2,1,0:T(8,128)(2,1)S(1)} %fusion), channel_id=1, source_target_pairs={{0,8},{1,9},{2,10},{3,11},{4,12},{5,13},{6,14},{7,15},{8,0},{9,1},... | collective-permute-start | bytes 245768 | tf_op jit(solution)/shard_map/ppermute | solution.py:202
  42.0 5.1 %collective-permute-start.9 = (bf16[3,4,64,128]{3,2,1,0:T(8,128)(2,1)S(1)}, bf16[3,4,64,128]{3,2,1,0:T(8,128)(2,1)S(1)}, u32[]{:S(2)}, u32[]{:S(2)}) collective-permute-start(bf16[3,4,64,128]{3,2,1,0:T(8,128)(2,1)S(1)} %get-tuple-element.94), channel_id=1, source_target_pairs={{0,1},{1,0},{2,3},{3,2},{4,5},{5,4},{6,7},{7,6},{8,9},{9,8},{10,11... | collective-permute-start | bytes 589832 | tf_op jit(solution)/shard_map/ppermute | solution.py:202
  42.1 6.1 %collective-permute-start.10 = (bf16[3,4,64,128]{3,2,1,0:T(8,128)(2,1)S(1)}, bf16[3,4,64,128]{3,2,1,0:T(8,128)(2,1)S(1)}, u32[]{:S(2)}, u32[]{:S(2)}) collective-permute-start(bf16[3,4,64,128]{3,2,1,0:T(8,128)(2,1)S(1)} %get-tuple-element.96), channel_id=1, source_target_pairs={{0,2},{1,3},{2,0},{3,1},{4,6},{5,7},{6,4},{7,5},{8,10},{9,11},{10,... | collective-permute-start | bytes 589832 | tf_op jit(solution)/shard_map/ppermute | solution.py:202
  48.2 7.2 %collective-permute-start.11 = (bf16[2,320,128]{2,1,0:T(8,128)(2,1)S(1)}, bf16[2,320,128]{2,1,0:T(8,128)(2,1)S(1)}, u32[]{:S(2)}, u32[]{:S(2)}) collective-permute-start(bf16[2,320,128]{2,1,0:T(8,128)(2,1)S(1)} %pad_maximum_fusion.5), channel_id=1, source_target_pairs={{0,4},{1,5},{2,6},{3,7},{4,0},{5,1},{6,2},{7,3},{8,12},{9,13},{10,... | collective-permute-start | bytes 491528 | tf_op jit(solution)/shard_map/ppermute | solution.py:202
  51.6 12.3 %collective-permute-start.5 = (bf16[4,256,128]{2,1,0:T(8,128)(2,1)S(1)}, bf16[4,256,128]{2,1,0:T(8,128)(2,1)S(1)}, u32[]{:S(2)}, u32[]{:S(2)}) collective-permute-start(bf16[4,256,128]{2,1,0:T(8,128)(2,1)S(1)} %slice_add_fusion.1), channel_id=1, source_target_pairs={{0,2},{1,3},{2,0},{3,1},{4,6},{5,7},{6,4},{7,5},{8,10},{9,11},{10,... | collective-permute-start | bytes 786440 | tf_op jit(solution)/shard_map/ppermute | solution.py:202
  51.9 12.0 %collective-permute-start.12 = (bf16[3,4,64,128]{3,2,1,0:T(8,128)(2,1)S(1)}, bf16[3,4,64,128]{3,2,1,0:T(8,128)(2,1)S(1)}, u32[]{:S(2)}, u32[]{:S(2)}) collective-permute-start(bf16[3,4,64,128]{3,2,1,0:T(8,128)(2,1)S(1)} %get-tuple-element.99), channel_id=1, source_target_pairs={{0,3},{1,2},{2,1},{3,0},{4,7},{5,6},{6,5},{7,4},{8,11},{9,10},{10,... | collective-permute-start | bytes 589832 | tf_op jit(solution)/shard_map/ppermute | solution.py:202
  63.9 9.0 %collective-permute-start.13 = (bf16[4,320,128]{2,1,0:T(8,128)(2,1)S(1)}, bf16[4,320,128]{2,1,0:T(8,128)(2,1)S(1)}, u32[]{:S(2)}, u32[]{:S(2)}) collective-permute-start(bf16[4,320,128]{2,1,0:T(8,128)(2,1)S(1)} %pad_maximum_fusion.2), channel_id=1, source_target_pairs={{0,2},{1,3},{2,0},{3,1},{4,6},{5,7},{6,4},{7,5},{8,10},{9,11},{10,... | collective-permute-start | bytes 983048 | tf_op jit(solution)/shard_map/ppermute | solution.py:202
  64.1 8.8 %collective-permute-start.14 = (bf16[3,4,64,128]{3,2,1,0:T(8,128)(2,1)S(1)}, bf16[3,4,64,128]{3,2,1,0:T(8,128)(2,1)S(1)}, u32[]{:S(2)}, u32[]{:S(2)}) collective-permute-start(bf16[3,4,64,128]{3,2,1,0:T(8,128)(2,1)S(1)} %get-tuple-element.102), channel_id=1, source_target_pairs={{0,12},{1,13},{2,14},{3,15},{4,8},{5,9},{6,10},{7,11},{8,4},{9,5},... | collective-permute-start | bytes 589832 | tf_op jit(solution)/shard_map/ppermute | solution.py:202
  73.0 4.7 %collective-permute-start.15 = (bf16[8,320,128]{2,1,0:T(8,128)(2,1)S(1)}, bf16[8,320,128]{2,1,0:T(8,128)(2,1)S(1)}, u32[]{:S(2)}, u32[]{:S(2)}) collective-permute-start(bf16[8,320,128]{2,1,0:T(8,128)(2,1)S(1)} %pad_maximum_fusion.1), channel_id=1, source_target_pairs={{0,1},{1,0},{2,3},{3,2},{4,5},{5,4},{6,7},{7,6},{8,9},{9,8},{10,11... | collective-permute-start | bytes 1966088 | tf_op jit(solution)/shard_map/ppermute | solution.py:202
  73.4 9.0 %collective-permute-start.16 = (bf16[3,4,64,128]{3,2,1,0:T(8,128)(2,1)S(1)}, bf16[3,4,64,128]{3,2,1,0:T(8,128)(2,1)S(1)}, u32[]{:S(2)}, u32[]{:S(2)}) collective-permute-start(bf16[3,4,64,128]{3,2,1,0:T(8,128)(2,1)S(1)} %get-tuple-element.105), channel_id=1, source_target_pairs={{0,13},{1,12},{2,15},{3,14},{4,9},{5,8},{6,11},{7,10},{8,5},{9,4},... | collective-permute-start | bytes 589832 | tf_op jit(solution)/shard_map/ppermute | solution.py:202
  73.4 20.0 %collective-permute-start.23 = (bf16[3,4,64,128]{3,2,1,0:T(8,128)(2,1)S(1)}, bf16[3,4,64,128]{3,2,1,0:T(8,128)(2,1)S(1)}, u32[]{:S(2)}, u32[]{:S(2)}) collective-permute-start(bf16[3,4,64,128]{3,2,1,0:T(8,128)(2,1)S(1)} %get-tuple-element.113), channel_id=1, source_target_pairs={{0,4},{1,5},{2,6},{3,7},{4,0},{5,1},{6,2},{7,3},{8,12},{9,13},{10,... | collective-permute-start | bytes 589832 | tf_op jit(solution)/shard_map/ppermute | solution.py:202
  75.9 6.5 %copy-start.2 = (bf16[2,64,5120]{2,1,0:T(8,128)(2,1)S(1)}, bf16[2,64,5120]{2,1,0:T(8,128)(2,1)}, u32[]{:S(2)}) copy-start(bf16[2,64,5120]{2,1,0:T(8,128)(2,1)} %x_ref.1) | copy-start | bytes 3932164
  75.9 17.5 %collective-permute-start.22 = (bf16[2,4,64,128]{3,2,1,0:T(8,128)(2,1)S(1)}, bf16[2,4,64,128]{3,2,1,0:T(8,128)(2,1)S(1)}, u32[]{:S(2)}, u32[]{:S(2)}) collective-permute-start(bf16[2,4,64,128]{3,2,1,0:T(8,128)(2,1)S(1)} %get-tuple-element.111), channel_id=1, source_target_pairs={{0,10},{1,11},{2,8},{3,9},{4,14},{5,15},{6,12},{7,13},{8,2},{9,3},... | collective-permute-start | bytes 393224 | tf_op jit(solution)/shard_map/ppermute | solution.py:202
  83.2 6.0 %collective-permute-start.21 = (bf16[64,128]{1,0:T(8,128)(2,1)S(1)}, bf16[64,128]{1,0:T(8,128)(2,1)S(1)}, u32[]{:S(2)}, u32[]{:S(2)}) collective-permute-start(bf16[64,128]{1,0:T(8,128)(2,1)S(1)} %low_rank.1), channel_id=1, source_target_pairs={{0,12},{1,13},{2,14},{3,15},{4,8},{5,9},{6,10},{7,11},{8,4},{9,5},... | collective-permute-start | bytes 49160 | tf_op jit(solution)/shard_map/ppermute | solution.py:202
  83.3 10.0 %collective-permute-start.20 = (bf16[64,128]{1,0:T(8,128)(2,1)S(1)}, bf16[64,128]{1,0:T(8,128)(2,1)S(1)}, u32[]{:S(2)}, u32[]{:S(2)}) collective-permute-start(bf16[64,128]{1,0:T(8,128)(2,1)S(1)} %low_rank.1), channel_id=1, source_target_pairs={{0,8},{1,9},{2,10},{3,11},{4,12},{5,13},{6,14},{7,15},{8,0},{9,1},... | collective-permute-start | bytes 49160 | tf_op jit(solution)/shard_map/ppermute | solution.py:202
  89.1 4.3 %collective-permute-start.19 = (bf16[64,128]{1,0:T(8,128)(2,1)S(1)}, bf16[64,128]{1,0:T(8,128)(2,1)S(1)}, u32[]{:S(2)}, u32[]{:S(2)}) collective-permute-start(bf16[64,128]{1,0:T(8,128)(2,1)S(1)} %low_rank.1), channel_id=1, source_target_pairs={{0,4},{1,5},{2,6},{3,7},{4,0},{5,1},{6,2},{7,3},{8,12},{9,13},{10,... | collective-permute-start | bytes 49160 | tf_op jit(solution)/shard_map/ppermute | solution.py:202
  89.2 13.7 %collective-permute-start.17 = (bf16[2,256,128]{2,1,0:T(8,128)(2,1)S(1)}, bf16[2,256,128]{2,1,0:T(8,128)(2,1)S(1)}, u32[]{:S(2)}, u32[]{:S(2)}) collective-permute-start(bf16[2,256,128]{2,1,0:T(8,128)(2,1)S(1)} %slice_add_fusion.4), channel_id=1, source_target_pairs={{0,4},{1,5},{2,6},{3,7},{4,0},{5,1},{6,2},{7,3},{8,12},{9,13},{10,... | collective-permute-start | bytes 393224 | tf_op jit(solution)/shard_map/ppermute | solution.py:202
  93.4 4.7 %collective-permute-start.26 = (bf16[4,64,128]{2,1,0:T(8,128)(2,1)S(1)}, bf16[4,64,128]{2,1,0:T(8,128)(2,1)S(1)}, u32[]{:S(2)}, u32[]{:S(2)}) collective-permute-start(bf16[4,64,128]{2,1,0:T(8,128)(2,1)S(1)} %pad_maximum_fusion.6.refs_0_), channel_id=1, source_target_pairs={{0,3},{1,2},{2,1},{3,0},{4,7},{5,6},{6,5},{7,4},{8,11},{9,10},{10,... | collective-permute-start | bytes 196616 | tf_op jit(solution)/shard_map/ppermute | solution.py:202
  95.0 4.5 %collective-permute-start.25 = (bf16[4,64,128]{2,1,0:T(8,128)(2,1)S(1)}, bf16[4,64,128]{2,1,0:T(8,128)(2,1)S(1)}, u32[]{:S(2)}, u32[]{:S(2)}) collective-permute-start(bf16[4,64,128]{2,1,0:T(8,128)(2,1)S(1)} %pad_maximum_fusion.6.refs_0_), channel_id=1, source_target_pairs={{0,2},{1,3},{2,0},{3,1},{4,6},{5,7},{6,4},{7,5},{8,10},{9,11},{10,... | collective-permute-start | bytes 196616 | tf_op jit(solution)/shard_map/ppermute | solution.py:202
  95.5 7.4 %collective-permute-start.24 = (bf16[4,64,128]{2,1,0:T(8,128)(2,1)S(1)}, bf16[4,64,128]{2,1,0:T(8,128)(2,1)S(1)}, u32[]{:S(2)}, u32[]{:S(2)}) collective-permute-start(bf16[4,64,128]{2,1,0:T(8,128)(2,1)S(1)} %pad_maximum_fusion.6.refs_0_), channel_id=1, source_target_pairs={{0,1},{1,0},{2,3},{3,2},{4,5},{5,4},{6,7},{7,6},{8,9},{9,8},{10,11... | collective-permute-start | bytes 196616 | tf_op jit(solution)/shard_map/ppermute | solution.py:202
  95.6 15.6 %collective-permute-start.30 = (bf16[2,4,64,128]{3,2,1,0:T(8,128)(2,1)S(1)}, bf16[2,4,64,128]{3,2,1,0:T(8,128)(2,1)S(1)}, u32[]{:S(2)}, u32[]{:S(2)}) collective-permute-start(bf16[2,4,64,128]{3,2,1,0:T(8,128)(2,1)S(1)} %get-tuple-element.123), channel_id=1, source_target_pairs={{0,11},{1,10},{2,9},{3,8},{4,15},{5,14},{6,13},{7,12},{8,3},{9,2},... | collective-permute-start | bytes 393224 | tf_op jit(solution)/shard_map/ppermute | solution.py:202
  98.1 13.1 %collective-permute-start.31 = (bf16[2,4,64,128]{3,2,1,0:T(8,128)(2,1)S(1)}, bf16[2,4,64,128]{3,2,1,0:T(8,128)(2,1)S(1)}, u32[]{:S(2)}, u32[]{:S(2)}) collective-permute-start(bf16[2,4,64,128]{3,2,1,0:T(8,128)(2,1)S(1)} %get-tuple-element.125), channel_id=1, source_target_pairs={{0,14},{1,15},{2,12},{3,13},{4,10},{5,11},{6,8},{7,9},{8,6},{9,7},... | collective-permute-start | bytes 393224 | tf_op jit(solution)/shard_map/ppermute | solution.py:202
  99.5 15.4 %collective-permute-start.32 = (bf16[2,4,64,128]{3,2,1,0:T(8,128)(2,1)S(1)}, bf16[2,4,64,128]{3,2,1,0:T(8,128)(2,1)S(1)}, u32[]{:S(2)}, u32[]{:S(2)}) collective-permute-start(bf16[2,4,64,128]{3,2,1,0:T(8,128)(2,1)S(1)} %get-tuple-element.127), channel_id=1, source_target_pairs={{0,15},{1,14},{2,13},{3,12},{4,11},{5,10},{6,9},{7,8},{8,7},{9,6},... | collective-permute-start | bytes 393224 | tf_op jit(solution)/shard_map/ppermute | solution.py:202
  102.9 21.2 %collective-permute-start.27 = (bf16[3,4,64,128]{3,2,1,0:T(8,128)(2,1)S(1)}, bf16[3,4,64,128]{3,2,1,0:T(8,128)(2,1)S(1)}, u32[]{:S(2)}, u32[]{:S(2)}) collective-permute-start(bf16[3,4,64,128]{3,2,1,0:T(8,128)(2,1)S(1)} %get-tuple-element.117), channel_id=1, source_target_pairs={{0,5},{1,4},{2,7},{3,6},{4,1},{5,0},{6,3},{7,2},{8,13},{9,12},{10,... | collective-permute-start | bytes 589832 | tf_op jit(solution)/shard_map/ppermute | solution.py:202
  102.9 25.1 %collective-permute-start.28 = (bf16[3,4,64,128]{3,2,1,0:T(8,128)(2,1)S(1)}, bf16[3,4,64,128]{3,2,1,0:T(8,128)(2,1)S(1)}, u32[]{:S(2)}, u32[]{:S(2)}) collective-permute-start(bf16[3,4,64,128]{3,2,1,0:T(8,128)(2,1)S(1)} %get-tuple-element.119), channel_id=1, source_target_pairs={{0,6},{1,7},{2,4},{3,5},{4,2},{5,3},{6,0},{7,1},{8,14},{9,15},{10,... | collective-permute-start | bytes 589832 | tf_op jit(solution)/shard_map/ppermute | solution.py:202
  111.1 12.1 %collective-permute-start.18 = (bf16[1,256,128]{2,1,0:T(8,128)(2,1)S(1)}, bf16[1,256,128]{2,1,0:T(8,128)(2,1)S(1)}, u32[]{:S(2)}, u32[]{:S(2)}) collective-permute-start(bf16[1,256,128]{2,1,0:T(8,128)(2,1)S(1)} %slice_add_fusion.12), channel_id=1, source_target_pairs={{0,8},{1,9},{2,10},{3,11},{4,12},{5,13},{6,14},{7,15},{8,0},{9,1},... | collective-permute-start | bytes 196616 | tf_op jit(solution)/shard_map/ppermute | solution.py:202
  111.1 29.2 %collective-permute-start.35 = (bf16[1,4,64,128]{3,2,1,0:T(8,128)(2,1)S(1)}, bf16[1,4,64,128]{3,2,1,0:T(8,128)(2,1)S(1)}, u32[]{:S(2)}, u32[]{:S(2)}) collective-permute-start(bf16[1,4,64,128]{3,2,1,0:T(8,128)(2,1)S(1)} %get-tuple-element.134), channel_id=1, source_target_pairs={{0,10},{1,11},{2,8},{3,9},{4,14},{5,15},{6,12},{7,13},{8,2},{9,3},... | collective-permute-start | bytes 196616 | tf_op jit(solution)/shard_map/ppermute | solution.py:202
  114.9 25.4 %collective-permute-start.36 = (bf16[1,4,64,128]{3,2,1,0:T(8,128)(2,1)S(1)}, bf16[1,4,64,128]{3,2,1,0:T(8,128)(2,1)S(1)}, u32[]{:S(2)}, u32[]{:S(2)}) collective-permute-start(bf16[1,4,64,128]{3,2,1,0:T(8,128)(2,1)S(1)} %get-tuple-element.136), channel_id=1, source_target_pairs={{0,11},{1,10},{2,9},{3,8},{4,15},{5,14},{6,13},{7,12},{8,3},{9,2},... | collective-permute-start | bytes 196616 | tf_op jit(solution)/shard_map/ppermute | solution.py:202
  123.3 17.1 %collective-permute-start.37 = (bf16[1,4,64,128]{3,2,1,0:T(8,128)(2,1)S(1)}, bf16[1,4,64,128]{3,2,1,0:T(8,128)(2,1)S(1)}, u32[]{:S(2)}, u32[]{:S(2)}) collective-permute-start(bf16[1,4,64,128]{3,2,1,0:T(8,128)(2,1)S(1)} %get-tuple-element.138), channel_id=1, source_target_pairs={{0,14},{1,15},{2,12},{3,13},{4,10},{5,11},{6,8},{7,9},{8,6},{9,7},... | collective-permute-start | bytes 196616 | tf_op jit(solution)/shard_map/ppermute | solution.py:202
  124.1 16.3 %collective-permute-start.38 = (bf16[1,4,64,128]{3,2,1,0:T(8,128)(2,1)S(1)}, bf16[1,4,64,128]{3,2,1,0:T(8,128)(2,1)S(1)}, u32[]{:S(2)}, u32[]{:S(2)}) collective-permute-start(bf16[1,4,64,128]{3,2,1,0:T(8,128)(2,1)S(1)} %get-tuple-element.140), channel_id=1, source_target_pairs={{0,15},{1,14},{2,13},{3,12},{4,11},{5,10},{6,9},{7,8},{8,7},{9,6},... | collective-permute-start | bytes 196616 | tf_op jit(solution)/shard_map/ppermute | solution.py:202
  128.1 7.7 %collective-permute-start.29 = (bf16[3,4,64,128]{3,2,1,0:T(8,128)(2,1)S(1)}, bf16[3,4,64,128]{3,2,1,0:T(8,128)(2,1)S(1)}, u32[]{:S(2)}, u32[]{:S(2)}) collective-permute-start(bf16[3,4,64,128]{3,2,1,0:T(8,128)(2,1)S(1)} %get-tuple-element.121), channel_id=1, source_target_pairs={{0,7},{1,6},{2,5},{3,4},{4,3},{5,2},{6,1},{7,0},{8,15},{9,14},{10,... | collective-permute-start | bytes 589832 | tf_op jit(solution)/shard_map/ppermute | solution.py:202
  143.6 12.5 %collective-permute-start.40 = (bf16[2,4,64,128]{3,2,1,0:T(8,128)(2,1)S(1)}, bf16[2,4,64,128]{3,2,1,0:T(8,128)(2,1)S(1)}, u32[]{:S(2)}, u32[]{:S(2)}) collective-permute-start(bf16[2,4,64,128]{3,2,1,0:T(8,128)(2,1)S(1)} %get-tuple-element.142), channel_id=1, source_target_pairs={{0,14},{1,15},{2,12},{3,13},{4,10},{5,11},{6,8},{7,9},{8,6},{9,7},... | collective-permute-start | bytes 393224 | tf_op jit(solution)/shard_map/ppermute | solution.py:202
  145.3 19.4 %collective-permute-start.39 = (bf16[2,4,64,128]{3,2,1,0:T(8,128)(2,1)S(1)}, bf16[2,4,64,128]{3,2,1,0:T(8,128)(2,1)S(1)}, u32[]{:S(2)}, u32[]{:S(2)}) collective-permute-start(bf16[2,4,64,128]{3,2,1,0:T(8,128)(2,1)S(1)} %get-tuple-element.141), channel_id=1, source_target_pairs={{0,10},{1,11},{2,8},{3,9},{4,14},{5,15},{6,12},{7,13},{8,2},{9,3},... | collective-permute-start | bytes 393224 | tf_op jit(solution)/shard_map/ppermute | solution.py:202
  147.2 17.5 %collective-permute-start.34 = (bf16[2,4,64,128]{3,2,1,0:T(8,128)(2,1)S(1)}, bf16[2,4,64,128]{3,2,1,0:T(8,128)(2,1)S(1)}, u32[]{:S(2)}, u32[]{:S(2)}) collective-permute-start(bf16[2,4,64,128]{3,2,1,0:T(8,128)(2,1)S(1)} %get-tuple-element.131), channel_id=1, source_target_pairs={{0,12},{1,13},{2,14},{3,15},{4,8},{5,9},{6,10},{7,11},{8,4},{9,5},... | collective-permute-start | bytes 393224 | tf_op jit(solution)/shard_map/ppermute | solution.py:202
  148.4 22.3 %collective-permute-start.33 = (bf16[2,4,64,128]{3,2,1,0:T(8,128)(2,1)S(1)}, bf16[2,4,64,128]{3,2,1,0:T(8,128)(2,1)S(1)}, u32[]{:S(2)}, u32[]{:S(2)}) collective-permute-start(bf16[2,4,64,128]{3,2,1,0:T(8,128)(2,1)S(1)} %get-tuple-element.130), channel_id=1, source_target_pairs={{0,8},{1,9},{2,10},{3,11},{4,12},{5,13},{6,14},{7,15},{8,0},{9,1},... | collective-permute-start | bytes 393224 | tf_op jit(solution)/shard_map/ppermute | solution.py:202
  155.6 15.8 %collective-permute-start.43 = (bf16[2,4,64,128]{3,2,1,0:T(8,128)(2,1)S(1)}, bf16[2,4,64,128]{3,2,1,0:T(8,128)(2,1)S(1)}, u32[]{:S(2)}, u32[]{:S(2)}) collective-permute-start(bf16[2,4,64,128]{3,2,1,0:T(8,128)(2,1)S(1)} %get-tuple-element.148), channel_id=1, source_target_pairs={{0,2},{1,3},{2,0},{3,1},{4,6},{5,7},{6,4},{7,5},{8,10},{9,11},{10,... | collective-permute-start | bytes 393224 | tf_op jit(solution)/shard_map/ppermute | solution.py:202
  156.1 15.4 %collective-permute-start.42 = (bf16[2,4,64,128]{3,2,1,0:T(8,128)(2,1)S(1)}, bf16[2,4,64,128]{3,2,1,0:T(8,128)(2,1)S(1)}, u32[]{:S(2)}, u32[]{:S(2)}) collective-permute-start(bf16[2,4,64,128]{3,2,1,0:T(8,128)(2,1)S(1)} %get-tuple-element.145), channel_id=1, source_target_pairs={{0,6},{1,7},{2,4},{3,5},{4,2},{5,3},{6,0},{7,1},{8,14},{9,15},{10,... | collective-permute-start | bytes 393224 | tf_op jit(solution)/shard_map/ppermute | solution.py:202
  164.6 8.8 %collective-permute-start.41 = (bf16[2,4,64,128]{3,2,1,0:T(8,128)(2,1)S(1)}, bf16[2,4,64,128]{3,2,1,0:T(8,128)(2,1)S(1)}, u32[]{:S(2)}, u32[]{:S(2)}) collective-permute-start(bf16[2,4,64,128]{3,2,1,0:T(8,128)(2,1)S(1)} %get-tuple-element.144), channel_id=1, source_target_pairs={{0,4},{1,5},{2,6},{3,7},{4,0},{5,1},{6,2},{7,3},{8,12},{9,13},{10,... | collective-permute-start | bytes 393224 | tf_op jit(solution)/shard_map/ppermute | solution.py:202
  170.8 3.3 %collective-permute-start.44 = (bf16[4,4,64,128]{3,2,1,0:T(8,128)(2,1)S(1)}, bf16[4,4,64,128]{3,2,1,0:T(8,128)(2,1)S(1)}, u32[]{:S(2)}, u32[]{:S(2)}) collective-permute-start(bf16[4,4,64,128]{3,2,1,0:T(8,128)(2,1)S(1)} %pad_maximum_fusion.3), channel_id=1, source_target_pairs={{0,1},{1,0},{2,3},{3,2},{4,5},{5,4},{6,7},{7,6},{8,9},{9,8},{10,11... | collective-permute-start | bytes 786440 | tf_op jit(solution)/shard_map/ppermute | solution.py:202
  173.5 1.8 %collective-permute-start.45 = (bf16[4,4,64,128]{3,2,1,0:T(8,128)(2,1)S(1)}, bf16[4,4,64,128]{3,2,1,0:T(8,128)(2,1)S(1)}, u32[]{:S(2)}, u32[]{:S(2)}) collective-permute-start(bf16[4,4,64,128]{3,2,1,0:T(8,128)(2,1)S(1)} %pad_maximum_fusion.4), channel_id=1, source_target_pairs={{0,1},{1,0},{2,3},{3,2},{4,5},{5,4},{6,7},{7,6},{8,9},{9,8},{10,11... | collective-permute-start | bytes 786440 | tf_op jit(solution)/shard_map/ppermute | solution.py:202
  (6 other events, 17.3 us)

commit v6 on v3

v6 whole, which is shorter than its diff:
```python
import functools
import math

import jax
import jax.numpy as jnp
from jax import lax
from jax.experimental import pallas as pl
from jax.experimental.pallas import tpu as pltpu
from jax.sharding import PartitionSpec as P

LANES = 128
ANY = pl.BlockSpec(memory_space=pl.ANY)
VMEM = pl.BlockSpec(memory_space=pltpu.VMEM)
SMEM = pl.BlockSpec(memory_space=pltpu.SMEM)


def bit_count(n):
    bits = n.bit_length() - 1
    assert 1 << bits == n
    return bits


def reversed_bits(j, bits):
    out = 0
    for i in range(bits):
        out = out | (((j >> i) & 1) << (bits - 1 - i))
    return out


def pick_kernel(shape, me_ref, row_ref, req_ref, down_ref, up_ref, *refs):
    devs, bits, per_video, pairs, col_split, rows, tiles = shape
    downs, ups = refs[: bits + 1], refs[bits + 1 : 2 * bits + 2]
    down, up, sems = refs[2 * bits + 2 :]
    slots, ranks, _ = down_ref.shape
    videos = down.shape[0]
    me = me_ref[0]
    for s in range(videos):
        place = row_ref[req_ref[s]]
        slot = place % slots
        owned = place // slots == me
        copies = [
            pltpu.make_async_copy(down_ref.at[slot], down.at[s], sems.at[2 * s]),
            pltpu.make_async_copy(up_ref.at[slot], up.at[s], sems.at[2 * s + 1]),
        ]

        @pl.when(owned)
        def _():
            for copy in copies:
                copy.start()
            for copy in copies:
                copy.wait()

        @pl.when(jnp.logical_not(owned))
        def _():
            down[s] = jnp.zeros(down.shape[1:], down.dtype)
            up[s] = jnp.zeros(up.shape[1:], up.dtype)

    for j in range(devs):
        step = bits - j.bit_length()
        at = j - (1 << (j.bit_length() - 1)) if j else 0
        dev = me ^ reversed_bits(j, bits)
        video = dev // per_video
        place = dev % per_video
        row = pl.multiple_of((place // col_split) * rows, rows)
        for t in range(tiles):
            col = pl.multiple_of(((place % col_split) * tiles + t) * LANES, LANES)
            downs[step][at, t * rows : (t + 1) * rows, :] = down[
                video, pl.ds(row, rows), pl.ds(col, LANES)
            ]
        for p in range(pairs):
            col = pl.multiple_of((place * pairs + p) * LANES, LANES)
            ups[step][at, p * ranks : (p + 1) * ranks, :] = up[video, :, pl.ds(col, LANES)]


def low_rank_kernel(shape, x_ref, g_ref, q_ref, out_ref, down):
    devs, _, per_video, _, col_split, rows, tiles = shape
    for dev in range(devs):
        video = dev // per_video
        place = dev % per_video
        row = (place // col_split) * rows
        for t in range(tiles):
            col = ((place % col_split) * tiles + t) * LANES
            down[video, row : row + rows, col : col + LANES] = g_ref[
                dev, t * rows : (t + 1) * rows, :
            ]
    first = q_ref.shape[1]
    out_ref[:, :first] = q_ref[...]
    for s in range(x_ref.shape[0]):
        low = lax.dot_general(
            x_ref[s], down[s], (((1,), (1,)), ((), ())), preferred_element_type=jnp.float32
        ).astype(out_ref.dtype)
        half = low.shape[0] // 2
        low = jnp.concatenate([low[:half], low[half:]], axis=1)
        for dev in range(s * per_video, (s + 1) * per_video):
            out_ref[dev, first:] = low


def add_delta(base, low, up, second):
    devs, toks, width = base.shape
    ranks = up.shape[0]
    row = lax.broadcasted_iota(jnp.int32, up.shape, 0)
    part = jnp.where(row // (ranks // 2) == second, up, jnp.zeros_like(up))
    none = jnp.zeros_like(part)
    deltas = [
        jnp.dot(low, jnp.concatenate(pair, axis=0), preferred_element_type=jnp.float32)
        for pair in ((part, none), (none, part))
    ]
    delta = jnp.concatenate([d.reshape(devs, toks // 2, width) for d in deltas], axis=1)
    return (base.astype(jnp.float32) + delta).astype(base.dtype).reshape(devs * toks, width)


def attend_kernel(block, up_ref, q_ref, low_ref, k_ref, v_ref, out_ref, q_mix):
    devs, toks, width = q_ref.shape
    length = devs * toks
    low = low_ref[...].reshape(length // 2, low_ref.shape[2])
    up = up_ref[...]
    keys = k_ref[...].reshape(length, width)
    vals = add_delta(v_ref[...], low, up, 1)
    q_mix[...] = add_delta(q_ref[...], low, up, 0)
    scale = math.log2(math.e) / math.sqrt(width)
    for b in range(0, devs, block):
        q = q_mix[b * toks : (b + block) * toks, :]
        scores = lax.dot_general(
            q, keys, (((1,), (1,)), ((), ())), preferred_element_type=jnp.float32
        )
        top = jnp.max(scores, axis=1, keepdims=True)
        weights = jnp.exp2((scores - top) * scale)
        total = jnp.sum(weights, axis=1, keepdims=True)
        mixed = jnp.dot(weights.astype(jnp.bfloat16), vals, preferred_element_type=jnp.float32)
        out_ref[b : b + block] = (mixed / total).astype(jnp.bfloat16).reshape(block, toks, width)


def body(
    normed_token_features,
    queries,
    projected_keys,
    values,
    adapter_down_factors,
    adapter_up_factors,
    adapter_store_row,
    requests,
):
    videos, toks, model_width = normed_token_features.shape
    heads = queries.shape[1]
    width = queries.shape[3]
    _, ranks, up_width = adapter_up_factors.shape
    devs = lax.axis_size("seq")
    bits = bit_count(devs)
    me = lax.axis_index("seq").astype(jnp.int32)[None]
    pairs = videos * heads // devs
    per_video = devs // videos
    length = devs * toks
    col_split = math.gcd(per_video, model_width // LANES)
    rows = ranks * col_split // per_video
    tiles = model_width // col_split // LANES
    shape = (devs, bits, per_video, pairs, col_split, rows, tiles)

    def swap(tensor, k):
        return lax.ppermute(tensor, "seq", [(i, i ^ k) for i in range(devs)])

    def exchange(tensor):
        return lax.all_to_all(tensor, "seq", split_axis=0, concat_axis=0, tiled=True)

    def by_pairs(tensor):
        return tensor.reshape(devs, pairs, toks, width)

    def after(array, *others):
        return lax.optimization_barrier((array, others))[0]

    def halving(parts, received, i):
        h = devs >> (i + 1) if i < bits else 0
        size = max(h, 1)
        return sum((r[h : h + size] for r in received), parts[i])

    keys = exchange(by_pairs(projected_keys))

    steps = [devs >> (i + 1) for i in range(bits)] + [1]
    piece_shapes = [(h, tiles * rows, LANES) for h in steps] + [
        (h, pairs * ranks, LANES) for h in steps
    ]
    pieces = pl.pallas_call(
        functools.partial(pick_kernel, shape),
        in_specs=[SMEM, SMEM, SMEM, ANY, ANY],
        out_specs=[VMEM] * (2 * bits + 2),
        out_shape=[jax.ShapeDtypeStruct(s, jnp.bfloat16) for s in piece_shapes],
        scratch_shapes=[
            pltpu.VMEM((videos, ranks, model_width), jnp.bfloat16),
            pltpu.VMEM((videos, ranks, up_width), jnp.bfloat16),
            pltpu.SemaphoreType.DMA((2 * videos,)),
        ],
        compiler_params=pltpu.CompilerParams(vmem_limit_bytes=24 << 20),
        cost_estimate=pl.CostEstimate(
            flops=0,
            bytes_accessed=4 * videos * ranks * (model_width + up_width),
            transcendentals=0,
        ),
        name="pick_factors",
    )(me, adapter_store_row, requests, adapter_down_factors, adapter_up_factors)
    down_pieces, up_pieces = pieces[: bits + 1], pieces[bits + 1 :]

    down_got, up_got = [], []
    for i in range(bits):
        piece = halving(down_pieces, down_got, i)
        if i == 2:
            piece = after(piece, keys)
        down_got.append(swap(piece, 1 << i))
        up_got.append(swap(after(halving(up_pieces, up_got, i), piece), 1 << i))
    shard = halving(down_pieces, down_got, bits)
    up_here = halving(up_pieces, up_got, bits).reshape(pairs, ranks, LANES)
    gathered = lax.all_gather(shard, "seq", axis=0, tiled=True)
    vals = exchange(after(by_pairs(values), shard))

    asked = pl.pallas_call(
        functools.partial(low_rank_kernel, shape),
        in_specs=[VMEM, VMEM, VMEM],
        out_specs=VMEM,
        scratch_shapes=[pltpu.VMEM((videos, ranks, model_width), jnp.bfloat16)],
        out_shape=jax.ShapeDtypeStruct((devs, pairs * toks + toks // 2, width), jnp.bfloat16),
        compiler_params=pltpu.CompilerParams(vmem_limit_bytes=24 << 20),
        cost_estimate=pl.CostEstimate(
            flops=2 * videos * toks * ranks * model_width,
            bytes_accessed=2 * videos * (toks + ranks) * model_width,
            transcendentals=0,
        ),
        name="low_rank",
    )(
        normed_token_features,
        after(gathered, vals, up_here),
        queries.reshape(devs, pairs * toks, width),
    )
    asked = exchange(asked)

    part_spec = pl.BlockSpec((devs, pl.squeezed, toks, width), lambda p: (0, p, 0, 0))
    mixed = pl.pallas_call(
        functools.partial(attend_kernel, math.gcd(devs, max(1, 512 // toks))),
        grid=(pairs,),
        in_specs=[
            pl.BlockSpec((pl.squeezed, ranks, LANES), lambda p: (p, 0, 0)),
            pl.BlockSpec((devs, toks, width), lambda p: (0, p, 0)),
            pl.BlockSpec((devs, toks // 2, width), lambda p: (0, 2 * pairs, 0)),
            part_spec,
            part_spec,
        ],
        out_specs=part_spec,
        out_shape=jax.ShapeDtypeStruct((devs, pairs, toks, width), jnp.bfloat16),
        scratch_shapes=[pltpu.VMEM((length, width), jnp.bfloat16)],
        compiler_params=pltpu.CompilerParams(vmem_limit_bytes=48 << 20),
        cost_estimate=pl.CostEstimate(
            flops=4 * pairs * length * length * width,
            bytes_accessed=8 * pairs * length * width,
            transcendentals=pairs * length * length,
        ),
        name="attend",
    )(up_here, asked, asked, keys, vals)
    return exchange(mixed).reshape(videos, heads, toks, width)


def solution(mesh):
    in_specs = (
        P("grp", "seq", None),
        P("grp", None, "seq", None),
        P("grp", None, "seq", None),
        P("grp", None, "seq", None),
        P("seq", None, None),
        P("seq", None, None),
        P(),
        P("grp"),
    )
    out_specs = P("grp", None, "seq", None)
    return jax.shard_map(body, mesh=mesh, in_specs=in_specs, out_specs=out_specs, check_vma=False)
```

time: 266 us -> 181 us (0.68)
  waiting for transfers between devices: 146 us -> 60.9 us
    psum x1 -> x0, waiting for transfers between devices: 76.6 us -> none  [body(): down = lax.psum(down_part, 'seq')]
    reduce_scatter x1 -> x0, waiting for transfers between devices: 41.9 us -> none  [body(): up_here = lax.psum_scatter(up_parts, 'seq', scatter_dimension=0, tiled=True)]
    ppermute x6 -> x8, waiting for transfers between devices: 5.81 us -> 45 us  [swap(): return lax.ppermute(tensor, 'seq', [(i, i ^ k) for i in range(devs)])]
    all_to_all x2, waiting for transfers between devices: 20.7 us -> 3.66 us  [exchange(): lax.all_to_all(tensor, 'seq', split_axis=0, concat_axis=0, tiled=True)]
    all_gather x0 -> x1, waiting for transfers between devices: none -> 12.2 us  [body(): gathered = lax.all_gather(shard, 'seq', axis=0, tiled=True)]
    ppermute x6 -> x8, starting transfers between devices: 9.51 us -> 11.6 us  [swap(): return lax.ppermute(tensor, 'seq', [(i, i ^ k) for i in range(devs)])]
    unnamed x19 -> x25, local copies, waits for them, and re-layouts: 5.79 us -> 4.07 us
  transfers between devices with their start and end apart: 10 -> 11, of which waited for: 7 -> 10; matrix products, arithmetic and copies ran while one was open for 0% -> 1% of each run, Pallas kernels for 1% -> 1%
where the time goes in v6:
time: 181 us
  blocking collectives  61.8 us (34%)
  waiting for transfers between devices  60.9 us (34%)
  starting transfers between devices  26.5 us (15%)
  between operations  13.6 us (8%)
  Pallas kernels  11.4 us (6%)
  local copies, waits for them, and re-layouts  4.07 us (2%)
  other arithmetic  2.63 us (1%)
    all_to_all x2, blocking collectives, exchange(): lax.all_to_all(tensor, 'seq', split_axis=0, concat_axis=0, tiled=True)  61.8 us
    ppermute x8, waiting for transfers between devices, swap(): return lax.ppermute(tensor, 'seq', [(i, i ^ k) for i in range(devs)])  45 us
    all_to_all x2, starting transfers between devices, exchange(): lax.all_to_all(tensor, 'seq', split_axis=0, concat_axis=0, tiled=True)  14.8 us
    all_gather x1, waiting for transfers between devices, body(): gathered = lax.all_gather(shard, 'seq', axis=0, tiled=True)  12.2 us
    ppermute x8, starting transfers between devices, swap(): return lax.ppermute(tensor, 'seq', [(i, i ^ k) for i in range(devs)])  11.6 us
    pallas_call x1, Pallas kernels, body(): pl.pallas_call(functools.partial(attend_kernel, math.gcd(devs, max(1, 512...  9.28 us
    unnamed x25, local copies, waits for them, and re-layouts  4.07 us
    all_to_all x2, waiting for transfers between devices, exchange(): lax.all_to_all(tensor, 'seq', split_axis=0, concat_axis=0, tiled=True)  3.66 us
  transfers between devices with their start and end apart: 11, of which 10 were waited for; matrix products, arithmetic and copies ran while one was open for 1% of the time, Pallas kernels for 1%

profile of v6, /device:TPU:1, one launch (start us, length us, event | category | flops | bytes accessed | tf_op | source)
XLA Modules:
  0.0 180.8 jit_solution(9991652460506010542)
XLA Ops:
  6.5 7.5 %all-to-all-start = ((bf16[16,4,64,128]{3,2,1,0:T(8,128)(2,1)}), bf16[16,4,64,128]{3,2,1,0:T(8,128)(2,1)S(1)}, u32[]{:S(2)}, u32[]{:S(2)}) async-start(bf16[16,4,64,128]{3,2,1,0:T(8,128)(2,1)} %bitcast.9), calls=%async_computation | async-start | bytes 2097152 | tf_op jit(solution)/shard_map/all_to_all | solution.py:162
  14.0 0.0 all-gather.2.cloned.1.call-start
  14.1 0.0 copy-done.10
  14.1 0.0 copy-done.9
  14.1 0.0 copy-done.1
  14.1 0.0 copy-start
  14.1 1.7 copy-done
  15.8 1.5 pick_factors.1
  17.4 0.0 copy-start.5
  17.4 0.0 copy-start.6
  17.4 0.0 copy-start.7
  17.4 0.0 copy-start.11
  17.4 0.2 collective-permute-start.1
  17.6 2.0 %collective-permute-done.1 = bf16[8,320,128]{2,1,0:T(8,128)(2,1)S(1)} collective-permute-done((bf16[8,320,128]{2,1,0:T(8,128)(2,1)S(1)}, bf16[8,320,128]{2,1,0:T(8,128)(2,1)S(1)}, u32[]{:S(2)}, u32[]{:S(2)}) %collective-permute-start.1) | collective-permute-done | bytes 655392 | tf_op jit(solution)/shard_map/ppermute | solution.py:159
  19.6 1.5 collective-permute-start.3
  21.1 12.4 %collective-permute-done.3 = bf16[4,320,128]{2,1,0:T(8,128)(2,1)S(1)} collective-permute-done((bf16[4,320,128]{2,1,0:T(8,128)(2,1)S(1)}, bf16[4,320,128]{2,1,0:T(8,128)(2,1)S(1)}, u32[]{:S(2)}, u32[]{:S(2)}) %collective-permute-start.3) | collective-permute-done | bytes 327712 | tf_op jit(solution)/shard_map/ppermute | solution.py:159
  33.5 0.0 copy-done.5
  33.5 0.0 copy-done.11
  33.5 3.7 %all-to-all-done.k_ref = bf16[16,4,64,128]{3,2,1,0:T(8,128)(2,1)S(1)} async-done(((bf16[16,4,64,128]{3,2,1,0:T(8,128)(2,1)}), bf16[16,4,64,128]{3,2,1,0:T(8,128)(2,1)S(1)}, u32[]{:S(2)}, u32[]{:S(2)}) %all-to-all-start) | async-done | bytes 1048608 | tf_op jit(solution)/shard_map/all_to_all | solution.py:162
  37.2 3.1 %collective-permute-start.5 = (bf16[2,320,128]{2,1,0:T(8,128)(2,1)S(1)}, bf16[2,320,128]{2,1,0:T(8,128)(2,1)S(1)}, u32[]{:S(2)}, u32[]{:S(2)}) collective-permute-start(bf16[2,320,128]{2,1,0:T(8,128)(2,1)S(1)} %slice_add_fusion.2), channel_id=1, source_target_pairs={{0,4},{1,5},{2,6},{3,7},{4,0},{5,1},{6,2},{7,3},{8,12},{9,13},{10,... | collective-permute-start | bytes 491528 | tf_op jit(solution)/shard_map/ppermute | solution.py:159
  40.3 4.6 %collective-permute-done.5 = bf16[2,320,128]{2,1,0:T(8,128)(2,1)S(1)} collective-permute-done((bf16[2,320,128]{2,1,0:T(8,128)(2,1)S(1)}, bf16[2,320,128]{2,1,0:T(8,128)(2,1)S(1)}, u32[]{:S(2)}, u32[]{:S(2)}) %collective-permute-start.5) | collective-permute-done | bytes 163872 | tf_op jit(solution)/shard_map/ppermute | solution.py:159
  44.9 1.0 collective-permute-start.7
  45.9 3.6 %collective-permute-done.7 = bf16[1,320,128]{2,1,0:T(8,128)(2,1)S(1)} collective-permute-done((bf16[1,320,128]{2,1,0:T(8,128)(2,1)S(1)}, bf16[1,320,128]{2,1,0:T(8,128)(2,1)S(1)}, u32[]{:S(2)}, u32[]{:S(2)}) %collective-permute-start.7) | collective-permute-done | bytes 81952 | tf_op jit(solution)/shard_map/ppermute | solution.py:159
  49.5 0.7 fusion
  50.1 0.0 all-gather.2.cloned.1.call-update
  50.2 0.0 copy-start.4
  50.2 7.4 %all-to-all-start.1 = ((bf16[16,4,64,128]{3,2,1,0:T(8,128)(2,1)}), bf16[16,4,64,128]{3,2,1,0:T(8,128)(2,1)}, u32[]{:S(2)}, u32[]{:S(2)}) async-start(bf16[16,4,64,128]{3,2,1,0:T(8,128)(2,1)} %bitcast.3), calls=%async_computation.1 | async-start | bytes 2097152 | tf_op jit(solution)/shard_map/all_to_all | solution.py:162
  57.5 0.0 copy-start.2
  57.5 0.2 collective-permute-start
  57.8 2.0 %collective-permute-done = bf16[8,256,128]{2,1,0:T(8,128)(2,1)S(1)} collective-permute-done((bf16[8,256,128]{2,1,0:T(8,128)(2,1)}, bf16[8,256,128]{2,1,0:T(8,128)(2,1)S(1)}, u32[]{:S(2)}, u32[]{:S(2)}) %collective-permute-start) | collective-permute-done | bytes 524320 | tf_op jit(solution)/shard_map/ppermute | solution.py:159
  59.7 1.0 slice_add_fusion.1
  60.7 1.5 collective-permute-start.2
  62.2 12.6 %collective-permute-done.2 = bf16[4,256,128]{2,1,0:T(8,128)(2,1)S(1)} collective-permute-done((bf16[4,256,128]{2,1,0:T(8,128)(2,1)S(1)}, bf16[4,256,128]{2,1,0:T(8,128)(2,1)S(1)}, u32[]{:S(2)}, u32[]{:S(2)}) %collective-permute-start.2) | collective-permute-done | bytes 262176 | tf_op jit(solution)/shard_map/ppermute | solution.py:159
  74.8 0.1 collective-permute-start.4
  74.9 5.5 %collective-permute-done.4 = bf16[2,256,128]{2,1,0:T(8,128)(2,1)S(1)} collective-permute-done((bf16[2,256,128]{2,1,0:T(8,128)(2,1)S(1)}, bf16[2,256,128]{2,1,0:T(8,128)(2,1)S(1)}, u32[]{:S(2)}, u32[]{:S(2)}) %collective-permute-start.4) | collective-permute-done | bytes 131104 | tf_op jit(solution)/shard_map/ppermute | solution.py:159
  80.4 0.9 slice_add_fusion.12
  81.2 4.1 %collective-permute-start.6 = (bf16[1,256,128]{2,1,0:T(8,128)(2,1)S(1)}, bf16[1,256,128]{2,1,0:T(8,128)(2,1)S(1)}, u32[]{:S(2)}, u32[]{:S(2)}) collective-permute-start(bf16[1,256,128]{2,1,0:T(8,128)(2,1)S(1)} %slice_add_fusion.12), channel_id=1, source_target_pairs={{0,8},{1,9},{2,10},{3,11},{4,12},{5,13},{6,14},{7,15},{8,0},{9,1},... | collective-permute-start | bytes 196616 | tf_op jit(solution)/shard_map/ppermute | solution.py:159
  85.3 2.4 %collective-permute-done.6 = bf16[1,256,128]{2,1,0:T(8,128)(2,1)S(1)} collective-permute-done((bf16[1,256,128]{2,1,0:T(8,128)(2,1)S(1)}, bf16[1,256,128]{2,1,0:T(8,128)(2,1)S(1)}, u32[]{:S(2)}, u32[]{:S(2)}) %collective-permute-start.6) | collective-permute-done | bytes 65568 | tf_op jit(solution)/shard_map/ppermute | solution.py:159
  87.7 0.0 copy-done.8
  87.7 0.0 all-to-all-done.1.v_ref
  87.7 12.2 %all-gather.2.cloned.1.call-done.g_ref = bf16[16,320,128]{2,1,0:T(8,128)(2,1)} async-done(((bf16[1,320,128]{2,1,0:T(8,128)(2,1)}), bf16[16,320,128]{2,1,0:T(8,128)(2,1)}) %all-gather.2.cloned.1.call-update) | async-done | bytes 1310736 | tf_op jit(solution)/shard_map/all_gather | solution.py:210
  100.0 0.0 copy-done.4
  100.0 1.3 copy-done.3
  101.3 0.6 low_rank.1
  101.9 33.4 %all_to_all.20.q_ref.low_ref = bf16[16,288,128]{2,1,0:T(8,128)(2,1)S(1)} all-to-all(bf16[16,288,128]{2,1,0:T(8,128)(2,1)S(1)} %low_rank.1), channel_id=1, replica_groups=mesh['grp'=2,'seq'=16] {'seq'}, dimensions={0} | all-to-all | bytes 2359296 | tf_op jit(solution)/shard_map/all_to_all | solution.py:162
  135.3 9.3 %attend.1 = bf16[16,4,64,128]{3,2,1,0:T(8,128)(2,1)S(1)} custom-call(bf16[4,64,128]{2,1,0:T(8,128)(2,1)S(1)} %bitcast.7, bf16[16,288,128]{2,1,0:T(8,128)(2,1)S(1)} %all_to_all.20.q_ref.low_ref, bf16[16,288,128]{2,1,0:T(8,128)(2,1)S(1)} %all_to_all.20.q_ref.low_ref, bf16[16,4,64,128]{3,2,1,0:T(8,128)(2,1)S(1)} %all-to-all-done.k_ref, ...), custom_call_target="tpu_custom_call" | custom-call | flops 2147483648 | bytes 4194304 | tf_op jit(solution)/shard_map/attend/pallas_call | solution.py:234
  144.6 28.4 %all_to_all.21 = bf16[16,4,64,128]{3,2,1,0:T(8,128)(2,1)S(1)} all-to-all(bf16[16,4,64,128]{3,2,1,0:T(8,128)(2,1)S(1)} %attend.1), channel_id=1, replica_groups=mesh['grp'=2,'seq'=16] {'seq'}, dimensions={0} | all-to-all | bytes 2097152 | tf_op jit(solution)/shard_map/all_to_all | solution.py:162
  173.0 1.0 copy.10
  (13 shorter events, 0.1 us)
Async XLA Ops:
  6.5 7.5 %copy-start.10 = (s32[2]{0:T(128)S(1)}, s32[2]{0:T(128)}, u32[]{:S(2)}) copy-start(s32[2]{0:T(128)} %req_ref.1) | copy-start | bytes 28
  6.5 7.5 %copy-start.9 = (s32[64]{0:T(128)S(1)}, s32[64]{0:T(128)}, u32[]{:S(2)}) copy-start(s32[64]{0:T(128)} %row_ref.1) | copy-start | bytes 772
  6.5 7.6 %copy-start.1 = (bf16[4,64,4096]{2,1,0:T(8,128)(2,1)S(1)}, bf16[4,64,4096]{2,1,0:T(8,128)(2,1)}, u32[]{:S(2)}) copy-start(bf16[4,64,4096]{2,1,0:T(8,128)(2,1)} %up_ref.1) | copy-start | bytes 6291460
  6.5 30.6 %all-to-all-start = ((bf16[16,4,64,128]{3,2,1,0:T(8,128)(2,1)}), bf16[16,4,64,128]{3,2,1,0:T(8,128)(2,1)S(1)}, u32[]{:S(2)}, u32[]{:S(2)}) async-start(bf16[16,4,64,128]{3,2,1,0:T(8,128)(2,1)} %bitcast.9), calls=%async_computation | async-start | bytes 2097152 | tf_op jit(solution)/shard_map/all_to_all | solution.py:162
  14.0 85.9 %all-gather.2.cloned.1.call-start = ((), (), s32[]{:S(2)}) async-start(), calls=%async_computation.4 | async-start | bytes 1392640 | tf_op jit(solution)/shard_map/all_gather | solution.py:210
  14.1 1.7 copy-start
  17.4 16.1 %copy-start.5 = (bf16[4,256,128]{2,1,0:T(8,128)(2,1)}, bf16[4,256,128]{2,1,0:T(8,128)(2,1)S(1)}, u32[]{:S(2)}) copy-start(bf16[4,256,128]{2,1,0:T(8,128)(2,1)S(1)} %get-tuple-element.26) | copy-start | bytes 786436
  17.4 16.1 %copy-start.6 = (bf16[1,256,128]{2,1,0:T(8,128)(2,1)}, bf16[1,256,128]{2,1,0:T(8,128)(2,1)S(1)}, u32[]{:S(2)}) copy-start(bf16[1,256,128]{2,1,0:T(8,128)(2,1)S(1)} %get-tuple-element.33) | copy-start | bytes 196612
  17.4 16.1 %copy-start.7 = (bf16[1,256,128]{2,1,0:T(8,128)(2,1)}, bf16[1,256,128]{2,1,0:T(8,128)(2,1)S(1)}, u32[]{:S(2)}) copy-start(bf16[1,256,128]{2,1,0:T(8,128)(2,1)S(1)} %get-tuple-element.22) | copy-start | bytes 196612
  17.4 16.1 %copy-start.11 = (bf16[8,256,128]{2,1,0:T(8,128)(2,1)}, bf16[8,256,128]{2,1,0:T(8,128)(2,1)S(1)}, u32[]{:S(2)}) copy-start(bf16[8,256,128]{2,1,0:T(8,128)(2,1)S(1)} %get-tuple-element.25) | copy-start | bytes 1572868
  17.4 2.2 %collective-permute-start.1 = (bf16[8,320,128]{2,1,0:T(8,128)(2,1)S(1)}, bf16[8,320,128]{2,1,0:T(8,128)(2,1)S(1)}, u32[]{:S(2)}, u32[]{:S(2)}) collective-permute-start(bf16[8,320,128]{2,1,0:T(8,128)(2,1)S(1)} %get-tuple-element.24), channel_id=1, source_target_pairs={{0,1},{1,0},{2,3},{3,2},{4,5},{5,4},{6,7},{7,6},{8,9},{9,8},{10,11... | collective-permute-start | bytes 1966088 | tf_op jit(solution)/shard_map/ppermute | solution.py:159
  19.6 13.8 %collective-permute-start.3 = (bf16[4,320,128]{2,1,0:T(8,128)(2,1)S(1)}, bf16[4,320,128]{2,1,0:T(8,128)(2,1)S(1)}, u32[]{:S(2)}, u32[]{:S(2)}) collective-permute-start(bf16[4,320,128]{2,1,0:T(8,128)(2,1)S(1)} %slice_add_fusion), channel_id=1, source_target_pairs={{0,2},{1,3},{2,0},{3,1},{4,6},{5,7},{6,4},{7,5},{8,10},{9,11},{10,... | collective-permute-start | bytes 983048 | tf_op jit(solution)/shard_map/ppermute | solution.py:159
  37.2 7.7 %collective-permute-start.5 = (bf16[2,320,128]{2,1,0:T(8,128)(2,1)S(1)}, bf16[2,320,128]{2,1,0:T(8,128)(2,1)S(1)}, u32[]{:S(2)}, u32[]{:S(2)}) collective-permute-start(bf16[2,320,128]{2,1,0:T(8,128)(2,1)S(1)} %slice_add_fusion.2), channel_id=1, source_target_pairs={{0,4},{1,5},{2,6},{3,7},{4,0},{5,1},{6,2},{7,3},{8,12},{9,13},{10,... | collective-permute-start | bytes 491528 | tf_op jit(solution)/shard_map/ppermute | solution.py:159
  44.9 4.6 %collective-permute-start.7 = (bf16[1,320,128]{2,1,0:T(8,128)(2,1)S(1)}, bf16[1,320,128]{2,1,0:T(8,128)(2,1)S(1)}, u32[]{:S(2)}, u32[]{:S(2)}) collective-permute-start(bf16[1,320,128]{2,1,0:T(8,128)(2,1)S(1)} %slice_add_fusion.9), channel_id=1, source_target_pairs={{0,8},{1,9},{2,10},{3,11},{4,12},{5,13},{6,14},{7,15},{8,0},{9,1},... | collective-permute-start | bytes 245768 | tf_op jit(solution)/shard_map/ppermute | solution.py:159
  50.2 49.8 %copy-start.4 = (bf16[2,32,64,128]{3,2,1,0:T(8,128)(2,1)S(1)}, bf16[2,32,64,128]{3,2,1,0:T(8,128)(2,1)}, u32[]{:S(2)}) copy-start(bf16[2,32,64,128]{3,2,1,0:T(8,128)(2,1)} %param.9) | copy-start | bytes 3145732
  50.2 37.6 %all-to-all-start.1 = ((bf16[16,4,64,128]{3,2,1,0:T(8,128)(2,1)}), bf16[16,4,64,128]{3,2,1,0:T(8,128)(2,1)}, u32[]{:S(2)}, u32[]{:S(2)}) async-start(bf16[16,4,64,128]{3,2,1,0:T(8,128)(2,1)} %bitcast.3), calls=%async_computation.1 | async-start | bytes 2097152 | tf_op jit(solution)/shard_map/all_to_all | solution.py:162
  57.5 30.2 %copy-start.8 = (bf16[1,256,128]{2,1,0:T(8,128)(2,1)S(1)}, bf16[1,256,128]{2,1,0:T(8,128)(2,1)}, u32[]{:S(2)}) copy-start(bf16[1,256,128]{2,1,0:T(8,128)(2,1)} %copy-done.7) | copy-start | bytes 196612
  57.5 42.4 %copy-start.2 = (bf16[2,64,5120]{2,1,0:T(8,128)(2,1)S(1)}, bf16[2,64,5120]{2,1,0:T(8,128)(2,1)}, u32[]{:S(2)}) copy-start(bf16[2,64,5120]{2,1,0:T(8,128)(2,1)} %x_ref.1) | copy-start | bytes 3932164
  57.5 2.2 %collective-permute-start = (bf16[8,256,128]{2,1,0:T(8,128)(2,1)}, bf16[8,256,128]{2,1,0:T(8,128)(2,1)S(1)}, u32[]{:S(2)}, u32[]{:S(2)}) collective-permute-start(bf16[8,256,128]{2,1,0:T(8,128)(2,1)} %copy-done.11), channel_id=1, source_target_pairs={{0,1},{1,0},{2,3},{3,2},{4,5},{5,4},{6,7},{7,6},{8,9},{9,8},{10,11... | collective-permute-start | bytes 1572872 | tf_op jit(solution)/shard_map/ppermute | solution.py:159
  60.7 14.1 %collective-permute-start.2 = (bf16[4,256,128]{2,1,0:T(8,128)(2,1)S(1)}, bf16[4,256,128]{2,1,0:T(8,128)(2,1)S(1)}, u32[]{:S(2)}, u32[]{:S(2)}) collective-permute-start(bf16[4,256,128]{2,1,0:T(8,128)(2,1)S(1)} %slice_add_fusion.1), channel_id=1, source_target_pairs={{0,2},{1,3},{2,0},{3,1},{4,6},{5,7},{6,4},{7,5},{8,10},{9,11},{10,... | collective-permute-start | bytes 786440 | tf_op jit(solution)/shard_map/ppermute | solution.py:159
  74.8 5.6 %collective-permute-start.4 = (bf16[2,256,128]{2,1,0:T(8,128)(2,1)S(1)}, bf16[2,256,128]{2,1,0:T(8,128)(2,1)S(1)}, u32[]{:S(2)}, u32[]{:S(2)}) collective-permute-start(bf16[2,256,128]{2,1,0:T(8,128)(2,1)S(1)} %slice_add_fusion.4), channel_id=1, source_target_pairs={{0,4},{1,5},{2,6},{3,7},{4,0},{5,1},{6,2},{7,3},{8,12},{9,13},{10,... | collective-permute-start | bytes 393224 | tf_op jit(solution)/shard_map/ppermute | solution.py:159
  81.2 6.4 %collective-permute-start.6 = (bf16[1,256,128]{2,1,0:T(8,128)(2,1)S(1)}, bf16[1,256,128]{2,1,0:T(8,128)(2,1)S(1)}, u32[]{:S(2)}, u32[]{:S(2)}) collective-permute-start(bf16[1,256,128]{2,1,0:T(8,128)(2,1)S(1)} %slice_add_fusion.12), channel_id=1, source_target_pairs={{0,8},{1,9},{2,10},{3,11},{4,12},{5,13},{6,14},{7,15},{8,0},{9,1},... | collective-permute-start | bytes 196616 | tf_op jit(solution)/shard_map/ppermute | solution.py:159
  100.0 1.3 copy-start.3
Sparse Core Ops, SparseCore 0:
  50.3 49.6 all-gather.1

commit v7 on v6

--- a/solution.py
+++ b/solution.py
@@ -9,6 +9,7 @@
 from jax.sharding import PartitionSpec as P
 
 LANES = 128
+LOW = 4
 ANY = pl.BlockSpec(memory_space=pl.ANY)
 VMEM = pl.BlockSpec(memory_space=pltpu.VMEM)
 SMEM = pl.BlockSpec(memory_space=pltpu.SMEM)
@@ -72,51 +73,51 @@
             ups[step][at, p * ranks : (p + 1) * ranks, :] = up[video, :, pl.ds(col, LANES)]
 
 
-def low_rank_kernel(shape, x_ref, g_ref, q_ref, out_ref, down):
-    devs, _, per_video, _, col_split, rows, tiles = shape
-    for dev in range(devs):
+def low_rank_kernel(shape, me_ref, x_ref, g_ref, out_ref, down):
+    devs, bits, per_video, _, col_split, rows, tiles = shape
+    for j in range(devs):
+        dev = me_ref[0] ^ reversed_bits(j, bits)
         video = dev // per_video
         place = dev % per_video
-        row = (place // col_split) * rows
+        row = pl.multiple_of((place // col_split) * rows, rows)
         for t in range(tiles):
-            col = ((place % col_split) * tiles + t) * LANES
-            down[video, row : row + rows, col : col + LANES] = g_ref[
-                dev, t * rows : (t + 1) * rows, :
-            ]
-    first = q_ref.shape[1]
-    out_ref[:, :first] = q_ref[...]
-    for s in range(x_ref.shape[0]):
-        low = lax.dot_general(
+            col = pl.multiple_of(((place % col_split) * tiles + t) * LANES, LANES)
+            down[video, pl.ds(row, rows), pl.ds(col, LANES)] = g_ref[j, t * rows : (t + 1) * rows, :]
+    parts = [
+        lax.dot_general(
             x_ref[s], down[s], (((1,), (1,)), ((), ())), preferred_element_type=jnp.float32
-        ).astype(out_ref.dtype)
-        half = low.shape[0] // 2
-        low = jnp.concatenate([low[:half], low[half:]], axis=1)
-        for dev in range(s * per_video, (s + 1) * per_video):
-            out_ref[dev, first:] = low
-
-
-def add_delta(base, low, up, second):
-    devs, toks, width = base.shape
-    ranks = up.shape[0]
+        )
+        for s in range(x_ref.shape[0])
+    ]
+    out_ref[...] = jnp.concatenate(parts, axis=1).astype(out_ref.dtype)
+
+
+def up_part(up_ref, video, videos, second):
+    up = jnp.concatenate([up_ref[...]] * videos, axis=0)
+    ranks = up_ref.shape[0]
     row = lax.broadcasted_iota(jnp.int32, up.shape, 0)
-    part = jnp.where(row // (ranks // 2) == second, up, jnp.zeros_like(up))
-    none = jnp.zeros_like(part)
-    deltas = [
-        jnp.dot(low, jnp.concatenate(pair, axis=0), preferred_element_type=jnp.float32)
-        for pair in ((part, none), (none, part))
-    ]
-    delta = jnp.concatenate([d.reshape(devs, toks // 2, width) for d in deltas], axis=1)
-    return (base.astype(jnp.float32) + delta).astype(base.dtype).reshape(devs * toks, width)
-
-
-def attend_kernel(block, up_ref, q_ref, low_ref, k_ref, v_ref, out_ref, q_mix):
+    half = (row % ranks) // (ranks // 2)
+    keep = (row // ranks == video) & (half == second)
+    return jnp.where(keep, up, jnp.zeros_like(up))
+
+
+def attend_kernel(per_video, block, me_ref, up_ref, q_ref, k_ref, v_ref, *refs):
+    low_refs, out_ref, low, q_mix = refs[:LOW], refs[LOW], refs[LOW + 1], refs[LOW + 2]
     devs, toks, width = q_ref.shape
     length = devs * toks
-    low = low_ref[...].reshape(length // 2, low_ref.shape[2])
-    up = up_ref[...]
+    videos = low.shape[2] // up_ref.shape[0]
+    me = me_ref[0]
+    for k in range(devs):
+        low[me ^ k] = low_refs[k % LOW][k // LOW]
+    low_all = low[...].reshape(length, low.shape[2])
+    up_q, up_v = (up_part(up_ref, me // per_video, videos, i) for i in range(2))
     keys = k_ref[...].reshape(length, width)
-    vals = add_delta(v_ref[...], low, up, 1)
-    q_mix[...] = add_delta(q_ref[...], low, up, 0)
+    delta_v = jnp.dot(low_all, up_v, preferred_element_type=jnp.float32)
+    vals = (v_ref[...].reshape(length, width).astype(jnp.float32) + delta_v).astype(jnp.bfloat16)
+    delta_q = jnp.dot(low_all, up_q, preferred_element_type=jnp.float32)
+    q_mix[...] = (q_ref[...].reshape(length, width).astype(jnp.float32) + delta_q).astype(
+        jnp.bfloat16
+    )
     scale = math.log2(math.e) / math.sqrt(width)
     for b in range(0, devs, block):
         q = q_mix[b * toks : (b + block) * toks, :]
@@ -199,23 +200,37 @@
     down_pieces, up_pieces = pieces[: bits + 1], pieces[bits + 1 :]
 
     down_got, up_got = [], []
+
+    def send_up(i, *others):
+        up_got.append(swap(after(halving(up_pieces, up_got, i), *others), 1 << i))
+
     for i in range(bits):
         piece = halving(down_pieces, down_got, i)
         if i == 2:
             piece = after(piece, keys)
+        if i >= 2:
+            piece = after(piece, up_got[i - 2])
+        if 0 < i < bits - 1:
+            send_up(i - 1, piece)
         down_got.append(swap(piece, 1 << i))
-        up_got.append(swap(after(halving(up_pieces, up_got, i), piece), 1 << i))
-    shard = halving(down_pieces, down_got, bits)
-    up_here = halving(up_pieces, up_got, bits).reshape(pairs, ranks, LANES)
-    gathered = lax.all_gather(shard, "seq", axis=0, tiled=True)
-    vals = exchange(after(by_pairs(values), shard))
-
-    asked = pl.pallas_call(
+    gathered = halving(down_pieces, down_got, bits)
+    for i in reversed(range(bits)):
+        if i >= bits - 3:
+            gathered = after(gathered, up_got[2 * bits - 4 - i])
+        if i >= bits - 2:
+            send_up(2 * bits - 3 - i, gathered)
+        if i == 1:
+            up_here = halving(up_pieces, up_got, bits).reshape(pairs, ranks, LANES)
+            asked = jnp.concatenate([by_pairs(values), by_pairs(queries)], axis=1)
+            asked = exchange(after(asked, gathered, up_here))
+        gathered = jnp.concatenate([gathered, swap(gathered, 1 << i)], axis=0)
+
+    low = pl.pallas_call(
         functools.partial(low_rank_kernel, shape),
-        in_specs=[VMEM, VMEM, VMEM],
+        in_specs=[SMEM, VMEM, VMEM],
         out_specs=VMEM,
         scratch_shapes=[pltpu.VMEM((videos, ranks, model_width), jnp.bfloat16)],
-        out_shape=jax.ShapeDtypeStruct((devs, pairs * toks + toks // 2, width), jnp.bfloat16),
+        out_shape=jax.ShapeDtypeStruct((toks, videos * ranks), jnp.bfloat16),
         compiler_params=pltpu.CompilerParams(vmem_limit_bytes=24 << 20),
         cost_estimate=pl.CostEstimate(
             flops=2 * videos * toks * ranks * model_width,
@@ -223,27 +238,25 @@
             transcendentals=0,
         ),
         name="low_rank",
-    )(
-        normed_token_features,
-        after(gathered, vals, up_here),
-        queries.reshape(devs, pairs * toks, width),
-    )
-    asked = exchange(asked)
-
+    )(me, normed_token_features, gathered)
+    far = jnp.stack([low] + [swap(low, LOW * i) for i in range(1, devs // LOW)])
+    lows = [far] + [swap(far, i) for i in range(1, LOW)]
+
+    low_spec = pl.BlockSpec((devs // LOW, toks, videos * ranks), lambda p: (0, 0, 0))
     part_spec = pl.BlockSpec((devs, pl.squeezed, toks, width), lambda p: (0, p, 0, 0))
+    later_spec = pl.BlockSpec((devs, pl.squeezed, toks, width), lambda p: (0, pairs + p, 0, 0))
     mixed = pl.pallas_call(
-        functools.partial(attend_kernel, math.gcd(devs, max(1, 512 // toks))),
+        functools.partial(attend_kernel, per_video, math.gcd(devs, max(1, 512 // toks))),
         grid=(pairs,),
-        in_specs=[
-            pl.BlockSpec((pl.squeezed, ranks, LANES), lambda p: (p, 0, 0)),
-            pl.BlockSpec((devs, toks, width), lambda p: (0, p, 0)),
-            pl.BlockSpec((devs, toks // 2, width), lambda p: (0, 2 * pairs, 0)),
-            part_spec,
-            part_spec,
-        ],
+        in_specs=[SMEM, pl.BlockSpec((pl.squeezed, ranks, LANES), lambda p: (p, 0, 0))]
+        + [later_spec, part_spec, part_spec]
+        + [low_spec] * LOW,
         out_specs=part_spec,
         out_shape=jax.ShapeDtypeStruct((devs, pairs, toks, width), jnp.bfloat16),
-        scratch_shapes=[pltpu.VMEM((length, width), jnp.bfloat16)],
+        scratch_shapes=[
+            pltpu.VMEM((devs, toks, videos * ranks), jnp.bfloat16),
+            pltpu.VMEM((length, width), jnp.bfloat16),
+        ],
         compiler_params=pltpu.CompilerParams(vmem_limit_bytes=48 << 20),
         cost_estimate=pl.CostEstimate(
             flops=4 * pairs * length * length * width,
@@ -251,7 +264,7 @@
             transcendentals=pairs * length * length,
         ),
         name="attend",
-    )(up_here, asked, asked, keys, vals)
+    )(me, up_here, asked, keys, asked, *lows)
     return exchange(mixed).reshape(videos, heads, toks, width)
 
 

time: 181 us -> 168 us (0.928)
  blocking collectives: 61.8 us -> 28.7 us
  waiting for transfers between devices: 60.9 us -> 81.4 us
  between operations: 13.6 us -> 0.21 us
  other arithmetic: 2.63 us -> 10.6 us
  starting transfers between devices: 26.5 us -> 31.1 us
    ppermute x8 -> x18, waiting for transfers between devices: 45 us -> 78.3 us  [swap(): return lax.ppermute(tensor, 'seq', [(i, i ^ k) for i in range(devs)])]
    all_to_all x2 -> x1, blocking collectives: 61.8 us -> 28.7 us  [exchange(): lax.all_to_all(tensor, 'seq', split_axis=0, concat_axis=0, tiled=True)]
    all_gather x1 -> x0, waiting for transfers between devices: 12.2 us -> none  [body(): gathered = lax.all_gather(shard, 'seq', axis=0, tiled=True)]
    ppermute x8 -> x18, starting transfers between devices: 11.6 us -> 18 us  [swap(): return lax.ppermute(tensor, 'seq', [(i, i ^ k) for i in range(devs)])]
    concatenate x0 -> x5, other arithmetic: none -> 4.44 us  [the longest x4 2.9 us: body(): gathered = jnp.concatenate([gathered, swap(gathered, 1 << i)], axis=0)]
    add x8, other arithmetic: 2.63 us -> 6.17 us  [halving(): return sum((r[h:h + size] for r in received), parts[i])]
    unnamed x25 -> x27, local copies, waits for them, and re-layouts: 4.07 us -> 2.75 us
  transfers between devices with their start and end apart: 11 -> 20, of which waited for: 10 -> 15; matrix products, arithmetic and copies ran while one was open for 1% -> 5% of each run, Pallas kernels for 1% -> 2%
where the time goes in v7:
time: 168 us; the launch traced here: 167 us
  waiting for transfers between devices  81.4 us (48%)
  starting transfers between devices  31.1 us (19%)
  blocking collectives  28.7 us (17%)
  Pallas kernels  12.3 us (7%)
  other arithmetic  10.6 us (6%)
  local copies, waits for them, and re-layouts  2.75 us (2%)
    ppermute x18, waiting for transfers between devices, swap(): return lax.ppermute(tensor, 'seq', [(i, i ^ k) for i in range(devs)])  78.3 us
    all_to_all x1, blocking collectives, exchange(): lax.all_to_all(tensor, 'seq', split_axis=0, concat_axis=0, tiled=True)  28.7 us
    ppermute x18, starting transfers between devices, swap(): return lax.ppermute(tensor, 'seq', [(i, i ^ k) for i in range(devs)])  18 us
    all_to_all x2, starting transfers between devices, exchange(): lax.all_to_all(tensor, 'seq', split_axis=0, concat_axis=0, tiled=True)  13.1 us
    pallas_call x1, Pallas kernels, body(): pl.pallas_call(functools.partial(attend_kernel, per_video, math.gcd(devs,...  9.12 us
    add x8, other arithmetic, halving(): return sum((r[h:h + size] for r in received), parts[i])  6.17 us
  transfers between devices with their start and end apart: 20, of which 15 were waited for; matrix products, arithmetic and copies ran while one was open for 5% of the time, Pallas kernels for 2%

profile of v7, /device:TPU:1, one launch (start us, length us, event | category | flops | bytes accessed | tf_op | source)
XLA Modules:
  0.0 167.1 jit_solution(14235158677267347997)
XLA Ops:
  0.0 7.5 %all-to-all-start = ((bf16[16,4,64,128]{3,2,1,0:T(8,128)(2,1)}), bf16[16,4,64,128]{3,2,1,0:T(8,128)(2,1)S(1)}, u32[]{:S(2)}, u32[]{:S(2)}) async-start(bf16[16,4,64,128]{3,2,1,0:T(8,128)(2,1)} %bitcast.13), calls=%async_computation | async-start | bytes 2097152 | tf_op jit(solution)/shard_map/all_to_all | solution.py:163
  7.5 1.7 %copy-done = bf16[4,64,5120]{2,1,0:T(8,128)(2,1)S(1)} copy-done((bf16[4,64,5120]{2,1,0:T(8,128)(2,1)S(1)}, bf16[4,64,5120]{2,1,0:T(8,128)(2,1)}, u32[]{:S(2)}) %copy-start) | copy-done | bytes 2621464
  9.3 2.3 %pick_factors.1 = (bf16[8,320,128]{2,1,0:T(8,128)(2,1)S(1)}, bf16[4,320,128]{2,1,0:T(8,128)(2,1)S(1)}, bf16[2,320,128]{2,1,0:T(8,128)(2,1)S(1)}, bf16[1,320,128]...) custom-call(s32[1]{0:T(128)} %bitcast.me_ref, ...), custom_call_target="tpu_custom_call" | custom-call | bytes 4718592 | tf_op jit(solution)/shard_map/pick_factors/pallas_call | solution.py:182
  11.6 0.3 collective-permute-start
  11.9 1.8 %collective-permute-done = bf16[8,320,128]{2,1,0:T(8,128)(2,1)S(1)} collective-permute-done((bf16[8,320,128]{2,1,0:T(8,128)(2,1)S(1)}, bf16[8,320,128]{2,1,0:T(8,128)(2,1)S(1)}, u32[]{:S(2)}, u32[]{:S(2)}) %collective-permute-start) | collective-permute-done | bytes 655392 | tf_op jit(solution)/shard_map/ppermute | solution.py:160
  13.8 1.5 collective-permute-start.2
  15.2 0.6 collective-permute-start.1
  15.9 11.0 %collective-permute-done.2 = bf16[4,320,128]{2,1,0:T(8,128)(2,1)S(1)} collective-permute-done((bf16[4,320,128]{2,1,0:T(8,128)(2,1)S(1)}, bf16[4,320,128]{2,1,0:T(8,128)(2,1)S(1)}, u32[]{:S(2)}, u32[]{:S(2)}) %collective-permute-start.2) | collective-permute-done | bytes 327712 | tf_op jit(solution)/shard_map/ppermute | solution.py:160
  26.9 0.7 slice_add_fusion.2
  27.5 3.1 %all-to-all-done.k_ref = bf16[16,4,64,128]{3,2,1,0:T(8,128)(2,1)S(1)} async-done(((bf16[16,4,64,128]{3,2,1,0:T(8,128)(2,1)}), bf16[16,4,64,128]{3,2,1,0:T(8,128)(2,1)S(1)}, u32[]{:S(2)}, u32[]{:S(2)}) %all-to-all-start) | async-done | bytes 1048608 | tf_op jit(solution)/shard_map/all_to_all | solution.py:163
  30.6 3.1 %collective-permute-start.4 = (bf16[2,320,128]{2,1,0:T(8,128)(2,1)}, bf16[2,320,128]{2,1,0:T(8,128)(2,1)S(1)}, u32[]{:S(2)}, u32[]{:S(2)}) collective-permute-start(bf16[2,320,128]{2,1,0:T(8,128)(2,1)} %slice_add_fusion.2), channel_id=1, source_target_pairs={{0,4},{1,5},{2,6},{3,7},{4,0},{5,1},{6,2},{7,3},{8,12},{9,13},{10,... | collective-permute-start | bytes 491528 | tf_op jit(solution)/shard_map/ppermute | solution.py:160
  33.7 1.0 slice_add_fusion.1
  34.7 1.3 collective-permute-start.3
  36.0 2.6 %collective-permute-done.4 = bf16[2,320,128]{2,1,0:T(8,128)(2,1)S(1)} collective-permute-done((bf16[2,320,128]{2,1,0:T(8,128)(2,1)}, bf16[2,320,128]{2,1,0:T(8,128)(2,1)S(1)}, u32[]{:S(2)}, u32[]{:S(2)}) %collective-permute-start.4) | collective-permute-done | bytes 163872 | tf_op jit(solution)/shard_map/ppermute | solution.py:160
  38.6 0.9 slice_add_fusion.6
  39.5 3.2 %collective-permute-done.3 = bf16[4,256,128]{2,1,0:T(8,128)(2,1)S(1)} collective-permute-done((bf16[4,256,128]{2,1,0:T(8,128)(2,1)S(1)}, bf16[4,256,128]{2,1,0:T(8,128)(2,1)S(1)}, u32[]{:S(2)}, u32[]{:S(2)}) %collective-permute-start.3) | collective-permute-done | bytes 262176 | tf_op jit(solution)/shard_map/ppermute | solution.py:160
  42.8 6.9 %collective-permute-done.5 = bf16[1,320,128]{2,1,0:T(8,128)(2,1)S(1)} collective-permute-done((bf16[1,320,128]{2,1,0:T(8,128)(2,1)S(1)}, bf16[1,320,128]{2,1,0:T(8,128)(2,1)S(1)}, u32[]{:S(2)}, u32[]{:S(2)}) %collective-permute-start.5) | collective-permute-done | bytes 81952 | tf_op jit(solution)/shard_map/ppermute | solution.py:160
  49.6 0.9 fusion
  50.5 0.1 collective-permute-start.7
  50.6 0.9 slice_add_fusion.4
  51.6 4.5 %collective-permute-done.7 = bf16[1,320,128]{2,1,0:T(8,128)(2,1)S(1)} collective-permute-done((bf16[1,320,128]{2,1,0:T(8,128)(2,1)S(1)}, bf16[1,320,128]{2,1,0:T(8,128)(2,1)S(1)}, u32[]{:S(2)}, u32[]{:S(2)}) %collective-permute-start.7) | collective-permute-done | bytes 81952 | tf_op jit(solution)/shard_map/ppermute | solution.py:160
  56.2 2.1 %collective-permute-done.6 = bf16[2,256,128]{2,1,0:T(8,128)(2,1)S(1)} collective-permute-done((bf16[2,256,128]{2,1,0:T(8,128)(2,1)S(1)}, bf16[2,256,128]{2,1,0:T(8,128)(2,1)S(1)}, u32[]{:S(2)}, u32[]{:S(2)}) %collective-permute-start.6) | collective-permute-done | bytes 131104 | tf_op jit(solution)/shard_map/ppermute | solution.py:160
  58.3 0.9 slice_add_fusion.12
  59.2 1.5 pad_maximum_fusion
  60.8 1.4 collective-permute-start.9
  62.2 1.0 collective-permute-done.8
  63.2 0.9 fusion.1
  64.1 2.0 %collective-permute-done.9 = bf16[2,320,128]{2,1,0:T(8,128)(2,1)S(1)} collective-permute-done((bf16[2,320,128]{2,1,0:T(8,128)(2,1)S(1)}, bf16[2,320,128]{2,1,0:T(8,128)(2,1)S(1)}, u32[]{:S(2)}, u32[]{:S(2)}) %collective-permute-start.9) | collective-permute-done | bytes 163872 | tf_op jit(solution)/shard_map/ppermute | solution.py:160
  66.1 0.8 pad_maximum_fusion.3
  66.8 5.6 %all-to-all-start.1 = ((bf16[16,8,64,128]{3,2,1,0:T(8,128)(2,1)}), bf16[16,8,64,128]{3,2,1,0:T(8,128)(2,1)S(1)}, u32[]{:S(2)}, u32[]{:S(2)}) async-start(bf16[16,8,64,128]{3,2,1,0:T(8,128)(2,1)} %pad_maximum_fusion), calls=%async_computation.1 | async-start | bytes 4194304 | tf_op jit(solution)/shard_map/all_to_all | solution.py:163
  72.4 1.5 collective-permute-start.10
  73.9 24.3 %collective-permute-done.10 = bf16[4,320,128]{2,1,0:T(8,128)(2,1)S(1)} collective-permute-done((bf16[4,320,128]{2,1,0:T(8,128)(2,1)}, bf16[4,320,128]{2,1,0:T(8,128)(2,1)S(1)}, u32[]{:S(2)}, u32[]{:S(2)}) %collective-permute-start.10) | collective-permute-done | bytes 327712 | tf_op jit(solution)/shard_map/ppermute | solution.py:160
  98.2 1.0 pad_maximum_fusion.2
  99.2 1.3 collective-permute-start.11
  100.5 1.7 %collective-permute-done.11 = bf16[8,320,128]{2,1,0:T(8,128)(2,1)S(1)} collective-permute-done((bf16[8,320,128]{2,1,0:T(8,128)(2,1)S(1)}, bf16[8,320,128]{2,1,0:T(8,128)(2,1)S(1)}, u32[]{:S(2)}, u32[]{:S(2)}) %collective-permute-start.11) | collective-permute-done | bytes 655392 | tf_op jit(solution)/shard_map/ppermute | solution.py:160
  102.2 1.1 pad_maximum_fusion.1.g_ref
  103.3 0.9 low_rank.1
  104.3 3.4 %collective-permute-start.13 = (bf16[64,128]{1,0:T(8,128)(2,1)S(1)}, bf16[64,128]{1,0:T(8,128)(2,1)S(1)}, u32[]{:S(2)}, u32[]{:S(2)}) collective-permute-start(bf16[64,128]{1,0:T(8,128)(2,1)S(1)} %low_rank.1), channel_id=1, source_target_pairs={{0,8},{1,9},{2,10},{3,11},{4,12},{5,13},{6,14},{7,15},{8,0},{9,1},... | collective-permute-start | bytes 49160 | tf_op jit(solution)/shard_map/ppermute | solution.py:160
  107.7 0.1 collective-permute-start.14
  107.8 13.6 %collective-permute-done.13 = bf16[64,128]{1,0:T(8,128)(2,1)S(1)} collective-permute-done((bf16[64,128]{1,0:T(8,128)(2,1)S(1)}, bf16[64,128]{1,0:T(8,128)(2,1)S(1)}, u32[]{:S(2)}, u32[]{:S(2)}) %collective-permute-start.13) | collective-permute-done | bytes 16416 | tf_op jit(solution)/shard_map/ppermute | solution.py:160
  121.5 1.4 collective-permute-start.15
  122.9 1.3 collective-permute-start.16
  124.2 0.4 collective-permute-start.17
  124.6 2.0 %collective-permute-done.16.refs_2_ = bf16[4,64,128]{2,1,0:T(8,128)(2,1)S(1)} collective-permute-done((bf16[4,64,128]{2,1,0:T(8,128)(2,1)S(1)}, bf16[4,64,128]{2,1,0:T(8,128)(2,1)S(1)}, u32[]{:S(2)}, u32[]{:S(2)}) %collective-permute-start.16) | collective-permute-done | bytes 65568 | tf_op jit(solution)/shard_map/ppermute | solution.py:160
  126.6 1.7 %collective-permute-done.17.refs_3_ = bf16[4,64,128]{2,1,0:T(8,128)(2,1)S(1)} collective-permute-done((bf16[4,64,128]{2,1,0:T(8,128)(2,1)S(1)}, bf16[4,64,128]{2,1,0:T(8,128)(2,1)S(1)}, u32[]{:S(2)}, u32[]{:S(2)}) %collective-permute-start.17) | collective-permute-done | bytes 65568 | tf_op jit(solution)/shard_map/ppermute | solution.py:160
  128.2 9.1 %attend.1 = bf16[16,4,64,128]{3,2,1,0:T(8,128)(2,1)S(1)} custom-call(s32[1]{0:T(128)} %bitcast.me_ref, bf16[4,64,128]{2,1,0:T(8,128)(2,1)S(1)} %bitcast.11, bf16[16,8,64,128]{3,2,1,0:T(8,128)(2,1)S(1)} %all-to-all-done.1.q_ref.v_ref, bf16[16,4,64,128]{3,2,1,0:T(8,128)(2,1)S(1)} %all-to-all-done.k_ref, ...), custom_call_target="tpu_custom_call" | custom-call | flops 2147483648 | bytes 4194304 | tf_op jit(solution)/shard_map/attend/pallas_call | solution.py:248
  137.4 28.7 %all_to_all.15 = bf16[16,4,64,128]{3,2,1,0:T(8,128)(2,1)S(1)} all-to-all(bf16[16,4,64,128]{3,2,1,0:T(8,128)(2,1)S(1)} %attend.1), channel_id=1, replica_groups=mesh['grp'=2,'seq'=16] {'seq'}, dimensions={0} | all-to-all | bytes 2097152 | tf_op jit(solution)/shard_map/all_to_all | solution.py:163
  166.1 1.0 copy.10
  (37 shorter events, 0.4 us)
Async XLA Ops:
  0.0 7.5 %copy-start.1 = (bf16[4,64,4096]{2,1,0:T(8,128)(2,1)S(1)}, bf16[4,64,4096]{2,1,0:T(8,128)(2,1)}, u32[]{:S(2)}) copy-start(bf16[4,64,4096]{2,1,0:T(8,128)(2,1)} %up_ref.1) | copy-start | bytes 6291460
  0.0 7.5 %copy-start.9 = (s32[64]{0:T(128)S(1)}, s32[64]{0:T(128)}, u32[]{:S(2)}) copy-start(s32[64]{0:T(128)} %row_ref.1) | copy-start | bytes 772
  0.0 7.5 %copy-start.10 = (s32[2]{0:T(128)S(1)}, s32[2]{0:T(128)}, u32[]{:S(2)}) copy-start(s32[2]{0:T(128)} %req_ref.1) | copy-start | bytes 28
  0.0 30.6 %all-to-all-start = ((bf16[16,4,64,128]{3,2,1,0:T(8,128)(2,1)}), bf16[16,4,64,128]{3,2,1,0:T(8,128)(2,1)S(1)}, u32[]{:S(2)}, u32[]{:S(2)}) async-start(bf16[16,4,64,128]{3,2,1,0:T(8,128)(2,1)} %bitcast.13), calls=%async_computation | async-start | bytes 2097152 | tf_op jit(solution)/shard_map/all_to_all | solution.py:163
  7.5 1.7 %copy-start = (bf16[4,64,5120]{2,1,0:T(8,128)(2,1)S(1)}, bf16[4,64,5120]{2,1,0:T(8,128)(2,1)}, u32[]{:S(2)}) copy-start(bf16[4,64,5120]{2,1,0:T(8,128)(2,1)} %down_ref.1) | copy-start | bytes 7864324
  11.5 15.3 %copy-start.3 = (bf16[1,320,128]{2,1,0:T(8,128)(2,1)}, bf16[1,320,128]{2,1,0:T(8,128)(2,1)S(1)}, u32[]{:S(2)}) copy-start(bf16[1,320,128]{2,1,0:T(8,128)(2,1)S(1)} %get-tuple-element.38) | copy-start | bytes 245764
  11.6 15.3 %copy-start.4 = (bf16[1,320,128]{2,1,0:T(8,128)(2,1)}, bf16[1,320,128]{2,1,0:T(8,128)(2,1)S(1)}, u32[]{:S(2)}) copy-start(bf16[1,320,128]{2,1,0:T(8,128)(2,1)S(1)} %get-tuple-element.37) | copy-start | bytes 245764
  11.6 15.3 %copy-start.5 = (bf16[1,256,128]{2,1,0:T(8,128)(2,1)}, bf16[1,256,128]{2,1,0:T(8,128)(2,1)S(1)}, u32[]{:S(2)}) copy-start(bf16[1,256,128]{2,1,0:T(8,128)(2,1)S(1)} %get-tuple-element.42) | copy-start | bytes 196612
  11.6 15.3 %copy-start.7 = (bf16[1,256,128]{2,1,0:T(8,128)(2,1)}, bf16[1,256,128]{2,1,0:T(8,128)(2,1)S(1)}, u32[]{:S(2)}) copy-start(bf16[1,256,128]{2,1,0:T(8,128)(2,1)S(1)} %get-tuple-element.26) | copy-start | bytes 196612
  11.6 2.2 %collective-permute-start = (bf16[8,320,128]{2,1,0:T(8,128)(2,1)S(1)}, bf16[8,320,128]{2,1,0:T(8,128)(2,1)S(1)}, u32[]{:S(2)}, u32[]{:S(2)}) collective-permute-start(bf16[8,320,128]{2,1,0:T(8,128)(2,1)S(1)} %get-tuple-element.29), channel_id=1, source_target_pairs={{0,1},{1,0},{2,3},{3,2},{4,5},{5,4},{6,7},{7,6},{8,9},{9,8},{10,11... | collective-permute-start | bytes 1966088 | tf_op jit(solution)/shard_map/ppermute | solution.py:160
  13.8 45.5 %copy-start.11 = (bf16[2,32,64,128]{3,2,1,0:T(8,128)(2,1)S(1)}, bf16[2,32,64,128]{3,2,1,0:T(8,128)(2,1)}, u32[]{:S(2)}) copy-start(bf16[2,32,64,128]{3,2,1,0:T(8,128)(2,1)} %param.9) | copy-start | bytes 3145732
  13.8 13.0 %collective-permute-start.2 = (bf16[4,320,128]{2,1,0:T(8,128)(2,1)S(1)}, bf16[4,320,128]{2,1,0:T(8,128)(2,1)S(1)}, u32[]{:S(2)}, u32[]{:S(2)}) collective-permute-start(bf16[4,320,128]{2,1,0:T(8,128)(2,1)S(1)} %slice_add_fusion), channel_id=1, source_target_pairs={{0,2},{1,3},{2,0},{3,1},{4,6},{5,7},{6,4},{7,5},{8,10},{9,11},{10,... | collective-permute-start | bytes 983048 | tf_op jit(solution)/shard_map/ppermute | solution.py:160
  15.2 15.4 %collective-permute-start.1 = (bf16[8,256,128]{2,1,0:T(8,128)(2,1)}, bf16[8,256,128]{2,1,0:T(8,128)(2,1)}, u32[]{:S(2)}, u32[]{:S(2)}) collective-permute-start(bf16[8,256,128]{2,1,0:T(8,128)(2,1)} %get-tuple-element.30), channel_id=1, source_target_pairs={{0,1},{1,0},{2,3},{3,2},{4,5},{5,4},{6,7},{7,6},{8,9},{9,8},{10,11... | collective-permute-start | bytes 1572872 | tf_op jit(solution)/shard_map/ppermute | solution.py:160
  27.5 30.7 %copy-start.6 = (bf16[1,256,128]{2,1,0:T(8,128)(2,1)S(1)}, bf16[1,256,128]{2,1,0:T(8,128)(2,1)}, u32[]{:S(2)}) copy-start(bf16[1,256,128]{2,1,0:T(8,128)(2,1)} %copy-done.5) | copy-start | bytes 196612
  30.6 28.6 %copy-start.12 = (bf16[2,32,64,128]{3,2,1,0:T(8,128)(2,1)S(1)}, bf16[2,32,64,128]{3,2,1,0:T(8,128)(2,1)}, u32[]{:S(2)}) copy-start(bf16[2,32,64,128]{3,2,1,0:T(8,128)(2,1)} %param.11) | copy-start | bytes 3145732
  30.6 8.0 %collective-permute-start.4 = (bf16[2,320,128]{2,1,0:T(8,128)(2,1)}, bf16[2,320,128]{2,1,0:T(8,128)(2,1)S(1)}, u32[]{:S(2)}, u32[]{:S(2)}) collective-permute-start(bf16[2,320,128]{2,1,0:T(8,128)(2,1)} %slice_add_fusion.2), channel_id=1, source_target_pairs={{0,4},{1,5},{2,6},{3,7},{4,0},{5,1},{6,2},{7,3},{8,12},{9,13},{10,... | collective-permute-start | bytes 491528 | tf_op jit(solution)/shard_map/ppermute | solution.py:160
  34.7 8.0 %collective-permute-start.3 = (bf16[4,256,128]{2,1,0:T(8,128)(2,1)S(1)}, bf16[4,256,128]{2,1,0:T(8,128)(2,1)S(1)}, u32[]{:S(2)}, u32[]{:S(2)}) collective-permute-start(bf16[4,256,128]{2,1,0:T(8,128)(2,1)S(1)} %slice_add_fusion.1), channel_id=1, source_target_pairs={{0,2},{1,3},{2,0},{3,1},{4,6},{5,7},{6,4},{7,5},{8,10},{9,11},{10,... | collective-permute-start | bytes 786440 | tf_op jit(solution)/shard_map/ppermute | solution.py:160
  42.7 6.9 %collective-permute-start.5 = (bf16[1,320,128]{2,1,0:T(8,128)(2,1)S(1)}, bf16[1,320,128]{2,1,0:T(8,128)(2,1)S(1)}, u32[]{:S(2)}, u32[]{:S(2)}) collective-permute-start(bf16[1,320,128]{2,1,0:T(8,128)(2,1)S(1)} %slice_add_fusion.6), channel_id=1, source_target_pairs={{0,8},{1,9},{2,10},{3,11},{4,12},{5,13},{6,14},{7,15},{8,0},{9,1},... | collective-permute-start | bytes 245768 | tf_op jit(solution)/shard_map/ppermute | solution.py:160
  50.5 5.6 %collective-permute-start.7 = (bf16[1,320,128]{2,1,0:T(8,128)(2,1)S(1)}, bf16[1,320,128]{2,1,0:T(8,128)(2,1)S(1)}, u32[]{:S(2)}, u32[]{:S(2)}) collective-permute-start(bf16[1,320,128]{2,1,0:T(8,128)(2,1)S(1)} %fusion), channel_id=1, source_target_pairs={{0,8},{1,9},{2,10},{3,11},{4,12},{5,13},{6,14},{7,15},{8,0},{9,1},... | collective-permute-start | bytes 245768 | tf_op jit(solution)/shard_map/ppermute | solution.py:160
  51.6 6.7 %collective-permute-start.6 = (bf16[2,256,128]{2,1,0:T(8,128)(2,1)S(1)}, bf16[2,256,128]{2,1,0:T(8,128)(2,1)S(1)}, u32[]{:S(2)}, u32[]{:S(2)}) collective-permute-start(bf16[2,256,128]{2,1,0:T(8,128)(2,1)S(1)} %slice_add_fusion.4), channel_id=1, source_target_pairs={{0,4},{1,5},{2,6},{3,7},{4,0},{5,1},{6,2},{7,3},{8,12},{9,13},{10,... | collective-permute-start | bytes 393224 | tf_op jit(solution)/shard_map/ppermute | solution.py:160
  59.1 4.1 %collective-permute-start.8 = (bf16[1,256,128]{2,1,0:T(8,128)(2,1)S(1)}, bf16[1,256,128]{2,1,0:T(8,128)(2,1)S(1)}, u32[]{:S(2)}, u32[]{:S(2)}) collective-permute-start(bf16[1,256,128]{2,1,0:T(8,128)(2,1)S(1)} %slice_add_fusion.12), channel_id=1, source_target_pairs={{0,8},{1,9},{2,10},{3,11},{4,12},{5,13},{6,14},{7,15},{8,0},{9,1},... | collective-permute-start | bytes 196616 | tf_op jit(solution)/shard_map/ppermute | solution.py:160
  59.2 4.0 %copy-start.8 = (bf16[1,256,128]{2,1,0:T(8,128)(2,1)S(1)}, bf16[1,256,128]{2,1,0:T(8,128)(2,1)}, u32[]{:S(2)}) copy-start(bf16[1,256,128]{2,1,0:T(8,128)(2,1)} %copy-done.7) | copy-start | bytes 196612
  60.8 5.3 %collective-permute-start.9 = (bf16[2,320,128]{2,1,0:T(8,128)(2,1)S(1)}, bf16[2,320,128]{2,1,0:T(8,128)(2,1)S(1)}, u32[]{:S(2)}, u32[]{:S(2)}) collective-permute-start(bf16[2,320,128]{2,1,0:T(8,128)(2,1)S(1)} %pad_maximum_fusion.4), channel_id=1, source_target_pairs={{0,4},{1,5},{2,6},{3,7},{4,0},{5,1},{6,2},{7,3},{8,12},{9,13},{10,... | collective-permute-start | bytes 491528 | tf_op jit(solution)/shard_map/ppermute | solution.py:160
  66.8 61.4 %all-to-all-start.1 = ((bf16[16,8,64,128]{3,2,1,0:T(8,128)(2,1)}), bf16[16,8,64,128]{3,2,1,0:T(8,128)(2,1)S(1)}, u32[]{:S(2)}, u32[]{:S(2)}) async-start(bf16[16,8,64,128]{3,2,1,0:T(8,128)(2,1)} %pad_maximum_fusion), calls=%async_computation.1 | async-start | bytes 4194304 | tf_op jit(solution)/shard_map/all_to_all | solution.py:163
  72.4 30.9 %copy-start.2 = (bf16[2,64,5120]{2,1,0:T(8,128)(2,1)S(1)}, bf16[2,64,5120]{2,1,0:T(8,128)(2,1)}, u32[]{:S(2)}) copy-start(bf16[2,64,5120]{2,1,0:T(8,128)(2,1)} %x_ref.1) | copy-start | bytes 3932164
  72.4 25.8 %collective-permute-start.10 = (bf16[4,320,128]{2,1,0:T(8,128)(2,1)}, bf16[4,320,128]{2,1,0:T(8,128)(2,1)S(1)}, u32[]{:S(2)}, u32[]{:S(2)}) collective-permute-start(bf16[4,320,128]{2,1,0:T(8,128)(2,1)} %pad_maximum_fusion.3), channel_id=1, source_target_pairs={{0,2},{1,3},{2,0},{3,1},{4,6},{5,7},{6,4},{7,5},{8,10},{9,11},{10,... | collective-permute-start | bytes 983048 | tf_op jit(solution)/shard_map/ppermute | solution.py:160
  99.2 3.0 %collective-permute-start.11 = (bf16[8,320,128]{2,1,0:T(8,128)(2,1)S(1)}, bf16[8,320,128]{2,1,0:T(8,128)(2,1)S(1)}, u32[]{:S(2)}, u32[]{:S(2)}) collective-permute-start(bf16[8,320,128]{2,1,0:T(8,128)(2,1)S(1)} %pad_maximum_fusion.2), channel_id=1, source_target_pairs={{0,1},{1,0},{2,3},{3,2},{4,5},{5,4},{6,7},{7,6},{8,9},{9,8},{10,11... | collective-permute-start | bytes 1966088 | tf_op jit(solution)/shard_map/ppermute | solution.py:160
  104.2 3.6 %collective-permute-start.12 = (bf16[64,128]{1,0:T(8,128)(2,1)S(1)}, bf16[64,128]{1,0:T(8,128)(2,1)S(1)}, u32[]{:S(2)}, u32[]{:S(2)}) collective-permute-start(bf16[64,128]{1,0:T(8,128)(2,1)S(1)} %low_rank.1), channel_id=1, source_target_pairs={{0,4},{1,5},{2,6},{3,7},{4,0},{5,1},{6,2},{7,3},{8,12},{9,13},{10,... | collective-permute-start | bytes 49160 | tf_op jit(solution)/shard_map/ppermute | solution.py:160
  104.3 17.2 %collective-permute-start.13 = (bf16[64,128]{1,0:T(8,128)(2,1)S(1)}, bf16[64,128]{1,0:T(8,128)(2,1)S(1)}, u32[]{:S(2)}, u32[]{:S(2)}) collective-permute-start(bf16[64,128]{1,0:T(8,128)(2,1)S(1)} %low_rank.1), channel_id=1, source_target_pairs={{0,8},{1,9},{2,10},{3,11},{4,12},{5,13},{6,14},{7,15},{8,0},{9,1},... | collective-permute-start | bytes 49160 | tf_op jit(solution)/shard_map/ppermute | solution.py:160
  107.7 13.7 %collective-permute-start.14 = (bf16[64,128]{1,0:T(8,128)(2,1)S(1)}, bf16[64,128]{1,0:T(8,128)(2,1)S(1)}, u32[]{:S(2)}, u32[]{:S(2)}) collective-permute-start(bf16[64,128]{1,0:T(8,128)(2,1)S(1)} %low_rank.1), channel_id=1, source_target_pairs={{0,12},{1,13},{2,14},{3,15},{4,8},{5,9},{6,10},{7,11},{8,4},{9,5},... | collective-permute-start | bytes 49160 | tf_op jit(solution)/shard_map/ppermute | solution.py:160
  121.5 3.1 %collective-permute-start.15 = (bf16[4,64,128]{2,1,0:T(8,128)(2,1)S(1)}, bf16[4,64,128]{2,1,0:T(8,128)(2,1)S(1)}, u32[]{:S(2)}, u32[]{:S(2)}) collective-permute-start(bf16[4,64,128]{2,1,0:T(8,128)(2,1)S(1)} %pad_maximum_fusion.5.refs_0_), channel_id=1, source_target_pairs={{0,1},{1,0},{2,3},{3,2},{4,5},{5,4},{6,7},{7,6},{8,9},{9,8},{10,11... | collective-permute-start | bytes 196616 | tf_op jit(solution)/shard_map/ppermute | solution.py:160
  122.9 3.7 %collective-permute-start.16 = (bf16[4,64,128]{2,1,0:T(8,128)(2,1)S(1)}, bf16[4,64,128]{2,1,0:T(8,128)(2,1)S(1)}, u32[]{:S(2)}, u32[]{:S(2)}) collective-permute-start(bf16[4,64,128]{2,1,0:T(8,128)(2,1)S(1)} %pad_maximum_fusion.5.refs_0_), channel_id=1, source_target_pairs={{0,2},{1,3},{2,0},{3,1},{4,6},{5,7},{6,4},{7,5},{8,10},{9,11},{10,... | collective-permute-start | bytes 196616 | tf_op jit(solution)/shard_map/ppermute | solution.py:160
  124.2 4.0 %collective-permute-start.17 = (bf16[4,64,128]{2,1,0:T(8,128)(2,1)S(1)}, bf16[4,64,128]{2,1,0:T(8,128)(2,1)S(1)}, u32[]{:S(2)}, u32[]{:S(2)}) collective-permute-start(bf16[4,64,128]{2,1,0:T(8,128)(2,1)S(1)} %pad_maximum_fusion.5.refs_0_), channel_id=1, source_target_pairs={{0,3},{1,2},{2,1},{3,0},{4,7},{5,6},{6,5},{7,4},{8,11},{9,10},{10,... | collective-permute-start | bytes 196616 | tf_op jit(solution)/shard_map/ppermute | solution.py:160

commit v8 on v7

--- a/solution.py
+++ b/solution.py
@@ -30,8 +30,8 @@
 
 def pick_kernel(shape, me_ref, row_ref, req_ref, down_ref, up_ref, *refs):
     devs, bits, per_video, pairs, col_split, rows, tiles = shape
-    downs, ups = refs[: bits + 1], refs[bits + 1 : 2 * bits + 2]
-    down, up, sems = refs[2 * bits + 2 :]
+    downs, ups = refs[:bits], refs[bits : 2 * bits + 1]
+    down, up, sems = refs[2 * bits + 1 :]
     slots, ranks, _ = down_ref.shape
     videos = down.shape[0]
     me = me_ref[0]
@@ -65,7 +65,7 @@
         row = pl.multiple_of((place // col_split) * rows, rows)
         for t in range(tiles):
             col = pl.multiple_of(((place % col_split) * tiles + t) * LANES, LANES)
-            downs[step][at, t * rows : (t + 1) * rows, :] = down[
+            downs[min(step, bits - 1)][at if j > 1 else j, t * rows : (t + 1) * rows, :] = down[
                 video, pl.ds(row, rows), pl.ds(col, LANES)
             ]
         for p in range(pairs):
@@ -176,13 +176,13 @@
     keys = exchange(by_pairs(projected_keys))
 
     steps = [devs >> (i + 1) for i in range(bits)] + [1]
-    piece_shapes = [(h, tiles * rows, LANES) for h in steps] + [
+    piece_shapes = [(h, tiles * rows, LANES) for h in steps[: bits - 1] + [2]] + [
         (h, pairs * ranks, LANES) for h in steps
     ]
     pieces = pl.pallas_call(
         functools.partial(pick_kernel, shape),
         in_specs=[SMEM, SMEM, SMEM, ANY, ANY],
-        out_specs=[VMEM] * (2 * bits + 2),
+        out_specs=[VMEM] * (2 * bits + 1),
         out_shape=[jax.ShapeDtypeStruct(s, jnp.bfloat16) for s in piece_shapes],
         scratch_shapes=[
             pltpu.VMEM((videos, ranks, model_width), jnp.bfloat16),
@@ -197,32 +197,32 @@
         ),
         name="pick_factors",
     )(me, adapter_store_row, requests, adapter_down_factors, adapter_up_factors)
-    down_pieces, up_pieces = pieces[: bits + 1], pieces[bits + 1 :]
+    down_pieces, up_pieces = pieces[:bits], pieces[bits:]
 
     down_got, up_got = [], []
 
     def send_up(i, *others):
         up_got.append(swap(after(halving(up_pieces, up_got, i), *others), 1 << i))
 
-    for i in range(bits):
+    for i in range(bits - 1):
         piece = halving(down_pieces, down_got, i)
+        if i == 1:
+            send_up(0, piece)
         if i == 2:
-            piece = after(piece, keys)
-        if i >= 2:
-            piece = after(piece, up_got[i - 2])
-        if 0 < i < bits - 1:
-            send_up(i - 1, piece)
+            piece = after(piece, keys, up_got[0])
         down_got.append(swap(piece, 1 << i))
-    gathered = halving(down_pieces, down_got, bits)
-    for i in reversed(range(bits)):
-        if i >= bits - 3:
-            gathered = after(gathered, up_got[2 * bits - 4 - i])
-        if i >= bits - 2:
-            send_up(2 * bits - 3 - i, gathered)
+    gathered = sum((r[:2] for r in down_got), down_pieces[-1])
+    other = swap(gathered, 1 << (bits - 1))
+    gathered = gathered + jnp.concatenate([other[1:], other[:1]], axis=0)
+    for i in reversed(range(bits - 1)):
         if i == 1:
-            up_here = halving(up_pieces, up_got, bits).reshape(pairs, ranks, LANES)
             asked = jnp.concatenate([by_pairs(values), by_pairs(queries)], axis=1)
-            asked = exchange(after(asked, gathered, up_here))
+            asked = exchange(after(asked, gathered))
+            send_up(1, gathered)
+        if i == 0:
+            gathered = after(gathered, up_got[1])
+            for j in range(2, bits - 1):
+                send_up(j, gathered)
         gathered = jnp.concatenate([gathered, swap(gathered, 1 << i)], axis=0)
 
     low = pl.pallas_call(
@@ -240,6 +240,9 @@
         name="low_rank",
     )(me, normed_token_features, gathered)
     far = jnp.stack([low] + [swap(low, LOW * i) for i in range(1, devs // LOW)])
+    far = after(far, up_got[-1])
+    send_up(bits - 1)
+    up_here = halving(up_pieces, up_got, bits).reshape(pairs, ranks, LANES)
     lows = [far] + [swap(far, i) for i in range(1, LOW)]
 
     low_spec = pl.BlockSpec((devs // LOW, toks, videos * ranks), lambda p: (0, 0, 0))

time: 168 us -> 159 us (0.946)
  waiting for transfers between devices: 81.4 us -> 72.8 us
  starting transfers between devices: 31.1 us -> 32.9 us
    ppermute x18 -> x17, waiting for transfers between devices: 78.3 us -> 69.9 us  [swap(): return lax.ppermute(tensor, 'seq', [(i, i ^ k) for i in range(devs)])]
    all_to_all x2, starting transfers between devices: 13.1 us -> 14.9 us  [exchange(): lax.all_to_all(tensor, 'seq', split_axis=0, concat_axis=0, tiled=True)]
    add x8 -> x6, other arithmetic: 6.17 us -> 4.41 us  [halving(): return sum((r[h:h + size] for r in received), parts[i])]
    ppermute x18 -> x17, starting transfers between devices: 18 us -> 18 us  [swap(): return lax.ppermute(tensor, 'seq', [(i, i ^ k) for i in range(devs)])]
  transfers between devices with their start and end apart: 20 -> 19, of which waited for: 15 -> 13; matrix products, arithmetic and copies ran while one was open for 5% -> 4% of each run, Pallas kernels for 2% -> 2%
where the time goes in v8:
time: 159 us
  waiting for transfers between devices  72.8 us (46%)
  starting transfers between devices  32.9 us (21%)
  blocking collectives  28.4 us (18%)
  Pallas kernels  11.5 us (7%)
  other arithmetic  9.94 us (6%)
  local copies, waits for them, and re-layouts  2.81 us (2%)
    ppermute x17, waiting for transfers between devices, swap(): return lax.ppermute(tensor, 'seq', [(i, i ^ k) for i in range(devs)])  69.9 us
    all_to_all x1, blocking collectives, exchange(): lax.all_to_all(tensor, 'seq', split_axis=0, concat_axis=0, tiled=True)  28.4 us
    ppermute x17, starting transfers between devices, swap(): return lax.ppermute(tensor, 'seq', [(i, i ^ k) for i in range(devs)])  18 us
    all_to_all x2, starting transfers between devices, exchange(): lax.all_to_all(tensor, 'seq', split_axis=0, concat_axis=0, tiled=True)  14.9 us
    pallas_call x1, Pallas kernels, body(): pl.pallas_call(functools.partial(attend_kernel, per_video, math.gcd(devs,...  9.12 us
    add x6, other arithmetic, halving(): return sum((r[h:h + size] for r in received), parts[i])  4.41 us
  transfers between devices with their start and end apart: 19, of which 13 were waited for; matrix products, arithmetic and copies ran while one was open for 4% of the time, Pallas kernels for 2%

profile of v8, /device:TPU:1, one launch (start us, length us, event | category | flops | bytes accessed | tf_op | source)
XLA Modules:
  0.0 158.7 jit_solution(6944821762359440494)
XLA Ops:
  0.0 7.5 %all-to-all-start = ((bf16[16,4,64,128]{3,2,1,0:T(8,128)(2,1)}), bf16[16,4,64,128]{3,2,1,0:T(8,128)(2,1)S(1)}, u32[]{:S(2)}, u32[]{:S(2)}) async-start(bf16[16,4,64,128]{3,2,1,0:T(8,128)(2,1)} %bitcast.13), calls=%async_computation | async-start | bytes 2097152 | tf_op jit(solution)/shard_map/all_to_all | solution.py:163
  7.5 1.7 %copy-done = bf16[4,64,5120]{2,1,0:T(8,128)(2,1)S(1)} copy-done((bf16[4,64,5120]{2,1,0:T(8,128)(2,1)S(1)}, bf16[4,64,5120]{2,1,0:T(8,128)(2,1)}, u32[]{:S(2)}) %copy-start) | copy-done | bytes 2621464
  9.3 1.5 pick_factors.1
  10.8 0.2 collective-permute-start
  11.0 2.0 %collective-permute-done = bf16[8,320,128]{2,1,0:T(8,128)(2,1)S(1)} collective-permute-done((bf16[8,320,128]{2,1,0:T(8,128)(2,1)S(1)}, bf16[8,320,128]{2,1,0:T(8,128)(2,1)S(1)}, u32[]{:S(2)}, u32[]{:S(2)}) %collective-permute-start) | collective-permute-done | bytes 655392 | tf_op jit(solution)/shard_map/ppermute | solution.py:160
  13.0 1.5 collective-permute-start.2
  14.5 0.6 collective-permute-start.1
  15.1 11.8 %collective-permute-done.2 = bf16[4,320,128]{2,1,0:T(8,128)(2,1)S(1)} collective-permute-done((bf16[4,320,128]{2,1,0:T(8,128)(2,1)S(1)}, bf16[4,320,128]{2,1,0:T(8,128)(2,1)S(1)}, u32[]{:S(2)}, u32[]{:S(2)}) %collective-permute-start.2) | collective-permute-done | bytes 327712 | tf_op jit(solution)/shard_map/ppermute | solution.py:160
  27.0 0.7 slice_add_fusion.2
  27.7 0.0 copy-done.14
  27.7 2.9 %all-to-all-done.k_ref = bf16[16,4,64,128]{3,2,1,0:T(8,128)(2,1)S(1)} async-done(((bf16[16,4,64,128]{3,2,1,0:T(8,128)(2,1)}), bf16[16,4,64,128]{3,2,1,0:T(8,128)(2,1)S(1)}, u32[]{:S(2)}, u32[]{:S(2)}) %all-to-all-start) | async-done | bytes 1048608 | tf_op jit(solution)/shard_map/all_to_all | solution.py:163
  30.6 3.1 %collective-permute-start.3 = (bf16[2,320,128]{2,1,0:T(8,128)(2,1)}, bf16[2,320,128]{2,1,0:T(8,128)(2,1)S(1)}, u32[]{:S(2)}, u32[]{:S(2)}) collective-permute-start(bf16[2,320,128]{2,1,0:T(8,128)(2,1)} %slice_add_fusion.2), channel_id=1, source_target_pairs={{0,4},{1,5},{2,6},{3,7},{4,0},{5,1},{6,2},{7,3},{8,12},{9,13},{10,... | collective-permute-start | bytes 491528 | tf_op jit(solution)/shard_map/ppermute | solution.py:160
  33.7 4.8 %collective-permute-done.3 = bf16[2,320,128]{2,1,0:T(8,128)(2,1)S(1)} collective-permute-done((bf16[2,320,128]{2,1,0:T(8,128)(2,1)}, bf16[2,320,128]{2,1,0:T(8,128)(2,1)S(1)}, u32[]{:S(2)}, u32[]{:S(2)}) %collective-permute-start.3) | collective-permute-done | bytes 163872 | tf_op jit(solution)/shard_map/ppermute | solution.py:160
  38.5 1.1 fusion
  39.7 1.0 collective-permute-start.4
  40.7 8.8 %collective-permute-done.4 = bf16[2,320,128]{2,1,0:T(8,128)(2,1)S(1)} collective-permute-done((bf16[2,320,128]{2,1,0:T(8,128)(2,1)S(1)}, bf16[2,320,128]{2,1,0:T(8,128)(2,1)S(1)}, u32[]{:S(2)}, u32[]{:S(2)}) %collective-permute-start.4) | collective-permute-done | bytes 163872 | tf_op jit(solution)/shard_map/ppermute | solution.py:160
  49.6 0.1 collective-permute-start.5
  49.7 1.5 pad_maximum_fusion
  51.2 2.7 %collective-permute-done.5 = bf16[2,320,128]{2,1,0:T(8,128)(2,1)} collective-permute-done((bf16[2,320,128]{2,1,0:T(8,128)(2,1)S(1)}, bf16[2,320,128]{2,1,0:T(8,128)(2,1)}, u32[]{:S(2)}, u32[]{:S(2)}) %collective-permute-start.5) | collective-permute-done | bytes 163872 | tf_op jit(solution)/shard_map/ppermute | solution.py:160
  53.9 1.7 %pad_maximum_fusion.3 = bf16[4,320,128]{2,1,0:T(8,128)(2,1)} fusion(bf16[2,320,128]{2,1,0:T(8,128)(2,1)} %collective-permute-done.5, bf16[2,320,128]{2,1,0:T(8,128)(2,1)S(1)} %maximum_add_fusion), kind=kLoop, calls=%fused_computation.4 | loop fusion | flops 163840 | bytes 655360 | tf_op jit(solution)/shard_map/concatenate | solution.py:226
  55.6 7.4 %all-to-all-start.1 = ((bf16[16,8,64,128]{3,2,1,0:T(8,128)(2,1)}), bf16[16,8,64,128]{3,2,1,0:T(8,128)(2,1)S(1)}, u32[]{:S(2)}, u32[]{:S(2)}) async-start(bf16[16,8,64,128]{3,2,1,0:T(8,128)(2,1)} %pad_maximum_fusion), calls=%async_computation.1 | async-start | bytes 4194304 | tf_op jit(solution)/shard_map/all_to_all | solution.py:163
  63.0 1.4 collective-permute-start.7
  64.4 1.0 slice_add_fusion.1
  65.4 0.1 collective-permute-start.6
  65.5 23.2 %collective-permute-done.7 = bf16[4,320,128]{2,1,0:T(8,128)(2,1)S(1)} collective-permute-done((bf16[4,320,128]{2,1,0:T(8,128)(2,1)}, bf16[4,320,128]{2,1,0:T(8,128)(2,1)S(1)}, u32[]{:S(2)}, u32[]{:S(2)}) %collective-permute-start.7) | collective-permute-done | bytes 327712 | tf_op jit(solution)/shard_map/ppermute | solution.py:160
  88.8 1.1 pad_maximum_fusion.2
  89.8 6.0 %collective-permute-done.6 = bf16[4,256,128]{2,1,0:T(8,128)(2,1)S(1)} collective-permute-done((bf16[4,256,128]{2,1,0:T(8,128)(2,1)S(1)}, bf16[4,256,128]{2,1,0:T(8,128)(2,1)S(1)}, u32[]{:S(2)}, u32[]{:S(2)}) %collective-permute-start.6) | collective-permute-done | bytes 262176 | tf_op jit(solution)/shard_map/ppermute | solution.py:160
  95.8 0.6 collective-permute-start.10
  96.4 0.9 slice_add_fusion.6
  97.4 0.4 collective-permute-start.8
  97.7 0.4 collective-permute-done.10
  98.1 0.1 pad_maximum_fusion.1.g_ref
  98.3 0.9 low_rank.1
  99.2 5.2 %collective-permute-start.13 = (bf16[64,128]{1,0:T(8,128)(2,1)S(1)}, bf16[64,128]{1,0:T(8,128)(2,1)S(1)}, u32[]{:S(2)}, u32[]{:S(2)}) collective-permute-start(bf16[64,128]{1,0:T(8,128)(2,1)S(1)} %low_rank.1), channel_id=1, source_target_pairs={{0,12},{1,13},{2,14},{3,15},{4,8},{5,9},{6,10},{7,11},{8,4},{9,5},... | collective-permute-start | bytes 49160 | tf_op jit(solution)/shard_map/ppermute | solution.py:160
  104.3 0.4 collective-permute-start.11
  104.7 3.9 %collective-permute-done.8 = bf16[2,256,128]{2,1,0:T(8,128)(2,1)S(1)} collective-permute-done((bf16[2,256,128]{2,1,0:T(8,128)(2,1)S(1)}, bf16[2,256,128]{2,1,0:T(8,128)(2,1)S(1)}, u32[]{:S(2)}, u32[]{:S(2)}) %collective-permute-start.8) | collective-permute-done | bytes 131104 | tf_op jit(solution)/shard_map/ppermute | solution.py:160
  108.6 0.9 slice_add_fusion.8
  109.5 0.1 collective-permute-start.9
  109.6 3.6 %collective-permute-done.12 = bf16[64,128]{1,0:T(8,128)(2,1)S(1)} collective-permute-done((bf16[64,128]{1,0:T(8,128)(2,1)S(1)}, bf16[64,128]{1,0:T(8,128)(2,1)S(1)}, u32[]{:S(2)}, u32[]{:S(2)}) %collective-permute-start.12) | collective-permute-done | bytes 16416 | tf_op jit(solution)/shard_map/ppermute | solution.py:160
  113.2 1.7 %collective-permute-start.14 = (bf16[4,64,128]{2,1,0:T(8,128)(2,1)S(1)}, bf16[4,64,128]{2,1,0:T(8,128)(2,1)S(1)}, u32[]{:S(2)}, u32[]{:S(2)}) collective-permute-start(bf16[4,64,128]{2,1,0:T(8,128)(2,1)S(1)} %pad_maximum_fusion.4.refs_0_), channel_id=1, source_target_pairs={{0,1},{1,0},{2,3},{3,2},{4,5},{5,4},{6,7},{7,6},{8,9},{9,8},{10,11... | collective-permute-start | bytes 196616 | tf_op jit(solution)/shard_map/ppermute | solution.py:160
  114.9 0.2 collective-permute-start.15
  115.0 1.6 collective-permute-start.16
  116.6 0.9 fusion.1
  117.5 1.1 collective-permute-done.15.refs_2_
  118.5 1.6 collective-permute-done.16.refs_3_
  120.1 9.1 %attend.1 = bf16[16,4,64,128]{3,2,1,0:T(8,128)(2,1)S(1)} custom-call(s32[1]{0:T(128)} %bitcast.me_ref, bf16[4,64,128]{2,1,0:T(8,128)(2,1)S(1)} %bitcast.11, bf16[16,8,64,128]{3,2,1,0:T(8,128)(2,1)S(1)} %all-to-all-done.1.q_ref.v_ref, bf16[16,4,64,128]{3,2,1,0:T(8,128)(2,1)S(1)} %all-to-all-done.k_ref, ...), custom_call_target="tpu_custom_call" | custom-call | flops 2147483648 | bytes 4194304 | tf_op jit(solution)/shard_map/attend/pallas_call | solution.py:251
  129.2 28.4 %all_to_all.15 = bf16[16,4,64,128]{3,2,1,0:T(8,128)(2,1)S(1)} all-to-all(bf16[16,4,64,128]{3,2,1,0:T(8,128)(2,1)S(1)} %attend.1), channel_id=1, replica_groups=mesh['grp'=2,'seq'=16] {'seq'}, dimensions={0} | all-to-all | bytes 2097152 | tf_op jit(solution)/shard_map/all_to_all | solution.py:163
  157.7 1.0 copy.10
  (39 shorter events, 0.2 us)
Async XLA Ops:
  0.0 7.5 %copy-start.8 = (s32[64]{0:T(128)S(1)}, s32[64]{0:T(128)}, u32[]{:S(2)}) copy-start(s32[64]{0:T(128)} %row_ref.1) | copy-start | bytes 772
  0.0 7.5 %copy-start.9 = (s32[2]{0:T(128)S(1)}, s32[2]{0:T(128)}, u32[]{:S(2)}) copy-start(s32[2]{0:T(128)} %req_ref.1) | copy-start | bytes 28
  0.0 7.5 %copy-start.1 = (bf16[4,64,4096]{2,1,0:T(8,128)(2,1)S(1)}, bf16[4,64,4096]{2,1,0:T(8,128)(2,1)}, u32[]{:S(2)}) copy-start(bf16[4,64,4096]{2,1,0:T(8,128)(2,1)} %up_ref.1) | copy-start | bytes 6291460
  0.0 30.6 %all-to-all-start = ((bf16[16,4,64,128]{3,2,1,0:T(8,128)(2,1)}), bf16[16,4,64,128]{3,2,1,0:T(8,128)(2,1)S(1)}, u32[]{:S(2)}, u32[]{:S(2)}) async-start(bf16[16,4,64,128]{3,2,1,0:T(8,128)(2,1)} %bitcast.13), calls=%async_computation | async-start | bytes 2097152 | tf_op jit(solution)/shard_map/all_to_all | solution.py:163
  7.5 1.7 %copy-start = (bf16[4,64,5120]{2,1,0:T(8,128)(2,1)S(1)}, bf16[4,64,5120]{2,1,0:T(8,128)(2,1)}, u32[]{:S(2)}) copy-start(bf16[4,64,5120]{2,1,0:T(8,128)(2,1)} %down_ref.1) | copy-start | bytes 7864324
  10.8 16.9 %copy-start.3 = (bf16[2,320,128]{2,1,0:T(8,128)(2,1)}, bf16[2,320,128]{2,1,0:T(8,128)(2,1)S(1)}, u32[]{:S(2)}) copy-start(bf16[2,320,128]{2,1,0:T(8,128)(2,1)S(1)} %get-tuple-element.27) | copy-start | bytes 491524
  10.8 16.9 %copy-start.4 = (bf16[1,256,128]{2,1,0:T(8,128)(2,1)}, bf16[1,256,128]{2,1,0:T(8,128)(2,1)S(1)}, u32[]{:S(2)}) copy-start(bf16[1,256,128]{2,1,0:T(8,128)(2,1)S(1)} %get-tuple-element.34) | copy-start | bytes 196612
  10.8 16.9 %copy-start.6 = (bf16[1,256,128]{2,1,0:T(8,128)(2,1)}, bf16[1,256,128]{2,1,0:T(8,128)(2,1)S(1)}, u32[]{:S(2)}) copy-start(bf16[1,256,128]{2,1,0:T(8,128)(2,1)S(1)} %get-tuple-element.21) | copy-start | bytes 196612
  10.8 38.8 %copy-start.11 = (bf16[2,32,64,128]{3,2,1,0:T(8,128)(2,1)S(1)}, bf16[2,32,64,128]{3,2,1,0:T(8,128)(2,1)}, u32[]{:S(2)}) copy-start(bf16[2,32,64,128]{3,2,1,0:T(8,128)(2,1)} %param.9) | copy-start | bytes 3145732
  10.8 38.8 %copy-start.12 = (bf16[2,32,64,128]{3,2,1,0:T(8,128)(2,1)S(1)}, bf16[2,32,64,128]{3,2,1,0:T(8,128)(2,1)}, u32[]{:S(2)}) copy-start(bf16[2,32,64,128]{3,2,1,0:T(8,128)(2,1)} %param.11) | copy-start | bytes 3145732
  10.8 2.2 %collective-permute-start = (bf16[8,320,128]{2,1,0:T(8,128)(2,1)S(1)}, bf16[8,320,128]{2,1,0:T(8,128)(2,1)S(1)}, u32[]{:S(2)}, u32[]{:S(2)}) collective-permute-start(bf16[8,320,128]{2,1,0:T(8,128)(2,1)S(1)} %get-tuple-element.24), channel_id=1, source_target_pairs={{0,1},{1,0},{2,3},{3,2},{4,5},{5,4},{6,7},{7,6},{8,9},{9,8},{10,11... | collective-permute-start | bytes 1966088 | tf_op jit(solution)/shard_map/ppermute | solution.py:160
  13.0 14.7 %copy-start.13 = (bf16[8,320,128]{2,1,0:T(8,128)(2,1)}, bf16[8,320,128]{2,1,0:T(8,128)(2,1)S(1)}, u32[]{:S(2)}) copy-start(bf16[8,320,128]{2,1,0:T(8,128)(2,1)S(1)} %collective-permute-done) | copy-start | bytes 1966084
  13.0 13.9 %collective-permute-start.2 = (bf16[4,320,128]{2,1,0:T(8,128)(2,1)S(1)}, bf16[4,320,128]{2,1,0:T(8,128)(2,1)S(1)}, u32[]{:S(2)}, u32[]{:S(2)}) collective-permute-start(bf16[4,320,128]{2,1,0:T(8,128)(2,1)S(1)} %slice_add_fusion), channel_id=1, source_target_pairs={{0,2},{1,3},{2,0},{3,1},{4,6},{5,7},{6,4},{7,5},{8,10},{9,11},{10,... | collective-permute-start | bytes 983048 | tf_op jit(solution)/shard_map/ppermute | solution.py:160
  14.5 13.3 %collective-permute-start.1 = (bf16[8,256,128]{2,1,0:T(8,128)(2,1)S(1)}, bf16[8,256,128]{2,1,0:T(8,128)(2,1)}, u32[]{:S(2)}, u32[]{:S(2)}) collective-permute-start(bf16[8,256,128]{2,1,0:T(8,128)(2,1)S(1)} %get-tuple-element.25), channel_id=1, source_target_pairs={{0,1},{1,0},{2,3},{3,2},{4,5},{5,4},{6,7},{7,6},{8,9},{9,8},{10,11... | collective-permute-start | bytes 1572872 | tf_op jit(solution)/shard_map/ppermute | solution.py:160
  27.0 0.8 copy-start.14
  30.6 7.9 %collective-permute-start.3 = (bf16[2,320,128]{2,1,0:T(8,128)(2,1)}, bf16[2,320,128]{2,1,0:T(8,128)(2,1)S(1)}, u32[]{:S(2)}, u32[]{:S(2)}) collective-permute-start(bf16[2,320,128]{2,1,0:T(8,128)(2,1)} %slice_add_fusion.2), channel_id=1, source_target_pairs={{0,4},{1,5},{2,6},{3,7},{4,0},{5,1},{6,2},{7,3},{8,12},{9,13},{10,... | collective-permute-start | bytes 491528 | tf_op jit(solution)/shard_map/ppermute | solution.py:160
  39.7 9.9 %collective-permute-start.4 = (bf16[2,320,128]{2,1,0:T(8,128)(2,1)S(1)}, bf16[2,320,128]{2,1,0:T(8,128)(2,1)S(1)}, u32[]{:S(2)}, u32[]{:S(2)}) collective-permute-start(bf16[2,320,128]{2,1,0:T(8,128)(2,1)S(1)} %fusion), channel_id=1, source_target_pairs={{0,8},{1,9},{2,10},{3,11},{4,12},{5,13},{6,14},{7,15},{8,0},{9,1},... | collective-permute-start | bytes 491528 | tf_op jit(solution)/shard_map/ppermute | solution.py:160
  49.6 4.4 %copy-start.10 = (bf16[2,320,128]{2,1,0:T(8,128)(2,1)}, bf16[2,320,128]{2,1,0:T(8,128)(2,1)S(1)}, u32[]{:S(2)}) copy-start(bf16[2,320,128]{2,1,0:T(8,128)(2,1)S(1)} %maximum_add_fusion) | copy-start | bytes 491524
  49.6 4.3 %collective-permute-start.5 = (bf16[2,320,128]{2,1,0:T(8,128)(2,1)S(1)}, bf16[2,320,128]{2,1,0:T(8,128)(2,1)}, u32[]{:S(2)}, u32[]{:S(2)}) collective-permute-start(bf16[2,320,128]{2,1,0:T(8,128)(2,1)S(1)} %maximum_add_fusion), channel_id=1, source_target_pairs={{0,4},{1,5},{2,6},{3,7},{4,0},{5,1},{6,2},{7,3},{8,12},{9,13},{10,... | collective-permute-start | bytes 491528 | tf_op jit(solution)/shard_map/ppermute | solution.py:160
  55.6 64.5 %all-to-all-start.1 = ((bf16[16,8,64,128]{3,2,1,0:T(8,128)(2,1)}), bf16[16,8,64,128]{3,2,1,0:T(8,128)(2,1)S(1)}, u32[]{:S(2)}, u32[]{:S(2)}) async-start(bf16[16,8,64,128]{3,2,1,0:T(8,128)(2,1)} %pad_maximum_fusion), calls=%async_computation.1 | async-start | bytes 4194304 | tf_op jit(solution)/shard_map/all_to_all | solution.py:163
  63.0 25.8 %collective-permute-start.7 = (bf16[4,320,128]{2,1,0:T(8,128)(2,1)}, bf16[4,320,128]{2,1,0:T(8,128)(2,1)S(1)}, u32[]{:S(2)}, u32[]{:S(2)}) collective-permute-start(bf16[4,320,128]{2,1,0:T(8,128)(2,1)} %pad_maximum_fusion.3), channel_id=1, source_target_pairs={{0,2},{1,3},{2,0},{3,1},{4,6},{5,7},{6,4},{7,5},{8,10},{9,11},{10,... | collective-permute-start | bytes 983048 | tf_op jit(solution)/shard_map/ppermute | solution.py:160
  65.4 32.9 %copy-start.2 = (bf16[2,64,5120]{2,1,0:T(8,128)(2,1)S(1)}, bf16[2,64,5120]{2,1,0:T(8,128)(2,1)}, u32[]{:S(2)}) copy-start(bf16[2,64,5120]{2,1,0:T(8,128)(2,1)} %x_ref.1) | copy-start | bytes 3932164
  65.4 30.4 %collective-permute-start.6 = (bf16[4,256,128]{2,1,0:T(8,128)(2,1)S(1)}, bf16[4,256,128]{2,1,0:T(8,128)(2,1)S(1)}, u32[]{:S(2)}, u32[]{:S(2)}) collective-permute-start(bf16[4,256,128]{2,1,0:T(8,128)(2,1)S(1)} %slice_add_fusion.1), channel_id=1, source_target_pairs={{0,2},{1,3},{2,0},{3,1},{4,6},{5,7},{6,4},{7,5},{8,10},{9,11},{10,... | collective-permute-start | bytes 786440 | tf_op jit(solution)/shard_map/ppermute | solution.py:160
  95.8 2.3 %collective-permute-start.10 = (bf16[8,320,128]{2,1,0:T(8,128)(2,1)S(1)}, bf16[8,320,128]{2,1,0:T(8,128)(2,1)S(1)}, u32[]{:S(2)}, u32[]{:S(2)}) collective-permute-start(bf16[8,320,128]{2,1,0:T(8,128)(2,1)S(1)} %pad_maximum_fusion.2), channel_id=1, source_target_pairs={{0,1},{1,0},{2,3},{3,2},{4,5},{5,4},{6,7},{7,6},{8,9},{9,8},{10,11... | collective-permute-start | bytes 1966088 | tf_op jit(solution)/shard_map/ppermute | solution.py:160
  97.3 11.3 %copy-start.5 = (bf16[1,256,128]{2,1,0:T(8,128)(2,1)S(1)}, bf16[1,256,128]{2,1,0:T(8,128)(2,1)}, u32[]{:S(2)}) copy-start(bf16[1,256,128]{2,1,0:T(8,128)(2,1)} %copy-done.4) | copy-start | bytes 196612
  97.4 11.3 %collective-permute-start.8 = (bf16[2,256,128]{2,1,0:T(8,128)(2,1)S(1)}, bf16[2,256,128]{2,1,0:T(8,128)(2,1)S(1)}, u32[]{:S(2)}, u32[]{:S(2)}) collective-permute-start(bf16[2,256,128]{2,1,0:T(8,128)(2,1)S(1)} %slice_add_fusion.6), channel_id=1, source_target_pairs={{0,4},{1,5},{2,6},{3,7},{4,0},{5,1},{6,2},{7,3},{8,12},{9,13},{10,... | collective-permute-start | bytes 393224 | tf_op jit(solution)/shard_map/ppermute | solution.py:160
  98.3 18.3 %copy-start.7 = (bf16[1,256,128]{2,1,0:T(8,128)(2,1)S(1)}, bf16[1,256,128]{2,1,0:T(8,128)(2,1)}, u32[]{:S(2)}) copy-start(bf16[1,256,128]{2,1,0:T(8,128)(2,1)} %copy-done.6) | copy-start | bytes 196612
  99.2 10.4 %collective-permute-start.13 = (bf16[64,128]{1,0:T(8,128)(2,1)S(1)}, bf16[64,128]{1,0:T(8,128)(2,1)S(1)}, u32[]{:S(2)}, u32[]{:S(2)}) collective-permute-start(bf16[64,128]{1,0:T(8,128)(2,1)S(1)} %low_rank.1), channel_id=1, source_target_pairs={{0,12},{1,13},{2,14},{3,15},{4,8},{5,9},{6,10},{7,11},{8,4},{9,5},... | collective-permute-start | bytes 49160 | tf_op jit(solution)/shard_map/ppermute | solution.py:160
  104.3 8.8 %collective-permute-start.12 = (bf16[64,128]{1,0:T(8,128)(2,1)S(1)}, bf16[64,128]{1,0:T(8,128)(2,1)S(1)}, u32[]{:S(2)}, u32[]{:S(2)}) collective-permute-start(bf16[64,128]{1,0:T(8,128)(2,1)S(1)} %low_rank.1), channel_id=1, source_target_pairs={{0,8},{1,9},{2,10},{3,11},{4,12},{5,13},{6,14},{7,15},{8,0},{9,1},... | collective-permute-start | bytes 49160 | tf_op jit(solution)/shard_map/ppermute | solution.py:160
  104.3 8.8 %collective-permute-start.11 = (bf16[64,128]{1,0:T(8,128)(2,1)S(1)}, bf16[64,128]{1,0:T(8,128)(2,1)S(1)}, u32[]{:S(2)}, u32[]{:S(2)}) collective-permute-start(bf16[64,128]{1,0:T(8,128)(2,1)S(1)} %low_rank.1), channel_id=1, source_target_pairs={{0,4},{1,5},{2,6},{3,7},{4,0},{5,1},{6,2},{7,3},{8,12},{9,13},{10,... | collective-permute-start | bytes 49160 | tf_op jit(solution)/shard_map/ppermute | solution.py:160
  109.5 7.1 %collective-permute-start.9 = (bf16[1,256,128]{2,1,0:T(8,128)(2,1)S(1)}, bf16[1,256,128]{2,1,0:T(8,128)(2,1)S(1)}, u32[]{:S(2)}, u32[]{:S(2)}) collective-permute-start(bf16[1,256,128]{2,1,0:T(8,128)(2,1)S(1)} %slice_add_fusion.8), channel_id=1, source_target_pairs={{0,8},{1,9},{2,10},{3,11},{4,12},{5,13},{6,14},{7,15},{8,0},{9,1},... | collective-permute-start | bytes 196616 | tf_op jit(solution)/shard_map/ppermute | solution.py:160
  113.2 4.3 %collective-permute-start.14 = (bf16[4,64,128]{2,1,0:T(8,128)(2,1)S(1)}, bf16[4,64,128]{2,1,0:T(8,128)(2,1)S(1)}, u32[]{:S(2)}, u32[]{:S(2)}) collective-permute-start(bf16[4,64,128]{2,1,0:T(8,128)(2,1)S(1)} %pad_maximum_fusion.4.refs_0_), channel_id=1, source_target_pairs={{0,1},{1,0},{2,3},{3,2},{4,5},{5,4},{6,7},{7,6},{8,9},{9,8},{10,11... | collective-permute-start | bytes 196616 | tf_op jit(solution)/shard_map/ppermute | solution.py:160
  114.9 3.7 %collective-permute-start.15 = (bf16[4,64,128]{2,1,0:T(8,128)(2,1)S(1)}, bf16[4,64,128]{2,1,0:T(8,128)(2,1)S(1)}, u32[]{:S(2)}, u32[]{:S(2)}) collective-permute-start(bf16[4,64,128]{2,1,0:T(8,128)(2,1)S(1)} %pad_maximum_fusion.4.refs_0_), channel_id=1, source_target_pairs={{0,2},{1,3},{2,0},{3,1},{4,6},{5,7},{6,4},{7,5},{8,10},{9,11},{10,... | collective-permute-start | bytes 196616 | tf_op jit(solution)/shard_map/ppermute | solution.py:160
  115.0 5.1 %collective-permute-start.16 = (bf16[4,64,128]{2,1,0:T(8,128)(2,1)S(1)}, bf16[4,64,128]{2,1,0:T(8,128)(2,1)S(1)}, u32[]{:S(2)}, u32[]{:S(2)}) collective-permute-start(bf16[4,64,128]{2,1,0:T(8,128)(2,1)S(1)} %pad_maximum_fusion.4.refs_0_), channel_id=1, source_target_pairs={{0,3},{1,2},{2,1},{3,0},{4,7},{5,6},{6,5},{7,4},{8,11},{9,10},{10,... | collective-permute-start | bytes 196616 | tf_op jit(solution)/shard_map/ppermute | solution.py:160

commit v9 on v8

--- a/solution.py
+++ b/solution.py
@@ -71,6 +71,10 @@
         for p in range(pairs):
             col = pl.multiple_of((place * pairs + p) * LANES, LANES)
             ups[step][at, p * ranks : (p + 1) * ranks, :] = up[video, :, pl.ds(col, LANES)]
+
+
+def copy_kernel(in_ref, out_ref):
+    out_ref[...] = in_ref[...]
 
 
 def low_rank_kernel(shape, me_ref, x_ref, g_ref, out_ref, down):
@@ -210,19 +214,32 @@
             send_up(0, piece)
         if i == 2:
             piece = after(piece, keys, up_got[0])
+        if i == bits - 2:
+            vals = exchange(after(by_pairs(values), piece))
+            send_up(1, piece)
         down_got.append(swap(piece, 1 << i))
     gathered = sum((r[:2] for r in down_got), down_pieces[-1])
+    for j in range(2, bits - 1):
+        send_up(j, gathered)
     other = swap(gathered, 1 << (bits - 1))
     gathered = gathered + jnp.concatenate([other[1:], other[:1]], axis=0)
+    gathered = after(gathered, vals)
+    asked = pl.pallas_call(
+        copy_kernel,
+        in_specs=[VMEM],
+        out_specs=VMEM,
+        out_shape=jax.ShapeDtypeStruct((devs, pairs, toks, width), jnp.bfloat16),
+        compiler_params=pltpu.CompilerParams(vmem_limit_bytes=24 << 20),
+        cost_estimate=pl.CostEstimate(
+            flops=0, bytes_accessed=4 * pairs * length * width, transcendentals=0
+        ),
+        name="stage_queries",
+    )(after(by_pairs(queries), gathered))
+    asked = exchange(asked)
     for i in reversed(range(bits - 1)):
-        if i == 1:
-            asked = jnp.concatenate([by_pairs(values), by_pairs(queries)], axis=1)
-            asked = exchange(after(asked, gathered))
-            send_up(1, gathered)
         if i == 0:
-            gathered = after(gathered, up_got[1])
-            for j in range(2, bits - 1):
-                send_up(j, gathered)
+            gathered = after(gathered, *up_got)
+            send_up(bits - 1, gathered)
         gathered = jnp.concatenate([gathered, swap(gathered, 1 << i)], axis=0)
 
     low = pl.pallas_call(
@@ -240,19 +257,16 @@
         name="low_rank",
     )(me, normed_token_features, gathered)
     far = jnp.stack([low] + [swap(low, LOW * i) for i in range(1, devs // LOW)])
-    far = after(far, up_got[-1])
-    send_up(bits - 1)
     up_here = halving(up_pieces, up_got, bits).reshape(pairs, ranks, LANES)
     lows = [far] + [swap(far, i) for i in range(1, LOW)]
 
     low_spec = pl.BlockSpec((devs // LOW, toks, videos * ranks), lambda p: (0, 0, 0))
     part_spec = pl.BlockSpec((devs, pl.squeezed, toks, width), lambda p: (0, p, 0, 0))
-    later_spec = pl.BlockSpec((devs, pl.squeezed, toks, width), lambda p: (0, pairs + p, 0, 0))
     mixed = pl.pallas_call(
         functools.partial(attend_kernel, per_video, math.gcd(devs, max(1, 512 // toks))),
         grid=(pairs,),
         in_specs=[SMEM, pl.BlockSpec((pl.squeezed, ranks, LANES), lambda p: (p, 0, 0))]
-        + [later_spec, part_spec, part_spec]
+        + [part_spec] * 3
         + [low_spec] * LOW,
         out_specs=part_spec,
         out_shape=jax.ShapeDtypeStruct((devs, pairs, toks, width), jnp.bfloat16),
@@ -267,7 +281,7 @@
             transcendentals=pairs * length * length,
         ),
         name="attend",
-    )(me, up_here, asked, keys, asked, *lows)
+    )(me, up_here, asked, keys, vals, *lows)
     return exchange(mixed).reshape(videos, heads, toks, width)
 
 

time: 159 us -> 159 us (level)
  waiting for transfers between devices: 72.8 us -> 63.5 us
  starting transfers between devices: 32.9 us -> 41.2 us
    ppermute x17, waiting for transfers between devices: 69.9 us -> 60.6 us  [swap(): return lax.ppermute(tensor, 'seq', [(i, i ^ k) for i in range(devs)])]
    ppermute x17, starting transfers between devices: 18 us -> 22.3 us  [swap(): return lax.ppermute(tensor, 'seq', [(i, i ^ k) for i in range(devs)])]
    all_to_all x2 -> x3, starting transfers between devices: 14.9 us -> 18.9 us  [exchange(): lax.all_to_all(tensor, 'seq', split_axis=0, concat_axis=0, tiled=True)]
  transfers between devices with their start and end apart: 19 -> 20, of which waited for: 13 -> 10; matrix products, arithmetic and copies ran while one was open for 4% -> 6% of each run, Pallas kernels for 2% -> 2%
where the time goes in v9:
time: 159 us; the launch traced here: 158 us
  waiting for transfers between devices  63.5 us (40%)
  starting transfers between devices  41.2 us (26%)
  blocking collectives  29 us (18%)
  Pallas kernels  12.5 us (8%)
  other arithmetic  9.1 us (6%)
  local copies, waits for them, and re-layouts  2.81 us (2%)
    ppermute x17, waiting for transfers between devices, swap(): return lax.ppermute(tensor, 'seq', [(i, i ^ k) for i in range(devs)])  60.6 us
    all_to_all x1, blocking collectives, exchange(): lax.all_to_all(tensor, 'seq', split_axis=0, concat_axis=0, tiled=True)  29 us
    ppermute x17, starting transfers between devices, swap(): return lax.ppermute(tensor, 'seq', [(i, i ^ k) for i in range(devs)])  22.3 us
    all_to_all x3, starting transfers between devices, exchange(): lax.all_to_all(tensor, 'seq', split_axis=0, concat_axis=0, tiled=True)  18.9 us
    pallas_call x1, Pallas kernels, body(): pl.pallas_call(functools.partial(attend_kernel, per_video, math.gcd(devs,...  9.11 us
    add x6, other arithmetic, halving(): return sum((r[h:h + size] for r in received), parts[i])  5.24 us
  transfers between devices with their start and end apart: 20, of which 10 were waited for; matrix products, arithmetic and copies ran while one was open for 6% of the time, Pallas kernels for 2%

profile of v9, /device:TPU:1, one launch (start us, length us, event | category | flops | bytes accessed | tf_op | source)
XLA Modules:
  0.0 158.4 jit_solution(5382484525833474650)
XLA Ops:
  0.0 7.5 %all-to-all-start = ((bf16[16,4,64,128]{3,2,1,0:T(8,128)(2,1)}), bf16[16,4,64,128]{3,2,1,0:T(8,128)(2,1)S(1)}, u32[]{:S(2)}, u32[]{:S(2)}) async-start(bf16[16,4,64,128]{3,2,1,0:T(8,128)(2,1)} %bitcast.14), calls=%async_computation | async-start | bytes 2097152 | tf_op jit(solution)/shard_map/all_to_all | solution.py:167
  7.5 0.0 copy-start
  7.5 1.7 %copy-done = bf16[4,64,5120]{2,1,0:T(8,128)(2,1)S(1)} copy-done((bf16[4,64,5120]{2,1,0:T(8,128)(2,1)S(1)}, bf16[4,64,5120]{2,1,0:T(8,128)(2,1)}, u32[]{:S(2)}) %copy-start) | copy-done | bytes 2621464
  9.3 1.5 pick_factors.1
  10.8 0.2 collective-permute-start
  11.0 2.0 %collective-permute-done = bf16[8,320,128]{2,1,0:T(8,128)(2,1)S(1)} collective-permute-done((bf16[8,320,128]{2,1,0:T(8,128)(2,1)S(1)}, bf16[8,320,128]{2,1,0:T(8,128)(2,1)S(1)}, u32[]{:S(2)}, u32[]{:S(2)}) %collective-permute-start) | collective-permute-done | bytes 655392 | tf_op jit(solution)/shard_map/ppermute | solution.py:164
  13.0 1.6 %collective-permute-start.2 = (bf16[4,320,128]{2,1,0:T(8,128)(2,1)S(1)}, bf16[4,320,128]{2,1,0:T(8,128)(2,1)S(1)}, u32[]{:S(2)}, u32[]{:S(2)}) collective-permute-start(bf16[4,320,128]{2,1,0:T(8,128)(2,1)S(1)} %slice_add_fusion), channel_id=1, source_target_pairs={{0,2},{1,3},{2,0},{3,1},{4,6},{5,7},{6,4},{7,5},{8,10},{9,11},{10,... | collective-permute-start | bytes 983048 | tf_op jit(solution)/shard_map/ppermute | solution.py:164
  14.6 0.7 collective-permute-start.1
  15.3 11.6 %collective-permute-done.2 = bf16[4,320,128]{2,1,0:T(8,128)(2,1)S(1)} collective-permute-done((bf16[4,320,128]{2,1,0:T(8,128)(2,1)S(1)}, bf16[4,320,128]{2,1,0:T(8,128)(2,1)S(1)}, u32[]{:S(2)}, u32[]{:S(2)}) %collective-permute-start.2) | collective-permute-done | bytes 327712 | tf_op jit(solution)/shard_map/ppermute | solution.py:164
  26.9 0.7 slice_add_fusion.4
  27.6 0.0 copy-done.13
  27.7 3.0 %all-to-all-done.k_ref = bf16[16,4,64,128]{3,2,1,0:T(8,128)(2,1)S(1)} async-done(((bf16[16,4,64,128]{3,2,1,0:T(8,128)(2,1)}), bf16[16,4,64,128]{3,2,1,0:T(8,128)(2,1)S(1)}, u32[]{:S(2)}, u32[]{:S(2)}) %all-to-all-start) | async-done | bytes 1048608 | tf_op jit(solution)/shard_map/all_to_all | solution.py:167
  30.6 6.7 %all-to-all-start.1 = ((bf16[16,4,64,128]{3,2,1,0:T(8,128)(2,1)}), bf16[16,4,64,128]{3,2,1,0:T(8,128)(2,1)S(1)}, u32[]{:S(2)}, u32[]{:S(2)}) async-start(bf16[16,4,64,128]{3,2,1,0:T(8,128)(2,1)} %bitcast.2), calls=%async_computation.1 | async-start | bytes 2097152 | tf_op jit(solution)/shard_map/all_to_all | solution.py:167
  37.3 1.5 collective-permute-start.4
  38.8 19.8 %collective-permute-done.4 = bf16[2,320,128]{2,1,0:T(8,128)(2,1)S(1)} collective-permute-done((bf16[2,320,128]{2,1,0:T(8,128)(2,1)}, bf16[2,320,128]{2,1,0:T(8,128)(2,1)S(1)}, u32[]{:S(2)}, u32[]{:S(2)}) %collective-permute-start.4) | collective-permute-done | bytes 163872 | tf_op jit(solution)/shard_map/ppermute | solution.py:164
  58.5 1.1 fusion
  59.6 3.8 %collective-permute-start.6 = (bf16[2,320,128]{2,1,0:T(8,128)(2,1)S(1)}, bf16[2,320,128]{2,1,0:T(8,128)(2,1)S(1)}, u32[]{:S(2)}, u32[]{:S(2)}) collective-permute-start(bf16[2,320,128]{2,1,0:T(8,128)(2,1)S(1)} %fusion), channel_id=1, source_target_pairs={{0,8},{1,9},{2,10},{3,11},{4,12},{5,13},{6,14},{7,15},{8,0},{9,1},... | collective-permute-start | bytes 491528 | tf_op jit(solution)/shard_map/ppermute | solution.py:164
  63.4 7.7 %collective-permute-done.6 = bf16[2,320,128]{2,1,0:T(8,128)(2,1)S(1)} collective-permute-done((bf16[2,320,128]{2,1,0:T(8,128)(2,1)S(1)}, bf16[2,320,128]{2,1,0:T(8,128)(2,1)S(1)}, u32[]{:S(2)}, u32[]{:S(2)}) %collective-permute-start.6) | collective-permute-done | bytes 163872 | tf_op jit(solution)/shard_map/ppermute | solution.py:164
  71.2 0.7 maximum_add_fusion
  71.9 1.7 %slice_add_fusion.1 = bf16[4,256,128]{2,1,0:T(8,128)(2,1)} fusion(bf16[4,256,128]{2,1,0:T(8,128)(2,1)S(1)} %get-tuple-element.28, bf16[8,256,128]{2,1,0:T(8,128)(2,1)} %collective-permute-done.1), kind=kLoop, calls=%fused_computation.4 | loop fusion | flops 131072 | bytes 786432 | tf_op jit(solution)/shard_map/add | solution.py:178
  73.6 1.5 collective-permute-start.3
  75.0 1.0 stage_queries.1
  76.1 4.7 %all-to-all-start.2 = ((bf16[16,4,64,128]{3,2,1,0:T(8,128)(2,1)}), bf16[16,4,64,128]{3,2,1,0:T(8,128)(2,1)S(1)}, u32[]{:S(2)}, u32[]{:S(2)}) async-start(bf16[16,4,64,128]{3,2,1,0:T(8,128)(2,1)} %stage_queries.1), calls=%async_computation.2 | async-start | bytes 2097152 | tf_op jit(solution)/shard_map/all_to_all | solution.py:167
  80.8 0.9 pad_maximum_fusion.2
  81.7 1.5 collective-permute-start.8
  83.2 1.0 slice_add_fusion.6
  84.1 1.2 collective-permute-start.5
  85.4 13.1 %collective-permute-done.8 = bf16[4,320,128]{2,1,0:T(8,128)(2,1)S(1)} collective-permute-done((bf16[4,320,128]{2,1,0:T(8,128)(2,1)S(1)}, bf16[4,320,128]{2,1,0:T(8,128)(2,1)S(1)}, u32[]{:S(2)}, u32[]{:S(2)}) %collective-permute-start.8) | collective-permute-done | bytes 327712 | tf_op jit(solution)/shard_map/ppermute | solution.py:164
  98.5 1.0 pad_maximum_fusion.1
  99.5 1.7 %collective-permute-done.5 = bf16[2,256,128]{2,1,0:T(8,128)(2,1)S(1)} collective-permute-done((bf16[2,256,128]{2,1,0:T(8,128)(2,1)S(1)}, bf16[2,256,128]{2,1,0:T(8,128)(2,1)S(1)}, u32[]{:S(2)}, u32[]{:S(2)}) %collective-permute-start.5) | collective-permute-done | bytes 131104 | tf_op jit(solution)/shard_map/ppermute | solution.py:164
  101.2 0.6 collective-permute-start.10
  101.8 1.7 %collective-permute-done.10 = bf16[8,320,128]{2,1,0:T(8,128)(2,1)S(1)} collective-permute-done((bf16[8,320,128]{2,1,0:T(8,128)(2,1)S(1)}, bf16[8,320,128]{2,1,0:T(8,128)(2,1)S(1)}, u32[]{:S(2)}, u32[]{:S(2)}) %collective-permute-start.10) | collective-permute-done | bytes 655392 | tf_op jit(solution)/shard_map/ppermute | solution.py:164
  103.6 0.1 pad_maximum_fusion.g_ref
  103.7 0.9 low_rank.1
  104.6 3.1 %collective-permute-start.13 = (bf16[64,128]{1,0:T(8,128)(2,1)S(1)}, bf16[64,128]{1,0:T(8,128)(2,1)S(1)}, u32[]{:S(2)}, u32[]{:S(2)}) collective-permute-start(bf16[64,128]{1,0:T(8,128)(2,1)S(1)} %low_rank.1), channel_id=1, source_target_pairs={{0,12},{1,13},{2,14},{3,15},{4,8},{5,9},{6,10},{7,11},{8,4},{9,5},... | collective-permute-start | bytes 49160 | tf_op jit(solution)/shard_map/ppermute | solution.py:164
  107.7 1.1 collective-permute-start.12
  108.8 0.2 collective-permute-start.11
  109.0 0.9 slice_add_fusion.8
  109.9 2.4 %collective-permute-start.9 = (bf16[1,256,128]{2,1,0:T(8,128)(2,1)S(1)}, bf16[1,256,128]{2,1,0:T(8,128)(2,1)S(1)}, u32[]{:S(2)}, u32[]{:S(2)}) collective-permute-start(bf16[1,256,128]{2,1,0:T(8,128)(2,1)S(1)} %slice_add_fusion.8), channel_id=1, source_target_pairs={{0,8},{1,9},{2,10},{3,11},{4,12},{5,13},{6,14},{7,15},{8,0},{9,1},... | collective-permute-start | bytes 196616 | tf_op jit(solution)/shard_map/ppermute | solution.py:164
  112.3 2.6 %collective-permute-start.16 = (bf16[4,64,128]{2,1,0:T(8,128)(2,1)S(1)}, bf16[4,64,128]{2,1,0:T(8,128)(2,1)S(1)}, u32[]{:S(2)}, u32[]{:S(2)}) collective-permute-start(bf16[4,64,128]{2,1,0:T(8,128)(2,1)S(1)} %pad_maximum_fusion.3.refs_0_), channel_id=1, source_target_pairs={{0,3},{1,2},{2,1},{3,0},{4,7},{5,6},{6,5},{7,4},{8,11},{9,10},{10,... | collective-permute-start | bytes 196616 | tf_op jit(solution)/shard_map/ppermute | solution.py:164
  115.0 0.3 collective-permute-start.15
  115.2 0.2 collective-permute-start.14
  115.4 0.9 fusion.1
  116.3 1.5 collective-permute-done.16.refs_3_
  117.8 1.4 collective-permute-done.15.refs_2_
  119.3 9.1 %attend.1 = bf16[16,4,64,128]{3,2,1,0:T(8,128)(2,1)S(1)} custom-call(s32[1]{0:T(128)} %bitcast.me_ref, bf16[4,64,128]{2,1,0:T(8,128)(2,1)S(1)} %bitcast.12, bf16[16,4,64,128]{3,2,1,0:T(8,128)(2,1)S(1)} %all-to-all-done.2.q_ref, bf16[16,4,64,128]{3,2,1,0:T(8,128)(2,1)S(1)} %all-to-all-done.k_ref, bf16[16,4,64,128]{3,2,1,0:T(8,128)(2,1)S(1)} %all-to-all-done.1.v_ref, ...), custom_call_target="tpu_custom_call" | custom-call | flops 2147483648 | bytes 4194304 | tf_op jit(solution)/shard_map/attend/pallas_call | solution.py:265
  128.4 29.0 %all_to_all.20 = bf16[16,4,64,128]{3,2,1,0:T(8,128)(2,1)S(1)} all-to-all(bf16[16,4,64,128]{3,2,1,0:T(8,128)(2,1)S(1)} %attend.1), channel_id=1, replica_groups=mesh['grp'=2,'seq'=16] {'seq'}, dimensions={0} | all-to-all | bytes 2097152 | tf_op jit(solution)/shard_map/all_to_all | solution.py:167
  157.4 1.0 copy.10
  (39 shorter events, 0.1 us)
Async XLA Ops:
  0.0 7.5 %copy-start.10 = (s32[2]{0:T(128)S(1)}, s32[2]{0:T(128)}, u32[]{:S(2)}) copy-start(s32[2]{0:T(128)} %req_ref.1) | copy-start | bytes 28
  0.0 7.5 %copy-start.9 = (s32[64]{0:T(128)S(1)}, s32[64]{0:T(128)}, u32[]{:S(2)}) copy-start(s32[64]{0:T(128)} %row_ref.1) | copy-start | bytes 772
  0.0 7.5 %copy-start.1 = (bf16[4,64,4096]{2,1,0:T(8,128)(2,1)S(1)}, bf16[4,64,4096]{2,1,0:T(8,128)(2,1)}, u32[]{:S(2)}) copy-start(bf16[4,64,4096]{2,1,0:T(8,128)(2,1)} %up_ref.1) | copy-start | bytes 6291460
  0.0 30.6 %all-to-all-start = ((bf16[16,4,64,128]{3,2,1,0:T(8,128)(2,1)}), bf16[16,4,64,128]{3,2,1,0:T(8,128)(2,1)S(1)}, u32[]{:S(2)}, u32[]{:S(2)}) async-start(bf16[16,4,64,128]{3,2,1,0:T(8,128)(2,1)} %bitcast.14), calls=%async_computation | async-start | bytes 2097152 | tf_op jit(solution)/shard_map/all_to_all | solution.py:167
  7.5 1.7 %copy-start = (bf16[4,64,5120]{2,1,0:T(8,128)(2,1)S(1)}, bf16[4,64,5120]{2,1,0:T(8,128)(2,1)}, u32[]{:S(2)}) copy-start(bf16[4,64,5120]{2,1,0:T(8,128)(2,1)} %down_ref.1) | copy-start | bytes 7864324
  10.8 16.9 %copy-start.4 = (bf16[2,320,128]{2,1,0:T(8,128)(2,1)}, bf16[2,320,128]{2,1,0:T(8,128)(2,1)S(1)}, u32[]{:S(2)}) copy-start(bf16[2,320,128]{2,1,0:T(8,128)(2,1)S(1)} %get-tuple-element.33) | copy-start | bytes 491524
  10.8 16.8 %copy-start.5 = (bf16[1,256,128]{2,1,0:T(8,128)(2,1)}, bf16[1,256,128]{2,1,0:T(8,128)(2,1)S(1)}, u32[]{:S(2)}) copy-start(bf16[1,256,128]{2,1,0:T(8,128)(2,1)S(1)} %get-tuple-element.35) | copy-start | bytes 196612
  10.8 16.8 %copy-start.7 = (bf16[1,256,128]{2,1,0:T(8,128)(2,1)}, bf16[1,256,128]{2,1,0:T(8,128)(2,1)S(1)}, u32[]{:S(2)}) copy-start(bf16[1,256,128]{2,1,0:T(8,128)(2,1)S(1)} %get-tuple-element.23) | copy-start | bytes 196612
  10.8 2.2 %collective-permute-start = (bf16[8,320,128]{2,1,0:T(8,128)(2,1)S(1)}, bf16[8,320,128]{2,1,0:T(8,128)(2,1)S(1)}, u32[]{:S(2)}, u32[]{:S(2)}) collective-permute-start(bf16[8,320,128]{2,1,0:T(8,128)(2,1)S(1)} %get-tuple-element.26), channel_id=1, source_target_pairs={{0,1},{1,0},{2,3},{3,2},{4,5},{5,4},{6,7},{7,6},{8,9},{9,8},{10,11... | collective-permute-start | bytes 1966088 | tf_op jit(solution)/shard_map/ppermute | solution.py:164
  13.0 14.7 %copy-start.12 = (bf16[8,320,128]{2,1,0:T(8,128)(2,1)}, bf16[8,320,128]{2,1,0:T(8,128)(2,1)S(1)}, u32[]{:S(2)}) copy-start(bf16[8,320,128]{2,1,0:T(8,128)(2,1)S(1)} %collective-permute-done) | copy-start | bytes 1966084
  13.0 13.9 %collective-permute-start.2 = (bf16[4,320,128]{2,1,0:T(8,128)(2,1)S(1)}, bf16[4,320,128]{2,1,0:T(8,128)(2,1)S(1)}, u32[]{:S(2)}, u32[]{:S(2)}) collective-permute-start(bf16[4,320,128]{2,1,0:T(8,128)(2,1)S(1)} %slice_add_fusion), channel_id=1, source_target_pairs={{0,2},{1,3},{2,0},{3,1},{4,6},{5,7},{6,4},{7,5},{8,10},{9,11},{10,... | collective-permute-start | bytes 983048 | tf_op jit(solution)/shard_map/ppermute | solution.py:164
  14.6 13.1 %collective-permute-start.1 = (bf16[8,256,128]{2,1,0:T(8,128)(2,1)S(1)}, bf16[8,256,128]{2,1,0:T(8,128)(2,1)}, u32[]{:S(2)}, u32[]{:S(2)}) collective-permute-start(bf16[8,256,128]{2,1,0:T(8,128)(2,1)S(1)} %get-tuple-element.27), channel_id=1, source_target_pairs={{0,1},{1,0},{2,3},{3,2},{4,5},{5,4},{6,7},{7,6},{8,9},{9,8},{10,11... | collective-permute-start | bytes 1572872 | tf_op jit(solution)/shard_map/ppermute | solution.py:164
  26.9 0.8 copy-start.13
  30.6 41.2 %all-to-all-start.1 = ((bf16[16,4,64,128]{3,2,1,0:T(8,128)(2,1)}), bf16[16,4,64,128]{3,2,1,0:T(8,128)(2,1)S(1)}, u32[]{:S(2)}, u32[]{:S(2)}) async-start(bf16[16,4,64,128]{3,2,1,0:T(8,128)(2,1)} %bitcast.2), calls=%async_computation.1 | async-start | bytes 2097152 | tf_op jit(solution)/shard_map/all_to_all | solution.py:167
  37.3 37.7 %copy-start.3 = (bf16[2,32,64,128]{3,2,1,0:T(8,128)(2,1)S(1)}, bf16[2,32,64,128]{3,2,1,0:T(8,128)(2,1)}, u32[]{:S(2)}) copy-start(bf16[2,32,64,128]{3,2,1,0:T(8,128)(2,1)} %param.9) | copy-start | bytes 3145732
  37.3 21.2 %collective-permute-start.4 = (bf16[2,320,128]{2,1,0:T(8,128)(2,1)}, bf16[2,320,128]{2,1,0:T(8,128)(2,1)S(1)}, u32[]{:S(2)}, u32[]{:S(2)}) collective-permute-start(bf16[2,320,128]{2,1,0:T(8,128)(2,1)} %slice_add_fusion.4), channel_id=1, source_target_pairs={{0,4},{1,5},{2,6},{3,7},{4,0},{5,1},{6,2},{7,3},{8,12},{9,13},{10,... | collective-permute-start | bytes 491528 | tf_op jit(solution)/shard_map/ppermute | solution.py:164
  59.6 11.5 %collective-permute-start.6 = (bf16[2,320,128]{2,1,0:T(8,128)(2,1)S(1)}, bf16[2,320,128]{2,1,0:T(8,128)(2,1)S(1)}, u32[]{:S(2)}, u32[]{:S(2)}) collective-permute-start(bf16[2,320,128]{2,1,0:T(8,128)(2,1)S(1)} %fusion), channel_id=1, source_target_pairs={{0,8},{1,9},{2,10},{3,11},{4,12},{5,13},{6,14},{7,15},{8,0},{9,1},... | collective-permute-start | bytes 491528 | tf_op jit(solution)/shard_map/ppermute | solution.py:164
  71.9 8.9 %collective-permute-start.7 = (bf16[2,320,128]{2,1,0:T(8,128)(2,1)}, bf16[2,320,128]{2,1,0:T(8,128)(2,1)}, u32[]{:S(2)}, u32[]{:S(2)}) collective-permute-start(bf16[2,320,128]{2,1,0:T(8,128)(2,1)} %maximum_add_fusion), channel_id=1, source_target_pairs={{0,4},{1,5},{2,6},{3,7},{4,0},{5,1},{6,2},{7,3},{8,12},{9,13},{10,... | collective-permute-start | bytes 491528 | tf_op jit(solution)/shard_map/ppermute | solution.py:164
  73.6 9.6 %collective-permute-start.3 = (bf16[4,256,128]{2,1,0:T(8,128)(2,1)}, bf16[4,256,128]{2,1,0:T(8,128)(2,1)}, u32[]{:S(2)}, u32[]{:S(2)}) collective-permute-start(bf16[4,256,128]{2,1,0:T(8,128)(2,1)} %slice_add_fusion.1), channel_id=1, source_target_pairs={{0,2},{1,3},{2,0},{3,1},{4,6},{5,7},{6,4},{7,5},{8,10},{9,11},{10,... | collective-permute-start | bytes 786440 | tf_op jit(solution)/shard_map/ppermute | solution.py:164
  76.1 4.7 %copy-start.11 = (bf16[2,320,128]{2,1,0:T(8,128)(2,1)S(1)}, bf16[2,320,128]{2,1,0:T(8,128)(2,1)}, u32[]{:S(2)}) copy-start(bf16[2,320,128]{2,1,0:T(8,128)(2,1)} %maximum_add_fusion) | copy-start | bytes 491524
  76.1 43.2 %all-to-all-start.2 = ((bf16[16,4,64,128]{3,2,1,0:T(8,128)(2,1)}), bf16[16,4,64,128]{3,2,1,0:T(8,128)(2,1)S(1)}, u32[]{:S(2)}, u32[]{:S(2)}) async-start(bf16[16,4,64,128]{3,2,1,0:T(8,128)(2,1)} %stage_queries.1), calls=%async_computation.2 | async-start | bytes 2097152 | tf_op jit(solution)/shard_map/all_to_all | solution.py:167
  81.7 16.8 %collective-permute-start.8 = (bf16[4,320,128]{2,1,0:T(8,128)(2,1)S(1)}, bf16[4,320,128]{2,1,0:T(8,128)(2,1)S(1)}, u32[]{:S(2)}, u32[]{:S(2)}) collective-permute-start(bf16[4,320,128]{2,1,0:T(8,128)(2,1)S(1)} %pad_maximum_fusion.2), channel_id=1, source_target_pairs={{0,2},{1,3},{2,0},{3,1},{4,6},{5,7},{6,4},{7,5},{8,10},{9,11},{10,... | collective-permute-start | bytes 983048 | tf_op jit(solution)/shard_map/ppermute | solution.py:164
  84.1 17.1 %collective-permute-start.5 = (bf16[2,256,128]{2,1,0:T(8,128)(2,1)S(1)}, bf16[2,256,128]{2,1,0:T(8,128)(2,1)S(1)}, u32[]{:S(2)}, u32[]{:S(2)}) collective-permute-start(bf16[2,256,128]{2,1,0:T(8,128)(2,1)S(1)} %slice_add_fusion.6), channel_id=1, source_target_pairs={{0,4},{1,5},{2,6},{3,7},{4,0},{5,1},{6,2},{7,3},{8,12},{9,13},{10,... | collective-permute-start | bytes 393224 | tf_op jit(solution)/shard_map/ppermute | solution.py:164
  99.5 4.2 %copy-start.2 = (bf16[2,64,5120]{2,1,0:T(8,128)(2,1)S(1)}, bf16[2,64,5120]{2,1,0:T(8,128)(2,1)}, u32[]{:S(2)}) copy-start(bf16[2,64,5120]{2,1,0:T(8,128)(2,1)} %x_ref.1) | copy-start | bytes 3932164
  101.2 2.3 %collective-permute-start.10 = (bf16[8,320,128]{2,1,0:T(8,128)(2,1)S(1)}, bf16[8,320,128]{2,1,0:T(8,128)(2,1)S(1)}, u32[]{:S(2)}, u32[]{:S(2)}) collective-permute-start(bf16[8,320,128]{2,1,0:T(8,128)(2,1)S(1)} %pad_maximum_fusion.1), channel_id=1, source_target_pairs={{0,1},{1,0},{2,3},{3,2},{4,5},{5,4},{6,7},{7,6},{8,9},{9,8},{10,11... | collective-permute-start | bytes 1966088 | tf_op jit(solution)/shard_map/ppermute | solution.py:164
  103.7 5.3 %copy-start.6 = (bf16[1,256,128]{2,1,0:T(8,128)(2,1)S(1)}, bf16[1,256,128]{2,1,0:T(8,128)(2,1)}, u32[]{:S(2)}) copy-start(bf16[1,256,128]{2,1,0:T(8,128)(2,1)} %copy-done.5) | copy-start | bytes 196612
  103.7 11.7 %copy-start.8 = (bf16[1,256,128]{2,1,0:T(8,128)(2,1)S(1)}, bf16[1,256,128]{2,1,0:T(8,128)(2,1)}, u32[]{:S(2)}) copy-start(bf16[1,256,128]{2,1,0:T(8,128)(2,1)} %copy-done.7) | copy-start | bytes 196612
  104.6 7.7 %collective-permute-start.13 = (bf16[64,128]{1,0:T(8,128)(2,1)S(1)}, bf16[64,128]{1,0:T(8,128)(2,1)S(1)}, u32[]{:S(2)}, u32[]{:S(2)}) collective-permute-start(bf16[64,128]{1,0:T(8,128)(2,1)S(1)} %low_rank.1), channel_id=1, source_target_pairs={{0,12},{1,13},{2,14},{3,15},{4,8},{5,9},{6,10},{7,11},{8,4},{9,5},... | collective-permute-start | bytes 49160 | tf_op jit(solution)/shard_map/ppermute | solution.py:164
  107.7 4.6 %collective-permute-start.12 = (bf16[64,128]{1,0:T(8,128)(2,1)S(1)}, bf16[64,128]{1,0:T(8,128)(2,1)S(1)}, u32[]{:S(2)}, u32[]{:S(2)}) collective-permute-start(bf16[64,128]{1,0:T(8,128)(2,1)S(1)} %low_rank.1), channel_id=1, source_target_pairs={{0,8},{1,9},{2,10},{3,11},{4,12},{5,13},{6,14},{7,15},{8,0},{9,1},... | collective-permute-start | bytes 49160 | tf_op jit(solution)/shard_map/ppermute | solution.py:164
  108.8 3.5 %collective-permute-start.11 = (bf16[64,128]{1,0:T(8,128)(2,1)S(1)}, bf16[64,128]{1,0:T(8,128)(2,1)S(1)}, u32[]{:S(2)}, u32[]{:S(2)}) collective-permute-start(bf16[64,128]{1,0:T(8,128)(2,1)S(1)} %low_rank.1), channel_id=1, source_target_pairs={{0,4},{1,5},{2,6},{3,7},{4,0},{5,1},{6,2},{7,3},{8,12},{9,13},{10,... | collective-permute-start | bytes 49160 | tf_op jit(solution)/shard_map/ppermute | solution.py:164
  109.9 5.6 %collective-permute-start.9 = (bf16[1,256,128]{2,1,0:T(8,128)(2,1)S(1)}, bf16[1,256,128]{2,1,0:T(8,128)(2,1)S(1)}, u32[]{:S(2)}, u32[]{:S(2)}) collective-permute-start(bf16[1,256,128]{2,1,0:T(8,128)(2,1)S(1)} %slice_add_fusion.8), channel_id=1, source_target_pairs={{0,8},{1,9},{2,10},{3,11},{4,12},{5,13},{6,14},{7,15},{8,0},{9,1},... | collective-permute-start | bytes 196616 | tf_op jit(solution)/shard_map/ppermute | solution.py:164
  112.3 5.5 %collective-permute-start.16 = (bf16[4,64,128]{2,1,0:T(8,128)(2,1)S(1)}, bf16[4,64,128]{2,1,0:T(8,128)(2,1)S(1)}, u32[]{:S(2)}, u32[]{:S(2)}) collective-permute-start(bf16[4,64,128]{2,1,0:T(8,128)(2,1)S(1)} %pad_maximum_fusion.3.refs_0_), channel_id=1, source_target_pairs={{0,3},{1,2},{2,1},{3,0},{4,7},{5,6},{6,5},{7,4},{8,11},{9,10},{10,... | collective-permute-start | bytes 196616 | tf_op jit(solution)/shard_map/ppermute | solution.py:164
  115.0 4.3 %collective-permute-start.15 = (bf16[4,64,128]{2,1,0:T(8,128)(2,1)S(1)}, bf16[4,64,128]{2,1,0:T(8,128)(2,1)S(1)}, u32[]{:S(2)}, u32[]{:S(2)}) collective-permute-start(bf16[4,64,128]{2,1,0:T(8,128)(2,1)S(1)} %pad_maximum_fusion.3.refs_0_), channel_id=1, source_target_pairs={{0,2},{1,3},{2,0},{3,1},{4,6},{5,7},{6,4},{7,5},{8,10},{9,11},{10,... | collective-permute-start | bytes 196616 | tf_op jit(solution)/shard_map/ppermute | solution.py:164
  115.2 4.0 %collective-permute-start.14 = (bf16[4,64,128]{2,1,0:T(8,128)(2,1)S(1)}, bf16[4,64,128]{2,1,0:T(8,128)(2,1)S(1)}, u32[]{:S(2)}, u32[]{:S(2)}) collective-permute-start(bf16[4,64,128]{2,1,0:T(8,128)(2,1)S(1)} %pad_maximum_fusion.3.refs_0_), channel_id=1, source_target_pairs={{0,1},{1,0},{2,3},{3,2},{4,5},{5,4},{6,7},{7,6},{8,9},{9,8},{10,11... | collective-permute-start | bytes 196616 | tf_op jit(solution)/shard_map/ppermute | solution.py:164

commit v10 on v7

--- a/solution.py
+++ b/solution.py
@@ -30,8 +30,8 @@
 
 def pick_kernel(shape, me_ref, row_ref, req_ref, down_ref, up_ref, *refs):
     devs, bits, per_video, pairs, col_split, rows, tiles = shape
-    downs, ups = refs[: bits + 1], refs[bits + 1 : 2 * bits + 2]
-    down, up, sems = refs[2 * bits + 2 :]
+    downs, ups = refs[: bits - 1], refs[bits - 1 : 2 * bits - 2]
+    down, up, sems = refs[2 * bits - 2 :]
     slots, ranks, _ = down_ref.shape
     videos = down.shape[0]
     me = me_ref[0]
@@ -57,8 +57,8 @@
             up[s] = jnp.zeros(up.shape[1:], up.dtype)
 
     for j in range(devs):
-        step = bits - j.bit_length()
-        at = j - (1 << (j.bit_length() - 1)) if j else 0
+        step = min(bits - j.bit_length(), bits - 2)
+        at = j - (1 << (j.bit_length() - 1)) if j >= LOW else j
         dev = me ^ reversed_bits(j, bits)
         video = dev // per_video
         place = dev % per_video
@@ -71,6 +71,10 @@
         for p in range(pairs):
             col = pl.multiple_of((place * pairs + p) * LANES, LANES)
             ups[step][at, p * ranks : (p + 1) * ranks, :] = up[video, :, pl.ds(col, LANES)]
+
+
+def copy_kernel(in_ref, out_ref):
+    out_ref[...] = in_ref[...]
 
 
 def low_rank_kernel(shape, me_ref, x_ref, g_ref, out_ref, down):
@@ -168,21 +172,27 @@
     def after(array, *others):
         return lax.optimization_barrier((array, others))[0]
 
+    quarter = devs // LOW
+    others = (2 * quarter, quarter, 3 * quarter)
+
     def halving(parts, received, i):
-        h = devs >> (i + 1) if i < bits else 0
-        size = max(h, 1)
-        return sum((r[h : h + size] for r in received), parts[i])
+        size = parts[i].shape[0]
+        start = size if i < bits - 2 else 0
+        return sum((r[start : start + size] for r in received), parts[i])
+
+    def to_others(shards):
+        return [swap(shards[j + 1 : j + 2], k) for j, k in enumerate(others)]
 
     keys = exchange(by_pairs(projected_keys))
 
-    steps = [devs >> (i + 1) for i in range(bits)] + [1]
+    steps = [devs >> (i + 1) for i in range(bits - 2)] + [LOW]
     piece_shapes = [(h, tiles * rows, LANES) for h in steps] + [
         (h, pairs * ranks, LANES) for h in steps
     ]
     pieces = pl.pallas_call(
         functools.partial(pick_kernel, shape),
         in_specs=[SMEM, SMEM, SMEM, ANY, ANY],
-        out_specs=[VMEM] * (2 * bits + 2),
+        out_specs=[VMEM] * (2 * bits - 2),
         out_shape=[jax.ShapeDtypeStruct(s, jnp.bfloat16) for s in piece_shapes],
         scratch_shapes=[
             pltpu.VMEM((videos, ranks, model_width), jnp.bfloat16),
@@ -197,33 +207,41 @@
         ),
         name="pick_factors",
     )(me, adapter_store_row, requests, adapter_down_factors, adapter_up_factors)
-    down_pieces, up_pieces = pieces[: bits + 1], pieces[bits + 1 :]
+    down_pieces, up_pieces = pieces[: bits - 1], pieces[bits - 1 :]
+
+    def stage(tensor):
+        return pl.pallas_call(
+            copy_kernel,
+            in_specs=[VMEM],
+            out_specs=VMEM,
+            out_shape=jax.ShapeDtypeStruct((devs, pairs, toks, width), jnp.bfloat16),
+            compiler_params=pltpu.CompilerParams(vmem_limit_bytes=24 << 20),
+            cost_estimate=pl.CostEstimate(
+                flops=0, bytes_accessed=4 * pairs * length * width, transcendentals=0
+            ),
+            name="stage",
+        )(tensor)
 
     down_got, up_got = [], []
-
-    def send_up(i, *others):
-        up_got.append(swap(after(halving(up_pieces, up_got, i), *others), 1 << i))
-
-    for i in range(bits):
+    for i in range(bits - 2):
         piece = halving(down_pieces, down_got, i)
-        if i == 2:
-            piece = after(piece, keys)
-        if i >= 2:
-            piece = after(piece, up_got[i - 2])
-        if 0 < i < bits - 1:
-            send_up(i - 1, piece)
+        if i > 0:
+            up_got.append(swap(after(halving(up_pieces, up_got, i - 1), piece), 1 << (i - 1)))
         down_got.append(swap(piece, 1 << i))
-    gathered = halving(down_pieces, down_got, bits)
-    for i in reversed(range(bits)):
-        if i >= bits - 3:
-            gathered = after(gathered, up_got[2 * bits - 4 - i])
-        if i >= bits - 2:
-            send_up(2 * bits - 3 - i, gathered)
-        if i == 1:
-            up_here = halving(up_pieces, up_got, bits).reshape(pairs, ranks, LANES)
-            asked = jnp.concatenate([by_pairs(values), by_pairs(queries)], axis=1)
-            asked = exchange(after(asked, gathered, up_here))
+    shards = halving(down_pieces, down_got, bits - 2)
+    shards = after(shards, keys, *up_got)
+    vals = exchange(stage(after(by_pairs(values), shards)))
+    up_got.append(swap(after(halving(up_pieces, up_got, bits - 3), shards), 1 << (bits - 3)))
+    shard = shards[:1] + sum(to_others(shards))
+    shard = after(shard, *up_got)
+    up_shards = after(halving(up_pieces, up_got, bits - 2), shard)
+    up_here = (up_shards[:1] + sum(to_others(up_shards))).reshape(pairs, ranks, LANES)
+    gathered = jnp.concatenate([shard] + [swap(shard, k) for k in others], axis=0)
+    gathered = after(gathered, vals)
+    asked = exchange(after(by_pairs(queries), vals))
+    for i in reversed(range(bits - 2)):
         gathered = jnp.concatenate([gathered, swap(gathered, 1 << i)], axis=0)
+    gathered = after(gathered, up_here)
 
     low = pl.pallas_call(
         functools.partial(low_rank_kernel, shape),
@@ -244,12 +262,11 @@
 
     low_spec = pl.BlockSpec((devs // LOW, toks, videos * ranks), lambda p: (0, 0, 0))
     part_spec = pl.BlockSpec((devs, pl.squeezed, toks, width), lambda p: (0, p, 0, 0))
-    later_spec = pl.BlockSpec((devs, pl.squeezed, toks, width), lambda p: (0, pairs + p, 0, 0))
     mixed = pl.pallas_call(
         functools.partial(attend_kernel, per_video, math.gcd(devs, max(1, 512 // toks))),
         grid=(pairs,),
         in_specs=[SMEM, pl.BlockSpec((pl.squeezed, ranks, LANES), lambda p: (p, 0, 0))]
-        + [later_spec, part_spec, part_spec]
+        + [part_spec] * 3
         + [low_spec] * LOW,
         out_specs=part_spec,
         out_shape=jax.ShapeDtypeStruct((devs, pairs, toks, width), jnp.bfloat16),
@@ -264,7 +281,7 @@
             transcendentals=pairs * length * length,
         ),
         name="attend",
-    )(me, up_here, asked, keys, asked, *lows)
+    )(me, up_here, asked, keys, vals, *lows)
     return exchange(mixed).reshape(videos, heads, toks, width)
 
 

time: 168 us -> 180 us (1.071)
  starting transfers between devices: 31.1 us -> 48.8 us
  other arithmetic: 10.6 us -> 4.04 us
  local copies, waits for them, and re-layouts: 2.75 us -> 4.63 us
    ppermute x18 -> x21, waiting for transfers between devices: 78.3 us -> 60.4 us  [swap(): return lax.ppermute(tensor, 'seq', [(i, i ^ k) for i in range(devs)])]
    all_to_all x2 -> x3, waiting for transfers between devices: 3.1 us -> 19.7 us  [exchange(): lax.all_to_all(tensor, 'seq', split_axis=0, concat_axis=0, tiled=True)]
    all_to_all x2 -> x3, starting transfers between devices: 13.1 us -> 24.7 us  [exchange(): lax.all_to_all(tensor, 'seq', split_axis=0, concat_axis=0, tiled=True)]
    ppermute x18 -> x21, starting transfers between devices: 18 us -> 24.1 us  [swap(): return lax.ppermute(tensor, 'seq', [(i, i ^ k) for i in range(devs)])]
    concatenate x4 -> x2, other arithmetic: 2.9 us -> 0.19 us  [body(): gathered = jnp.concatenate([gathered, swap(gathered, 1 << i)], axis=0)]
    add x8 -> x6, other arithmetic: 6.17 us -> 3.8 us  [the longest x4 2.76 us: halving(): return sum((r[start:start + size] for r in received), parts[i])]
    unnamed x27 -> x19, local copies, waits for them, and re-layouts: 2.75 us -> 3.9 us
  transfers between devices with their start and end apart: 20 -> 24, of which waited for: 15 -> 14; matrix products, arithmetic and copies ran while one was open for 5% -> 3% of each run, Pallas kernels for 2% -> 1%
where the time goes in v10:
time: 180 us; the launch traced here: 179 us
  waiting for transfers between devices  80.1 us (44%)
  starting transfers between devices  48.8 us (27%)
  blocking collectives  29 us (16%)
  Pallas kernels  12.5 us (7%)
  local copies, waits for them, and re-layouts  4.63 us (3%)
  other arithmetic  4.04 us (2%)
    ppermute x21, waiting for transfers between devices, swap(): return lax.ppermute(tensor, 'seq', [(i, i ^ k) for i in range(devs)])  60.4 us
    all_to_all x1, blocking collectives, exchange(): lax.all_to_all(tensor, 'seq', split_axis=0, concat_axis=0, tiled=True)  29 us
    all_to_all x3, starting transfers between devices, exchange(): lax.all_to_all(tensor, 'seq', split_axis=0, concat_axis=0, tiled=True)  24.7 us
    ppermute x21, starting transfers between devices, swap(): return lax.ppermute(tensor, 'seq', [(i, i ^ k) for i in range(devs)])  24.1 us
    all_to_all x3, waiting for transfers between devices, exchange(): lax.all_to_all(tensor, 'seq', split_axis=0, concat_axis=0, tiled=True)  19.7 us
    pallas_call x1, Pallas kernels, body(): pl.pallas_call(functools.partial(attend_kernel, per_video, math.gcd(devs,...  9.11 us
    unnamed x19, local copies, waits for them, and re-layouts  3.9 us
  transfers between devices with their start and end apart: 24, of which 14 were waited for; matrix products, arithmetic and copies ran while one was open for 3% of the time, Pallas kernels for 1%

profile of v10, /device:TPU:1, one launch (start us, length us, event | category | flops | bytes accessed | tf_op | source)
XLA Modules:
  0.0 179.3 jit_solution(2479765450931992015)
XLA Ops:
  0.0 7.5 %all-to-all-start = ((bf16[16,4,64,128]{3,2,1,0:T(8,128)(2,1)}), bf16[16,4,64,128]{3,2,1,0:T(8,128)(2,1)S(1)}, u32[]{:S(2)}, u32[]{:S(2)}) async-start(bf16[16,4,64,128]{3,2,1,0:T(8,128)(2,1)} %bitcast.14), calls=%async_computation | async-start | bytes 2097152 | tf_op jit(solution)/shard_map/all_to_all | solution.py:167
  7.5 1.7 copy-done
  9.3 1.5 pick_factors.1
  10.8 0.2 collective-permute-start
  11.0 2.0 %collective-permute-done = bf16[8,320,128]{2,1,0:T(8,128)(2,1)S(1)} collective-permute-done((bf16[8,320,128]{2,1,0:T(8,128)(2,1)S(1)}, bf16[8,320,128]{2,1,0:T(8,128)(2,1)S(1)}, u32[]{:S(2)}, u32[]{:S(2)}) %collective-permute-start) | collective-permute-done | bytes 655392 | tf_op jit(solution)/shard_map/ppermute | solution.py:164
  13.0 1.5 collective-permute-start.2
  14.5 0.6 collective-permute-start.1
  15.1 11.8 %collective-permute-done.2 = bf16[4,320,128]{2,1,0:T(8,128)(2,1)S(1)} collective-permute-done((bf16[4,320,128]{2,1,0:T(8,128)(2,1)S(1)}, bf16[4,320,128]{2,1,0:T(8,128)(2,1)S(1)}, u32[]{:S(2)}, u32[]{:S(2)}) %collective-permute-start.2) | collective-permute-done | bytes 327712 | tf_op jit(solution)/shard_map/ppermute | solution.py:164
  27.0 3.6 %all-to-all-done.k_ref = bf16[16,4,64,128]{3,2,1,0:T(8,128)(2,1)S(1)} async-done(((bf16[16,4,64,128]{3,2,1,0:T(8,128)(2,1)}), bf16[16,4,64,128]{3,2,1,0:T(8,128)(2,1)S(1)}, u32[]{:S(2)}, u32[]{:S(2)}) %all-to-all-start) | async-done | bytes 1048608 | tf_op jit(solution)/shard_map/all_to_all | solution.py:167
  30.6 1.0 stage.1
  31.7 6.7 %all-to-all-start.1 = ((bf16[16,4,64,128]{3,2,1,0:T(8,128)(2,1)}), bf16[16,4,64,128]{3,2,1,0:T(8,128)(2,1)S(1)}, u32[]{:S(2)}, u32[]{:S(2)}) async-start(bf16[16,4,64,128]{3,2,1,0:T(8,128)(2,1)} %stage.1), calls=%async_computation.1 | async-start | bytes 2097152 | tf_op jit(solution)/shard_map/all_to_all | solution.py:167
  38.4 0.7 fusion.2
  39.1 1.4 collective-permute-start.5
  40.5 2.1 %collective-permute-start.6 = (bf16[1,320,128]{2,1,0:T(8,128)(2,1)}, bf16[1,320,128]{2,1,0:T(8,128)(2,1)}, u32[]{:S(2)}, u32[]{:S(2)}) collective-permute-start(bf16[1,320,128]{2,1,0:T(8,128)(2,1)} %get-tuple-element.36), channel_id=1, source_target_pairs={{0,12},{1,13},{2,14},{3,15},{4,8},{5,9},{6,10},{7,11},{8,4},{9,5},... | collective-permute-start | bytes 245768 | tf_op jit(solution)/shard_map/ppermute | solution.py:164
  42.6 1.7 slice_add_fusion.2
  44.2 1.2 collective-permute-start.3
  45.4 16.1 %all-to-all-done.1.v_ref = bf16[16,4,64,128]{3,2,1,0:T(8,128)(2,1)S(1)} async-done(((bf16[16,4,64,128]{3,2,1,0:T(8,128)(2,1)}), bf16[16,4,64,128]{3,2,1,0:T(8,128)(2,1)S(1)}, u32[]{:S(2)}, u32[]{:S(2)}) %all-to-all-start.1) | async-done | bytes 1048608 | tf_op jit(solution)/shard_map/all_to_all | solution.py:167
  61.5 10.6 %all-to-all-start.2 = ((bf16[16,4,64,128]{3,2,1,0:T(8,128)(2,1)}), bf16[16,4,64,128]{3,2,1,0:T(8,128)(2,1)S(1)}, u32[]{:S(2)}, u32[]{:S(2)}) async-start(bf16[16,4,64,128]{3,2,1,0:T(8,128)(2,1)} %bitcast.15), calls=%async_computation.2 | async-start | bytes 2097152 | tf_op jit(solution)/shard_map/all_to_all | solution.py:167
  72.1 1.0 add_add_fusion
  73.1 3.3 %collective-permute-start.12 = (bf16[1,320,128]{2,1,0:T(8,128)(2,1)S(1)}, bf16[1,320,128]{2,1,0:T(8,128)(2,1)S(1)}, u32[]{:S(2)}, u32[]{:S(2)}) collective-permute-start(bf16[1,320,128]{2,1,0:T(8,128)(2,1)S(1)} %add_add_fusion), channel_id=1, source_target_pairs={{0,12},{1,13},{2,14},{3,15},{4,8},{5,9},{6,10},{7,11},{8,4},{9,5},... | collective-permute-start | bytes 245768 | tf_op jit(solution)/shard_map/ppermute | solution.py:164
  76.4 0.4 collective-permute-start.10
  76.8 18.2 %collective-permute-done.12 = bf16[1,320,128]{2,1,0:T(8,128)(2,1)S(1)} collective-permute-done((bf16[1,320,128]{2,1,0:T(8,128)(2,1)S(1)}, bf16[1,320,128]{2,1,0:T(8,128)(2,1)S(1)}, u32[]{:S(2)}, u32[]{:S(2)}) %collective-permute-start.12) | collective-permute-done | bytes 81952 | tf_op jit(solution)/shard_map/ppermute | solution.py:164
  95.0 9.9 %collective-permute-done.10 = bf16[1,320,128]{2,1,0:T(8,128)(2,1)S(1)} collective-permute-done((bf16[1,320,128]{2,1,0:T(8,128)(2,1)S(1)}, bf16[1,320,128]{2,1,0:T(8,128)(2,1)S(1)}, u32[]{:S(2)}, u32[]{:S(2)}) %collective-permute-start.10) | collective-permute-done | bytes 81952 | tf_op jit(solution)/shard_map/ppermute | solution.py:164
  104.9 1.3 collective-permute-start.13
  106.2 7.1 %collective-permute-done.13 = bf16[4,320,128]{2,1,0:T(8,128)(2,1)S(1)} collective-permute-done((bf16[4,320,128]{2,1,0:T(8,128)(2,1)S(1)}, bf16[4,320,128]{2,1,0:T(8,128)(2,1)S(1)}, u32[]{:S(2)}, u32[]{:S(2)}) %collective-permute-start.13) | collective-permute-done | bytes 327712 | tf_op jit(solution)/shard_map/ppermute | solution.py:164
  113.4 1.8 %collective-permute-start.14 = (bf16[8,320,128]{2,1,0:T(8,128)(2,1)S(1)}, bf16[8,320,128]{2,1,0:T(8,128)(2,1)S(1)}, u32[]{:S(2)}, u32[]{:S(2)}) collective-permute-start(bf16[8,320,128]{2,1,0:T(8,128)(2,1)S(1)} %pad_maximum_fusion.1), channel_id=1, source_target_pairs={{0,1},{1,0},{2,3},{3,2},{4,5},{5,4},{6,7},{7,6},{8,9},{9,8},{10,11... | collective-permute-start | bytes 1966088 | tf_op jit(solution)/shard_map/ppermute | solution.py:164
  115.2 1.0 fusion.1
  116.2 0.1 collective-permute-start.8
  116.3 1.2 collective-permute-start.9
  117.6 1.4 collective-permute-start.7
  119.0 1.1 collective-permute-done.8
  120.0 1.9 %collective-permute-done.9 = bf16[1,256,128]{2,1,0:T(8,128)(2,1)S(1)} collective-permute-done((bf16[1,256,128]{2,1,0:T(8,128)(2,1)S(1)}, bf16[1,256,128]{2,1,0:T(8,128)(2,1)S(1)}, u32[]{:S(2)}, u32[]{:S(2)}) %collective-permute-start.9) | collective-permute-done | bytes 65568 | tf_op jit(solution)/shard_map/ppermute | solution.py:164
  121.9 3.2 %collective-permute-done.7 = bf16[1,256,128]{2,1,0:T(8,128)(2,1)S(1)} collective-permute-done((bf16[1,256,128]{2,1,0:T(8,128)(2,1)S(1)}, bf16[1,256,128]{2,1,0:T(8,128)(2,1)S(1)}, u32[]{:S(2)}, u32[]{:S(2)}) %collective-permute-start.7) | collective-permute-done | bytes 65568 | tf_op jit(solution)/shard_map/ppermute | solution.py:164
  125.2 0.1 pad_maximum_fusion.g_ref
  125.3 1.2 copy-done.2
  126.5 0.9 low_rank.1
  127.4 1.5 collective-permute-start.17
  128.8 2.1 %collective-permute-start.15 = (bf16[64,128]{1,0:T(8,128)(2,1)S(1)}, bf16[64,128]{1,0:T(8,128)(2,1)S(1)}, u32[]{:S(2)}, u32[]{:S(2)}) collective-permute-start(bf16[64,128]{1,0:T(8,128)(2,1)S(1)} %low_rank.1), channel_id=1, source_target_pairs={{0,4},{1,5},{2,6},{3,7},{4,0},{5,1},{6,2},{7,3},{8,12},{9,13},{10,... | collective-permute-start | bytes 49160 | tf_op jit(solution)/shard_map/ppermute | solution.py:164
  131.0 0.8 collective-permute-done.17
  131.8 0.5 collective-permute-done.16
  132.3 3.6 %collective-permute-start.20 = (bf16[4,64,128]{2,1,0:T(8,128)(2,1)S(1)}, bf16[4,64,128]{2,1,0:T(8,128)(2,1)S(1)}, u32[]{:S(2)}, u32[]{:S(2)}) collective-permute-start(bf16[4,64,128]{2,1,0:T(8,128)(2,1)S(1)} %pad_maximum_fusion.3.refs_0_), channel_id=1, source_target_pairs={{0,3},{1,2},{2,1},{3,0},{4,7},{5,6},{6,5},{7,4},{8,11},{9,10},{10,... | collective-permute-start | bytes 196616 | tf_op jit(solution)/shard_map/ppermute | solution.py:164
  135.9 0.3 collective-permute-start.19
  136.2 0.2 collective-permute-start.18
  136.4 2.4 %collective-permute-done.20.refs_3_ = bf16[4,64,128]{2,1,0:T(8,128)(2,1)S(1)} collective-permute-done((bf16[4,64,128]{2,1,0:T(8,128)(2,1)S(1)}, bf16[4,64,128]{2,1,0:T(8,128)(2,1)S(1)}, u32[]{:S(2)}, u32[]{:S(2)}) %collective-permute-start.20) | collective-permute-done | bytes 65568 | tf_op jit(solution)/shard_map/ppermute | solution.py:164
  138.8 1.4 collective-permute-done.19.refs_2_
  140.2 9.1 %attend.1 = bf16[16,4,64,128]{3,2,1,0:T(8,128)(2,1)S(1)} custom-call(s32[1]{0:T(128)} %bitcast.me_ref, bf16[4,64,128]{2,1,0:T(8,128)(2,1)S(1)} %bitcast.12, bf16[16,4,64,128]{3,2,1,0:T(8,128)(2,1)S(1)} %all-to-all-done.2.q_ref, bf16[16,4,64,128]{3,2,1,0:T(8,128)(2,1)S(1)} %all-to-all-done.k_ref, bf16[16,4,64,128]{3,2,1,0:T(8,128)(2,1)S(1)} %all-to-all-done.1.v_ref, ...), custom_call_target="tpu_custom_call" | custom-call | flops 2147483648 | bytes 4194304 | tf_op jit(solution)/shard_map/attend/pallas_call | solution.py:265
  149.3 29.0 %all_to_all.20 = bf16[16,4,64,128]{3,2,1,0:T(8,128)(2,1)S(1)} all-to-all(bf16[16,4,64,128]{3,2,1,0:T(8,128)(2,1)S(1)} %attend.1), channel_id=1, replica_groups=mesh['grp'=2,'seq'=16] {'seq'}, dimensions={0} | all-to-all | bytes 2097152 | tf_op jit(solution)/shard_map/all_to_all | solution.py:167
  178.4 1.0 copy.10
  (36 shorter events, 0.3 us)
Async XLA Ops:
  0.0 7.5 %copy-start.7 = (s32[2]{0:T(128)S(1)}, s32[2]{0:T(128)}, u32[]{:S(2)}) copy-start(s32[2]{0:T(128)} %req_ref.1) | copy-start | bytes 28
  0.0 7.5 %copy-start.6 = (s32[64]{0:T(128)S(1)}, s32[64]{0:T(128)}, u32[]{:S(2)}) copy-start(s32[64]{0:T(128)} %row_ref.1) | copy-start | bytes 772
  0.0 7.5 %copy-start.1 = (bf16[4,64,4096]{2,1,0:T(8,128)(2,1)S(1)}, bf16[4,64,4096]{2,1,0:T(8,128)(2,1)}, u32[]{:S(2)}) copy-start(bf16[4,64,4096]{2,1,0:T(8,128)(2,1)} %up_ref.1) | copy-start | bytes 6291460
  0.0 30.6 %all-to-all-start = ((bf16[16,4,64,128]{3,2,1,0:T(8,128)(2,1)}), bf16[16,4,64,128]{3,2,1,0:T(8,128)(2,1)S(1)}, u32[]{:S(2)}, u32[]{:S(2)}) async-start(bf16[16,4,64,128]{3,2,1,0:T(8,128)(2,1)} %bitcast.14), calls=%async_computation | async-start | bytes 2097152 | tf_op jit(solution)/shard_map/all_to_all | solution.py:167
  7.5 1.7 copy-start
  10.8 16.2 %copy-start.4 = (bf16[4,256,128]{2,1,0:T(8,128)(2,1)}, bf16[4,256,128]{2,1,0:T(8,128)(2,1)S(1)}, u32[]{:S(2)}) copy-start(bf16[4,256,128]{2,1,0:T(8,128)(2,1)S(1)} %get-tuple-element.20) | copy-start | bytes 786436
  10.8 19.8 %copy-start.3 = (bf16[2,32,64,128]{3,2,1,0:T(8,128)(2,1)S(1)}, bf16[2,32,64,128]{3,2,1,0:T(8,128)(2,1)}, u32[]{:S(2)}) copy-start(bf16[2,32,64,128]{3,2,1,0:T(8,128)(2,1)} %param.11) | copy-start | bytes 3145732
  10.8 2.2 %collective-permute-start = (bf16[8,320,128]{2,1,0:T(8,128)(2,1)S(1)}, bf16[8,320,128]{2,1,0:T(8,128)(2,1)S(1)}, u32[]{:S(2)}, u32[]{:S(2)}) collective-permute-start(bf16[8,320,128]{2,1,0:T(8,128)(2,1)S(1)} %get-tuple-element.23), channel_id=1, source_target_pairs={{0,1},{1,0},{2,3},{3,2},{4,5},{5,4},{6,7},{7,6},{8,9},{9,8},{10,11... | collective-permute-start | bytes 1966088 | tf_op jit(solution)/shard_map/ppermute | solution.py:164
  13.0 13.9 %collective-permute-start.2 = (bf16[4,320,128]{2,1,0:T(8,128)(2,1)S(1)}, bf16[4,320,128]{2,1,0:T(8,128)(2,1)S(1)}, u32[]{:S(2)}, u32[]{:S(2)}) collective-permute-start(bf16[4,320,128]{2,1,0:T(8,128)(2,1)S(1)} %slice_add_fusion.1), channel_id=1, source_target_pairs={{0,2},{1,3},{2,0},{3,1},{4,6},{5,7},{6,4},{7,5},{8,10},{9,11},{10,... | collective-permute-start | bytes 983048 | tf_op jit(solution)/shard_map/ppermute | solution.py:164
  14.5 12.5 %collective-permute-start.1 = (bf16[8,256,128]{2,1,0:T(8,128)(2,1)S(1)}, bf16[8,256,128]{2,1,0:T(8,128)(2,1)}, u32[]{:S(2)}, u32[]{:S(2)}) collective-permute-start(bf16[8,256,128]{2,1,0:T(8,128)(2,1)S(1)} %get-tuple-element.24), channel_id=1, source_target_pairs={{0,1},{1,0},{2,3},{3,2},{4,5},{5,4},{6,7},{7,6},{8,9},{9,8},{10,11... | collective-permute-start | bytes 1572872 | tf_op jit(solution)/shard_map/ppermute | solution.py:164
  27.0 11.4 %copy-start.8 = (bf16[4,320,128]{2,1,0:T(8,128)(2,1)}, bf16[4,320,128]{2,1,0:T(8,128)(2,1)S(1)}, u32[]{:S(2)}) copy-start(bf16[4,320,128]{2,1,0:T(8,128)(2,1)S(1)} %fusion) | copy-start | bytes 983044
  31.7 29.8 %all-to-all-start.1 = ((bf16[16,4,64,128]{3,2,1,0:T(8,128)(2,1)}), bf16[16,4,64,128]{3,2,1,0:T(8,128)(2,1)S(1)}, u32[]{:S(2)}, u32[]{:S(2)}) async-start(bf16[16,4,64,128]{3,2,1,0:T(8,128)(2,1)} %stage.1), calls=%async_computation.1 | async-start | bytes 2097152 | tf_op jit(solution)/shard_map/all_to_all | solution.py:167
  39.1 33.0 %collective-permute-start.5 = (bf16[1,320,128]{2,1,0:T(8,128)(2,1)}, bf16[1,320,128]{2,1,0:T(8,128)(2,1)S(1)}, u32[]{:S(2)}, u32[]{:S(2)}) collective-permute-start(bf16[1,320,128]{2,1,0:T(8,128)(2,1)} %get-tuple-element.35), channel_id=1, source_target_pairs={{0,4},{1,5},{2,6},{3,7},{4,0},{5,1},{6,2},{7,3},{8,12},{9,13},{10,... | collective-permute-start | bytes 245768 | tf_op jit(solution)/shard_map/ppermute | solution.py:164
  40.5 31.6 %collective-permute-start.6 = (bf16[1,320,128]{2,1,0:T(8,128)(2,1)}, bf16[1,320,128]{2,1,0:T(8,128)(2,1)}, u32[]{:S(2)}, u32[]{:S(2)}) collective-permute-start(bf16[1,320,128]{2,1,0:T(8,128)(2,1)} %get-tuple-element.36), channel_id=1, source_target_pairs={{0,12},{1,13},{2,14},{3,15},{4,8},{5,9},{6,10},{7,11},{8,4},{9,5},... | collective-permute-start | bytes 245768 | tf_op jit(solution)/shard_map/ppermute | solution.py:164
  42.5 29.5 %collective-permute-start.4 = (bf16[1,320,128]{2,1,0:T(8,128)(2,1)}, bf16[1,320,128]{2,1,0:T(8,128)(2,1)}, u32[]{:S(2)}, u32[]{:S(2)}) collective-permute-start(bf16[1,320,128]{2,1,0:T(8,128)(2,1)} %get-tuple-element.37), channel_id=1, source_target_pairs={{0,8},{1,9},{2,10},{3,11},{4,12},{5,13},{6,14},{7,15},{8,0},{9,1},... | collective-permute-start | bytes 245768 | tf_op jit(solution)/shard_map/ppermute | solution.py:164
  44.2 28.9 %collective-permute-start.3 = (bf16[4,256,128]{2,1,0:T(8,128)(2,1)}, bf16[4,256,128]{2,1,0:T(8,128)(2,1)S(1)}, u32[]{:S(2)}, u32[]{:S(2)}) collective-permute-start(bf16[4,256,128]{2,1,0:T(8,128)(2,1)} %slice_add_fusion.2), channel_id=1, source_target_pairs={{0,2},{1,3},{2,0},{3,1},{4,6},{5,7},{6,4},{7,5},{8,10},{9,11},{10,... | collective-permute-start | bytes 786440 | tf_op jit(solution)/shard_map/ppermute | solution.py:164
  61.5 78.7 %all-to-all-start.2 = ((bf16[16,4,64,128]{3,2,1,0:T(8,128)(2,1)}), bf16[16,4,64,128]{3,2,1,0:T(8,128)(2,1)S(1)}, u32[]{:S(2)}, u32[]{:S(2)}) async-start(bf16[16,4,64,128]{3,2,1,0:T(8,128)(2,1)} %bitcast.15), calls=%async_computation.2 | async-start | bytes 2097152 | tf_op jit(solution)/shard_map/all_to_all | solution.py:167
  72.1 43.2 %copy-start.5 = (bf16[4,256,128]{2,1,0:T(8,128)(2,1)S(1)}, bf16[4,256,128]{2,1,0:T(8,128)(2,1)}, u32[]{:S(2)}) copy-start(bf16[4,256,128]{2,1,0:T(8,128)(2,1)} %copy-done.4) | copy-start | bytes 786436
  73.1 21.8 %collective-permute-start.12 = (bf16[1,320,128]{2,1,0:T(8,128)(2,1)S(1)}, bf16[1,320,128]{2,1,0:T(8,128)(2,1)S(1)}, u32[]{:S(2)}, u32[]{:S(2)}) collective-permute-start(bf16[1,320,128]{2,1,0:T(8,128)(2,1)S(1)} %add_add_fusion), channel_id=1, source_target_pairs={{0,12},{1,13},{2,14},{3,15},{4,8},{5,9},{6,10},{7,11},{8,4},{9,5},... | collective-permute-start | bytes 245768 | tf_op jit(solution)/shard_map/ppermute | solution.py:164
  76.4 18.6 %collective-permute-start.11 = (bf16[1,320,128]{2,1,0:T(8,128)(2,1)S(1)}, bf16[1,320,128]{2,1,0:T(8,128)(2,1)S(1)}, u32[]{:S(2)}, u32[]{:S(2)}) collective-permute-start(bf16[1,320,128]{2,1,0:T(8,128)(2,1)S(1)} %add_add_fusion), channel_id=1, source_target_pairs={{0,4},{1,5},{2,6},{3,7},{4,0},{5,1},{6,2},{7,3},{8,12},{9,13},{10,... | collective-permute-start | bytes 245768 | tf_op jit(solution)/shard_map/ppermute | solution.py:164
  76.4 28.5 %collective-permute-start.10 = (bf16[1,320,128]{2,1,0:T(8,128)(2,1)S(1)}, bf16[1,320,128]{2,1,0:T(8,128)(2,1)S(1)}, u32[]{:S(2)}, u32[]{:S(2)}) collective-permute-start(bf16[1,320,128]{2,1,0:T(8,128)(2,1)S(1)} %add_add_fusion), channel_id=1, source_target_pairs={{0,8},{1,9},{2,10},{3,11},{4,12},{5,13},{6,14},{7,15},{8,0},{9,1},... | collective-permute-start | bytes 245768 | tf_op jit(solution)/shard_map/ppermute | solution.py:164
  104.9 8.4 %collective-permute-start.13 = (bf16[4,320,128]{2,1,0:T(8,128)(2,1)S(1)}, bf16[4,320,128]{2,1,0:T(8,128)(2,1)S(1)}, u32[]{:S(2)}, u32[]{:S(2)}) collective-permute-start(bf16[4,320,128]{2,1,0:T(8,128)(2,1)S(1)} %pad_maximum_fusion.2), channel_id=1, source_target_pairs={{0,2},{1,3},{2,0},{3,1},{4,6},{5,7},{6,4},{7,5},{8,10},{9,11},{10,... | collective-permute-start | bytes 983048 | tf_op jit(solution)/shard_map/ppermute | solution.py:164
  113.4 11.8 %collective-permute-start.14 = (bf16[8,320,128]{2,1,0:T(8,128)(2,1)S(1)}, bf16[8,320,128]{2,1,0:T(8,128)(2,1)S(1)}, u32[]{:S(2)}, u32[]{:S(2)}) collective-permute-start(bf16[8,320,128]{2,1,0:T(8,128)(2,1)S(1)} %pad_maximum_fusion.1), channel_id=1, source_target_pairs={{0,1},{1,0},{2,3},{3,2},{4,5},{5,4},{6,7},{7,6},{8,9},{9,8},{10,11... | collective-permute-start | bytes 1966088 | tf_op jit(solution)/shard_map/ppermute | solution.py:164
  116.2 3.8 %collective-permute-start.8 = (bf16[1,256,128]{2,1,0:T(8,128)(2,1)S(1)}, bf16[1,256,128]{2,1,0:T(8,128)(2,1)S(1)}, u32[]{:S(2)}, u32[]{:S(2)}) collective-permute-start(bf16[1,256,128]{2,1,0:T(8,128)(2,1)S(1)} %get-tuple-element.38), channel_id=1, source_target_pairs={{0,4},{1,5},{2,6},{3,7},{4,0},{5,1},{6,2},{7,3},{8,12},{9,13},{10,... | collective-permute-start | bytes 196616 | tf_op jit(solution)/shard_map/ppermute | solution.py:164
  116.3 5.6 %collective-permute-start.9 = (bf16[1,256,128]{2,1,0:T(8,128)(2,1)S(1)}, bf16[1,256,128]{2,1,0:T(8,128)(2,1)S(1)}, u32[]{:S(2)}, u32[]{:S(2)}) collective-permute-start(bf16[1,256,128]{2,1,0:T(8,128)(2,1)S(1)} %get-tuple-element.39), channel_id=1, source_target_pairs={{0,12},{1,13},{2,14},{3,15},{4,8},{5,9},{6,10},{7,11},{8,4},{9,5},... | collective-permute-start | bytes 196616 | tf_op jit(solution)/shard_map/ppermute | solution.py:164
  117.6 7.6 %collective-permute-start.7 = (bf16[1,256,128]{2,1,0:T(8,128)(2,1)S(1)}, bf16[1,256,128]{2,1,0:T(8,128)(2,1)S(1)}, u32[]{:S(2)}, u32[]{:S(2)}) collective-permute-start(bf16[1,256,128]{2,1,0:T(8,128)(2,1)S(1)} %get-tuple-element.40), channel_id=1, source_target_pairs={{0,8},{1,9},{2,10},{3,11},{4,12},{5,13},{6,14},{7,15},{8,0},{9,1},... | collective-permute-start | bytes 196616 | tf_op jit(solution)/shard_map/ppermute | solution.py:164
  125.2 1.3 copy-start.2
  127.4 4.5 %collective-permute-start.17 = (bf16[64,128]{1,0:T(8,128)(2,1)S(1)}, bf16[64,128]{1,0:T(8,128)(2,1)S(1)}, u32[]{:S(2)}, u32[]{:S(2)}) collective-permute-start(bf16[64,128]{1,0:T(8,128)(2,1)S(1)} %low_rank.1), channel_id=1, source_target_pairs={{0,12},{1,13},{2,14},{3,15},{4,8},{5,9},{6,10},{7,11},{8,4},{9,5},... | collective-permute-start | bytes 49160 | tf_op jit(solution)/shard_map/ppermute | solution.py:164
  128.8 3.5 %collective-permute-start.16 = (bf16[64,128]{1,0:T(8,128)(2,1)S(1)}, bf16[64,128]{1,0:T(8,128)(2,1)S(1)}, u32[]{:S(2)}, u32[]{:S(2)}) collective-permute-start(bf16[64,128]{1,0:T(8,128)(2,1)S(1)} %low_rank.1), channel_id=1, source_target_pairs={{0,8},{1,9},{2,10},{3,11},{4,12},{5,13},{6,14},{7,15},{8,0},{9,1},... | collective-permute-start | bytes 49160 | tf_op jit(solution)/shard_map/ppermute | solution.py:164
  128.8 3.5 %collective-permute-start.15 = (bf16[64,128]{1,0:T(8,128)(2,1)S(1)}, bf16[64,128]{1,0:T(8,128)(2,1)S(1)}, u32[]{:S(2)}, u32[]{:S(2)}) collective-permute-start(bf16[64,128]{1,0:T(8,128)(2,1)S(1)} %low_rank.1), channel_id=1, source_target_pairs={{0,4},{1,5},{2,6},{3,7},{4,0},{5,1},{6,2},{7,3},{8,12},{9,13},{10,... | collective-permute-start | bytes 49160 | tf_op jit(solution)/shard_map/ppermute | solution.py:164
  132.3 6.5 %collective-permute-start.20 = (bf16[4,64,128]{2,1,0:T(8,128)(2,1)S(1)}, bf16[4,64,128]{2,1,0:T(8,128)(2,1)S(1)}, u32[]{:S(2)}, u32[]{:S(2)}) collective-permute-start(bf16[4,64,128]{2,1,0:T(8,128)(2,1)S(1)} %pad_maximum_fusion.3.refs_0_), channel_id=1, source_target_pairs={{0,3},{1,2},{2,1},{3,0},{4,7},{5,6},{6,5},{7,4},{8,11},{9,10},{10,... | collective-permute-start | bytes 196616 | tf_op jit(solution)/shard_map/ppermute | solution.py:164
  135.9 4.3 %collective-permute-start.19 = (bf16[4,64,128]{2,1,0:T(8,128)(2,1)S(1)}, bf16[4,64,128]{2,1,0:T(8,128)(2,1)S(1)}, u32[]{:S(2)}, u32[]{:S(2)}) collective-permute-start(bf16[4,64,128]{2,1,0:T(8,128)(2,1)S(1)} %pad_maximum_fusion.3.refs_0_), channel_id=1, source_target_pairs={{0,2},{1,3},{2,0},{3,1},{4,6},{5,7},{6,4},{7,5},{8,10},{9,11},{10,... | collective-permute-start | bytes 196616 | tf_op jit(solution)/shard_map/ppermute | solution.py:164
  136.2 4.0 %collective-permute-start.18 = (bf16[4,64,128]{2,1,0:T(8,128)(2,1)S(1)}, bf16[4,64,128]{2,1,0:T(8,128)(2,1)S(1)}, u32[]{:S(2)}, u32[]{:S(2)}) collective-permute-start(bf16[4,64,128]{2,1,0:T(8,128)(2,1)S(1)} %pad_maximum_fusion.3.refs_0_), channel_id=1, source_target_pairs={{0,1},{1,0},{2,3},{3,2},{4,5},{5,4},{6,7},{7,6},{8,9},{9,8},{10,11... | collective-permute-start | bytes 196616 | tf_op jit(solution)/shard_map/ppermute | solution.py:164

commit v11 on v10

--- a/solution.py
+++ b/solution.py
@@ -71,10 +71,6 @@
         for p in range(pairs):
             col = pl.multiple_of((place * pairs + p) * LANES, LANES)
             ups[step][at, p * ranks : (p + 1) * ranks, :] = up[video, :, pl.ds(col, LANES)]
-
-
-def copy_kernel(in_ref, out_ref):
-    out_ref[...] = in_ref[...]
 
 
 def low_rank_kernel(shape, me_ref, x_ref, g_ref, out_ref, down):
@@ -209,39 +205,28 @@
     )(me, adapter_store_row, requests, adapter_down_factors, adapter_up_factors)
     down_pieces, up_pieces = pieces[: bits - 1], pieces[bits - 1 :]
 
-    def stage(tensor):
-        return pl.pallas_call(
-            copy_kernel,
-            in_specs=[VMEM],
-            out_specs=VMEM,
-            out_shape=jax.ShapeDtypeStruct((devs, pairs, toks, width), jnp.bfloat16),
-            compiler_params=pltpu.CompilerParams(vmem_limit_bytes=24 << 20),
-            cost_estimate=pl.CostEstimate(
-                flops=0, bytes_accessed=4 * pairs * length * width, transcendentals=0
-            ),
-            name="stage",
-        )(tensor)
-
     down_got, up_got = [], []
+
+    def send_up(i, *others):
+        up_got.append(swap(after(halving(up_pieces, up_got, i), *others), 1 << i))
+
     for i in range(bits - 2):
         piece = halving(down_pieces, down_got, i)
         if i > 0:
-            up_got.append(swap(after(halving(up_pieces, up_got, i - 1), piece), 1 << (i - 1)))
+            send_up(i - 1, piece)
         down_got.append(swap(piece, 1 << i))
-    shards = halving(down_pieces, down_got, bits - 2)
-    shards = after(shards, keys, *up_got)
-    vals = exchange(stage(after(by_pairs(values), shards)))
-    up_got.append(swap(after(halving(up_pieces, up_got, bits - 3), shards), 1 << (bits - 3)))
-    shard = shards[:1] + sum(to_others(shards))
-    shard = after(shard, *up_got)
-    up_shards = after(halving(up_pieces, up_got, bits - 2), shard)
+    shards = after(halving(down_pieces, down_got, bits - 2), keys, *up_got)
+    got = to_others(shards)
+    vals = exchange(after(by_pairs(values), got[1]))
+    shard = shards[:1] + sum(got)
+    send_up(bits - 3, shard)
+    spread = [swap(shard, k) for k in others]
+    asked = exchange(after(by_pairs(queries), vals, spread[1], up_got[-1]))
+    gathered = jnp.concatenate([shard] + spread, axis=0)
+    up_shards = after(halving(up_pieces, up_got, bits - 2), vals)
     up_here = (up_shards[:1] + sum(to_others(up_shards))).reshape(pairs, ranks, LANES)
-    gathered = jnp.concatenate([shard] + [swap(shard, k) for k in others], axis=0)
-    gathered = after(gathered, vals)
-    asked = exchange(after(by_pairs(queries), vals))
     for i in reversed(range(bits - 2)):
         gathered = jnp.concatenate([gathered, swap(gathered, 1 << i)], axis=0)
-    gathered = after(gathered, up_here)
 
     low = pl.pallas_call(
         functools.partial(low_rank_kernel, shape),
@@ -258,6 +243,7 @@
         name="low_rank",
     )(me, normed_token_features, gathered)
     far = jnp.stack([low] + [swap(low, LOW * i) for i in range(1, devs // LOW)])
+    far = after(far, up_here)
     lows = [far] + [swap(far, i) for i in range(1, LOW)]
 
     low_spec = pl.BlockSpec((devs // LOW, toks, videos * ranks), lambda p: (0, 0, 0))

time: 180 us -> 170 us (0.944)
  waiting for transfers between devices: 80.1 us -> 73.5 us
  other arithmetic: 4.04 us -> 0.91 us
    all_to_all x3, waiting for transfers between devices: 19.7 us -> 3.65 us  [exchange(): lax.all_to_all(tensor, 'seq', split_axis=0, concat_axis=0, tiled=True)]
    ppermute x21, waiting for transfers between devices: 60.4 us -> 69.9 us  [swap(): return lax.ppermute(tensor, 'seq', [(i, i ^ k) for i in range(devs)])]
    ppermute x21, starting transfers between devices: 24.1 us -> 29.7 us  [swap(): return lax.ppermute(tensor, 'seq', [(i, i ^ k) for i in range(devs)])]
    all_to_all x3, starting transfers between devices: 24.7 us -> 19.7 us  [exchange(): lax.all_to_all(tensor, 'seq', split_axis=0, concat_axis=0, tiled=True)]
    add x4, other arithmetic: 2.76 us -> 0.16 us  [halving(): return sum((r[start:start + size] for r in received), parts[i])]
  transfers between devices with their start and end apart: 24 -> 24, of which waited for: 14 -> 13; matrix products, arithmetic and copies ran while one was open for 3% -> 2% of each run, Pallas kernels for 1% -> 1%
where the time goes in v11:
time: 170 us
  waiting for transfers between devices  73.5 us (43%)
  starting transfers between devices  49.3 us (29%)
  blocking collectives  27.9 us (16%)
  Pallas kernels  12.3 us (7%)
  local copies, waits for them, and re-layouts  5.61 us (3%)
    ppermute x21, waiting for transfers between devices, swap(): return lax.ppermute(tensor, 'seq', [(i, i ^ k) for i in range(devs)])  69.9 us
    ppermute x21, starting transfers between devices, swap(): return lax.ppermute(tensor, 'seq', [(i, i ^ k) for i in range(devs)])  29.7 us
    all_to_all x1, blocking collectives, exchange(): lax.all_to_all(tensor, 'seq', split_axis=0, concat_axis=0, tiled=True)  27.9 us
    all_to_all x3, starting transfers between devices, exchange(): lax.all_to_all(tensor, 'seq', split_axis=0, concat_axis=0, tiled=True)  19.7 us
    pallas_call x1, Pallas kernels, body(): pl.pallas_call(functools.partial(attend_kernel, per_video, math.gcd(devs,...  9.96 us
    unnamed x19, local copies, waits for them, and re-layouts  4.69 us
    all_to_all x3, waiting for transfers between devices, exchange(): lax.all_to_all(tensor, 'seq', split_axis=0, concat_axis=0, tiled=True)  3.65 us
  transfers between devices with their start and end apart: 24, of which 13 were waited for; matrix products, arithmetic and copies ran while one was open for 2% of the time, Pallas kernels for 1%

profile of v11, /device:TPU:1, one launch (start us, length us, event | category | flops | bytes accessed | tf_op | source)
XLA Modules:
  0.0 169.8 jit_solution(17435683134512045021)
XLA Ops:
  0.0 7.5 %all-to-all-start = ((bf16[16,4,64,128]{3,2,1,0:T(8,128)(2,1)}), bf16[16,4,64,128]{3,2,1,0:T(8,128)(2,1)S(1)}, u32[]{:S(2)}, u32[]{:S(2)}) async-start(bf16[16,4,64,128]{3,2,1,0:T(8,128)(2,1)} %bitcast.13), calls=%async_computation | async-start | bytes 2097152 | tf_op jit(solution)/shard_map/all_to_all | solution.py:163
  7.5 0.0 copy-start
  7.5 1.7 %copy-done = bf16[4,64,5120]{2,1,0:T(8,128)(2,1)S(1)} copy-done((bf16[4,64,5120]{2,1,0:T(8,128)(2,1)S(1)}, bf16[4,64,5120]{2,1,0:T(8,128)(2,1)}, u32[]{:S(2)}) %copy-start) | copy-done | bytes 2621464
  9.3 1.5 pick_factors.1
  10.8 0.3 collective-permute-start
  11.1 1.8 %collective-permute-done = bf16[8,320,128]{2,1,0:T(8,128)(2,1)S(1)} collective-permute-done((bf16[8,320,128]{2,1,0:T(8,128)(2,1)S(1)}, bf16[8,320,128]{2,1,0:T(8,128)(2,1)S(1)}, u32[]{:S(2)}, u32[]{:S(2)}) %collective-permute-start) | collective-permute-done | bytes 655392 | tf_op jit(solution)/shard_map/ppermute | solution.py:160
  13.0 1.5 collective-permute-start.2
  14.5 0.6 collective-permute-start.1
  15.1 11.8 %collective-permute-done.2 = bf16[4,320,128]{2,1,0:T(8,128)(2,1)S(1)} collective-permute-done((bf16[4,320,128]{2,1,0:T(8,128)(2,1)S(1)}, bf16[4,320,128]{2,1,0:T(8,128)(2,1)S(1)}, u32[]{:S(2)}, u32[]{:S(2)}) %collective-permute-start.2) | collective-permute-done | bytes 327712 | tf_op jit(solution)/shard_map/ppermute | solution.py:160
  27.0 3.6 %all-to-all-done.k_ref = bf16[16,4,64,128]{3,2,1,0:T(8,128)(2,1)S(1)} async-done(((bf16[16,4,64,128]{3,2,1,0:T(8,128)(2,1)}), bf16[16,4,64,128]{3,2,1,0:T(8,128)(2,1)S(1)}, u32[]{:S(2)}, u32[]{:S(2)}) %all-to-all-start) | async-done | bytes 1048608 | tf_op jit(solution)/shard_map/all_to_all | solution.py:163
  30.7 3.2 %collective-permute-start.4 = (bf16[1,320,128]{2,1,0:T(8,128)(2,1)S(1)}, bf16[1,320,128]{2,1,0:T(8,128)(2,1)S(1)}, u32[]{:S(2)}, u32[]{:S(2)}) collective-permute-start(bf16[1,320,128]{2,1,0:T(8,128)(2,1)S(1)} %get-tuple-element.35), channel_id=1, source_target_pairs={{0,4},{1,5},{2,6},{3,7},{4,0},{5,1},{6,2},{7,3},{8,12},{9,13},{10,... | collective-permute-start | bytes 245768 | tf_op jit(solution)/shard_map/ppermute | solution.py:160
  33.8 2.8 %collective-permute-done.4 = bf16[1,320,128]{2,1,0:T(8,128)(2,1)S(1)} collective-permute-done((bf16[1,320,128]{2,1,0:T(8,128)(2,1)S(1)}, bf16[1,320,128]{2,1,0:T(8,128)(2,1)S(1)}, u32[]{:S(2)}, u32[]{:S(2)}) %collective-permute-start.4) | collective-permute-done | bytes 81952 | tf_op jit(solution)/shard_map/ppermute | solution.py:160
  36.7 5.4 %all-to-all-start.1 = ((bf16[16,4,64,128]{3,2,1,0:T(8,128)(2,1)}), bf16[16,4,64,128]{3,2,1,0:T(8,128)(2,1)}, u32[]{:S(2)}, u32[]{:S(2)}) async-start(bf16[16,4,64,128]{3,2,1,0:T(8,128)(2,1)} %bitcast.2), calls=%async_computation.1 | async-start | bytes 2097152 | tf_op jit(solution)/shard_map/all_to_all | solution.py:163
  42.1 2.3 %collective-permute-start.3 = (bf16[1,320,128]{2,1,0:T(8,128)(2,1)S(1)}, bf16[1,320,128]{2,1,0:T(8,128)(2,1)S(1)}, u32[]{:S(2)}, u32[]{:S(2)}) collective-permute-start(bf16[1,320,128]{2,1,0:T(8,128)(2,1)S(1)} %get-tuple-element.37), channel_id=1, source_target_pairs={{0,8},{1,9},{2,10},{3,11},{4,12},{5,13},{6,14},{7,15},{8,0},{9,1},... | collective-permute-start | bytes 245768 | tf_op jit(solution)/shard_map/ppermute | solution.py:160
  44.3 1.2 collective-permute-start.5
  45.6 27.5 %collective-permute-done.3 = bf16[1,320,128]{2,1,0:T(8,128)(2,1)S(1)} collective-permute-done((bf16[1,320,128]{2,1,0:T(8,128)(2,1)S(1)}, bf16[1,320,128]{2,1,0:T(8,128)(2,1)S(1)}, u32[]{:S(2)}, u32[]{:S(2)}) %collective-permute-start.3) | collective-permute-done | bytes 81952 | tf_op jit(solution)/shard_map/ppermute | solution.py:160
  73.1 0.7 constant_dynamic-update-slice_fusion.4
  73.8 1.2 collective-permute-start.6
  75.0 2.0 %collective-permute-start.10 = (bf16[1,320,128]{2,1,0:T(8,128)(2,1)S(1)}, bf16[1,320,128]{2,1,0:T(8,128)(2,1)S(1)}, u32[]{:S(2)}, u32[]{:S(2)}) collective-permute-start(bf16[1,320,128]{2,1,0:T(8,128)(2,1)S(1)} %get-tuple-element.32), channel_id=1, source_target_pairs={{0,4},{1,5},{2,6},{3,7},{4,0},{5,1},{6,2},{7,3},{8,12},{9,13},{10,... | collective-permute-start | bytes 245768 | tf_op jit(solution)/shard_map/ppermute | solution.py:160
  77.0 2.1 %collective-permute-start.12 = (bf16[1,320,128]{2,1,0:T(8,128)(2,1)S(1)}, bf16[1,320,128]{2,1,0:T(8,128)(2,1)S(1)}, u32[]{:S(2)}, u32[]{:S(2)}) collective-permute-start(bf16[1,320,128]{2,1,0:T(8,128)(2,1)S(1)} %get-tuple-element.32), channel_id=1, source_target_pairs={{0,12},{1,13},{2,14},{3,15},{4,8},{5,9},{6,10},{7,11},{8,4},{9,5},... | collective-permute-start | bytes 245768 | tf_op jit(solution)/shard_map/ppermute | solution.py:160
  79.1 0.0 collective-permute-done.10
  79.1 1.1 collective-permute-done.6
  80.2 6.8 %all-to-all-start.2 = ((bf16[16,4,64,128]{3,2,1,0:T(8,128)(2,1)}), bf16[16,4,64,128]{3,2,1,0:T(8,128)(2,1)}, u32[]{:S(2)}, u32[]{:S(2)}) async-start(bf16[16,4,64,128]{3,2,1,0:T(8,128)(2,1)} %bitcast.4), calls=%async_computation.2 | async-start | bytes 2097152 | tf_op jit(solution)/shard_map/all_to_all | solution.py:163
  87.1 1.5 collective-permute-start.13
  88.6 0.7 constant_dynamic-update-slice_fusion.3
  89.2 0.7 constant_dynamic-update-slice_fusion.2
  89.9 0.7 constant_dynamic-update-slice_fusion.1
  90.5 14.3 %collective-permute-done.13 = bf16[4,320,128]{2,1,0:T(8,128)(2,1)S(1)} collective-permute-done((bf16[4,320,128]{2,1,0:T(8,128)(2,1)S(1)}, bf16[4,320,128]{2,1,0:T(8,128)(2,1)S(1)}, u32[]{:S(2)}, u32[]{:S(2)}) %collective-permute-start.13) | collective-permute-done | bytes 327712 | tf_op jit(solution)/shard_map/ppermute | solution.py:160
  104.8 0.8 constant_dynamic-update-slice_fusion
  105.6 0.9 collective-permute-start.14
  106.6 1.9 %collective-permute-done.14 = bf16[8,320,128]{2,1,0:T(8,128)(2,1)S(1)} collective-permute-done((bf16[8,320,128]{2,1,0:T(8,128)(2,1)}, bf16[8,320,128]{2,1,0:T(8,128)(2,1)S(1)}, u32[]{:S(2)}, u32[]{:S(2)}) %collective-permute-start.14) | collective-permute-done | bytes 655392 | tf_op jit(solution)/shard_map/ppermute | solution.py:160
  108.5 0.1 constant_dynamic-update-slice_fusion.5.g_ref
  108.6 0.9 low_rank.1
  109.4 1.6 collective-permute-start.15
  111.1 3.1 %collective-permute-start.16 = (bf16[64,128]{1,0:T(8,128)(2,1)S(1)}, bf16[64,128]{1,0:T(8,128)(2,1)S(1)}, u32[]{:S(2)}, u32[]{:S(2)}) collective-permute-start(bf16[64,128]{1,0:T(8,128)(2,1)S(1)} %low_rank.1), channel_id=1, source_target_pairs={{0,8},{1,9},{2,10},{3,11},{4,12},{5,13},{6,14},{7,15},{8,0},{9,1},... | collective-permute-start | bytes 49160 | tf_op jit(solution)/shard_map/ppermute | solution.py:160
  114.2 1.3 collective-permute-start.7
  115.5 2.3 %collective-permute-start.8 = (bf16[1,256,128]{2,1,0:T(8,128)(2,1)S(1)}, bf16[1,256,128]{2,1,0:T(8,128)(2,1)S(1)}, u32[]{:S(2)}, u32[]{:S(2)}) collective-permute-start(bf16[1,256,128]{2,1,0:T(8,128)(2,1)S(1)} %get-tuple-element.38), channel_id=1, source_target_pairs={{0,4},{1,5},{2,6},{3,7},{4,0},{5,1},{6,2},{7,3},{8,12},{9,13},{10,... | collective-permute-start | bytes 196616 | tf_op jit(solution)/shard_map/ppermute | solution.py:160
  117.8 0.0 collective-permute-start.9
  117.8 0.7 collective-permute-done.17
  118.6 1.9 %collective-permute-done.8 = bf16[1,256,128]{2,1,0:T(8,128)(2,1)S(1)} collective-permute-done((bf16[1,256,128]{2,1,0:T(8,128)(2,1)S(1)}, bf16[1,256,128]{2,1,0:T(8,128)(2,1)S(1)}, u32[]{:S(2)}, u32[]{:S(2)}) %collective-permute-start.8) | collective-permute-done | bytes 65568 | tf_op jit(solution)/shard_map/ppermute | solution.py:160
  120.5 2.3 %collective-permute-done.9 = bf16[1,256,128]{2,1,0:T(8,128)(2,1)S(1)} collective-permute-done((bf16[1,256,128]{2,1,0:T(8,128)(2,1)S(1)}, bf16[1,256,128]{2,1,0:T(8,128)(2,1)S(1)}, u32[]{:S(2)}, u32[]{:S(2)}) %collective-permute-start.9) | collective-permute-done | bytes 65568 | tf_op jit(solution)/shard_map/ppermute | solution.py:160
  122.8 2.9 %collective-permute-start.18 = (bf16[4,64,128]{2,1,0:T(8,128)(2,1)S(1)}, bf16[4,64,128]{2,1,0:T(8,128)(2,1)S(1)}, u32[]{:S(2)}, u32[]{:S(2)}) collective-permute-start(bf16[4,64,128]{2,1,0:T(8,128)(2,1)S(1)} %pad_maximum_fusion.1.refs_0_), channel_id=1, source_target_pairs={{0,1},{1,0},{2,3},{3,2},{4,5},{5,4},{6,7},{7,6},{8,9},{9,8},{10,11... | collective-permute-start | bytes 196616 | tf_op jit(solution)/shard_map/ppermute | solution.py:160
  125.7 1.7 %collective-permute-start.20 = (bf16[4,64,128]{2,1,0:T(8,128)(2,1)S(1)}, bf16[4,64,128]{2,1,0:T(8,128)(2,1)S(1)}, u32[]{:S(2)}, u32[]{:S(2)}) collective-permute-start(bf16[4,64,128]{2,1,0:T(8,128)(2,1)S(1)} %pad_maximum_fusion.1.refs_0_), channel_id=1, source_target_pairs={{0,3},{1,2},{2,1},{3,0},{4,7},{5,6},{6,5},{7,4},{8,11},{9,10},{10,... | collective-permute-start | bytes 196616 | tf_op jit(solution)/shard_map/ppermute | solution.py:160
  127.4 2.0 %collective-permute-done.19.refs_2_ = bf16[4,64,128]{2,1,0:T(8,128)(2,1)S(1)} collective-permute-done((bf16[4,64,128]{2,1,0:T(8,128)(2,1)S(1)}, bf16[4,64,128]{2,1,0:T(8,128)(2,1)S(1)}, u32[]{:S(2)}, u32[]{:S(2)}) %collective-permute-start.19) | collective-permute-done | bytes 65568 | tf_op jit(solution)/shard_map/ppermute | solution.py:160
  129.4 1.6 collective-permute-done.20.refs_3_
  131.0 10.0 %attend.1 = bf16[16,4,64,128]{3,2,1,0:T(8,128)(2,1)S(1)} custom-call(s32[1]{0:T(128)} %bitcast.me_ref, bf16[4,64,128]{2,1,0:T(8,128)(2,1)S(1)} %bitcast.11, bf16[16,4,64,128]{3,2,1,0:T(8,128)(2,1)} %all-to-all-done.2.q_ref, bf16[16,4,64,128]{3,2,1,0:T(8,128)(2,1)S(1)} %all-to-all-done.k_ref, bf16[16,4,64,128]{3,2,1,0:T(8,128)(2,1)} %all-to-all-done.1.v_ref, ...), custom_call_target="tpu_custom_call" | custom-call | flops 2147483648 | bytes 4194304 | tf_op jit(solution)/shard_map/attend/pallas_call | solution.py:251
  140.9 27.9 %all_to_all.20 = bf16[16,4,64,128]{3,2,1,0:T(8,128)(2,1)S(1)} all-to-all(bf16[16,4,64,128]{3,2,1,0:T(8,128)(2,1)S(1)} %attend.1), channel_id=1, replica_groups=mesh['grp'=2,'seq'=16] {'seq'}, dimensions={0} | all-to-all | bytes 2097152 | tf_op jit(solution)/shard_map/all_to_all | solution.py:163
  168.9 1.0 copy.19
  (35 shorter events, 0.3 us)
Async XLA Ops:
  0.0 7.5 %copy-start.1 = (bf16[4,64,4096]{2,1,0:T(8,128)(2,1)S(1)}, bf16[4,64,4096]{2,1,0:T(8,128)(2,1)}, u32[]{:S(2)}) copy-start(bf16[4,64,4096]{2,1,0:T(8,128)(2,1)} %up_ref.1) | copy-start | bytes 6291460
  0.0 7.5 %copy-start.5 = (s32[64]{0:T(128)S(1)}, s32[64]{0:T(128)}, u32[]{:S(2)}) copy-start(s32[64]{0:T(128)} %row_ref.1) | copy-start | bytes 772
  0.0 7.5 %copy-start.6 = (s32[2]{0:T(128)S(1)}, s32[2]{0:T(128)}, u32[]{:S(2)}) copy-start(s32[2]{0:T(128)} %req_ref.1) | copy-start | bytes 28
  0.0 30.6 %all-to-all-start = ((bf16[16,4,64,128]{3,2,1,0:T(8,128)(2,1)}), bf16[16,4,64,128]{3,2,1,0:T(8,128)(2,1)S(1)}, u32[]{:S(2)}, u32[]{:S(2)}) async-start(bf16[16,4,64,128]{3,2,1,0:T(8,128)(2,1)} %bitcast.13), calls=%async_computation | async-start | bytes 2097152 | tf_op jit(solution)/shard_map/all_to_all | solution.py:163
  7.5 1.7 %copy-start = (bf16[4,64,5120]{2,1,0:T(8,128)(2,1)S(1)}, bf16[4,64,5120]{2,1,0:T(8,128)(2,1)}, u32[]{:S(2)}) copy-start(bf16[4,64,5120]{2,1,0:T(8,128)(2,1)} %down_ref.1) | copy-start | bytes 7864324
  10.8 16.2 %copy-start.3 = (bf16[4,256,128]{2,1,0:T(8,128)(2,1)}, bf16[4,256,128]{2,1,0:T(8,128)(2,1)S(1)}, u32[]{:S(2)}) copy-start(bf16[4,256,128]{2,1,0:T(8,128)(2,1)S(1)} %get-tuple-element.18) | copy-start | bytes 786436
  10.8 2.2 %collective-permute-start = (bf16[8,320,128]{2,1,0:T(8,128)(2,1)S(1)}, bf16[8,320,128]{2,1,0:T(8,128)(2,1)S(1)}, u32[]{:S(2)}, u32[]{:S(2)}) collective-permute-start(bf16[8,320,128]{2,1,0:T(8,128)(2,1)S(1)} %get-tuple-element.21), channel_id=1, source_target_pairs={{0,1},{1,0},{2,3},{3,2},{4,5},{5,4},{6,7},{7,6},{8,9},{9,8},{10,11... | collective-permute-start | bytes 1966088 | tf_op jit(solution)/shard_map/ppermute | solution.py:160
  13.0 13.9 %collective-permute-start.2 = (bf16[4,320,128]{2,1,0:T(8,128)(2,1)S(1)}, bf16[4,320,128]{2,1,0:T(8,128)(2,1)S(1)}, u32[]{:S(2)}, u32[]{:S(2)}) collective-permute-start(bf16[4,320,128]{2,1,0:T(8,128)(2,1)S(1)} %slice_add_fusion.1), channel_id=1, source_target_pairs={{0,2},{1,3},{2,0},{3,1},{4,6},{5,7},{6,4},{7,5},{8,10},{9,11},{10,... | collective-permute-start | bytes 983048 | tf_op jit(solution)/shard_map/ppermute | solution.py:160
  14.5 12.5 %collective-permute-start.1 = (bf16[8,256,128]{2,1,0:T(8,128)(2,1)S(1)}, bf16[8,256,128]{2,1,0:T(8,128)(2,1)S(1)}, u32[]{:S(2)}, u32[]{:S(2)}) collective-permute-start(bf16[8,256,128]{2,1,0:T(8,128)(2,1)S(1)} %get-tuple-element.22), channel_id=1, source_target_pairs={{0,1},{1,0},{2,3},{3,2},{4,5},{5,4},{6,7},{7,6},{8,9},{9,8},{10,11... | collective-permute-start | bytes 1572872 | tf_op jit(solution)/shard_map/ppermute | solution.py:160
  30.7 6.0 %collective-permute-start.4 = (bf16[1,320,128]{2,1,0:T(8,128)(2,1)S(1)}, bf16[1,320,128]{2,1,0:T(8,128)(2,1)S(1)}, u32[]{:S(2)}, u32[]{:S(2)}) collective-permute-start(bf16[1,320,128]{2,1,0:T(8,128)(2,1)S(1)} %get-tuple-element.35), channel_id=1, source_target_pairs={{0,4},{1,5},{2,6},{3,7},{4,0},{5,1},{6,2},{7,3},{8,12},{9,13},{10,... | collective-permute-start | bytes 245768 | tf_op jit(solution)/shard_map/ppermute | solution.py:160
  36.7 43.6 %all-to-all-start.1 = ((bf16[16,4,64,128]{3,2,1,0:T(8,128)(2,1)}), bf16[16,4,64,128]{3,2,1,0:T(8,128)(2,1)}, u32[]{:S(2)}, u32[]{:S(2)}) async-start(bf16[16,4,64,128]{3,2,1,0:T(8,128)(2,1)} %bitcast.2), calls=%async_computation.1 | async-start | bytes 2097152 | tf_op jit(solution)/shard_map/all_to_all | solution.py:163
  42.1 31.0 %collective-permute-start.3 = (bf16[1,320,128]{2,1,0:T(8,128)(2,1)S(1)}, bf16[1,320,128]{2,1,0:T(8,128)(2,1)S(1)}, u32[]{:S(2)}, u32[]{:S(2)}) collective-permute-start(bf16[1,320,128]{2,1,0:T(8,128)(2,1)S(1)} %get-tuple-element.37), channel_id=1, source_target_pairs={{0,8},{1,9},{2,10},{3,11},{4,12},{5,13},{6,14},{7,15},{8,0},{9,1},... | collective-permute-start | bytes 245768 | tf_op jit(solution)/shard_map/ppermute | solution.py:160
  44.3 28.8 %collective-permute-start.5 = (bf16[1,320,128]{2,1,0:T(8,128)(2,1)S(1)}, bf16[1,320,128]{2,1,0:T(8,128)(2,1)S(1)}, u32[]{:S(2)}, u32[]{:S(2)}) collective-permute-start(bf16[1,320,128]{2,1,0:T(8,128)(2,1)S(1)} %get-tuple-element.36), channel_id=1, source_target_pairs={{0,12},{1,13},{2,14},{3,15},{4,8},{5,9},{6,10},{7,11},{8,4},{9,5},... | collective-permute-start | bytes 245768 | tf_op jit(solution)/shard_map/ppermute | solution.py:160
  73.8 6.5 %collective-permute-start.6 = (bf16[4,256,128]{2,1,0:T(8,128)(2,1)S(1)}, bf16[4,256,128]{2,1,0:T(8,128)(2,1)S(1)}, u32[]{:S(2)}, u32[]{:S(2)}) collective-permute-start(bf16[4,256,128]{2,1,0:T(8,128)(2,1)S(1)} %slice_add_fusion.2), channel_id=1, source_target_pairs={{0,2},{1,3},{2,0},{3,1},{4,6},{5,7},{6,4},{7,5},{8,10},{9,11},{10,... | collective-permute-start | bytes 786440 | tf_op jit(solution)/shard_map/ppermute | solution.py:160
  75.0 4.2 %collective-permute-start.10 = (bf16[1,320,128]{2,1,0:T(8,128)(2,1)S(1)}, bf16[1,320,128]{2,1,0:T(8,128)(2,1)S(1)}, u32[]{:S(2)}, u32[]{:S(2)}) collective-permute-start(bf16[1,320,128]{2,1,0:T(8,128)(2,1)S(1)} %get-tuple-element.32), channel_id=1, source_target_pairs={{0,4},{1,5},{2,6},{3,7},{4,0},{5,1},{6,2},{7,3},{8,12},{9,13},{10,... | collective-permute-start | bytes 245768 | tf_op jit(solution)/shard_map/ppermute | solution.py:160
  77.0 10.0 %collective-permute-start.11 = (bf16[1,320,128]{2,1,0:T(8,128)(2,1)S(1)}, bf16[1,320,128]{2,1,0:T(8,128)(2,1)S(1)}, u32[]{:S(2)}, u32[]{:S(2)}) collective-permute-start(bf16[1,320,128]{2,1,0:T(8,128)(2,1)S(1)} %get-tuple-element.32), channel_id=1, source_target_pairs={{0,8},{1,9},{2,10},{3,11},{4,12},{5,13},{6,14},{7,15},{8,0},{9,1},... | collective-permute-start | bytes 245768 | tf_op jit(solution)/shard_map/ppermute | solution.py:160
  77.0 10.0 %collective-permute-start.12 = (bf16[1,320,128]{2,1,0:T(8,128)(2,1)S(1)}, bf16[1,320,128]{2,1,0:T(8,128)(2,1)S(1)}, u32[]{:S(2)}, u32[]{:S(2)}) collective-permute-start(bf16[1,320,128]{2,1,0:T(8,128)(2,1)S(1)} %get-tuple-element.32), channel_id=1, source_target_pairs={{0,12},{1,13},{2,14},{3,15},{4,8},{5,9},{6,10},{7,11},{8,4},{9,5},... | collective-permute-start | bytes 245768 | tf_op jit(solution)/shard_map/ppermute | solution.py:160
  80.2 50.7 %all-to-all-start.2 = ((bf16[16,4,64,128]{3,2,1,0:T(8,128)(2,1)}), bf16[16,4,64,128]{3,2,1,0:T(8,128)(2,1)}, u32[]{:S(2)}, u32[]{:S(2)}) async-start(bf16[16,4,64,128]{3,2,1,0:T(8,128)(2,1)} %bitcast.4), calls=%async_computation.2 | async-start | bytes 2097152 | tf_op jit(solution)/shard_map/all_to_all | solution.py:163
  87.0 19.5 %copy-start.4 = (bf16[4,256,128]{2,1,0:T(8,128)(2,1)S(1)}, bf16[4,256,128]{2,1,0:T(8,128)(2,1)}, u32[]{:S(2)}) copy-start(bf16[4,256,128]{2,1,0:T(8,128)(2,1)} %copy-done.3) | copy-start | bytes 786436
  87.1 17.7 %collective-permute-start.13 = (bf16[4,320,128]{2,1,0:T(8,128)(2,1)S(1)}, bf16[4,320,128]{2,1,0:T(8,128)(2,1)S(1)}, u32[]{:S(2)}, u32[]{:S(2)}) collective-permute-start(bf16[4,320,128]{2,1,0:T(8,128)(2,1)S(1)} %pad_maximum_fusion), channel_id=1, source_target_pairs={{0,2},{1,3},{2,0},{3,1},{4,6},{5,7},{6,4},{7,5},{8,10},{9,11},{10,... | collective-permute-start | bytes 983048 | tf_op jit(solution)/shard_map/ppermute | solution.py:160
  105.6 2.9 %copy-start.2 = (bf16[2,64,5120]{2,1,0:T(8,128)(2,1)S(1)}, bf16[2,64,5120]{2,1,0:T(8,128)(2,1)}, u32[]{:S(2)}) copy-start(bf16[2,64,5120]{2,1,0:T(8,128)(2,1)} %x_ref.1) | copy-start | bytes 3932164
  105.6 2.8 %collective-permute-start.14 = (bf16[8,320,128]{2,1,0:T(8,128)(2,1)}, bf16[8,320,128]{2,1,0:T(8,128)(2,1)S(1)}, u32[]{:S(2)}, u32[]{:S(2)}) collective-permute-start(bf16[8,320,128]{2,1,0:T(8,128)(2,1)} %get-tuple-element.33), channel_id=1, source_target_pairs={{0,1},{1,0},{2,3},{3,2},{4,5},{5,4},{6,7},{7,6},{8,9},{9,8},{10,11... | collective-permute-start | bytes 1966088 | tf_op jit(solution)/shard_map/ppermute | solution.py:160
  109.4 8.4 %collective-permute-start.15 = (bf16[64,128]{1,0:T(8,128)(2,1)S(1)}, bf16[64,128]{1,0:T(8,128)(2,1)S(1)}, u32[]{:S(2)}, u32[]{:S(2)}) collective-permute-start(bf16[64,128]{1,0:T(8,128)(2,1)S(1)} %low_rank.1), channel_id=1, source_target_pairs={{0,4},{1,5},{2,6},{3,7},{4,0},{5,1},{6,2},{7,3},{8,12},{9,13},{10,... | collective-permute-start | bytes 49160 | tf_op jit(solution)/shard_map/ppermute | solution.py:160
  111.1 6.7 %collective-permute-start.16 = (bf16[64,128]{1,0:T(8,128)(2,1)S(1)}, bf16[64,128]{1,0:T(8,128)(2,1)S(1)}, u32[]{:S(2)}, u32[]{:S(2)}) collective-permute-start(bf16[64,128]{1,0:T(8,128)(2,1)S(1)} %low_rank.1), channel_id=1, source_target_pairs={{0,8},{1,9},{2,10},{3,11},{4,12},{5,13},{6,14},{7,15},{8,0},{9,1},... | collective-permute-start | bytes 49160 | tf_op jit(solution)/shard_map/ppermute | solution.py:160
  114.2 4.4 %collective-permute-start.17 = (bf16[64,128]{1,0:T(8,128)(2,1)S(1)}, bf16[64,128]{1,0:T(8,128)(2,1)S(1)}, u32[]{:S(2)}, u32[]{:S(2)}) collective-permute-start(bf16[64,128]{1,0:T(8,128)(2,1)S(1)} %low_rank.1), channel_id=1, source_target_pairs={{0,12},{1,13},{2,14},{3,15},{4,8},{5,9},{6,10},{7,11},{8,4},{9,5},... | collective-permute-start | bytes 49160 | tf_op jit(solution)/shard_map/ppermute | solution.py:160
  114.2 4.4 %collective-permute-start.7 = (bf16[1,256,128]{2,1,0:T(8,128)(2,1)S(1)}, bf16[1,256,128]{2,1,0:T(8,128)(2,1)S(1)}, u32[]{:S(2)}, u32[]{:S(2)}) collective-permute-start(bf16[1,256,128]{2,1,0:T(8,128)(2,1)S(1)} %get-tuple-element.40), channel_id=1, source_target_pairs={{0,8},{1,9},{2,10},{3,11},{4,12},{5,13},{6,14},{7,15},{8,0},{9,1},... | collective-permute-start | bytes 196616 | tf_op jit(solution)/shard_map/ppermute | solution.py:160
  115.5 5.0 %collective-permute-start.8 = (bf16[1,256,128]{2,1,0:T(8,128)(2,1)S(1)}, bf16[1,256,128]{2,1,0:T(8,128)(2,1)S(1)}, u32[]{:S(2)}, u32[]{:S(2)}) collective-permute-start(bf16[1,256,128]{2,1,0:T(8,128)(2,1)S(1)} %get-tuple-element.38), channel_id=1, source_target_pairs={{0,4},{1,5},{2,6},{3,7},{4,0},{5,1},{6,2},{7,3},{8,12},{9,13},{10,... | collective-permute-start | bytes 196616 | tf_op jit(solution)/shard_map/ppermute | solution.py:160
  117.8 5.0 %collective-permute-start.9 = (bf16[1,256,128]{2,1,0:T(8,128)(2,1)S(1)}, bf16[1,256,128]{2,1,0:T(8,128)(2,1)S(1)}, u32[]{:S(2)}, u32[]{:S(2)}) collective-permute-start(bf16[1,256,128]{2,1,0:T(8,128)(2,1)S(1)} %get-tuple-element.39), channel_id=1, source_target_pairs={{0,12},{1,13},{2,14},{3,15},{4,8},{5,9},{6,10},{7,11},{8,4},{9,5},... | collective-permute-start | bytes 196616 | tf_op jit(solution)/shard_map/ppermute | solution.py:160
  122.8 4.6 %collective-permute-start.18 = (bf16[4,64,128]{2,1,0:T(8,128)(2,1)S(1)}, bf16[4,64,128]{2,1,0:T(8,128)(2,1)S(1)}, u32[]{:S(2)}, u32[]{:S(2)}) collective-permute-start(bf16[4,64,128]{2,1,0:T(8,128)(2,1)S(1)} %pad_maximum_fusion.1.refs_0_), channel_id=1, source_target_pairs={{0,1},{1,0},{2,3},{3,2},{4,5},{5,4},{6,7},{7,6},{8,9},{9,8},{10,11... | collective-permute-start | bytes 196616 | tf_op jit(solution)/shard_map/ppermute | solution.py:160
  125.7 3.7 %collective-permute-start.19 = (bf16[4,64,128]{2,1,0:T(8,128)(2,1)S(1)}, bf16[4,64,128]{2,1,0:T(8,128)(2,1)S(1)}, u32[]{:S(2)}, u32[]{:S(2)}) collective-permute-start(bf16[4,64,128]{2,1,0:T(8,128)(2,1)S(1)} %pad_maximum_fusion.1.refs_0_), channel_id=1, source_target_pairs={{0,2},{1,3},{2,0},{3,1},{4,6},{5,7},{6,4},{7,5},{8,10},{9,11},{10,... | collective-permute-start | bytes 196616 | tf_op jit(solution)/shard_map/ppermute | solution.py:160
  125.7 5.2 %collective-permute-start.20 = (bf16[4,64,128]{2,1,0:T(8,128)(2,1)S(1)}, bf16[4,64,128]{2,1,0:T(8,128)(2,1)S(1)}, u32[]{:S(2)}, u32[]{:S(2)}) collective-permute-start(bf16[4,64,128]{2,1,0:T(8,128)(2,1)S(1)} %pad_maximum_fusion.1.refs_0_), channel_id=1, source_target_pairs={{0,3},{1,2},{2,1},{3,0},{4,7},{5,6},{6,5},{7,4},{8,11},{9,10},{10,... | collective-permute-start | bytes 196616 | tf_op jit(solution)/shard_map/ppermute | solution.py:160

commit v12 on v11

--- a/solution.py
+++ b/solution.py
@@ -216,14 +216,12 @@
             send_up(i - 1, piece)
         down_got.append(swap(piece, 1 << i))
     shards = after(halving(down_pieces, down_got, bits - 2), keys, *up_got)
-    got = to_others(shards)
-    vals = exchange(after(by_pairs(values), got[1]))
-    shard = shards[:1] + sum(got)
-    send_up(bits - 3, shard)
-    spread = [swap(shard, k) for k in others]
-    asked = exchange(after(by_pairs(queries), vals, spread[1], up_got[-1]))
-    gathered = jnp.concatenate([shard] + spread, axis=0)
-    up_shards = after(halving(up_pieces, up_got, bits - 2), vals)
+    send_up(bits - 3, shards)
+    shard = shards[:1] + sum(to_others(shards))
+    gathered = jnp.concatenate([shard] + [swap(shard, k) for k in others], axis=0)
+    asked = jnp.concatenate([by_pairs(values), by_pairs(queries)], axis=1)
+    asked = exchange(after(asked, gathered, up_got[-1]))
+    up_shards = after(halving(up_pieces, up_got, bits - 2), gathered)
     up_here = (up_shards[:1] + sum(to_others(up_shards))).reshape(pairs, ranks, LANES)
     for i in reversed(range(bits - 2)):
         gathered = jnp.concatenate([gathered, swap(gathered, 1 << i)], axis=0)
@@ -248,11 +246,12 @@
 
     low_spec = pl.BlockSpec((devs // LOW, toks, videos * ranks), lambda p: (0, 0, 0))
     part_spec = pl.BlockSpec((devs, pl.squeezed, toks, width), lambda p: (0, p, 0, 0))
+    later_spec = pl.BlockSpec((devs, pl.squeezed, toks, width), lambda p: (0, pairs + p, 0, 0))
     mixed = pl.pallas_call(
         functools.partial(attend_kernel, per_video, math.gcd(devs, max(1, 512 // toks))),
         grid=(pairs,),
         in_specs=[SMEM, pl.BlockSpec((pl.squeezed, ranks, LANES), lambda p: (p, 0, 0))]
-        + [part_spec] * 3
+        + [later_spec, part_spec, part_spec]
         + [low_spec] * LOW,
         out_specs=part_spec,
         out_shape=jax.ShapeDtypeStruct((devs, pairs, toks, width), jnp.bfloat16),
@@ -267,7 +266,7 @@
             transcendentals=pairs * length * length,
         ),
         name="attend",
-    )(me, up_here, asked, keys, vals, *lows)
+    )(me, up_here, asked, keys, asked, *lows)
     return exchange(mixed).reshape(videos, heads, toks, width)
 
 

time: 170 us -> 162 us (0.953)
  starting transfers between devices: 49.3 us -> 41.2 us
  waiting for transfers between devices: 73.5 us -> 67.4 us
  local copies, waits for them, and re-layouts: 5.61 us -> 8.87 us
  other arithmetic: 0.91 us -> 3.49 us
    all_to_all x3 -> x2, starting transfers between devices: 19.7 us -> 13.5 us  [exchange(): lax.all_to_all(tensor, 'seq', split_axis=0, concat_axis=0, tiled=True)]
    ppermute x21, waiting for transfers between devices: 69.9 us -> 63.8 us  [swap(): return lax.ppermute(tensor, 'seq', [(i, i ^ k) for i in range(devs)])]
    unnamed x19 -> x33, local copies, waits for them, and re-layouts: 4.69 us -> 7.95 us
    ppermute x21, starting transfers between devices: 29.7 us -> 27.6 us  [swap(): return lax.ppermute(tensor, 'seq', [(i, i ^ k) for i in range(devs)])]
    all_to_all x3 -> x2, waiting for transfers between devices: 3.65 us -> 3.63 us  [exchange(): lax.all_to_all(tensor, 'seq', split_axis=0, concat_axis=0, tiled=True)]
  transfers between devices with their start and end apart: 24 -> 23, of which waited for: 13 -> 12; matrix products, arithmetic and copies ran while one was open for 2% -> 6% of each run, Pallas kernels for 1% -> 1%
where the time goes in v12:
time: 162 us; the launch traced here: 161 us
  waiting for transfers between devices  67.4 us (42%)
  starting transfers between devices  41.2 us (25%)
  blocking collectives  28.7 us (18%)
  Pallas kernels  11.5 us (7%)
  local copies, waits for them, and re-layouts  8.87 us (5%)
  other arithmetic  3.49 us (2%)
    ppermute x21, waiting for transfers between devices, swap(): return lax.ppermute(tensor, 'seq', [(i, i ^ k) for i in range(devs)])  63.8 us
    all_to_all x1, blocking collectives, exchange(): lax.all_to_all(tensor, 'seq', split_axis=0, concat_axis=0, tiled=True)  28.7 us
    ppermute x21, starting transfers between devices, swap(): return lax.ppermute(tensor, 'seq', [(i, i ^ k) for i in range(devs)])  27.6 us
    all_to_all x2, starting transfers between devices, exchange(): lax.all_to_all(tensor, 'seq', split_axis=0, concat_axis=0, tiled=True)  13.5 us
    pallas_call x1, Pallas kernels, body(): pl.pallas_call(functools.partial(attend_kernel, per_video, math.gcd(devs,...  9.12 us
    unnamed x33, local copies, waits for them, and re-layouts  7.95 us
    all_to_all x2, waiting for transfers between devices, exchange(): lax.all_to_all(tensor, 'seq', split_axis=0, concat_axis=0, tiled=True)  3.63 us
  transfers between devices with their start and end apart: 23, of which 12 were waited for; matrix products, arithmetic and copies ran while one was open for 6% of the time, Pallas kernels for 1%

profile of v12, /device:TPU:1, one launch (start us, length us, event | category | flops | bytes accessed | tf_op | source)
XLA Modules:
  0.0 161.4 jit_solution(7805752672793394614)
XLA Ops:
  0.0 7.5 %all-to-all-start = ((bf16[16,4,64,128]{3,2,1,0:T(8,128)(2,1)}), bf16[16,4,64,128]{3,2,1,0:T(8,128)(2,1)S(1)}, u32[]{:S(2)}, u32[]{:S(2)}) async-start(bf16[16,4,64,128]{3,2,1,0:T(8,128)(2,1)} %bitcast.13), calls=%async_computation | async-start | bytes 2097152 | tf_op jit(solution)/shard_map/all_to_all | solution.py:163
  7.5 1.7 %copy-done = bf16[4,64,5120]{2,1,0:T(8,128)(2,1)S(1)} copy-done((bf16[4,64,5120]{2,1,0:T(8,128)(2,1)S(1)}, bf16[4,64,5120]{2,1,0:T(8,128)(2,1)}, u32[]{:S(2)}) %copy-start) | copy-done | bytes 2621464
  9.3 1.5 pick_factors.1
  10.8 0.2 collective-permute-start
  11.0 2.0 %collective-permute-done = bf16[8,320,128]{2,1,0:T(8,128)(2,1)S(1)} collective-permute-done((bf16[8,320,128]{2,1,0:T(8,128)(2,1)S(1)}, bf16[8,320,128]{2,1,0:T(8,128)(2,1)S(1)}, u32[]{:S(2)}, u32[]{:S(2)}) %collective-permute-start) | collective-permute-done | bytes 655392 | tf_op jit(solution)/shard_map/ppermute | solution.py:160
  13.0 1.5 collective-permute-start.2
  14.5 0.6 collective-permute-start.1
  15.1 11.8 %collective-permute-done.2 = bf16[4,320,128]{2,1,0:T(8,128)(2,1)S(1)} collective-permute-done((bf16[4,320,128]{2,1,0:T(8,128)(2,1)S(1)}, bf16[4,320,128]{2,1,0:T(8,128)(2,1)S(1)}, u32[]{:S(2)}, u32[]{:S(2)}) %collective-permute-start.2) | collective-permute-done | bytes 327712 | tf_op jit(solution)/shard_map/ppermute | solution.py:160
  27.0 3.6 %all-to-all-done.k_ref = bf16[16,4,64,128]{3,2,1,0:T(8,128)(2,1)S(1)} async-done(((bf16[16,4,64,128]{3,2,1,0:T(8,128)(2,1)}), bf16[16,4,64,128]{3,2,1,0:T(8,128)(2,1)S(1)}, u32[]{:S(2)}, u32[]{:S(2)}) %all-to-all-start) | async-done | bytes 1048608 | tf_op jit(solution)/shard_map/all_to_all | solution.py:163
  30.7 3.9 %collective-permute-start.4 = (bf16[1,320,128]{2,1,0:T(8,128)(2,1)S(1)}, bf16[1,320,128]{2,1,0:T(8,128)(2,1)S(1)}, u32[]{:S(2)}, u32[]{:S(2)}) collective-permute-start(bf16[1,320,128]{2,1,0:T(8,128)(2,1)S(1)} %get-tuple-element.35), channel_id=1, source_target_pairs={{0,8},{1,9},{2,10},{3,11},{4,12},{5,13},{6,14},{7,15},{8,0},{9,1},... | collective-permute-start | bytes 245768 | tf_op jit(solution)/shard_map/ppermute | solution.py:160
  34.5 1.4 collective-permute-start.6
  35.9 1.3 collective-permute-start.3
  37.2 0.9 collective-permute-done.5
  38.1 4.2 %collective-permute-done.6 = bf16[1,320,128]{2,1,0:T(8,128)(2,1)S(1)} collective-permute-done((bf16[1,320,128]{2,1,0:T(8,128)(2,1)S(1)}, bf16[1,320,128]{2,1,0:T(8,128)(2,1)S(1)}, u32[]{:S(2)}, u32[]{:S(2)}) %collective-permute-start.6) | collective-permute-done | bytes 81952 | tf_op jit(solution)/shard_map/ppermute | solution.py:160
  42.3 0.7 constant_dynamic-update-slice_fusion.4
  43.0 0.6 collective-permute-start.8
  43.6 2.9 %collective-permute-start.9 = (bf16[1,320,128]{2,1,0:T(8,128)(2,1)S(1)}, bf16[1,320,128]{2,1,0:T(8,128)(2,1)S(1)}, u32[]{:S(2)}, u32[]{:S(2)}) collective-permute-start(bf16[1,320,128]{2,1,0:T(8,128)(2,1)S(1)} %get-tuple-element.30), channel_id=1, source_target_pairs={{0,12},{1,13},{2,14},{3,15},{4,8},{5,9},{6,10},{7,11},{8,4},{9,5},... | collective-permute-start | bytes 245768 | tf_op jit(solution)/shard_map/ppermute | solution.py:160
  46.5 1.5 pad_maximum_fusion
  48.1 2.6 %collective-permute-done.9 = bf16[1,320,128]{2,1,0:T(8,128)(2,1)S(1)} collective-permute-done((bf16[1,320,128]{2,1,0:T(8,128)(2,1)S(1)}, bf16[1,320,128]{2,1,0:T(8,128)(2,1)S(1)}, u32[]{:S(2)}, u32[]{:S(2)}) %collective-permute-start.9) | collective-permute-done | bytes 81952 | tf_op jit(solution)/shard_map/ppermute | solution.py:160
  50.8 0.6 copy-done.11
  51.4 6.0 %all-to-all-start.1 = ((bf16[16,8,64,128]{3,2,1,0:T(8,128)(2,1)}), bf16[16,8,64,128]{3,2,1,0:T(8,128)(2,1)S(1)}, u32[]{:S(2)}, u32[]{:S(2)}) async-start(bf16[16,8,64,128]{3,2,1,0:T(8,128)(2,1)} %pad_maximum_fusion), calls=%async_computation.1 | async-start | bytes 4194304 | tf_op jit(solution)/shard_map/all_to_all | solution.py:163
  57.4 1.5 collective-permute-start.13
  58.9 1.5 constant_dynamic-update-slice_fusion.3
  60.4 1.5 constant_dynamic-update-slice_fusion.2
  62.0 1.5 constant_dynamic-update-slice_fusion.1
  63.5 19.7 %collective-permute-done.13 = bf16[4,320,128]{2,1,0:T(8,128)(2,1)S(1)} collective-permute-done((bf16[4,320,128]{2,1,0:T(8,128)(2,1)S(1)}, bf16[4,320,128]{2,1,0:T(8,128)(2,1)S(1)}, u32[]{:S(2)}, u32[]{:S(2)}) %collective-permute-start.13) | collective-permute-done | bytes 327712 | tf_op jit(solution)/shard_map/ppermute | solution.py:160
  83.2 0.8 constant_dynamic-update-slice_fusion
  84.0 1.2 collective-permute-start.14
  85.2 1.1 fusion.1
  86.3 0.1 collective-permute-start.10
  86.4 3.4 %collective-permute-start.11 = (bf16[1,256,128]{2,1,0:T(8,128)(2,1)S(1)}, bf16[1,256,128]{2,1,0:T(8,128)(2,1)S(1)}, u32[]{:S(2)}, u32[]{:S(2)}) collective-permute-start(bf16[1,256,128]{2,1,0:T(8,128)(2,1)S(1)} %get-tuple-element.36), channel_id=1, source_target_pairs={{0,4},{1,5},{2,6},{3,7},{4,0},{5,1},{6,2},{7,3},{8,12},{9,13},{10,... | collective-permute-start | bytes 196616 | tf_op jit(solution)/shard_map/ppermute | solution.py:160
  89.8 0.2 collective-permute-start.12
  89.9 0.1 constant_dynamic-update-slice_fusion.5.g_ref
  90.0 0.9 low_rank.1
  90.9 0.3 collective-permute-start.15
  91.2 3.2 %collective-permute-start.16 = (bf16[64,128]{1,0:T(8,128)(2,1)S(1)}, bf16[64,128]{1,0:T(8,128)(2,1)S(1)}, u32[]{:S(2)}, u32[]{:S(2)}) collective-permute-start(bf16[64,128]{1,0:T(8,128)(2,1)S(1)} %low_rank.1), channel_id=1, source_target_pairs={{0,8},{1,9},{2,10},{3,11},{4,12},{5,13},{6,14},{7,15},{8,0},{9,1},... | collective-permute-start | bytes 49160 | tf_op jit(solution)/shard_map/ppermute | solution.py:160
  94.4 15.9 %collective-permute-done.10 = bf16[1,256,128]{2,1,0:T(8,128)(2,1)S(1)} collective-permute-done((bf16[1,256,128]{2,1,0:T(8,128)(2,1)S(1)}, bf16[1,256,128]{2,1,0:T(8,128)(2,1)S(1)}, u32[]{:S(2)}, u32[]{:S(2)}) %collective-permute-start.10) | collective-permute-done | bytes 65568 | tf_op jit(solution)/shard_map/ppermute | solution.py:160
  110.2 1.3 collective-permute-start.17
  111.6 0.1 collective-permute-done.16
  111.7 2.9 %collective-permute-done.17 = bf16[64,128]{1,0:T(8,128)(2,1)S(1)} collective-permute-done((bf16[64,128]{1,0:T(8,128)(2,1)S(1)}, bf16[64,128]{1,0:T(8,128)(2,1)S(1)}, u32[]{:S(2)}, u32[]{:S(2)}) %collective-permute-start.17) | collective-permute-done | bytes 16416 | tf_op jit(solution)/shard_map/ppermute | solution.py:160
  114.6 2.6 %collective-permute-start.18 = (bf16[4,64,128]{2,1,0:T(8,128)(2,1)S(1)}, bf16[4,64,128]{2,1,0:T(8,128)(2,1)S(1)}, u32[]{:S(2)}, u32[]{:S(2)}) collective-permute-start(bf16[4,64,128]{2,1,0:T(8,128)(2,1)S(1)} %pad_maximum_fusion.2.refs_0_), channel_id=1, source_target_pairs={{0,1},{1,0},{2,3},{3,2},{4,5},{5,4},{6,7},{7,6},{8,9},{9,8},{10,11... | collective-permute-start | bytes 196616 | tf_op jit(solution)/shard_map/ppermute | solution.py:160
  117.2 1.3 collective-permute-start.19
  118.5 0.4 collective-permute-start.20
  118.9 2.0 %collective-permute-done.19.refs_2_ = bf16[4,64,128]{2,1,0:T(8,128)(2,1)S(1)} collective-permute-done((bf16[4,64,128]{2,1,0:T(8,128)(2,1)S(1)}, bf16[4,64,128]{2,1,0:T(8,128)(2,1)S(1)}, u32[]{:S(2)}, u32[]{:S(2)}) %collective-permute-start.19) | collective-permute-done | bytes 65568 | tf_op jit(solution)/shard_map/ppermute | solution.py:160
  120.9 1.7 %collective-permute-done.20.refs_3_ = bf16[4,64,128]{2,1,0:T(8,128)(2,1)S(1)} collective-permute-done((bf16[4,64,128]{2,1,0:T(8,128)(2,1)S(1)}, bf16[4,64,128]{2,1,0:T(8,128)(2,1)S(1)}, u32[]{:S(2)}, u32[]{:S(2)}) %collective-permute-start.20) | collective-permute-done | bytes 65568 | tf_op jit(solution)/shard_map/ppermute | solution.py:160
  122.6 9.1 %attend.1 = bf16[16,4,64,128]{3,2,1,0:T(8,128)(2,1)S(1)} custom-call(s32[1]{0:T(128)} %bitcast.me_ref, bf16[4,64,128]{2,1,0:T(8,128)(2,1)S(1)} %bitcast.11, bf16[16,8,64,128]{3,2,1,0:T(8,128)(2,1)S(1)} %all-to-all-done.1.q_ref.v_ref, bf16[16,4,64,128]{3,2,1,0:T(8,128)(2,1)S(1)} %all-to-all-done.k_ref, ...), custom_call_target="tpu_custom_call" | custom-call | flops 2147483648 | bytes 4194304 | tf_op jit(solution)/shard_map/attend/pallas_call | solution.py:250
  131.7 28.7 %all_to_all.15 = bf16[16,4,64,128]{3,2,1,0:T(8,128)(2,1)S(1)} all-to-all(bf16[16,4,64,128]{3,2,1,0:T(8,128)(2,1)S(1)} %attend.1), channel_id=1, replica_groups=mesh['grp'=2,'seq'=16] {'seq'}, dimensions={0} | all-to-all | bytes 2097152 | tf_op jit(solution)/shard_map/all_to_all | solution.py:163
  160.4 1.0 copy.19
  (48 shorter events, 0.3 us)
Async XLA Ops:
  0.0 7.5 %copy-start.1 = (bf16[4,64,4096]{2,1,0:T(8,128)(2,1)S(1)}, bf16[4,64,4096]{2,1,0:T(8,128)(2,1)}, u32[]{:S(2)}) copy-start(bf16[4,64,4096]{2,1,0:T(8,128)(2,1)} %up_ref.1) | copy-start | bytes 6291460
  0.0 7.5 %copy-start.5 = (s32[64]{0:T(128)S(1)}, s32[64]{0:T(128)}, u32[]{:S(2)}) copy-start(s32[64]{0:T(128)} %row_ref.1) | copy-start | bytes 772
  0.0 7.5 %copy-start.6 = (s32[2]{0:T(128)S(1)}, s32[2]{0:T(128)}, u32[]{:S(2)}) copy-start(s32[2]{0:T(128)} %req_ref.1) | copy-start | bytes 28
  0.0 30.6 %all-to-all-start = ((bf16[16,4,64,128]{3,2,1,0:T(8,128)(2,1)}), bf16[16,4,64,128]{3,2,1,0:T(8,128)(2,1)S(1)}, u32[]{:S(2)}, u32[]{:S(2)}) async-start(bf16[16,4,64,128]{3,2,1,0:T(8,128)(2,1)} %bitcast.13), calls=%async_computation | async-start | bytes 2097152 | tf_op jit(solution)/shard_map/all_to_all | solution.py:163
  7.5 1.7 %copy-start = (bf16[4,64,5120]{2,1,0:T(8,128)(2,1)S(1)}, bf16[4,64,5120]{2,1,0:T(8,128)(2,1)}, u32[]{:S(2)}) copy-start(bf16[4,64,5120]{2,1,0:T(8,128)(2,1)} %down_ref.1) | copy-start | bytes 7864324
  10.8 16.2 %copy-start.3 = (bf16[4,256,128]{2,1,0:T(8,128)(2,1)}, bf16[4,256,128]{2,1,0:T(8,128)(2,1)S(1)}, u32[]{:S(2)}) copy-start(bf16[4,256,128]{2,1,0:T(8,128)(2,1)S(1)} %get-tuple-element.17) | copy-start | bytes 786436
  10.8 2.2 %collective-permute-start = (bf16[8,320,128]{2,1,0:T(8,128)(2,1)S(1)}, bf16[8,320,128]{2,1,0:T(8,128)(2,1)S(1)}, u32[]{:S(2)}, u32[]{:S(2)}) collective-permute-start(bf16[8,320,128]{2,1,0:T(8,128)(2,1)S(1)} %get-tuple-element.20), channel_id=1, source_target_pairs={{0,1},{1,0},{2,3},{3,2},{4,5},{5,4},{6,7},{7,6},{8,9},{9,8},{10,11... | collective-permute-start | bytes 1966088 | tf_op jit(solution)/shard_map/ppermute | solution.py:160
  13.0 13.9 %collective-permute-start.2 = (bf16[4,320,128]{2,1,0:T(8,128)(2,1)S(1)}, bf16[4,320,128]{2,1,0:T(8,128)(2,1)S(1)}, u32[]{:S(2)}, u32[]{:S(2)}) collective-permute-start(bf16[4,320,128]{2,1,0:T(8,128)(2,1)S(1)} %slice_add_fusion.1), channel_id=1, source_target_pairs={{0,2},{1,3},{2,0},{3,1},{4,6},{5,7},{6,4},{7,5},{8,10},{9,11},{10,... | collective-permute-start | bytes 983048 | tf_op jit(solution)/shard_map/ppermute | solution.py:160
  14.5 12.5 %collective-permute-start.1 = (bf16[8,256,128]{2,1,0:T(8,128)(2,1)S(1)}, bf16[8,256,128]{2,1,0:T(8,128)(2,1)S(1)}, u32[]{:S(2)}, u32[]{:S(2)}) collective-permute-start(bf16[8,256,128]{2,1,0:T(8,128)(2,1)S(1)} %get-tuple-element.21), channel_id=1, source_target_pairs={{0,1},{1,0},{2,3},{3,2},{4,5},{5,4},{6,7},{7,6},{8,9},{9,8},{10,11... | collective-permute-start | bytes 1572872 | tf_op jit(solution)/shard_map/ppermute | solution.py:160
  26.9 19.6 %copy-start.7 = (bf16[2,32,64,128]{3,2,1,0:T(8,128)(2,1)S(1)}, bf16[2,32,64,128]{3,2,1,0:T(8,128)(2,1)}, u32[]{:S(2)}) copy-start(bf16[2,32,64,128]{3,2,1,0:T(8,128)(2,1)} %param.9) | copy-start | bytes 3145732
  27.0 11.1 %copy-start.9 = (bf16[8,256,128]{2,1,0:T(8,128)(2,1)}, bf16[8,256,128]{2,1,0:T(8,128)(2,1)S(1)}, u32[]{:S(2)}) copy-start(bf16[8,256,128]{2,1,0:T(8,128)(2,1)S(1)} %collective-permute-done.1) | copy-start | bytes 1572868
  30.6 15.9 %copy-start.8 = (bf16[2,32,64,128]{3,2,1,0:T(8,128)(2,1)S(1)}, bf16[2,32,64,128]{3,2,1,0:T(8,128)(2,1)}, u32[]{:S(2)}) copy-start(bf16[2,32,64,128]{3,2,1,0:T(8,128)(2,1)} %param.11) | copy-start | bytes 3145732
  30.7 6.6 %collective-permute-start.4 = (bf16[1,320,128]{2,1,0:T(8,128)(2,1)S(1)}, bf16[1,320,128]{2,1,0:T(8,128)(2,1)S(1)}, u32[]{:S(2)}, u32[]{:S(2)}) collective-permute-start(bf16[1,320,128]{2,1,0:T(8,128)(2,1)S(1)} %get-tuple-element.35), channel_id=1, source_target_pairs={{0,8},{1,9},{2,10},{3,11},{4,12},{5,13},{6,14},{7,15},{8,0},{9,1},... | collective-permute-start | bytes 245768 | tf_op jit(solution)/shard_map/ppermute | solution.py:160
  34.5 3.6 %collective-permute-start.5 = (bf16[1,320,128]{2,1,0:T(8,128)(2,1)S(1)}, bf16[1,320,128]{2,1,0:T(8,128)(2,1)S(1)}, u32[]{:S(2)}, u32[]{:S(2)}) collective-permute-start(bf16[1,320,128]{2,1,0:T(8,128)(2,1)S(1)} %get-tuple-element.33), channel_id=1, source_target_pairs={{0,4},{1,5},{2,6},{3,7},{4,0},{5,1},{6,2},{7,3},{8,12},{9,13},{10,... | collective-permute-start | bytes 245768 | tf_op jit(solution)/shard_map/ppermute | solution.py:160
  34.5 7.7 %collective-permute-start.6 = (bf16[1,320,128]{2,1,0:T(8,128)(2,1)S(1)}, bf16[1,320,128]{2,1,0:T(8,128)(2,1)S(1)}, u32[]{:S(2)}, u32[]{:S(2)}) collective-permute-start(bf16[1,320,128]{2,1,0:T(8,128)(2,1)S(1)} %get-tuple-element.34), channel_id=1, source_target_pairs={{0,12},{1,13},{2,14},{3,15},{4,8},{5,9},{6,10},{7,11},{8,4},{9,5},... | collective-permute-start | bytes 245768 | tf_op jit(solution)/shard_map/ppermute | solution.py:160
  35.9 14.8 %collective-permute-start.3 = (bf16[4,256,128]{2,1,0:T(8,128)(2,1)S(1)}, bf16[4,256,128]{2,1,0:T(8,128)(2,1)}, u32[]{:S(2)}, u32[]{:S(2)}) collective-permute-start(bf16[4,256,128]{2,1,0:T(8,128)(2,1)S(1)} %slice_add_fusion.2), channel_id=1, source_target_pairs={{0,2},{1,3},{2,0},{3,1},{4,6},{5,7},{6,4},{7,5},{8,10},{9,11},{10,... | collective-permute-start | bytes 786440 | tf_op jit(solution)/shard_map/ppermute | solution.py:160
  43.0 5.1 %collective-permute-start.7 = (bf16[1,320,128]{2,1,0:T(8,128)(2,1)S(1)}, bf16[1,320,128]{2,1,0:T(8,128)(2,1)S(1)}, u32[]{:S(2)}, u32[]{:S(2)}) collective-permute-start(bf16[1,320,128]{2,1,0:T(8,128)(2,1)S(1)} %get-tuple-element.30), channel_id=1, source_target_pairs={{0,8},{1,9},{2,10},{3,11},{4,12},{5,13},{6,14},{7,15},{8,0},{9,1},... | collective-permute-start | bytes 245768 | tf_op jit(solution)/shard_map/ppermute | solution.py:160
  43.0 5.1 %collective-permute-start.8 = (bf16[1,320,128]{2,1,0:T(8,128)(2,1)S(1)}, bf16[1,320,128]{2,1,0:T(8,128)(2,1)S(1)}, u32[]{:S(2)}, u32[]{:S(2)}) collective-permute-start(bf16[1,320,128]{2,1,0:T(8,128)(2,1)S(1)} %get-tuple-element.30), channel_id=1, source_target_pairs={{0,4},{1,5},{2,6},{3,7},{4,0},{5,1},{6,2},{7,3},{8,12},{9,13},{10,... | collective-permute-start | bytes 245768 | tf_op jit(solution)/shard_map/ppermute | solution.py:160
  43.6 7.1 %collective-permute-start.9 = (bf16[1,320,128]{2,1,0:T(8,128)(2,1)S(1)}, bf16[1,320,128]{2,1,0:T(8,128)(2,1)S(1)}, u32[]{:S(2)}, u32[]{:S(2)}) collective-permute-start(bf16[1,320,128]{2,1,0:T(8,128)(2,1)S(1)} %get-tuple-element.30), channel_id=1, source_target_pairs={{0,12},{1,13},{2,14},{3,15},{4,8},{5,9},{6,10},{7,11},{8,4},{9,5},... | collective-permute-start | bytes 245768 | tf_op jit(solution)/shard_map/ppermute | solution.py:160
  48.1 2.7 %copy-start.13 = (bf16[1,320,128]{2,1,0:T(8,128)(2,1)}, bf16[1,320,128]{2,1,0:T(8,128)(2,1)S(1)}, u32[]{:S(2)}) copy-start(bf16[1,320,128]{2,1,0:T(8,128)(2,1)S(1)} %collective-permute-done.7) | copy-start | bytes 245764
  48.1 2.7 %copy-start.12 = (bf16[1,320,128]{2,1,0:T(8,128)(2,1)}, bf16[1,320,128]{2,1,0:T(8,128)(2,1)S(1)}, u32[]{:S(2)}) copy-start(bf16[1,320,128]{2,1,0:T(8,128)(2,1)S(1)} %collective-permute-done.8) | copy-start | bytes 245764
  50.7 0.6 copy-start.11
  51.4 71.2 %all-to-all-start.1 = ((bf16[16,8,64,128]{3,2,1,0:T(8,128)(2,1)}), bf16[16,8,64,128]{3,2,1,0:T(8,128)(2,1)S(1)}, u32[]{:S(2)}, u32[]{:S(2)}) async-start(bf16[16,8,64,128]{3,2,1,0:T(8,128)(2,1)} %pad_maximum_fusion), calls=%async_computation.1 | async-start | bytes 4194304 | tf_op jit(solution)/shard_map/all_to_all | solution.py:163
  57.4 27.8 %copy-start.4 = (bf16[4,256,128]{2,1,0:T(8,128)(2,1)S(1)}, bf16[4,256,128]{2,1,0:T(8,128)(2,1)}, u32[]{:S(2)}) copy-start(bf16[4,256,128]{2,1,0:T(8,128)(2,1)} %copy-done.3) | copy-start | bytes 786436
  57.4 27.8 %copy-start.10 = (bf16[8,256,128]{2,1,0:T(8,128)(2,1)S(1)}, bf16[8,256,128]{2,1,0:T(8,128)(2,1)}, u32[]{:S(2)}) copy-start(bf16[8,256,128]{2,1,0:T(8,128)(2,1)} %copy-done.9) | copy-start | bytes 1572868
  57.4 25.7 %collective-permute-start.13 = (bf16[4,320,128]{2,1,0:T(8,128)(2,1)S(1)}, bf16[4,320,128]{2,1,0:T(8,128)(2,1)S(1)}, u32[]{:S(2)}, u32[]{:S(2)}) collective-permute-start(bf16[4,320,128]{2,1,0:T(8,128)(2,1)S(1)} %pad_maximum_fusion.1), channel_id=1, source_target_pairs={{0,2},{1,3},{2,0},{3,1},{4,6},{5,7},{6,4},{7,5},{8,10},{9,11},{10,... | collective-permute-start | bytes 983048 | tf_op jit(solution)/shard_map/ppermute | solution.py:160
  84.0 6.0 %collective-permute-start.14 = (bf16[8,320,128]{2,1,0:T(8,128)(2,1)}, bf16[8,320,128]{2,1,0:T(8,128)(2,1)S(1)}, u32[]{:S(2)}, u32[]{:S(2)}) collective-permute-start(bf16[8,320,128]{2,1,0:T(8,128)(2,1)} %get-tuple-element.31), channel_id=1, source_target_pairs={{0,1},{1,0},{2,3},{3,2},{4,5},{5,4},{6,7},{7,6},{8,9},{9,8},{10,11... | collective-permute-start | bytes 1966088 | tf_op jit(solution)/shard_map/ppermute | solution.py:160
  85.2 4.8 %copy-start.2 = (bf16[2,64,5120]{2,1,0:T(8,128)(2,1)S(1)}, bf16[2,64,5120]{2,1,0:T(8,128)(2,1)}, u32[]{:S(2)}) copy-start(bf16[2,64,5120]{2,1,0:T(8,128)(2,1)} %x_ref.1) | copy-start | bytes 3932164
  86.3 23.9 %collective-permute-start.10 = (bf16[1,256,128]{2,1,0:T(8,128)(2,1)S(1)}, bf16[1,256,128]{2,1,0:T(8,128)(2,1)S(1)}, u32[]{:S(2)}, u32[]{:S(2)}) collective-permute-start(bf16[1,256,128]{2,1,0:T(8,128)(2,1)S(1)} %get-tuple-element.38), channel_id=1, source_target_pairs={{0,8},{1,9},{2,10},{3,11},{4,12},{5,13},{6,14},{7,15},{8,0},{9,1},... | collective-permute-start | bytes 196616 | tf_op jit(solution)/shard_map/ppermute | solution.py:160
  86.4 25.1 %collective-permute-start.11 = (bf16[1,256,128]{2,1,0:T(8,128)(2,1)S(1)}, bf16[1,256,128]{2,1,0:T(8,128)(2,1)S(1)}, u32[]{:S(2)}, u32[]{:S(2)}) collective-permute-start(bf16[1,256,128]{2,1,0:T(8,128)(2,1)S(1)} %get-tuple-element.36), channel_id=1, source_target_pairs={{0,4},{1,5},{2,6},{3,7},{4,0},{5,1},{6,2},{7,3},{8,12},{9,13},{10,... | collective-permute-start | bytes 196616 | tf_op jit(solution)/shard_map/ppermute | solution.py:160
  89.8 21.8 %collective-permute-start.12 = (bf16[1,256,128]{2,1,0:T(8,128)(2,1)S(1)}, bf16[1,256,128]{2,1,0:T(8,128)(2,1)S(1)}, u32[]{:S(2)}, u32[]{:S(2)}) collective-permute-start(bf16[1,256,128]{2,1,0:T(8,128)(2,1)S(1)} %get-tuple-element.37), channel_id=1, source_target_pairs={{0,12},{1,13},{2,14},{3,15},{4,8},{5,9},{6,10},{7,11},{8,4},{9,5},... | collective-permute-start | bytes 196616 | tf_op jit(solution)/shard_map/ppermute | solution.py:160
  90.9 20.7 %collective-permute-start.15 = (bf16[64,128]{1,0:T(8,128)(2,1)S(1)}, bf16[64,128]{1,0:T(8,128)(2,1)S(1)}, u32[]{:S(2)}, u32[]{:S(2)}) collective-permute-start(bf16[64,128]{1,0:T(8,128)(2,1)S(1)} %low_rank.1), channel_id=1, source_target_pairs={{0,4},{1,5},{2,6},{3,7},{4,0},{5,1},{6,2},{7,3},{8,12},{9,13},{10,... | collective-permute-start | bytes 49160 | tf_op jit(solution)/shard_map/ppermute | solution.py:160
  91.2 20.5 %collective-permute-start.16 = (bf16[64,128]{1,0:T(8,128)(2,1)S(1)}, bf16[64,128]{1,0:T(8,128)(2,1)S(1)}, u32[]{:S(2)}, u32[]{:S(2)}) collective-permute-start(bf16[64,128]{1,0:T(8,128)(2,1)S(1)} %low_rank.1), channel_id=1, source_target_pairs={{0,8},{1,9},{2,10},{3,11},{4,12},{5,13},{6,14},{7,15},{8,0},{9,1},... | collective-permute-start | bytes 49160 | tf_op jit(solution)/shard_map/ppermute | solution.py:160
  110.2 4.4 %collective-permute-start.17 = (bf16[64,128]{1,0:T(8,128)(2,1)S(1)}, bf16[64,128]{1,0:T(8,128)(2,1)S(1)}, u32[]{:S(2)}, u32[]{:S(2)}) collective-permute-start(bf16[64,128]{1,0:T(8,128)(2,1)S(1)} %low_rank.1), channel_id=1, source_target_pairs={{0,12},{1,13},{2,14},{3,15},{4,8},{5,9},{6,10},{7,11},{8,4},{9,5},... | collective-permute-start | bytes 49160 | tf_op jit(solution)/shard_map/ppermute | solution.py:160
  114.6 4.3 %collective-permute-start.18 = (bf16[4,64,128]{2,1,0:T(8,128)(2,1)S(1)}, bf16[4,64,128]{2,1,0:T(8,128)(2,1)S(1)}, u32[]{:S(2)}, u32[]{:S(2)}) collective-permute-start(bf16[4,64,128]{2,1,0:T(8,128)(2,1)S(1)} %pad_maximum_fusion.2.refs_0_), channel_id=1, source_target_pairs={{0,1},{1,0},{2,3},{3,2},{4,5},{5,4},{6,7},{7,6},{8,9},{9,8},{10,11... | collective-permute-start | bytes 196616 | tf_op jit(solution)/shard_map/ppermute | solution.py:160
  117.2 3.7 %collective-permute-start.19 = (bf16[4,64,128]{2,1,0:T(8,128)(2,1)S(1)}, bf16[4,64,128]{2,1,0:T(8,128)(2,1)S(1)}, u32[]{:S(2)}, u32[]{:S(2)}) collective-permute-start(bf16[4,64,128]{2,1,0:T(8,128)(2,1)S(1)} %pad_maximum_fusion.2.refs_0_), channel_id=1, source_target_pairs={{0,2},{1,3},{2,0},{3,1},{4,6},{5,7},{6,4},{7,5},{8,10},{9,11},{10,... | collective-permute-start | bytes 196616 | tf_op jit(solution)/shard_map/ppermute | solution.py:160
  118.5 4.0 %collective-permute-start.20 = (bf16[4,64,128]{2,1,0:T(8,128)(2,1)S(1)}, bf16[4,64,128]{2,1,0:T(8,128)(2,1)S(1)}, u32[]{:S(2)}, u32[]{:S(2)}) collective-permute-start(bf16[4,64,128]{2,1,0:T(8,128)(2,1)S(1)} %pad_maximum_fusion.2.refs_0_), channel_id=1, source_target_pairs={{0,3},{1,2},{2,1},{3,0},{4,7},{5,6},{6,5},{7,4},{8,11},{9,10},{10,... | collective-permute-start | bytes 196616 | tf_op jit(solution)/shard_map/ppermute | solution.py:160

commit v13 on v6

--- a/solution.py
+++ b/solution.py
@@ -9,6 +9,7 @@
 from jax.sharding import PartitionSpec as P
 
 LANES = 128
+LOW = 4
 ANY = pl.BlockSpec(memory_space=pl.ANY)
 VMEM = pl.BlockSpec(memory_space=pltpu.VMEM)
 SMEM = pl.BlockSpec(memory_space=pltpu.SMEM)
@@ -29,8 +30,8 @@
 
 def pick_kernel(shape, me_ref, row_ref, req_ref, down_ref, up_ref, *refs):
     devs, bits, per_video, pairs, col_split, rows, tiles = shape
-    downs, ups = refs[: bits + 1], refs[bits + 1 : 2 * bits + 2]
-    down, up, sems = refs[2 * bits + 2 :]
+    downs, ups = refs[: bits - 1], refs[bits - 1 : 2 * bits - 2]
+    down, up, sems = refs[2 * bits - 2 :]
     slots, ranks, _ = down_ref.shape
     videos = down.shape[0]
     me = me_ref[0]
@@ -56,8 +57,8 @@
             up[s] = jnp.zeros(up.shape[1:], up.dtype)
 
     for j in range(devs):
-        step = bits - j.bit_length()
-        at = j - (1 << (j.bit_length() - 1)) if j else 0
+        step = min(bits - j.bit_length(), bits - 2)
+        at = j - (1 << (j.bit_length() - 1)) if j >= LOW else j
         dev = me ^ reversed_bits(j, bits)
         video = dev // per_video
         place = dev % per_video
@@ -72,17 +73,16 @@
             ups[step][at, p * ranks : (p + 1) * ranks, :] = up[video, :, pl.ds(col, LANES)]
 
 
-def low_rank_kernel(shape, x_ref, g_ref, q_ref, out_ref, down):
-    devs, _, per_video, _, col_split, rows, tiles = shape
-    for dev in range(devs):
+def low_rank_kernel(shape, me_ref, x_ref, g_ref, q_ref, out_ref, down):
+    devs, bits, per_video, _, col_split, rows, tiles = shape
+    for j in range(devs):
+        dev = me_ref[0] ^ reversed_bits(j, bits)
         video = dev // per_video
         place = dev % per_video
-        row = (place // col_split) * rows
+        row = pl.multiple_of((place // col_split) * rows, rows)
         for t in range(tiles):
-            col = ((place % col_split) * tiles + t) * LANES
-            down[video, row : row + rows, col : col + LANES] = g_ref[
-                dev, t * rows : (t + 1) * rows, :
-            ]
+            col = pl.multiple_of(((place % col_split) * tiles + t) * LANES, LANES)
+            down[video, pl.ds(row, rows), pl.ds(col, LANES)] = g_ref[j, t * rows : (t + 1) * rows, :]
     first = q_ref.shape[1]
     out_ref[:, :first] = q_ref[...]
     for s in range(x_ref.shape[0]):
@@ -167,21 +167,27 @@
     def after(array, *others):
         return lax.optimization_barrier((array, others))[0]
 
+    quarter = devs // LOW
+    others = (2 * quarter, quarter, 3 * quarter)
+
     def halving(parts, received, i):
-        h = devs >> (i + 1) if i < bits else 0
-        size = max(h, 1)
-        return sum((r[h : h + size] for r in received), parts[i])
+        size = parts[i].shape[0]
+        start = size if i < bits - 2 else 0
+        return sum((r[start : start + size] for r in received), parts[i])
+
+    def to_others(shards):
+        return [swap(shards[j + 1 : j + 2], k) for j, k in enumerate(others)]
 
     keys = exchange(by_pairs(projected_keys))
 
-    steps = [devs >> (i + 1) for i in range(bits)] + [1]
+    steps = [devs >> (i + 1) for i in range(bits - 2)] + [LOW]
     piece_shapes = [(h, tiles * rows, LANES) for h in steps] + [
         (h, pairs * ranks, LANES) for h in steps
     ]
     pieces = pl.pallas_call(
         functools.partial(pick_kernel, shape),
         in_specs=[SMEM, SMEM, SMEM, ANY, ANY],
-        out_specs=[VMEM] * (2 * bits + 2),
+        out_specs=[VMEM] * (2 * bits - 2),
         out_shape=[jax.ShapeDtypeStruct(s, jnp.bfloat16) for s in piece_shapes],
         scratch_shapes=[
             pltpu.VMEM((videos, ranks, model_width), jnp.bfloat16),
@@ -196,23 +202,31 @@
         ),
         name="pick_factors",
     )(me, adapter_store_row, requests, adapter_down_factors, adapter_up_factors)
-    down_pieces, up_pieces = pieces[: bits + 1], pieces[bits + 1 :]
+    down_pieces, up_pieces = pieces[: bits - 1], pieces[bits - 1 :]
 
     down_got, up_got = [], []
-    for i in range(bits):
+
+    def send_up(i, *others):
+        up_got.append(swap(after(halving(up_pieces, up_got, i), *others), 1 << i))
+
+    for i in range(bits - 2):
         piece = halving(down_pieces, down_got, i)
-        if i == 2:
-            piece = after(piece, keys)
+        if i > 0:
+            send_up(i - 1, piece)
         down_got.append(swap(piece, 1 << i))
-        up_got.append(swap(after(halving(up_pieces, up_got, i), piece), 1 << i))
-    shard = halving(down_pieces, down_got, bits)
-    up_here = halving(up_pieces, up_got, bits).reshape(pairs, ranks, LANES)
-    gathered = lax.all_gather(shard, "seq", axis=0, tiled=True)
-    vals = exchange(after(by_pairs(values), shard))
+    shards = after(halving(down_pieces, down_got, bits - 2), keys, *up_got)
+    send_up(bits - 3, shards)
+    shard = shards[:1] + sum(to_others(shards))
+    gathered = jnp.concatenate([shard] + [swap(shard, k) for k in others], axis=0)
+    vals = exchange(after(by_pairs(values), gathered, up_got[-1]))
+    up_shards = after(halving(up_pieces, up_got, bits - 2), gathered)
+    up_here = (up_shards[:1] + sum(to_others(up_shards))).reshape(pairs, ranks, LANES)
+    for i in reversed(range(bits - 2)):
+        gathered = jnp.concatenate([gathered, swap(gathered, 1 << i)], axis=0)
 
     asked = pl.pallas_call(
         functools.partial(low_rank_kernel, shape),
-        in_specs=[VMEM, VMEM, VMEM],
+        in_specs=[SMEM, VMEM, VMEM, VMEM],
         out_specs=VMEM,
         scratch_shapes=[pltpu.VMEM((videos, ranks, model_width), jnp.bfloat16)],
         out_shape=jax.ShapeDtypeStruct((devs, pairs * toks + toks // 2, width), jnp.bfloat16),
@@ -223,11 +237,7 @@
             transcendentals=0,
         ),
         name="low_rank",
-    )(
-        normed_token_features,
-        after(gathered, vals, up_here),
-        queries.reshape(devs, pairs * toks, width),
-    )
+    )(me, normed_token_features, gathered, queries.reshape(devs, pairs * toks, width))
     asked = exchange(asked)
 
     part_spec = pl.BlockSpec((devs, pl.squeezed, toks, width), lambda p: (0, p, 0, 0))

time: 181 us -> 164 us (0.906)
  blocking collectives: 61.8 us -> 29.5 us
  waiting for transfers between devices: 60.9 us -> 75.3 us
  between operations: 13.6 us -> 0.21 us
  starting transfers between devices: 26.5 us -> 37.4 us
  local copies, waits for them, and re-layouts: 4.07 us -> 8.51 us
    all_to_all x2 -> x1, blocking collectives: 61.8 us -> 29.5 us  [exchange(): lax.all_to_all(tensor, 'seq', split_axis=0, concat_axis=0, tiled=True)]
    ppermute x8 -> x15, waiting for transfers between devices: 45 us -> 71.6 us  [swap(): return lax.ppermute(tensor, 'seq', [(i, i ^ k) for i in range(devs)])]
    all_gather x1 -> x0, waiting for transfers between devices: 12.2 us -> none  [body(): gathered = lax.all_gather(shard, 'seq', axis=0, tiled=True)]
    ppermute x8 -> x15, starting transfers between devices: 11.6 us -> 17.4 us  [swap(): return lax.ppermute(tensor, 'seq', [(i, i ^ k) for i in range(devs)])]
    all_to_all x2 -> x3, starting transfers between devices: 14.8 us -> 19.9 us  [exchange(): lax.all_to_all(tensor, 'seq', split_axis=0, concat_axis=0, tiled=True)]
    unnamed x25 -> x29, local copies, waits for them, and re-layouts: 4.07 us -> 7.58 us
    add x8 -> x5, other arithmetic: 2.63 us -> 0.17 us  [the longest x4 0.15 us: halving(): return sum((r[start:start + size] for r in received), parts[i])]
    all_to_all x2 -> x3, waiting for transfers between devices: 3.66 us -> 3.65 us  [exchange(): lax.all_to_all(tensor, 'seq', split_axis=0, concat_axis=0, tiled=True)]
  transfers between devices with their start and end apart: 11 -> 18, of which waited for: 10 -> 11; matrix products, arithmetic and copies ran while one was open for 1% -> 2% of each run, Pallas kernels for 1% -> 2%
where the time goes in v13:
time: 164 us
  waiting for transfers between devices  75.3 us (46%)
  starting transfers between devices  37.4 us (23%)
  blocking collectives  29.5 us (18%)
  Pallas kernels  11.9 us (7%)
  local copies, waits for them, and re-layouts  8.51 us (5%)
    ppermute x15, waiting for transfers between devices, swap(): return lax.ppermute(tensor, 'seq', [(i, i ^ k) for i in range(devs)])  71.6 us
    all_to_all x1, blocking collectives, exchange(): lax.all_to_all(tensor, 'seq', split_axis=0, concat_axis=0, tiled=True)  29.5 us
    all_to_all x3, starting transfers between devices, exchange(): lax.all_to_all(tensor, 'seq', split_axis=0, concat_axis=0, tiled=True)  19.9 us
    ppermute x15, starting transfers between devices, swap(): return lax.ppermute(tensor, 'seq', [(i, i ^ k) for i in range(devs)])  17.4 us
    pallas_call x1, Pallas kernels, body(): pl.pallas_call(functools.partial(attend_kernel, math.gcd(devs, max(1, 512...  8.48 us
    unnamed x29, local copies, waits for them, and re-layouts  7.58 us
    all_to_all x3, waiting for transfers between devices, exchange(): lax.all_to_all(tensor, 'seq', split_axis=0, concat_axis=0, tiled=True)  3.65 us
  transfers between devices with their start and end apart: 18, of which 11 were waited for; matrix products, arithmetic and copies ran while one was open for 2% of the time, Pallas kernels for 2%

profile of v13, /device:TPU:1, one launch (start us, length us, event | category | flops | bytes accessed | tf_op | source)
XLA Modules:
  0.0 163.7 jit_solution(2454236448582136395)
XLA Ops:
  0.0 7.5 %all-to-all-start = ((bf16[16,4,64,128]{3,2,1,0:T(8,128)(2,1)}), bf16[16,4,64,128]{3,2,1,0:T(8,128)(2,1)S(1)}, u32[]{:S(2)}, u32[]{:S(2)}) async-start(bf16[16,4,64,128]{3,2,1,0:T(8,128)(2,1)} %bitcast.9), calls=%async_computation | async-start | bytes 2097152 | tf_op jit(solution)/shard_map/all_to_all | solution.py:162
  7.5 0.0 copy-start
  7.5 1.7 %copy-done = bf16[4,64,5120]{2,1,0:T(8,128)(2,1)S(1)} copy-done((bf16[4,64,5120]{2,1,0:T(8,128)(2,1)S(1)}, bf16[4,64,5120]{2,1,0:T(8,128)(2,1)}, u32[]{:S(2)}) %copy-start) | copy-done | bytes 2621464
  9.3 1.5 pick_factors.1
  10.8 0.2 collective-permute-start
  11.0 2.0 %collective-permute-done = bf16[8,320,128]{2,1,0:T(8,128)(2,1)S(1)} collective-permute-done((bf16[8,320,128]{2,1,0:T(8,128)(2,1)S(1)}, bf16[8,320,128]{2,1,0:T(8,128)(2,1)S(1)}, u32[]{:S(2)}, u32[]{:S(2)}) %collective-permute-start) | collective-permute-done | bytes 655392 | tf_op jit(solution)/shard_map/ppermute | solution.py:159
  13.0 1.5 collective-permute-start.2
  14.5 0.6 collective-permute-start.1
  15.1 11.8 %collective-permute-done.2 = bf16[4,320,128]{2,1,0:T(8,128)(2,1)S(1)} collective-permute-done((bf16[4,320,128]{2,1,0:T(8,128)(2,1)S(1)}, bf16[4,320,128]{2,1,0:T(8,128)(2,1)S(1)}, u32[]{:S(2)}, u32[]{:S(2)}) %collective-permute-start.2) | collective-permute-done | bytes 327712 | tf_op jit(solution)/shard_map/ppermute | solution.py:159
  27.0 0.0 collective-permute-done.1
  27.0 3.6 %all-to-all-done.k_ref = bf16[16,4,64,128]{3,2,1,0:T(8,128)(2,1)S(1)} async-done(((bf16[16,4,64,128]{3,2,1,0:T(8,128)(2,1)}), bf16[16,4,64,128]{3,2,1,0:T(8,128)(2,1)S(1)}, u32[]{:S(2)}, u32[]{:S(2)}) %all-to-all-start) | async-done | bytes 1048608 | tf_op jit(solution)/shard_map/all_to_all | solution.py:162
  30.7 3.1 %collective-permute-start.6 = (bf16[1,320,128]{2,1,0:T(8,128)(2,1)S(1)}, bf16[1,320,128]{2,1,0:T(8,128)(2,1)S(1)}, u32[]{:S(2)}, u32[]{:S(2)}) collective-permute-start(bf16[1,320,128]{2,1,0:T(8,128)(2,1)S(1)} %get-tuple-element.32), channel_id=1, source_target_pairs={{0,12},{1,13},{2,14},{3,15},{4,8},{5,9},{6,10},{7,11},{8,4},{9,5},... | collective-permute-start | bytes 245768 | tf_op jit(solution)/shard_map/ppermute | solution.py:159
  33.8 1.2 collective-permute-start.4
  35.0 0.0 collective-permute-start.5
  35.0 1.3 collective-permute-start.3
  36.4 0.3 collective-permute-done.6
  36.7 5.5 %collective-permute-done.4 = bf16[1,320,128]{2,1,0:T(8,128)(2,1)S(1)} collective-permute-done((bf16[1,320,128]{2,1,0:T(8,128)(2,1)S(1)}, bf16[1,320,128]{2,1,0:T(8,128)(2,1)S(1)}, u32[]{:S(2)}, u32[]{:S(2)}) %collective-permute-start.4) | collective-permute-done | bytes 81952 | tf_op jit(solution)/shard_map/ppermute | solution.py:159
  42.2 0.0 collective-permute-done.5
  42.2 0.7 constant_dynamic-update-slice_fusion.4
  42.9 2.7 %collective-permute-start.9 = (bf16[1,320,128]{2,1,0:T(8,128)(2,1)S(1)}, bf16[1,320,128]{2,1,0:T(8,128)(2,1)S(1)}, u32[]{:S(2)}, u32[]{:S(2)}) collective-permute-start(bf16[1,320,128]{2,1,0:T(8,128)(2,1)S(1)} %get-tuple-element.28), channel_id=1, source_target_pairs={{0,12},{1,13},{2,14},{3,15},{4,8},{5,9},{6,10},{7,11},{8,4},{9,5},... | collective-permute-start | bytes 245768 | tf_op jit(solution)/shard_map/ppermute | solution.py:159
  45.6 0.8 collective-permute-start.7
  46.4 1.5 collective-permute-done.9
  48.0 3.6 %collective-permute-done.8 = bf16[1,320,128]{2,1,0:T(8,128)(2,1)S(1)} collective-permute-done((bf16[1,320,128]{2,1,0:T(8,128)(2,1)S(1)}, bf16[1,320,128]{2,1,0:T(8,128)(2,1)S(1)}, u32[]{:S(2)}, u32[]{:S(2)}) %collective-permute-start.8) | collective-permute-done | bytes 81952 | tf_op jit(solution)/shard_map/ppermute | solution.py:159
  51.6 0.0 collective-permute-done.7
  51.6 0.0 collective-permute-done.3
  51.6 0.7 copy-done.10
  52.3 6.1 %all-to-all-start.2 = ((bf16[16,4,64,128]{3,2,1,0:T(8,128)(2,1)}), bf16[16,4,64,128]{3,2,1,0:T(8,128)(2,1)S(1)}, u32[]{:S(2)}, u32[]{:S(2)}) async-start(bf16[16,4,64,128]{3,2,1,0:T(8,128)(2,1)} %bitcast.4), calls=%async_computation.2 | async-start | bytes 2097152 | tf_op jit(solution)/shard_map/all_to_all | solution.py:162
  58.4 1.5 collective-permute-start.13
  59.9 0.7 constant_dynamic-update-slice_fusion.3
  60.5 0.7 constant_dynamic-update-slice_fusion.2
  61.2 0.7 constant_dynamic-update-slice_fusion.1
  61.8 14.4 %collective-permute-done.13 = bf16[4,320,128]{2,1,0:T(8,128)(2,1)S(1)} collective-permute-done((bf16[4,320,128]{2,1,0:T(8,128)(2,1)S(1)}, bf16[4,320,128]{2,1,0:T(8,128)(2,1)S(1)}, u32[]{:S(2)}, u32[]{:S(2)}) %collective-permute-start.13) | collective-permute-done | bytes 327712 | tf_op jit(solution)/shard_map/ppermute | solution.py:159
  76.2 0.8 constant_dynamic-update-slice_fusion
  77.0 0.9 collective-permute-start.14
  77.9 1.9 %collective-permute-done.14 = bf16[8,320,128]{2,1,0:T(8,128)(2,1)S(1)} collective-permute-done((bf16[8,320,128]{2,1,0:T(8,128)(2,1)}, bf16[8,320,128]{2,1,0:T(8,128)(2,1)S(1)}, u32[]{:S(2)}, u32[]{:S(2)}) %collective-permute-start.14) | collective-permute-done | bytes 655392 | tf_op jit(solution)/shard_map/ppermute | solution.py:159
  79.8 0.1 constant_dynamic-update-slice_fusion.5.g_ref
  79.9 1.9 %low_rank.1 = bf16[16,288,128]{2,1,0:T(8,128)(2,1)} custom-call(s32[1]{0:T(128)} %bitcast.me_ref, bf16[2,64,5120]{2,1,0:T(8,128)(2,1)S(1)} %copy-done.2, bf16[16,320,128]{2,1,0:T(8,128)(2,1)S(1)} %constant_dynamic-update-slice_fusion.5.g_ref, bf16[16,256,128]{2,1,0:T(8,128)(2,1)S(1)} %bitcast.6), custom_call_target="tpu_custom_call" | custom-call | flops 83886080 | bytes 2621440 | tf_op jit(solution)/shard_map/low_rank/pallas_call | solution.py:227
  81.9 1.0 copy-done.4
  82.9 6.4 %all-to-all-start.1 = ((bf16[16,288,128]{2,1,0:T(8,128)(2,1)}), bf16[16,288,128]{2,1,0:T(8,128)(2,1)S(1)}, u32[]{:S(2)}, u32[]{:S(2)}) async-start(bf16[16,288,128]{2,1,0:T(8,128)(2,1)} %low_rank.1), calls=%async_computation.1 | async-start | bytes 2359296 | tf_op jit(solution)/shard_map/all_to_all | solution.py:162
  89.3 3.3 %collective-permute-start.12 = (bf16[1,256,128]{2,1,0:T(8,128)(2,1)S(1)}, bf16[1,256,128]{2,1,0:T(8,128)(2,1)S(1)}, u32[]{:S(2)}, u32[]{:S(2)}) collective-permute-start(bf16[1,256,128]{2,1,0:T(8,128)(2,1)S(1)} %get-tuple-element.35), channel_id=1, source_target_pairs={{0,12},{1,13},{2,14},{3,15},{4,8},{5,9},{6,10},{7,11},{8,4},{9,5},... | collective-permute-start | bytes 196616 | tf_op jit(solution)/shard_map/ppermute | solution.py:159
  92.6 0.4 collective-permute-start.11
  93.0 20.9 %collective-permute-done.12 = bf16[1,256,128]{2,1,0:T(8,128)(2,1)S(1)} collective-permute-done((bf16[1,256,128]{2,1,0:T(8,128)(2,1)S(1)}, bf16[1,256,128]{2,1,0:T(8,128)(2,1)S(1)}, u32[]{:S(2)}, u32[]{:S(2)}) %collective-permute-start.12) | collective-permute-done | bytes 65568 | tf_op jit(solution)/shard_map/ppermute | solution.py:159
  113.9 9.6 %collective-permute-done.10 = bf16[1,256,128]{2,1,0:T(8,128)(2,1)S(1)} collective-permute-done((bf16[1,256,128]{2,1,0:T(8,128)(2,1)S(1)}, bf16[1,256,128]{2,1,0:T(8,128)(2,1)S(1)}, u32[]{:S(2)}, u32[]{:S(2)}) %collective-permute-start.10) | collective-permute-done | bytes 65568 | tf_op jit(solution)/shard_map/ppermute | solution.py:159
  123.5 0.0 copy-start.5
  123.5 1.2 copy-done.5
  124.7 8.5 %attend.1 = bf16[16,4,64,128]{3,2,1,0:T(8,128)(2,1)S(1)} custom-call(bf16[4,64,128]{2,1,0:T(8,128)(2,1)S(1)} %bitcast.7, bf16[16,288,128]{2,1,0:T(8,128)(2,1)S(1)} %all-to-all-done.1.q_ref.low_ref, bf16[16,288,128]{2,1,0:T(8,128)(2,1)S(1)} %all-to-all-done.1.q_ref.low_ref, bf16[16,4,64,128]{3,2,1,0:T(8,128)(2,1)S(1)} %all-to-all-done.k_ref, ...), custom_call_target="tpu_custom_call" | custom-call | flops 2147483648 | bytes 4194304 | tf_op jit(solution)/shard_map/attend/pallas_call | solution.py:244
  133.2 29.5 %all_to_all.20 = bf16[16,4,64,128]{3,2,1,0:T(8,128)(2,1)S(1)} all-to-all(bf16[16,4,64,128]{3,2,1,0:T(8,128)(2,1)S(1)} %attend.1), channel_id=1, replica_groups=mesh['grp'=2,'seq'=16] {'seq'}, dimensions={0} | all-to-all | bytes 2097152 | tf_op jit(solution)/shard_map/all_to_all | solution.py:162
  162.7 1.0 copy.19
  (32 shorter events, 0.3 us)
Async XLA Ops:
  0.0 7.5 %copy-start.8 = (s32[64]{0:T(128)S(1)}, s32[64]{0:T(128)}, u32[]{:S(2)}) copy-start(s32[64]{0:T(128)} %row_ref.1) | copy-start | bytes 772
  0.0 7.5 %copy-start.9 = (s32[2]{0:T(128)S(1)}, s32[2]{0:T(128)}, u32[]{:S(2)}) copy-start(s32[2]{0:T(128)} %req_ref.1) | copy-start | bytes 28
  0.0 7.5 %copy-start.1 = (bf16[4,64,4096]{2,1,0:T(8,128)(2,1)S(1)}, bf16[4,64,4096]{2,1,0:T(8,128)(2,1)}, u32[]{:S(2)}) copy-start(bf16[4,64,4096]{2,1,0:T(8,128)(2,1)} %up_ref.1) | copy-start | bytes 6291460
  0.0 30.6 %all-to-all-start = ((bf16[16,4,64,128]{3,2,1,0:T(8,128)(2,1)}), bf16[16,4,64,128]{3,2,1,0:T(8,128)(2,1)S(1)}, u32[]{:S(2)}, u32[]{:S(2)}) async-start(bf16[16,4,64,128]{3,2,1,0:T(8,128)(2,1)} %bitcast.9), calls=%async_computation | async-start | bytes 2097152 | tf_op jit(solution)/shard_map/all_to_all | solution.py:162
  7.5 1.7 %copy-start = (bf16[4,64,5120]{2,1,0:T(8,128)(2,1)S(1)}, bf16[4,64,5120]{2,1,0:T(8,128)(2,1)}, u32[]{:S(2)}) copy-start(bf16[4,64,5120]{2,1,0:T(8,128)(2,1)} %down_ref.1) | copy-start | bytes 7864324
  10.8 16.2 %copy-start.6 = (bf16[4,256,128]{2,1,0:T(8,128)(2,1)}, bf16[4,256,128]{2,1,0:T(8,128)(2,1)S(1)}, u32[]{:S(2)}) copy-start(bf16[4,256,128]{2,1,0:T(8,128)(2,1)S(1)} %get-tuple-element.16) | copy-start | bytes 786436
  10.8 2.2 %collective-permute-start = (bf16[8,320,128]{2,1,0:T(8,128)(2,1)S(1)}, bf16[8,320,128]{2,1,0:T(8,128)(2,1)S(1)}, u32[]{:S(2)}, u32[]{:S(2)}) collective-permute-start(bf16[8,320,128]{2,1,0:T(8,128)(2,1)S(1)} %get-tuple-element.19), channel_id=1, source_target_pairs={{0,1},{1,0},{2,3},{3,2},{4,5},{5,4},{6,7},{7,6},{8,9},{9,8},{10,11... | collective-permute-start | bytes 1966088 | tf_op jit(solution)/shard_map/ppermute | solution.py:159
  13.0 13.9 %collective-permute-start.2 = (bf16[4,320,128]{2,1,0:T(8,128)(2,1)S(1)}, bf16[4,320,128]{2,1,0:T(8,128)(2,1)S(1)}, u32[]{:S(2)}, u32[]{:S(2)}) collective-permute-start(bf16[4,320,128]{2,1,0:T(8,128)(2,1)S(1)} %slice_add_fusion.1), channel_id=1, source_target_pairs={{0,2},{1,3},{2,0},{3,1},{4,6},{5,7},{6,4},{7,5},{8,10},{9,11},{10,... | collective-permute-start | bytes 983048 | tf_op jit(solution)/shard_map/ppermute | solution.py:159
  14.5 12.5 %collective-permute-start.1 = (bf16[8,256,128]{2,1,0:T(8,128)(2,1)S(1)}, bf16[8,256,128]{2,1,0:T(8,128)(2,1)S(1)}, u32[]{:S(2)}, u32[]{:S(2)}) collective-permute-start(bf16[8,256,128]{2,1,0:T(8,128)(2,1)S(1)} %get-tuple-element.20), channel_id=1, source_target_pairs={{0,1},{1,0},{2,3},{3,2},{4,5},{5,4},{6,7},{7,6},{8,9},{9,8},{10,11... | collective-permute-start | bytes 1572872 | tf_op jit(solution)/shard_map/ppermute | solution.py:159
  30.7 6.1 %collective-permute-start.6 = (bf16[1,320,128]{2,1,0:T(8,128)(2,1)S(1)}, bf16[1,320,128]{2,1,0:T(8,128)(2,1)S(1)}, u32[]{:S(2)}, u32[]{:S(2)}) collective-permute-start(bf16[1,320,128]{2,1,0:T(8,128)(2,1)S(1)} %get-tuple-element.32), channel_id=1, source_target_pairs={{0,12},{1,13},{2,14},{3,15},{4,8},{5,9},{6,10},{7,11},{8,4},{9,5},... | collective-permute-start | bytes 245768 | tf_op jit(solution)/shard_map/ppermute | solution.py:159
  33.8 8.4 %collective-permute-start.4 = (bf16[1,320,128]{2,1,0:T(8,128)(2,1)S(1)}, bf16[1,320,128]{2,1,0:T(8,128)(2,1)S(1)}, u32[]{:S(2)}, u32[]{:S(2)}) collective-permute-start(bf16[1,320,128]{2,1,0:T(8,128)(2,1)S(1)} %get-tuple-element.33), channel_id=1, source_target_pairs={{0,8},{1,9},{2,10},{3,11},{4,12},{5,13},{6,14},{7,15},{8,0},{9,1},... | collective-permute-start | bytes 245768 | tf_op jit(solution)/shard_map/ppermute | solution.py:159
  35.0 7.2 %collective-permute-start.5 = (bf16[1,320,128]{2,1,0:T(8,128)(2,1)S(1)}, bf16[1,320,128]{2,1,0:T(8,128)(2,1)S(1)}, u32[]{:S(2)}, u32[]{:S(2)}) collective-permute-start(bf16[1,320,128]{2,1,0:T(8,128)(2,1)S(1)} %get-tuple-element.31), channel_id=1, source_target_pairs={{0,4},{1,5},{2,6},{3,7},{4,0},{5,1},{6,2},{7,3},{8,12},{9,13},{10,... | collective-permute-start | bytes 245768 | tf_op jit(solution)/shard_map/ppermute | solution.py:159
  35.0 16.6 %collective-permute-start.3 = (bf16[4,256,128]{2,1,0:T(8,128)(2,1)S(1)}, bf16[4,256,128]{2,1,0:T(8,128)(2,1)S(1)}, u32[]{:S(2)}, u32[]{:S(2)}) collective-permute-start(bf16[4,256,128]{2,1,0:T(8,128)(2,1)S(1)} %slice_add_fusion.2), channel_id=1, source_target_pairs={{0,2},{1,3},{2,0},{3,1},{4,6},{5,7},{6,4},{7,5},{8,10},{9,11},{10,... | collective-permute-start | bytes 786440 | tf_op jit(solution)/shard_map/ppermute | solution.py:159
  42.9 5.1 %collective-permute-start.9 = (bf16[1,320,128]{2,1,0:T(8,128)(2,1)S(1)}, bf16[1,320,128]{2,1,0:T(8,128)(2,1)S(1)}, u32[]{:S(2)}, u32[]{:S(2)}) collective-permute-start(bf16[1,320,128]{2,1,0:T(8,128)(2,1)S(1)} %get-tuple-element.28), channel_id=1, source_target_pairs={{0,12},{1,13},{2,14},{3,15},{4,8},{5,9},{6,10},{7,11},{8,4},{9,5},... | collective-permute-start | bytes 245768 | tf_op jit(solution)/shard_map/ppermute | solution.py:159
  45.6 6.0 %collective-permute-start.8 = (bf16[1,320,128]{2,1,0:T(8,128)(2,1)S(1)}, bf16[1,320,128]{2,1,0:T(8,128)(2,1)S(1)}, u32[]{:S(2)}, u32[]{:S(2)}) collective-permute-start(bf16[1,320,128]{2,1,0:T(8,128)(2,1)S(1)} %get-tuple-element.28), channel_id=1, source_target_pairs={{0,4},{1,5},{2,6},{3,7},{4,0},{5,1},{6,2},{7,3},{8,12},{9,13},{10,... | collective-permute-start | bytes 245768 | tf_op jit(solution)/shard_map/ppermute | solution.py:159
  45.6 6.0 %collective-permute-start.7 = (bf16[1,320,128]{2,1,0:T(8,128)(2,1)S(1)}, bf16[1,320,128]{2,1,0:T(8,128)(2,1)S(1)}, u32[]{:S(2)}, u32[]{:S(2)}) collective-permute-start(bf16[1,320,128]{2,1,0:T(8,128)(2,1)S(1)} %get-tuple-element.28), channel_id=1, source_target_pairs={{0,8},{1,9},{2,10},{3,11},{4,12},{5,13},{6,14},{7,15},{8,0},{9,1},... | collective-permute-start | bytes 245768 | tf_op jit(solution)/shard_map/ppermute | solution.py:159
  51.6 0.7 copy-start.10
  52.3 29.5 %all-to-all-start.2 = ((bf16[16,4,64,128]{3,2,1,0:T(8,128)(2,1)}), bf16[16,4,64,128]{3,2,1,0:T(8,128)(2,1)S(1)}, u32[]{:S(2)}, u32[]{:S(2)}) async-start(bf16[16,4,64,128]{3,2,1,0:T(8,128)(2,1)} %bitcast.4), calls=%async_computation.2 | async-start | bytes 2097152 | tf_op jit(solution)/shard_map/all_to_all | solution.py:162
  58.4 17.8 %collective-permute-start.13 = (bf16[4,320,128]{2,1,0:T(8,128)(2,1)S(1)}, bf16[4,320,128]{2,1,0:T(8,128)(2,1)S(1)}, u32[]{:S(2)}, u32[]{:S(2)}) collective-permute-start(bf16[4,320,128]{2,1,0:T(8,128)(2,1)S(1)} %pad_maximum_fusion), channel_id=1, source_target_pairs={{0,2},{1,3},{2,0},{3,1},{4,6},{5,7},{6,4},{7,5},{8,10},{9,11},{10,... | collective-permute-start | bytes 983048 | tf_op jit(solution)/shard_map/ppermute | solution.py:159
  61.2 18.8 %copy-start.2 = (bf16[2,64,5120]{2,1,0:T(8,128)(2,1)S(1)}, bf16[2,64,5120]{2,1,0:T(8,128)(2,1)}, u32[]{:S(2)}) copy-start(bf16[2,64,5120]{2,1,0:T(8,128)(2,1)} %x_ref.1) | copy-start | bytes 3932164
  61.2 18.8 %copy-start.3 = (bf16[2,32,64,128]{3,2,1,0:T(8,128)(2,1)S(1)}, bf16[2,32,64,128]{3,2,1,0:T(8,128)(2,1)}, u32[]{:S(2)}) copy-start(bf16[2,32,64,128]{3,2,1,0:T(8,128)(2,1)} %param.9) | copy-start | bytes 3145732
  77.0 2.8 %collective-permute-start.14 = (bf16[8,320,128]{2,1,0:T(8,128)(2,1)}, bf16[8,320,128]{2,1,0:T(8,128)(2,1)S(1)}, u32[]{:S(2)}, u32[]{:S(2)}) collective-permute-start(bf16[8,320,128]{2,1,0:T(8,128)(2,1)} %get-tuple-element.29), channel_id=1, source_target_pairs={{0,1},{1,0},{2,3},{3,2},{4,5},{5,4},{6,7},{7,6},{8,9},{9,8},{10,11... | collective-permute-start | bytes 1966088 | tf_op jit(solution)/shard_map/ppermute | solution.py:159
  81.9 7.4 %copy-start.7 = (bf16[4,256,128]{2,1,0:T(8,128)(2,1)S(1)}, bf16[4,256,128]{2,1,0:T(8,128)(2,1)}, u32[]{:S(2)}) copy-start(bf16[4,256,128]{2,1,0:T(8,128)(2,1)} %copy-done.6) | copy-start | bytes 786436
  81.9 7.4 %copy-start.11 = (bf16[4,256,128]{2,1,0:T(8,128)(2,1)S(1)}, bf16[4,256,128]{2,1,0:T(8,128)(2,1)}, u32[]{:S(2)}) copy-start(bf16[4,256,128]{2,1,0:T(8,128)(2,1)} %copy-done.10) | copy-start | bytes 786436
  81.9 1.0 copy-start.4
  82.9 40.6 %all-to-all-start.1 = ((bf16[16,288,128]{2,1,0:T(8,128)(2,1)}), bf16[16,288,128]{2,1,0:T(8,128)(2,1)S(1)}, u32[]{:S(2)}, u32[]{:S(2)}) async-start(bf16[16,288,128]{2,1,0:T(8,128)(2,1)} %low_rank.1), calls=%async_computation.1 | async-start | bytes 2359296 | tf_op jit(solution)/shard_map/all_to_all | solution.py:162
  89.3 24.6 %collective-permute-start.12 = (bf16[1,256,128]{2,1,0:T(8,128)(2,1)S(1)}, bf16[1,256,128]{2,1,0:T(8,128)(2,1)S(1)}, u32[]{:S(2)}, u32[]{:S(2)}) collective-permute-start(bf16[1,256,128]{2,1,0:T(8,128)(2,1)S(1)} %get-tuple-element.35), channel_id=1, source_target_pairs={{0,12},{1,13},{2,14},{3,15},{4,8},{5,9},{6,10},{7,11},{8,4},{9,5},... | collective-permute-start | bytes 196616 | tf_op jit(solution)/shard_map/ppermute | solution.py:159
  92.6 30.9 %collective-permute-start.10 = (bf16[1,256,128]{2,1,0:T(8,128)(2,1)S(1)}, bf16[1,256,128]{2,1,0:T(8,128)(2,1)S(1)}, u32[]{:S(2)}, u32[]{:S(2)}) collective-permute-start(bf16[1,256,128]{2,1,0:T(8,128)(2,1)S(1)} %get-tuple-element.36), channel_id=1, source_target_pairs={{0,8},{1,9},{2,10},{3,11},{4,12},{5,13},{6,14},{7,15},{8,0},{9,1},... | collective-permute-start | bytes 196616 | tf_op jit(solution)/shard_map/ppermute | solution.py:159
  92.6 30.9 %collective-permute-start.11 = (bf16[1,256,128]{2,1,0:T(8,128)(2,1)S(1)}, bf16[1,256,128]{2,1,0:T(8,128)(2,1)S(1)}, u32[]{:S(2)}, u32[]{:S(2)}) collective-permute-start(bf16[1,256,128]{2,1,0:T(8,128)(2,1)S(1)} %get-tuple-element.34), channel_id=1, source_target_pairs={{0,4},{1,5},{2,6},{3,7},{4,0},{5,1},{6,2},{7,3},{8,12},{9,13},{10,... | collective-permute-start | bytes 196616 | tf_op jit(solution)/shard_map/ppermute | solution.py:159
  123.5 1.2 copy-start.5

commit v14 on v13

--- a/solution.py
+++ b/solution.py
@@ -214,15 +214,18 @@
         if i > 0:
             send_up(i - 1, piece)
         down_got.append(swap(piece, 1 << i))
-    shards = after(halving(down_pieces, down_got, bits - 2), keys, *up_got)
-    send_up(bits - 3, shards)
+    send_up(bits - 3, piece)
+    shards = after(halving(down_pieces, down_got, bits - 2), keys, *up_got[:-1])
     shard = shards[:1] + sum(to_others(shards))
+    shard = after(shard, up_got[-1])
     gathered = jnp.concatenate([shard] + [swap(shard, k) for k in others], axis=0)
-    vals = exchange(after(by_pairs(values), gathered, up_got[-1]))
+    vals = exchange(after(by_pairs(values), gathered))
     up_shards = after(halving(up_pieces, up_got, bits - 2), gathered)
     up_here = (up_shards[:1] + sum(to_others(up_shards))).reshape(pairs, ranks, LANES)
     for i in reversed(range(bits - 2)):
         gathered = jnp.concatenate([gathered, swap(gathered, 1 << i)], axis=0)
+
+    gathered = after(gathered, up_here)
 
     asked = pl.pallas_call(
         functools.partial(low_rank_kernel, shape),

time: 164 us -> 166 us (1.012)
  blocking collectives: 29.5 us -> 62.1 us
  waiting for transfers between devices: 75.3 us -> 50.2 us
  starting transfers between devices: 37.4 us -> 34 us
  local copies, waits for them, and re-layouts: 8.51 us -> 6.38 us
    all_to_all x1 -> x2, blocking collectives: 29.5 us -> 62.1 us  [exchange(): lax.all_to_all(tensor, 'seq', split_axis=0, concat_axis=0, tiled=True)]
    ppermute x15, waiting for transfers between devices: 71.6 us -> 46.6 us  [swap(): return lax.ppermute(tensor, 'seq', [(i, i ^ k) for i in range(devs)])]
    all_to_all x3 -> x2, starting transfers between devices: 19.9 us -> 15.3 us  [exchange(): lax.all_to_all(tensor, 'seq', split_axis=0, concat_axis=0, tiled=True)]
    unnamed x29 -> x23, local copies, waits for them, and re-layouts: 7.58 us -> 5.45 us
    all_to_all x3 -> x2, waiting for transfers between devices: 3.65 us -> 3.65 us  [exchange(): lax.all_to_all(tensor, 'seq', split_axis=0, concat_axis=0, tiled=True)]
  transfers between devices with their start and end apart: 18 -> 17, of which waited for: 11 -> 10; matrix products, arithmetic and copies ran while one was open for 2% -> 2% of each run, Pallas kernels for 2% -> 1%
where the time goes in v14:
time: 166 us; the launch traced here: 165 us
  blocking collectives  62.1 us (37%)
  waiting for transfers between devices  50.2 us (30%)
  starting transfers between devices  34 us (20%)
  Pallas kernels  11.7 us (7%)
  local copies, waits for them, and re-layouts  6.38 us (4%)
    all_to_all x2, blocking collectives, exchange(): lax.all_to_all(tensor, 'seq', split_axis=0, concat_axis=0, tiled=True)  62.1 us
    ppermute x15, waiting for transfers between devices, swap(): return lax.ppermute(tensor, 'seq', [(i, i ^ k) for i in range(devs)])  46.6 us
    ppermute x15, starting transfers between devices, swap(): return lax.ppermute(tensor, 'seq', [(i, i ^ k) for i in range(devs)])  18.6 us
    all_to_all x2, starting transfers between devices, exchange(): lax.all_to_all(tensor, 'seq', split_axis=0, concat_axis=0, tiled=True)  15.3 us
    pallas_call x1, Pallas kernels, body(): pl.pallas_call(functools.partial(attend_kernel, math.gcd(devs, max(1, 512...  9.27 us
    unnamed x23, local copies, waits for them, and re-layouts  5.45 us
    all_to_all x2, waiting for transfers between devices, exchange(): lax.all_to_all(tensor, 'seq', split_axis=0, concat_axis=0, tiled=True)  3.65 us
  transfers between devices with their start and end apart: 17, of which 10 were waited for; matrix products, arithmetic and copies ran while one was open for 2% of the time, Pallas kernels for 1%

profile of v14, /device:TPU:1, one launch (start us, length us, event | category | flops | bytes accessed | tf_op | source)
XLA Modules:
  0.0 165.3 jit_solution(8947919300429841211)
XLA Ops:
  0.0 7.5 %all-to-all-start = ((bf16[16,4,64,128]{3,2,1,0:T(8,128)(2,1)}), bf16[16,4,64,128]{3,2,1,0:T(8,128)(2,1)S(1)}, u32[]{:S(2)}, u32[]{:S(2)}) async-start(bf16[16,4,64,128]{3,2,1,0:T(8,128)(2,1)} %bitcast.9), calls=%async_computation | async-start | bytes 2097152 | tf_op jit(solution)/shard_map/all_to_all | solution.py:162
  7.5 0.0 copy-start
  7.5 1.7 %copy-done = bf16[4,64,5120]{2,1,0:T(8,128)(2,1)S(1)} copy-done((bf16[4,64,5120]{2,1,0:T(8,128)(2,1)S(1)}, bf16[4,64,5120]{2,1,0:T(8,128)(2,1)}, u32[]{:S(2)}) %copy-start) | copy-done | bytes 2621464
  9.3 1.5 pick_factors.1
  10.8 0.2 collective-permute-start
  11.0 2.0 %collective-permute-done = bf16[8,320,128]{2,1,0:T(8,128)(2,1)S(1)} collective-permute-done((bf16[8,320,128]{2,1,0:T(8,128)(2,1)S(1)}, bf16[8,320,128]{2,1,0:T(8,128)(2,1)S(1)}, u32[]{:S(2)}, u32[]{:S(2)}) %collective-permute-start) | collective-permute-done | bytes 655392 | tf_op jit(solution)/shard_map/ppermute | solution.py:159
  13.0 1.5 collective-permute-start.3
  14.5 0.6 collective-permute-start.1
  15.1 11.8 %collective-permute-done.3 = bf16[4,320,128]{2,1,0:T(8,128)(2,1)S(1)} collective-permute-done((bf16[4,320,128]{2,1,0:T(8,128)(2,1)S(1)}, bf16[4,320,128]{2,1,0:T(8,128)(2,1)S(1)}, u32[]{:S(2)}, u32[]{:S(2)}) %collective-permute-start.3) | collective-permute-done | bytes 327712 | tf_op jit(solution)/shard_map/ppermute | solution.py:159
  27.0 0.0 collective-permute-done.1
  27.0 3.6 %all-to-all-done.k_ref = bf16[16,4,64,128]{3,2,1,0:T(8,128)(2,1)S(1)} async-done(((bf16[16,4,64,128]{3,2,1,0:T(8,128)(2,1)}), bf16[16,4,64,128]{3,2,1,0:T(8,128)(2,1)S(1)}, u32[]{:S(2)}, u32[]{:S(2)}) %all-to-all-start) | async-done | bytes 1048608 | tf_op jit(solution)/shard_map/all_to_all | solution.py:162
  30.7 3.1 %collective-permute-start.6 = (bf16[1,320,128]{2,1,0:T(8,128)(2,1)S(1)}, bf16[1,320,128]{2,1,0:T(8,128)(2,1)S(1)}, u32[]{:S(2)}, u32[]{:S(2)}) collective-permute-start(bf16[1,320,128]{2,1,0:T(8,128)(2,1)S(1)} %get-tuple-element.34), channel_id=1, source_target_pairs={{0,12},{1,13},{2,14},{3,15},{4,8},{5,9},{6,10},{7,11},{8,4},{9,5},... | collective-permute-start | bytes 245768 | tf_op jit(solution)/shard_map/ppermute | solution.py:159
  33.8 1.2 collective-permute-start.4
  35.0 0.0 collective-permute-start.5
  35.0 1.3 collective-permute-start.2
  36.4 0.3 collective-permute-done.6
  36.7 5.5 %collective-permute-done.4 = bf16[1,320,128]{2,1,0:T(8,128)(2,1)S(1)} collective-permute-done((bf16[1,320,128]{2,1,0:T(8,128)(2,1)S(1)}, bf16[1,320,128]{2,1,0:T(8,128)(2,1)S(1)}, u32[]{:S(2)}, u32[]{:S(2)}) %collective-permute-start.4) | collective-permute-done | bytes 81952 | tf_op jit(solution)/shard_map/ppermute | solution.py:159
  42.2 0.0 collective-permute-done.5
  42.2 0.0 collective-permute-done.2
  42.2 1.1 collective-permute-start.7
  43.4 2.1 %collective-permute-start.8 = (bf16[1,320,128]{2,1,0:T(8,128)(2,1)S(1)}, bf16[1,320,128]{2,1,0:T(8,128)(2,1)S(1)}, u32[]{:S(2)}, u32[]{:S(2)}) collective-permute-start(bf16[1,320,128]{2,1,0:T(8,128)(2,1)S(1)} %add_add_fusion), channel_id=1, source_target_pairs={{0,4},{1,5},{2,6},{3,7},{4,0},{5,1},{6,2},{7,3},{8,12},{9,13},{10,... | collective-permute-start | bytes 245768 | tf_op jit(solution)/shard_map/ppermute | solution.py:159
  45.4 0.4 collective-permute-start.9
  45.9 0.7 constant_dynamic-update-slice_fusion.8
  46.5 0.9 collective-permute-done.7
  47.4 0.7 constant_dynamic-update-slice_fusion.7
  48.1 0.0 collective-permute-done.8
  48.1 0.7 constant_dynamic-update-slice_fusion.6
  48.8 2.6 %collective-permute-done.9 = bf16[1,320,128]{2,1,0:T(8,128)(2,1)S(1)} collective-permute-done((bf16[1,320,128]{2,1,0:T(8,128)(2,1)S(1)}, bf16[1,320,128]{2,1,0:T(8,128)(2,1)S(1)}, u32[]{:S(2)}, u32[]{:S(2)}) %collective-permute-start.9) | collective-permute-done | bytes 81952 | tf_op jit(solution)/shard_map/ppermute | solution.py:159
  51.4 0.7 constant_dynamic-update-slice_fusion.5
  52.1 7.9 %all-to-all-start.2 = ((bf16[16,4,64,128]{3,2,1,0:T(8,128)(2,1)}), bf16[16,4,64,128]{3,2,1,0:T(8,128)(2,1)}, u32[]{:S(2)}, u32[]{:S(2)}) async-start(bf16[16,4,64,128]{3,2,1,0:T(8,128)(2,1)} %bitcast.10), calls=%async_computation.2 | async-start | bytes 2097152 | tf_op jit(solution)/shard_map/all_to_all | solution.py:162
  59.9 1.4 collective-permute-start.13
  61.3 16.4 %collective-permute-done.13 = bf16[4,320,128]{2,1,0:T(8,128)(2,1)S(1)} collective-permute-done((bf16[4,320,128]{2,1,0:T(8,128)(2,1)}, bf16[4,320,128]{2,1,0:T(8,128)(2,1)S(1)}, u32[]{:S(2)}, u32[]{:S(2)}) %collective-permute-start.13) | collective-permute-done | bytes 327712 | tf_op jit(solution)/shard_map/ppermute | solution.py:159
  77.7 0.8 constant_dynamic-update-slice_fusion.4
  78.5 0.9 collective-permute-start.14
  79.5 4.5 %collective-permute-start.12 = (bf16[1,256,128]{2,1,0:T(8,128)(2,1)S(1)}, bf16[1,256,128]{2,1,0:T(8,128)(2,1)S(1)}, u32[]{:S(2)}, u32[]{:S(2)}) collective-permute-start(bf16[1,256,128]{2,1,0:T(8,128)(2,1)S(1)} %get-tuple-element.37), channel_id=1, source_target_pairs={{0,12},{1,13},{2,14},{3,15},{4,8},{5,9},{6,10},{7,11},{8,4},{9,5},... | collective-permute-start | bytes 196616 | tf_op jit(solution)/shard_map/ppermute | solution.py:159
  83.9 0.0 collective-permute-start.10
  83.9 0.4 collective-permute-start.11
  84.3 2.1 %collective-permute-done.12 = bf16[1,256,128]{2,1,0:T(8,128)(2,1)S(1)} collective-permute-done((bf16[1,256,128]{2,1,0:T(8,128)(2,1)S(1)}, bf16[1,256,128]{2,1,0:T(8,128)(2,1)S(1)}, u32[]{:S(2)}, u32[]{:S(2)}) %collective-permute-start.12) | collective-permute-done | bytes 65568 | tf_op jit(solution)/shard_map/ppermute | solution.py:159
  86.4 4.9 %collective-permute-done.10 = bf16[1,256,128]{2,1,0:T(8,128)(2,1)S(1)} collective-permute-done((bf16[1,256,128]{2,1,0:T(8,128)(2,1)S(1)}, bf16[1,256,128]{2,1,0:T(8,128)(2,1)S(1)}, u32[]{:S(2)}, u32[]{:S(2)}) %collective-permute-start.10) | collective-permute-done | bytes 65568 | tf_op jit(solution)/shard_map/ppermute | solution.py:159
  91.3 0.0 collective-permute-done.11
  91.3 0.6 add_add_fusion.1
  92.0 0.1 constant_dynamic-update-slice_fusion.9.g_ref
  92.1 0.9 low_rank.1
  93.0 0.0 all-to-all-done.2.v_ref
  93.0 33.7 %all_to_all.20.q_ref.low_ref = bf16[16,288,128]{2,1,0:T(8,128)(2,1)S(1)} all-to-all(bf16[16,288,128]{2,1,0:T(8,128)(2,1)S(1)} %low_rank.1), channel_id=1, replica_groups=mesh['grp'=2,'seq'=16] {'seq'}, dimensions={0} | all-to-all | bytes 2359296 | tf_op jit(solution)/shard_map/all_to_all | solution.py:162
  126.7 9.3 %attend.1 = bf16[16,4,64,128]{3,2,1,0:T(8,128)(2,1)S(1)} custom-call(bf16[4,64,128]{2,1,0:T(8,128)(2,1)S(1)} %bitcast.7, bf16[16,288,128]{2,1,0:T(8,128)(2,1)S(1)} %all_to_all.20.q_ref.low_ref, bf16[16,288,128]{2,1,0:T(8,128)(2,1)S(1)} %all_to_all.20.q_ref.low_ref, bf16[16,4,64,128]{3,2,1,0:T(8,128)(2,1)S(1)} %all-to-all-done.k_ref, ...), custom_call_target="tpu_custom_call" | custom-call | flops 2147483648 | bytes 4194304 | tf_op jit(solution)/shard_map/attend/pallas_call | solution.py:247
  136.0 28.4 %all_to_all.21 = bf16[16,4,64,128]{3,2,1,0:T(8,128)(2,1)S(1)} all-to-all(bf16[16,4,64,128]{3,2,1,0:T(8,128)(2,1)S(1)} %attend.1), channel_id=1, replica_groups=mesh['grp'=2,'seq'=16] {'seq'}, dimensions={0} | all-to-all | bytes 2097152 | tf_op jit(solution)/shard_map/all_to_all | solution.py:162
  164.4 1.0 copy.22
  (24 shorter events, 0.2 us)
Async XLA Ops:
  0.0 7.5 %copy-start.7 = (s32[64]{0:T(128)S(1)}, s32[64]{0:T(128)}, u32[]{:S(2)}) copy-start(s32[64]{0:T(128)} %row_ref.1) | copy-start | bytes 772
  0.0 7.5 %copy-start.8 = (s32[2]{0:T(128)S(1)}, s32[2]{0:T(128)}, u32[]{:S(2)}) copy-start(s32[2]{0:T(128)} %req_ref.1) | copy-start | bytes 28
  0.0 7.5 %copy-start.1 = (bf16[4,64,4096]{2,1,0:T(8,128)(2,1)S(1)}, bf16[4,64,4096]{2,1,0:T(8,128)(2,1)}, u32[]{:S(2)}) copy-start(bf16[4,64,4096]{2,1,0:T(8,128)(2,1)} %up_ref.1) | copy-start | bytes 6291460
  0.0 30.6 %all-to-all-start = ((bf16[16,4,64,128]{3,2,1,0:T(8,128)(2,1)}), bf16[16,4,64,128]{3,2,1,0:T(8,128)(2,1)S(1)}, u32[]{:S(2)}, u32[]{:S(2)}) async-start(bf16[16,4,64,128]{3,2,1,0:T(8,128)(2,1)} %bitcast.9), calls=%async_computation | async-start | bytes 2097152 | tf_op jit(solution)/shard_map/all_to_all | solution.py:162
  7.5 1.7 %copy-start = (bf16[4,64,5120]{2,1,0:T(8,128)(2,1)S(1)}, bf16[4,64,5120]{2,1,0:T(8,128)(2,1)}, u32[]{:S(2)}) copy-start(bf16[4,64,5120]{2,1,0:T(8,128)(2,1)} %down_ref.1) | copy-start | bytes 7864324
  10.8 16.2 %copy-start.4 = (bf16[4,256,128]{2,1,0:T(8,128)(2,1)}, bf16[4,256,128]{2,1,0:T(8,128)(2,1)S(1)}, u32[]{:S(2)}) copy-start(bf16[4,256,128]{2,1,0:T(8,128)(2,1)S(1)} %get-tuple-element.18) | copy-start | bytes 786436
  10.8 2.2 %collective-permute-start = (bf16[8,320,128]{2,1,0:T(8,128)(2,1)S(1)}, bf16[8,320,128]{2,1,0:T(8,128)(2,1)S(1)}, u32[]{:S(2)}, u32[]{:S(2)}) collective-permute-start(bf16[8,320,128]{2,1,0:T(8,128)(2,1)S(1)} %get-tuple-element.21), channel_id=1, source_target_pairs={{0,1},{1,0},{2,3},{3,2},{4,5},{5,4},{6,7},{7,6},{8,9},{9,8},{10,11... | collective-permute-start | bytes 1966088 | tf_op jit(solution)/shard_map/ppermute | solution.py:159
  13.0 13.9 %collective-permute-start.3 = (bf16[4,320,128]{2,1,0:T(8,128)(2,1)S(1)}, bf16[4,320,128]{2,1,0:T(8,128)(2,1)S(1)}, u32[]{:S(2)}, u32[]{:S(2)}) collective-permute-start(bf16[4,320,128]{2,1,0:T(8,128)(2,1)S(1)} %slice_add_fusion.1), channel_id=1, source_target_pairs={{0,2},{1,3},{2,0},{3,1},{4,6},{5,7},{6,4},{7,5},{8,10},{9,11},{10,... | collective-permute-start | bytes 983048 | tf_op jit(solution)/shard_map/ppermute | solution.py:159
  14.5 12.5 %collective-permute-start.1 = (bf16[8,256,128]{2,1,0:T(8,128)(2,1)S(1)}, bf16[8,256,128]{2,1,0:T(8,128)(2,1)S(1)}, u32[]{:S(2)}, u32[]{:S(2)}) collective-permute-start(bf16[8,256,128]{2,1,0:T(8,128)(2,1)S(1)} %get-tuple-element.22), channel_id=1, source_target_pairs={{0,1},{1,0},{2,3},{3,2},{4,5},{5,4},{6,7},{7,6},{8,9},{9,8},{10,11... | collective-permute-start | bytes 1572872 | tf_op jit(solution)/shard_map/ppermute | solution.py:159
  30.7 6.1 %collective-permute-start.6 = (bf16[1,320,128]{2,1,0:T(8,128)(2,1)S(1)}, bf16[1,320,128]{2,1,0:T(8,128)(2,1)S(1)}, u32[]{:S(2)}, u32[]{:S(2)}) collective-permute-start(bf16[1,320,128]{2,1,0:T(8,128)(2,1)S(1)} %get-tuple-element.34), channel_id=1, source_target_pairs={{0,12},{1,13},{2,14},{3,15},{4,8},{5,9},{6,10},{7,11},{8,4},{9,5},... | collective-permute-start | bytes 245768 | tf_op jit(solution)/shard_map/ppermute | solution.py:159
  33.8 8.4 %collective-permute-start.4 = (bf16[1,320,128]{2,1,0:T(8,128)(2,1)S(1)}, bf16[1,320,128]{2,1,0:T(8,128)(2,1)S(1)}, u32[]{:S(2)}, u32[]{:S(2)}) collective-permute-start(bf16[1,320,128]{2,1,0:T(8,128)(2,1)S(1)} %get-tuple-element.35), channel_id=1, source_target_pairs={{0,8},{1,9},{2,10},{3,11},{4,12},{5,13},{6,14},{7,15},{8,0},{9,1},... | collective-permute-start | bytes 245768 | tf_op jit(solution)/shard_map/ppermute | solution.py:159
  35.0 7.2 %collective-permute-start.5 = (bf16[1,320,128]{2,1,0:T(8,128)(2,1)S(1)}, bf16[1,320,128]{2,1,0:T(8,128)(2,1)S(1)}, u32[]{:S(2)}, u32[]{:S(2)}) collective-permute-start(bf16[1,320,128]{2,1,0:T(8,128)(2,1)S(1)} %get-tuple-element.33), channel_id=1, source_target_pairs={{0,4},{1,5},{2,6},{3,7},{4,0},{5,1},{6,2},{7,3},{8,12},{9,13},{10,... | collective-permute-start | bytes 245768 | tf_op jit(solution)/shard_map/ppermute | solution.py:159
  35.0 7.2 %collective-permute-start.2 = (bf16[4,256,128]{2,1,0:T(8,128)(2,1)S(1)}, bf16[4,256,128]{2,1,0:T(8,128)(2,1)S(1)}, u32[]{:S(2)}, u32[]{:S(2)}) collective-permute-start(bf16[4,256,128]{2,1,0:T(8,128)(2,1)S(1)} %slice_add_fusion.2), channel_id=1, source_target_pairs={{0,2},{1,3},{2,0},{3,1},{4,6},{5,7},{6,4},{7,5},{8,10},{9,11},{10,... | collective-permute-start | bytes 786440 | tf_op jit(solution)/shard_map/ppermute | solution.py:159
  42.2 5.1 %collective-permute-start.7 = (bf16[1,320,128]{2,1,0:T(8,128)(2,1)S(1)}, bf16[1,320,128]{2,1,0:T(8,128)(2,1)S(1)}, u32[]{:S(2)}, u32[]{:S(2)}) collective-permute-start(bf16[1,320,128]{2,1,0:T(8,128)(2,1)S(1)} %add_add_fusion), channel_id=1, source_target_pairs={{0,8},{1,9},{2,10},{3,11},{4,12},{5,13},{6,14},{7,15},{8,0},{9,1},... | collective-permute-start | bytes 245768 | tf_op jit(solution)/shard_map/ppermute | solution.py:159
  43.4 4.7 %collective-permute-start.8 = (bf16[1,320,128]{2,1,0:T(8,128)(2,1)S(1)}, bf16[1,320,128]{2,1,0:T(8,128)(2,1)S(1)}, u32[]{:S(2)}, u32[]{:S(2)}) collective-permute-start(bf16[1,320,128]{2,1,0:T(8,128)(2,1)S(1)} %add_add_fusion), channel_id=1, source_target_pairs={{0,4},{1,5},{2,6},{3,7},{4,0},{5,1},{6,2},{7,3},{8,12},{9,13},{10,... | collective-permute-start | bytes 245768 | tf_op jit(solution)/shard_map/ppermute | solution.py:159
  45.4 5.9 %collective-permute-start.9 = (bf16[1,320,128]{2,1,0:T(8,128)(2,1)S(1)}, bf16[1,320,128]{2,1,0:T(8,128)(2,1)S(1)}, u32[]{:S(2)}, u32[]{:S(2)}) collective-permute-start(bf16[1,320,128]{2,1,0:T(8,128)(2,1)S(1)} %add_add_fusion), channel_id=1, source_target_pairs={{0,12},{1,13},{2,14},{3,15},{4,8},{5,9},{6,10},{7,11},{8,4},{9,5},... | collective-permute-start | bytes 245768 | tf_op jit(solution)/shard_map/ppermute | solution.py:159
  52.1 27.3 %copy-start.5 = (bf16[4,256,128]{2,1,0:T(8,128)(2,1)S(1)}, bf16[4,256,128]{2,1,0:T(8,128)(2,1)}, u32[]{:S(2)}) copy-start(bf16[4,256,128]{2,1,0:T(8,128)(2,1)} %copy-done.4) | copy-start | bytes 786436
  52.1 40.9 %all-to-all-start.2 = ((bf16[16,4,64,128]{3,2,1,0:T(8,128)(2,1)}), bf16[16,4,64,128]{3,2,1,0:T(8,128)(2,1)}, u32[]{:S(2)}, u32[]{:S(2)}) async-start(bf16[16,4,64,128]{3,2,1,0:T(8,128)(2,1)} %bitcast.10), calls=%async_computation.2 | async-start | bytes 2097152 | tf_op jit(solution)/shard_map/all_to_all | solution.py:162
  59.9 17.8 %collective-permute-start.13 = (bf16[4,320,128]{2,1,0:T(8,128)(2,1)}, bf16[4,320,128]{2,1,0:T(8,128)(2,1)S(1)}, u32[]{:S(2)}, u32[]{:S(2)}) collective-permute-start(bf16[4,320,128]{2,1,0:T(8,128)(2,1)} %get-tuple-element.41), channel_id=1, source_target_pairs={{0,2},{1,3},{2,0},{3,1},{4,6},{5,7},{6,4},{7,5},{8,10},{9,11},{10,... | collective-permute-start | bytes 983048 | tf_op jit(solution)/shard_map/ppermute | solution.py:159
  78.5 13.4 %collective-permute-start.14 = (bf16[8,320,128]{2,1,0:T(8,128)(2,1)}, bf16[8,320,128]{2,1,0:T(8,128)(2,1)S(1)}, u32[]{:S(2)}, u32[]{:S(2)}) collective-permute-start(bf16[8,320,128]{2,1,0:T(8,128)(2,1)} %get-tuple-element.31), channel_id=1, source_target_pairs={{0,1},{1,0},{2,3},{3,2},{4,5},{5,4},{6,7},{7,6},{8,9},{9,8},{10,11... | collective-permute-start | bytes 1966088 | tf_op jit(solution)/shard_map/ppermute | solution.py:159
  79.4 12.6 %copy-start.2 = (bf16[2,64,5120]{2,1,0:T(8,128)(2,1)S(1)}, bf16[2,64,5120]{2,1,0:T(8,128)(2,1)}, u32[]{:S(2)}) copy-start(bf16[2,64,5120]{2,1,0:T(8,128)(2,1)} %x_ref.1) | copy-start | bytes 3932164
  79.4 12.6 %copy-start.3 = (bf16[2,32,64,128]{3,2,1,0:T(8,128)(2,1)S(1)}, bf16[2,32,64,128]{3,2,1,0:T(8,128)(2,1)}, u32[]{:S(2)}) copy-start(bf16[2,32,64,128]{3,2,1,0:T(8,128)(2,1)} %param.9) | copy-start | bytes 3145732
  79.5 7.0 %collective-permute-start.12 = (bf16[1,256,128]{2,1,0:T(8,128)(2,1)S(1)}, bf16[1,256,128]{2,1,0:T(8,128)(2,1)S(1)}, u32[]{:S(2)}, u32[]{:S(2)}) collective-permute-start(bf16[1,256,128]{2,1,0:T(8,128)(2,1)S(1)} %get-tuple-element.37), channel_id=1, source_target_pairs={{0,12},{1,13},{2,14},{3,15},{4,8},{5,9},{6,10},{7,11},{8,4},{9,5},... | collective-permute-start | bytes 196616 | tf_op jit(solution)/shard_map/ppermute | solution.py:159
  83.9 7.4 %collective-permute-start.10 = (bf16[1,256,128]{2,1,0:T(8,128)(2,1)S(1)}, bf16[1,256,128]{2,1,0:T(8,128)(2,1)S(1)}, u32[]{:S(2)}, u32[]{:S(2)}) collective-permute-start(bf16[1,256,128]{2,1,0:T(8,128)(2,1)S(1)} %get-tuple-element.38), channel_id=1, source_target_pairs={{0,8},{1,9},{2,10},{3,11},{4,12},{5,13},{6,14},{7,15},{8,0},{9,1},... | collective-permute-start | bytes 196616 | tf_op jit(solution)/shard_map/ppermute | solution.py:159
  83.9 7.4 %collective-permute-start.11 = (bf16[1,256,128]{2,1,0:T(8,128)(2,1)S(1)}, bf16[1,256,128]{2,1,0:T(8,128)(2,1)S(1)}, u32[]{:S(2)}, u32[]{:S(2)}) collective-permute-start(bf16[1,256,128]{2,1,0:T(8,128)(2,1)S(1)} %get-tuple-element.36), channel_id=1, source_target_pairs={{0,4},{1,5},{2,6},{3,7},{4,0},{5,1},{6,2},{7,3},{8,12},{9,13},{10,... | collective-permute-start | bytes 196616 | tf_op jit(solution)/shard_map/ppermute | solution.py:159
  93.0 33.7 %copy-start.6 = (bf16[1,256,128]{2,1,0:T(8,128)(2,1)S(1)}, bf16[1,256,128]{2,1,0:T(8,128)(2,1)}, u32[]{:S(2)}) copy-start(bf16[1,256,128]{2,1,0:T(8,128)(2,1)} %add_add_fusion.1) | copy-start | bytes 196612

commit v15 on v13

--- a/solution.py
+++ b/solution.py
@@ -73,16 +73,47 @@
             ups[step][at, p * ranks : (p + 1) * ranks, :] = up[video, :, pl.ds(col, LANES)]
 
 
-def low_rank_kernel(shape, me_ref, x_ref, g_ref, q_ref, out_ref, down):
+def sum_kernel(picks, *refs):
+    outs = refs[-len(picks) :]
+    for out, terms in zip(outs, picks):
+        size = out.shape[0]
+        parts = [refs[i][first : first + size] for i, first in terms]
+        out[...] = sum(parts[1:], parts[0])
+
+
+def join_kernel(*refs):
+    out, first = refs[-1], 0
+    for ref in refs[:-1]:
+        out[first : first + ref.shape[0]] = ref[...]
+        first += ref.shape[0]
+
+
+def on_vmem(kernel, shapes, name, *arrays):
+    return pl.pallas_call(
+        kernel,
+        in_specs=[VMEM] * len(arrays),
+        out_specs=[VMEM] * len(shapes),
+        out_shape=[jax.ShapeDtypeStruct(s, arrays[0].dtype) for s in shapes],
+        compiler_params=pltpu.CompilerParams(vmem_limit_bytes=16 << 20),
+        cost_estimate=pl.CostEstimate(
+            flops=0, bytes_accessed=2 * sum(a.size for a in arrays), transcendentals=0
+        ),
+        name=name,
+    )(*arrays)
+
+
+def low_rank_kernel(shape, me_ref, x_ref, q_ref, *refs):
     devs, bits, per_video, _, col_split, rows, tiles = shape
-    for j in range(devs):
+    parts, out_ref, down = refs[:-2], refs[-2], refs[-1]
+    blocks = [(ref, i) for ref in parts for i in range(ref.shape[0])]
+    for j, (ref, i) in enumerate(blocks):
         dev = me_ref[0] ^ reversed_bits(j, bits)
         video = dev // per_video
         place = dev % per_video
         row = pl.multiple_of((place // col_split) * rows, rows)
         for t in range(tiles):
             col = pl.multiple_of(((place % col_split) * tiles + t) * LANES, LANES)
-            down[video, pl.ds(row, rows), pl.ds(col, LANES)] = g_ref[j, t * rows : (t + 1) * rows, :]
+            down[video, pl.ds(row, rows), pl.ds(col, LANES)] = ref[i, t * rows : (t + 1) * rows, :]
     first = q_ref.shape[1]
     out_ref[:, :first] = q_ref[...]
     for s in range(x_ref.shape[0]):
@@ -172,11 +203,30 @@
 
     def halving(parts, received, i):
         size = parts[i].shape[0]
-        start = size if i < bits - 2 else 0
-        return sum((r[start : start + size] for r in received), parts[i])
+        terms = [(0, 0)] + [(1 + n, size) for n in range(len(received))]
+        return on_vmem(
+            functools.partial(sum_kernel, [terms]), [parts[i].shape], "halve", parts[i], *received
+        )[0]
+
+    def splitting(parts, received):
+        size = (1,) + parts[-1].shape[1:]
+        picks = [[(n, j) for n in range(1 + len(received))] for j in range(LOW)]
+        return on_vmem(
+            functools.partial(sum_kernel, picks), [size] * LOW, "split", parts[-1], *received
+        )
 
     def to_others(shards):
-        return [swap(shards[j + 1 : j + 2], k) for j, k in enumerate(others)]
+        return [swap(shard, k) for shard, k in zip(shards[1:], others)]
+
+    def total(shard, received):
+        picks = [[(n, 0) for n in range(LOW)]]
+        return on_vmem(
+            functools.partial(sum_kernel, picks), [shard.shape], "total", shard, *received
+        )[0]
+
+    def join(arrays):
+        count = sum(a.shape[0] for a in arrays)
+        return on_vmem(join_kernel, [(count,) + arrays[0].shape[1:]], "join", *arrays)[0]
 
     keys = exchange(by_pairs(projected_keys))
 
@@ -210,23 +260,29 @@
         up_got.append(swap(after(halving(up_pieces, up_got, i), *others), 1 << i))
 
     for i in range(bits - 2):
-        piece = halving(down_pieces, down_got, i)
+        piece = down_pieces[0] if i == 0 else halving(down_pieces, down_got, i)
         if i > 0:
-            send_up(i - 1, piece)
+            part = up_pieces[0] if i == 1 else halving(up_pieces, up_got, i - 1)
+            up_got.append(swap(after(part, piece), 1 << (i - 1)))
         down_got.append(swap(piece, 1 << i))
-    shards = after(halving(down_pieces, down_got, bits - 2), keys, *up_got)
-    send_up(bits - 3, shards)
-    shard = shards[:1] + sum(to_others(shards))
-    gathered = jnp.concatenate([shard] + [swap(shard, k) for k in others], axis=0)
-    vals = exchange(after(by_pairs(values), gathered, up_got[-1]))
-    up_shards = after(halving(up_pieces, up_got, bits - 2), gathered)
-    up_here = (up_shards[:1] + sum(to_others(up_shards))).reshape(pairs, ranks, LANES)
+    part = after(halving(up_pieces, up_got, bits - 3), piece)
+    up_got.append(swap(part, 1 << (bits - 3)))
+    held = splitting((after(down_pieces[-1], keys, *up_got[:-1]),), down_got)
+    shard = after(total(held[0], to_others(held)), up_got[-1])
+    up_held = splitting((after(up_pieces[-1], shard),), up_got)
+    gathered = [shard] + [swap(shard, k) for k in others]
+    up_here = total(up_held[0], to_others(up_held))
+    vals = exchange(after(by_pairs(values), *gathered, up_here))
+    up_here = up_here.reshape(pairs, ranks, LANES)
+    joined = join(gathered)
     for i in reversed(range(bits - 2)):
-        gathered = jnp.concatenate([gathered, swap(gathered, 1 << i)], axis=0)
+        gathered = [joined, swap(joined, 1 << i)]
+        if i > 0:
+            joined = join(gathered)
 
     asked = pl.pallas_call(
         functools.partial(low_rank_kernel, shape),
-        in_specs=[SMEM, VMEM, VMEM, VMEM],
+        in_specs=[SMEM, VMEM, VMEM] + [VMEM] * len(gathered),
         out_specs=VMEM,
         scratch_shapes=[pltpu.VMEM((videos, ranks, model_width), jnp.bfloat16)],
         out_shape=jax.ShapeDtypeStruct((devs, pairs * toks + toks // 2, width), jnp.bfloat16),
@@ -237,7 +293,7 @@
             transcendentals=0,
         ),
         name="low_rank",
-    )(me, normed_token_features, gathered, queries.reshape(devs, pairs * toks, width))
+    )(me, normed_token_features, queries.reshape(devs, pairs * toks, width), *gathered)
     asked = exchange(asked)
 
     part_spec = pl.BlockSpec((devs, pl.squeezed, toks, width), lambda p: (0, p, 0, 0))

time: 164 us -> 161 us (0.982)
  blocking collectives: 29.5 us -> 64.2 us
  waiting for transfers between devices: 75.3 us -> 49.7 us
  starting transfers between devices: 37.4 us -> 30.2 us
  local copies, waits for them, and re-layouts: 8.51 us -> 3.71 us
    ppermute x15, waiting for transfers between devices: 71.6 us -> 34.4 us  [swap(): return lax.ppermute(tensor, 'seq', [(i, i ^ k) for i in range(devs)])]
    all_to_all x1 -> x2, blocking collectives: 29.5 us -> 64.2 us  [exchange(): lax.all_to_all(tensor, 'seq', split_axis=0, concat_axis=0, tiled=True)]
    all_to_all x3 -> x2, waiting for transfers between devices: 3.65 us -> 15.3 us  [exchange(): lax.all_to_all(tensor, 'seq', split_axis=0, concat_axis=0, tiled=True)]
    all_to_all x3 -> x2, starting transfers between devices: 19.9 us -> 14.6 us  [exchange(): lax.all_to_all(tensor, 'seq', split_axis=0, concat_axis=0, tiled=True)]
    unnamed x29 -> x17, local copies, waits for them, and re-layouts: 7.58 us -> 3.71 us
    ppermute x15, starting transfers between devices: 17.4 us -> 15.6 us  [swap(): return lax.ppermute(tensor, 'seq', [(i, i ^ k) for i in range(devs)])]
  transfers between devices with their start and end apart: 18 -> 17, of which waited for: 11 -> 11; matrix products, arithmetic and copies ran while one was open for 2% -> 0% of each run, Pallas kernels for 2% -> 2%
where the time goes in v15:
time: 161 us
  blocking collectives  64.2 us (40%)
  waiting for transfers between devices  49.7 us (31%)
  starting transfers between devices  30.2 us (19%)
  Pallas kernels  12.9 us (8%)
  local copies, waits for them, and re-layouts  3.71 us (2%)
    all_to_all x2, blocking collectives, exchange(): lax.all_to_all(tensor, 'seq', split_axis=0, concat_axis=0, tiled=True)  64.2 us
    ppermute x15, waiting for transfers between devices, swap(): return lax.ppermute(tensor, 'seq', [(i, i ^ k) for i in range(devs)])  34.4 us
    ppermute x15, starting transfers between devices, swap(): return lax.ppermute(tensor, 'seq', [(i, i ^ k) for i in range(devs)])  15.6 us
    all_to_all x2, waiting for transfers between devices, exchange(): lax.all_to_all(tensor, 'seq', split_axis=0, concat_axis=0, tiled=True)  15.3 us
    all_to_all x2, starting transfers between devices, exchange(): lax.all_to_all(tensor, 'seq', split_axis=0, concat_axis=0, tiled=True)  14.6 us
    pallas_call x1, Pallas kernels, body(): pl.pallas_call(functools.partial(attend_kernel, math.gcd(devs, max(1, 512...  9.27 us
    unnamed x17, local copies, waits for them, and re-layouts  3.71 us
  transfers between devices with their start and end apart: 17, of which 11 were waited for; matrix products, arithmetic and copies ran while one was open for 0% of the time, Pallas kernels for 2%

profile of v15, /device:TPU:1, one launch (start us, length us, event | category | flops | bytes accessed | tf_op | source)
XLA Modules:
  0.0 160.9 jit_solution(10415243881501669645)
XLA Ops:
  0.0 7.5 %all-to-all-start = ((bf16[16,4,64,128]{3,2,1,0:T(8,128)(2,1)}), bf16[16,4,64,128]{3,2,1,0:T(8,128)(2,1)S(1)}, u32[]{:S(2)}, u32[]{:S(2)}) async-start(bf16[16,4,64,128]{3,2,1,0:T(8,128)(2,1)} %bitcast.9), calls=%async_computation | async-start | bytes 2097152 | tf_op jit(solution)/shard_map/all_to_all | solution.py:193
  7.5 0.0 copy-start
  7.5 1.7 %copy-done = bf16[4,64,5120]{2,1,0:T(8,128)(2,1)S(1)} copy-done((bf16[4,64,5120]{2,1,0:T(8,128)(2,1)S(1)}, bf16[4,64,5120]{2,1,0:T(8,128)(2,1)}, u32[]{:S(2)}) %copy-start) | copy-done | bytes 2621464
  9.3 1.5 pick_factors.1
  10.8 0.0 copy-start.4
  10.8 0.2 collective-permute-start
  11.0 2.0 %collective-permute-done.refs_1_ = bf16[8,320,128]{2,1,0:T(8,128)(2,1)S(1)} collective-permute-done((bf16[8,320,128]{2,1,0:T(8,128)(2,1)S(1)}, bf16[8,320,128]{2,1,0:T(8,128)(2,1)S(1)}, u32[]{:S(2)}, u32[]{:S(2)}) %collective-permute-start) | collective-permute-done | bytes 655392 | tf_op jit(solution)/shard_map/ppermute | solution.py:190
  13.0 0.1 halve.2
  13.1 0.2 collective-permute-start.1
  13.3 1.6 %collective-permute-start.2 = (bf16[4,320,128]{2,1,0:T(8,128)(2,1)S(1)}, bf16[4,320,128]{2,1,0:T(8,128)(2,1)S(1)}, u32[]{:S(2)}, u32[]{:S(2)}) collective-permute-start(bf16[4,320,128]{2,1,0:T(8,128)(2,1)S(1)} %halve.2), channel_id=1, source_target_pairs={{0,2},{1,3},{2,0},{3,1},{4,6},{5,7},{6,4},{7,5},{8,10},{9,11},{10,... | collective-permute-start | bytes 983048 | tf_op jit(solution)/shard_map/ppermute | solution.py:190
  14.9 0.2 collective-permute-done.1.refs_1_
  15.1 0.8 halve.3
  15.8 1.4 collective-permute-start.6
  17.2 13.4 %all-to-all-done.k_ref = bf16[16,4,64,128]{3,2,1,0:T(8,128)(2,1)S(1)} async-done(((bf16[16,4,64,128]{3,2,1,0:T(8,128)(2,1)}), bf16[16,4,64,128]{3,2,1,0:T(8,128)(2,1)S(1)}, u32[]{:S(2)}, u32[]{:S(2)}) %all-to-all-start) | async-done | bytes 1048608 | tf_op jit(solution)/shard_map/all_to_all | solution.py:193
  30.7 0.0 collective-permute-done.2.refs_2_
  30.7 1.0 copy-done.5
  31.6 0.1 split.2
  31.7 3.9 %collective-permute-start.3 = (bf16[1,320,128]{2,1,0:T(8,128)(2,1)S(1)}, bf16[1,320,128]{2,1,0:T(8,128)(2,1)S(1)}, u32[]{:S(2)}, u32[]{:S(2)}) collective-permute-start(bf16[1,320,128]{2,1,0:T(8,128)(2,1)S(1)} %get-tuple-element.33), channel_id=1, source_target_pairs={{0,8},{1,9},{2,10},{3,11},{4,12},{5,13},{6,14},{7,15},{8,0},{9,1},... | collective-permute-start | bytes 245768 | tf_op jit(solution)/shard_map/ppermute | solution.py:190
  35.6 0.0 collective-permute-start.4
  35.6 1.4 collective-permute-start.5
  37.0 0.5 collective-permute-done.3.refs_1_
  37.4 1.8 %collective-permute-done.4.refs_2_ = bf16[1,320,128]{2,1,0:T(8,128)(2,1)S(1)} collective-permute-done((bf16[1,320,128]{2,1,0:T(8,128)(2,1)S(1)}, bf16[1,320,128]{2,1,0:T(8,128)(2,1)S(1)}, u32[]{:S(2)}, u32[]{:S(2)}) %collective-permute-start.4) | collective-permute-done | bytes 81952 | tf_op jit(solution)/shard_map/ppermute | solution.py:190
  39.2 4.1 %collective-permute-done.5.refs_3_ = bf16[1,320,128]{2,1,0:T(8,128)(2,1)S(1)} collective-permute-done((bf16[1,320,128]{2,1,0:T(8,128)(2,1)S(1)}, bf16[1,320,128]{2,1,0:T(8,128)(2,1)S(1)}, u32[]{:S(2)}, u32[]{:S(2)}) %collective-permute-start.5) | collective-permute-done | bytes 81952 | tf_op jit(solution)/shard_map/ppermute | solution.py:190
  43.3 0.0 collective-permute-done.6.refs_2_
  43.3 0.1 split.3
  43.4 0.1 collective-permute-start.7
  43.5 2.4 %collective-permute-start.10 = (bf16[1,320,128]{2,1,0:T(8,128)(2,1)S(1)}, bf16[1,320,128]{2,1,0:T(8,128)(2,1)S(1)}, u32[]{:S(2)}, u32[]{:S(2)}) collective-permute-start(bf16[1,320,128]{2,1,0:T(8,128)(2,1)S(1)} %total.2.refs_0_), channel_id=1, source_target_pairs={{0,8},{1,9},{2,10},{3,11},{4,12},{5,13},{6,14},{7,15},{8,0},{9,1},... | collective-permute-start | bytes 245768 | tf_op jit(solution)/shard_map/ppermute | solution.py:190
  45.8 0.0 collective-permute-start.11
  45.8 1.3 collective-permute-start.12
  47.1 0.2 collective-permute-start.8
  47.3 1.7 %collective-permute-done.7.refs_1_ = bf16[1,256,128]{2,1,0:T(8,128)(2,1)S(1)} collective-permute-done((bf16[1,256,128]{2,1,0:T(8,128)(2,1)S(1)}, bf16[1,256,128]{2,1,0:T(8,128)(2,1)S(1)}, u32[]{:S(2)}, u32[]{:S(2)}) %collective-permute-start.7) | collective-permute-done | bytes 65568 | tf_op jit(solution)/shard_map/ppermute | solution.py:190
  49.0 0.7 collective-permute-start.9
  49.7 6.3 %collective-permute-done.8.refs_2_ = bf16[1,256,128]{2,1,0:T(8,128)(2,1)S(1)} collective-permute-done((bf16[1,256,128]{2,1,0:T(8,128)(2,1)S(1)}, bf16[1,256,128]{2,1,0:T(8,128)(2,1)S(1)}, u32[]{:S(2)}, u32[]{:S(2)}) %collective-permute-start.8) | collective-permute-done | bytes 65568 | tf_op jit(solution)/shard_map/ppermute | solution.py:190
  55.9 0.0 collective-permute-done.9.refs_3_
  56.0 0.0 collective-permute-done.10.refs_1_
  56.0 0.0 collective-permute-done.11.refs_2_
  56.0 0.0 copy-start.3
  56.0 7.2 %all-to-all-start.2 = ((bf16[16,4,64,128]{3,2,1,0:T(8,128)(2,1)}), bf16[16,4,64,128]{3,2,1,0:T(8,128)(2,1)}, u32[]{:S(2)}, u32[]{:S(2)}) async-start(bf16[16,4,64,128]{3,2,1,0:T(8,128)(2,1)} %bitcast.10), calls=%async_computation.2 | async-start | bytes 2097152 | tf_op jit(solution)/shard_map/all_to_all | solution.py:193
  63.2 1.5 collective-permute-start.13
  64.7 16.3 %collective-permute-done.13.refs_1_ = bf16[4,320,128]{2,1,0:T(8,128)(2,1)S(1)} collective-permute-done((bf16[4,320,128]{2,1,0:T(8,128)(2,1)S(1)}, bf16[4,320,128]{2,1,0:T(8,128)(2,1)S(1)}, u32[]{:S(2)}, u32[]{:S(2)}) %collective-permute-start.13) | collective-permute-done | bytes 327712 | tf_op jit(solution)/shard_map/ppermute | solution.py:190
  81.0 0.9 collective-permute-start.14
  82.0 1.7 %collective-permute-done.14.refs_1_ = bf16[8,320,128]{2,1,0:T(8,128)(2,1)S(1)} collective-permute-done((bf16[8,320,128]{2,1,0:T(8,128)(2,1)S(1)}, bf16[8,320,128]{2,1,0:T(8,128)(2,1)S(1)}, u32[]{:S(2)}, u32[]{:S(2)}) %collective-permute-start.14) | collective-permute-done | bytes 655392 | tf_op jit(solution)/shard_map/ppermute | solution.py:190
  83.7 0.9 low_rank.1
  84.6 1.9 %all-to-all-done.2.v_ref = bf16[16,4,64,128]{3,2,1,0:T(8,128)(2,1)} async-done(((bf16[16,4,64,128]{3,2,1,0:T(8,128)(2,1)}), bf16[16,4,64,128]{3,2,1,0:T(8,128)(2,1)}, u32[]{:S(2)}, u32[]{:S(2)}) %all-to-all-start.2) | async-done | bytes 1048608 | tf_op jit(solution)/shard_map/all_to_all | solution.py:193
  86.5 35.8 %all_to_all.20.q_ref.low_ref = bf16[16,288,128]{2,1,0:T(8,128)(2,1)S(1)} all-to-all(bf16[16,288,128]{2,1,0:T(8,128)(2,1)S(1)} %low_rank.1), channel_id=1, replica_groups=mesh['grp'=2,'seq'=16] {'seq'}, dimensions={0} | all-to-all | bytes 2359296 | tf_op jit(solution)/shard_map/all_to_all | solution.py:193
  122.3 9.3 %attend.1 = bf16[16,4,64,128]{3,2,1,0:T(8,128)(2,1)S(1)} custom-call(bf16[4,64,128]{2,1,0:T(8,128)(2,1)S(1)} %bitcast.7, bf16[16,288,128]{2,1,0:T(8,128)(2,1)S(1)} %all_to_all.20.q_ref.low_ref, bf16[16,288,128]{2,1,0:T(8,128)(2,1)S(1)} %all_to_all.20.q_ref.low_ref, bf16[16,4,64,128]{3,2,1,0:T(8,128)(2,1)S(1)} %all-to-all-done.k_ref, ...), custom_call_target="tpu_custom_call" | custom-call | flops 2147483648 | bytes 4194304 | tf_op jit(solution)/shard_map/attend/pallas_call | solution.py:300
  131.6 28.4 %all_to_all.21 = bf16[16,4,64,128]{3,2,1,0:T(8,128)(2,1)S(1)} all-to-all(bf16[16,4,64,128]{3,2,1,0:T(8,128)(2,1)S(1)} %attend.1), channel_id=1, replica_groups=mesh['grp'=2,'seq'=16] {'seq'}, dimensions={0} | all-to-all | bytes 2097152 | tf_op jit(solution)/shard_map/all_to_all | solution.py:193
  159.9 1.0 copy.10
  (16 shorter events, 0.2 us)
Async XLA Ops:
  0.0 7.5 %copy-start.6 = (s32[64]{0:T(128)S(1)}, s32[64]{0:T(128)}, u32[]{:S(2)}) copy-start(s32[64]{0:T(128)} %row_ref.1) | copy-start | bytes 772
  0.0 7.5 %copy-start.7 = (s32[2]{0:T(128)S(1)}, s32[2]{0:T(128)}, u32[]{:S(2)}) copy-start(s32[2]{0:T(128)} %req_ref.1) | copy-start | bytes 28
  0.0 7.5 %copy-start.1 = (bf16[4,64,4096]{2,1,0:T(8,128)(2,1)S(1)}, bf16[4,64,4096]{2,1,0:T(8,128)(2,1)}, u32[]{:S(2)}) copy-start(bf16[4,64,4096]{2,1,0:T(8,128)(2,1)} %up_ref.1) | copy-start | bytes 6291460
  0.0 30.6 %all-to-all-start = ((bf16[16,4,64,128]{3,2,1,0:T(8,128)(2,1)}), bf16[16,4,64,128]{3,2,1,0:T(8,128)(2,1)S(1)}, u32[]{:S(2)}, u32[]{:S(2)}) async-start(bf16[16,4,64,128]{3,2,1,0:T(8,128)(2,1)} %bitcast.9), calls=%async_computation | async-start | bytes 2097152 | tf_op jit(solution)/shard_map/all_to_all | solution.py:193
  7.5 1.7 %copy-start = (bf16[4,64,5120]{2,1,0:T(8,128)(2,1)S(1)}, bf16[4,64,5120]{2,1,0:T(8,128)(2,1)}, u32[]{:S(2)}) copy-start(bf16[4,64,5120]{2,1,0:T(8,128)(2,1)} %down_ref.1) | copy-start | bytes 7864324
  10.8 5.1 %copy-start.4 = (bf16[4,320,128]{2,1,0:T(8,128)(2,1)}, bf16[4,320,128]{2,1,0:T(8,128)(2,1)S(1)}, u32[]{:S(2)}) copy-start(bf16[4,320,128]{2,1,0:T(8,128)(2,1)S(1)} %get-tuple-element.31.refs_0_) | copy-start | bytes 983044
  10.8 2.2 %collective-permute-start = (bf16[8,320,128]{2,1,0:T(8,128)(2,1)S(1)}, bf16[8,320,128]{2,1,0:T(8,128)(2,1)S(1)}, u32[]{:S(2)}, u32[]{:S(2)}) collective-permute-start(bf16[8,320,128]{2,1,0:T(8,128)(2,1)S(1)} %get-tuple-element.29), channel_id=1, source_target_pairs={{0,1},{1,0},{2,3},{3,2},{4,5},{5,4},{6,7},{7,6},{8,9},{9,8},{10,11... | collective-permute-start | bytes 1966088 | tf_op jit(solution)/shard_map/ppermute | solution.py:190
  13.1 2.0 %collective-permute-start.1 = (bf16[8,256,128]{2,1,0:T(8,128)(2,1)S(1)}, bf16[8,256,128]{2,1,0:T(8,128)(2,1)S(1)}, u32[]{:S(2)}, u32[]{:S(2)}) collective-permute-start(bf16[8,256,128]{2,1,0:T(8,128)(2,1)S(1)} %get-tuple-element.30), channel_id=1, source_target_pairs={{0,1},{1,0},{2,3},{3,2},{4,5},{5,4},{6,7},{7,6},{8,9},{9,8},{10,11... | collective-permute-start | bytes 1572872 | tf_op jit(solution)/shard_map/ppermute | solution.py:190
  13.3 17.4 %collective-permute-start.2 = (bf16[4,320,128]{2,1,0:T(8,128)(2,1)S(1)}, bf16[4,320,128]{2,1,0:T(8,128)(2,1)S(1)}, u32[]{:S(2)}, u32[]{:S(2)}) collective-permute-start(bf16[4,320,128]{2,1,0:T(8,128)(2,1)S(1)} %halve.2), channel_id=1, source_target_pairs={{0,2},{1,3},{2,0},{3,1},{4,6},{5,7},{6,4},{7,5},{8,10},{9,11},{10,... | collective-permute-start | bytes 983048 | tf_op jit(solution)/shard_map/ppermute | solution.py:190
  15.8 27.5 %collective-permute-start.6 = (bf16[4,256,128]{2,1,0:T(8,128)(2,1)}, bf16[4,256,128]{2,1,0:T(8,128)(2,1)S(1)}, u32[]{:S(2)}, u32[]{:S(2)}) collective-permute-start(bf16[4,256,128]{2,1,0:T(8,128)(2,1)} %halve.3), channel_id=1, source_target_pairs={{0,2},{1,3},{2,0},{3,1},{4,6},{5,7},{6,4},{7,5},{8,10},{9,11},{10,... | collective-permute-start | bytes 786440 | tf_op jit(solution)/shard_map/ppermute | solution.py:190
  30.7 1.0 copy-start.5
  31.7 5.7 %collective-permute-start.3 = (bf16[1,320,128]{2,1,0:T(8,128)(2,1)S(1)}, bf16[1,320,128]{2,1,0:T(8,128)(2,1)S(1)}, u32[]{:S(2)}, u32[]{:S(2)}) collective-permute-start(bf16[1,320,128]{2,1,0:T(8,128)(2,1)S(1)} %get-tuple-element.33), channel_id=1, source_target_pairs={{0,8},{1,9},{2,10},{3,11},{4,12},{5,13},{6,14},{7,15},{8,0},{9,1},... | collective-permute-start | bytes 245768 | tf_op jit(solution)/shard_map/ppermute | solution.py:190
  35.6 3.6 %collective-permute-start.4 = (bf16[1,320,128]{2,1,0:T(8,128)(2,1)S(1)}, bf16[1,320,128]{2,1,0:T(8,128)(2,1)S(1)}, u32[]{:S(2)}, u32[]{:S(2)}) collective-permute-start(bf16[1,320,128]{2,1,0:T(8,128)(2,1)S(1)} %get-tuple-element.34), channel_id=1, source_target_pairs={{0,4},{1,5},{2,6},{3,7},{4,0},{5,1},{6,2},{7,3},{8,12},{9,13},{10,... | collective-permute-start | bytes 245768 | tf_op jit(solution)/shard_map/ppermute | solution.py:190
  35.6 7.7 %collective-permute-start.5 = (bf16[1,320,128]{2,1,0:T(8,128)(2,1)S(1)}, bf16[1,320,128]{2,1,0:T(8,128)(2,1)S(1)}, u32[]{:S(2)}, u32[]{:S(2)}) collective-permute-start(bf16[1,320,128]{2,1,0:T(8,128)(2,1)S(1)} %get-tuple-element.35), channel_id=1, source_target_pairs={{0,12},{1,13},{2,14},{3,15},{4,8},{5,9},{6,10},{7,11},{8,4},{9,5},... | collective-permute-start | bytes 245768 | tf_op jit(solution)/shard_map/ppermute | solution.py:190
  43.4 5.6 %collective-permute-start.7 = (bf16[1,256,128]{2,1,0:T(8,128)(2,1)S(1)}, bf16[1,256,128]{2,1,0:T(8,128)(2,1)S(1)}, u32[]{:S(2)}, u32[]{:S(2)}) collective-permute-start(bf16[1,256,128]{2,1,0:T(8,128)(2,1)S(1)} %get-tuple-element.41), channel_id=1, source_target_pairs={{0,8},{1,9},{2,10},{3,11},{4,12},{5,13},{6,14},{7,15},{8,0},{9,1},... | collective-permute-start | bytes 196616 | tf_op jit(solution)/shard_map/ppermute | solution.py:190
  43.5 12.5 %collective-permute-start.10 = (bf16[1,320,128]{2,1,0:T(8,128)(2,1)S(1)}, bf16[1,320,128]{2,1,0:T(8,128)(2,1)S(1)}, u32[]{:S(2)}, u32[]{:S(2)}) collective-permute-start(bf16[1,320,128]{2,1,0:T(8,128)(2,1)S(1)} %total.2.refs_0_), channel_id=1, source_target_pairs={{0,8},{1,9},{2,10},{3,11},{4,12},{5,13},{6,14},{7,15},{8,0},{9,1},... | collective-permute-start | bytes 245768 | tf_op jit(solution)/shard_map/ppermute | solution.py:190
  45.8 10.1 %collective-permute-start.11 = (bf16[1,320,128]{2,1,0:T(8,128)(2,1)S(1)}, bf16[1,320,128]{2,1,0:T(8,128)(2,1)S(1)}, u32[]{:S(2)}, u32[]{:S(2)}) collective-permute-start(bf16[1,320,128]{2,1,0:T(8,128)(2,1)S(1)} %total.2.refs_0_), channel_id=1, source_target_pairs={{0,4},{1,5},{2,6},{3,7},{4,0},{5,1},{6,2},{7,3},{8,12},{9,13},{10,... | collective-permute-start | bytes 245768 | tf_op jit(solution)/shard_map/ppermute | solution.py:190
  45.8 10.1 %collective-permute-start.12 = (bf16[1,320,128]{2,1,0:T(8,128)(2,1)S(1)}, bf16[1,320,128]{2,1,0:T(8,128)(2,1)S(1)}, u32[]{:S(2)}, u32[]{:S(2)}) collective-permute-start(bf16[1,320,128]{2,1,0:T(8,128)(2,1)S(1)} %total.2.refs_0_), channel_id=1, source_target_pairs={{0,12},{1,13},{2,14},{3,15},{4,8},{5,9},{6,10},{7,11},{8,4},{9,5},... | collective-permute-start | bytes 245768 | tf_op jit(solution)/shard_map/ppermute | solution.py:190
  47.1 8.8 %collective-permute-start.8 = (bf16[1,256,128]{2,1,0:T(8,128)(2,1)S(1)}, bf16[1,256,128]{2,1,0:T(8,128)(2,1)S(1)}, u32[]{:S(2)}, u32[]{:S(2)}) collective-permute-start(bf16[1,256,128]{2,1,0:T(8,128)(2,1)S(1)} %get-tuple-element.42), channel_id=1, source_target_pairs={{0,4},{1,5},{2,6},{3,7},{4,0},{5,1},{6,2},{7,3},{8,12},{9,13},{10,... | collective-permute-start | bytes 196616 | tf_op jit(solution)/shard_map/ppermute | solution.py:190
  49.0 7.0 %collective-permute-start.9 = (bf16[1,256,128]{2,1,0:T(8,128)(2,1)S(1)}, bf16[1,256,128]{2,1,0:T(8,128)(2,1)S(1)}, u32[]{:S(2)}, u32[]{:S(2)}) collective-permute-start(bf16[1,256,128]{2,1,0:T(8,128)(2,1)S(1)} %get-tuple-element.43), channel_id=1, source_target_pairs={{0,12},{1,13},{2,14},{3,15},{4,8},{5,9},{6,10},{7,11},{8,4},{9,5},... | collective-permute-start | bytes 196616 | tf_op jit(solution)/shard_map/ppermute | solution.py:190
  56.0 27.7 %copy-start.3 = (bf16[2,32,64,128]{3,2,1,0:T(8,128)(2,1)S(1)}, bf16[2,32,64,128]{3,2,1,0:T(8,128)(2,1)}, u32[]{:S(2)}) copy-start(bf16[2,32,64,128]{3,2,1,0:T(8,128)(2,1)} %param.9) | copy-start | bytes 3145732
  56.0 30.4 %all-to-all-start.2 = ((bf16[16,4,64,128]{3,2,1,0:T(8,128)(2,1)}), bf16[16,4,64,128]{3,2,1,0:T(8,128)(2,1)}, u32[]{:S(2)}, u32[]{:S(2)}) async-start(bf16[16,4,64,128]{3,2,1,0:T(8,128)(2,1)} %bitcast.10), calls=%async_computation.2 | async-start | bytes 2097152 | tf_op jit(solution)/shard_map/all_to_all | solution.py:193
  63.2 20.5 %copy-start.2 = (bf16[2,64,5120]{2,1,0:T(8,128)(2,1)S(1)}, bf16[2,64,5120]{2,1,0:T(8,128)(2,1)}, u32[]{:S(2)}) copy-start(bf16[2,64,5120]{2,1,0:T(8,128)(2,1)} %x_ref.1) | copy-start | bytes 3932164
  63.2 17.8 %collective-permute-start.13 = (bf16[4,320,128]{2,1,0:T(8,128)(2,1)S(1)}, bf16[4,320,128]{2,1,0:T(8,128)(2,1)S(1)}, u32[]{:S(2)}, u32[]{:S(2)}) collective-permute-start(bf16[4,320,128]{2,1,0:T(8,128)(2,1)S(1)} %join.2.refs_0_), channel_id=1, source_target_pairs={{0,2},{1,3},{2,0},{3,1},{4,6},{5,7},{6,4},{7,5},{8,10},{9,11},{10,... | collective-permute-start | bytes 983048 | tf_op jit(solution)/shard_map/ppermute | solution.py:190
  81.0 2.7 %collective-permute-start.14 = (bf16[8,320,128]{2,1,0:T(8,128)(2,1)S(1)}, bf16[8,320,128]{2,1,0:T(8,128)(2,1)S(1)}, u32[]{:S(2)}, u32[]{:S(2)}) collective-permute-start(bf16[8,320,128]{2,1,0:T(8,128)(2,1)S(1)} %join.3.refs_0_), channel_id=1, source_target_pairs={{0,1},{1,0},{2,3},{3,2},{4,5},{5,4},{6,7},{7,6},{8,9},{9,8},{10,11... | collective-permute-start | bytes 1966088 | tf_op jit(solution)/shard_map/ppermute | solution.py:190

commit v16 on v15

--- a/solution.py
+++ b/solution.py
@@ -102,7 +102,7 @@
     )(*arrays)
 
 
-def low_rank_kernel(shape, me_ref, x_ref, q_ref, *refs):
+def low_rank_kernel(shape, me_ref, x_ref, *refs):
     devs, bits, per_video, _, col_split, rows, tiles = shape
     parts, out_ref, down = refs[:-2], refs[-2], refs[-1]
     blocks = [(ref, i) for ref in parts for i in range(ref.shape[0])]
@@ -114,16 +114,20 @@
         for t in range(tiles):
             col = pl.multiple_of(((place % col_split) * tiles + t) * LANES, LANES)
             down[video, pl.ds(row, rows), pl.ds(col, LANES)] = ref[i, t * rows : (t + 1) * rows, :]
-    first = q_ref.shape[1]
-    out_ref[:, :first] = q_ref[...]
     for s in range(x_ref.shape[0]):
         low = lax.dot_general(
             x_ref[s], down[s], (((1,), (1,)), ((), ())), preferred_element_type=jnp.float32
         ).astype(out_ref.dtype)
         half = low.shape[0] // 2
-        low = jnp.concatenate([low[:half], low[half:]], axis=1)
-        for dev in range(s * per_video, (s + 1) * per_video):
-            out_ref[dev, first:] = low
+        out_ref[s] = jnp.concatenate([low[:half], low[half:]], axis=1)
+
+
+def choose_kernel(per_video, me_ref, *refs):
+    ins, outs = refs[:LOW], refs[LOW:]
+    for i, out in enumerate(outs):
+        video = (me_ref[0] ^ (LOW * i)) // per_video
+        for j in range(LOW):
+            out[j] = ins[j][video]
 
 
 def add_delta(base, low, up, second):
@@ -140,10 +144,13 @@
     return (base.astype(jnp.float32) + delta).astype(base.dtype).reshape(devs * toks, width)
 
 
-def attend_kernel(block, up_ref, q_ref, low_ref, k_ref, v_ref, out_ref, q_mix):
+def attend_kernel(block, me_ref, up_ref, q_ref, k_ref, v_ref, *refs):
+    low_refs, out_ref, low_all, q_mix = refs[:-3], refs[-3], refs[-2], refs[-1]
     devs, toks, width = q_ref.shape
     length = devs * toks
-    low = low_ref[...].reshape(length // 2, low_ref.shape[2])
+    for k in range(devs):
+        low_all[me_ref[0] ^ k] = low_refs[k // LOW][k % LOW]
+    low = low_all[...].reshape(length // 2, low_all.shape[2])
     up = up_ref[...]
     keys = k_ref[...].reshape(length, width)
     vals = add_delta(v_ref[...], low, up, 1)
@@ -269,23 +276,45 @@
     up_got.append(swap(part, 1 << (bits - 3)))
     held = splitting((after(down_pieces[-1], keys, *up_got[:-1]),), down_got)
     shard = after(total(held[0], to_others(held)), up_got[-1])
-    up_held = splitting((after(up_pieces[-1], shard),), up_got)
     gathered = [shard] + [swap(shard, k) for k in others]
-    up_here = total(up_held[0], to_others(up_held))
-    vals = exchange(after(by_pairs(values), *gathered, up_here))
-    up_here = up_here.reshape(pairs, ranks, LANES)
+    asked = jnp.concatenate([by_pairs(values), by_pairs(queries)], axis=1)
+    asked = exchange(after(asked, *gathered))
+
+    up_part = after(up_pieces[-1], *gathered)
+    pair_shape = (2,) + up_part.shape[1:]
+    near_pair, far_pair = on_vmem(
+        functools.partial(sum_kernel, [[(n, 2 * h) for n in range(1 + len(up_got))] for h in (0, 1)]),
+        [pair_shape] * 2,
+        "split",
+        up_part,
+        *up_got,
+    )
+    came = swap(far_pair, quarter)
+    one_shape = (1,) + up_part.shape[1:]
+    kept, sent = on_vmem(
+        functools.partial(sum_kernel, [[(n, h) for n in range(2)] for h in (0, 1)]),
+        [one_shape] * 2,
+        "split",
+        near_pair,
+        came,
+    )
+    last = swap(sent, 2 * quarter)
+    up_here = on_vmem(
+        functools.partial(sum_kernel, [[(0, 0), (1, 0)]]), [one_shape], "total", kept, last
+    )[0].reshape(pairs, ranks, LANES)
     joined = join(gathered)
     for i in reversed(range(bits - 2)):
         gathered = [joined, swap(joined, 1 << i)]
         if i > 0:
             joined = join(gathered)
 
-    asked = pl.pallas_call(
+    low_shape = (videos, toks // 2, 2 * ranks)
+    low = pl.pallas_call(
         functools.partial(low_rank_kernel, shape),
-        in_specs=[SMEM, VMEM, VMEM] + [VMEM] * len(gathered),
+        in_specs=[SMEM, VMEM] + [VMEM] * len(gathered),
         out_specs=VMEM,
         scratch_shapes=[pltpu.VMEM((videos, ranks, model_width), jnp.bfloat16)],
-        out_shape=jax.ShapeDtypeStruct((devs, pairs * toks + toks // 2, width), jnp.bfloat16),
+        out_shape=jax.ShapeDtypeStruct(low_shape, jnp.bfloat16),
         compiler_params=pltpu.CompilerParams(vmem_limit_bytes=24 << 20),
         cost_estimate=pl.CostEstimate(
             flops=2 * videos * toks * ranks * model_width,
@@ -293,23 +322,33 @@
             transcendentals=0,
         ),
         name="low_rank",
-    )(me, normed_token_features, queries.reshape(devs, pairs * toks, width), *gathered)
-    asked = exchange(asked)
+    )(me, normed_token_features, *gathered)
+    nearby = [after(low, came)] + [swap(low, k) for k in range(1, LOW)]
+    chosen = pl.pallas_call(
+        functools.partial(choose_kernel, per_video),
+        in_specs=[SMEM] + [VMEM] * LOW,
+        out_specs=[VMEM] * quarter,
+        out_shape=[jax.ShapeDtypeStruct((LOW,) + low_shape[1:], jnp.bfloat16)] * quarter,
+        cost_estimate=pl.CostEstimate(flops=0, bytes_accessed=8 * low.size, transcendentals=0),
+        name="choose",
+    )(me, *nearby)
+    lows = [chosen[0]] + [swap(chosen[i], LOW * i) for i in range(1, quarter)]
 
     part_spec = pl.BlockSpec((devs, pl.squeezed, toks, width), lambda p: (0, p, 0, 0))
+    later_spec = pl.BlockSpec((devs, pl.squeezed, toks, width), lambda p: (0, pairs + p, 0, 0))
+    low_spec = pl.BlockSpec((LOW,) + low_shape[1:], lambda p: (0, 0, 0))
     mixed = pl.pallas_call(
         functools.partial(attend_kernel, math.gcd(devs, max(1, 512 // toks))),
         grid=(pairs,),
-        in_specs=[
-            pl.BlockSpec((pl.squeezed, ranks, LANES), lambda p: (p, 0, 0)),
-            pl.BlockSpec((devs, toks, width), lambda p: (0, p, 0)),
-            pl.BlockSpec((devs, toks // 2, width), lambda p: (0, 2 * pairs, 0)),
-            part_spec,
-            part_spec,
-        ],
+        in_specs=[SMEM, pl.BlockSpec((pl.squeezed, ranks, LANES), lambda p: (p, 0, 0))]
+        + [later_spec, part_spec, part_spec]
+        + [low_spec] * quarter,
         out_specs=part_spec,
         out_shape=jax.ShapeDtypeStruct((devs, pairs, toks, width), jnp.bfloat16),
-        scratch_shapes=[pltpu.VMEM((length, width), jnp.bfloat16)],
+        scratch_shapes=[
+            pltpu.VMEM((devs,) + low_shape[1:], jnp.bfloat16),
+            pltpu.VMEM((length, width), jnp.bfloat16),
+        ],
         compiler_params=pltpu.CompilerParams(vmem_limit_bytes=48 << 20),
         cost_estimate=pl.CostEstimate(
             flops=4 * pairs * length * length * width,
@@ -317,7 +356,7 @@
             transcendentals=pairs * length * length,
         ),
         name="attend",
-    )(up_here, asked, asked, keys, vals)
+    )(me, up_here, asked, keys, asked, *lows)
     return exchange(mixed).reshape(videos, heads, toks, width)
 
 

time: 161 us -> 155 us (0.963)
  blocking collectives: 64.2 us -> 31.6 us
  waiting for transfers between devices: 49.7 us -> 63.3 us
  starting transfers between devices: 30.2 us -> 39.6 us
  other arithmetic: 0 us -> 2.77 us
    all_to_all x2 -> x1, blocking collectives: 64.2 us -> 31.6 us  [exchange(): lax.all_to_all(tensor, 'seq', split_axis=0, concat_axis=0, tiled=True)]
    ppermute x15 -> x20, waiting for transfers between devices: 34.4 us -> 49 us  [swap(): return lax.ppermute(tensor, 'seq', [(i, i ^ k) for i in range(devs)])]
    ppermute x15 -> x20, starting transfers between devices: 15.6 us -> 25.5 us  [swap(): return lax.ppermute(tensor, 'seq', [(i, i ^ k) for i in range(devs)])]
    concatenate x0 -> x1, other arithmetic: none -> 2.77 us  [body(): asked = jnp.concatenate([by_pairs(values), by_pairs(queries)], axis=1)]
    unnamed x17 -> x23, local copies, waits for them, and re-layouts: 3.71 us -> 4.08 us
  transfers between devices with their start and end apart: 17 -> 22, of which waited for: 11 -> 13; matrix products, arithmetic and copies ran while one was open for 0% -> 2% of each run, Pallas kernels for 2% -> 3%
where the time goes in v16:
time: 155 us
  waiting for transfers between devices  63.3 us (41%)
  starting transfers between devices  39.6 us (26%)
  blocking collectives  31.6 us (20%)
  Pallas kernels  13.4 us (9%)
  local copies, waits for them, and re-layouts  4.08 us (3%)
  other arithmetic  2.77 us (2%)
    ppermute x20, waiting for transfers between devices, swap(): return lax.ppermute(tensor, 'seq', [(i, i ^ k) for i in range(devs)])  49 us
    all_to_all x1, blocking collectives, exchange(): lax.all_to_all(tensor, 'seq', split_axis=0, concat_axis=0, tiled=True)  31.6 us
    ppermute x20, starting transfers between devices, swap(): return lax.ppermute(tensor, 'seq', [(i, i ^ k) for i in range(devs)])  25.5 us
    all_to_all x2, waiting for transfers between devices, exchange(): lax.all_to_all(tensor, 'seq', split_axis=0, concat_axis=0, tiled=True)  14.2 us
    all_to_all x2, starting transfers between devices, exchange(): lax.all_to_all(tensor, 'seq', split_axis=0, concat_axis=0, tiled=True)  14.1 us
    pallas_call x1, Pallas kernels, body(): pl.pallas_call(functools.partial(attend_kernel, math.gcd(devs, max(1, 512...  9.13 us
    unnamed x23, local copies, waits for them, and re-layouts  4.08 us
  transfers between devices with their start and end apart: 22, of which 13 were waited for; matrix products, arithmetic and copies ran while one was open for 2% of the time, Pallas kernels for 3%

profile of v16, /device:TPU:1, one launch (start us, length us, event | category | flops | bytes accessed | tf_op | source)
XLA Modules:
  0.0 154.8 jit_solution(2066105163719889862)
XLA Ops:
  0.0 7.5 %all-to-all-start = ((bf16[16,4,64,128]{3,2,1,0:T(8,128)(2,1)}), bf16[16,4,64,128]{3,2,1,0:T(8,128)(2,1)}, u32[]{:S(2)}, u32[]{:S(2)}) async-start(bf16[16,4,64,128]{3,2,1,0:T(8,128)(2,1)} %bitcast.8), calls=%async_computation | async-start | bytes 2097152 | tf_op jit(solution)/shard_map/all_to_all | solution.py:200
  7.5 0.0 copy-start
  7.5 1.7 %copy-done = bf16[4,64,5120]{2,1,0:T(8,128)(2,1)S(1)} copy-done((bf16[4,64,5120]{2,1,0:T(8,128)(2,1)S(1)}, bf16[4,64,5120]{2,1,0:T(8,128)(2,1)}, u32[]{:S(2)}) %copy-start) | copy-done | bytes 2621464
  9.3 1.5 pick_factors.1
  10.8 0.2 collective-permute-start
  11.0 1.9 %collective-permute-done.refs_1_ = bf16[8,320,128]{2,1,0:T(8,128)(2,1)S(1)} collective-permute-done((bf16[8,320,128]{2,1,0:T(8,128)(2,1)S(1)}, bf16[8,320,128]{2,1,0:T(8,128)(2,1)S(1)}, u32[]{:S(2)}, u32[]{:S(2)}) %collective-permute-start) | collective-permute-done | bytes 655392 | tf_op jit(solution)/shard_map/ppermute | solution.py:197
  13.0 0.1 halve.2
  13.0 0.2 collective-permute-start.1
  13.3 1.6 %collective-permute-start.2 = (bf16[4,320,128]{2,1,0:T(8,128)(2,1)S(1)}, bf16[4,320,128]{2,1,0:T(8,128)(2,1)S(1)}, u32[]{:S(2)}, u32[]{:S(2)}) collective-permute-start(bf16[4,320,128]{2,1,0:T(8,128)(2,1)S(1)} %halve.2), channel_id=1, source_target_pairs={{0,2},{1,3},{2,0},{3,1},{4,6},{5,7},{6,4},{7,5},{8,10},{9,11},{10,... | collective-permute-start | bytes 983048 | tf_op jit(solution)/shard_map/ppermute | solution.py:197
  14.8 0.2 collective-permute-done.1.refs_1_
  15.0 0.1 halve.3
  15.1 1.5 collective-permute-start.6
  16.5 14.2 %all-to-all-done.k_ref = bf16[16,4,64,128]{3,2,1,0:T(8,128)(2,1)} async-done(((bf16[16,4,64,128]{3,2,1,0:T(8,128)(2,1)}), bf16[16,4,64,128]{3,2,1,0:T(8,128)(2,1)}, u32[]{:S(2)}, u32[]{:S(2)}) %all-to-all-start) | async-done | bytes 1048608 | tf_op jit(solution)/shard_map/all_to_all | solution.py:200
  30.8 0.1 split.3
  30.9 3.9 %collective-permute-start.3 = (bf16[1,320,128]{2,1,0:T(8,128)(2,1)S(1)}, bf16[1,320,128]{2,1,0:T(8,128)(2,1)S(1)}, u32[]{:S(2)}, u32[]{:S(2)}) collective-permute-start(bf16[1,320,128]{2,1,0:T(8,128)(2,1)S(1)} %get-tuple-element.38), channel_id=1, source_target_pairs={{0,8},{1,9},{2,10},{3,11},{4,12},{5,13},{6,14},{7,15},{8,0},{9,1},... | collective-permute-start | bytes 245768 | tf_op jit(solution)/shard_map/ppermute | solution.py:197
  34.7 1.4 collective-permute-start.5
  36.1 0.5 collective-permute-done.3.refs_1_
  36.6 1.8 %collective-permute-done.4.refs_2_ = bf16[1,320,128]{2,1,0:T(8,128)(2,1)S(1)} collective-permute-done((bf16[1,320,128]{2,1,0:T(8,128)(2,1)S(1)}, bf16[1,320,128]{2,1,0:T(8,128)(2,1)S(1)}, u32[]{:S(2)}, u32[]{:S(2)}) %collective-permute-start.4) | collective-permute-done | bytes 81952 | tf_op jit(solution)/shard_map/ppermute | solution.py:197
  38.3 4.1 %collective-permute-done.5.refs_3_ = bf16[1,320,128]{2,1,0:T(8,128)(2,1)S(1)} collective-permute-done((bf16[1,320,128]{2,1,0:T(8,128)(2,1)S(1)}, bf16[1,320,128]{2,1,0:T(8,128)(2,1)S(1)}, u32[]{:S(2)}, u32[]{:S(2)}) %collective-permute-start.5) | collective-permute-done | bytes 81952 | tf_op jit(solution)/shard_map/ppermute | solution.py:197
  42.4 0.1 collective-permute-start.7
  42.5 0.6 collective-permute-start.8
  43.2 2.9 %collective-permute-start.9 = (bf16[1,320,128]{2,1,0:T(8,128)(2,1)S(1)}, bf16[1,320,128]{2,1,0:T(8,128)(2,1)S(1)}, u32[]{:S(2)}, u32[]{:S(2)}) collective-permute-start(bf16[1,320,128]{2,1,0:T(8,128)(2,1)S(1)} %total.2.refs_0_), channel_id=1, source_target_pairs={{0,12},{1,13},{2,14},{3,15},{4,8},{5,9},{6,10},{7,11},{8,4},{9,5},... | collective-permute-start | bytes 245768 | tf_op jit(solution)/shard_map/ppermute | solution.py:197
  46.1 2.8 %pad_maximum_fusion = bf16[16,8,64,128]{3,2,1,0:T(8,128)(2,1)} fusion(bf16[16,4,64,128]{3,2,1,0:T(8,128)(2,1)S(1)} %bitcast.9, bf16[16,4,64,128]{3,2,1,0:T(8,128)(2,1)} %bitcast.10), kind=kLoop, calls=%fused_computation | loop fusion | flops 1048576 | bytes 4194304 | tf_op jit(solution)/shard_map/concatenate | solution.py:280
  48.8 1.2 collective-permute-done.9.refs_3_
  50.0 6.6 %all-to-all-start.1 = ((bf16[16,8,64,128]{3,2,1,0:T(8,128)(2,1)}), bf16[16,8,64,128]{3,2,1,0:T(8,128)(2,1)S(1)}, u32[]{:S(2)}, u32[]{:S(2)}) async-start(bf16[16,8,64,128]{3,2,1,0:T(8,128)(2,1)} %pad_maximum_fusion), calls=%async_computation.1 | async-start | bytes 4194304 | tf_op jit(solution)/shard_map/all_to_all | solution.py:200
  56.6 1.5 collective-permute-start.12
  58.1 24.3 %collective-permute-done.12.refs_1_ = bf16[4,320,128]{2,1,0:T(8,128)(2,1)S(1)} collective-permute-done((bf16[4,320,128]{2,1,0:T(8,128)(2,1)S(1)}, bf16[4,320,128]{2,1,0:T(8,128)(2,1)S(1)}, u32[]{:S(2)}, u32[]{:S(2)}) %collective-permute-start.12) | collective-permute-done | bytes 327712 | tf_op jit(solution)/shard_map/ppermute | solution.py:197
  82.4 1.3 collective-permute-start.13
  83.7 0.1 split.4
  83.8 0.1 collective-permute-start.10
  83.9 10.0 %collective-permute-done.10.refs_1_ = bf16[2,256,128]{2,1,0:T(8,128)(2,1)S(1)} collective-permute-done((bf16[2,256,128]{2,1,0:T(8,128)(2,1)S(1)}, bf16[2,256,128]{2,1,0:T(8,128)(2,1)S(1)}, u32[]{:S(2)}, u32[]{:S(2)}) %collective-permute-start.10) | collective-permute-done | bytes 131104 | tf_op jit(solution)/shard_map/ppermute | solution.py:197
  93.9 3.9 %collective-permute-start.11 = (bf16[1,256,128]{2,1,0:T(8,128)(2,1)S(1)}, bf16[1,256,128]{2,1,0:T(8,128)(2,1)S(1)}, u32[]{:S(2)}, u32[]{:S(2)}) collective-permute-start(bf16[1,256,128]{2,1,0:T(8,128)(2,1)S(1)} %get-tuple-element.48), channel_id=1, source_target_pairs={{0,8},{1,9},{2,10},{3,11},{4,12},{5,13},{6,14},{7,15},{8,0},{9,1},... | collective-permute-start | bytes 196616 | tf_op jit(solution)/shard_map/ppermute | solution.py:197
  97.8 0.9 low_rank.1.refs_0_
  98.7 1.2 collective-permute-start.14
  99.9 1.3 collective-permute-start.15
  101.2 0.4 collective-permute-start.16
  101.6 0.9 collective-permute-done.15.refs_2_
  102.5 1.9 %collective-permute-done.16.refs_3_ = bf16[2,32,128]{2,1,0:T(8,128)(2,1)S(1)} collective-permute-done((bf16[2,32,128]{2,1,0:T(8,128)(2,1)S(1)}, bf16[2,32,128]{2,1,0:T(8,128)(2,1)S(1)}, u32[]{:S(2)}, u32[]{:S(2)}) %collective-permute-start.16) | collective-permute-done | bytes 16416 | tf_op jit(solution)/shard_map/ppermute | solution.py:197
  104.4 0.6 copy-done.10
  105.0 1.4 choose.1
  106.4 1.1 collective-permute-start.17
  107.5 2.5 %collective-permute-start.19 = (bf16[4,32,128]{2,1,0:T(8,128)(2,1)}, bf16[4,32,128]{2,1,0:T(8,128)(2,1)S(1)}, u32[]{:S(2)}, u32[]{:S(2)}) collective-permute-start(bf16[4,32,128]{2,1,0:T(8,128)(2,1)} %get-tuple-element.54), channel_id=1, source_target_pairs={{0,12},{1,13},{2,14},{3,15},{4,8},{5,9},{6,10},{7,11},{8,4},{9,5},... | collective-permute-start | bytes 98312 | tf_op jit(solution)/shard_map/ppermute | solution.py:197
  110.0 1.7 %collective-permute-done.18.refs_2_ = bf16[4,32,128]{2,1,0:T(8,128)(2,1)S(1)} collective-permute-done((bf16[4,32,128]{2,1,0:T(8,128)(2,1)}, bf16[4,32,128]{2,1,0:T(8,128)(2,1)S(1)}, u32[]{:S(2)}, u32[]{:S(2)}) %collective-permute-start.18) | collective-permute-done | bytes 32800 | tf_op jit(solution)/shard_map/ppermute | solution.py:197
  111.7 0.6 collective-permute-done.19.refs_3_
  112.3 0.8 copy-done.6
  113.1 9.1 %attend.1 = bf16[16,4,64,128]{3,2,1,0:T(8,128)(2,1)S(1)} custom-call(s32[1]{0:T(128)} %bitcast.me_ref, bf16[4,64,128]{2,1,0:T(8,128)(2,1)S(1)} %bitcast.6, bf16[16,8,64,128]{3,2,1,0:T(8,128)(2,1)S(1)} %all-to-all-done.1.q_ref.v_ref, bf16[16,4,64,128]{3,2,1,0:T(8,128)(2,1)} %all-to-all-done.k_ref, bf16[16,8,64,128]{3,2,1,0:T(8,128)(2,1)S(1)} %all-to-all-done.1.q_ref.v_ref, ...), custom_call_target="tpu_custom_call" | custom-call | flops 2147483648 | bytes 4194304 | tf_op jit(solution)/shard_map/attend/pallas_call | solution.py:340
  122.2 31.6 %all_to_all.15 = bf16[16,4,64,128]{3,2,1,0:T(8,128)(2,1)S(1)} all-to-all(bf16[16,4,64,128]{3,2,1,0:T(8,128)(2,1)S(1)} %attend.1), channel_id=1, replica_groups=mesh['grp'=2,'seq'=16] {'seq'}, dimensions={0} | all-to-all | bytes 2097152 | tf_op jit(solution)/shard_map/all_to_all | solution.py:200
  153.9 1.0 copy.10
  (34 shorter events, 0.2 us)
Async XLA Ops:
  0.0 7.5 %copy-start.1 = (bf16[4,64,4096]{2,1,0:T(8,128)(2,1)S(1)}, bf16[4,64,4096]{2,1,0:T(8,128)(2,1)}, u32[]{:S(2)}) copy-start(bf16[4,64,4096]{2,1,0:T(8,128)(2,1)} %up_ref.1) | copy-start | bytes 6291460
  0.0 7.5 %copy-start.4 = (s32[64]{0:T(128)S(1)}, s32[64]{0:T(128)}, u32[]{:S(2)}) copy-start(s32[64]{0:T(128)} %row_ref.1) | copy-start | bytes 772
  0.0 7.5 %copy-start.5 = (s32[2]{0:T(128)S(1)}, s32[2]{0:T(128)}, u32[]{:S(2)}) copy-start(s32[2]{0:T(128)} %req_ref.1) | copy-start | bytes 28
  0.0 30.7 %all-to-all-start = ((bf16[16,4,64,128]{3,2,1,0:T(8,128)(2,1)}), bf16[16,4,64,128]{3,2,1,0:T(8,128)(2,1)}, u32[]{:S(2)}, u32[]{:S(2)}) async-start(bf16[16,4,64,128]{3,2,1,0:T(8,128)(2,1)} %bitcast.8), calls=%async_computation | async-start | bytes 2097152 | tf_op jit(solution)/shard_map/all_to_all | solution.py:200
  7.5 1.7 %copy-start = (bf16[4,64,5120]{2,1,0:T(8,128)(2,1)S(1)}, bf16[4,64,5120]{2,1,0:T(8,128)(2,1)}, u32[]{:S(2)}) copy-start(bf16[4,64,5120]{2,1,0:T(8,128)(2,1)} %down_ref.1) | copy-start | bytes 7864324
  10.8 2.2 %collective-permute-start = (bf16[8,320,128]{2,1,0:T(8,128)(2,1)S(1)}, bf16[8,320,128]{2,1,0:T(8,128)(2,1)S(1)}, u32[]{:S(2)}, u32[]{:S(2)}) collective-permute-start(bf16[8,320,128]{2,1,0:T(8,128)(2,1)S(1)} %get-tuple-element.34), channel_id=1, source_target_pairs={{0,1},{1,0},{2,3},{3,2},{4,5},{5,4},{6,7},{7,6},{8,9},{9,8},{10,11... | collective-permute-start | bytes 1966088 | tf_op jit(solution)/shard_map/ppermute | solution.py:197
  13.0 2.0 %collective-permute-start.1 = (bf16[8,256,128]{2,1,0:T(8,128)(2,1)S(1)}, bf16[8,256,128]{2,1,0:T(8,128)(2,1)S(1)}, u32[]{:S(2)}, u32[]{:S(2)}) collective-permute-start(bf16[8,256,128]{2,1,0:T(8,128)(2,1)S(1)} %get-tuple-element.35), channel_id=1, source_target_pairs={{0,1},{1,0},{2,3},{3,2},{4,5},{5,4},{6,7},{7,6},{8,9},{9,8},{10,11... | collective-permute-start | bytes 1572872 | tf_op jit(solution)/shard_map/ppermute | solution.py:197
  13.3 17.5 %collective-permute-start.2 = (bf16[4,320,128]{2,1,0:T(8,128)(2,1)S(1)}, bf16[4,320,128]{2,1,0:T(8,128)(2,1)S(1)}, u32[]{:S(2)}, u32[]{:S(2)}) collective-permute-start(bf16[4,320,128]{2,1,0:T(8,128)(2,1)S(1)} %halve.2), channel_id=1, source_target_pairs={{0,2},{1,3},{2,0},{3,1},{4,6},{5,7},{6,4},{7,5},{8,10},{9,11},{10,... | collective-permute-start | bytes 983048 | tf_op jit(solution)/shard_map/ppermute | solution.py:197
  15.1 27.4 %collective-permute-start.6 = (bf16[4,256,128]{2,1,0:T(8,128)(2,1)S(1)}, bf16[4,256,128]{2,1,0:T(8,128)(2,1)S(1)}, u32[]{:S(2)}, u32[]{:S(2)}) collective-permute-start(bf16[4,256,128]{2,1,0:T(8,128)(2,1)S(1)} %halve.3), channel_id=1, source_target_pairs={{0,2},{1,3},{2,0},{3,1},{4,6},{5,7},{6,4},{7,5},{8,10},{9,11},{10,... | collective-permute-start | bytes 786440 | tf_op jit(solution)/shard_map/ppermute | solution.py:197
  30.8 15.3 %copy-start.7 = (bf16[2,32,64,128]{3,2,1,0:T(8,128)(2,1)S(1)}, bf16[2,32,64,128]{3,2,1,0:T(8,128)(2,1)}, u32[]{:S(2)}) copy-start(bf16[2,32,64,128]{3,2,1,0:T(8,128)(2,1)} %param.9) | copy-start | bytes 3145732
  30.9 5.7 %collective-permute-start.3 = (bf16[1,320,128]{2,1,0:T(8,128)(2,1)S(1)}, bf16[1,320,128]{2,1,0:T(8,128)(2,1)S(1)}, u32[]{:S(2)}, u32[]{:S(2)}) collective-permute-start(bf16[1,320,128]{2,1,0:T(8,128)(2,1)S(1)} %get-tuple-element.38), channel_id=1, source_target_pairs={{0,8},{1,9},{2,10},{3,11},{4,12},{5,13},{6,14},{7,15},{8,0},{9,1},... | collective-permute-start | bytes 245768 | tf_op jit(solution)/shard_map/ppermute | solution.py:197
  34.7 3.6 %collective-permute-start.4 = (bf16[1,320,128]{2,1,0:T(8,128)(2,1)S(1)}, bf16[1,320,128]{2,1,0:T(8,128)(2,1)S(1)}, u32[]{:S(2)}, u32[]{:S(2)}) collective-permute-start(bf16[1,320,128]{2,1,0:T(8,128)(2,1)S(1)} %get-tuple-element.39), channel_id=1, source_target_pairs={{0,4},{1,5},{2,6},{3,7},{4,0},{5,1},{6,2},{7,3},{8,12},{9,13},{10,... | collective-permute-start | bytes 245768 | tf_op jit(solution)/shard_map/ppermute | solution.py:197
  34.7 7.7 %collective-permute-start.5 = (bf16[1,320,128]{2,1,0:T(8,128)(2,1)S(1)}, bf16[1,320,128]{2,1,0:T(8,128)(2,1)S(1)}, u32[]{:S(2)}, u32[]{:S(2)}) collective-permute-start(bf16[1,320,128]{2,1,0:T(8,128)(2,1)S(1)} %get-tuple-element.40), channel_id=1, source_target_pairs={{0,12},{1,13},{2,14},{3,15},{4,8},{5,9},{6,10},{7,11},{8,4},{9,5},... | collective-permute-start | bytes 245768 | tf_op jit(solution)/shard_map/ppermute | solution.py:197
  42.4 6.4 %collective-permute-start.7 = (bf16[1,320,128]{2,1,0:T(8,128)(2,1)S(1)}, bf16[1,320,128]{2,1,0:T(8,128)(2,1)S(1)}, u32[]{:S(2)}, u32[]{:S(2)}) collective-permute-start(bf16[1,320,128]{2,1,0:T(8,128)(2,1)S(1)} %total.2.refs_0_), channel_id=1, source_target_pairs={{0,8},{1,9},{2,10},{3,11},{4,12},{5,13},{6,14},{7,15},{8,0},{9,1},... | collective-permute-start | bytes 245768 | tf_op jit(solution)/shard_map/ppermute | solution.py:197
  42.5 6.3 %collective-permute-start.8 = (bf16[1,320,128]{2,1,0:T(8,128)(2,1)S(1)}, bf16[1,320,128]{2,1,0:T(8,128)(2,1)S(1)}, u32[]{:S(2)}, u32[]{:S(2)}) collective-permute-start(bf16[1,320,128]{2,1,0:T(8,128)(2,1)S(1)} %total.2.refs_0_), channel_id=1, source_target_pairs={{0,4},{1,5},{2,6},{3,7},{4,0},{5,1},{6,2},{7,3},{8,12},{9,13},{10,... | collective-permute-start | bytes 245768 | tf_op jit(solution)/shard_map/ppermute | solution.py:197
  43.2 6.9 %collective-permute-start.9 = (bf16[1,320,128]{2,1,0:T(8,128)(2,1)S(1)}, bf16[1,320,128]{2,1,0:T(8,128)(2,1)S(1)}, u32[]{:S(2)}, u32[]{:S(2)}) collective-permute-start(bf16[1,320,128]{2,1,0:T(8,128)(2,1)S(1)} %total.2.refs_0_), channel_id=1, source_target_pairs={{0,12},{1,13},{2,14},{3,15},{4,8},{5,9},{6,10},{7,11},{8,4},{9,5},... | collective-permute-start | bytes 245768 | tf_op jit(solution)/shard_map/ppermute | solution.py:197
  50.0 62.3 %all-to-all-start.1 = ((bf16[16,8,64,128]{3,2,1,0:T(8,128)(2,1)}), bf16[16,8,64,128]{3,2,1,0:T(8,128)(2,1)S(1)}, u32[]{:S(2)}, u32[]{:S(2)}) async-start(bf16[16,8,64,128]{3,2,1,0:T(8,128)(2,1)} %pad_maximum_fusion), calls=%async_computation.1 | async-start | bytes 4194304 | tf_op jit(solution)/shard_map/all_to_all | solution.py:200
  56.6 41.3 %copy-start.2 = (bf16[2,64,5120]{2,1,0:T(8,128)(2,1)S(1)}, bf16[2,64,5120]{2,1,0:T(8,128)(2,1)}, u32[]{:S(2)}) copy-start(bf16[2,64,5120]{2,1,0:T(8,128)(2,1)} %x_ref.1) | copy-start | bytes 3932164
  56.6 25.7 %collective-permute-start.12 = (bf16[4,320,128]{2,1,0:T(8,128)(2,1)S(1)}, bf16[4,320,128]{2,1,0:T(8,128)(2,1)S(1)}, u32[]{:S(2)}, u32[]{:S(2)}) collective-permute-start(bf16[4,320,128]{2,1,0:T(8,128)(2,1)S(1)} %join.2.refs_0_), channel_id=1, source_target_pairs={{0,2},{1,3},{2,0},{3,1},{4,6},{5,7},{6,4},{7,5},{8,10},{9,11},{10,... | collective-permute-start | bytes 983048 | tf_op jit(solution)/shard_map/ppermute | solution.py:197
  82.4 15.4 %collective-permute-start.13 = (bf16[8,320,128]{2,1,0:T(8,128)(2,1)S(1)}, bf16[8,320,128]{2,1,0:T(8,128)(2,1)S(1)}, u32[]{:S(2)}, u32[]{:S(2)}) collective-permute-start(bf16[8,320,128]{2,1,0:T(8,128)(2,1)S(1)} %join.3.refs_0_), channel_id=1, source_target_pairs={{0,1},{1,0},{2,3},{3,2},{4,5},{5,4},{6,7},{7,6},{8,9},{9,8},{10,11... | collective-permute-start | bytes 1966088 | tf_op jit(solution)/shard_map/ppermute | solution.py:197
  83.8 10.1 %collective-permute-start.10 = (bf16[2,256,128]{2,1,0:T(8,128)(2,1)S(1)}, bf16[2,256,128]{2,1,0:T(8,128)(2,1)S(1)}, u32[]{:S(2)}, u32[]{:S(2)}) collective-permute-start(bf16[2,256,128]{2,1,0:T(8,128)(2,1)S(1)} %get-tuple-element.46), channel_id=1, source_target_pairs={{0,4},{1,5},{2,6},{3,7},{4,0},{5,1},{6,2},{7,3},{8,12},{9,13},{10,... | collective-permute-start | bytes 393224 | tf_op jit(solution)/shard_map/ppermute | solution.py:197
  93.9 16.1 %collective-permute-start.11 = (bf16[1,256,128]{2,1,0:T(8,128)(2,1)S(1)}, bf16[1,256,128]{2,1,0:T(8,128)(2,1)S(1)}, u32[]{:S(2)}, u32[]{:S(2)}) collective-permute-start(bf16[1,256,128]{2,1,0:T(8,128)(2,1)S(1)} %get-tuple-element.48), channel_id=1, source_target_pairs={{0,8},{1,9},{2,10},{3,11},{4,12},{5,13},{6,14},{7,15},{8,0},{9,1},... | collective-permute-start | bytes 196616 | tf_op jit(solution)/shard_map/ppermute | solution.py:197
  98.7 5.7 %copy-start.3 = (bf16[2,32,128]{2,1,0:T(8,128)(2,1)}, bf16[2,32,128]{2,1,0:T(8,128)(2,1)S(1)}, u32[]{:S(2)}) copy-start(bf16[2,32,128]{2,1,0:T(8,128)(2,1)S(1)} %low_rank.1.refs_0_) | copy-start | bytes 49156
  98.7 2.9 %collective-permute-start.14 = (bf16[2,32,128]{2,1,0:T(8,128)(2,1)S(1)}, bf16[2,32,128]{2,1,0:T(8,128)(2,1)S(1)}, u32[]{:S(2)}, u32[]{:S(2)}) collective-permute-start(bf16[2,32,128]{2,1,0:T(8,128)(2,1)S(1)} %low_rank.1.refs_0_), channel_id=1, source_target_pairs={{0,1},{1,0},{2,3},{3,2},{4,5},{5,4},{6,7},{7,6},{8,9},{9,8},{10,11... | collective-permute-start | bytes 49160 | tf_op jit(solution)/shard_map/ppermute | solution.py:197
  99.9 2.6 %collective-permute-start.15 = (bf16[2,32,128]{2,1,0:T(8,128)(2,1)S(1)}, bf16[2,32,128]{2,1,0:T(8,128)(2,1)S(1)}, u32[]{:S(2)}, u32[]{:S(2)}) collective-permute-start(bf16[2,32,128]{2,1,0:T(8,128)(2,1)S(1)} %low_rank.1.refs_0_), channel_id=1, source_target_pairs={{0,2},{1,3},{2,0},{3,1},{4,6},{5,7},{6,4},{7,5},{8,10},{9,11},{10,... | collective-permute-start | bytes 49160 | tf_op jit(solution)/shard_map/ppermute | solution.py:197
  101.2 3.2 %collective-permute-start.16 = (bf16[2,32,128]{2,1,0:T(8,128)(2,1)S(1)}, bf16[2,32,128]{2,1,0:T(8,128)(2,1)S(1)}, u32[]{:S(2)}, u32[]{:S(2)}) collective-permute-start(bf16[2,32,128]{2,1,0:T(8,128)(2,1)S(1)} %low_rank.1.refs_0_), channel_id=1, source_target_pairs={{0,3},{1,2},{2,1},{3,0},{4,7},{5,6},{6,5},{7,4},{8,11},{9,10},{10,... | collective-permute-start | bytes 49160 | tf_op jit(solution)/shard_map/ppermute | solution.py:197
  101.6 2.8 %copy-start.8 = (bf16[2,32,128]{2,1,0:T(8,128)(2,1)}, bf16[2,32,128]{2,1,0:T(8,128)(2,1)S(1)}, u32[]{:S(2)}) copy-start(bf16[2,32,128]{2,1,0:T(8,128)(2,1)S(1)} %collective-permute-done.14.refs_1_) | copy-start | bytes 49156
  102.5 1.9 %copy-start.9 = (bf16[2,32,128]{2,1,0:T(8,128)(2,1)}, bf16[2,32,128]{2,1,0:T(8,128)(2,1)S(1)}, u32[]{:S(2)}) copy-start(bf16[2,32,128]{2,1,0:T(8,128)(2,1)S(1)} %collective-permute-done.15.refs_2_) | copy-start | bytes 49156
  104.4 0.6 copy-start.10
  106.4 3.6 %collective-permute-start.17 = (bf16[4,32,128]{2,1,0:T(8,128)(2,1)}, bf16[4,32,128]{2,1,0:T(8,128)(2,1)S(1)}, u32[]{:S(2)}, u32[]{:S(2)}) collective-permute-start(bf16[4,32,128]{2,1,0:T(8,128)(2,1)} %get-tuple-element.52), channel_id=1, source_target_pairs={{0,4},{1,5},{2,6},{3,7},{4,0},{5,1},{6,2},{7,3},{8,12},{9,13},{10,... | collective-permute-start | bytes 98312 | tf_op jit(solution)/shard_map/ppermute | solution.py:197
  107.5 4.2 %collective-permute-start.18 = (bf16[4,32,128]{2,1,0:T(8,128)(2,1)}, bf16[4,32,128]{2,1,0:T(8,128)(2,1)S(1)}, u32[]{:S(2)}, u32[]{:S(2)}) collective-permute-start(bf16[4,32,128]{2,1,0:T(8,128)(2,1)} %get-tuple-element.53), channel_id=1, source_target_pairs={{0,8},{1,9},{2,10},{3,11},{4,12},{5,13},{6,14},{7,15},{8,0},{9,1},... | collective-permute-start | bytes 98312 | tf_op jit(solution)/shard_map/ppermute | solution.py:197
  107.5 4.9 %collective-permute-start.19 = (bf16[4,32,128]{2,1,0:T(8,128)(2,1)}, bf16[4,32,128]{2,1,0:T(8,128)(2,1)S(1)}, u32[]{:S(2)}, u32[]{:S(2)}) collective-permute-start(bf16[4,32,128]{2,1,0:T(8,128)(2,1)} %get-tuple-element.54), channel_id=1, source_target_pairs={{0,12},{1,13},{2,14},{3,15},{4,8},{5,9},{6,10},{7,11},{8,4},{9,5},... | collective-permute-start | bytes 98312 | tf_op jit(solution)/shard_map/ppermute | solution.py:197
  112.3 0.8 copy-start.6

commit v17 on v16

--- a/solution.py
+++ b/solution.py
@@ -277,8 +277,8 @@
     held = splitting((after(down_pieces[-1], keys, *up_got[:-1]),), down_got)
     shard = after(total(held[0], to_others(held)), up_got[-1])
     gathered = [shard] + [swap(shard, k) for k in others]
-    asked = jnp.concatenate([by_pairs(values), by_pairs(queries)], axis=1)
-    asked = exchange(after(asked, *gathered))
+    vals = exchange(after(by_pairs(values), *gathered))
+    asked = exchange(after(by_pairs(queries), vals))
 
     up_part = after(up_pieces[-1], *gathered)
     pair_shape = (2,) + up_part.shape[1:]
@@ -306,7 +306,7 @@
     for i in reversed(range(bits - 2)):
         gathered = [joined, swap(joined, 1 << i)]
         if i > 0:
-            joined = join(gathered)
+            joined = after(join(gathered), came)
 
     low_shape = (videos, toks // 2, 2 * ranks)
     low = pl.pallas_call(
@@ -323,7 +323,7 @@
         ),
         name="low_rank",
     )(me, normed_token_features, *gathered)
-    nearby = [after(low, came)] + [swap(low, k) for k in range(1, LOW)]
+    nearby = [low] + [swap(low, k) for k in range(1, LOW)]
     chosen = pl.pallas_call(
         functools.partial(choose_kernel, per_video),
         in_specs=[SMEM] + [VMEM] * LOW,
@@ -335,13 +335,12 @@
     lows = [chosen[0]] + [swap(chosen[i], LOW * i) for i in range(1, quarter)]
 
     part_spec = pl.BlockSpec((devs, pl.squeezed, toks, width), lambda p: (0, p, 0, 0))
-    later_spec = pl.BlockSpec((devs, pl.squeezed, toks, width), lambda p: (0, pairs + p, 0, 0))
     low_spec = pl.BlockSpec((LOW,) + low_shape[1:], lambda p: (0, 0, 0))
     mixed = pl.pallas_call(
         functools.partial(attend_kernel, math.gcd(devs, max(1, 512 // toks))),
         grid=(pairs,),
         in_specs=[SMEM, pl.BlockSpec((pl.squeezed, ranks, LANES), lambda p: (p, 0, 0))]
-        + [later_spec, part_spec, part_spec]
+        + [part_spec] * 3
         + [low_spec] * quarter,
         out_specs=part_spec,
         out_shape=jax.ShapeDtypeStruct((devs, pairs, toks, width), jnp.bfloat16),
@@ -356,7 +355,7 @@
             transcendentals=pairs * length * length,
         ),
         name="attend",
-    )(me, up_here, asked, keys, asked, *lows)
+    )(me, up_here, asked, keys, vals, *lows)
     return exchange(mixed).reshape(videos, heads, toks, width)
 
 

time: 155 us -> 168 us (1.084)
  blocking collectives: 31.6 us -> 62.9 us
  waiting for transfers between devices: 63.3 us -> 49 us
  other arithmetic: 2.77 us -> 0 us
  starting transfers between devices: 39.6 us -> 37.4 us
    all_to_all x1 -> x2, blocking collectives: 31.6 us -> 62.9 us  [exchange(): lax.all_to_all(tensor, 'seq', split_axis=0, concat_axis=0, tiled=True)]
    ppermute x20, waiting for transfers between devices: 49 us -> 35.6 us  [swap(): return lax.ppermute(tensor, 'seq', [(i, i ^ k) for i in range(devs)])]
    concatenate x1 -> x0, other arithmetic: 2.77 us -> none  [body(): asked = jnp.concatenate([by_pairs(values), by_pairs(queries)], axis=1)]
    all_to_all x2, starting transfers between devices: 14.1 us -> 12.1 us  [exchange(): lax.all_to_all(tensor, 'seq', split_axis=0, concat_axis=0, tiled=True)]
    unnamed x23 -> x29, local copies, waits for them, and re-layouts: 4.08 us -> 4.09 us
  transfers between devices with their start and end apart: 22 -> 22, of which waited for: 13 -> 14; matrix products, arithmetic and copies ran while one was open for 2% -> 0% of each run, Pallas kernels for 3% -> 3%
where the time goes in v17:
time: 168 us
  blocking collectives  62.9 us (37%)
  waiting for transfers between devices  49 us (29%)
  starting transfers between devices  37.4 us (22%)
  Pallas kernels  14.1 us (8%)
  local copies, waits for them, and re-layouts  4.09 us (2%)
    all_to_all x2, blocking collectives, exchange(): lax.all_to_all(tensor, 'seq', split_axis=0, concat_axis=0, tiled=True)  62.9 us
    ppermute x20, waiting for transfers between devices, swap(): return lax.ppermute(tensor, 'seq', [(i, i ^ k) for i in range(devs)])  35.6 us
    ppermute x20, starting transfers between devices, swap(): return lax.ppermute(tensor, 'seq', [(i, i ^ k) for i in range(devs)])  25.3 us
    all_to_all x2, waiting for transfers between devices, exchange(): lax.all_to_all(tensor, 'seq', split_axis=0, concat_axis=0, tiled=True)  13.4 us
    all_to_all x2, starting transfers between devices, exchange(): lax.all_to_all(tensor, 'seq', split_axis=0, concat_axis=0, tiled=True)  12.1 us
    pallas_call x1, Pallas kernels, body(): pl.pallas_call(functools.partial(attend_kernel, math.gcd(devs, max(1, 512...  9.07 us
    unnamed x29, local copies, waits for them, and re-layouts  4.09 us
  transfers between devices with their start and end apart: 22, of which 14 were waited for; matrix products, arithmetic and copies ran while one was open for 0% of the time, Pallas kernels for 3%

profile of v17, /device:TPU:1, one launch (start us, length us, event | category | flops | bytes accessed | tf_op | source)
XLA Modules:
  0.0 167.7 jit_solution(8411609935195458920)
XLA Ops:
  0.0 7.5 %all-to-all-start = ((bf16[16,4,64,128]{3,2,1,0:T(8,128)(2,1)}), bf16[16,4,64,128]{3,2,1,0:T(8,128)(2,1)S(1)}, u32[]{:S(2)}, u32[]{:S(2)}) async-start(bf16[16,4,64,128]{3,2,1,0:T(8,128)(2,1)} %bitcast.8), calls=%async_computation | async-start | bytes 2097152 | tf_op jit(solution)/shard_map/all_to_all | solution.py:200
  7.5 1.7 %copy-done = bf16[4,64,5120]{2,1,0:T(8,128)(2,1)S(1)} copy-done((bf16[4,64,5120]{2,1,0:T(8,128)(2,1)S(1)}, bf16[4,64,5120]{2,1,0:T(8,128)(2,1)}, u32[]{:S(2)}) %copy-start) | copy-done | bytes 2621464
  9.3 1.5 pick_factors.1
  10.8 0.2 collective-permute-start
  11.0 2.0 %collective-permute-done.refs_1_ = bf16[8,320,128]{2,1,0:T(8,128)(2,1)S(1)} collective-permute-done((bf16[8,320,128]{2,1,0:T(8,128)(2,1)S(1)}, bf16[8,320,128]{2,1,0:T(8,128)(2,1)S(1)}, u32[]{:S(2)}, u32[]{:S(2)}) %collective-permute-start) | collective-permute-done | bytes 655392 | tf_op jit(solution)/shard_map/ppermute | solution.py:197
  13.0 0.1 halve.2
  13.1 0.2 collective-permute-start.1
  13.3 1.6 collective-permute-start.2
  14.9 0.2 collective-permute-done.1.refs_1_
  15.1 0.8 halve.3
  15.8 1.4 collective-permute-start.6
  17.2 13.4 %all-to-all-done.k_ref = bf16[16,4,64,128]{3,2,1,0:T(8,128)(2,1)S(1)} async-done(((bf16[16,4,64,128]{3,2,1,0:T(8,128)(2,1)}), bf16[16,4,64,128]{3,2,1,0:T(8,128)(2,1)S(1)}, u32[]{:S(2)}, u32[]{:S(2)}) %all-to-all-start) | async-done | bytes 1048608 | tf_op jit(solution)/shard_map/all_to_all | solution.py:200
  30.7 0.1 split.3
  30.8 3.9 %collective-permute-start.3 = (bf16[1,320,128]{2,1,0:T(8,128)(2,1)S(1)}, bf16[1,320,128]{2,1,0:T(8,128)(2,1)S(1)}, u32[]{:S(2)}, u32[]{:S(2)}) collective-permute-start(bf16[1,320,128]{2,1,0:T(8,128)(2,1)S(1)} %get-tuple-element.39), channel_id=1, source_target_pairs={{0,8},{1,9},{2,10},{3,11},{4,12},{5,13},{6,14},{7,15},{8,0},{9,1},... | collective-permute-start | bytes 245768 | tf_op jit(solution)/shard_map/ppermute | solution.py:197
  34.6 1.4 collective-permute-start.5
  36.0 0.5 collective-permute-done.3.refs_1_
  36.5 1.8 %collective-permute-done.4.refs_2_ = bf16[1,320,128]{2,1,0:T(8,128)(2,1)S(1)} collective-permute-done((bf16[1,320,128]{2,1,0:T(8,128)(2,1)S(1)}, bf16[1,320,128]{2,1,0:T(8,128)(2,1)S(1)}, u32[]{:S(2)}, u32[]{:S(2)}) %collective-permute-start.4) | collective-permute-done | bytes 81952 | tf_op jit(solution)/shard_map/ppermute | solution.py:197
  38.2 4.1 %collective-permute-done.5.refs_3_ = bf16[1,320,128]{2,1,0:T(8,128)(2,1)S(1)} collective-permute-done((bf16[1,320,128]{2,1,0:T(8,128)(2,1)S(1)}, bf16[1,320,128]{2,1,0:T(8,128)(2,1)S(1)}, u32[]{:S(2)}, u32[]{:S(2)}) %collective-permute-start.5) | collective-permute-done | bytes 81952 | tf_op jit(solution)/shard_map/ppermute | solution.py:197
  42.3 0.1 collective-permute-start.7
  42.4 0.6 collective-permute-start.8
  43.1 2.9 %collective-permute-start.9 = (bf16[1,320,128]{2,1,0:T(8,128)(2,1)S(1)}, bf16[1,320,128]{2,1,0:T(8,128)(2,1)S(1)}, u32[]{:S(2)}, u32[]{:S(2)}) collective-permute-start(bf16[1,320,128]{2,1,0:T(8,128)(2,1)S(1)} %total.2.refs_0_), channel_id=1, source_target_pairs={{0,12},{1,13},{2,14},{3,15},{4,8},{5,9},{6,10},{7,11},{8,4},{9,5},... | collective-permute-start | bytes 245768 | tf_op jit(solution)/shard_map/ppermute | solution.py:197
  46.0 0.7 collective-permute-done.7.refs_1_
  46.7 3.2 %collective-permute-done.9.refs_3_ = bf16[1,320,128]{2,1,0:T(8,128)(2,1)S(1)} collective-permute-done((bf16[1,320,128]{2,1,0:T(8,128)(2,1)S(1)}, bf16[1,320,128]{2,1,0:T(8,128)(2,1)S(1)}, u32[]{:S(2)}, u32[]{:S(2)}) %collective-permute-start.9) | collective-permute-done | bytes 81952 | tf_op jit(solution)/shard_map/ppermute | solution.py:197
  49.9 31.7 %all_to_all.20.v_ref = bf16[16,4,64,128]{3,2,1,0:T(8,128)(2,1)} all-to-all(bf16[16,4,64,128]{3,2,1,0:T(8,128)(2,1)S(1)} %bitcast.9), channel_id=1, replica_groups=mesh['grp'=2,'seq'=16] {'seq'}, dimensions={0} | all-to-all | bytes 2097152 | tf_op jit(solution)/shard_map/all_to_all | solution.py:200
  81.6 4.6 %all-to-all-start.2 = ((bf16[16,4,64,128]{3,2,1,0:T(8,128)(2,1)}), bf16[16,4,64,128]{3,2,1,0:T(8,128)(2,1)}, u32[]{:S(2)}, u32[]{:S(2)}) async-start(bf16[16,4,64,128]{3,2,1,0:T(8,128)(2,1)} %bitcast.10), calls=%async_computation.2 | async-start | bytes 2097152 | tf_op jit(solution)/shard_map/all_to_all | solution.py:200
  86.3 1.5 collective-permute-start.12
  87.7 0.1 split.4
  87.8 1.2 collective-permute-start.10
  89.1 15.0 %collective-permute-done.12.refs_1_ = bf16[4,320,128]{2,1,0:T(8,128)(2,1)S(1)} collective-permute-done((bf16[4,320,128]{2,1,0:T(8,128)(2,1)S(1)}, bf16[4,320,128]{2,1,0:T(8,128)(2,1)S(1)}, u32[]{:S(2)}, u32[]{:S(2)}) %collective-permute-start.12) | collective-permute-done | bytes 327712 | tf_op jit(solution)/shard_map/ppermute | solution.py:197
  104.1 2.7 %collective-permute-done.10.refs_1_ = bf16[2,256,128]{2,1,0:T(8,128)(2,1)S(1)} collective-permute-done((bf16[2,256,128]{2,1,0:T(8,128)(2,1)S(1)}, bf16[2,256,128]{2,1,0:T(8,128)(2,1)S(1)}, u32[]{:S(2)}, u32[]{:S(2)}) %collective-permute-start.10) | collective-permute-done | bytes 131104 | tf_op jit(solution)/shard_map/ppermute | solution.py:197
  106.8 0.6 collective-permute-start.13
  107.4 4.1 %collective-permute-start.11 = (bf16[1,256,128]{2,1,0:T(8,128)(2,1)S(1)}, bf16[1,256,128]{2,1,0:T(8,128)(2,1)S(1)}, u32[]{:S(2)}, u32[]{:S(2)}) collective-permute-start(bf16[1,256,128]{2,1,0:T(8,128)(2,1)S(1)} %get-tuple-element.49), channel_id=1, source_target_pairs={{0,8},{1,9},{2,10},{3,11},{4,12},{5,13},{6,14},{7,15},{8,0},{9,1},... | collective-permute-start | bytes 196616 | tf_op jit(solution)/shard_map/ppermute | solution.py:197
  111.5 0.9 low_rank.1.refs_0_
  112.3 0.3 collective-permute-start.14
  112.7 1.2 collective-permute-start.15
  113.9 0.7 collective-permute-start.16
  114.5 1.0 collective-permute-done.15.refs_2_
  115.5 1.6 collective-permute-done.16.refs_3_
  117.2 0.6 copy-done.13
  117.8 1.4 choose.1
  119.2 1.7 %collective-permute-start.18 = (bf16[4,32,128]{2,1,0:T(8,128)(2,1)}, bf16[4,32,128]{2,1,0:T(8,128)(2,1)S(1)}, u32[]{:S(2)}, u32[]{:S(2)}) collective-permute-start(bf16[4,32,128]{2,1,0:T(8,128)(2,1)} %get-tuple-element.55), channel_id=1, source_target_pairs={{0,8},{1,9},{2,10},{3,11},{4,12},{5,13},{6,14},{7,15},{8,0},{9,1},... | collective-permute-start | bytes 98312 | tf_op jit(solution)/shard_map/ppermute | solution.py:197
  120.9 1.9 %collective-permute-start.19 = (bf16[4,32,128]{2,1,0:T(8,128)(2,1)}, bf16[4,32,128]{2,1,0:T(8,128)(2,1)S(1)}, u32[]{:S(2)}, u32[]{:S(2)}) collective-permute-start(bf16[4,32,128]{2,1,0:T(8,128)(2,1)} %get-tuple-element.56), channel_id=1, source_target_pairs={{0,12},{1,13},{2,14},{3,15},{4,8},{5,9},{6,10},{7,11},{8,4},{9,5},... | collective-permute-start | bytes 98312 | tf_op jit(solution)/shard_map/ppermute | solution.py:197
  122.8 0.5 collective-permute-done.18.refs_2_
  123.2 2.5 %collective-permute-done.19.refs_3_ = bf16[4,32,128]{2,1,0:T(8,128)(2,1)S(1)} collective-permute-done((bf16[4,32,128]{2,1,0:T(8,128)(2,1)}, bf16[4,32,128]{2,1,0:T(8,128)(2,1)S(1)}, u32[]{:S(2)}, u32[]{:S(2)}) %collective-permute-start.19) | collective-permute-done | bytes 32800 | tf_op jit(solution)/shard_map/ppermute | solution.py:197
  125.7 0.8 copy-done.9
  126.5 9.1 %attend.1 = bf16[16,4,64,128]{3,2,1,0:T(8,128)(2,1)S(1)} custom-call(s32[1]{0:T(128)} %bitcast.me_ref, bf16[4,64,128]{2,1,0:T(8,128)(2,1)S(1)} %bitcast.6, bf16[16,4,64,128]{3,2,1,0:T(8,128)(2,1)} %all-to-all-done.2.q_ref, bf16[16,4,64,128]{3,2,1,0:T(8,128)(2,1)S(1)} %all-to-all-done.k_ref, bf16[16,4,64,128]{3,2,1,0:T(8,128)(2,1)S(1)} %copy-done.3, ...), custom_call_target="tpu_custom_call" | custom-call | flops 2147483648 | bytes 4194304 | tf_op jit(solution)/shard_map/attend/pallas_call | solution.py:339
  135.6 31.2 %all_to_all.21 = bf16[16,4,64,128]{3,2,1,0:T(8,128)(2,1)S(1)} all-to-all(bf16[16,4,64,128]{3,2,1,0:T(8,128)(2,1)S(1)} %attend.1), channel_id=1, replica_groups=mesh['grp'=2,'seq'=16] {'seq'}, dimensions={0} | all-to-all | bytes 2097152 | tf_op jit(solution)/shard_map/all_to_all | solution.py:200
  166.8 1.0 copy.10
  (40 shorter events, 0.2 us)
Async XLA Ops:
  0.0 7.5 %copy-start.1 = (bf16[4,64,4096]{2,1,0:T(8,128)(2,1)S(1)}, bf16[4,64,4096]{2,1,0:T(8,128)(2,1)}, u32[]{:S(2)}) copy-start(bf16[4,64,4096]{2,1,0:T(8,128)(2,1)} %up_ref.1) | copy-start | bytes 6291460
  0.0 7.5 %copy-start.7 = (s32[64]{0:T(128)S(1)}, s32[64]{0:T(128)}, u32[]{:S(2)}) copy-start(s32[64]{0:T(128)} %row_ref.1) | copy-start | bytes 772
  0.0 7.5 %copy-start.8 = (s32[2]{0:T(128)S(1)}, s32[2]{0:T(128)}, u32[]{:S(2)}) copy-start(s32[2]{0:T(128)} %req_ref.1) | copy-start | bytes 28
  0.0 30.6 %all-to-all-start = ((bf16[16,4,64,128]{3,2,1,0:T(8,128)(2,1)}), bf16[16,4,64,128]{3,2,1,0:T(8,128)(2,1)S(1)}, u32[]{:S(2)}, u32[]{:S(2)}) async-start(bf16[16,4,64,128]{3,2,1,0:T(8,128)(2,1)} %bitcast.8), calls=%async_computation | async-start | bytes 2097152 | tf_op jit(solution)/shard_map/all_to_all | solution.py:200
  7.5 1.7 %copy-start = (bf16[4,64,5120]{2,1,0:T(8,128)(2,1)S(1)}, bf16[4,64,5120]{2,1,0:T(8,128)(2,1)}, u32[]{:S(2)}) copy-start(bf16[4,64,5120]{2,1,0:T(8,128)(2,1)} %down_ref.1) | copy-start | bytes 7864324
  10.8 5.1 %copy-start.4 = (bf16[4,256,128]{2,1,0:T(8,128)(2,1)}, bf16[4,256,128]{2,1,0:T(8,128)(2,1)S(1)}, u32[]{:S(2)}) copy-start(bf16[4,256,128]{2,1,0:T(8,128)(2,1)S(1)} %get-tuple-element.45.refs_0_) | copy-start | bytes 786436
  10.8 2.2 %collective-permute-start = (bf16[8,320,128]{2,1,0:T(8,128)(2,1)S(1)}, bf16[8,320,128]{2,1,0:T(8,128)(2,1)S(1)}, u32[]{:S(2)}, u32[]{:S(2)}) collective-permute-start(bf16[8,320,128]{2,1,0:T(8,128)(2,1)S(1)} %get-tuple-element.35), channel_id=1, source_target_pairs={{0,1},{1,0},{2,3},{3,2},{4,5},{5,4},{6,7},{7,6},{8,9},{9,8},{10,11... | collective-permute-start | bytes 1966088 | tf_op jit(solution)/shard_map/ppermute | solution.py:197
  13.1 2.0 %collective-permute-start.1 = (bf16[8,256,128]{2,1,0:T(8,128)(2,1)S(1)}, bf16[8,256,128]{2,1,0:T(8,128)(2,1)S(1)}, u32[]{:S(2)}, u32[]{:S(2)}) collective-permute-start(bf16[8,256,128]{2,1,0:T(8,128)(2,1)S(1)} %get-tuple-element.36), channel_id=1, source_target_pairs={{0,1},{1,0},{2,3},{3,2},{4,5},{5,4},{6,7},{7,6},{8,9},{9,8},{10,11... | collective-permute-start | bytes 1572872 | tf_op jit(solution)/shard_map/ppermute | solution.py:197
  13.3 17.4 %collective-permute-start.2 = (bf16[4,320,128]{2,1,0:T(8,128)(2,1)S(1)}, bf16[4,320,128]{2,1,0:T(8,128)(2,1)S(1)}, u32[]{:S(2)}, u32[]{:S(2)}) collective-permute-start(bf16[4,320,128]{2,1,0:T(8,128)(2,1)S(1)} %halve.2), channel_id=1, source_target_pairs={{0,2},{1,3},{2,0},{3,1},{4,6},{5,7},{6,4},{7,5},{8,10},{9,11},{10,... | collective-permute-start | bytes 983048 | tf_op jit(solution)/shard_map/ppermute | solution.py:197
  15.8 26.5 %collective-permute-start.6 = (bf16[4,256,128]{2,1,0:T(8,128)(2,1)}, bf16[4,256,128]{2,1,0:T(8,128)(2,1)S(1)}, u32[]{:S(2)}, u32[]{:S(2)}) collective-permute-start(bf16[4,256,128]{2,1,0:T(8,128)(2,1)} %halve.3), channel_id=1, source_target_pairs={{0,2},{1,3},{2,0},{3,1},{4,6},{5,7},{6,4},{7,5},{8,10},{9,11},{10,... | collective-permute-start | bytes 786440 | tf_op jit(solution)/shard_map/ppermute | solution.py:197
  30.7 19.3 %copy-start.10 = (bf16[2,32,64,128]{3,2,1,0:T(8,128)(2,1)S(1)}, bf16[2,32,64,128]{3,2,1,0:T(8,128)(2,1)}, u32[]{:S(2)}) copy-start(bf16[2,32,64,128]{3,2,1,0:T(8,128)(2,1)} %param.11) | copy-start | bytes 3145732
  30.8 5.7 %collective-permute-start.3 = (bf16[1,320,128]{2,1,0:T(8,128)(2,1)S(1)}, bf16[1,320,128]{2,1,0:T(8,128)(2,1)S(1)}, u32[]{:S(2)}, u32[]{:S(2)}) collective-permute-start(bf16[1,320,128]{2,1,0:T(8,128)(2,1)S(1)} %get-tuple-element.39), channel_id=1, source_target_pairs={{0,8},{1,9},{2,10},{3,11},{4,12},{5,13},{6,14},{7,15},{8,0},{9,1},... | collective-permute-start | bytes 245768 | tf_op jit(solution)/shard_map/ppermute | solution.py:197
  34.6 3.6 %collective-permute-start.4 = (bf16[1,320,128]{2,1,0:T(8,128)(2,1)S(1)}, bf16[1,320,128]{2,1,0:T(8,128)(2,1)S(1)}, u32[]{:S(2)}, u32[]{:S(2)}) collective-permute-start(bf16[1,320,128]{2,1,0:T(8,128)(2,1)S(1)} %get-tuple-element.40), channel_id=1, source_target_pairs={{0,4},{1,5},{2,6},{3,7},{4,0},{5,1},{6,2},{7,3},{8,12},{9,13},{10,... | collective-permute-start | bytes 245768 | tf_op jit(solution)/shard_map/ppermute | solution.py:197
  34.6 7.7 %collective-permute-start.5 = (bf16[1,320,128]{2,1,0:T(8,128)(2,1)S(1)}, bf16[1,320,128]{2,1,0:T(8,128)(2,1)S(1)}, u32[]{:S(2)}, u32[]{:S(2)}) collective-permute-start(bf16[1,320,128]{2,1,0:T(8,128)(2,1)S(1)} %get-tuple-element.41), channel_id=1, source_target_pairs={{0,12},{1,13},{2,14},{3,15},{4,8},{5,9},{6,10},{7,11},{8,4},{9,5},... | collective-permute-start | bytes 245768 | tf_op jit(solution)/shard_map/ppermute | solution.py:197
  42.3 4.3 %collective-permute-start.7 = (bf16[1,320,128]{2,1,0:T(8,128)(2,1)S(1)}, bf16[1,320,128]{2,1,0:T(8,128)(2,1)S(1)}, u32[]{:S(2)}, u32[]{:S(2)}) collective-permute-start(bf16[1,320,128]{2,1,0:T(8,128)(2,1)S(1)} %total.2.refs_0_), channel_id=1, source_target_pairs={{0,8},{1,9},{2,10},{3,11},{4,12},{5,13},{6,14},{7,15},{8,0},{9,1},... | collective-permute-start | bytes 245768 | tf_op jit(solution)/shard_map/ppermute | solution.py:197
  42.4 4.2 %collective-permute-start.8 = (bf16[1,320,128]{2,1,0:T(8,128)(2,1)S(1)}, bf16[1,320,128]{2,1,0:T(8,128)(2,1)S(1)}, u32[]{:S(2)}, u32[]{:S(2)}) collective-permute-start(bf16[1,320,128]{2,1,0:T(8,128)(2,1)S(1)} %total.2.refs_0_), channel_id=1, source_target_pairs={{0,4},{1,5},{2,6},{3,7},{4,0},{5,1},{6,2},{7,3},{8,12},{9,13},{10,... | collective-permute-start | bytes 245768 | tf_op jit(solution)/shard_map/ppermute | solution.py:197
  43.1 6.9 %collective-permute-start.9 = (bf16[1,320,128]{2,1,0:T(8,128)(2,1)S(1)}, bf16[1,320,128]{2,1,0:T(8,128)(2,1)S(1)}, u32[]{:S(2)}, u32[]{:S(2)}) collective-permute-start(bf16[1,320,128]{2,1,0:T(8,128)(2,1)S(1)} %total.2.refs_0_), channel_id=1, source_target_pairs={{0,12},{1,13},{2,14},{3,15},{4,8},{5,9},{6,10},{7,11},{8,4},{9,5},... | collective-permute-start | bytes 245768 | tf_op jit(solution)/shard_map/ppermute | solution.py:197
  49.9 37.8 %copy-start.5 = (bf16[4,256,128]{2,1,0:T(8,128)(2,1)S(1)}, bf16[4,256,128]{2,1,0:T(8,128)(2,1)}, u32[]{:S(2)}) copy-start(bf16[4,256,128]{2,1,0:T(8,128)(2,1)} %copy-done.4) | copy-start | bytes 786436
  81.6 44.1 %all-to-all-start.2 = ((bf16[16,4,64,128]{3,2,1,0:T(8,128)(2,1)}), bf16[16,4,64,128]{3,2,1,0:T(8,128)(2,1)}, u32[]{:S(2)}, u32[]{:S(2)}) async-start(bf16[16,4,64,128]{3,2,1,0:T(8,128)(2,1)} %bitcast.10), calls=%async_computation.2 | async-start | bytes 2097152 | tf_op jit(solution)/shard_map/all_to_all | solution.py:200
  86.2 25.2 %copy-start.2 = (bf16[2,64,5120]{2,1,0:T(8,128)(2,1)S(1)}, bf16[2,64,5120]{2,1,0:T(8,128)(2,1)}, u32[]{:S(2)}) copy-start(bf16[2,64,5120]{2,1,0:T(8,128)(2,1)} %x_ref.1) | copy-start | bytes 3932164
  86.3 17.8 %collective-permute-start.12 = (bf16[4,320,128]{2,1,0:T(8,128)(2,1)S(1)}, bf16[4,320,128]{2,1,0:T(8,128)(2,1)S(1)}, u32[]{:S(2)}, u32[]{:S(2)}) collective-permute-start(bf16[4,320,128]{2,1,0:T(8,128)(2,1)S(1)} %join.2.refs_0_), channel_id=1, source_target_pairs={{0,2},{1,3},{2,0},{3,1},{4,6},{5,7},{6,4},{7,5},{8,10},{9,11},{10,... | collective-permute-start | bytes 983048 | tf_op jit(solution)/shard_map/ppermute | solution.py:197
  87.8 37.9 %copy-start.3 = (bf16[16,4,64,128]{3,2,1,0:T(8,128)(2,1)S(1)}, bf16[16,4,64,128]{3,2,1,0:T(8,128)(2,1)}, u32[]{:S(2)}) copy-start(bf16[16,4,64,128]{3,2,1,0:T(8,128)(2,1)} %all_to_all.20.v_ref) | copy-start | bytes 3145732
  87.8 18.9 %collective-permute-start.10 = (bf16[2,256,128]{2,1,0:T(8,128)(2,1)S(1)}, bf16[2,256,128]{2,1,0:T(8,128)(2,1)S(1)}, u32[]{:S(2)}, u32[]{:S(2)}) collective-permute-start(bf16[2,256,128]{2,1,0:T(8,128)(2,1)S(1)} %get-tuple-element.47), channel_id=1, source_target_pairs={{0,4},{1,5},{2,6},{3,7},{4,0},{5,1},{6,2},{7,3},{8,12},{9,13},{10,... | collective-permute-start | bytes 393224 | tf_op jit(solution)/shard_map/ppermute | solution.py:197
  106.8 4.7 %collective-permute-start.13 = (bf16[8,320,128]{2,1,0:T(8,128)(2,1)S(1)}, bf16[8,320,128]{2,1,0:T(8,128)(2,1)S(1)}, u32[]{:S(2)}, u32[]{:S(2)}) collective-permute-start(bf16[8,320,128]{2,1,0:T(8,128)(2,1)S(1)} %join.3.refs_0_), channel_id=1, source_target_pairs={{0,1},{1,0},{2,3},{3,2},{4,5},{5,4},{6,7},{7,6},{8,9},{9,8},{10,11... | collective-permute-start | bytes 1966088 | tf_op jit(solution)/shard_map/ppermute | solution.py:197
  107.4 15.4 %collective-permute-start.11 = (bf16[1,256,128]{2,1,0:T(8,128)(2,1)S(1)}, bf16[1,256,128]{2,1,0:T(8,128)(2,1)S(1)}, u32[]{:S(2)}, u32[]{:S(2)}) collective-permute-start(bf16[1,256,128]{2,1,0:T(8,128)(2,1)S(1)} %get-tuple-element.49), channel_id=1, source_target_pairs={{0,8},{1,9},{2,10},{3,11},{4,12},{5,13},{6,14},{7,15},{8,0},{9,1},... | collective-permute-start | bytes 196616 | tf_op jit(solution)/shard_map/ppermute | solution.py:197
  112.3 4.8 %copy-start.6 = (bf16[2,32,128]{2,1,0:T(8,128)(2,1)}, bf16[2,32,128]{2,1,0:T(8,128)(2,1)S(1)}, u32[]{:S(2)}) copy-start(bf16[2,32,128]{2,1,0:T(8,128)(2,1)S(1)} %low_rank.1.refs_0_) | copy-start | bytes 49156
  112.3 2.2 %collective-permute-start.14 = (bf16[2,32,128]{2,1,0:T(8,128)(2,1)S(1)}, bf16[2,32,128]{2,1,0:T(8,128)(2,1)S(1)}, u32[]{:S(2)}, u32[]{:S(2)}) collective-permute-start(bf16[2,32,128]{2,1,0:T(8,128)(2,1)S(1)} %low_rank.1.refs_0_), channel_id=1, source_target_pairs={{0,1},{1,0},{2,3},{3,2},{4,5},{5,4},{6,7},{7,6},{8,9},{9,8},{10,11... | collective-permute-start | bytes 49160 | tf_op jit(solution)/shard_map/ppermute | solution.py:197
  112.7 2.8 %collective-permute-start.15 = (bf16[2,32,128]{2,1,0:T(8,128)(2,1)S(1)}, bf16[2,32,128]{2,1,0:T(8,128)(2,1)S(1)}, u32[]{:S(2)}, u32[]{:S(2)}) collective-permute-start(bf16[2,32,128]{2,1,0:T(8,128)(2,1)S(1)} %low_rank.1.refs_0_), channel_id=1, source_target_pairs={{0,2},{1,3},{2,0},{3,1},{4,6},{5,7},{6,4},{7,5},{8,10},{9,11},{10,... | collective-permute-start | bytes 49160 | tf_op jit(solution)/shard_map/ppermute | solution.py:197
  113.9 3.3 %collective-permute-start.16 = (bf16[2,32,128]{2,1,0:T(8,128)(2,1)S(1)}, bf16[2,32,128]{2,1,0:T(8,128)(2,1)S(1)}, u32[]{:S(2)}, u32[]{:S(2)}) collective-permute-start(bf16[2,32,128]{2,1,0:T(8,128)(2,1)S(1)} %low_rank.1.refs_0_), channel_id=1, source_target_pairs={{0,3},{1,2},{2,1},{3,0},{4,7},{5,6},{6,5},{7,4},{8,11},{9,10},{10,... | collective-permute-start | bytes 49160 | tf_op jit(solution)/shard_map/ppermute | solution.py:197
  114.5 2.6 %copy-start.11 = (bf16[2,32,128]{2,1,0:T(8,128)(2,1)}, bf16[2,32,128]{2,1,0:T(8,128)(2,1)S(1)}, u32[]{:S(2)}) copy-start(bf16[2,32,128]{2,1,0:T(8,128)(2,1)S(1)} %collective-permute-done.14.refs_1_) | copy-start | bytes 49156
  115.5 1.6 copy-start.12
  117.2 0.6 copy-start.13
  119.2 3.6 %collective-permute-start.17 = (bf16[4,32,128]{2,1,0:T(8,128)(2,1)}, bf16[4,32,128]{2,1,0:T(8,128)(2,1)S(1)}, u32[]{:S(2)}, u32[]{:S(2)}) collective-permute-start(bf16[4,32,128]{2,1,0:T(8,128)(2,1)} %get-tuple-element.54), channel_id=1, source_target_pairs={{0,4},{1,5},{2,6},{3,7},{4,0},{5,1},{6,2},{7,3},{8,12},{9,13},{10,... | collective-permute-start | bytes 98312 | tf_op jit(solution)/shard_map/ppermute | solution.py:197
  119.2 4.0 %collective-permute-start.18 = (bf16[4,32,128]{2,1,0:T(8,128)(2,1)}, bf16[4,32,128]{2,1,0:T(8,128)(2,1)S(1)}, u32[]{:S(2)}, u32[]{:S(2)}) collective-permute-start(bf16[4,32,128]{2,1,0:T(8,128)(2,1)} %get-tuple-element.55), channel_id=1, source_target_pairs={{0,8},{1,9},{2,10},{3,11},{4,12},{5,13},{6,14},{7,15},{8,0},{9,1},... | collective-permute-start | bytes 98312 | tf_op jit(solution)/shard_map/ppermute | solution.py:197
  120.9 4.9 %collective-permute-start.19 = (bf16[4,32,128]{2,1,0:T(8,128)(2,1)}, bf16[4,32,128]{2,1,0:T(8,128)(2,1)S(1)}, u32[]{:S(2)}, u32[]{:S(2)}) collective-permute-start(bf16[4,32,128]{2,1,0:T(8,128)(2,1)} %get-tuple-element.56), channel_id=1, source_target_pairs={{0,12},{1,13},{2,14},{3,15},{4,8},{5,9},{6,10},{7,11},{8,4},{9,5},... | collective-permute-start | bytes 98312 | tf_op jit(solution)/shard_map/ppermute | solution.py:197
  125.7 0.8 copy-start.9

commit v18 on v17

--- a/solution.py
+++ b/solution.py
@@ -278,7 +278,6 @@
     shard = after(total(held[0], to_others(held)), up_got[-1])
     gathered = [shard] + [swap(shard, k) for k in others]
     vals = exchange(after(by_pairs(values), *gathered))
-    asked = exchange(after(by_pairs(queries), vals))
 
     up_part = after(up_pieces[-1], *gathered)
     pair_shape = (2,) + up_part.shape[1:]
@@ -307,6 +306,7 @@
         gathered = [joined, swap(joined, 1 << i)]
         if i > 0:
             joined = after(join(gathered), came)
+    asked = exchange(after(by_pairs(queries), vals, joined))
 
     low_shape = (videos, toks // 2, 2 * ranks)
     low = pl.pallas_call(

time: 168 us -> 158 us (0.940)
  blocking collectives: 62.9 us -> 29.9 us
  waiting for transfers between devices: 49 us -> 64.4 us
  starting transfers between devices: 37.4 us -> 44.2 us
    all_to_all x2 -> x1, blocking collectives: 62.9 us -> 29.9 us  [exchange(): lax.all_to_all(tensor, 'seq', split_axis=0, concat_axis=0, tiled=True)]
    ppermute x20, waiting for transfers between devices: 35.6 us -> 48.2 us  [swap(): return lax.ppermute(tensor, 'seq', [(i, i ^ k) for i in range(devs)])]
    all_to_all x2 -> x3, starting transfers between devices: 12.1 us -> 20.7 us  [exchange(): lax.all_to_all(tensor, 'seq', split_axis=0, concat_axis=0, tiled=True)]
    all_to_all x2 -> x3, waiting for transfers between devices: 13.4 us -> 16.2 us  [exchange(): lax.all_to_all(tensor, 'seq', split_axis=0, concat_axis=0, tiled=True)]
    ppermute x20, starting transfers between devices: 25.3 us -> 23.5 us  [swap(): return lax.ppermute(tensor, 'seq', [(i, i ^ k) for i in range(devs)])]
    unnamed x29 -> x25, local copies, waits for them, and re-layouts: 4.09 us -> 4.09 us
  transfers between devices with their start and end apart: 22 -> 23, of which waited for: 14 -> 15; matrix products, arithmetic and copies ran while one was open for 0% -> 0% of each run, Pallas kernels for 3% -> 4%
where the time goes in v18:
time: 158 us
  waiting for transfers between devices  64.4 us (41%)
  starting transfers between devices  44.2 us (28%)
  blocking collectives  29.9 us (19%)
  Pallas kernels  15.1 us (10%)
  local copies, waits for them, and re-layouts  4.09 us (3%)
    ppermute x20, waiting for transfers between devices, swap(): return lax.ppermute(tensor, 'seq', [(i, i ^ k) for i in range(devs)])  48.2 us
    all_to_all x1, blocking collectives, exchange(): lax.all_to_all(tensor, 'seq', split_axis=0, concat_axis=0, tiled=True)  29.9 us
    ppermute x20, starting transfers between devices, swap(): return lax.ppermute(tensor, 'seq', [(i, i ^ k) for i in range(devs)])  23.5 us
    all_to_all x3, starting transfers between devices, exchange(): lax.all_to_all(tensor, 'seq', split_axis=0, concat_axis=0, tiled=True)  20.7 us
    all_to_all x3, waiting for transfers between devices, exchange(): lax.all_to_all(tensor, 'seq', split_axis=0, concat_axis=0, tiled=True)  16.2 us
    pallas_call x1, Pallas kernels, body(): pl.pallas_call(functools.partial(attend_kernel, math.gcd(devs, max(1, 512...  9.14 us
    unnamed x25, local copies, waits for them, and re-layouts  4.09 us
  transfers between devices with their start and end apart: 23, of which 15 were waited for; matrix products, arithmetic and copies ran while one was open for 0% of the time, Pallas kernels for 4%

profile of v18, /device:TPU:1, one launch (start us, length us, event | category | flops | bytes accessed | tf_op | source)
XLA Modules:
  0.0 157.8 jit_solution(5027483949594805426)
XLA Ops:
  0.0 7.5 %all-to-all-start = ((bf16[16,4,64,128]{3,2,1,0:T(8,128)(2,1)}), bf16[16,4,64,128]{3,2,1,0:T(8,128)(2,1)S(1)}, u32[]{:S(2)}, u32[]{:S(2)}) async-start(bf16[16,4,64,128]{3,2,1,0:T(8,128)(2,1)} %bitcast.8), calls=%async_computation | async-start | bytes 2097152 | tf_op jit(solution)/shard_map/all_to_all | solution.py:200
  7.5 1.7 %copy-done = bf16[4,64,5120]{2,1,0:T(8,128)(2,1)S(1)} copy-done((bf16[4,64,5120]{2,1,0:T(8,128)(2,1)S(1)}, bf16[4,64,5120]{2,1,0:T(8,128)(2,1)}, u32[]{:S(2)}) %copy-start) | copy-done | bytes 2621464
  9.3 1.5 pick_factors.1
  10.8 0.2 collective-permute-start
  11.0 2.0 %collective-permute-done.refs_1_ = bf16[8,320,128]{2,1,0:T(8,128)(2,1)S(1)} collective-permute-done((bf16[8,320,128]{2,1,0:T(8,128)(2,1)S(1)}, bf16[8,320,128]{2,1,0:T(8,128)(2,1)S(1)}, u32[]{:S(2)}, u32[]{:S(2)}) %collective-permute-start) | collective-permute-done | bytes 655392 | tf_op jit(solution)/shard_map/ppermute | solution.py:197
  13.0 0.1 halve.2
  13.1 0.2 collective-permute-start.1
  13.3 1.6 %collective-permute-start.2 = (bf16[4,320,128]{2,1,0:T(8,128)(2,1)S(1)}, bf16[4,320,128]{2,1,0:T(8,128)(2,1)S(1)}, u32[]{:S(2)}, u32[]{:S(2)}) collective-permute-start(bf16[4,320,128]{2,1,0:T(8,128)(2,1)S(1)} %halve.2), channel_id=1, source_target_pairs={{0,2},{1,3},{2,0},{3,1},{4,6},{5,7},{6,4},{7,5},{8,10},{9,11},{10,... | collective-permute-start | bytes 983048 | tf_op jit(solution)/shard_map/ppermute | solution.py:197
  14.9 0.2 collective-permute-done.1.refs_1_
  15.1 0.8 halve.3
  15.8 1.4 collective-permute-start.6
  17.2 13.4 %all-to-all-done.k_ref = bf16[16,4,64,128]{3,2,1,0:T(8,128)(2,1)S(1)} async-done(((bf16[16,4,64,128]{3,2,1,0:T(8,128)(2,1)}), bf16[16,4,64,128]{3,2,1,0:T(8,128)(2,1)S(1)}, u32[]{:S(2)}, u32[]{:S(2)}) %all-to-all-start) | async-done | bytes 1048608 | tf_op jit(solution)/shard_map/all_to_all | solution.py:200
  30.7 0.1 split.3
  30.8 3.9 %collective-permute-start.3 = (bf16[1,320,128]{2,1,0:T(8,128)(2,1)S(1)}, bf16[1,320,128]{2,1,0:T(8,128)(2,1)S(1)}, u32[]{:S(2)}, u32[]{:S(2)}) collective-permute-start(bf16[1,320,128]{2,1,0:T(8,128)(2,1)S(1)} %get-tuple-element.39), channel_id=1, source_target_pairs={{0,8},{1,9},{2,10},{3,11},{4,12},{5,13},{6,14},{7,15},{8,0},{9,1},... | collective-permute-start | bytes 245768 | tf_op jit(solution)/shard_map/ppermute | solution.py:197
  34.6 1.4 collective-permute-start.5
  36.0 0.5 collective-permute-done.3.refs_1_
  36.5 1.8 %collective-permute-done.4.refs_2_ = bf16[1,320,128]{2,1,0:T(8,128)(2,1)S(1)} collective-permute-done((bf16[1,320,128]{2,1,0:T(8,128)(2,1)S(1)}, bf16[1,320,128]{2,1,0:T(8,128)(2,1)S(1)}, u32[]{:S(2)}, u32[]{:S(2)}) %collective-permute-start.4) | collective-permute-done | bytes 81952 | tf_op jit(solution)/shard_map/ppermute | solution.py:197
  38.2 4.1 %collective-permute-done.5.refs_3_ = bf16[1,320,128]{2,1,0:T(8,128)(2,1)S(1)} collective-permute-done((bf16[1,320,128]{2,1,0:T(8,128)(2,1)S(1)}, bf16[1,320,128]{2,1,0:T(8,128)(2,1)S(1)}, u32[]{:S(2)}, u32[]{:S(2)}) %collective-permute-start.5) | collective-permute-done | bytes 81952 | tf_op jit(solution)/shard_map/ppermute | solution.py:197
  42.4 0.6 collective-permute-start.8
  43.1 2.9 %collective-permute-start.9 = (bf16[1,320,128]{2,1,0:T(8,128)(2,1)S(1)}, bf16[1,320,128]{2,1,0:T(8,128)(2,1)S(1)}, u32[]{:S(2)}, u32[]{:S(2)}) collective-permute-start(bf16[1,320,128]{2,1,0:T(8,128)(2,1)S(1)} %total.2.refs_0_), channel_id=1, source_target_pairs={{0,12},{1,13},{2,14},{3,15},{4,8},{5,9},{6,10},{7,11},{8,4},{9,5},... | collective-permute-start | bytes 245768 | tf_op jit(solution)/shard_map/ppermute | solution.py:197
  46.0 0.7 collective-permute-done.7.refs_1_
  46.7 3.2 %collective-permute-done.9.refs_3_ = bf16[1,320,128]{2,1,0:T(8,128)(2,1)S(1)} collective-permute-done((bf16[1,320,128]{2,1,0:T(8,128)(2,1)S(1)}, bf16[1,320,128]{2,1,0:T(8,128)(2,1)S(1)}, u32[]{:S(2)}, u32[]{:S(2)}) %collective-permute-start.9) | collective-permute-done | bytes 81952 | tf_op jit(solution)/shard_map/ppermute | solution.py:197
  49.9 6.5 %all-to-all-start.1 = ((bf16[16,4,64,128]{3,2,1,0:T(8,128)(2,1)}), bf16[16,4,64,128]{3,2,1,0:T(8,128)(2,1)}, u32[]{:S(2)}, u32[]{:S(2)}) async-start(bf16[16,4,64,128]{3,2,1,0:T(8,128)(2,1)} %bitcast.9), calls=%async_computation.1 | async-start | bytes 2097152 | tf_op jit(solution)/shard_map/all_to_all | solution.py:200
  56.4 1.5 collective-permute-start.12
  57.9 1.0 split.4
  58.9 1.2 collective-permute-start.10
  60.1 14.0 %collective-permute-done.12.refs_1_ = bf16[4,320,128]{2,1,0:T(8,128)(2,1)S(1)} collective-permute-done((bf16[4,320,128]{2,1,0:T(8,128)(2,1)S(1)}, bf16[4,320,128]{2,1,0:T(8,128)(2,1)S(1)}, u32[]{:S(2)}, u32[]{:S(2)}) %collective-permute-start.12) | collective-permute-done | bytes 327712 | tf_op jit(solution)/shard_map/ppermute | solution.py:197
  74.2 2.6 %collective-permute-done.10.refs_1_ = bf16[2,256,128]{2,1,0:T(8,128)(2,1)S(1)} collective-permute-done((bf16[2,256,128]{2,1,0:T(8,128)(2,1)S(1)}, bf16[2,256,128]{2,1,0:T(8,128)(2,1)S(1)}, u32[]{:S(2)}, u32[]{:S(2)}) %collective-permute-start.10) | collective-permute-done | bytes 131104 | tf_op jit(solution)/shard_map/ppermute | solution.py:197
  76.9 2.7 %all-to-all-done.1.v_ref = bf16[16,4,64,128]{3,2,1,0:T(8,128)(2,1)} async-done(((bf16[16,4,64,128]{3,2,1,0:T(8,128)(2,1)}), bf16[16,4,64,128]{3,2,1,0:T(8,128)(2,1)}, u32[]{:S(2)}, u32[]{:S(2)}) %all-to-all-start.1) | async-done | bytes 1048608 | tf_op jit(solution)/shard_map/all_to_all | solution.py:200
  79.6 6.7 %all-to-all-start.2 = ((bf16[16,4,64,128]{3,2,1,0:T(8,128)(2,1)}), bf16[16,4,64,128]{3,2,1,0:T(8,128)(2,1)}, u32[]{:S(2)}, u32[]{:S(2)}) async-start(bf16[16,4,64,128]{3,2,1,0:T(8,128)(2,1)} %bitcast.10), calls=%async_computation.2 | async-start | bytes 2097152 | tf_op jit(solution)/shard_map/all_to_all | solution.py:200
  86.3 0.2 collective-permute-start.13
  86.6 2.5 %collective-permute-start.11 = (bf16[1,256,128]{2,1,0:T(8,128)(2,1)S(1)}, bf16[1,256,128]{2,1,0:T(8,128)(2,1)S(1)}, u32[]{:S(2)}, u32[]{:S(2)}) collective-permute-start(bf16[1,256,128]{2,1,0:T(8,128)(2,1)S(1)} %get-tuple-element.49), channel_id=1, source_target_pairs={{0,8},{1,9},{2,10},{3,11},{4,12},{5,13},{6,14},{7,15},{8,0},{9,1},... | collective-permute-start | bytes 196616 | tf_op jit(solution)/shard_map/ppermute | solution.py:197
  89.1 0.9 low_rank.1.refs_0_
  89.9 0.5 collective-permute-start.14
  90.4 1.2 collective-permute-start.15
  91.6 0.5 collective-permute-start.16
  92.2 2.0 %collective-permute-done.15.refs_2_ = bf16[2,32,128]{2,1,0:T(8,128)(2,1)S(1)} collective-permute-done((bf16[2,32,128]{2,1,0:T(8,128)(2,1)S(1)}, bf16[2,32,128]{2,1,0:T(8,128)(2,1)S(1)}, u32[]{:S(2)}, u32[]{:S(2)}) %collective-permute-start.15) | collective-permute-done | bytes 16416 | tf_op jit(solution)/shard_map/ppermute | solution.py:197
  94.2 1.2 collective-permute-done.16.refs_3_
  95.4 0.6 copy-done.11
  96.0 1.4 choose.1
  97.4 0.8 collective-permute-start.17
  98.2 2.9 %collective-permute-start.18 = (bf16[4,32,128]{2,1,0:T(8,128)(2,1)}, bf16[4,32,128]{2,1,0:T(8,128)(2,1)S(1)}, u32[]{:S(2)}, u32[]{:S(2)}) collective-permute-start(bf16[4,32,128]{2,1,0:T(8,128)(2,1)} %get-tuple-element.55), channel_id=1, source_target_pairs={{0,8},{1,9},{2,10},{3,11},{4,12},{5,13},{6,14},{7,15},{8,0},{9,1},... | collective-permute-start | bytes 98312 | tf_op jit(solution)/shard_map/ppermute | solution.py:197
  101.1 15.2 %collective-permute-done.11.refs_1_ = bf16[1,256,128]{2,1,0:T(8,128)(2,1)S(1)} collective-permute-done((bf16[1,256,128]{2,1,0:T(8,128)(2,1)S(1)}, bf16[1,256,128]{2,1,0:T(8,128)(2,1)S(1)}, u32[]{:S(2)}, u32[]{:S(2)}) %collective-permute-start.11) | collective-permute-done | bytes 65568 | tf_op jit(solution)/shard_map/ppermute | solution.py:197
  116.3 0.7 collective-permute-done.18.refs_2_
  117.0 0.8 copy-done.8
  117.8 9.1 %attend.1 = bf16[16,4,64,128]{3,2,1,0:T(8,128)(2,1)S(1)} custom-call(s32[1]{0:T(128)} %bitcast.me_ref, bf16[4,64,128]{2,1,0:T(8,128)(2,1)S(1)} %bitcast.6, bf16[16,4,64,128]{3,2,1,0:T(8,128)(2,1)} %all-to-all-done.2.q_ref, bf16[16,4,64,128]{3,2,1,0:T(8,128)(2,1)S(1)} %all-to-all-done.k_ref, bf16[16,4,64,128]{3,2,1,0:T(8,128)(2,1)} %all-to-all-done.1.v_ref, ...), custom_call_target="tpu_custom_call" | custom-call | flops 2147483648 | bytes 4194304 | tf_op jit(solution)/shard_map/attend/pallas_call | solution.py:339
  126.9 29.9 %all_to_all.20 = bf16[16,4,64,128]{3,2,1,0:T(8,128)(2,1)S(1)} all-to-all(bf16[16,4,64,128]{3,2,1,0:T(8,128)(2,1)S(1)} %attend.1), channel_id=1, replica_groups=mesh['grp'=2,'seq'=16] {'seq'}, dimensions={0} | all-to-all | bytes 2097152 | tf_op jit(solution)/shard_map/all_to_all | solution.py:200
  156.8 1.0 copy.10
  (37 shorter events, 0.3 us)
Async XLA Ops:
  0.0 7.5 %copy-start.1 = (bf16[4,64,4096]{2,1,0:T(8,128)(2,1)S(1)}, bf16[4,64,4096]{2,1,0:T(8,128)(2,1)}, u32[]{:S(2)}) copy-start(bf16[4,64,4096]{2,1,0:T(8,128)(2,1)} %up_ref.1) | copy-start | bytes 6291460
  0.0 7.5 %copy-start.6 = (s32[64]{0:T(128)S(1)}, s32[64]{0:T(128)}, u32[]{:S(2)}) copy-start(s32[64]{0:T(128)} %row_ref.1) | copy-start | bytes 772
  0.0 7.5 %copy-start.7 = (s32[2]{0:T(128)S(1)}, s32[2]{0:T(128)}, u32[]{:S(2)}) copy-start(s32[2]{0:T(128)} %req_ref.1) | copy-start | bytes 28
  0.0 30.6 %all-to-all-start = ((bf16[16,4,64,128]{3,2,1,0:T(8,128)(2,1)}), bf16[16,4,64,128]{3,2,1,0:T(8,128)(2,1)S(1)}, u32[]{:S(2)}, u32[]{:S(2)}) async-start(bf16[16,4,64,128]{3,2,1,0:T(8,128)(2,1)} %bitcast.8), calls=%async_computation | async-start | bytes 2097152 | tf_op jit(solution)/shard_map/all_to_all | solution.py:200
  7.5 1.7 %copy-start = (bf16[4,64,5120]{2,1,0:T(8,128)(2,1)S(1)}, bf16[4,64,5120]{2,1,0:T(8,128)(2,1)}, u32[]{:S(2)}) copy-start(bf16[4,64,5120]{2,1,0:T(8,128)(2,1)} %down_ref.1) | copy-start | bytes 7864324
  10.8 5.1 %copy-start.3 = (bf16[4,256,128]{2,1,0:T(8,128)(2,1)}, bf16[4,256,128]{2,1,0:T(8,128)(2,1)S(1)}, u32[]{:S(2)}) copy-start(bf16[4,256,128]{2,1,0:T(8,128)(2,1)S(1)} %get-tuple-element.45.refs_0_) | copy-start | bytes 786436
  10.8 2.2 %collective-permute-start = (bf16[8,320,128]{2,1,0:T(8,128)(2,1)S(1)}, bf16[8,320,128]{2,1,0:T(8,128)(2,1)S(1)}, u32[]{:S(2)}, u32[]{:S(2)}) collective-permute-start(bf16[8,320,128]{2,1,0:T(8,128)(2,1)S(1)} %get-tuple-element.35), channel_id=1, source_target_pairs={{0,1},{1,0},{2,3},{3,2},{4,5},{5,4},{6,7},{7,6},{8,9},{9,8},{10,11... | collective-permute-start | bytes 1966088 | tf_op jit(solution)/shard_map/ppermute | solution.py:197
  13.1 2.0 %collective-permute-start.1 = (bf16[8,256,128]{2,1,0:T(8,128)(2,1)S(1)}, bf16[8,256,128]{2,1,0:T(8,128)(2,1)S(1)}, u32[]{:S(2)}, u32[]{:S(2)}) collective-permute-start(bf16[8,256,128]{2,1,0:T(8,128)(2,1)S(1)} %get-tuple-element.36), channel_id=1, source_target_pairs={{0,1},{1,0},{2,3},{3,2},{4,5},{5,4},{6,7},{7,6},{8,9},{9,8},{10,11... | collective-permute-start | bytes 1572872 | tf_op jit(solution)/shard_map/ppermute | solution.py:197
  13.3 17.4 %collective-permute-start.2 = (bf16[4,320,128]{2,1,0:T(8,128)(2,1)S(1)}, bf16[4,320,128]{2,1,0:T(8,128)(2,1)S(1)}, u32[]{:S(2)}, u32[]{:S(2)}) collective-permute-start(bf16[4,320,128]{2,1,0:T(8,128)(2,1)S(1)} %halve.2), channel_id=1, source_target_pairs={{0,2},{1,3},{2,0},{3,1},{4,6},{5,7},{6,4},{7,5},{8,10},{9,11},{10,... | collective-permute-start | bytes 983048 | tf_op jit(solution)/shard_map/ppermute | solution.py:197
  15.8 26.5 %collective-permute-start.6 = (bf16[4,256,128]{2,1,0:T(8,128)(2,1)}, bf16[4,256,128]{2,1,0:T(8,128)(2,1)}, u32[]{:S(2)}, u32[]{:S(2)}) collective-permute-start(bf16[4,256,128]{2,1,0:T(8,128)(2,1)} %halve.3), channel_id=1, source_target_pairs={{0,2},{1,3},{2,0},{3,1},{4,6},{5,7},{6,4},{7,5},{8,10},{9,11},{10,... | collective-permute-start | bytes 786440 | tf_op jit(solution)/shard_map/ppermute | solution.py:197
  30.7 27.2 %copy-start.4 = (bf16[4,256,128]{2,1,0:T(8,128)(2,1)S(1)}, bf16[4,256,128]{2,1,0:T(8,128)(2,1)}, u32[]{:S(2)}) copy-start(bf16[4,256,128]{2,1,0:T(8,128)(2,1)} %copy-done.3) | copy-start | bytes 786436
  30.8 5.7 %collective-permute-start.3 = (bf16[1,320,128]{2,1,0:T(8,128)(2,1)S(1)}, bf16[1,320,128]{2,1,0:T(8,128)(2,1)S(1)}, u32[]{:S(2)}, u32[]{:S(2)}) collective-permute-start(bf16[1,320,128]{2,1,0:T(8,128)(2,1)S(1)} %get-tuple-element.39), channel_id=1, source_target_pairs={{0,8},{1,9},{2,10},{3,11},{4,12},{5,13},{6,14},{7,15},{8,0},{9,1},... | collective-permute-start | bytes 245768 | tf_op jit(solution)/shard_map/ppermute | solution.py:197
  34.6 3.6 %collective-permute-start.4 = (bf16[1,320,128]{2,1,0:T(8,128)(2,1)S(1)}, bf16[1,320,128]{2,1,0:T(8,128)(2,1)S(1)}, u32[]{:S(2)}, u32[]{:S(2)}) collective-permute-start(bf16[1,320,128]{2,1,0:T(8,128)(2,1)S(1)} %get-tuple-element.40), channel_id=1, source_target_pairs={{0,4},{1,5},{2,6},{3,7},{4,0},{5,1},{6,2},{7,3},{8,12},{9,13},{10,... | collective-permute-start | bytes 245768 | tf_op jit(solution)/shard_map/ppermute | solution.py:197
  34.6 7.7 %collective-permute-start.5 = (bf16[1,320,128]{2,1,0:T(8,128)(2,1)S(1)}, bf16[1,320,128]{2,1,0:T(8,128)(2,1)S(1)}, u32[]{:S(2)}, u32[]{:S(2)}) collective-permute-start(bf16[1,320,128]{2,1,0:T(8,128)(2,1)S(1)} %get-tuple-element.41), channel_id=1, source_target_pairs={{0,12},{1,13},{2,14},{3,15},{4,8},{5,9},{6,10},{7,11},{8,4},{9,5},... | collective-permute-start | bytes 245768 | tf_op jit(solution)/shard_map/ppermute | solution.py:197
  42.3 4.3 %collective-permute-start.7 = (bf16[1,320,128]{2,1,0:T(8,128)(2,1)S(1)}, bf16[1,320,128]{2,1,0:T(8,128)(2,1)S(1)}, u32[]{:S(2)}, u32[]{:S(2)}) collective-permute-start(bf16[1,320,128]{2,1,0:T(8,128)(2,1)S(1)} %total.2.refs_0_), channel_id=1, source_target_pairs={{0,8},{1,9},{2,10},{3,11},{4,12},{5,13},{6,14},{7,15},{8,0},{9,1},... | collective-permute-start | bytes 245768 | tf_op jit(solution)/shard_map/ppermute | solution.py:197
  42.4 4.2 %collective-permute-start.8 = (bf16[1,320,128]{2,1,0:T(8,128)(2,1)S(1)}, bf16[1,320,128]{2,1,0:T(8,128)(2,1)S(1)}, u32[]{:S(2)}, u32[]{:S(2)}) collective-permute-start(bf16[1,320,128]{2,1,0:T(8,128)(2,1)S(1)} %total.2.refs_0_), channel_id=1, source_target_pairs={{0,4},{1,5},{2,6},{3,7},{4,0},{5,1},{6,2},{7,3},{8,12},{9,13},{10,... | collective-permute-start | bytes 245768 | tf_op jit(solution)/shard_map/ppermute | solution.py:197
  43.1 6.9 %collective-permute-start.9 = (bf16[1,320,128]{2,1,0:T(8,128)(2,1)S(1)}, bf16[1,320,128]{2,1,0:T(8,128)(2,1)S(1)}, u32[]{:S(2)}, u32[]{:S(2)}) collective-permute-start(bf16[1,320,128]{2,1,0:T(8,128)(2,1)S(1)} %total.2.refs_0_), channel_id=1, source_target_pairs={{0,12},{1,13},{2,14},{3,15},{4,8},{5,9},{6,10},{7,11},{8,4},{9,5},... | collective-permute-start | bytes 245768 | tf_op jit(solution)/shard_map/ppermute | solution.py:197
  49.9 29.7 %all-to-all-start.1 = ((bf16[16,4,64,128]{3,2,1,0:T(8,128)(2,1)}), bf16[16,4,64,128]{3,2,1,0:T(8,128)(2,1)}, u32[]{:S(2)}, u32[]{:S(2)}) async-start(bf16[16,4,64,128]{3,2,1,0:T(8,128)(2,1)} %bitcast.9), calls=%async_computation.1 | async-start | bytes 2097152 | tf_op jit(solution)/shard_map/all_to_all | solution.py:200
  56.4 17.8 %collective-permute-start.12 = (bf16[4,320,128]{2,1,0:T(8,128)(2,1)S(1)}, bf16[4,320,128]{2,1,0:T(8,128)(2,1)S(1)}, u32[]{:S(2)}, u32[]{:S(2)}) collective-permute-start(bf16[4,320,128]{2,1,0:T(8,128)(2,1)S(1)} %join.2.refs_0_), channel_id=1, source_target_pairs={{0,2},{1,3},{2,0},{3,1},{4,6},{5,7},{6,4},{7,5},{8,10},{9,11},{10,... | collective-permute-start | bytes 983048 | tf_op jit(solution)/shard_map/ppermute | solution.py:197
  58.9 30.2 %copy-start.2 = (bf16[2,64,5120]{2,1,0:T(8,128)(2,1)S(1)}, bf16[2,64,5120]{2,1,0:T(8,128)(2,1)}, u32[]{:S(2)}) copy-start(bf16[2,64,5120]{2,1,0:T(8,128)(2,1)} %x_ref.1) | copy-start | bytes 3932164
  58.9 18.0 %collective-permute-start.10 = (bf16[2,256,128]{2,1,0:T(8,128)(2,1)S(1)}, bf16[2,256,128]{2,1,0:T(8,128)(2,1)S(1)}, u32[]{:S(2)}, u32[]{:S(2)}) collective-permute-start(bf16[2,256,128]{2,1,0:T(8,128)(2,1)S(1)} %get-tuple-element.47), channel_id=1, source_target_pairs={{0,4},{1,5},{2,6},{3,7},{4,0},{5,1},{6,2},{7,3},{8,12},{9,13},{10,... | collective-permute-start | bytes 393224 | tf_op jit(solution)/shard_map/ppermute | solution.py:197
  79.6 37.4 %all-to-all-start.2 = ((bf16[16,4,64,128]{3,2,1,0:T(8,128)(2,1)}), bf16[16,4,64,128]{3,2,1,0:T(8,128)(2,1)}, u32[]{:S(2)}, u32[]{:S(2)}) async-start(bf16[16,4,64,128]{3,2,1,0:T(8,128)(2,1)} %bitcast.10), calls=%async_computation.2 | async-start | bytes 2097152 | tf_op jit(solution)/shard_map/all_to_all | solution.py:200
  86.3 2.8 %collective-permute-start.13 = (bf16[8,320,128]{2,1,0:T(8,128)(2,1)S(1)}, bf16[8,320,128]{2,1,0:T(8,128)(2,1)S(1)}, u32[]{:S(2)}, u32[]{:S(2)}) collective-permute-start(bf16[8,320,128]{2,1,0:T(8,128)(2,1)S(1)} %join.3.refs_0_), channel_id=1, source_target_pairs={{0,1},{1,0},{2,3},{3,2},{4,5},{5,4},{6,7},{7,6},{8,9},{9,8},{10,11... | collective-permute-start | bytes 1966088 | tf_op jit(solution)/shard_map/ppermute | solution.py:197
  86.6 29.7 %collective-permute-start.11 = (bf16[1,256,128]{2,1,0:T(8,128)(2,1)S(1)}, bf16[1,256,128]{2,1,0:T(8,128)(2,1)S(1)}, u32[]{:S(2)}, u32[]{:S(2)}) collective-permute-start(bf16[1,256,128]{2,1,0:T(8,128)(2,1)S(1)} %get-tuple-element.49), channel_id=1, source_target_pairs={{0,8},{1,9},{2,10},{3,11},{4,12},{5,13},{6,14},{7,15},{8,0},{9,1},... | collective-permute-start | bytes 196616 | tf_op jit(solution)/shard_map/ppermute | solution.py:197
  89.9 5.4 %copy-start.5 = (bf16[2,32,128]{2,1,0:T(8,128)(2,1)}, bf16[2,32,128]{2,1,0:T(8,128)(2,1)S(1)}, u32[]{:S(2)}) copy-start(bf16[2,32,128]{2,1,0:T(8,128)(2,1)S(1)} %low_rank.1.refs_0_) | copy-start | bytes 49156
  89.9 2.2 %collective-permute-start.14 = (bf16[2,32,128]{2,1,0:T(8,128)(2,1)S(1)}, bf16[2,32,128]{2,1,0:T(8,128)(2,1)S(1)}, u32[]{:S(2)}, u32[]{:S(2)}) collective-permute-start(bf16[2,32,128]{2,1,0:T(8,128)(2,1)S(1)} %low_rank.1.refs_0_), channel_id=1, source_target_pairs={{0,1},{1,0},{2,3},{3,2},{4,5},{5,4},{6,7},{7,6},{8,9},{9,8},{10,11... | collective-permute-start | bytes 49160 | tf_op jit(solution)/shard_map/ppermute | solution.py:197
  90.4 3.7 %collective-permute-start.15 = (bf16[2,32,128]{2,1,0:T(8,128)(2,1)S(1)}, bf16[2,32,128]{2,1,0:T(8,128)(2,1)S(1)}, u32[]{:S(2)}, u32[]{:S(2)}) collective-permute-start(bf16[2,32,128]{2,1,0:T(8,128)(2,1)S(1)} %low_rank.1.refs_0_), channel_id=1, source_target_pairs={{0,2},{1,3},{2,0},{3,1},{4,6},{5,7},{6,4},{7,5},{8,10},{9,11},{10,... | collective-permute-start | bytes 49160 | tf_op jit(solution)/shard_map/ppermute | solution.py:197
  91.6 3.7 %collective-permute-start.16 = (bf16[2,32,128]{2,1,0:T(8,128)(2,1)S(1)}, bf16[2,32,128]{2,1,0:T(8,128)(2,1)S(1)}, u32[]{:S(2)}, u32[]{:S(2)}) collective-permute-start(bf16[2,32,128]{2,1,0:T(8,128)(2,1)S(1)} %low_rank.1.refs_0_), channel_id=1, source_target_pairs={{0,3},{1,2},{2,1},{3,0},{4,7},{5,6},{6,5},{7,4},{8,11},{9,10},{10,... | collective-permute-start | bytes 49160 | tf_op jit(solution)/shard_map/ppermute | solution.py:197
  92.1 3.2 %copy-start.9 = (bf16[2,32,128]{2,1,0:T(8,128)(2,1)}, bf16[2,32,128]{2,1,0:T(8,128)(2,1)S(1)}, u32[]{:S(2)}) copy-start(bf16[2,32,128]{2,1,0:T(8,128)(2,1)S(1)} %collective-permute-done.14.refs_1_) | copy-start | bytes 49156
  94.2 1.2 copy-start.10
  95.4 0.6 copy-start.11
  97.4 18.9 %collective-permute-start.17 = (bf16[4,32,128]{2,1,0:T(8,128)(2,1)}, bf16[4,32,128]{2,1,0:T(8,128)(2,1)S(1)}, u32[]{:S(2)}, u32[]{:S(2)}) collective-permute-start(bf16[4,32,128]{2,1,0:T(8,128)(2,1)} %get-tuple-element.54), channel_id=1, source_target_pairs={{0,4},{1,5},{2,6},{3,7},{4,0},{5,1},{6,2},{7,3},{8,12},{9,13},{10,... | collective-permute-start | bytes 98312 | tf_op jit(solution)/shard_map/ppermute | solution.py:197
  98.2 18.9 %collective-permute-start.18 = (bf16[4,32,128]{2,1,0:T(8,128)(2,1)}, bf16[4,32,128]{2,1,0:T(8,128)(2,1)S(1)}, u32[]{:S(2)}, u32[]{:S(2)}) collective-permute-start(bf16[4,32,128]{2,1,0:T(8,128)(2,1)} %get-tuple-element.55), channel_id=1, source_target_pairs={{0,8},{1,9},{2,10},{3,11},{4,12},{5,13},{6,14},{7,15},{8,0},{9,1},... | collective-permute-start | bytes 98312 | tf_op jit(solution)/shard_map/ppermute | solution.py:197
  101.1 15.9 %collective-permute-start.19 = (bf16[4,32,128]{2,1,0:T(8,128)(2,1)}, bf16[4,32,128]{2,1,0:T(8,128)(2,1)S(1)}, u32[]{:S(2)}, u32[]{:S(2)}) collective-permute-start(bf16[4,32,128]{2,1,0:T(8,128)(2,1)} %get-tuple-element.56), channel_id=1, source_target_pairs={{0,12},{1,13},{2,14},{3,15},{4,8},{5,9},{6,10},{7,11},{8,4},{9,5},... | collective-permute-start | bytes 98312 | tf_op jit(solution)/shard_map/ppermute | solution.py:197
  117.0 0.8 copy-start.8

commit v19 on v16

--- a/solution.py
+++ b/solution.py
@@ -154,18 +154,24 @@
     up = up_ref[...]
     keys = k_ref[...].reshape(length, width)
     vals = add_delta(v_ref[...], low, up, 1)
+    vals = jnp.concatenate([vals, jnp.ones_like(vals)], axis=1)
     q_mix[...] = add_delta(q_ref[...], low, up, 0)
     scale = math.log2(math.e) / math.sqrt(width)
+
+    def score(b):
+        q = q_mix[b * toks : (b + block) * toks, :]
+        return lax.dot_general(q, keys, (((1,), (1,)), ((), ())), preferred_element_type=jnp.float32)
+
+    coming = score(0)
     for b in range(0, devs, block):
-        q = q_mix[b * toks : (b + block) * toks, :]
-        scores = lax.dot_general(
-            q, keys, (((1,), (1,)), ((), ())), preferred_element_type=jnp.float32
-        )
+        scores = coming
+        if b + block < devs:
+            coming = score(b + block)
         top = jnp.max(scores, axis=1, keepdims=True)
-        weights = jnp.exp2((scores - top) * scale)
-        total = jnp.sum(weights, axis=1, keepdims=True)
-        mixed = jnp.dot(weights.astype(jnp.bfloat16), vals, preferred_element_type=jnp.float32)
-        out_ref[b : b + block] = (mixed / total).astype(jnp.bfloat16).reshape(block, toks, width)
+        weights = jnp.exp2((scores - top) * scale).astype(jnp.bfloat16)
+        mixed = jnp.dot(weights, vals, preferred_element_type=jnp.float32)
+        out = mixed[:, :width] / mixed[:, width:]
+        out_ref[b : b + block] = out.astype(jnp.bfloat16).reshape(block, toks, width)
 
 
 def body(
@@ -338,7 +344,7 @@
     later_spec = pl.BlockSpec((devs, pl.squeezed, toks, width), lambda p: (0, pairs + p, 0, 0))
     low_spec = pl.BlockSpec((LOW,) + low_shape[1:], lambda p: (0, 0, 0))
     mixed = pl.pallas_call(
-        functools.partial(attend_kernel, math.gcd(devs, max(1, 512 // toks))),
+        functools.partial(attend_kernel, math.gcd(devs, max(1, 256 // toks))),
         grid=(pairs,),
         in_specs=[SMEM, pl.BlockSpec((pl.squeezed, ranks, LANES), lambda p: (p, 0, 0))]
         + [later_spec, part_spec, part_spec]

time: 155 us -> 154 us (level)
  no operation moved by 1% of the time
where the time goes in v19:
time: 154 us
  waiting for transfers between devices  63.3 us (41%)
  starting transfers between devices  39.6 us (26%)
  blocking collectives  31.7 us (21%)
  Pallas kernels  12.3 us (8%)
  local copies, waits for them, and re-layouts  4.08 us (3%)
  other arithmetic  2.77 us (2%)
    ppermute x20, waiting for transfers between devices, swap(): return lax.ppermute(tensor, 'seq', [(i, i ^ k) for i in range(devs)])  49 us
    all_to_all x1, blocking collectives, exchange(): lax.all_to_all(tensor, 'seq', split_axis=0, concat_axis=0, tiled=True)  31.7 us
    ppermute x20, starting transfers between devices, swap(): return lax.ppermute(tensor, 'seq', [(i, i ^ k) for i in range(devs)])  25.5 us
    all_to_all x2, waiting for transfers between devices, exchange(): lax.all_to_all(tensor, 'seq', split_axis=0, concat_axis=0, tiled=True)  14.2 us
    all_to_all x2, starting transfers between devices, exchange(): lax.all_to_all(tensor, 'seq', split_axis=0, concat_axis=0, tiled=True)  14.1 us
    pallas_call x1, Pallas kernels, body(): pl.pallas_call(functools.partial(attend_kernel, math.gcd(devs, max(1, 256...  8.07 us
    unnamed x23, local copies, waits for them, and re-layouts  4.08 us
  transfers between devices with their start and end apart: 22, of which 13 were waited for; matrix products, arithmetic and copies ran while one was open for 2% of the time, Pallas kernels for 3%

profile of v19, /device:TPU:1, one launch (start us, length us, event | category | flops | bytes accessed | tf_op | source)
XLA Modules:
  0.0 153.8 jit_solution(7631132047303814190)
XLA Ops:
  0.0 7.5 %all-to-all-start = ((bf16[16,4,64,128]{3,2,1,0:T(8,128)(2,1)}), bf16[16,4,64,128]{3,2,1,0:T(8,128)(2,1)}, u32[]{:S(2)}, u32[]{:S(2)}) async-start(bf16[16,4,64,128]{3,2,1,0:T(8,128)(2,1)} %bitcast.8), calls=%async_computation | async-start | bytes 2097152 | tf_op jit(solution)/shard_map/all_to_all | solution.py:206
  7.5 0.0 copy-start
  7.5 1.7 %copy-done = bf16[4,64,5120]{2,1,0:T(8,128)(2,1)S(1)} copy-done((bf16[4,64,5120]{2,1,0:T(8,128)(2,1)S(1)}, bf16[4,64,5120]{2,1,0:T(8,128)(2,1)}, u32[]{:S(2)}) %copy-start) | copy-done | bytes 2621464
  9.3 1.5 pick_factors.1
  10.8 0.2 collective-permute-start
  11.0 1.9 %collective-permute-done.refs_1_ = bf16[8,320,128]{2,1,0:T(8,128)(2,1)S(1)} collective-permute-done((bf16[8,320,128]{2,1,0:T(8,128)(2,1)S(1)}, bf16[8,320,128]{2,1,0:T(8,128)(2,1)S(1)}, u32[]{:S(2)}, u32[]{:S(2)}) %collective-permute-start) | collective-permute-done | bytes 655392 | tf_op jit(solution)/shard_map/ppermute | solution.py:203
  13.0 0.1 halve.2
  13.0 0.2 collective-permute-start.1
  13.3 1.6 %collective-permute-start.2 = (bf16[4,320,128]{2,1,0:T(8,128)(2,1)S(1)}, bf16[4,320,128]{2,1,0:T(8,128)(2,1)S(1)}, u32[]{:S(2)}, u32[]{:S(2)}) collective-permute-start(bf16[4,320,128]{2,1,0:T(8,128)(2,1)S(1)} %halve.2), channel_id=1, source_target_pairs={{0,2},{1,3},{2,0},{3,1},{4,6},{5,7},{6,4},{7,5},{8,10},{9,11},{10,... | collective-permute-start | bytes 983048 | tf_op jit(solution)/shard_map/ppermute | solution.py:203
  14.8 0.2 collective-permute-done.1.refs_1_
  15.0 0.1 halve.3
  15.1 1.5 collective-permute-start.6
  16.5 14.2 %all-to-all-done.k_ref = bf16[16,4,64,128]{3,2,1,0:T(8,128)(2,1)} async-done(((bf16[16,4,64,128]{3,2,1,0:T(8,128)(2,1)}), bf16[16,4,64,128]{3,2,1,0:T(8,128)(2,1)}, u32[]{:S(2)}, u32[]{:S(2)}) %all-to-all-start) | async-done | bytes 1048608 | tf_op jit(solution)/shard_map/all_to_all | solution.py:206
  30.8 0.1 split.3
  30.9 3.9 %collective-permute-start.3 = (bf16[1,320,128]{2,1,0:T(8,128)(2,1)S(1)}, bf16[1,320,128]{2,1,0:T(8,128)(2,1)S(1)}, u32[]{:S(2)}, u32[]{:S(2)}) collective-permute-start(bf16[1,320,128]{2,1,0:T(8,128)(2,1)S(1)} %get-tuple-element.38), channel_id=1, source_target_pairs={{0,8},{1,9},{2,10},{3,11},{4,12},{5,13},{6,14},{7,15},{8,0},{9,1},... | collective-permute-start | bytes 245768 | tf_op jit(solution)/shard_map/ppermute | solution.py:203
  34.7 1.4 collective-permute-start.5
  36.1 0.5 collective-permute-done.3.refs_1_
  36.6 1.8 %collective-permute-done.4.refs_2_ = bf16[1,320,128]{2,1,0:T(8,128)(2,1)S(1)} collective-permute-done((bf16[1,320,128]{2,1,0:T(8,128)(2,1)S(1)}, bf16[1,320,128]{2,1,0:T(8,128)(2,1)S(1)}, u32[]{:S(2)}, u32[]{:S(2)}) %collective-permute-start.4) | collective-permute-done | bytes 81952 | tf_op jit(solution)/shard_map/ppermute | solution.py:203
  38.3 4.1 %collective-permute-done.5.refs_3_ = bf16[1,320,128]{2,1,0:T(8,128)(2,1)S(1)} collective-permute-done((bf16[1,320,128]{2,1,0:T(8,128)(2,1)S(1)}, bf16[1,320,128]{2,1,0:T(8,128)(2,1)S(1)}, u32[]{:S(2)}, u32[]{:S(2)}) %collective-permute-start.5) | collective-permute-done | bytes 81952 | tf_op jit(solution)/shard_map/ppermute | solution.py:203
  42.4 0.1 collective-permute-start.7
  42.5 0.6 collective-permute-start.8
  43.2 2.9 %collective-permute-start.9 = (bf16[1,320,128]{2,1,0:T(8,128)(2,1)S(1)}, bf16[1,320,128]{2,1,0:T(8,128)(2,1)S(1)}, u32[]{:S(2)}, u32[]{:S(2)}) collective-permute-start(bf16[1,320,128]{2,1,0:T(8,128)(2,1)S(1)} %total.2.refs_0_), channel_id=1, source_target_pairs={{0,12},{1,13},{2,14},{3,15},{4,8},{5,9},{6,10},{7,11},{8,4},{9,5},... | collective-permute-start | bytes 245768 | tf_op jit(solution)/shard_map/ppermute | solution.py:203
  46.1 2.8 %pad_maximum_fusion = bf16[16,8,64,128]{3,2,1,0:T(8,128)(2,1)} fusion(bf16[16,4,64,128]{3,2,1,0:T(8,128)(2,1)S(1)} %bitcast.9, bf16[16,4,64,128]{3,2,1,0:T(8,128)(2,1)} %bitcast.10), kind=kLoop, calls=%fused_computation | loop fusion | flops 1048576 | bytes 4194304 | tf_op jit(solution)/shard_map/concatenate | solution.py:286
  48.8 1.2 collective-permute-done.9.refs_3_
  50.0 6.6 %all-to-all-start.1 = ((bf16[16,8,64,128]{3,2,1,0:T(8,128)(2,1)}), bf16[16,8,64,128]{3,2,1,0:T(8,128)(2,1)S(1)}, u32[]{:S(2)}, u32[]{:S(2)}) async-start(bf16[16,8,64,128]{3,2,1,0:T(8,128)(2,1)} %pad_maximum_fusion), calls=%async_computation.1 | async-start | bytes 4194304 | tf_op jit(solution)/shard_map/all_to_all | solution.py:206
  56.6 1.5 collective-permute-start.12
  58.1 24.3 %collective-permute-done.12.refs_1_ = bf16[4,320,128]{2,1,0:T(8,128)(2,1)S(1)} collective-permute-done((bf16[4,320,128]{2,1,0:T(8,128)(2,1)S(1)}, bf16[4,320,128]{2,1,0:T(8,128)(2,1)S(1)}, u32[]{:S(2)}, u32[]{:S(2)}) %collective-permute-start.12) | collective-permute-done | bytes 327712 | tf_op jit(solution)/shard_map/ppermute | solution.py:203
  82.4 1.3 collective-permute-start.13
  83.7 0.1 split.4
  83.8 0.1 collective-permute-start.10
  83.9 10.0 %collective-permute-done.10.refs_1_ = bf16[2,256,128]{2,1,0:T(8,128)(2,1)S(1)} collective-permute-done((bf16[2,256,128]{2,1,0:T(8,128)(2,1)S(1)}, bf16[2,256,128]{2,1,0:T(8,128)(2,1)S(1)}, u32[]{:S(2)}, u32[]{:S(2)}) %collective-permute-start.10) | collective-permute-done | bytes 131104 | tf_op jit(solution)/shard_map/ppermute | solution.py:203
  93.9 3.9 %collective-permute-start.11 = (bf16[1,256,128]{2,1,0:T(8,128)(2,1)S(1)}, bf16[1,256,128]{2,1,0:T(8,128)(2,1)S(1)}, u32[]{:S(2)}, u32[]{:S(2)}) collective-permute-start(bf16[1,256,128]{2,1,0:T(8,128)(2,1)S(1)} %get-tuple-element.48), channel_id=1, source_target_pairs={{0,8},{1,9},{2,10},{3,11},{4,12},{5,13},{6,14},{7,15},{8,0},{9,1},... | collective-permute-start | bytes 196616 | tf_op jit(solution)/shard_map/ppermute | solution.py:203
  97.8 0.9 low_rank.1.refs_0_
  98.7 1.2 collective-permute-start.14
  99.9 1.3 collective-permute-start.15
  101.2 0.4 collective-permute-start.16
  101.6 0.9 collective-permute-done.15.refs_2_
  102.5 1.9 %collective-permute-done.16.refs_3_ = bf16[2,32,128]{2,1,0:T(8,128)(2,1)S(1)} collective-permute-done((bf16[2,32,128]{2,1,0:T(8,128)(2,1)S(1)}, bf16[2,32,128]{2,1,0:T(8,128)(2,1)S(1)}, u32[]{:S(2)}, u32[]{:S(2)}) %collective-permute-start.16) | collective-permute-done | bytes 16416 | tf_op jit(solution)/shard_map/ppermute | solution.py:203
  104.4 0.6 copy-done.10
  105.0 1.4 choose.1
  106.4 1.1 collective-permute-start.17
  107.5 2.5 %collective-permute-start.19 = (bf16[4,32,128]{2,1,0:T(8,128)(2,1)}, bf16[4,32,128]{2,1,0:T(8,128)(2,1)S(1)}, u32[]{:S(2)}, u32[]{:S(2)}) collective-permute-start(bf16[4,32,128]{2,1,0:T(8,128)(2,1)} %get-tuple-element.54), channel_id=1, source_target_pairs={{0,12},{1,13},{2,14},{3,15},{4,8},{5,9},{6,10},{7,11},{8,4},{9,5},... | collective-permute-start | bytes 98312 | tf_op jit(solution)/shard_map/ppermute | solution.py:203
  110.0 1.7 %collective-permute-done.18.refs_2_ = bf16[4,32,128]{2,1,0:T(8,128)(2,1)S(1)} collective-permute-done((bf16[4,32,128]{2,1,0:T(8,128)(2,1)}, bf16[4,32,128]{2,1,0:T(8,128)(2,1)S(1)}, u32[]{:S(2)}, u32[]{:S(2)}) %collective-permute-start.18) | collective-permute-done | bytes 32800 | tf_op jit(solution)/shard_map/ppermute | solution.py:203
  111.7 0.6 collective-permute-done.19.refs_3_
  112.3 0.8 copy-done.6
  113.1 8.1 %attend.1 = bf16[16,4,64,128]{3,2,1,0:T(8,128)(2,1)S(1)} custom-call(s32[1]{0:T(128)} %bitcast.me_ref, bf16[4,64,128]{2,1,0:T(8,128)(2,1)S(1)} %bitcast.6, bf16[16,8,64,128]{3,2,1,0:T(8,128)(2,1)S(1)} %all-to-all-done.1.q_ref.v_ref, bf16[16,4,64,128]{3,2,1,0:T(8,128)(2,1)} %all-to-all-done.k_ref, bf16[16,8,64,128]{3,2,1,0:T(8,128)(2,1)S(1)} %all-to-all-done.1.q_ref.v_ref, ...), custom_call_target="tpu_custom_call" | custom-call | flops 2147483648 | bytes 4194304 | tf_op jit(solution)/shard_map/attend/pallas_call | solution.py:346
  121.2 31.7 %all_to_all.15 = bf16[16,4,64,128]{3,2,1,0:T(8,128)(2,1)S(1)} all-to-all(bf16[16,4,64,128]{3,2,1,0:T(8,128)(2,1)S(1)} %attend.1), channel_id=1, replica_groups=mesh['grp'=2,'seq'=16] {'seq'}, dimensions={0} | all-to-all | bytes 2097152 | tf_op jit(solution)/shard_map/all_to_all | solution.py:206
  152.8 1.0 copy.10
  (34 shorter events, 0.2 us)
Async XLA Ops:
  0.0 7.5 %copy-start.1 = (bf16[4,64,4096]{2,1,0:T(8,128)(2,1)S(1)}, bf16[4,64,4096]{2,1,0:T(8,128)(2,1)}, u32[]{:S(2)}) copy-start(bf16[4,64,4096]{2,1,0:T(8,128)(2,1)} %up_ref.1) | copy-start | bytes 6291460
  0.0 7.5 %copy-start.4 = (s32[64]{0:T(128)S(1)}, s32[64]{0:T(128)}, u32[]{:S(2)}) copy-start(s32[64]{0:T(128)} %row_ref.1) | copy-start | bytes 772
  0.0 7.5 %copy-start.5 = (s32[2]{0:T(128)S(1)}, s32[2]{0:T(128)}, u32[]{:S(2)}) copy-start(s32[2]{0:T(128)} %req_ref.1) | copy-start | bytes 28
  0.0 30.7 %all-to-all-start = ((bf16[16,4,64,128]{3,2,1,0:T(8,128)(2,1)}), bf16[16,4,64,128]{3,2,1,0:T(8,128)(2,1)}, u32[]{:S(2)}, u32[]{:S(2)}) async-start(bf16[16,4,64,128]{3,2,1,0:T(8,128)(2,1)} %bitcast.8), calls=%async_computation | async-start | bytes 2097152 | tf_op jit(solution)/shard_map/all_to_all | solution.py:206
  7.5 1.7 %copy-start = (bf16[4,64,5120]{2,1,0:T(8,128)(2,1)S(1)}, bf16[4,64,5120]{2,1,0:T(8,128)(2,1)}, u32[]{:S(2)}) copy-start(bf16[4,64,5120]{2,1,0:T(8,128)(2,1)} %down_ref.1) | copy-start | bytes 7864324
  10.8 2.2 %collective-permute-start = (bf16[8,320,128]{2,1,0:T(8,128)(2,1)S(1)}, bf16[8,320,128]{2,1,0:T(8,128)(2,1)S(1)}, u32[]{:S(2)}, u32[]{:S(2)}) collective-permute-start(bf16[8,320,128]{2,1,0:T(8,128)(2,1)S(1)} %get-tuple-element.34), channel_id=1, source_target_pairs={{0,1},{1,0},{2,3},{3,2},{4,5},{5,4},{6,7},{7,6},{8,9},{9,8},{10,11... | collective-permute-start | bytes 1966088 | tf_op jit(solution)/shard_map/ppermute | solution.py:203
  13.0 2.0 %collective-permute-start.1 = (bf16[8,256,128]{2,1,0:T(8,128)(2,1)S(1)}, bf16[8,256,128]{2,1,0:T(8,128)(2,1)S(1)}, u32[]{:S(2)}, u32[]{:S(2)}) collective-permute-start(bf16[8,256,128]{2,1,0:T(8,128)(2,1)S(1)} %get-tuple-element.35), channel_id=1, source_target_pairs={{0,1},{1,0},{2,3},{3,2},{4,5},{5,4},{6,7},{7,6},{8,9},{9,8},{10,11... | collective-permute-start | bytes 1572872 | tf_op jit(solution)/shard_map/ppermute | solution.py:203
  13.3 17.5 %collective-permute-start.2 = (bf16[4,320,128]{2,1,0:T(8,128)(2,1)S(1)}, bf16[4,320,128]{2,1,0:T(8,128)(2,1)S(1)}, u32[]{:S(2)}, u32[]{:S(2)}) collective-permute-start(bf16[4,320,128]{2,1,0:T(8,128)(2,1)S(1)} %halve.2), channel_id=1, source_target_pairs={{0,2},{1,3},{2,0},{3,1},{4,6},{5,7},{6,4},{7,5},{8,10},{9,11},{10,... | collective-permute-start | bytes 983048 | tf_op jit(solution)/shard_map/ppermute | solution.py:203
  15.1 27.4 %collective-permute-start.6 = (bf16[4,256,128]{2,1,0:T(8,128)(2,1)S(1)}, bf16[4,256,128]{2,1,0:T(8,128)(2,1)S(1)}, u32[]{:S(2)}, u32[]{:S(2)}) collective-permute-start(bf16[4,256,128]{2,1,0:T(8,128)(2,1)S(1)} %halve.3), channel_id=1, source_target_pairs={{0,2},{1,3},{2,0},{3,1},{4,6},{5,7},{6,4},{7,5},{8,10},{9,11},{10,... | collective-permute-start | bytes 786440 | tf_op jit(solution)/shard_map/ppermute | solution.py:203
  30.8 15.3 %copy-start.7 = (bf16[2,32,64,128]{3,2,1,0:T(8,128)(2,1)S(1)}, bf16[2,32,64,128]{3,2,1,0:T(8,128)(2,1)}, u32[]{:S(2)}) copy-start(bf16[2,32,64,128]{3,2,1,0:T(8,128)(2,1)} %param.9) | copy-start | bytes 3145732
  30.9 5.7 %collective-permute-start.3 = (bf16[1,320,128]{2,1,0:T(8,128)(2,1)S(1)}, bf16[1,320,128]{2,1,0:T(8,128)(2,1)S(1)}, u32[]{:S(2)}, u32[]{:S(2)}) collective-permute-start(bf16[1,320,128]{2,1,0:T(8,128)(2,1)S(1)} %get-tuple-element.38), channel_id=1, source_target_pairs={{0,8},{1,9},{2,10},{3,11},{4,12},{5,13},{6,14},{7,15},{8,0},{9,1},... | collective-permute-start | bytes 245768 | tf_op jit(solution)/shard_map/ppermute | solution.py:203
  34.7 3.6 %collective-permute-start.4 = (bf16[1,320,128]{2,1,0:T(8,128)(2,1)S(1)}, bf16[1,320,128]{2,1,0:T(8,128)(2,1)S(1)}, u32[]{:S(2)}, u32[]{:S(2)}) collective-permute-start(bf16[1,320,128]{2,1,0:T(8,128)(2,1)S(1)} %get-tuple-element.39), channel_id=1, source_target_pairs={{0,4},{1,5},{2,6},{3,7},{4,0},{5,1},{6,2},{7,3},{8,12},{9,13},{10,... | collective-permute-start | bytes 245768 | tf_op jit(solution)/shard_map/ppermute | solution.py:203
  34.7 7.7 %collective-permute-start.5 = (bf16[1,320,128]{2,1,0:T(8,128)(2,1)S(1)}, bf16[1,320,128]{2,1,0:T(8,128)(2,1)S(1)}, u32[]{:S(2)}, u32[]{:S(2)}) collective-permute-start(bf16[1,320,128]{2,1,0:T(8,128)(2,1)S(1)} %get-tuple-element.40), channel_id=1, source_target_pairs={{0,12},{1,13},{2,14},{3,15},{4,8},{5,9},{6,10},{7,11},{8,4},{9,5},... | collective-permute-start | bytes 245768 | tf_op jit(solution)/shard_map/ppermute | solution.py:203
  42.4 6.4 %collective-permute-start.7 = (bf16[1,320,128]{2,1,0:T(8,128)(2,1)S(1)}, bf16[1,320,128]{2,1,0:T(8,128)(2,1)S(1)}, u32[]{:S(2)}, u32[]{:S(2)}) collective-permute-start(bf16[1,320,128]{2,1,0:T(8,128)(2,1)S(1)} %total.2.refs_0_), channel_id=1, source_target_pairs={{0,8},{1,9},{2,10},{3,11},{4,12},{5,13},{6,14},{7,15},{8,0},{9,1},... | collective-permute-start | bytes 245768 | tf_op jit(solution)/shard_map/ppermute | solution.py:203
  42.5 6.3 %collective-permute-start.8 = (bf16[1,320,128]{2,1,0:T(8,128)(2,1)S(1)}, bf16[1,320,128]{2,1,0:T(8,128)(2,1)S(1)}, u32[]{:S(2)}, u32[]{:S(2)}) collective-permute-start(bf16[1,320,128]{2,1,0:T(8,128)(2,1)S(1)} %total.2.refs_0_), channel_id=1, source_target_pairs={{0,4},{1,5},{2,6},{3,7},{4,0},{5,1},{6,2},{7,3},{8,12},{9,13},{10,... | collective-permute-start | bytes 245768 | tf_op jit(solution)/shard_map/ppermute | solution.py:203
  43.2 6.9 %collective-permute-start.9 = (bf16[1,320,128]{2,1,0:T(8,128)(2,1)S(1)}, bf16[1,320,128]{2,1,0:T(8,128)(2,1)S(1)}, u32[]{:S(2)}, u32[]{:S(2)}) collective-permute-start(bf16[1,320,128]{2,1,0:T(8,128)(2,1)S(1)} %total.2.refs_0_), channel_id=1, source_target_pairs={{0,12},{1,13},{2,14},{3,15},{4,8},{5,9},{6,10},{7,11},{8,4},{9,5},... | collective-permute-start | bytes 245768 | tf_op jit(solution)/shard_map/ppermute | solution.py:203
  50.0 62.3 %all-to-all-start.1 = ((bf16[16,8,64,128]{3,2,1,0:T(8,128)(2,1)}), bf16[16,8,64,128]{3,2,1,0:T(8,128)(2,1)S(1)}, u32[]{:S(2)}, u32[]{:S(2)}) async-start(bf16[16,8,64,128]{3,2,1,0:T(8,128)(2,1)} %pad_maximum_fusion), calls=%async_computation.1 | async-start | bytes 4194304 | tf_op jit(solution)/shard_map/all_to_all | solution.py:206
  56.6 41.3 %copy-start.2 = (bf16[2,64,5120]{2,1,0:T(8,128)(2,1)S(1)}, bf16[2,64,5120]{2,1,0:T(8,128)(2,1)}, u32[]{:S(2)}) copy-start(bf16[2,64,5120]{2,1,0:T(8,128)(2,1)} %x_ref.1) | copy-start | bytes 3932164
  56.6 25.7 %collective-permute-start.12 = (bf16[4,320,128]{2,1,0:T(8,128)(2,1)S(1)}, bf16[4,320,128]{2,1,0:T(8,128)(2,1)S(1)}, u32[]{:S(2)}, u32[]{:S(2)}) collective-permute-start(bf16[4,320,128]{2,1,0:T(8,128)(2,1)S(1)} %join.2.refs_0_), channel_id=1, source_target_pairs={{0,2},{1,3},{2,0},{3,1},{4,6},{5,7},{6,4},{7,5},{8,10},{9,11},{10,... | collective-permute-start | bytes 983048 | tf_op jit(solution)/shard_map/ppermute | solution.py:203
  82.4 15.4 %collective-permute-start.13 = (bf16[8,320,128]{2,1,0:T(8,128)(2,1)S(1)}, bf16[8,320,128]{2,1,0:T(8,128)(2,1)S(1)}, u32[]{:S(2)}, u32[]{:S(2)}) collective-permute-start(bf16[8,320,128]{2,1,0:T(8,128)(2,1)S(1)} %join.3.refs_0_), channel_id=1, source_target_pairs={{0,1},{1,0},{2,3},{3,2},{4,5},{5,4},{6,7},{7,6},{8,9},{9,8},{10,11... | collective-permute-start | bytes 1966088 | tf_op jit(solution)/shard_map/ppermute | solution.py:203
  83.8 10.1 %collective-permute-start.10 = (bf16[2,256,128]{2,1,0:T(8,128)(2,1)S(1)}, bf16[2,256,128]{2,1,0:T(8,128)(2,1)S(1)}, u32[]{:S(2)}, u32[]{:S(2)}) collective-permute-start(bf16[2,256,128]{2,1,0:T(8,128)(2,1)S(1)} %get-tuple-element.46), channel_id=1, source_target_pairs={{0,4},{1,5},{2,6},{3,7},{4,0},{5,1},{6,2},{7,3},{8,12},{9,13},{10,... | collective-permute-start | bytes 393224 | tf_op jit(solution)/shard_map/ppermute | solution.py:203
  93.9 16.1 %collective-permute-start.11 = (bf16[1,256,128]{2,1,0:T(8,128)(2,1)S(1)}, bf16[1,256,128]{2,1,0:T(8,128)(2,1)S(1)}, u32[]{:S(2)}, u32[]{:S(2)}) collective-permute-start(bf16[1,256,128]{2,1,0:T(8,128)(2,1)S(1)} %get-tuple-element.48), channel_id=1, source_target_pairs={{0,8},{1,9},{2,10},{3,11},{4,12},{5,13},{6,14},{7,15},{8,0},{9,1},... | collective-permute-start | bytes 196616 | tf_op jit(solution)/shard_map/ppermute | solution.py:203
  98.7 5.7 %copy-start.3 = (bf16[2,32,128]{2,1,0:T(8,128)(2,1)}, bf16[2,32,128]{2,1,0:T(8,128)(2,1)S(1)}, u32[]{:S(2)}) copy-start(bf16[2,32,128]{2,1,0:T(8,128)(2,1)S(1)} %low_rank.1.refs_0_) | copy-start | bytes 49156
  98.7 2.9 %collective-permute-start.14 = (bf16[2,32,128]{2,1,0:T(8,128)(2,1)S(1)}, bf16[2,32,128]{2,1,0:T(8,128)(2,1)S(1)}, u32[]{:S(2)}, u32[]{:S(2)}) collective-permute-start(bf16[2,32,128]{2,1,0:T(8,128)(2,1)S(1)} %low_rank.1.refs_0_), channel_id=1, source_target_pairs={{0,1},{1,0},{2,3},{3,2},{4,5},{5,4},{6,7},{7,6},{8,9},{9,8},{10,11... | collective-permute-start | bytes 49160 | tf_op jit(solution)/shard_map/ppermute | solution.py:203
  99.9 2.6 %collective-permute-start.15 = (bf16[2,32,128]{2,1,0:T(8,128)(2,1)S(1)}, bf16[2,32,128]{2,1,0:T(8,128)(2,1)S(1)}, u32[]{:S(2)}, u32[]{:S(2)}) collective-permute-start(bf16[2,32,128]{2,1,0:T(8,128)(2,1)S(1)} %low_rank.1.refs_0_), channel_id=1, source_target_pairs={{0,2},{1,3},{2,0},{3,1},{4,6},{5,7},{6,4},{7,5},{8,10},{9,11},{10,... | collective-permute-start | bytes 49160 | tf_op jit(solution)/shard_map/ppermute | solution.py:203
  101.2 3.2 %collective-permute-start.16 = (bf16[2,32,128]{2,1,0:T(8,128)(2,1)S(1)}, bf16[2,32,128]{2,1,0:T(8,128)(2,1)S(1)}, u32[]{:S(2)}, u32[]{:S(2)}) collective-permute-start(bf16[2,32,128]{2,1,0:T(8,128)(2,1)S(1)} %low_rank.1.refs_0_), channel_id=1, source_target_pairs={{0,3},{1,2},{2,1},{3,0},{4,7},{5,6},{6,5},{7,4},{8,11},{9,10},{10,... | collective-permute-start | bytes 49160 | tf_op jit(solution)/shard_map/ppermute | solution.py:203
  101.6 2.8 %copy-start.8 = (bf16[2,32,128]{2,1,0:T(8,128)(2,1)}, bf16[2,32,128]{2,1,0:T(8,128)(2,1)S(1)}, u32[]{:S(2)}) copy-start(bf16[2,32,128]{2,1,0:T(8,128)(2,1)S(1)} %collective-permute-done.14.refs_1_) | copy-start | bytes 49156
  102.5 1.9 %copy-start.9 = (bf16[2,32,128]{2,1,0:T(8,128)(2,1)}, bf16[2,32,128]{2,1,0:T(8,128)(2,1)S(1)}, u32[]{:S(2)}) copy-start(bf16[2,32,128]{2,1,0:T(8,128)(2,1)S(1)} %collective-permute-done.15.refs_2_) | copy-start | bytes 49156
  104.4 0.6 copy-start.10
  106.4 3.6 %collective-permute-start.17 = (bf16[4,32,128]{2,1,0:T(8,128)(2,1)}, bf16[4,32,128]{2,1,0:T(8,128)(2,1)S(1)}, u32[]{:S(2)}, u32[]{:S(2)}) collective-permute-start(bf16[4,32,128]{2,1,0:T(8,128)(2,1)} %get-tuple-element.52), channel_id=1, source_target_pairs={{0,4},{1,5},{2,6},{3,7},{4,0},{5,1},{6,2},{7,3},{8,12},{9,13},{10,... | collective-permute-start | bytes 98312 | tf_op jit(solution)/shard_map/ppermute | solution.py:203
  107.5 4.2 %collective-permute-start.18 = (bf16[4,32,128]{2,1,0:T(8,128)(2,1)}, bf16[4,32,128]{2,1,0:T(8,128)(2,1)S(1)}, u32[]{:S(2)}, u32[]{:S(2)}) collective-permute-start(bf16[4,32,128]{2,1,0:T(8,128)(2,1)} %get-tuple-element.53), channel_id=1, source_target_pairs={{0,8},{1,9},{2,10},{3,11},{4,12},{5,13},{6,14},{7,15},{8,0},{9,1},... | collective-permute-start | bytes 98312 | tf_op jit(solution)/shard_map/ppermute | solution.py:203
  107.5 4.9 %collective-permute-start.19 = (bf16[4,32,128]{2,1,0:T(8,128)(2,1)}, bf16[4,32,128]{2,1,0:T(8,128)(2,1)S(1)}, u32[]{:S(2)}, u32[]{:S(2)}) collective-permute-start(bf16[4,32,128]{2,1,0:T(8,128)(2,1)} %get-tuple-element.54), channel_id=1, source_target_pairs={{0,12},{1,13},{2,14},{3,15},{4,8},{5,9},{6,10},{7,11},{8,4},{9,5},... | collective-permute-start | bytes 98312 | tf_op jit(solution)/shard_map/ppermute | solution.py:203
  112.3 0.8 copy-start.6

commit v20 on v19

--- a/solution.py
+++ b/solution.py
@@ -283,25 +283,24 @@
     held = splitting((after(down_pieces[-1], keys, *up_got[:-1]),), down_got)
     shard = after(total(held[0], to_others(held)), up_got[-1])
     gathered = [shard] + [swap(shard, k) for k in others]
-    asked = jnp.concatenate([by_pairs(values), by_pairs(queries)], axis=1)
-    asked = exchange(after(asked, *gathered))
-
-    up_part = after(up_pieces[-1], *gathered)
-    pair_shape = (2,) + up_part.shape[1:]
+
+    up_part = after(up_pieces[-1], shard)
     near_pair, far_pair = on_vmem(
         functools.partial(sum_kernel, [[(n, 2 * h) for n in range(1 + len(up_got))] for h in (0, 1)]),
-        [pair_shape] * 2,
+        [(2,) + up_part.shape[1:]] * 2,
         "split",
         up_part,
         *up_got,
     )
     came = swap(far_pair, quarter)
+    asked = jnp.concatenate([by_pairs(values), by_pairs(queries)], axis=1)
+    asked = exchange(after(asked, came, *gathered))
     one_shape = (1,) + up_part.shape[1:]
     kept, sent = on_vmem(
         functools.partial(sum_kernel, [[(n, h) for n in range(2)] for h in (0, 1)]),
         [one_shape] * 2,
         "split",
-        near_pair,
+        after(near_pair, *gathered),
         came,
     )
     last = swap(sent, 2 * quarter)
@@ -329,7 +328,7 @@
         ),
         name="low_rank",
     )(me, normed_token_features, *gathered)
-    nearby = [after(low, came)] + [swap(low, k) for k in range(1, LOW)]
+    nearby = [low] + [swap(low, k) for k in range(1, LOW)]
     chosen = pl.pallas_call(
         functools.partial(choose_kernel, per_video),
         in_specs=[SMEM] + [VMEM] * LOW,

time: 154 us -> 151 us (0.981)
  local copies, waits for them, and re-layouts: 4.08 us -> 9.58 us
  starting transfers between devices: 39.6 us -> 34.3 us
  blocking collectives: 31.7 us -> 29.8 us
  waiting for transfers between devices: 63.3 us -> 61.5 us
    unnamed x23 -> x39, local copies, waits for them, and re-layouts: 4.08 us -> 9.58 us
    ppermute x20, starting transfers between devices: 25.5 us -> 21 us  [swap(): return lax.ppermute(tensor, 'seq', [(i, i ^ k) for i in range(devs)])]
    all_to_all x1, blocking collectives: 31.7 us -> 29.8 us  [exchange(): lax.all_to_all(tensor, 'seq', split_axis=0, concat_axis=0, tiled=True)]
where the time goes in v20:
time: 151 us
  waiting for transfers between devices  61.5 us (41%)
  starting transfers between devices  34.3 us (23%)
  blocking collectives  29.8 us (20%)
  Pallas kernels  12.4 us (8%)
  local copies, waits for them, and re-layouts  9.58 us (6%)
  other arithmetic  2.76 us (2%)
    ppermute x20, waiting for transfers between devices, swap(): return lax.ppermute(tensor, 'seq', [(i, i ^ k) for i in range(devs)])  48.1 us
    all_to_all x1, blocking collectives, exchange(): lax.all_to_all(tensor, 'seq', split_axis=0, concat_axis=0, tiled=True)  29.8 us
    ppermute x20, starting transfers between devices, swap(): return lax.ppermute(tensor, 'seq', [(i, i ^ k) for i in range(devs)])  21 us
    all_to_all x2, waiting for transfers between devices, exchange(): lax.all_to_all(tensor, 'seq', split_axis=0, concat_axis=0, tiled=True)  13.4 us
    all_to_all x2, starting transfers between devices, exchange(): lax.all_to_all(tensor, 'seq', split_axis=0, concat_axis=0, tiled=True)  13.3 us
    unnamed x39, local copies, waits for them, and re-layouts  9.58 us
    pallas_call x1, Pallas kernels, body(): pl.pallas_call(functools.partial(attend_kernel, math.gcd(devs, max(1, 256...  7.23 us
  transfers between devices with their start and end apart: 22, of which 13 were waited for; matrix products, arithmetic and copies ran while one was open for 2% of the time, Pallas kernels for 3%

profile of v20, /device:TPU:1, one launch (start us, length us, event | category | flops | bytes accessed | tf_op | source)
XLA Modules:
  0.0 150.6 jit_solution(2169303725824282236)
XLA Ops:
  0.0 7.5 %all-to-all-start = ((bf16[16,4,64,128]{3,2,1,0:T(8,128)(2,1)}), bf16[16,4,64,128]{3,2,1,0:T(8,128)(2,1)S(1)}, u32[]{:S(2)}, u32[]{:S(2)}) async-start(bf16[16,4,64,128]{3,2,1,0:T(8,128)(2,1)} %bitcast.8), calls=%async_computation | async-start | bytes 2097152 | tf_op jit(solution)/shard_map/all_to_all | solution.py:206
  7.5 1.7 %copy-done = bf16[4,64,5120]{2,1,0:T(8,128)(2,1)S(1)} copy-done((bf16[4,64,5120]{2,1,0:T(8,128)(2,1)S(1)}, bf16[4,64,5120]{2,1,0:T(8,128)(2,1)}, u32[]{:S(2)}) %copy-start) | copy-done | bytes 2621464
  9.3 1.7 %pick_factors.1 = (bf16[8,320,128]{2,1,0:T(8,128)(2,1)S(1)}, bf16[4,320,128]{2,1,0:T(8,128)(2,1)S(1)}, bf16[4,320,128]{2,1,0:T(8,128)(2,1)S(1)}, bf16[8,256,128]...) custom-call(s32[1]{0:T(128)} %bitcast.me_ref, s32[64]{0:T(128)S(1)} %copy-done.12, ...), custom_call_target="tpu_custom_call" | custom-call | bytes 4718592 | tf_op jit(solution)/shard_map/pick_factors/pallas_call | solution.py:250
  11.0 2.1 %collective-permute-done.refs_1_ = bf16[8,320,128]{2,1,0:T(8,128)(2,1)S(1)} collective-permute-done((bf16[8,320,128]{2,1,0:T(8,128)(2,1)S(1)}, bf16[8,320,128]{2,1,0:T(8,128)(2,1)S(1)}, u32[]{:S(2)}, u32[]{:S(2)}) %collective-permute-start) | collective-permute-done | bytes 655392 | tf_op jit(solution)/shard_map/ppermute | solution.py:203
  13.1 0.1 halve.2
  13.2 0.2 collective-permute-start.1
  13.4 1.4 collective-permute-start.2
  14.9 0.3 collective-permute-done.1.refs_1_
  15.2 0.8 halve.3
  16.0 1.2 collective-permute-start.6
  17.2 13.4 %all-to-all-done.k_ref = bf16[16,4,64,128]{3,2,1,0:T(8,128)(2,1)S(1)} async-done(((bf16[16,4,64,128]{3,2,1,0:T(8,128)(2,1)}), bf16[16,4,64,128]{3,2,1,0:T(8,128)(2,1)S(1)}, u32[]{:S(2)}, u32[]{:S(2)}) %all-to-all-start) | async-done | bytes 1048608 | tf_op jit(solution)/shard_map/all_to_all | solution.py:206
  30.8 3.9 %collective-permute-start.3 = (bf16[1,320,128]{2,1,0:T(8,128)(2,1)S(1)}, bf16[1,320,128]{2,1,0:T(8,128)(2,1)S(1)}, u32[]{:S(2)}, u32[]{:S(2)}) collective-permute-start(bf16[1,320,128]{2,1,0:T(8,128)(2,1)S(1)} %get-tuple-element.38), channel_id=1, source_target_pairs={{0,8},{1,9},{2,10},{3,11},{4,12},{5,13},{6,14},{7,15},{8,0},{9,1},... | collective-permute-start | bytes 245768 | tf_op jit(solution)/shard_map/ppermute | solution.py:203
  34.6 1.4 collective-permute-start.5
  36.0 0.5 collective-permute-done.3.refs_1_
  36.5 1.8 %collective-permute-done.4.refs_2_ = bf16[1,320,128]{2,1,0:T(8,128)(2,1)S(1)} collective-permute-done((bf16[1,320,128]{2,1,0:T(8,128)(2,1)S(1)}, bf16[1,320,128]{2,1,0:T(8,128)(2,1)S(1)}, u32[]{:S(2)}, u32[]{:S(2)}) %collective-permute-start.4) | collective-permute-done | bytes 81952 | tf_op jit(solution)/shard_map/ppermute | solution.py:203
  38.2 4.1 %collective-permute-done.5.refs_3_ = bf16[1,320,128]{2,1,0:T(8,128)(2,1)S(1)} collective-permute-done((bf16[1,320,128]{2,1,0:T(8,128)(2,1)S(1)}, bf16[1,320,128]{2,1,0:T(8,128)(2,1)S(1)}, u32[]{:S(2)}, u32[]{:S(2)}) %collective-permute-start.5) | collective-permute-done | bytes 81952 | tf_op jit(solution)/shard_map/ppermute | solution.py:203
  42.4 0.6 collective-permute-start.8
  43.1 2.9 %collective-permute-start.9 = (bf16[1,320,128]{2,1,0:T(8,128)(2,1)S(1)}, bf16[1,320,128]{2,1,0:T(8,128)(2,1)S(1)}, u32[]{:S(2)}, u32[]{:S(2)}) collective-permute-start(bf16[1,320,128]{2,1,0:T(8,128)(2,1)S(1)} %total.2.refs_0_), channel_id=1, source_target_pairs={{0,12},{1,13},{2,14},{3,15},{4,8},{5,9},{6,10},{7,11},{8,4},{9,5},... | collective-permute-start | bytes 245768 | tf_op jit(solution)/shard_map/ppermute | solution.py:203
  46.0 0.9 copy-done.4
  47.1 2.8 %pad_maximum_fusion = bf16[16,8,64,128]{3,2,1,0:T(8,128)(2,1)} fusion(bf16[16,4,64,128]{3,2,1,0:T(8,128)(2,1)S(1)} %bitcast.9, bf16[16,4,64,128]{3,2,1,0:T(8,128)(2,1)} %bitcast.10), kind=kLoop, calls=%fused_computation | loop fusion | flops 1048576 | bytes 4194304 | tf_op jit(solution)/shard_map/concatenate | solution.py:296
  49.8 0.6 copy-done.5
  50.5 0.6 copy-done.7
  51.1 0.6 copy-done.9
  51.7 1.0 collective-permute-done.10.refs_1_
  52.7 5.8 %all-to-all-start.1 = ((bf16[16,8,64,128]{3,2,1,0:T(8,128)(2,1)}), bf16[16,8,64,128]{3,2,1,0:T(8,128)(2,1)S(1)}, u32[]{:S(2)}, u32[]{:S(2)}) async-start(bf16[16,8,64,128]{3,2,1,0:T(8,128)(2,1)} %pad_maximum_fusion), calls=%async_computation.1 | async-start | bytes 4194304 | tf_op jit(solution)/shard_map/all_to_all | solution.py:206
  58.6 0.9 copy-done.6
  59.5 0.9 copy-done.8
  60.3 0.9 copy-done.10
  61.3 1.5 collective-permute-start.12
  62.7 21.6 %collective-permute-done.12.refs_1_ = bf16[4,320,128]{2,1,0:T(8,128)(2,1)S(1)} collective-permute-done((bf16[4,320,128]{2,1,0:T(8,128)(2,1)S(1)}, bf16[4,320,128]{2,1,0:T(8,128)(2,1)S(1)}, u32[]{:S(2)}, u32[]{:S(2)}) %collective-permute-start.12) | collective-permute-done | bytes 327712 | tf_op jit(solution)/shard_map/ppermute | solution.py:203
  84.4 1.3 collective-permute-start.13
  85.8 1.6 %collective-permute-done.13.refs_1_ = bf16[8,320,128]{2,1,0:T(8,128)(2,1)S(1)} collective-permute-done((bf16[8,320,128]{2,1,0:T(8,128)(2,1)S(1)}, bf16[8,320,128]{2,1,0:T(8,128)(2,1)S(1)}, u32[]{:S(2)}, u32[]{:S(2)}) %collective-permute-start.13) | collective-permute-done | bytes 655392 | tf_op jit(solution)/shard_map/ppermute | solution.py:203
  87.4 0.9 low_rank.1.refs_0_
  88.3 0.4 collective-permute-start.14
  88.7 1.8 %collective-permute-start.16 = (bf16[2,32,128]{2,1,0:T(8,128)(2,1)S(1)}, bf16[2,32,128]{2,1,0:T(8,128)(2,1)S(1)}, u32[]{:S(2)}, u32[]{:S(2)}) collective-permute-start(bf16[2,32,128]{2,1,0:T(8,128)(2,1)S(1)} %low_rank.1.refs_0_), channel_id=1, source_target_pairs={{0,3},{1,2},{2,1},{3,0},{4,7},{5,6},{6,5},{7,4},{8,11},{9,10},{10,... | collective-permute-start | bytes 49160 | tf_op jit(solution)/shard_map/ppermute | solution.py:203
  90.5 0.8 collective-permute-done.15.refs_2_
  91.3 0.9 collective-permute-done.16.refs_3_
  92.2 0.6 copy-done.18
  92.8 1.4 choose.1
  94.2 2.0 %collective-permute-start.17 = (bf16[4,32,128]{2,1,0:T(8,128)(2,1)}, bf16[4,32,128]{2,1,0:T(8,128)(2,1)S(1)}, u32[]{:S(2)}, u32[]{:S(2)}) collective-permute-start(bf16[4,32,128]{2,1,0:T(8,128)(2,1)} %get-tuple-element.52), channel_id=1, source_target_pairs={{0,4},{1,5},{2,6},{3,7},{4,0},{5,1},{6,2},{7,3},{8,12},{9,13},{10,... | collective-permute-start | bytes 98312 | tf_op jit(solution)/shard_map/ppermute | solution.py:203
  96.2 1.4 collective-permute-start.18
  97.6 0.7 collective-permute-start.19
  98.3 12.8 %collective-permute-done.11.refs_1_ = bf16[1,256,128]{2,1,0:T(8,128)(2,1)S(1)} collective-permute-done((bf16[1,256,128]{2,1,0:T(8,128)(2,1)S(1)}, bf16[1,256,128]{2,1,0:T(8,128)(2,1)S(1)}, u32[]{:S(2)}, u32[]{:S(2)}) %collective-permute-start.11) | collective-permute-done | bytes 65568 | tf_op jit(solution)/shard_map/ppermute | solution.py:203
  111.2 0.7 collective-permute-done.18.refs_2_
  111.8 0.8 copy-done.14
  112.6 7.2 %attend.1 = bf16[16,4,64,128]{3,2,1,0:T(8,128)(2,1)S(1)} custom-call(s32[1]{0:T(128)} %bitcast.me_ref, bf16[4,64,128]{2,1,0:T(8,128)(2,1)S(1)} %bitcast.6, bf16[16,8,64,128]{3,2,1,0:T(8,128)(2,1)S(1)} %all-to-all-done.1.q_ref.v_ref, bf16[16,4,64,128]{3,2,1,0:T(8,128)(2,1)S(1)} %all-to-all-done.k_ref, ...), custom_call_target="tpu_custom_call" | custom-call | flops 2147483648 | bytes 4194304 | tf_op jit(solution)/shard_map/attend/pallas_call | solution.py:345
  119.8 29.8 %all_to_all.15 = bf16[16,4,64,128]{3,2,1,0:T(8,128)(2,1)S(1)} all-to-all(bf16[16,4,64,128]{3,2,1,0:T(8,128)(2,1)S(1)} %attend.1), channel_id=1, replica_groups=mesh['grp'=2,'seq'=16] {'seq'}, dimensions={0} | all-to-all | bytes 2097152 | tf_op jit(solution)/shard_map/all_to_all | solution.py:206
  149.7 1.0 copy.10
  (50 shorter events, 0.7 us)
Async XLA Ops:
  0.0 7.5 %copy-start.12 = (s32[64]{0:T(128)S(1)}, s32[64]{0:T(128)}, u32[]{:S(2)}) copy-start(s32[64]{0:T(128)} %row_ref.1) | copy-start | bytes 772
  0.0 7.5 %copy-start.13 = (s32[2]{0:T(128)S(1)}, s32[2]{0:T(128)}, u32[]{:S(2)}) copy-start(s32[2]{0:T(128)} %req_ref.1) | copy-start | bytes 28
  0.0 7.5 %copy-start.1 = (bf16[4,64,4096]{2,1,0:T(8,128)(2,1)S(1)}, bf16[4,64,4096]{2,1,0:T(8,128)(2,1)}, u32[]{:S(2)}) copy-start(bf16[4,64,4096]{2,1,0:T(8,128)(2,1)} %up_ref.1) | copy-start | bytes 6291460
  0.0 30.6 %all-to-all-start = ((bf16[16,4,64,128]{3,2,1,0:T(8,128)(2,1)}), bf16[16,4,64,128]{3,2,1,0:T(8,128)(2,1)S(1)}, u32[]{:S(2)}, u32[]{:S(2)}) async-start(bf16[16,4,64,128]{3,2,1,0:T(8,128)(2,1)} %bitcast.8), calls=%async_computation | async-start | bytes 2097152 | tf_op jit(solution)/shard_map/all_to_all | solution.py:206
  7.5 1.7 %copy-start = (bf16[4,64,5120]{2,1,0:T(8,128)(2,1)S(1)}, bf16[4,64,5120]{2,1,0:T(8,128)(2,1)}, u32[]{:S(2)}) copy-start(bf16[4,64,5120]{2,1,0:T(8,128)(2,1)} %down_ref.1) | copy-start | bytes 7864324
  11.0 5.1 %copy-start.3 = (bf16[4,256,128]{2,1,0:T(8,128)(2,1)}, bf16[4,256,128]{2,1,0:T(8,128)(2,1)S(1)}, u32[]{:S(2)}) copy-start(bf16[4,256,128]{2,1,0:T(8,128)(2,1)S(1)} %get-tuple-element.44.refs_0_) | copy-start | bytes 786436
  11.0 2.2 %collective-permute-start = (bf16[8,320,128]{2,1,0:T(8,128)(2,1)S(1)}, bf16[8,320,128]{2,1,0:T(8,128)(2,1)S(1)}, u32[]{:S(2)}, u32[]{:S(2)}) collective-permute-start(bf16[8,320,128]{2,1,0:T(8,128)(2,1)S(1)} %get-tuple-element.34), channel_id=1, source_target_pairs={{0,1},{1,0},{2,3},{3,2},{4,5},{5,4},{6,7},{7,6},{8,9},{9,8},{10,11... | collective-permute-start | bytes 1966088 | tf_op jit(solution)/shard_map/ppermute | solution.py:203
  13.2 2.0 %collective-permute-start.1 = (bf16[8,256,128]{2,1,0:T(8,128)(2,1)S(1)}, bf16[8,256,128]{2,1,0:T(8,128)(2,1)S(1)}, u32[]{:S(2)}, u32[]{:S(2)}) collective-permute-start(bf16[8,256,128]{2,1,0:T(8,128)(2,1)S(1)} %get-tuple-element.35), channel_id=1, source_target_pairs={{0,1},{1,0},{2,3},{3,2},{4,5},{5,4},{6,7},{7,6},{8,9},{9,8},{10,11... | collective-permute-start | bytes 1572872 | tf_op jit(solution)/shard_map/ppermute | solution.py:203
  13.4 17.2 %collective-permute-start.2 = (bf16[4,320,128]{2,1,0:T(8,128)(2,1)S(1)}, bf16[4,320,128]{2,1,0:T(8,128)(2,1)S(1)}, u32[]{:S(2)}, u32[]{:S(2)}) collective-permute-start(bf16[4,320,128]{2,1,0:T(8,128)(2,1)S(1)} %halve.2), channel_id=1, source_target_pairs={{0,2},{1,3},{2,0},{3,1},{4,6},{5,7},{6,4},{7,5},{8,10},{9,11},{10,... | collective-permute-start | bytes 983048 | tf_op jit(solution)/shard_map/ppermute | solution.py:203
  16.0 26.3 %collective-permute-start.6 = (bf16[4,256,128]{2,1,0:T(8,128)(2,1)}, bf16[4,256,128]{2,1,0:T(8,128)(2,1)S(1)}, u32[]{:S(2)}, u32[]{:S(2)}) collective-permute-start(bf16[4,256,128]{2,1,0:T(8,128)(2,1)} %halve.3), channel_id=1, source_target_pairs={{0,2},{1,3},{2,0},{3,1},{4,6},{5,7},{6,4},{7,5},{8,10},{9,11},{10,... | collective-permute-start | bytes 786440 | tf_op jit(solution)/shard_map/ppermute | solution.py:203
  30.7 16.4 %copy-start.15 = (bf16[2,32,64,128]{3,2,1,0:T(8,128)(2,1)S(1)}, bf16[2,32,64,128]{3,2,1,0:T(8,128)(2,1)}, u32[]{:S(2)}) copy-start(bf16[2,32,64,128]{3,2,1,0:T(8,128)(2,1)} %param.9) | copy-start | bytes 3145732
  30.8 5.7 %collective-permute-start.3 = (bf16[1,320,128]{2,1,0:T(8,128)(2,1)S(1)}, bf16[1,320,128]{2,1,0:T(8,128)(2,1)S(1)}, u32[]{:S(2)}, u32[]{:S(2)}) collective-permute-start(bf16[1,320,128]{2,1,0:T(8,128)(2,1)S(1)} %get-tuple-element.38), channel_id=1, source_target_pairs={{0,8},{1,9},{2,10},{3,11},{4,12},{5,13},{6,14},{7,15},{8,0},{9,1},... | collective-permute-start | bytes 245768 | tf_op jit(solution)/shard_map/ppermute | solution.py:203
  34.6 3.6 %collective-permute-start.4 = (bf16[1,320,128]{2,1,0:T(8,128)(2,1)S(1)}, bf16[1,320,128]{2,1,0:T(8,128)(2,1)S(1)}, u32[]{:S(2)}, u32[]{:S(2)}) collective-permute-start(bf16[1,320,128]{2,1,0:T(8,128)(2,1)S(1)} %get-tuple-element.39), channel_id=1, source_target_pairs={{0,4},{1,5},{2,6},{3,7},{4,0},{5,1},{6,2},{7,3},{8,12},{9,13},{10,... | collective-permute-start | bytes 245768 | tf_op jit(solution)/shard_map/ppermute | solution.py:203
  34.6 7.7 %collective-permute-start.5 = (bf16[1,320,128]{2,1,0:T(8,128)(2,1)S(1)}, bf16[1,320,128]{2,1,0:T(8,128)(2,1)S(1)}, u32[]{:S(2)}, u32[]{:S(2)}) collective-permute-start(bf16[1,320,128]{2,1,0:T(8,128)(2,1)S(1)} %get-tuple-element.40), channel_id=1, source_target_pairs={{0,12},{1,13},{2,14},{3,15},{4,8},{5,9},{6,10},{7,11},{8,4},{9,5},... | collective-permute-start | bytes 245768 | tf_op jit(solution)/shard_map/ppermute | solution.py:203
  42.3 7.5 %collective-permute-start.7 = (bf16[1,320,128]{2,1,0:T(8,128)(2,1)S(1)}, bf16[1,320,128]{2,1,0:T(8,128)(2,1)S(1)}, u32[]{:S(2)}, u32[]{:S(2)}) collective-permute-start(bf16[1,320,128]{2,1,0:T(8,128)(2,1)S(1)} %total.2.refs_0_), channel_id=1, source_target_pairs={{0,8},{1,9},{2,10},{3,11},{4,12},{5,13},{6,14},{7,15},{8,0},{9,1},... | collective-permute-start | bytes 245768 | tf_op jit(solution)/shard_map/ppermute | solution.py:203
  42.4 8.1 %collective-permute-start.8 = (bf16[1,320,128]{2,1,0:T(8,128)(2,1)S(1)}, bf16[1,320,128]{2,1,0:T(8,128)(2,1)S(1)}, u32[]{:S(2)}, u32[]{:S(2)}) collective-permute-start(bf16[1,320,128]{2,1,0:T(8,128)(2,1)S(1)} %total.2.refs_0_), channel_id=1, source_target_pairs={{0,4},{1,5},{2,6},{3,7},{4,0},{5,1},{6,2},{7,3},{8,12},{9,13},{10,... | collective-permute-start | bytes 245768 | tf_op jit(solution)/shard_map/ppermute | solution.py:203
  43.1 8.1 %collective-permute-start.9 = (bf16[1,320,128]{2,1,0:T(8,128)(2,1)S(1)}, bf16[1,320,128]{2,1,0:T(8,128)(2,1)S(1)}, u32[]{:S(2)}, u32[]{:S(2)}) collective-permute-start(bf16[1,320,128]{2,1,0:T(8,128)(2,1)S(1)} %total.2.refs_0_), channel_id=1, source_target_pairs={{0,12},{1,13},{2,14},{3,15},{4,8},{5,9},{6,10},{7,11},{8,4},{9,5},... | collective-permute-start | bytes 245768 | tf_op jit(solution)/shard_map/ppermute | solution.py:203
  46.0 0.9 copy-start.4
  47.0 5.7 %collective-permute-start.10 = (bf16[2,256,128]{2,1,0:T(8,128)(2,1)S(1)}, bf16[2,256,128]{2,1,0:T(8,128)(2,1)S(1)}, u32[]{:S(2)}, u32[]{:S(2)}) collective-permute-start(bf16[2,256,128]{2,1,0:T(8,128)(2,1)S(1)} %get-tuple-element.47), channel_id=1, source_target_pairs={{0,4},{1,5},{2,6},{3,7},{4,0},{5,1},{6,2},{7,3},{8,12},{9,13},{10,... | collective-permute-start | bytes 393224 | tf_op jit(solution)/shard_map/ppermute | solution.py:203
  49.8 0.6 copy-start.5
  50.5 0.6 copy-start.7
  51.1 0.6 copy-start.9
  52.7 59.1 %all-to-all-start.1 = ((bf16[16,8,64,128]{3,2,1,0:T(8,128)(2,1)}), bf16[16,8,64,128]{3,2,1,0:T(8,128)(2,1)S(1)}, u32[]{:S(2)}, u32[]{:S(2)}) async-start(bf16[16,8,64,128]{3,2,1,0:T(8,128)(2,1)} %pad_maximum_fusion), calls=%async_computation.1 | async-start | bytes 4194304 | tf_op jit(solution)/shard_map/all_to_all | solution.py:206
  58.6 0.9 copy-start.6
  59.5 0.9 copy-start.8
  60.3 0.9 copy-start.10
  61.2 26.2 %copy-start.2 = (bf16[2,64,5120]{2,1,0:T(8,128)(2,1)S(1)}, bf16[2,64,5120]{2,1,0:T(8,128)(2,1)}, u32[]{:S(2)}) copy-start(bf16[2,64,5120]{2,1,0:T(8,128)(2,1)} %x_ref.1) | copy-start | bytes 3932164
  61.3 23.1 %collective-permute-start.12 = (bf16[4,320,128]{2,1,0:T(8,128)(2,1)S(1)}, bf16[4,320,128]{2,1,0:T(8,128)(2,1)S(1)}, u32[]{:S(2)}, u32[]{:S(2)}) collective-permute-start(bf16[4,320,128]{2,1,0:T(8,128)(2,1)S(1)} %join.2.refs_0_), channel_id=1, source_target_pairs={{0,2},{1,3},{2,0},{3,1},{4,6},{5,7},{6,4},{7,5},{8,10},{9,11},{10,... | collective-permute-start | bytes 983048 | tf_op jit(solution)/shard_map/ppermute | solution.py:203
  84.4 3.0 %collective-permute-start.13 = (bf16[8,320,128]{2,1,0:T(8,128)(2,1)S(1)}, bf16[8,320,128]{2,1,0:T(8,128)(2,1)S(1)}, u32[]{:S(2)}, u32[]{:S(2)}) collective-permute-start(bf16[8,320,128]{2,1,0:T(8,128)(2,1)S(1)} %join.3.refs_0_), channel_id=1, source_target_pairs={{0,1},{1,0},{2,3},{3,2},{4,5},{5,4},{6,7},{7,6},{8,9},{9,8},{10,11... | collective-permute-start | bytes 1966088 | tf_op jit(solution)/shard_map/ppermute | solution.py:203
  85.7 25.4 %collective-permute-start.11 = (bf16[1,256,128]{2,1,0:T(8,128)(2,1)S(1)}, bf16[1,256,128]{2,1,0:T(8,128)(2,1)S(1)}, u32[]{:S(2)}, u32[]{:S(2)}) collective-permute-start(bf16[1,256,128]{2,1,0:T(8,128)(2,1)S(1)} %get-tuple-element.49), channel_id=1, source_target_pairs={{0,8},{1,9},{2,10},{3,11},{4,12},{5,13},{6,14},{7,15},{8,0},{9,1},... | collective-permute-start | bytes 196616 | tf_op jit(solution)/shard_map/ppermute | solution.py:203
  88.3 3.9 %copy-start.11 = (bf16[2,32,128]{2,1,0:T(8,128)(2,1)}, bf16[2,32,128]{2,1,0:T(8,128)(2,1)S(1)}, u32[]{:S(2)}) copy-start(bf16[2,32,128]{2,1,0:T(8,128)(2,1)S(1)} %low_rank.1.refs_0_) | copy-start | bytes 49156
  88.3 2.2 %collective-permute-start.14 = (bf16[2,32,128]{2,1,0:T(8,128)(2,1)S(1)}, bf16[2,32,128]{2,1,0:T(8,128)(2,1)S(1)}, u32[]{:S(2)}, u32[]{:S(2)}) collective-permute-start(bf16[2,32,128]{2,1,0:T(8,128)(2,1)S(1)} %low_rank.1.refs_0_), channel_id=1, source_target_pairs={{0,1},{1,0},{2,3},{3,2},{4,5},{5,4},{6,7},{7,6},{8,9},{9,8},{10,11... | collective-permute-start | bytes 49160 | tf_op jit(solution)/shard_map/ppermute | solution.py:203
  88.7 2.6 %collective-permute-start.15 = (bf16[2,32,128]{2,1,0:T(8,128)(2,1)S(1)}, bf16[2,32,128]{2,1,0:T(8,128)(2,1)S(1)}, u32[]{:S(2)}, u32[]{:S(2)}) collective-permute-start(bf16[2,32,128]{2,1,0:T(8,128)(2,1)S(1)} %low_rank.1.refs_0_), channel_id=1, source_target_pairs={{0,2},{1,3},{2,0},{3,1},{4,6},{5,7},{6,4},{7,5},{8,10},{9,11},{10,... | collective-permute-start | bytes 49160 | tf_op jit(solution)/shard_map/ppermute | solution.py:203
  88.7 3.5 %collective-permute-start.16 = (bf16[2,32,128]{2,1,0:T(8,128)(2,1)S(1)}, bf16[2,32,128]{2,1,0:T(8,128)(2,1)S(1)}, u32[]{:S(2)}, u32[]{:S(2)}) collective-permute-start(bf16[2,32,128]{2,1,0:T(8,128)(2,1)S(1)} %low_rank.1.refs_0_), channel_id=1, source_target_pairs={{0,3},{1,2},{2,1},{3,0},{4,7},{5,6},{6,5},{7,4},{8,11},{9,10},{10,... | collective-permute-start | bytes 49160 | tf_op jit(solution)/shard_map/ppermute | solution.py:203
  90.5 1.7 %copy-start.16 = (bf16[2,32,128]{2,1,0:T(8,128)(2,1)}, bf16[2,32,128]{2,1,0:T(8,128)(2,1)S(1)}, u32[]{:S(2)}) copy-start(bf16[2,32,128]{2,1,0:T(8,128)(2,1)S(1)} %collective-permute-done.14.refs_1_) | copy-start | bytes 49156
  91.3 0.9 copy-start.17
  92.2 0.6 copy-start.18
  94.2 16.9 %collective-permute-start.17 = (bf16[4,32,128]{2,1,0:T(8,128)(2,1)}, bf16[4,32,128]{2,1,0:T(8,128)(2,1)S(1)}, u32[]{:S(2)}, u32[]{:S(2)}) collective-permute-start(bf16[4,32,128]{2,1,0:T(8,128)(2,1)} %get-tuple-element.52), channel_id=1, source_target_pairs={{0,4},{1,5},{2,6},{3,7},{4,0},{5,1},{6,2},{7,3},{8,12},{9,13},{10,... | collective-permute-start | bytes 98312 | tf_op jit(solution)/shard_map/ppermute | solution.py:203
  96.2 15.6 %collective-permute-start.18 = (bf16[4,32,128]{2,1,0:T(8,128)(2,1)}, bf16[4,32,128]{2,1,0:T(8,128)(2,1)S(1)}, u32[]{:S(2)}, u32[]{:S(2)}) collective-permute-start(bf16[4,32,128]{2,1,0:T(8,128)(2,1)} %get-tuple-element.53), channel_id=1, source_target_pairs={{0,8},{1,9},{2,10},{3,11},{4,12},{5,13},{6,14},{7,15},{8,0},{9,1},... | collective-permute-start | bytes 98312 | tf_op jit(solution)/shard_map/ppermute | solution.py:203
  97.6 14.2 %collective-permute-start.19 = (bf16[4,32,128]{2,1,0:T(8,128)(2,1)}, bf16[4,32,128]{2,1,0:T(8,128)(2,1)S(1)}, u32[]{:S(2)}, u32[]{:S(2)}) collective-permute-start(bf16[4,32,128]{2,1,0:T(8,128)(2,1)} %get-tuple-element.54), channel_id=1, source_target_pairs={{0,12},{1,13},{2,14},{3,15},{4,8},{5,9},{6,10},{7,11},{8,4},{9,5},... | collective-permute-start | bytes 98312 | tf_op jit(solution)/shard_map/ppermute | solution.py:203
  111.8 0.8 copy-start.14

commit v21 on v20

--- a/solution.py
+++ b/solution.py
@@ -280,8 +280,8 @@
         down_got.append(swap(piece, 1 << i))
     part = after(halving(up_pieces, up_got, bits - 3), piece)
     up_got.append(swap(part, 1 << (bits - 3)))
-    held = splitting((after(down_pieces[-1], keys, *up_got[:-1]),), down_got)
-    shard = after(total(held[0], to_others(held)), up_got[-1])
+    held = splitting((after(down_pieces[-1], *up_got[:-1]),), down_got)
+    shard = after(total(held[0], to_others(held)), keys, up_got[-1])
     gathered = [shard] + [swap(shard, k) for k in others]
 
     up_part = after(up_pieces[-1], shard)
@@ -300,7 +300,7 @@
         functools.partial(sum_kernel, [[(n, h) for n in range(2)] for h in (0, 1)]),
         [one_shape] * 2,
         "split",
-        after(near_pair, *gathered),
+        near_pair,
         came,
     )
     last = swap(sent, 2 * quarter)

time: 151 us -> 148 us (0.980)
  waiting for transfers between devices: 61.5 us -> 57.6 us
  starting transfers between devices: 34.3 us -> 36.1 us
    all_to_all x2, waiting for transfers between devices: 13.4 us -> 0.01 us  [exchange(): lax.all_to_all(tensor, 'seq', split_axis=0, concat_axis=0, tiled=True)]
    ppermute x20, waiting for transfers between devices: 48.1 us -> 57.6 us  [swap(): return lax.ppermute(tensor, 'seq', [(i, i ^ k) for i in range(devs)])]
    ppermute x20, starting transfers between devices: 21 us -> 23.2 us  [swap(): return lax.ppermute(tensor, 'seq', [(i, i ^ k) for i in range(devs)])]
    unnamed x39 -> x37, local copies, waits for them, and re-layouts: 9.58 us -> 9.26 us
  transfers between devices with their start and end apart: 22 -> 22, of which waited for: 13 -> 11; matrix products, arithmetic and copies ran while one was open for 2% -> 2% of each run, Pallas kernels for 3% -> 3%
where the time goes in v21:
time: 148 us
  waiting for transfers between devices  57.6 us (39%)
  starting transfers between devices  36.1 us (24%)
  blocking collectives  29.8 us (20%)
  Pallas kernels  11.6 us (8%)
  local copies, waits for them, and re-layouts  9.26 us (6%)
  other arithmetic  3.07 us (2%)
    ppermute x20, waiting for transfers between devices, swap(): return lax.ppermute(tensor, 'seq', [(i, i ^ k) for i in range(devs)])  57.6 us
    all_to_all x1, blocking collectives, exchange(): lax.all_to_all(tensor, 'seq', split_axis=0, concat_axis=0, tiled=True)  29.8 us
    ppermute x20, starting transfers between devices, swap(): return lax.ppermute(tensor, 'seq', [(i, i ^ k) for i in range(devs)])  23.2 us
    all_to_all x2, starting transfers between devices, exchange(): lax.all_to_all(tensor, 'seq', split_axis=0, concat_axis=0, tiled=True)  13 us
    unnamed x37, local copies, waits for them, and re-layouts  9.26 us
    pallas_call x1, Pallas kernels, body(): pl.pallas_call(functools.partial(attend_kernel, math.gcd(devs, max(1, 256...  7.23 us
    concatenate x1, other arithmetic, body(): asked = jnp.concatenate([by_pairs(values), by_pairs(queries)], axis=1)  3.07 us
  transfers between devices with their start and end apart: 22, of which 11 were waited for; matrix products, arithmetic and copies ran while one was open for 2% of the time, Pallas kernels for 3%

profile of v21, /device:TPU:1, one launch (start us, length us, event | category | flops | bytes accessed | tf_op | source)
XLA Modules:
  0.0 147.7 jit_solution(15813914790473431923)
XLA Ops:
  0.0 7.5 %all-to-all-start = ((bf16[16,4,64,128]{3,2,1,0:T(8,128)(2,1)}), bf16[16,4,64,128]{3,2,1,0:T(8,128)(2,1)S(1)}, u32[]{:S(2)}, u32[]{:S(2)}) async-start(bf16[16,4,64,128]{3,2,1,0:T(8,128)(2,1)} %bitcast.8), calls=%async_computation | async-start | bytes 2097152 | tf_op jit(solution)/shard_map/all_to_all | solution.py:206
  7.5 1.7 %copy-done = bf16[4,64,5120]{2,1,0:T(8,128)(2,1)S(1)} copy-done((bf16[4,64,5120]{2,1,0:T(8,128)(2,1)S(1)}, bf16[4,64,5120]{2,1,0:T(8,128)(2,1)}, u32[]{:S(2)}) %copy-start) | copy-done | bytes 2621464
  9.3 1.5 %pick_factors.1 = (bf16[8,320,128]{2,1,0:T(8,128)(2,1)S(1)}, bf16[4,320,128]{2,1,0:T(8,128)(2,1)S(1)}, bf16[4,320,128]{2,1,0:T(8,128)(2,1)S(1)}, bf16[8,256,128]...) custom-call(s32[1]{0:T(128)} %bitcast.me_ref, s32[64]{0:T(128)S(1)} %copy-done.12, ...), custom_call_target="tpu_custom_call" | custom-call | bytes 4718592 | tf_op jit(solution)/shard_map/pick_factors/pallas_call | solution.py:250
  10.8 0.2 collective-permute-start
  11.0 2.0 %collective-permute-done.refs_1_ = bf16[8,320,128]{2,1,0:T(8,128)(2,1)S(1)} collective-permute-done((bf16[8,320,128]{2,1,0:T(8,128)(2,1)S(1)}, bf16[8,320,128]{2,1,0:T(8,128)(2,1)S(1)}, u32[]{:S(2)}, u32[]{:S(2)}) %collective-permute-start) | collective-permute-done | bytes 655392 | tf_op jit(solution)/shard_map/ppermute | solution.py:203
  13.1 0.2 collective-permute-start.1
  13.3 1.6 %collective-permute-start.2 = (bf16[4,320,128]{2,1,0:T(8,128)(2,1)S(1)}, bf16[4,320,128]{2,1,0:T(8,128)(2,1)S(1)}, u32[]{:S(2)}, u32[]{:S(2)}) collective-permute-start(bf16[4,320,128]{2,1,0:T(8,128)(2,1)S(1)} %halve.2), channel_id=1, source_target_pairs={{0,2},{1,3},{2,0},{3,1},{4,6},{5,7},{6,4},{7,5},{8,10},{9,11},{10,... | collective-permute-start | bytes 983048 | tf_op jit(solution)/shard_map/ppermute | solution.py:203
  14.9 0.2 collective-permute-done.1.refs_1_
  15.1 1.4 collective-permute-start.6
  16.6 10.3 %collective-permute-done.2.refs_2_ = bf16[4,320,128]{2,1,0:T(8,128)(2,1)S(1)} collective-permute-done((bf16[4,320,128]{2,1,0:T(8,128)(2,1)S(1)}, bf16[4,320,128]{2,1,0:T(8,128)(2,1)S(1)}, u32[]{:S(2)}, u32[]{:S(2)}) %collective-permute-start.2) | collective-permute-done | bytes 327712 | tf_op jit(solution)/shard_map/ppermute | solution.py:203
  26.9 0.2 split.3
  27.0 3.1 %collective-permute-start.3 = (bf16[1,320,128]{2,1,0:T(8,128)(2,1)S(1)}, bf16[1,320,128]{2,1,0:T(8,128)(2,1)S(1)}, u32[]{:S(2)}, u32[]{:S(2)}) collective-permute-start(bf16[1,320,128]{2,1,0:T(8,128)(2,1)S(1)} %get-tuple-element.37), channel_id=1, source_target_pairs={{0,8},{1,9},{2,10},{3,11},{4,12},{5,13},{6,14},{7,15},{8,0},{9,1},... | collective-permute-start | bytes 245768 | tf_op jit(solution)/shard_map/ppermute | solution.py:203
  30.2 0.1 collective-permute-start.4
  30.3 1.7 %collective-permute-start.5 = (bf16[1,320,128]{2,1,0:T(8,128)(2,1)S(1)}, bf16[1,320,128]{2,1,0:T(8,128)(2,1)S(1)}, u32[]{:S(2)}, u32[]{:S(2)}) collective-permute-start(bf16[1,320,128]{2,1,0:T(8,128)(2,1)S(1)} %get-tuple-element.39), channel_id=1, source_target_pairs={{0,12},{1,13},{2,14},{3,15},{4,8},{5,9},{6,10},{7,11},{8,4},{9,5},... | collective-permute-start | bytes 245768 | tf_op jit(solution)/shard_map/ppermute | solution.py:203
  32.0 5.7 %collective-permute-done.3.refs_1_ = bf16[1,320,128]{2,1,0:T(8,128)(2,1)S(1)} collective-permute-done((bf16[1,320,128]{2,1,0:T(8,128)(2,1)S(1)}, bf16[1,320,128]{2,1,0:T(8,128)(2,1)S(1)}, u32[]{:S(2)}, u32[]{:S(2)}) %collective-permute-start.3) | collective-permute-done | bytes 81952 | tf_op jit(solution)/shard_map/ppermute | solution.py:203
  37.7 3.0 %collective-permute-start.9 = (bf16[1,320,128]{2,1,0:T(8,128)(2,1)S(1)}, bf16[1,320,128]{2,1,0:T(8,128)(2,1)S(1)}, u32[]{:S(2)}, u32[]{:S(2)}) collective-permute-start(bf16[1,320,128]{2,1,0:T(8,128)(2,1)S(1)} %total.2.refs_0_), channel_id=1, source_target_pairs={{0,8},{1,9},{2,10},{3,11},{4,12},{5,13},{6,14},{7,15},{8,0},{9,1},... | collective-permute-start | bytes 245768 | tf_op jit(solution)/shard_map/ppermute | solution.py:203
  40.8 2.0 %collective-permute-start.11 = (bf16[1,320,128]{2,1,0:T(8,128)(2,1)S(1)}, bf16[1,320,128]{2,1,0:T(8,128)(2,1)S(1)}, u32[]{:S(2)}, u32[]{:S(2)}) collective-permute-start(bf16[1,320,128]{2,1,0:T(8,128)(2,1)S(1)} %total.2.refs_0_), channel_id=1, source_target_pairs={{0,12},{1,13},{2,14},{3,15},{4,8},{5,9},{6,10},{7,11},{8,4},{9,5},... | collective-permute-start | bytes 245768 | tf_op jit(solution)/shard_map/ppermute | solution.py:203
  42.9 0.6 copy-done.3
  43.5 0.6 collective-permute-start.7
  44.1 3.1 %pad_maximum_fusion = bf16[16,8,64,128]{3,2,1,0:T(8,128)(2,1)} fusion(bf16[16,4,64,128]{3,2,1,0:T(8,128)(2,1)} %bitcast.9, bf16[16,4,64,128]{3,2,1,0:T(8,128)(2,1)} %bitcast.10), kind=kLoop, calls=%fused_computation | loop fusion | flops 1048576 | bytes 4194304 | tf_op jit(solution)/shard_map/concatenate | solution.py:296
  47.2 0.6 copy-done.5
  47.8 0.6 copy-done.7
  48.4 0.6 copy-done.9
  49.1 1.1 collective-permute-done.7.refs_1_
  50.2 5.5 %all-to-all-start.1 = ((bf16[16,8,64,128]{3,2,1,0:T(8,128)(2,1)}), bf16[16,8,64,128]{3,2,1,0:T(8,128)(2,1)S(1)}, u32[]{:S(2)}, u32[]{:S(2)}) async-start(bf16[16,8,64,128]{3,2,1,0:T(8,128)(2,1)} %pad_maximum_fusion), calls=%async_computation.1 | async-start | bytes 4194304 | tf_op jit(solution)/shard_map/all_to_all | solution.py:206
  55.7 0.9 copy-done.6
  56.5 0.9 copy-done.8
  57.4 0.9 copy-done.10
  58.3 1.5 collective-permute-start.12
  59.8 21.6 %collective-permute-done.12.refs_1_ = bf16[4,320,128]{2,1,0:T(8,128)(2,1)S(1)} collective-permute-done((bf16[4,320,128]{2,1,0:T(8,128)(2,1)S(1)}, bf16[4,320,128]{2,1,0:T(8,128)(2,1)S(1)}, u32[]{:S(2)}, u32[]{:S(2)}) %collective-permute-start.12) | collective-permute-done | bytes 327712 | tf_op jit(solution)/shard_map/ppermute | solution.py:203
  81.5 1.3 collective-permute-start.13
  82.9 1.6 %collective-permute-done.13.refs_1_ = bf16[8,320,128]{2,1,0:T(8,128)(2,1)S(1)} collective-permute-done((bf16[8,320,128]{2,1,0:T(8,128)(2,1)S(1)}, bf16[8,320,128]{2,1,0:T(8,128)(2,1)S(1)}, u32[]{:S(2)}, u32[]{:S(2)}) %collective-permute-start.13) | collective-permute-done | bytes 655392 | tf_op jit(solution)/shard_map/ppermute | solution.py:203
  84.5 0.9 low_rank.1.refs_0_
  85.4 0.4 collective-permute-start.14
  85.8 1.8 %collective-permute-start.16 = (bf16[2,32,128]{2,1,0:T(8,128)(2,1)S(1)}, bf16[2,32,128]{2,1,0:T(8,128)(2,1)S(1)}, u32[]{:S(2)}, u32[]{:S(2)}) collective-permute-start(bf16[2,32,128]{2,1,0:T(8,128)(2,1)S(1)} %low_rank.1.refs_0_), channel_id=1, source_target_pairs={{0,3},{1,2},{2,1},{3,0},{4,7},{5,6},{6,5},{7,4},{8,11},{9,10},{10,... | collective-permute-start | bytes 49160 | tf_op jit(solution)/shard_map/ppermute | solution.py:203
  87.6 0.8 collective-permute-done.15.refs_2_
  88.4 0.9 collective-permute-done.16.refs_3_
  89.3 0.6 copy-done.17
  89.9 1.4 choose.1
  91.3 2.0 %collective-permute-start.17 = (bf16[4,32,128]{2,1,0:T(8,128)(2,1)}, bf16[4,32,128]{2,1,0:T(8,128)(2,1)S(1)}, u32[]{:S(2)}, u32[]{:S(2)}) collective-permute-start(bf16[4,32,128]{2,1,0:T(8,128)(2,1)} %get-tuple-element.50), channel_id=1, source_target_pairs={{0,4},{1,5},{2,6},{3,7},{4,0},{5,1},{6,2},{7,3},{8,12},{9,13},{10,... | collective-permute-start | bytes 98312 | tf_op jit(solution)/shard_map/ppermute | solution.py:203
  93.3 1.4 collective-permute-start.18
  94.7 0.7 collective-permute-start.19
  95.4 12.8 %collective-permute-done.8.refs_1_ = bf16[1,256,128]{2,1,0:T(8,128)(2,1)S(1)} collective-permute-done((bf16[1,256,128]{2,1,0:T(8,128)(2,1)S(1)}, bf16[1,256,128]{2,1,0:T(8,128)(2,1)S(1)}, u32[]{:S(2)}, u32[]{:S(2)}) %collective-permute-start.8) | collective-permute-done | bytes 65568 | tf_op jit(solution)/shard_map/ppermute | solution.py:203
  108.2 0.7 collective-permute-done.18.refs_2_
  108.9 0.8 copy-done.14
  109.7 7.2 %attend.1 = bf16[16,4,64,128]{3,2,1,0:T(8,128)(2,1)S(1)} custom-call(s32[1]{0:T(128)} %bitcast.me_ref, bf16[4,64,128]{2,1,0:T(8,128)(2,1)S(1)} %bitcast.6, bf16[16,8,64,128]{3,2,1,0:T(8,128)(2,1)S(1)} %all-to-all-done.1.q_ref.v_ref, bf16[16,4,64,128]{3,2,1,0:T(8,128)(2,1)S(1)} %all-to-all-done.k_ref, ...), custom_call_target="tpu_custom_call" | custom-call | flops 2147483648 | bytes 4194304 | tf_op jit(solution)/shard_map/attend/pallas_call | solution.py:345
  116.9 29.8 %all_to_all.15 = bf16[16,4,64,128]{3,2,1,0:T(8,128)(2,1)S(1)} all-to-all(bf16[16,4,64,128]{3,2,1,0:T(8,128)(2,1)S(1)} %attend.1), channel_id=1, replica_groups=mesh['grp'=2,'seq'=16] {'seq'}, dimensions={0} | all-to-all | bytes 2097152 | tf_op jit(solution)/shard_map/all_to_all | solution.py:206
  146.8 1.0 copy.10
  (48 shorter events, 0.7 us)
Async XLA Ops:
  0.0 7.5 %copy-start.12 = (s32[64]{0:T(128)S(1)}, s32[64]{0:T(128)}, u32[]{:S(2)}) copy-start(s32[64]{0:T(128)} %row_ref.1) | copy-start | bytes 772
  0.0 7.5 %copy-start.13 = (s32[2]{0:T(128)S(1)}, s32[2]{0:T(128)}, u32[]{:S(2)}) copy-start(s32[2]{0:T(128)} %req_ref.1) | copy-start | bytes 28
  0.0 7.5 %copy-start.1 = (bf16[4,64,4096]{2,1,0:T(8,128)(2,1)S(1)}, bf16[4,64,4096]{2,1,0:T(8,128)(2,1)}, u32[]{:S(2)}) copy-start(bf16[4,64,4096]{2,1,0:T(8,128)(2,1)} %up_ref.1) | copy-start | bytes 6291460
  0.0 37.7 %all-to-all-start = ((bf16[16,4,64,128]{3,2,1,0:T(8,128)(2,1)}), bf16[16,4,64,128]{3,2,1,0:T(8,128)(2,1)S(1)}, u32[]{:S(2)}, u32[]{:S(2)}) async-start(bf16[16,4,64,128]{3,2,1,0:T(8,128)(2,1)} %bitcast.8), calls=%async_computation | async-start | bytes 2097152 | tf_op jit(solution)/shard_map/all_to_all | solution.py:206
  7.5 1.7 %copy-start = (bf16[4,64,5120]{2,1,0:T(8,128)(2,1)S(1)}, bf16[4,64,5120]{2,1,0:T(8,128)(2,1)}, u32[]{:S(2)}) copy-start(bf16[4,64,5120]{2,1,0:T(8,128)(2,1)} %down_ref.1) | copy-start | bytes 7864324
  10.8 2.2 %collective-permute-start = (bf16[8,320,128]{2,1,0:T(8,128)(2,1)S(1)}, bf16[8,320,128]{2,1,0:T(8,128)(2,1)S(1)}, u32[]{:S(2)}, u32[]{:S(2)}) collective-permute-start(bf16[8,320,128]{2,1,0:T(8,128)(2,1)S(1)} %get-tuple-element.33), channel_id=1, source_target_pairs={{0,1},{1,0},{2,3},{3,2},{4,5},{5,4},{6,7},{7,6},{8,9},{9,8},{10,11... | collective-permute-start | bytes 1966088 | tf_op jit(solution)/shard_map/ppermute | solution.py:203
  13.1 2.0 %collective-permute-start.1 = (bf16[8,256,128]{2,1,0:T(8,128)(2,1)S(1)}, bf16[8,256,128]{2,1,0:T(8,128)(2,1)S(1)}, u32[]{:S(2)}, u32[]{:S(2)}) collective-permute-start(bf16[8,256,128]{2,1,0:T(8,128)(2,1)S(1)} %get-tuple-element.34), channel_id=1, source_target_pairs={{0,1},{1,0},{2,3},{3,2},{4,5},{5,4},{6,7},{7,6},{8,9},{9,8},{10,11... | collective-permute-start | bytes 1572872 | tf_op jit(solution)/shard_map/ppermute | solution.py:203
  13.3 13.6 %collective-permute-start.2 = (bf16[4,320,128]{2,1,0:T(8,128)(2,1)S(1)}, bf16[4,320,128]{2,1,0:T(8,128)(2,1)S(1)}, u32[]{:S(2)}, u32[]{:S(2)}) collective-permute-start(bf16[4,320,128]{2,1,0:T(8,128)(2,1)S(1)} %halve.2), channel_id=1, source_target_pairs={{0,2},{1,3},{2,0},{3,1},{4,6},{5,7},{6,4},{7,5},{8,10},{9,11},{10,... | collective-permute-start | bytes 983048 | tf_op jit(solution)/shard_map/ppermute | solution.py:203
  15.1 22.6 %collective-permute-start.6 = (bf16[4,256,128]{2,1,0:T(8,128)(2,1)S(1)}, bf16[4,256,128]{2,1,0:T(8,128)(2,1)S(1)}, u32[]{:S(2)}, u32[]{:S(2)}) collective-permute-start(bf16[4,256,128]{2,1,0:T(8,128)(2,1)S(1)} %halve.3), channel_id=1, source_target_pairs={{0,2},{1,3},{2,0},{3,1},{4,6},{5,7},{6,4},{7,5},{8,10},{9,11},{10,... | collective-permute-start | bytes 786440 | tf_op jit(solution)/shard_map/ppermute | solution.py:203
  27.0 10.6 %collective-permute-start.3 = (bf16[1,320,128]{2,1,0:T(8,128)(2,1)S(1)}, bf16[1,320,128]{2,1,0:T(8,128)(2,1)S(1)}, u32[]{:S(2)}, u32[]{:S(2)}) collective-permute-start(bf16[1,320,128]{2,1,0:T(8,128)(2,1)S(1)} %get-tuple-element.37), channel_id=1, source_target_pairs={{0,8},{1,9},{2,10},{3,11},{4,12},{5,13},{6,14},{7,15},{8,0},{9,1},... | collective-permute-start | bytes 245768 | tf_op jit(solution)/shard_map/ppermute | solution.py:203
  30.2 7.5 %collective-permute-start.4 = (bf16[1,320,128]{2,1,0:T(8,128)(2,1)S(1)}, bf16[1,320,128]{2,1,0:T(8,128)(2,1)S(1)}, u32[]{:S(2)}, u32[]{:S(2)}) collective-permute-start(bf16[1,320,128]{2,1,0:T(8,128)(2,1)S(1)} %get-tuple-element.38), channel_id=1, source_target_pairs={{0,4},{1,5},{2,6},{3,7},{4,0},{5,1},{6,2},{7,3},{8,12},{9,13},{10,... | collective-permute-start | bytes 245768 | tf_op jit(solution)/shard_map/ppermute | solution.py:203
  30.3 7.4 %collective-permute-start.5 = (bf16[1,320,128]{2,1,0:T(8,128)(2,1)S(1)}, bf16[1,320,128]{2,1,0:T(8,128)(2,1)S(1)}, u32[]{:S(2)}, u32[]{:S(2)}) collective-permute-start(bf16[1,320,128]{2,1,0:T(8,128)(2,1)S(1)} %get-tuple-element.39), channel_id=1, source_target_pairs={{0,12},{1,13},{2,14},{3,15},{4,8},{5,9},{6,10},{7,11},{8,4},{9,5},... | collective-permute-start | bytes 245768 | tf_op jit(solution)/shard_map/ppermute | solution.py:203
  37.7 9.4 %collective-permute-start.9 = (bf16[1,320,128]{2,1,0:T(8,128)(2,1)S(1)}, bf16[1,320,128]{2,1,0:T(8,128)(2,1)S(1)}, u32[]{:S(2)}, u32[]{:S(2)}) collective-permute-start(bf16[1,320,128]{2,1,0:T(8,128)(2,1)S(1)} %total.2.refs_0_), channel_id=1, source_target_pairs={{0,8},{1,9},{2,10},{3,11},{4,12},{5,13},{6,14},{7,15},{8,0},{9,1},... | collective-permute-start | bytes 245768 | tf_op jit(solution)/shard_map/ppermute | solution.py:203
  40.7 7.1 %collective-permute-start.10 = (bf16[1,320,128]{2,1,0:T(8,128)(2,1)S(1)}, bf16[1,320,128]{2,1,0:T(8,128)(2,1)S(1)}, u32[]{:S(2)}, u32[]{:S(2)}) collective-permute-start(bf16[1,320,128]{2,1,0:T(8,128)(2,1)S(1)} %total.2.refs_0_), channel_id=1, source_target_pairs={{0,4},{1,5},{2,6},{3,7},{4,0},{5,1},{6,2},{7,3},{8,12},{9,13},{10,... | collective-permute-start | bytes 245768 | tf_op jit(solution)/shard_map/ppermute | solution.py:203
  40.8 7.6 %collective-permute-start.11 = (bf16[1,320,128]{2,1,0:T(8,128)(2,1)S(1)}, bf16[1,320,128]{2,1,0:T(8,128)(2,1)S(1)}, u32[]{:S(2)}, u32[]{:S(2)}) collective-permute-start(bf16[1,320,128]{2,1,0:T(8,128)(2,1)S(1)} %total.2.refs_0_), channel_id=1, source_target_pairs={{0,12},{1,13},{2,14},{3,15},{4,8},{5,9},{6,10},{7,11},{8,4},{9,5},... | collective-permute-start | bytes 245768 | tf_op jit(solution)/shard_map/ppermute | solution.py:203
  42.9 0.7 copy-start.3
  43.5 6.6 %collective-permute-start.7 = (bf16[2,256,128]{2,1,0:T(8,128)(2,1)S(1)}, bf16[2,256,128]{2,1,0:T(8,128)(2,1)S(1)}, u32[]{:S(2)}, u32[]{:S(2)}) collective-permute-start(bf16[2,256,128]{2,1,0:T(8,128)(2,1)S(1)} %get-tuple-element.45), channel_id=1, source_target_pairs={{0,4},{1,5},{2,6},{3,7},{4,0},{5,1},{6,2},{7,3},{8,12},{9,13},{10,... | collective-permute-start | bytes 393224 | tf_op jit(solution)/shard_map/ppermute | solution.py:203
  47.2 35.6 %copy-start.4 = (bf16[2,256,128]{2,1,0:T(8,128)(2,1)S(1)}, bf16[2,256,128]{2,1,0:T(8,128)(2,1)}, u32[]{:S(2)}) copy-start(bf16[2,256,128]{2,1,0:T(8,128)(2,1)} %copy-done.3) | copy-start | bytes 393220
  47.2 0.6 copy-start.5
  47.8 0.6 copy-start.7
  48.4 0.6 copy-start.9
  50.2 58.7 %all-to-all-start.1 = ((bf16[16,8,64,128]{3,2,1,0:T(8,128)(2,1)}), bf16[16,8,64,128]{3,2,1,0:T(8,128)(2,1)S(1)}, u32[]{:S(2)}, u32[]{:S(2)}) async-start(bf16[16,8,64,128]{3,2,1,0:T(8,128)(2,1)} %pad_maximum_fusion), calls=%async_computation.1 | async-start | bytes 4194304 | tf_op jit(solution)/shard_map/all_to_all | solution.py:206
  55.7 0.9 copy-start.6
  56.5 0.9 copy-start.8
  57.4 0.9 copy-start.10
  58.3 26.2 %copy-start.2 = (bf16[2,64,5120]{2,1,0:T(8,128)(2,1)S(1)}, bf16[2,64,5120]{2,1,0:T(8,128)(2,1)}, u32[]{:S(2)}) copy-start(bf16[2,64,5120]{2,1,0:T(8,128)(2,1)} %x_ref.1) | copy-start | bytes 3932164
  58.3 23.1 %collective-permute-start.12 = (bf16[4,320,128]{2,1,0:T(8,128)(2,1)S(1)}, bf16[4,320,128]{2,1,0:T(8,128)(2,1)S(1)}, u32[]{:S(2)}, u32[]{:S(2)}) collective-permute-start(bf16[4,320,128]{2,1,0:T(8,128)(2,1)S(1)} %join.2.refs_0_), channel_id=1, source_target_pairs={{0,2},{1,3},{2,0},{3,1},{4,6},{5,7},{6,4},{7,5},{8,10},{9,11},{10,... | collective-permute-start | bytes 983048 | tf_op jit(solution)/shard_map/ppermute | solution.py:203
  81.5 3.0 %collective-permute-start.13 = (bf16[8,320,128]{2,1,0:T(8,128)(2,1)S(1)}, bf16[8,320,128]{2,1,0:T(8,128)(2,1)S(1)}, u32[]{:S(2)}, u32[]{:S(2)}) collective-permute-start(bf16[8,320,128]{2,1,0:T(8,128)(2,1)S(1)} %join.3.refs_0_), channel_id=1, source_target_pairs={{0,1},{1,0},{2,3},{3,2},{4,5},{5,4},{6,7},{7,6},{8,9},{9,8},{10,11... | collective-permute-start | bytes 1966088 | tf_op jit(solution)/shard_map/ppermute | solution.py:203
  82.8 25.4 %collective-permute-start.8 = (bf16[1,256,128]{2,1,0:T(8,128)(2,1)S(1)}, bf16[1,256,128]{2,1,0:T(8,128)(2,1)S(1)}, u32[]{:S(2)}, u32[]{:S(2)}) collective-permute-start(bf16[1,256,128]{2,1,0:T(8,128)(2,1)S(1)} %get-tuple-element.47), channel_id=1, source_target_pairs={{0,8},{1,9},{2,10},{3,11},{4,12},{5,13},{6,14},{7,15},{8,0},{9,1},... | collective-permute-start | bytes 196616 | tf_op jit(solution)/shard_map/ppermute | solution.py:203
  85.4 3.9 %copy-start.11 = (bf16[2,32,128]{2,1,0:T(8,128)(2,1)}, bf16[2,32,128]{2,1,0:T(8,128)(2,1)S(1)}, u32[]{:S(2)}) copy-start(bf16[2,32,128]{2,1,0:T(8,128)(2,1)S(1)} %low_rank.1.refs_0_) | copy-start | bytes 49156
  85.4 2.2 %collective-permute-start.14 = (bf16[2,32,128]{2,1,0:T(8,128)(2,1)S(1)}, bf16[2,32,128]{2,1,0:T(8,128)(2,1)S(1)}, u32[]{:S(2)}, u32[]{:S(2)}) collective-permute-start(bf16[2,32,128]{2,1,0:T(8,128)(2,1)S(1)} %low_rank.1.refs_0_), channel_id=1, source_target_pairs={{0,1},{1,0},{2,3},{3,2},{4,5},{5,4},{6,7},{7,6},{8,9},{9,8},{10,11... | collective-permute-start | bytes 49160 | tf_op jit(solution)/shard_map/ppermute | solution.py:203
  85.8 2.6 %collective-permute-start.15 = (bf16[2,32,128]{2,1,0:T(8,128)(2,1)S(1)}, bf16[2,32,128]{2,1,0:T(8,128)(2,1)S(1)}, u32[]{:S(2)}, u32[]{:S(2)}) collective-permute-start(bf16[2,32,128]{2,1,0:T(8,128)(2,1)S(1)} %low_rank.1.refs_0_), channel_id=1, source_target_pairs={{0,2},{1,3},{2,0},{3,1},{4,6},{5,7},{6,4},{7,5},{8,10},{9,11},{10,... | collective-permute-start | bytes 49160 | tf_op jit(solution)/shard_map/ppermute | solution.py:203
  85.8 3.5 %collective-permute-start.16 = (bf16[2,32,128]{2,1,0:T(8,128)(2,1)S(1)}, bf16[2,32,128]{2,1,0:T(8,128)(2,1)S(1)}, u32[]{:S(2)}, u32[]{:S(2)}) collective-permute-start(bf16[2,32,128]{2,1,0:T(8,128)(2,1)S(1)} %low_rank.1.refs_0_), channel_id=1, source_target_pairs={{0,3},{1,2},{2,1},{3,0},{4,7},{5,6},{6,5},{7,4},{8,11},{9,10},{10,... | collective-permute-start | bytes 49160 | tf_op jit(solution)/shard_map/ppermute | solution.py:203
  87.6 1.7 %copy-start.15 = (bf16[2,32,128]{2,1,0:T(8,128)(2,1)}, bf16[2,32,128]{2,1,0:T(8,128)(2,1)S(1)}, u32[]{:S(2)}) copy-start(bf16[2,32,128]{2,1,0:T(8,128)(2,1)S(1)} %collective-permute-done.14.refs_1_) | copy-start | bytes 49156
  88.4 0.9 copy-start.16
  89.3 0.6 copy-start.17
  91.3 16.9 %collective-permute-start.17 = (bf16[4,32,128]{2,1,0:T(8,128)(2,1)}, bf16[4,32,128]{2,1,0:T(8,128)(2,1)S(1)}, u32[]{:S(2)}, u32[]{:S(2)}) collective-permute-start(bf16[4,32,128]{2,1,0:T(8,128)(2,1)} %get-tuple-element.50), channel_id=1, source_target_pairs={{0,4},{1,5},{2,6},{3,7},{4,0},{5,1},{6,2},{7,3},{8,12},{9,13},{10,... | collective-permute-start | bytes 98312 | tf_op jit(solution)/shard_map/ppermute | solution.py:203
  93.3 15.6 %collective-permute-start.18 = (bf16[4,32,128]{2,1,0:T(8,128)(2,1)}, bf16[4,32,128]{2,1,0:T(8,128)(2,1)S(1)}, u32[]{:S(2)}, u32[]{:S(2)}) collective-permute-start(bf16[4,32,128]{2,1,0:T(8,128)(2,1)} %get-tuple-element.51), channel_id=1, source_target_pairs={{0,8},{1,9},{2,10},{3,11},{4,12},{5,13},{6,14},{7,15},{8,0},{9,1},... | collective-permute-start | bytes 98312 | tf_op jit(solution)/shard_map/ppermute | solution.py:203
  94.7 14.2 %collective-permute-start.19 = (bf16[4,32,128]{2,1,0:T(8,128)(2,1)}, bf16[4,32,128]{2,1,0:T(8,128)(2,1)S(1)}, u32[]{:S(2)}, u32[]{:S(2)}) collective-permute-start(bf16[4,32,128]{2,1,0:T(8,128)(2,1)} %get-tuple-element.52), channel_id=1, source_target_pairs={{0,12},{1,13},{2,14},{3,15},{4,8},{5,9},{6,10},{7,11},{8,4},{9,5},... | collective-permute-start | bytes 98312 | tf_op jit(solution)/shard_map/ppermute | solution.py:203
  108.9 0.8 copy-start.14

commit v22 on v21

--- a/solution.py
+++ b/solution.py
@@ -294,7 +294,8 @@
     )
     came = swap(far_pair, quarter)
     asked = jnp.concatenate([by_pairs(values), by_pairs(queries)], axis=1)
-    asked = exchange(after(asked, came, *gathered))
+    joined = join(gathered)
+    asked = exchange(after(asked, came, joined))
     one_shape = (1,) + up_part.shape[1:]
     kept, sent = on_vmem(
         functools.partial(sum_kernel, [[(n, h) for n in range(2)] for h in (0, 1)]),
@@ -307,7 +308,6 @@
     up_here = on_vmem(
         functools.partial(sum_kernel, [[(0, 0), (1, 0)]]), [one_shape], "total", kept, last
     )[0].reshape(pairs, ranks, LANES)
-    joined = join(gathered)
     for i in reversed(range(bits - 2)):
         gathered = [joined, swap(joined, 1 << i)]
         if i > 0:

time: 148 us -> 149 us (level)
  starting transfers between devices: 36.1 us -> 38.3 us
  local copies, waits for them, and re-layouts: 9.26 us -> 7.2 us
    ppermute x20, starting transfers between devices: 23.2 us -> 25.3 us  [swap(): return lax.ppermute(tensor, 'seq', [(i, i ^ k) for i in range(devs)])]
    unnamed x37 -> x31, local copies, waits for them, and re-layouts: 9.26 us -> 7.2 us
where the time goes in v22:
time: 149 us; the launch traced here: 148 us
  waiting for transfers between devices  58.6 us (39%)
  starting transfers between devices  38.3 us (26%)
  blocking collectives  29.9 us (20%)
  Pallas kernels  11.5 us (8%)
  local copies, waits for them, and re-layouts  7.2 us (5%)
  other arithmetic  2.77 us (2%)
    ppermute x20, waiting for transfers between devices, swap(): return lax.ppermute(tensor, 'seq', [(i, i ^ k) for i in range(devs)])  58.6 us
    all_to_all x1, blocking collectives, exchange(): lax.all_to_all(tensor, 'seq', split_axis=0, concat_axis=0, tiled=True)  29.9 us
    ppermute x20, starting transfers between devices, swap(): return lax.ppermute(tensor, 'seq', [(i, i ^ k) for i in range(devs)])  25.3 us
    all_to_all x2, starting transfers between devices, exchange(): lax.all_to_all(tensor, 'seq', split_axis=0, concat_axis=0, tiled=True)  13 us
    pallas_call x1, Pallas kernels, body(): pl.pallas_call(functools.partial(attend_kernel, math.gcd(devs, max(1, 256...  7.23 us
    unnamed x31, local copies, waits for them, and re-layouts  7.2 us
  transfers between devices with their start and end apart: 22, of which 11 were waited for; matrix products, arithmetic and copies ran while one was open for 2% of the time, Pallas kernels for 3%

profile of v22, /device:TPU:1, one launch (start us, length us, event | category | flops | bytes accessed | tf_op | source)
XLA Modules:
  0.0 148.4 jit_solution(13009165843515907711)
XLA Ops:
  0.0 7.5 %all-to-all-start = ((bf16[16,4,64,128]{3,2,1,0:T(8,128)(2,1)}), bf16[16,4,64,128]{3,2,1,0:T(8,128)(2,1)S(1)}, u32[]{:S(2)}, u32[]{:S(2)}) async-start(bf16[16,4,64,128]{3,2,1,0:T(8,128)(2,1)} %bitcast.8), calls=%async_computation | async-start | bytes 2097152 | tf_op jit(solution)/shard_map/all_to_all | solution.py:206
  7.5 1.7 %copy-done = bf16[4,64,5120]{2,1,0:T(8,128)(2,1)S(1)} copy-done((bf16[4,64,5120]{2,1,0:T(8,128)(2,1)S(1)}, bf16[4,64,5120]{2,1,0:T(8,128)(2,1)}, u32[]{:S(2)}) %copy-start) | copy-done | bytes 2621464
  9.3 1.5 %pick_factors.1 = (bf16[8,320,128]{2,1,0:T(8,128)(2,1)S(1)}, bf16[4,320,128]{2,1,0:T(8,128)(2,1)S(1)}, bf16[4,320,128]{2,1,0:T(8,128)(2,1)S(1)}, bf16[8,256,128]...) custom-call(s32[1]{0:T(128)} %bitcast.me_ref, s32[64]{0:T(128)S(1)} %copy-done.8, ...), custom_call_target="tpu_custom_call" | custom-call | bytes 4718592 | tf_op jit(solution)/shard_map/pick_factors/pallas_call | solution.py:250
  10.8 0.2 collective-permute-start
  11.0 2.0 %collective-permute-done.refs_1_ = bf16[8,320,128]{2,1,0:T(8,128)(2,1)S(1)} collective-permute-done((bf16[8,320,128]{2,1,0:T(8,128)(2,1)S(1)}, bf16[8,320,128]{2,1,0:T(8,128)(2,1)S(1)}, u32[]{:S(2)}, u32[]{:S(2)}) %collective-permute-start) | collective-permute-done | bytes 655392 | tf_op jit(solution)/shard_map/ppermute | solution.py:203
  13.0 0.1 halve.2
  13.0 0.2 collective-permute-start.1
  13.2 1.6 %collective-permute-start.2 = (bf16[4,320,128]{2,1,0:T(8,128)(2,1)S(1)}, bf16[4,320,128]{2,1,0:T(8,128)(2,1)S(1)}, u32[]{:S(2)}, u32[]{:S(2)}) collective-permute-start(bf16[4,320,128]{2,1,0:T(8,128)(2,1)S(1)} %halve.2), channel_id=1, source_target_pairs={{0,2},{1,3},{2,0},{3,1},{4,6},{5,7},{6,4},{7,5},{8,10},{9,11},{10,... | collective-permute-start | bytes 983048 | tf_op jit(solution)/shard_map/ppermute | solution.py:203
  14.9 0.2 collective-permute-done.1.refs_1_
  15.0 0.1 halve.3
  15.1 1.5 collective-permute-start.6
  16.5 10.4 %collective-permute-done.2.refs_2_ = bf16[4,320,128]{2,1,0:T(8,128)(2,1)S(1)} collective-permute-done((bf16[4,320,128]{2,1,0:T(8,128)(2,1)S(1)}, bf16[4,320,128]{2,1,0:T(8,128)(2,1)S(1)}, u32[]{:S(2)}, u32[]{:S(2)}) %collective-permute-start.2) | collective-permute-done | bytes 327712 | tf_op jit(solution)/shard_map/ppermute | solution.py:203
  26.9 0.1 split.3
  27.0 3.2 %collective-permute-start.3 = (bf16[1,320,128]{2,1,0:T(8,128)(2,1)S(1)}, bf16[1,320,128]{2,1,0:T(8,128)(2,1)S(1)}, u32[]{:S(2)}, u32[]{:S(2)}) collective-permute-start(bf16[1,320,128]{2,1,0:T(8,128)(2,1)S(1)} %get-tuple-element.37), channel_id=1, source_target_pairs={{0,8},{1,9},{2,10},{3,11},{4,12},{5,13},{6,14},{7,15},{8,0},{9,1},... | collective-permute-start | bytes 245768 | tf_op jit(solution)/shard_map/ppermute | solution.py:203
  30.2 1.6 %collective-permute-start.5 = (bf16[1,320,128]{2,1,0:T(8,128)(2,1)S(1)}, bf16[1,320,128]{2,1,0:T(8,128)(2,1)S(1)}, u32[]{:S(2)}, u32[]{:S(2)}) collective-permute-start(bf16[1,320,128]{2,1,0:T(8,128)(2,1)S(1)} %get-tuple-element.39), channel_id=1, source_target_pairs={{0,12},{1,13},{2,14},{3,15},{4,8},{5,9},{6,10},{7,11},{8,4},{9,5},... | collective-permute-start | bytes 245768 | tf_op jit(solution)/shard_map/ppermute | solution.py:203
  31.8 6.7 %collective-permute-done.3.refs_1_ = bf16[1,320,128]{2,1,0:T(8,128)(2,1)S(1)} collective-permute-done((bf16[1,320,128]{2,1,0:T(8,128)(2,1)S(1)}, bf16[1,320,128]{2,1,0:T(8,128)(2,1)S(1)}, u32[]{:S(2)}, u32[]{:S(2)}) %collective-permute-start.3) | collective-permute-done | bytes 81952 | tf_op jit(solution)/shard_map/ppermute | solution.py:203
  38.6 2.1 %collective-permute-start.9 = (bf16[1,320,128]{2,1,0:T(8,128)(2,1)S(1)}, bf16[1,320,128]{2,1,0:T(8,128)(2,1)S(1)}, u32[]{:S(2)}, u32[]{:S(2)}) collective-permute-start(bf16[1,320,128]{2,1,0:T(8,128)(2,1)S(1)} %total.2.refs_0_), channel_id=1, source_target_pairs={{0,8},{1,9},{2,10},{3,11},{4,12},{5,13},{6,14},{7,15},{8,0},{9,1},... | collective-permute-start | bytes 245768 | tf_op jit(solution)/shard_map/ppermute | solution.py:203
  40.7 0.1 collective-permute-start.10
  40.8 2.0 %collective-permute-start.11 = (bf16[1,320,128]{2,1,0:T(8,128)(2,1)S(1)}, bf16[1,320,128]{2,1,0:T(8,128)(2,1)S(1)}, u32[]{:S(2)}, u32[]{:S(2)}) collective-permute-start(bf16[1,320,128]{2,1,0:T(8,128)(2,1)S(1)} %total.2.refs_0_), channel_id=1, source_target_pairs={{0,12},{1,13},{2,14},{3,15},{4,8},{5,9},{6,10},{7,11},{8,4},{9,5},... | collective-permute-start | bytes 245768 | tf_op jit(solution)/shard_map/ppermute | solution.py:203
  42.8 0.1 split.4
  42.9 0.6 copy-done.3
  43.5 0.6 collective-permute-start.7
  44.1 2.8 %pad_maximum_fusion = bf16[16,8,64,128]{3,2,1,0:T(8,128)(2,1)} fusion(bf16[16,4,64,128]{3,2,1,0:T(8,128)(2,1)S(1)} %bitcast.9, bf16[16,4,64,128]{3,2,1,0:T(8,128)(2,1)} %bitcast.10), kind=kLoop, calls=%fused_computation | loop fusion | flops 1048576 | bytes 4194304 | tf_op jit(solution)/shard_map/concatenate | solution.py:296
  46.9 0.8 collective-permute-done.11.refs_3_
  47.7 2.5 %collective-permute-done.7.refs_1_ = bf16[2,256,128]{2,1,0:T(8,128)(2,1)S(1)} collective-permute-done((bf16[2,256,128]{2,1,0:T(8,128)(2,1)S(1)}, bf16[2,256,128]{2,1,0:T(8,128)(2,1)S(1)}, u32[]{:S(2)}, u32[]{:S(2)}) %collective-permute-start.7) | collective-permute-done | bytes 131104 | tf_op jit(solution)/shard_map/ppermute | solution.py:203
  50.2 0.7 copy-done.5
  50.8 5.5 %all-to-all-start.1 = ((bf16[16,8,64,128]{3,2,1,0:T(8,128)(2,1)}), bf16[16,8,64,128]{3,2,1,0:T(8,128)(2,1)S(1)}, u32[]{:S(2)}, u32[]{:S(2)}) async-start(bf16[16,8,64,128]{3,2,1,0:T(8,128)(2,1)} %pad_maximum_fusion), calls=%async_computation.1 | async-start | bytes 4194304 | tf_op jit(solution)/shard_map/all_to_all | solution.py:206
  56.3 1.5 collective-permute-start.12
  57.8 24.3 %collective-permute-done.12.refs_1_ = bf16[4,320,128]{2,1,0:T(8,128)(2,1)S(1)} collective-permute-done((bf16[4,320,128]{2,1,0:T(8,128)(2,1)S(1)}, bf16[4,320,128]{2,1,0:T(8,128)(2,1)S(1)}, u32[]{:S(2)}, u32[]{:S(2)}) %collective-permute-start.12) | collective-permute-done | bytes 327712 | tf_op jit(solution)/shard_map/ppermute | solution.py:203
  82.1 1.3 collective-permute-start.13
  83.4 0.9 copy-done.4
  84.3 0.9 copy-done.6
  85.3 0.1 collective-permute-start.8
  85.4 0.9 low_rank.1.refs_0_
  86.2 0.2 collective-permute-start.14
  86.4 2.0 %collective-permute-start.16 = (bf16[2,32,128]{2,1,0:T(8,128)(2,1)S(1)}, bf16[2,32,128]{2,1,0:T(8,128)(2,1)S(1)}, u32[]{:S(2)}, u32[]{:S(2)}) collective-permute-start(bf16[2,32,128]{2,1,0:T(8,128)(2,1)S(1)} %low_rank.1.refs_0_), channel_id=1, source_target_pairs={{0,3},{1,2},{2,1},{3,0},{4,7},{5,6},{6,5},{7,4},{8,11},{9,10},{10,... | collective-permute-start | bytes 49160 | tf_op jit(solution)/shard_map/ppermute | solution.py:203
  88.4 0.6 collective-permute-done.15.refs_2_
  89.0 1.1 collective-permute-done.16.refs_3_
  90.1 0.6 copy-done.14
  90.7 1.4 choose.1
  92.1 5.2 %collective-permute-start.17 = (bf16[4,32,128]{2,1,0:T(8,128)(2,1)}, bf16[4,32,128]{2,1,0:T(8,128)(2,1)S(1)}, u32[]{:S(2)}, u32[]{:S(2)}) collective-permute-start(bf16[4,32,128]{2,1,0:T(8,128)(2,1)} %get-tuple-element.50), channel_id=1, source_target_pairs={{0,4},{1,5},{2,6},{3,7},{4,0},{5,1},{6,2},{7,3},{8,12},{9,13},{10,... | collective-permute-start | bytes 98312 | tf_op jit(solution)/shard_map/ppermute | solution.py:203
  97.3 2.1 %collective-permute-start.19 = (bf16[4,32,128]{2,1,0:T(8,128)(2,1)}, bf16[4,32,128]{2,1,0:T(8,128)(2,1)S(1)}, u32[]{:S(2)}, u32[]{:S(2)}) collective-permute-start(bf16[4,32,128]{2,1,0:T(8,128)(2,1)} %get-tuple-element.52), channel_id=1, source_target_pairs={{0,12},{1,13},{2,14},{3,15},{4,8},{5,9},{6,10},{7,11},{8,4},{9,5},... | collective-permute-start | bytes 98312 | tf_op jit(solution)/shard_map/ppermute | solution.py:203
  99.5 9.4 %collective-permute-done.8.refs_1_ = bf16[1,256,128]{2,1,0:T(8,128)(2,1)S(1)} collective-permute-done((bf16[1,256,128]{2,1,0:T(8,128)(2,1)S(1)}, bf16[1,256,128]{2,1,0:T(8,128)(2,1)S(1)}, u32[]{:S(2)}, u32[]{:S(2)}) %collective-permute-start.8) | collective-permute-done | bytes 65568 | tf_op jit(solution)/shard_map/ppermute | solution.py:203
  108.9 0.7 collective-permute-done.18.refs_2_
  109.5 0.8 copy-done.10
  110.3 7.2 %attend.1 = bf16[16,4,64,128]{3,2,1,0:T(8,128)(2,1)S(1)} custom-call(s32[1]{0:T(128)} %bitcast.me_ref, bf16[4,64,128]{2,1,0:T(8,128)(2,1)S(1)} %bitcast.6, bf16[16,8,64,128]{3,2,1,0:T(8,128)(2,1)S(1)} %all-to-all-done.1.q_ref.v_ref, bf16[16,4,64,128]{3,2,1,0:T(8,128)(2,1)S(1)} %all-to-all-done.k_ref, ...), custom_call_target="tpu_custom_call" | custom-call | flops 2147483648 | bytes 4194304 | tf_op jit(solution)/shard_map/attend/pallas_call | solution.py:345
  117.5 29.9 %all_to_all.15 = bf16[16,4,64,128]{3,2,1,0:T(8,128)(2,1)S(1)} all-to-all(bf16[16,4,64,128]{3,2,1,0:T(8,128)(2,1)S(1)} %attend.1), channel_id=1, replica_groups=mesh['grp'=2,'seq'=16] {'seq'}, dimensions={0} | all-to-all | bytes 2097152 | tf_op jit(solution)/shard_map/all_to_all | solution.py:206
  147.4 1.0 copy.10
  (42 shorter events, 0.3 us)
Async XLA Ops:
  0.0 7.5 %copy-start.8 = (s32[64]{0:T(128)S(1)}, s32[64]{0:T(128)}, u32[]{:S(2)}) copy-start(s32[64]{0:T(128)} %row_ref.1) | copy-start | bytes 772
  0.0 7.5 %copy-start.9 = (s32[2]{0:T(128)S(1)}, s32[2]{0:T(128)}, u32[]{:S(2)}) copy-start(s32[2]{0:T(128)} %req_ref.1) | copy-start | bytes 28
  0.0 7.5 %copy-start.1 = (bf16[4,64,4096]{2,1,0:T(8,128)(2,1)S(1)}, bf16[4,64,4096]{2,1,0:T(8,128)(2,1)}, u32[]{:S(2)}) copy-start(bf16[4,64,4096]{2,1,0:T(8,128)(2,1)} %up_ref.1) | copy-start | bytes 6291460
  0.0 38.6 %all-to-all-start = ((bf16[16,4,64,128]{3,2,1,0:T(8,128)(2,1)}), bf16[16,4,64,128]{3,2,1,0:T(8,128)(2,1)S(1)}, u32[]{:S(2)}, u32[]{:S(2)}) async-start(bf16[16,4,64,128]{3,2,1,0:T(8,128)(2,1)} %bitcast.8), calls=%async_computation | async-start | bytes 2097152 | tf_op jit(solution)/shard_map/all_to_all | solution.py:206
  7.5 1.7 %copy-start = (bf16[4,64,5120]{2,1,0:T(8,128)(2,1)S(1)}, bf16[4,64,5120]{2,1,0:T(8,128)(2,1)}, u32[]{:S(2)}) copy-start(bf16[4,64,5120]{2,1,0:T(8,128)(2,1)} %down_ref.1) | copy-start | bytes 7864324
  10.8 2.2 %collective-permute-start = (bf16[8,320,128]{2,1,0:T(8,128)(2,1)S(1)}, bf16[8,320,128]{2,1,0:T(8,128)(2,1)S(1)}, u32[]{:S(2)}, u32[]{:S(2)}) collective-permute-start(bf16[8,320,128]{2,1,0:T(8,128)(2,1)S(1)} %get-tuple-element.33), channel_id=1, source_target_pairs={{0,1},{1,0},{2,3},{3,2},{4,5},{5,4},{6,7},{7,6},{8,9},{9,8},{10,11... | collective-permute-start | bytes 1966088 | tf_op jit(solution)/shard_map/ppermute | solution.py:203
  13.0 31.1 %copy-start.11 = (bf16[2,32,64,128]{3,2,1,0:T(8,128)(2,1)S(1)}, bf16[2,32,64,128]{3,2,1,0:T(8,128)(2,1)}, u32[]{:S(2)}) copy-start(bf16[2,32,64,128]{3,2,1,0:T(8,128)(2,1)} %param.9) | copy-start | bytes 3145732
  13.0 2.0 %collective-permute-start.1 = (bf16[8,256,128]{2,1,0:T(8,128)(2,1)S(1)}, bf16[8,256,128]{2,1,0:T(8,128)(2,1)S(1)}, u32[]{:S(2)}, u32[]{:S(2)}) collective-permute-start(bf16[8,256,128]{2,1,0:T(8,128)(2,1)S(1)} %get-tuple-element.34), channel_id=1, source_target_pairs={{0,1},{1,0},{2,3},{3,2},{4,5},{5,4},{6,7},{7,6},{8,9},{9,8},{10,11... | collective-permute-start | bytes 1572872 | tf_op jit(solution)/shard_map/ppermute | solution.py:203
  13.2 13.6 %collective-permute-start.2 = (bf16[4,320,128]{2,1,0:T(8,128)(2,1)S(1)}, bf16[4,320,128]{2,1,0:T(8,128)(2,1)S(1)}, u32[]{:S(2)}, u32[]{:S(2)}) collective-permute-start(bf16[4,320,128]{2,1,0:T(8,128)(2,1)S(1)} %halve.2), channel_id=1, source_target_pairs={{0,2},{1,3},{2,0},{3,1},{4,6},{5,7},{6,4},{7,5},{8,10},{9,11},{10,... | collective-permute-start | bytes 983048 | tf_op jit(solution)/shard_map/ppermute | solution.py:203
  15.1 23.5 %collective-permute-start.6 = (bf16[4,256,128]{2,1,0:T(8,128)(2,1)S(1)}, bf16[4,256,128]{2,1,0:T(8,128)(2,1)S(1)}, u32[]{:S(2)}, u32[]{:S(2)}) collective-permute-start(bf16[4,256,128]{2,1,0:T(8,128)(2,1)S(1)} %halve.3), channel_id=1, source_target_pairs={{0,2},{1,3},{2,0},{3,1},{4,6},{5,7},{6,4},{7,5},{8,10},{9,11},{10,... | collective-permute-start | bytes 786440 | tf_op jit(solution)/shard_map/ppermute | solution.py:203
  27.0 11.6 %collective-permute-start.3 = (bf16[1,320,128]{2,1,0:T(8,128)(2,1)S(1)}, bf16[1,320,128]{2,1,0:T(8,128)(2,1)S(1)}, u32[]{:S(2)}, u32[]{:S(2)}) collective-permute-start(bf16[1,320,128]{2,1,0:T(8,128)(2,1)S(1)} %get-tuple-element.37), channel_id=1, source_target_pairs={{0,8},{1,9},{2,10},{3,11},{4,12},{5,13},{6,14},{7,15},{8,0},{9,1},... | collective-permute-start | bytes 245768 | tf_op jit(solution)/shard_map/ppermute | solution.py:203
  30.2 8.3 %collective-permute-start.4 = (bf16[1,320,128]{2,1,0:T(8,128)(2,1)S(1)}, bf16[1,320,128]{2,1,0:T(8,128)(2,1)S(1)}, u32[]{:S(2)}, u32[]{:S(2)}) collective-permute-start(bf16[1,320,128]{2,1,0:T(8,128)(2,1)S(1)} %get-tuple-element.38), channel_id=1, source_target_pairs={{0,4},{1,5},{2,6},{3,7},{4,0},{5,1},{6,2},{7,3},{8,12},{9,13},{10,... | collective-permute-start | bytes 245768 | tf_op jit(solution)/shard_map/ppermute | solution.py:203
  30.2 8.3 %collective-permute-start.5 = (bf16[1,320,128]{2,1,0:T(8,128)(2,1)S(1)}, bf16[1,320,128]{2,1,0:T(8,128)(2,1)S(1)}, u32[]{:S(2)}, u32[]{:S(2)}) collective-permute-start(bf16[1,320,128]{2,1,0:T(8,128)(2,1)S(1)} %get-tuple-element.39), channel_id=1, source_target_pairs={{0,12},{1,13},{2,14},{3,15},{4,8},{5,9},{6,10},{7,11},{8,4},{9,5},... | collective-permute-start | bytes 245768 | tf_op jit(solution)/shard_map/ppermute | solution.py:203
  38.6 8.3 %collective-permute-start.9 = (bf16[1,320,128]{2,1,0:T(8,128)(2,1)S(1)}, bf16[1,320,128]{2,1,0:T(8,128)(2,1)S(1)}, u32[]{:S(2)}, u32[]{:S(2)}) collective-permute-start(bf16[1,320,128]{2,1,0:T(8,128)(2,1)S(1)} %total.2.refs_0_), channel_id=1, source_target_pairs={{0,8},{1,9},{2,10},{3,11},{4,12},{5,13},{6,14},{7,15},{8,0},{9,1},... | collective-permute-start | bytes 245768 | tf_op jit(solution)/shard_map/ppermute | solution.py:203
  40.7 6.2 %collective-permute-start.10 = (bf16[1,320,128]{2,1,0:T(8,128)(2,1)S(1)}, bf16[1,320,128]{2,1,0:T(8,128)(2,1)S(1)}, u32[]{:S(2)}, u32[]{:S(2)}) collective-permute-start(bf16[1,320,128]{2,1,0:T(8,128)(2,1)S(1)} %total.2.refs_0_), channel_id=1, source_target_pairs={{0,4},{1,5},{2,6},{3,7},{4,0},{5,1},{6,2},{7,3},{8,12},{9,13},{10,... | collective-permute-start | bytes 245768 | tf_op jit(solution)/shard_map/ppermute | solution.py:203
  40.8 6.8 %collective-permute-start.11 = (bf16[1,320,128]{2,1,0:T(8,128)(2,1)S(1)}, bf16[1,320,128]{2,1,0:T(8,128)(2,1)S(1)}, u32[]{:S(2)}, u32[]{:S(2)}) collective-permute-start(bf16[1,320,128]{2,1,0:T(8,128)(2,1)S(1)} %total.2.refs_0_), channel_id=1, source_target_pairs={{0,12},{1,13},{2,14},{3,15},{4,8},{5,9},{6,10},{7,11},{8,4},{9,5},... | collective-permute-start | bytes 245768 | tf_op jit(solution)/shard_map/ppermute | solution.py:203
  42.9 0.7 copy-start.3
  43.5 6.6 %collective-permute-start.7 = (bf16[2,256,128]{2,1,0:T(8,128)(2,1)S(1)}, bf16[2,256,128]{2,1,0:T(8,128)(2,1)S(1)}, u32[]{:S(2)}, u32[]{:S(2)}) collective-permute-start(bf16[2,256,128]{2,1,0:T(8,128)(2,1)S(1)} %get-tuple-element.45), channel_id=1, source_target_pairs={{0,4},{1,5},{2,6},{3,7},{4,0},{5,1},{6,2},{7,3},{8,12},{9,13},{10,... | collective-permute-start | bytes 393224 | tf_op jit(solution)/shard_map/ppermute | solution.py:203
  50.2 0.7 copy-start.5
  50.8 58.7 %all-to-all-start.1 = ((bf16[16,8,64,128]{3,2,1,0:T(8,128)(2,1)}), bf16[16,8,64,128]{3,2,1,0:T(8,128)(2,1)S(1)}, u32[]{:S(2)}, u32[]{:S(2)}) async-start(bf16[16,8,64,128]{3,2,1,0:T(8,128)(2,1)} %pad_maximum_fusion), calls=%async_computation.1 | async-start | bytes 4194304 | tf_op jit(solution)/shard_map/all_to_all | solution.py:206
  56.3 29.0 %copy-start.2 = (bf16[2,64,5120]{2,1,0:T(8,128)(2,1)S(1)}, bf16[2,64,5120]{2,1,0:T(8,128)(2,1)}, u32[]{:S(2)}) copy-start(bf16[2,64,5120]{2,1,0:T(8,128)(2,1)} %x_ref.1) | copy-start | bytes 3932164
  56.3 25.8 %collective-permute-start.12 = (bf16[4,320,128]{2,1,0:T(8,128)(2,1)S(1)}, bf16[4,320,128]{2,1,0:T(8,128)(2,1)S(1)}, u32[]{:S(2)}, u32[]{:S(2)}) collective-permute-start(bf16[4,320,128]{2,1,0:T(8,128)(2,1)S(1)} %join.2.refs_0_), channel_id=1, source_target_pairs={{0,2},{1,3},{2,0},{3,1},{4,6},{5,7},{6,4},{7,5},{8,10},{9,11},{10,... | collective-permute-start | bytes 983048 | tf_op jit(solution)/shard_map/ppermute | solution.py:203
  82.1 3.2 %collective-permute-start.13 = (bf16[8,320,128]{2,1,0:T(8,128)(2,1)S(1)}, bf16[8,320,128]{2,1,0:T(8,128)(2,1)S(1)}, u32[]{:S(2)}, u32[]{:S(2)}) collective-permute-start(bf16[8,320,128]{2,1,0:T(8,128)(2,1)S(1)} %join.3.refs_0_), channel_id=1, source_target_pairs={{0,1},{1,0},{2,3},{3,2},{4,5},{5,4},{6,7},{7,6},{8,9},{9,8},{10,11... | collective-permute-start | bytes 1966088 | tf_op jit(solution)/shard_map/ppermute | solution.py:203
  83.4 0.9 copy-start.4
  84.3 0.9 copy-start.6
  85.3 23.6 %collective-permute-start.8 = (bf16[1,256,128]{2,1,0:T(8,128)(2,1)S(1)}, bf16[1,256,128]{2,1,0:T(8,128)(2,1)S(1)}, u32[]{:S(2)}, u32[]{:S(2)}) collective-permute-start(bf16[1,256,128]{2,1,0:T(8,128)(2,1)S(1)} %get-tuple-element.47), channel_id=1, source_target_pairs={{0,8},{1,9},{2,10},{3,11},{4,12},{5,13},{6,14},{7,15},{8,0},{9,1},... | collective-permute-start | bytes 196616 | tf_op jit(solution)/shard_map/ppermute | solution.py:203
  86.2 3.9 %copy-start.7 = (bf16[2,32,128]{2,1,0:T(8,128)(2,1)}, bf16[2,32,128]{2,1,0:T(8,128)(2,1)S(1)}, u32[]{:S(2)}) copy-start(bf16[2,32,128]{2,1,0:T(8,128)(2,1)S(1)} %low_rank.1.refs_0_) | copy-start | bytes 49156
  86.2 2.2 %collective-permute-start.14 = (bf16[2,32,128]{2,1,0:T(8,128)(2,1)S(1)}, bf16[2,32,128]{2,1,0:T(8,128)(2,1)S(1)}, u32[]{:S(2)}, u32[]{:S(2)}) collective-permute-start(bf16[2,32,128]{2,1,0:T(8,128)(2,1)S(1)} %low_rank.1.refs_0_), channel_id=1, source_target_pairs={{0,1},{1,0},{2,3},{3,2},{4,5},{5,4},{6,7},{7,6},{8,9},{9,8},{10,11... | collective-permute-start | bytes 49160 | tf_op jit(solution)/shard_map/ppermute | solution.py:203
  86.4 2.6 %collective-permute-start.15 = (bf16[2,32,128]{2,1,0:T(8,128)(2,1)S(1)}, bf16[2,32,128]{2,1,0:T(8,128)(2,1)S(1)}, u32[]{:S(2)}, u32[]{:S(2)}) collective-permute-start(bf16[2,32,128]{2,1,0:T(8,128)(2,1)S(1)} %low_rank.1.refs_0_), channel_id=1, source_target_pairs={{0,2},{1,3},{2,0},{3,1},{4,6},{5,7},{6,4},{7,5},{8,10},{9,11},{10,... | collective-permute-start | bytes 49160 | tf_op jit(solution)/shard_map/ppermute | solution.py:203
  86.4 3.7 %collective-permute-start.16 = (bf16[2,32,128]{2,1,0:T(8,128)(2,1)S(1)}, bf16[2,32,128]{2,1,0:T(8,128)(2,1)S(1)}, u32[]{:S(2)}, u32[]{:S(2)}) collective-permute-start(bf16[2,32,128]{2,1,0:T(8,128)(2,1)S(1)} %low_rank.1.refs_0_), channel_id=1, source_target_pairs={{0,3},{1,2},{2,1},{3,0},{4,7},{5,6},{6,5},{7,4},{8,11},{9,10},{10,... | collective-permute-start | bytes 49160 | tf_op jit(solution)/shard_map/ppermute | solution.py:203
  88.4 1.7 %copy-start.12 = (bf16[2,32,128]{2,1,0:T(8,128)(2,1)}, bf16[2,32,128]{2,1,0:T(8,128)(2,1)S(1)}, u32[]{:S(2)}) copy-start(bf16[2,32,128]{2,1,0:T(8,128)(2,1)S(1)} %collective-permute-done.14.refs_1_) | copy-start | bytes 49156
  89.0 1.1 copy-start.13
  90.1 0.6 copy-start.14
  92.1 16.7 %collective-permute-start.17 = (bf16[4,32,128]{2,1,0:T(8,128)(2,1)}, bf16[4,32,128]{2,1,0:T(8,128)(2,1)S(1)}, u32[]{:S(2)}, u32[]{:S(2)}) collective-permute-start(bf16[4,32,128]{2,1,0:T(8,128)(2,1)} %get-tuple-element.50), channel_id=1, source_target_pairs={{0,4},{1,5},{2,6},{3,7},{4,0},{5,1},{6,2},{7,3},{8,12},{9,13},{10,... | collective-permute-start | bytes 98312 | tf_op jit(solution)/shard_map/ppermute | solution.py:203
  97.3 12.2 %collective-permute-start.18 = (bf16[4,32,128]{2,1,0:T(8,128)(2,1)}, bf16[4,32,128]{2,1,0:T(8,128)(2,1)S(1)}, u32[]{:S(2)}, u32[]{:S(2)}) collective-permute-start(bf16[4,32,128]{2,1,0:T(8,128)(2,1)} %get-tuple-element.51), channel_id=1, source_target_pairs={{0,8},{1,9},{2,10},{3,11},{4,12},{5,13},{6,14},{7,15},{8,0},{9,1},... | collective-permute-start | bytes 98312 | tf_op jit(solution)/shard_map/ppermute | solution.py:203
  97.3 12.2 %collective-permute-start.19 = (bf16[4,32,128]{2,1,0:T(8,128)(2,1)}, bf16[4,32,128]{2,1,0:T(8,128)(2,1)S(1)}, u32[]{:S(2)}, u32[]{:S(2)}) collective-permute-start(bf16[4,32,128]{2,1,0:T(8,128)(2,1)} %get-tuple-element.52), channel_id=1, source_target_pairs={{0,12},{1,13},{2,14},{3,15},{4,8},{5,9},{6,10},{7,11},{8,4},{9,5},... | collective-permute-start | bytes 98312 | tf_op jit(solution)/shard_map/ppermute | solution.py:203
  109.5 0.8 copy-start.10

commit v23 on v22

--- a/solution.py
+++ b/solution.py
@@ -81,6 +81,12 @@
         out[...] = sum(parts[1:], parts[0])
 
 
+def pack_kernel(v_ref, q_ref, out_ref):
+    pairs = v_ref.shape[1]
+    out_ref[:, :pairs] = v_ref[...]
+    out_ref[:, pairs:] = q_ref[...]
+
+
 def join_kernel(*refs):
     out, first = refs[-1], 0
     for ref in refs[:-1]:
@@ -94,7 +100,7 @@
         in_specs=[VMEM] * len(arrays),
         out_specs=[VMEM] * len(shapes),
         out_shape=[jax.ShapeDtypeStruct(s, arrays[0].dtype) for s in shapes],
-        compiler_params=pltpu.CompilerParams(vmem_limit_bytes=16 << 20),
+        compiler_params=pltpu.CompilerParams(vmem_limit_bytes=24 << 20),
         cost_estimate=pl.CostEstimate(
             flops=0, bytes_accessed=2 * sum(a.size for a in arrays), transcendentals=0
         ),
@@ -282,7 +288,7 @@
     up_got.append(swap(part, 1 << (bits - 3)))
     held = splitting((after(down_pieces[-1], *up_got[:-1]),), down_got)
     shard = after(total(held[0], to_others(held)), keys, up_got[-1])
-    gathered = [shard] + [swap(shard, k) for k in others]
+    both = join([shard, swap(shard, 2 * quarter)])
 
     up_part = after(up_pieces[-1], shard)
     near_pair, far_pair = on_vmem(
@@ -293,9 +299,10 @@
         *up_got,
     )
     came = swap(far_pair, quarter)
-    asked = jnp.concatenate([by_pairs(values), by_pairs(queries)], axis=1)
-    joined = join(gathered)
-    asked = exchange(after(asked, came, joined))
+    sources = lax.optimization_barrier((by_pairs(values), by_pairs(queries), both, came))[:2]
+    asked = on_vmem(pack_kernel, [(devs, 2 * pairs, toks, width)], "pack", *sources)[0]
+    asked = exchange(asked)
+    joined = join([both, swap(both, quarter)])
     one_shape = (1,) + up_part.shape[1:]
     kept, sent = on_vmem(
         functools.partial(sum_kernel, [[(n, h) for n in range(2)] for h in (0, 1)]),

time: 149 us -> 166 us (1.11)
  waiting for transfers between devices: 58.6 us -> 73.3 us
  other arithmetic: 2.77 us -> 0 us
  blocking collectives: 29.9 us -> 32.1 us
  Pallas kernels: 11.5 us -> 13.5 us
    ppermute x20 -> x19, waiting for transfers between devices: 58.6 us -> 73.3 us  [swap(): return lax.ppermute(tensor, 'seq', [(i, i ^ k) for i in range(devs)])]
    concatenate x1 -> x0, other arithmetic: 2.77 us -> none  [body(): asked = jnp.concatenate([by_pairs(values), by_pairs(queries)], axis=1)]
    all_to_all x1, blocking collectives: 29.9 us -> 32.1 us  [exchange(): lax.all_to_all(tensor, 'seq', split_axis=0, concat_axis=0, tiled=True)]
    ppermute x20 -> x19, starting transfers between devices: 25.3 us -> 25.5 us  [swap(): return lax.ppermute(tensor, 'seq', [(i, i ^ k) for i in range(devs)])]
    unnamed x31 -> x33, local copies, waits for them, and re-layouts: 7.2 us -> 7.32 us
  transfers between devices with their start and end apart: 22 -> 21, of which waited for: 11 -> 10; matrix products, arithmetic and copies ran while one was open for 2% -> 0% of each run, Pallas kernels for 3% -> 3%
where the time goes in v23:
time: 166 us
  waiting for transfers between devices  73.3 us (44%)
  starting transfers between devices  39.2 us (24%)
  blocking collectives  32.1 us (19%)
  Pallas kernels  13.5 us (8%)
  local copies, waits for them, and re-layouts  7.32 us (4%)
    ppermute x19, waiting for transfers between devices, swap(): return lax.ppermute(tensor, 'seq', [(i, i ^ k) for i in range(devs)])  73.3 us
    all_to_all x1, blocking collectives, exchange(): lax.all_to_all(tensor, 'seq', split_axis=0, concat_axis=0, tiled=True)  32.1 us
    ppermute x19, starting transfers between devices, swap(): return lax.ppermute(tensor, 'seq', [(i, i ^ k) for i in range(devs)])  25.5 us
    all_to_all x2, starting transfers between devices, exchange(): lax.all_to_all(tensor, 'seq', split_axis=0, concat_axis=0, tiled=True)  13.7 us
    unnamed x33, local copies, waits for them, and re-layouts  7.32 us
    pallas_call x1, Pallas kernels, body(): pl.pallas_call(functools.partial(attend_kernel, math.gcd(devs, max(1, 256...  7.23 us
  transfers between devices with their start and end apart: 21, of which 10 were waited for; matrix products, arithmetic and copies ran while one was open for 0% of the time, Pallas kernels for 3%

profile of v23, /device:TPU:1, one launch (start us, length us, event | category | flops | bytes accessed | tf_op | source)
XLA Modules:
  0.0 165.6 jit_solution(1976774195794756239)
XLA Ops:
  0.0 7.5 %all-to-all-start = ((bf16[16,4,64,128]{3,2,1,0:T(8,128)(2,1)}), bf16[16,4,64,128]{3,2,1,0:T(8,128)(2,1)S(1)}, u32[]{:S(2)}, u32[]{:S(2)}) async-start(bf16[16,4,64,128]{3,2,1,0:T(8,128)(2,1)} %bitcast.10), calls=%async_computation | async-start | bytes 2097152 | tf_op jit(solution)/shard_map/all_to_all | solution.py:212
  7.5 1.7 %copy-done = bf16[4,64,5120]{2,1,0:T(8,128)(2,1)S(1)} copy-done((bf16[4,64,5120]{2,1,0:T(8,128)(2,1)S(1)}, bf16[4,64,5120]{2,1,0:T(8,128)(2,1)}, u32[]{:S(2)}) %copy-start) | copy-done | bytes 2621464
  9.3 1.8 %pick_factors.1 = (bf16[8,320,128]{2,1,0:T(8,128)(2,1)S(1)}, bf16[4,320,128]{2,1,0:T(8,128)(2,1)S(1)}, bf16[4,320,128]{2,1,0:T(8,128)(2,1)S(1)}, bf16[8,256,128]...) custom-call(s32[1]{0:T(128)} %bitcast.me_ref, s32[64]{0:T(128)S(1)} %copy-done.10, ...), custom_call_target="tpu_custom_call" | custom-call | bytes 4718592 | tf_op jit(solution)/shard_map/pick_factors/pallas_call | solution.py:256
  11.1 0.1 collective-permute-start
  11.2 2.1 %collective-permute-done.refs_1_ = bf16[8,320,128]{2,1,0:T(8,128)(2,1)S(1)} collective-permute-done((bf16[8,320,128]{2,1,0:T(8,128)(2,1)S(1)}, bf16[8,320,128]{2,1,0:T(8,128)(2,1)S(1)}, u32[]{:S(2)}, u32[]{:S(2)}) %collective-permute-start) | collective-permute-done | bytes 655392 | tf_op jit(solution)/shard_map/ppermute | solution.py:209
  13.3 0.1 halve.2
  13.4 0.2 collective-permute-start.1
  13.6 1.3 collective-permute-start.2
  14.9 0.5 collective-permute-done.1.refs_1_
  15.4 0.1 halve.3
  15.5 1.1 collective-permute-start.6
  16.6 10.3 %collective-permute-done.2.refs_2_ = bf16[4,320,128]{2,1,0:T(8,128)(2,1)S(1)} collective-permute-done((bf16[4,320,128]{2,1,0:T(8,128)(2,1)S(1)}, bf16[4,320,128]{2,1,0:T(8,128)(2,1)S(1)}, u32[]{:S(2)}, u32[]{:S(2)}) %collective-permute-start.2) | collective-permute-done | bytes 327712 | tf_op jit(solution)/shard_map/ppermute | solution.py:209
  26.9 0.2 split.3
  27.0 3.2 %collective-permute-start.3 = (bf16[1,320,128]{2,1,0:T(8,128)(2,1)S(1)}, bf16[1,320,128]{2,1,0:T(8,128)(2,1)S(1)}, u32[]{:S(2)}, u32[]{:S(2)}) collective-permute-start(bf16[1,320,128]{2,1,0:T(8,128)(2,1)S(1)} %get-tuple-element.38), channel_id=1, source_target_pairs={{0,8},{1,9},{2,10},{3,11},{4,12},{5,13},{6,14},{7,15},{8,0},{9,1},... | collective-permute-start | bytes 245768 | tf_op jit(solution)/shard_map/ppermute | solution.py:209
  30.2 0.1 collective-permute-start.4
  30.3 1.7 %collective-permute-start.5 = (bf16[1,320,128]{2,1,0:T(8,128)(2,1)S(1)}, bf16[1,320,128]{2,1,0:T(8,128)(2,1)S(1)}, u32[]{:S(2)}, u32[]{:S(2)}) collective-permute-start(bf16[1,320,128]{2,1,0:T(8,128)(2,1)S(1)} %get-tuple-element.40), channel_id=1, source_target_pairs={{0,12},{1,13},{2,14},{3,15},{4,8},{5,9},{6,10},{7,11},{8,4},{9,5},... | collective-permute-start | bytes 245768 | tf_op jit(solution)/shard_map/ppermute | solution.py:209
  32.0 5.6 %collective-permute-done.3.refs_1_ = bf16[1,320,128]{2,1,0:T(8,128)(2,1)S(1)} collective-permute-done((bf16[1,320,128]{2,1,0:T(8,128)(2,1)S(1)}, bf16[1,320,128]{2,1,0:T(8,128)(2,1)S(1)}, u32[]{:S(2)}, u32[]{:S(2)}) %collective-permute-start.3) | collective-permute-done | bytes 81952 | tf_op jit(solution)/shard_map/ppermute | solution.py:209
  37.7 0.7 copy-done.5
  38.4 1.0 copy-done.6
  39.5 0.1 split.4
  39.6 3.0 %collective-permute-start.7 = (bf16[2,256,128]{2,1,0:T(8,128)(2,1)S(1)}, bf16[2,256,128]{2,1,0:T(8,128)(2,1)S(1)}, u32[]{:S(2)}, u32[]{:S(2)}) collective-permute-start(bf16[2,256,128]{2,1,0:T(8,128)(2,1)S(1)} %get-tuple-element.46), channel_id=1, source_target_pairs={{0,4},{1,5},{2,6},{3,7},{4,0},{5,1},{6,2},{7,3},{8,12},{9,13},{10,... | collective-permute-start | bytes 393224 | tf_op jit(solution)/shard_map/ppermute | solution.py:209
  42.5 0.1 collective-permute-start.9
  42.6 4.7 %collective-permute-done.9.refs_1_ = bf16[1,320,128]{2,1,0:T(8,128)(2,1)S(1)} collective-permute-done((bf16[1,320,128]{2,1,0:T(8,128)(2,1)S(1)}, bf16[1,320,128]{2,1,0:T(8,128)(2,1)S(1)}, u32[]{:S(2)}, u32[]{:S(2)}) %collective-permute-start.9) | collective-permute-done | bytes 81952 | tf_op jit(solution)/shard_map/ppermute | solution.py:209
  47.4 1.5 pack.1
  48.9 6.3 %all-to-all-start.1 = ((bf16[16,8,64,128]{3,2,1,0:T(8,128)(2,1)}), bf16[16,8,64,128]{3,2,1,0:T(8,128)(2,1)S(1)}, u32[]{:S(2)}, u32[]{:S(2)}) async-start(bf16[16,8,64,128]{3,2,1,0:T(8,128)(2,1)} %pack.1), calls=%async_computation.1 | async-start | bytes 4194304 | tf_op jit(solution)/shard_map/all_to_all | solution.py:212
  55.2 1.5 collective-permute-start.10
  56.6 36.3 %collective-permute-done.10.refs_1_ = bf16[2,320,128]{2,1,0:T(8,128)(2,1)S(1)} collective-permute-done((bf16[2,320,128]{2,1,0:T(8,128)(2,1)S(1)}, bf16[2,320,128]{2,1,0:T(8,128)(2,1)S(1)}, u32[]{:S(2)}, u32[]{:S(2)}) %collective-permute-start.10) | collective-permute-done | bytes 163872 | tf_op jit(solution)/shard_map/ppermute | solution.py:209
  93.0 1.6 collective-permute-start.11
  94.7 9.6 %collective-permute-done.11.refs_1_ = bf16[4,320,128]{2,1,0:T(8,128)(2,1)S(1)} collective-permute-done((bf16[4,320,128]{2,1,0:T(8,128)(2,1)S(1)}, bf16[4,320,128]{2,1,0:T(8,128)(2,1)S(1)}, u32[]{:S(2)}, u32[]{:S(2)}) %collective-permute-start.11) | collective-permute-done | bytes 327712 | tf_op jit(solution)/shard_map/ppermute | solution.py:209
  104.3 0.6 collective-permute-start.12
  104.9 0.9 copy-done.8
  105.8 5.4 %collective-permute-start.8 = (bf16[1,256,128]{2,1,0:T(8,128)(2,1)S(1)}, bf16[1,256,128]{2,1,0:T(8,128)(2,1)S(1)}, u32[]{:S(2)}, u32[]{:S(2)}) collective-permute-start(bf16[1,256,128]{2,1,0:T(8,128)(2,1)S(1)} %get-tuple-element.48), channel_id=1, source_target_pairs={{0,8},{1,9},{2,10},{3,11},{4,12},{5,13},{6,14},{7,15},{8,0},{9,1},... | collective-permute-start | bytes 196616 | tf_op jit(solution)/shard_map/ppermute | solution.py:209
  111.2 0.9 low_rank.1.refs_0_
  112.1 1.6 collective-permute-start.14
  113.7 0.5 collective-permute-start.13
  114.2 1.0 collective-permute-done.15.refs_3_
  115.3 0.6 copy-done.13
  115.9 0.6 copy-done.15
  116.5 1.4 choose.1
  117.9 0.2 collective-permute-start.16
  118.1 1.5 collective-permute-start.17
  119.6 1.8 %collective-permute-start.18 = (bf16[4,32,128]{2,1,0:T(8,128)(2,1)}, bf16[4,32,128]{2,1,0:T(8,128)(2,1)S(1)}, u32[]{:S(2)}, u32[]{:S(2)}) collective-permute-start(bf16[4,32,128]{2,1,0:T(8,128)(2,1)} %get-tuple-element.54), channel_id=1, source_target_pairs={{0,12},{1,13},{2,14},{3,15},{4,8},{5,9},{6,10},{7,11},{8,4},{9,5},... | collective-permute-start | bytes 98312 | tf_op jit(solution)/shard_map/ppermute | solution.py:209
  121.5 0.5 collective-permute-done.17.refs_2_
  121.9 2.6 %collective-permute-done.18.refs_3_ = bf16[4,32,128]{2,1,0:T(8,128)(2,1)S(1)} collective-permute-done((bf16[4,32,128]{2,1,0:T(8,128)(2,1)}, bf16[4,32,128]{2,1,0:T(8,128)(2,1)S(1)}, u32[]{:S(2)}, u32[]{:S(2)}) %collective-permute-start.18) | collective-permute-done | bytes 32800 | tf_op jit(solution)/shard_map/ppermute | solution.py:209
  124.5 0.8 copy-done.12
  125.3 7.2 %attend.1 = bf16[16,4,64,128]{3,2,1,0:T(8,128)(2,1)S(1)} custom-call(s32[1]{0:T(128)} %bitcast.me_ref, bf16[4,64,128]{2,1,0:T(8,128)(2,1)S(1)} %bitcast.8, bf16[16,8,64,128]{3,2,1,0:T(8,128)(2,1)S(1)} %all-to-all-done.1.q_ref.v_ref, bf16[16,4,64,128]{3,2,1,0:T(8,128)(2,1)S(1)} %all-to-all-done.k_ref, ...), custom_call_target="tpu_custom_call" | custom-call | flops 2147483648 | bytes 4194304 | tf_op jit(solution)/shard_map/attend/pallas_call | solution.py:352
  132.5 32.1 %all_to_all.15 = bf16[16,4,64,128]{3,2,1,0:T(8,128)(2,1)S(1)} all-to-all(bf16[16,4,64,128]{3,2,1,0:T(8,128)(2,1)S(1)} %attend.1), channel_id=1, replica_groups=mesh['grp'=2,'seq'=16] {'seq'}, dimensions={0} | all-to-all | bytes 2097152 | tf_op jit(solution)/shard_map/all_to_all | solution.py:212
  164.6 1.0 copy.10
  (43 shorter events, 0.3 us)
Async XLA Ops:
  0.0 7.5 %copy-start.11 = (s32[2]{0:T(128)S(1)}, s32[2]{0:T(128)}, u32[]{:S(2)}) copy-start(s32[2]{0:T(128)} %req_ref.1) | copy-start | bytes 28
  0.0 7.5 %copy-start.10 = (s32[64]{0:T(128)S(1)}, s32[64]{0:T(128)}, u32[]{:S(2)}) copy-start(s32[64]{0:T(128)} %row_ref.1) | copy-start | bytes 772
  0.0 7.5 %copy-start.1 = (bf16[4,64,4096]{2,1,0:T(8,128)(2,1)S(1)}, bf16[4,64,4096]{2,1,0:T(8,128)(2,1)}, u32[]{:S(2)}) copy-start(bf16[4,64,4096]{2,1,0:T(8,128)(2,1)} %up_ref.1) | copy-start | bytes 6291460
  0.0 38.4 %all-to-all-start = ((bf16[16,4,64,128]{3,2,1,0:T(8,128)(2,1)}), bf16[16,4,64,128]{3,2,1,0:T(8,128)(2,1)S(1)}, u32[]{:S(2)}, u32[]{:S(2)}) async-start(bf16[16,4,64,128]{3,2,1,0:T(8,128)(2,1)} %bitcast.10), calls=%async_computation | async-start | bytes 2097152 | tf_op jit(solution)/shard_map/all_to_all | solution.py:212
  7.5 1.7 %copy-start = (bf16[4,64,5120]{2,1,0:T(8,128)(2,1)S(1)}, bf16[4,64,5120]{2,1,0:T(8,128)(2,1)}, u32[]{:S(2)}) copy-start(bf16[4,64,5120]{2,1,0:T(8,128)(2,1)} %down_ref.1) | copy-start | bytes 7864324
  11.1 2.2 %collective-permute-start = (bf16[8,320,128]{2,1,0:T(8,128)(2,1)S(1)}, bf16[8,320,128]{2,1,0:T(8,128)(2,1)S(1)}, u32[]{:S(2)}, u32[]{:S(2)}) collective-permute-start(bf16[8,320,128]{2,1,0:T(8,128)(2,1)S(1)} %get-tuple-element.34), channel_id=1, source_target_pairs={{0,1},{1,0},{2,3},{3,2},{4,5},{5,4},{6,7},{7,6},{8,9},{9,8},{10,11... | collective-permute-start | bytes 1966088 | tf_op jit(solution)/shard_map/ppermute | solution.py:209
  13.4 34.0 %copy-start.3 = (bf16[2,32,64,128]{3,2,1,0:T(8,128)(2,1)S(1)}, bf16[2,32,64,128]{3,2,1,0:T(8,128)(2,1)}, u32[]{:S(2)}) copy-start(bf16[2,32,64,128]{3,2,1,0:T(8,128)(2,1)} %param.11) | copy-start | bytes 3145732
  13.4 2.0 %collective-permute-start.1 = (bf16[8,256,128]{2,1,0:T(8,128)(2,1)S(1)}, bf16[8,256,128]{2,1,0:T(8,128)(2,1)S(1)}, u32[]{:S(2)}, u32[]{:S(2)}) collective-permute-start(bf16[8,256,128]{2,1,0:T(8,128)(2,1)S(1)} %get-tuple-element.35), channel_id=1, source_target_pairs={{0,1},{1,0},{2,3},{3,2},{4,5},{5,4},{6,7},{7,6},{8,9},{9,8},{10,11... | collective-permute-start | bytes 1572872 | tf_op jit(solution)/shard_map/ppermute | solution.py:209
  13.6 13.2 %collective-permute-start.2 = (bf16[4,320,128]{2,1,0:T(8,128)(2,1)S(1)}, bf16[4,320,128]{2,1,0:T(8,128)(2,1)S(1)}, u32[]{:S(2)}, u32[]{:S(2)}) collective-permute-start(bf16[4,320,128]{2,1,0:T(8,128)(2,1)S(1)} %halve.2), channel_id=1, source_target_pairs={{0,2},{1,3},{2,0},{3,1},{4,6},{5,7},{6,4},{7,5},{8,10},{9,11},{10,... | collective-permute-start | bytes 983048 | tf_op jit(solution)/shard_map/ppermute | solution.py:209
  15.5 22.2 %collective-permute-start.6 = (bf16[4,256,128]{2,1,0:T(8,128)(2,1)S(1)}, bf16[4,256,128]{2,1,0:T(8,128)(2,1)S(1)}, u32[]{:S(2)}, u32[]{:S(2)}) collective-permute-start(bf16[4,256,128]{2,1,0:T(8,128)(2,1)S(1)} %halve.3), channel_id=1, source_target_pairs={{0,2},{1,3},{2,0},{3,1},{4,6},{5,7},{6,4},{7,5},{8,10},{9,11},{10,... | collective-permute-start | bytes 786440 | tf_op jit(solution)/shard_map/ppermute | solution.py:209
  27.0 10.7 %collective-permute-start.3 = (bf16[1,320,128]{2,1,0:T(8,128)(2,1)S(1)}, bf16[1,320,128]{2,1,0:T(8,128)(2,1)S(1)}, u32[]{:S(2)}, u32[]{:S(2)}) collective-permute-start(bf16[1,320,128]{2,1,0:T(8,128)(2,1)S(1)} %get-tuple-element.38), channel_id=1, source_target_pairs={{0,8},{1,9},{2,10},{3,11},{4,12},{5,13},{6,14},{7,15},{8,0},{9,1},... | collective-permute-start | bytes 245768 | tf_op jit(solution)/shard_map/ppermute | solution.py:209
  30.2 7.4 %collective-permute-start.4 = (bf16[1,320,128]{2,1,0:T(8,128)(2,1)S(1)}, bf16[1,320,128]{2,1,0:T(8,128)(2,1)S(1)}, u32[]{:S(2)}, u32[]{:S(2)}) collective-permute-start(bf16[1,320,128]{2,1,0:T(8,128)(2,1)S(1)} %get-tuple-element.39), channel_id=1, source_target_pairs={{0,4},{1,5},{2,6},{3,7},{4,0},{5,1},{6,2},{7,3},{8,12},{9,13},{10,... | collective-permute-start | bytes 245768 | tf_op jit(solution)/shard_map/ppermute | solution.py:209
  30.3 7.4 %collective-permute-start.5 = (bf16[1,320,128]{2,1,0:T(8,128)(2,1)S(1)}, bf16[1,320,128]{2,1,0:T(8,128)(2,1)S(1)}, u32[]{:S(2)}, u32[]{:S(2)}) collective-permute-start(bf16[1,320,128]{2,1,0:T(8,128)(2,1)S(1)} %get-tuple-element.40), channel_id=1, source_target_pairs={{0,12},{1,13},{2,14},{3,15},{4,8},{5,9},{6,10},{7,11},{8,4},{9,5},... | collective-permute-start | bytes 245768 | tf_op jit(solution)/shard_map/ppermute | solution.py:209
  37.7 0.7 copy-start.5
  38.4 9.0 %copy-start.4 = (bf16[2,32,64,128]{3,2,1,0:T(8,128)(2,1)S(1)}, bf16[2,32,64,128]{3,2,1,0:T(8,128)(2,1)}, u32[]{:S(2)}) copy-start(bf16[2,32,64,128]{3,2,1,0:T(8,128)(2,1)} %param.9) | copy-start | bytes 3145732
  38.4 1.0 copy-start.6
  39.6 7.8 %collective-permute-start.7 = (bf16[2,256,128]{2,1,0:T(8,128)(2,1)S(1)}, bf16[2,256,128]{2,1,0:T(8,128)(2,1)S(1)}, u32[]{:S(2)}, u32[]{:S(2)}) collective-permute-start(bf16[2,256,128]{2,1,0:T(8,128)(2,1)S(1)} %get-tuple-element.46), channel_id=1, source_target_pairs={{0,4},{1,5},{2,6},{3,7},{4,0},{5,1},{6,2},{7,3},{8,12},{9,13},{10,... | collective-permute-start | bytes 393224 | tf_op jit(solution)/shard_map/ppermute | solution.py:209
  42.5 4.8 %collective-permute-start.9 = (bf16[1,320,128]{2,1,0:T(8,128)(2,1)S(1)}, bf16[1,320,128]{2,1,0:T(8,128)(2,1)S(1)}, u32[]{:S(2)}, u32[]{:S(2)}) collective-permute-start(bf16[1,320,128]{2,1,0:T(8,128)(2,1)S(1)} %total.2.refs_0_), channel_id=1, source_target_pairs={{0,8},{1,9},{2,10},{3,11},{4,12},{5,13},{6,14},{7,15},{8,0},{9,1},... | collective-permute-start | bytes 245768 | tf_op jit(solution)/shard_map/ppermute | solution.py:209
  47.4 1.5 copy-start.7
  48.9 75.6 %all-to-all-start.1 = ((bf16[16,8,64,128]{3,2,1,0:T(8,128)(2,1)}), bf16[16,8,64,128]{3,2,1,0:T(8,128)(2,1)S(1)}, u32[]{:S(2)}, u32[]{:S(2)}) async-start(bf16[16,8,64,128]{3,2,1,0:T(8,128)(2,1)} %pack.1), calls=%async_computation.1 | async-start | bytes 4194304 | tf_op jit(solution)/shard_map/all_to_all | solution.py:212
  55.2 56.0 %copy-start.2 = (bf16[2,64,5120]{2,1,0:T(8,128)(2,1)S(1)}, bf16[2,64,5120]{2,1,0:T(8,128)(2,1)}, u32[]{:S(2)}) copy-start(bf16[2,64,5120]{2,1,0:T(8,128)(2,1)} %x_ref.1) | copy-start | bytes 3932164
  55.2 37.8 %collective-permute-start.10 = (bf16[2,320,128]{2,1,0:T(8,128)(2,1)S(1)}, bf16[2,320,128]{2,1,0:T(8,128)(2,1)S(1)}, u32[]{:S(2)}, u32[]{:S(2)}) collective-permute-start(bf16[2,320,128]{2,1,0:T(8,128)(2,1)S(1)} %join.3.refs_0_), channel_id=1, source_target_pairs={{0,4},{1,5},{2,6},{3,7},{4,0},{5,1},{6,2},{7,3},{8,12},{9,13},{10,... | collective-permute-start | bytes 491528 | tf_op jit(solution)/shard_map/ppermute | solution.py:209
  93.0 11.2 %collective-permute-start.11 = (bf16[4,320,128]{2,1,0:T(8,128)(2,1)S(1)}, bf16[4,320,128]{2,1,0:T(8,128)(2,1)S(1)}, u32[]{:S(2)}, u32[]{:S(2)}) collective-permute-start(bf16[4,320,128]{2,1,0:T(8,128)(2,1)S(1)} %join.4.refs_0_), channel_id=1, source_target_pairs={{0,2},{1,3},{2,0},{3,1},{4,6},{5,7},{6,4},{7,5},{8,10},{9,11},{10,... | collective-permute-start | bytes 983048 | tf_op jit(solution)/shard_map/ppermute | solution.py:209
  104.3 6.9 %collective-permute-start.12 = (bf16[8,320,128]{2,1,0:T(8,128)(2,1)S(1)}, bf16[8,320,128]{2,1,0:T(8,128)(2,1)S(1)}, u32[]{:S(2)}, u32[]{:S(2)}) collective-permute-start(bf16[8,320,128]{2,1,0:T(8,128)(2,1)S(1)} %join.5.refs_0_), channel_id=1, source_target_pairs={{0,1},{1,0},{2,3},{3,2},{4,5},{5,4},{6,7},{7,6},{8,9},{9,8},{10,11... | collective-permute-start | bytes 1966088 | tf_op jit(solution)/shard_map/ppermute | solution.py:209
  104.9 0.9 copy-start.8
  105.8 15.6 %collective-permute-start.8 = (bf16[1,256,128]{2,1,0:T(8,128)(2,1)S(1)}, bf16[1,256,128]{2,1,0:T(8,128)(2,1)S(1)}, u32[]{:S(2)}, u32[]{:S(2)}) collective-permute-start(bf16[1,256,128]{2,1,0:T(8,128)(2,1)S(1)} %get-tuple-element.48), channel_id=1, source_target_pairs={{0,8},{1,9},{2,10},{3,11},{4,12},{5,13},{6,14},{7,15},{8,0},{9,1},... | collective-permute-start | bytes 196616 | tf_op jit(solution)/shard_map/ppermute | solution.py:209
  112.1 3.2 %copy-start.9 = (bf16[2,32,128]{2,1,0:T(8,128)(2,1)}, bf16[2,32,128]{2,1,0:T(8,128)(2,1)S(1)}, u32[]{:S(2)}) copy-start(bf16[2,32,128]{2,1,0:T(8,128)(2,1)S(1)} %low_rank.1.refs_0_) | copy-start | bytes 49156
  112.1 3.2 %collective-permute-start.15 = (bf16[2,32,128]{2,1,0:T(8,128)(2,1)S(1)}, bf16[2,32,128]{2,1,0:T(8,128)(2,1)S(1)}, u32[]{:S(2)}, u32[]{:S(2)}) collective-permute-start(bf16[2,32,128]{2,1,0:T(8,128)(2,1)S(1)} %low_rank.1.refs_0_), channel_id=1, source_target_pairs={{0,3},{1,2},{2,1},{3,0},{4,7},{5,6},{6,5},{7,4},{8,11},{9,10},{10,... | collective-permute-start | bytes 49160 | tf_op jit(solution)/shard_map/ppermute | solution.py:209
  112.1 3.2 %collective-permute-start.14 = (bf16[2,32,128]{2,1,0:T(8,128)(2,1)S(1)}, bf16[2,32,128]{2,1,0:T(8,128)(2,1)S(1)}, u32[]{:S(2)}, u32[]{:S(2)}) collective-permute-start(bf16[2,32,128]{2,1,0:T(8,128)(2,1)S(1)} %low_rank.1.refs_0_), channel_id=1, source_target_pairs={{0,2},{1,3},{2,0},{3,1},{4,6},{5,7},{6,4},{7,5},{8,10},{9,11},{10,... | collective-permute-start | bytes 49160 | tf_op jit(solution)/shard_map/ppermute | solution.py:209
  113.7 1.5 collective-permute-start.13
  115.3 0.6 copy-start.13
  115.3 0.6 copy-start.14
  115.9 0.6 copy-start.15
  117.9 3.6 %collective-permute-start.16 = (bf16[4,32,128]{2,1,0:T(8,128)(2,1)}, bf16[4,32,128]{2,1,0:T(8,128)(2,1)S(1)}, u32[]{:S(2)}, u32[]{:S(2)}) collective-permute-start(bf16[4,32,128]{2,1,0:T(8,128)(2,1)} %get-tuple-element.52), channel_id=1, source_target_pairs={{0,4},{1,5},{2,6},{3,7},{4,0},{5,1},{6,2},{7,3},{8,12},{9,13},{10,... | collective-permute-start | bytes 98312 | tf_op jit(solution)/shard_map/ppermute | solution.py:209
  118.1 3.9 %collective-permute-start.17 = (bf16[4,32,128]{2,1,0:T(8,128)(2,1)}, bf16[4,32,128]{2,1,0:T(8,128)(2,1)S(1)}, u32[]{:S(2)}, u32[]{:S(2)}) collective-permute-start(bf16[4,32,128]{2,1,0:T(8,128)(2,1)} %get-tuple-element.53), channel_id=1, source_target_pairs={{0,8},{1,9},{2,10},{3,11},{4,12},{5,13},{6,14},{7,15},{8,0},{9,1},... | collective-permute-start | bytes 98312 | tf_op jit(solution)/shard_map/ppermute | solution.py:209
  119.6 4.9 %collective-permute-start.18 = (bf16[4,32,128]{2,1,0:T(8,128)(2,1)}, bf16[4,32,128]{2,1,0:T(8,128)(2,1)S(1)}, u32[]{:S(2)}, u32[]{:S(2)}) collective-permute-start(bf16[4,32,128]{2,1,0:T(8,128)(2,1)} %get-tuple-element.54), channel_id=1, source_target_pairs={{0,12},{1,13},{2,14},{3,15},{4,8},{5,9},{6,10},{7,11},{8,4},{9,5},... | collective-permute-start | bytes 98312 | tf_op jit(solution)/shard_map/ppermute | solution.py:209
  124.5 0.8 copy-start.12

commit v24 on v22

--- a/solution.py
+++ b/solution.py
@@ -284,30 +284,9 @@
     shard = after(total(held[0], to_others(held)), keys, up_got[-1])
     gathered = [shard] + [swap(shard, k) for k in others]
 
-    up_part = after(up_pieces[-1], shard)
-    near_pair, far_pair = on_vmem(
-        functools.partial(sum_kernel, [[(n, 2 * h) for n in range(1 + len(up_got))] for h in (0, 1)]),
-        [(2,) + up_part.shape[1:]] * 2,
-        "split",
-        up_part,
-        *up_got,
-    )
-    came = swap(far_pair, quarter)
+    joined = join(gathered)
     asked = jnp.concatenate([by_pairs(values), by_pairs(queries)], axis=1)
-    joined = join(gathered)
-    asked = exchange(after(asked, came, joined))
-    one_shape = (1,) + up_part.shape[1:]
-    kept, sent = on_vmem(
-        functools.partial(sum_kernel, [[(n, h) for n in range(2)] for h in (0, 1)]),
-        [one_shape] * 2,
-        "split",
-        near_pair,
-        came,
-    )
-    last = swap(sent, 2 * quarter)
-    up_here = on_vmem(
-        functools.partial(sum_kernel, [[(0, 0), (1, 0)]]), [one_shape], "total", kept, last
-    )[0].reshape(pairs, ranks, LANES)
+    asked = exchange(after(asked, joined))
     for i in reversed(range(bits - 2)):
         gathered = [joined, swap(joined, 1 << i)]
         if i > 0:
@@ -328,6 +307,27 @@
         ),
         name="low_rank",
     )(me, normed_token_features, *gathered)
+    up_part = after(up_pieces[-1], low)
+    near_pair, far_pair = on_vmem(
+        functools.partial(sum_kernel, [[(n, 2 * h) for n in range(1 + len(up_got))] for h in (0, 1)]),
+        [(2,) + up_part.shape[1:]] * 2,
+        "split",
+        up_part,
+        *up_got,
+    )
+    came = swap(far_pair, quarter)
+    one_shape = (1,) + up_part.shape[1:]
+    kept, sent = on_vmem(
+        functools.partial(sum_kernel, [[(n, h) for n in range(2)] for h in (0, 1)]),
+        [one_shape] * 2,
+        "split",
+        near_pair,
+        came,
+    )
+    last = swap(sent, 2 * quarter)
+    up_here = on_vmem(
+        functools.partial(sum_kernel, [[(0, 0), (1, 0)]]), [one_shape], "total", kept, last
+    )[0].reshape(pairs, ranks, LANES)
     nearby = [low] + [swap(low, k) for k in range(1, LOW)]
     chosen = pl.pallas_call(
         functools.partial(choose_kernel, per_video),

time: 149 us -> 150 us (level)
  local copies, waits for them, and re-layouts: 7.2 us -> 4.08 us
  starting transfers between devices: 38.3 us -> 39.9 us
  blocking collectives: 29.9 us -> 31.4 us
    unnamed x31 -> x21, local copies, waits for them, and re-layouts: 7.2 us -> 4.08 us
    all_to_all x1, blocking collectives: 29.9 us -> 31.4 us  [exchange(): lax.all_to_all(tensor, 'seq', split_axis=0, concat_axis=0, tiled=True)]
  transfers between devices with their start and end apart: 22 -> 22, of which waited for: 11 -> 12; matrix products, arithmetic and copies ran while one was open for 2% -> 2% of each run, Pallas kernels for 3% -> 3%
where the time goes in v24:
time: 150 us
  waiting for transfers between devices  58.9 us (39%)
  starting transfers between devices  39.9 us (27%)
  blocking collectives  31.4 us (21%)
  Pallas kernels  12.3 us (8%)
  local copies, waits for them, and re-layouts  4.08 us (3%)
  other arithmetic  3.09 us (2%)
    ppermute x20, waiting for transfers between devices, swap(): return lax.ppermute(tensor, 'seq', [(i, i ^ k) for i in range(devs)])  58.9 us
    all_to_all x1, blocking collectives, exchange(): lax.all_to_all(tensor, 'seq', split_axis=0, concat_axis=0, tiled=True)  31.4 us
    ppermute x20, starting transfers between devices, swap(): return lax.ppermute(tensor, 'seq', [(i, i ^ k) for i in range(devs)])  26.5 us
    all_to_all x2, starting transfers between devices, exchange(): lax.all_to_all(tensor, 'seq', split_axis=0, concat_axis=0, tiled=True)  13.4 us
    pallas_call x1, Pallas kernels, body(): pl.pallas_call(functools.partial(attend_kernel, math.gcd(devs, max(1, 256...  8.07 us
    unnamed x21, local copies, waits for them, and re-layouts  4.08 us
    concatenate x1, other arithmetic, body(): asked = jnp.concatenate([by_pairs(values), by_pairs(queries)], axis=1)  3.09 us
  transfers between devices with their start and end apart: 22, of which 12 were waited for; matrix products, arithmetic and copies ran while one was open for 2% of the time, Pallas kernels for 3%

profile of v24, /device:TPU:1, one launch (start us, length us, event | category | flops | bytes accessed | tf_op | source)
XLA Modules:
  0.0 149.8 jit_solution(18148923296942082473)
XLA Ops:
  0.0 7.5 %all-to-all-start = ((bf16[16,4,64,128]{3,2,1,0:T(8,128)(2,1)}), bf16[16,4,64,128]{3,2,1,0:T(8,128)(2,1)}, u32[]{:S(2)}, u32[]{:S(2)}) async-start(bf16[16,4,64,128]{3,2,1,0:T(8,128)(2,1)} %bitcast.8), calls=%async_computation | async-start | bytes 2097152 | tf_op jit(solution)/shard_map/all_to_all | solution.py:206
  7.5 0.0 copy-start
  7.5 1.7 %copy-done = bf16[4,64,5120]{2,1,0:T(8,128)(2,1)S(1)} copy-done((bf16[4,64,5120]{2,1,0:T(8,128)(2,1)S(1)}, bf16[4,64,5120]{2,1,0:T(8,128)(2,1)}, u32[]{:S(2)}) %copy-start) | copy-done | bytes 2621464
  9.3 1.5 %pick_factors.1 = (bf16[8,320,128]{2,1,0:T(8,128)(2,1)S(1)}, bf16[4,320,128]{2,1,0:T(8,128)(2,1)S(1)}, bf16[4,320,128]{2,1,0:T(8,128)(2,1)S(1)}, bf16[8,256,128]...) custom-call(s32[1]{0:T(128)} %bitcast.me_ref, s32[64]{0:T(128)S(1)} %copy-done.4, ...), custom_call_target="tpu_custom_call" | custom-call | bytes 4718592 | tf_op jit(solution)/shard_map/pick_factors/pallas_call | solution.py:250
  10.8 0.2 collective-permute-start
  11.0 1.9 %collective-permute-done.refs_1_ = bf16[8,320,128]{2,1,0:T(8,128)(2,1)S(1)} collective-permute-done((bf16[8,320,128]{2,1,0:T(8,128)(2,1)S(1)}, bf16[8,320,128]{2,1,0:T(8,128)(2,1)S(1)}, u32[]{:S(2)}, u32[]{:S(2)}) %collective-permute-start) | collective-permute-done | bytes 655392 | tf_op jit(solution)/shard_map/ppermute | solution.py:203
  13.0 0.1 halve.2
  13.0 0.2 collective-permute-start.1
  13.3 1.6 %collective-permute-start.2 = (bf16[4,320,128]{2,1,0:T(8,128)(2,1)S(1)}, bf16[4,320,128]{2,1,0:T(8,128)(2,1)S(1)}, u32[]{:S(2)}, u32[]{:S(2)}) collective-permute-start(bf16[4,320,128]{2,1,0:T(8,128)(2,1)S(1)} %halve.2), channel_id=1, source_target_pairs={{0,2},{1,3},{2,0},{3,1},{4,6},{5,7},{6,4},{7,5},{8,10},{9,11},{10,... | collective-permute-start | bytes 983048 | tf_op jit(solution)/shard_map/ppermute | solution.py:203
  14.8 0.2 collective-permute-done.1.refs_1_
  15.0 0.1 halve.3
  15.1 1.5 collective-permute-start.6
  16.5 10.4 %collective-permute-done.2.refs_2_ = bf16[4,320,128]{2,1,0:T(8,128)(2,1)S(1)} collective-permute-done((bf16[4,320,128]{2,1,0:T(8,128)(2,1)S(1)}, bf16[4,320,128]{2,1,0:T(8,128)(2,1)S(1)}, u32[]{:S(2)}, u32[]{:S(2)}) %collective-permute-start.2) | collective-permute-done | bytes 327712 | tf_op jit(solution)/shard_map/ppermute | solution.py:203
  26.9 0.1 split.3
  27.0 3.2 %collective-permute-start.3 = (bf16[1,320,128]{2,1,0:T(8,128)(2,1)S(1)}, bf16[1,320,128]{2,1,0:T(8,128)(2,1)S(1)}, u32[]{:S(2)}, u32[]{:S(2)}) collective-permute-start(bf16[1,320,128]{2,1,0:T(8,128)(2,1)S(1)} %get-tuple-element.37), channel_id=1, source_target_pairs={{0,8},{1,9},{2,10},{3,11},{4,12},{5,13},{6,14},{7,15},{8,0},{9,1},... | collective-permute-start | bytes 245768 | tf_op jit(solution)/shard_map/ppermute | solution.py:203
  30.2 0.1 collective-permute-start.4
  30.2 1.7 %collective-permute-start.5 = (bf16[1,320,128]{2,1,0:T(8,128)(2,1)S(1)}, bf16[1,320,128]{2,1,0:T(8,128)(2,1)S(1)}, u32[]{:S(2)}, u32[]{:S(2)}) collective-permute-start(bf16[1,320,128]{2,1,0:T(8,128)(2,1)S(1)} %get-tuple-element.39), channel_id=1, source_target_pairs={{0,12},{1,13},{2,14},{3,15},{4,8},{5,9},{6,10},{7,11},{8,4},{9,5},... | collective-permute-start | bytes 245768 | tf_op jit(solution)/shard_map/ppermute | solution.py:203
  31.9 5.8 %collective-permute-done.3.refs_1_ = bf16[1,320,128]{2,1,0:T(8,128)(2,1)S(1)} collective-permute-done((bf16[1,320,128]{2,1,0:T(8,128)(2,1)S(1)}, bf16[1,320,128]{2,1,0:T(8,128)(2,1)S(1)}, u32[]{:S(2)}, u32[]{:S(2)}) %collective-permute-start.3) | collective-permute-done | bytes 81952 | tf_op jit(solution)/shard_map/ppermute | solution.py:203
  37.7 3.0 %collective-permute-start.7 = (bf16[1,320,128]{2,1,0:T(8,128)(2,1)S(1)}, bf16[1,320,128]{2,1,0:T(8,128)(2,1)S(1)}, u32[]{:S(2)}, u32[]{:S(2)}) collective-permute-start(bf16[1,320,128]{2,1,0:T(8,128)(2,1)S(1)} %total.2.refs_0_), channel_id=1, source_target_pairs={{0,8},{1,9},{2,10},{3,11},{4,12},{5,13},{6,14},{7,15},{8,0},{9,1},... | collective-permute-start | bytes 245768 | tf_op jit(solution)/shard_map/ppermute | solution.py:203
  40.7 0.1 collective-permute-start.8
  40.8 2.0 %collective-permute-start.9 = (bf16[1,320,128]{2,1,0:T(8,128)(2,1)S(1)}, bf16[1,320,128]{2,1,0:T(8,128)(2,1)S(1)}, u32[]{:S(2)}, u32[]{:S(2)}) collective-permute-start(bf16[1,320,128]{2,1,0:T(8,128)(2,1)S(1)} %total.2.refs_0_), channel_id=1, source_target_pairs={{0,12},{1,13},{2,14},{3,15},{4,8},{5,9},{6,10},{7,11},{8,4},{9,5},... | collective-permute-start | bytes 245768 | tf_op jit(solution)/shard_map/ppermute | solution.py:203
  42.8 3.1 %pad_maximum_fusion = bf16[16,8,64,128]{3,2,1,0:T(8,128)(2,1)} fusion(bf16[16,4,64,128]{3,2,1,0:T(8,128)(2,1)} %bitcast.9, bf16[16,4,64,128]{3,2,1,0:T(8,128)(2,1)} %bitcast.10), kind=kLoop, calls=%fused_computation | loop fusion | flops 1048576 | bytes 4194304 | tf_op jit(solution)/shard_map/concatenate | solution.py:288
  45.9 1.7 %collective-permute-done.9.refs_3_ = bf16[1,320,128]{2,1,0:T(8,128)(2,1)S(1)} collective-permute-done((bf16[1,320,128]{2,1,0:T(8,128)(2,1)S(1)}, bf16[1,320,128]{2,1,0:T(8,128)(2,1)S(1)}, u32[]{:S(2)}, u32[]{:S(2)}) %collective-permute-start.9) | collective-permute-done | bytes 81952 | tf_op jit(solution)/shard_map/ppermute | solution.py:203
  47.7 5.9 %all-to-all-start.1 = ((bf16[16,8,64,128]{3,2,1,0:T(8,128)(2,1)}), bf16[16,8,64,128]{3,2,1,0:T(8,128)(2,1)S(1)}, u32[]{:S(2)}, u32[]{:S(2)}) async-start(bf16[16,8,64,128]{3,2,1,0:T(8,128)(2,1)} %pad_maximum_fusion), calls=%async_computation.1 | async-start | bytes 4194304 | tf_op jit(solution)/shard_map/all_to_all | solution.py:206
  53.5 1.5 collective-permute-start.10
  55.0 24.3 %collective-permute-done.10.refs_1_ = bf16[4,320,128]{2,1,0:T(8,128)(2,1)S(1)} collective-permute-done((bf16[4,320,128]{2,1,0:T(8,128)(2,1)S(1)}, bf16[4,320,128]{2,1,0:T(8,128)(2,1)S(1)}, u32[]{:S(2)}, u32[]{:S(2)}) %collective-permute-start.10) | collective-permute-done | bytes 327712 | tf_op jit(solution)/shard_map/ppermute | solution.py:203
  79.3 1.3 collective-permute-start.11
  80.6 1.7 %collective-permute-done.11.refs_1_ = bf16[8,320,128]{2,1,0:T(8,128)(2,1)S(1)} collective-permute-done((bf16[8,320,128]{2,1,0:T(8,128)(2,1)S(1)}, bf16[8,320,128]{2,1,0:T(8,128)(2,1)S(1)}, u32[]{:S(2)}, u32[]{:S(2)}) %collective-permute-start.11) | collective-permute-done | bytes 655392 | tf_op jit(solution)/shard_map/ppermute | solution.py:203
  82.4 0.9 low_rank.1.refs_0_
  83.2 0.1 split.4
  83.3 0.1 collective-permute-start.12
  83.4 7.4 %collective-permute-done.12.refs_1_ = bf16[2,256,128]{2,1,0:T(8,128)(2,1)S(1)} collective-permute-done((bf16[2,256,128]{2,1,0:T(8,128)(2,1)S(1)}, bf16[2,256,128]{2,1,0:T(8,128)(2,1)S(1)}, u32[]{:S(2)}, u32[]{:S(2)}) %collective-permute-start.12) | collective-permute-done | bytes 131104 | tf_op jit(solution)/shard_map/ppermute | solution.py:203
  90.9 3.9 %collective-permute-start.13 = (bf16[1,256,128]{2,1,0:T(8,128)(2,1)S(1)}, bf16[1,256,128]{2,1,0:T(8,128)(2,1)S(1)}, u32[]{:S(2)}, u32[]{:S(2)}) collective-permute-start(bf16[1,256,128]{2,1,0:T(8,128)(2,1)S(1)} %get-tuple-element.47), channel_id=1, source_target_pairs={{0,8},{1,9},{2,10},{3,11},{4,12},{5,13},{6,14},{7,15},{8,0},{9,1},... | collective-permute-start | bytes 196616 | tf_op jit(solution)/shard_map/ppermute | solution.py:203
  94.8 1.2 collective-permute-start.14
  95.9 1.3 collective-permute-start.15
  97.2 0.3 collective-permute-start.16
  97.6 0.9 collective-permute-done.15.refs_2_
  98.5 1.9 %collective-permute-done.16.refs_3_ = bf16[2,32,128]{2,1,0:T(8,128)(2,1)S(1)} collective-permute-done((bf16[2,32,128]{2,1,0:T(8,128)(2,1)S(1)}, bf16[2,32,128]{2,1,0:T(8,128)(2,1)S(1)}, u32[]{:S(2)}, u32[]{:S(2)}) %collective-permute-start.16) | collective-permute-done | bytes 16416 | tf_op jit(solution)/shard_map/ppermute | solution.py:203
  100.4 0.6 copy-done.9
  101.0 1.4 choose.1
  102.4 1.1 collective-permute-start.18
  103.6 2.4 %collective-permute-start.19 = (bf16[4,32,128]{2,1,0:T(8,128)(2,1)}, bf16[4,32,128]{2,1,0:T(8,128)(2,1)S(1)}, u32[]{:S(2)}, u32[]{:S(2)}) collective-permute-start(bf16[4,32,128]{2,1,0:T(8,128)(2,1)} %get-tuple-element.52), channel_id=1, source_target_pairs={{0,12},{1,13},{2,14},{3,15},{4,8},{5,9},{6,10},{7,11},{8,4},{9,5},... | collective-permute-start | bytes 98312 | tf_op jit(solution)/shard_map/ppermute | solution.py:203
  106.0 0.5 collective-permute-done.18.refs_2_
  106.5 2.1 %collective-permute-done.19.refs_3_ = bf16[4,32,128]{2,1,0:T(8,128)(2,1)S(1)} collective-permute-done((bf16[4,32,128]{2,1,0:T(8,128)(2,1)}, bf16[4,32,128]{2,1,0:T(8,128)(2,1)S(1)}, u32[]{:S(2)}, u32[]{:S(2)}) %collective-permute-start.19) | collective-permute-done | bytes 32800 | tf_op jit(solution)/shard_map/ppermute | solution.py:203
  108.6 0.8 copy-done.6
  109.3 8.1 %attend.1 = bf16[16,4,64,128]{3,2,1,0:T(8,128)(2,1)S(1)} custom-call(s32[1]{0:T(128)} %bitcast.me_ref, bf16[4,64,128]{2,1,0:T(8,128)(2,1)S(1)} %bitcast.6, bf16[16,8,64,128]{3,2,1,0:T(8,128)(2,1)S(1)} %all-to-all-done.1.q_ref.v_ref, bf16[16,4,64,128]{3,2,1,0:T(8,128)(2,1)} %all-to-all-done.k_ref, bf16[16,8,64,128]{3,2,1,0:T(8,128)(2,1)S(1)} %all-to-all-done.1.q_ref.v_ref, ...), custom_call_target="tpu_custom_call" | custom-call | flops 2147483648 | bytes 4194304 | tf_op jit(solution)/shard_map/attend/pallas_call | solution.py:345
  117.4 31.4 %all_to_all.15 = bf16[16,4,64,128]{3,2,1,0:T(8,128)(2,1)S(1)} all-to-all(bf16[16,4,64,128]{3,2,1,0:T(8,128)(2,1)S(1)} %attend.1), channel_id=1, replica_groups=mesh['grp'=2,'seq'=16] {'seq'}, dimensions={0} | all-to-all | bytes 2097152 | tf_op jit(solution)/shard_map/all_to_all | solution.py:206
  148.8 1.0 copy.10
  (32 shorter events, 0.2 us)
Async XLA Ops:
  0.0 7.5 %copy-start.4 = (s32[64]{0:T(128)S(1)}, s32[64]{0:T(128)}, u32[]{:S(2)}) copy-start(s32[64]{0:T(128)} %row_ref.1) | copy-start | bytes 772
  0.0 7.5 %copy-start.5 = (s32[2]{0:T(128)S(1)}, s32[2]{0:T(128)}, u32[]{:S(2)}) copy-start(s32[2]{0:T(128)} %req_ref.1) | copy-start | bytes 28
  0.0 7.5 %copy-start.1 = (bf16[4,64,4096]{2,1,0:T(8,128)(2,1)S(1)}, bf16[4,64,4096]{2,1,0:T(8,128)(2,1)}, u32[]{:S(2)}) copy-start(bf16[4,64,4096]{2,1,0:T(8,128)(2,1)} %up_ref.1) | copy-start | bytes 6291460
  0.0 37.7 %all-to-all-start = ((bf16[16,4,64,128]{3,2,1,0:T(8,128)(2,1)}), bf16[16,4,64,128]{3,2,1,0:T(8,128)(2,1)}, u32[]{:S(2)}, u32[]{:S(2)}) async-start(bf16[16,4,64,128]{3,2,1,0:T(8,128)(2,1)} %bitcast.8), calls=%async_computation | async-start | bytes 2097152 | tf_op jit(solution)/shard_map/all_to_all | solution.py:206
  7.5 1.7 %copy-start = (bf16[4,64,5120]{2,1,0:T(8,128)(2,1)S(1)}, bf16[4,64,5120]{2,1,0:T(8,128)(2,1)}, u32[]{:S(2)}) copy-start(bf16[4,64,5120]{2,1,0:T(8,128)(2,1)} %down_ref.1) | copy-start | bytes 7864324
  10.8 2.2 %collective-permute-start = (bf16[8,320,128]{2,1,0:T(8,128)(2,1)S(1)}, bf16[8,320,128]{2,1,0:T(8,128)(2,1)S(1)}, u32[]{:S(2)}, u32[]{:S(2)}) collective-permute-start(bf16[8,320,128]{2,1,0:T(8,128)(2,1)S(1)} %get-tuple-element.33), channel_id=1, source_target_pairs={{0,1},{1,0},{2,3},{3,2},{4,5},{5,4},{6,7},{7,6},{8,9},{9,8},{10,11... | collective-permute-start | bytes 1966088 | tf_op jit(solution)/shard_map/ppermute | solution.py:203
  13.0 2.0 %collective-permute-start.1 = (bf16[8,256,128]{2,1,0:T(8,128)(2,1)S(1)}, bf16[8,256,128]{2,1,0:T(8,128)(2,1)S(1)}, u32[]{:S(2)}, u32[]{:S(2)}) collective-permute-start(bf16[8,256,128]{2,1,0:T(8,128)(2,1)S(1)} %get-tuple-element.34), channel_id=1, source_target_pairs={{0,1},{1,0},{2,3},{3,2},{4,5},{5,4},{6,7},{7,6},{8,9},{9,8},{10,11... | collective-permute-start | bytes 1572872 | tf_op jit(solution)/shard_map/ppermute | solution.py:203
  13.3 13.6 %collective-permute-start.2 = (bf16[4,320,128]{2,1,0:T(8,128)(2,1)S(1)}, bf16[4,320,128]{2,1,0:T(8,128)(2,1)S(1)}, u32[]{:S(2)}, u32[]{:S(2)}) collective-permute-start(bf16[4,320,128]{2,1,0:T(8,128)(2,1)S(1)} %halve.2), channel_id=1, source_target_pairs={{0,2},{1,3},{2,0},{3,1},{4,6},{5,7},{6,4},{7,5},{8,10},{9,11},{10,... | collective-permute-start | bytes 983048 | tf_op jit(solution)/shard_map/ppermute | solution.py:203
  15.1 22.7 %collective-permute-start.6 = (bf16[4,256,128]{2,1,0:T(8,128)(2,1)S(1)}, bf16[4,256,128]{2,1,0:T(8,128)(2,1)S(1)}, u32[]{:S(2)}, u32[]{:S(2)}) collective-permute-start(bf16[4,256,128]{2,1,0:T(8,128)(2,1)S(1)} %halve.3), channel_id=1, source_target_pairs={{0,2},{1,3},{2,0},{3,1},{4,6},{5,7},{6,4},{7,5},{8,10},{9,11},{10,... | collective-permute-start | bytes 786440 | tf_op jit(solution)/shard_map/ppermute | solution.py:203
  27.0 10.7 %collective-permute-start.3 = (bf16[1,320,128]{2,1,0:T(8,128)(2,1)S(1)}, bf16[1,320,128]{2,1,0:T(8,128)(2,1)S(1)}, u32[]{:S(2)}, u32[]{:S(2)}) collective-permute-start(bf16[1,320,128]{2,1,0:T(8,128)(2,1)S(1)} %get-tuple-element.37), channel_id=1, source_target_pairs={{0,8},{1,9},{2,10},{3,11},{4,12},{5,13},{6,14},{7,15},{8,0},{9,1},... | collective-permute-start | bytes 245768 | tf_op jit(solution)/shard_map/ppermute | solution.py:203
  30.2 7.5 %collective-permute-start.4 = (bf16[1,320,128]{2,1,0:T(8,128)(2,1)S(1)}, bf16[1,320,128]{2,1,0:T(8,128)(2,1)S(1)}, u32[]{:S(2)}, u32[]{:S(2)}) collective-permute-start(bf16[1,320,128]{2,1,0:T(8,128)(2,1)S(1)} %get-tuple-element.38), channel_id=1, source_target_pairs={{0,4},{1,5},{2,6},{3,7},{4,0},{5,1},{6,2},{7,3},{8,12},{9,13},{10,... | collective-permute-start | bytes 245768 | tf_op jit(solution)/shard_map/ppermute | solution.py:203
  30.2 7.4 %collective-permute-start.5 = (bf16[1,320,128]{2,1,0:T(8,128)(2,1)S(1)}, bf16[1,320,128]{2,1,0:T(8,128)(2,1)S(1)}, u32[]{:S(2)}, u32[]{:S(2)}) collective-permute-start(bf16[1,320,128]{2,1,0:T(8,128)(2,1)S(1)} %get-tuple-element.39), channel_id=1, source_target_pairs={{0,12},{1,13},{2,14},{3,15},{4,8},{5,9},{6,10},{7,11},{8,4},{9,5},... | collective-permute-start | bytes 245768 | tf_op jit(solution)/shard_map/ppermute | solution.py:203
  37.7 8.1 %collective-permute-start.7 = (bf16[1,320,128]{2,1,0:T(8,128)(2,1)S(1)}, bf16[1,320,128]{2,1,0:T(8,128)(2,1)S(1)}, u32[]{:S(2)}, u32[]{:S(2)}) collective-permute-start(bf16[1,320,128]{2,1,0:T(8,128)(2,1)S(1)} %total.2.refs_0_), channel_id=1, source_target_pairs={{0,8},{1,9},{2,10},{3,11},{4,12},{5,13},{6,14},{7,15},{8,0},{9,1},... | collective-permute-start | bytes 245768 | tf_op jit(solution)/shard_map/ppermute | solution.py:203
  40.7 5.2 %collective-permute-start.8 = (bf16[1,320,128]{2,1,0:T(8,128)(2,1)S(1)}, bf16[1,320,128]{2,1,0:T(8,128)(2,1)S(1)}, u32[]{:S(2)}, u32[]{:S(2)}) collective-permute-start(bf16[1,320,128]{2,1,0:T(8,128)(2,1)S(1)} %total.2.refs_0_), channel_id=1, source_target_pairs={{0,4},{1,5},{2,6},{3,7},{4,0},{5,1},{6,2},{7,3},{8,12},{9,13},{10,... | collective-permute-start | bytes 245768 | tf_op jit(solution)/shard_map/ppermute | solution.py:203
  40.8 6.8 %collective-permute-start.9 = (bf16[1,320,128]{2,1,0:T(8,128)(2,1)S(1)}, bf16[1,320,128]{2,1,0:T(8,128)(2,1)S(1)}, u32[]{:S(2)}, u32[]{:S(2)}) collective-permute-start(bf16[1,320,128]{2,1,0:T(8,128)(2,1)S(1)} %total.2.refs_0_), channel_id=1, source_target_pairs={{0,12},{1,13},{2,14},{3,15},{4,8},{5,9},{6,10},{7,11},{8,4},{9,5},... | collective-permute-start | bytes 245768 | tf_op jit(solution)/shard_map/ppermute | solution.py:203
  47.7 60.9 %all-to-all-start.1 = ((bf16[16,8,64,128]{3,2,1,0:T(8,128)(2,1)}), bf16[16,8,64,128]{3,2,1,0:T(8,128)(2,1)S(1)}, u32[]{:S(2)}, u32[]{:S(2)}) async-start(bf16[16,8,64,128]{3,2,1,0:T(8,128)(2,1)} %pad_maximum_fusion), calls=%async_computation.1 | async-start | bytes 4194304 | tf_op jit(solution)/shard_map/all_to_all | solution.py:206
  53.5 28.8 %copy-start.2 = (bf16[2,64,5120]{2,1,0:T(8,128)(2,1)S(1)}, bf16[2,64,5120]{2,1,0:T(8,128)(2,1)}, u32[]{:S(2)}) copy-start(bf16[2,64,5120]{2,1,0:T(8,128)(2,1)} %x_ref.1) | copy-start | bytes 3932164
  53.5 25.8 %collective-permute-start.10 = (bf16[4,320,128]{2,1,0:T(8,128)(2,1)S(1)}, bf16[4,320,128]{2,1,0:T(8,128)(2,1)S(1)}, u32[]{:S(2)}, u32[]{:S(2)}) collective-permute-start(bf16[4,320,128]{2,1,0:T(8,128)(2,1)S(1)} %join.2.refs_0_), channel_id=1, source_target_pairs={{0,2},{1,3},{2,0},{3,1},{4,6},{5,7},{6,4},{7,5},{8,10},{9,11},{10,... | collective-permute-start | bytes 983048 | tf_op jit(solution)/shard_map/ppermute | solution.py:203
  79.3 3.0 %collective-permute-start.11 = (bf16[8,320,128]{2,1,0:T(8,128)(2,1)S(1)}, bf16[8,320,128]{2,1,0:T(8,128)(2,1)S(1)}, u32[]{:S(2)}, u32[]{:S(2)}) collective-permute-start(bf16[8,320,128]{2,1,0:T(8,128)(2,1)S(1)} %join.3.refs_0_), channel_id=1, source_target_pairs={{0,1},{1,0},{2,3},{3,2},{4,5},{5,4},{6,7},{7,6},{8,9},{9,8},{10,11... | collective-permute-start | bytes 1966088 | tf_op jit(solution)/shard_map/ppermute | solution.py:203
  83.2 17.2 %copy-start.3 = (bf16[2,32,128]{2,1,0:T(8,128)(2,1)}, bf16[2,32,128]{2,1,0:T(8,128)(2,1)S(1)}, u32[]{:S(2)}) copy-start(bf16[2,32,128]{2,1,0:T(8,128)(2,1)S(1)} %low_rank.1.refs_0_) | copy-start | bytes 49156
  83.3 7.5 %collective-permute-start.12 = (bf16[2,256,128]{2,1,0:T(8,128)(2,1)S(1)}, bf16[2,256,128]{2,1,0:T(8,128)(2,1)S(1)}, u32[]{:S(2)}, u32[]{:S(2)}) collective-permute-start(bf16[2,256,128]{2,1,0:T(8,128)(2,1)S(1)} %get-tuple-element.45), channel_id=1, source_target_pairs={{0,4},{1,5},{2,6},{3,7},{4,0},{5,1},{6,2},{7,3},{8,12},{9,13},{10,... | collective-permute-start | bytes 393224 | tf_op jit(solution)/shard_map/ppermute | solution.py:203
  90.9 15.1 %collective-permute-start.13 = (bf16[1,256,128]{2,1,0:T(8,128)(2,1)S(1)}, bf16[1,256,128]{2,1,0:T(8,128)(2,1)S(1)}, u32[]{:S(2)}, u32[]{:S(2)}) collective-permute-start(bf16[1,256,128]{2,1,0:T(8,128)(2,1)S(1)} %get-tuple-element.47), channel_id=1, source_target_pairs={{0,8},{1,9},{2,10},{3,11},{4,12},{5,13},{6,14},{7,15},{8,0},{9,1},... | collective-permute-start | bytes 196616 | tf_op jit(solution)/shard_map/ppermute | solution.py:203
  94.8 2.8 %collective-permute-start.14 = (bf16[2,32,128]{2,1,0:T(8,128)(2,1)S(1)}, bf16[2,32,128]{2,1,0:T(8,128)(2,1)S(1)}, u32[]{:S(2)}, u32[]{:S(2)}) collective-permute-start(bf16[2,32,128]{2,1,0:T(8,128)(2,1)S(1)} %low_rank.1.refs_0_), channel_id=1, source_target_pairs={{0,1},{1,0},{2,3},{3,2},{4,5},{5,4},{6,7},{7,6},{8,9},{9,8},{10,11... | collective-permute-start | bytes 49160 | tf_op jit(solution)/shard_map/ppermute | solution.py:203
  95.9 2.6 %collective-permute-start.15 = (bf16[2,32,128]{2,1,0:T(8,128)(2,1)S(1)}, bf16[2,32,128]{2,1,0:T(8,128)(2,1)S(1)}, u32[]{:S(2)}, u32[]{:S(2)}) collective-permute-start(bf16[2,32,128]{2,1,0:T(8,128)(2,1)S(1)} %low_rank.1.refs_0_), channel_id=1, source_target_pairs={{0,2},{1,3},{2,0},{3,1},{4,6},{5,7},{6,4},{7,5},{8,10},{9,11},{10,... | collective-permute-start | bytes 49160 | tf_op jit(solution)/shard_map/ppermute | solution.py:203
  97.2 3.2 %collective-permute-start.16 = (bf16[2,32,128]{2,1,0:T(8,128)(2,1)S(1)}, bf16[2,32,128]{2,1,0:T(8,128)(2,1)S(1)}, u32[]{:S(2)}, u32[]{:S(2)}) collective-permute-start(bf16[2,32,128]{2,1,0:T(8,128)(2,1)S(1)} %low_rank.1.refs_0_), channel_id=1, source_target_pairs={{0,3},{1,2},{2,1},{3,0},{4,7},{5,6},{6,5},{7,4},{8,11},{9,10},{10,... | collective-permute-start | bytes 49160 | tf_op jit(solution)/shard_map/ppermute | solution.py:203
  97.6 2.9 %copy-start.7 = (bf16[2,32,128]{2,1,0:T(8,128)(2,1)}, bf16[2,32,128]{2,1,0:T(8,128)(2,1)S(1)}, u32[]{:S(2)}) copy-start(bf16[2,32,128]{2,1,0:T(8,128)(2,1)S(1)} %collective-permute-done.14.refs_1_) | copy-start | bytes 49156
  98.5 1.9 %copy-start.8 = (bf16[2,32,128]{2,1,0:T(8,128)(2,1)}, bf16[2,32,128]{2,1,0:T(8,128)(2,1)S(1)}, u32[]{:S(2)}) copy-start(bf16[2,32,128]{2,1,0:T(8,128)(2,1)S(1)} %collective-permute-done.15.refs_2_) | copy-start | bytes 49156
  100.4 0.6 copy-start.9
  102.4 3.6 %collective-permute-start.17 = (bf16[4,32,128]{2,1,0:T(8,128)(2,1)}, bf16[4,32,128]{2,1,0:T(8,128)(2,1)S(1)}, u32[]{:S(2)}, u32[]{:S(2)}) collective-permute-start(bf16[4,32,128]{2,1,0:T(8,128)(2,1)} %get-tuple-element.50), channel_id=1, source_target_pairs={{0,4},{1,5},{2,6},{3,7},{4,0},{5,1},{6,2},{7,3},{8,12},{9,13},{10,... | collective-permute-start | bytes 98312 | tf_op jit(solution)/shard_map/ppermute | solution.py:203
  102.4 4.0 %collective-permute-start.18 = (bf16[4,32,128]{2,1,0:T(8,128)(2,1)}, bf16[4,32,128]{2,1,0:T(8,128)(2,1)S(1)}, u32[]{:S(2)}, u32[]{:S(2)}) collective-permute-start(bf16[4,32,128]{2,1,0:T(8,128)(2,1)} %get-tuple-element.51), channel_id=1, source_target_pairs={{0,8},{1,9},{2,10},{3,11},{4,12},{5,13},{6,14},{7,15},{8,0},{9,1},... | collective-permute-start | bytes 98312 | tf_op jit(solution)/shard_map/ppermute | solution.py:203
  103.6 5.0 %collective-permute-start.19 = (bf16[4,32,128]{2,1,0:T(8,128)(2,1)}, bf16[4,32,128]{2,1,0:T(8,128)(2,1)S(1)}, u32[]{:S(2)}, u32[]{:S(2)}) collective-permute-start(bf16[4,32,128]{2,1,0:T(8,128)(2,1)} %get-tuple-element.52), channel_id=1, source_target_pairs={{0,12},{1,13},{2,14},{3,15},{4,8},{5,9},{6,10},{7,11},{8,4},{9,5},... | collective-permute-start | bytes 98312 | tf_op jit(solution)/shard_map/ppermute | solution.py:203
  108.6 0.8 copy-start.6

commit v25 on v24

--- a/solution.py
+++ b/solution.py
@@ -307,7 +307,16 @@
         ),
         name="low_rank",
     )(me, normed_token_features, *gathered)
-    up_part = after(up_pieces[-1], low)
+    nearby = [low] + [swap(low, k) for k in range(1, LOW)]
+    chosen = pl.pallas_call(
+        functools.partial(choose_kernel, per_video),
+        in_specs=[SMEM] + [VMEM] * LOW,
+        out_specs=[VMEM] * quarter,
+        out_shape=[jax.ShapeDtypeStruct((LOW,) + low_shape[1:], jnp.bfloat16)] * quarter,
+        cost_estimate=pl.CostEstimate(flops=0, bytes_accessed=8 * low.size, transcendentals=0),
+        name="choose",
+    )(me, *nearby)
+    up_part = after(up_pieces[-1], chosen[0])
     near_pair, far_pair = on_vmem(
         functools.partial(sum_kernel, [[(n, 2 * h) for n in range(1 + len(up_got))] for h in (0, 1)]),
         [(2,) + up_part.shape[1:]] * 2,
@@ -328,15 +337,6 @@
     up_here = on_vmem(
         functools.partial(sum_kernel, [[(0, 0), (1, 0)]]), [one_shape], "total", kept, last
     )[0].reshape(pairs, ranks, LANES)
-    nearby = [low] + [swap(low, k) for k in range(1, LOW)]
-    chosen = pl.pallas_call(
-        functools.partial(choose_kernel, per_video),
-        in_specs=[SMEM] + [VMEM] * LOW,
-        out_specs=[VMEM] * quarter,
-        out_shape=[jax.ShapeDtypeStruct((LOW,) + low_shape[1:], jnp.bfloat16)] * quarter,
-        cost_estimate=pl.CostEstimate(flops=0, bytes_accessed=8 * low.size, transcendentals=0),
-        name="choose",
-    )(me, *nearby)
     lows = [chosen[0]] + [swap(chosen[i], LOW * i) for i in range(1, quarter)]
 
     part_spec = pl.BlockSpec((devs, pl.squeezed, toks, width), lambda p: (0, p, 0, 0))

time: 150 us -> 152 us (1.013)
  starting transfers between devices: 39.9 us -> 35.6 us
  waiting for transfers between devices: 58.9 us -> 62.7 us
  blocking collectives: 31.4 us -> 34.9 us
  other arithmetic: 3.09 us -> 1.54 us
    ppermute x20, starting transfers between devices: 26.5 us -> 22.2 us  [swap(): return lax.ppermute(tensor, 'seq', [(i, i ^ k) for i in range(devs)])]
    ppermute x20, waiting for transfers between devices: 58.9 us -> 62.7 us  [swap(): return lax.ppermute(tensor, 'seq', [(i, i ^ k) for i in range(devs)])]
    all_to_all x1, blocking collectives: 31.4 us -> 34.9 us  [exchange(): lax.all_to_all(tensor, 'seq', split_axis=0, concat_axis=0, tiled=True)]
    concatenate x1, other arithmetic: 3.09 us -> 1.54 us  [body(): asked = jnp.concatenate([by_pairs(values), by_pairs(queries)], axis=1)]
    unnamed x21 -> x25, local copies, waits for them, and re-layouts: 4.08 us -> 4.09 us
  transfers between devices with their start and end apart: 22 -> 22, of which waited for: 12 -> 13; matrix products, arithmetic and copies ran while one was open for 2% -> 1% of each run, Pallas kernels for 3% -> 3%
where the time goes in v25:
time: 152 us; the launch traced here: 151 us
  waiting for transfers between devices  62.7 us (41%)
  starting transfers between devices  35.6 us (23%)
  blocking collectives  34.9 us (23%)
  Pallas kernels  12.3 us (8%)
  local copies, waits for them, and re-layouts  4.09 us (3%)
  other arithmetic  1.54 us (1%)
    ppermute x20, waiting for transfers between devices, swap(): return lax.ppermute(tensor, 'seq', [(i, i ^ k) for i in range(devs)])  62.7 us
    all_to_all x1, blocking collectives, exchange(): lax.all_to_all(tensor, 'seq', split_axis=0, concat_axis=0, tiled=True)  34.9 us
    ppermute x20, starting transfers between devices, swap(): return lax.ppermute(tensor, 'seq', [(i, i ^ k) for i in range(devs)])  22.2 us
    all_to_all x2, starting transfers between devices, exchange(): lax.all_to_all(tensor, 'seq', split_axis=0, concat_axis=0, tiled=True)  13.4 us
    pallas_call x1, Pallas kernels, body(): pl.pallas_call(functools.partial(attend_kernel, math.gcd(devs, max(1, 256...  8.06 us
    unnamed x25, local copies, waits for them, and re-layouts  4.09 us
  transfers between devices with their start and end apart: 22, of which 13 were waited for; matrix products, arithmetic and copies ran while one was open for 1% of the time, Pallas kernels for 3%

profile of v25, /device:TPU:1, one launch (start us, length us, event | category | flops | bytes accessed | tf_op | source)
XLA Modules:
  0.0 151.3 jit_solution(5417257813037018875)
XLA Ops:
  0.0 7.5 %all-to-all-start = ((bf16[16,4,64,128]{3,2,1,0:T(8,128)(2,1)}), bf16[16,4,64,128]{3,2,1,0:T(8,128)(2,1)}, u32[]{:S(2)}, u32[]{:S(2)}) async-start(bf16[16,4,64,128]{3,2,1,0:T(8,128)(2,1)} %bitcast.8), calls=%async_computation | async-start | bytes 2097152 | tf_op jit(solution)/shard_map/all_to_all | solution.py:206
  7.5 1.7 %copy-done = bf16[4,64,5120]{2,1,0:T(8,128)(2,1)S(1)} copy-done((bf16[4,64,5120]{2,1,0:T(8,128)(2,1)S(1)}, bf16[4,64,5120]{2,1,0:T(8,128)(2,1)}, u32[]{:S(2)}) %copy-start) | copy-done | bytes 2621464
  9.3 1.5 pick_factors.1
  10.8 0.2 collective-permute-start
  11.0 1.9 %collective-permute-done.refs_1_ = bf16[8,320,128]{2,1,0:T(8,128)(2,1)S(1)} collective-permute-done((bf16[8,320,128]{2,1,0:T(8,128)(2,1)S(1)}, bf16[8,320,128]{2,1,0:T(8,128)(2,1)S(1)}, u32[]{:S(2)}, u32[]{:S(2)}) %collective-permute-start) | collective-permute-done | bytes 655392 | tf_op jit(solution)/shard_map/ppermute | solution.py:203
  13.0 0.1 halve.2
  13.1 0.2 collective-permute-start.1
  13.3 1.6 %collective-permute-start.2 = (bf16[4,320,128]{2,1,0:T(8,128)(2,1)S(1)}, bf16[4,320,128]{2,1,0:T(8,128)(2,1)S(1)}, u32[]{:S(2)}, u32[]{:S(2)}) collective-permute-start(bf16[4,320,128]{2,1,0:T(8,128)(2,1)S(1)} %halve.2), channel_id=1, source_target_pairs={{0,2},{1,3},{2,0},{3,1},{4,6},{5,7},{6,4},{7,5},{8,10},{9,11},{10,... | collective-permute-start | bytes 983048 | tf_op jit(solution)/shard_map/ppermute | solution.py:203
  14.9 0.2 collective-permute-done.1.refs_1_
  15.0 0.1 halve.3
  15.1 1.5 collective-permute-start.6
  16.5 10.3 %collective-permute-done.2.refs_2_ = bf16[4,320,128]{2,1,0:T(8,128)(2,1)S(1)} collective-permute-done((bf16[4,320,128]{2,1,0:T(8,128)(2,1)S(1)}, bf16[4,320,128]{2,1,0:T(8,128)(2,1)S(1)}, u32[]{:S(2)}, u32[]{:S(2)}) %collective-permute-start.2) | collective-permute-done | bytes 327712 | tf_op jit(solution)/shard_map/ppermute | solution.py:203
  26.9 0.1 split.3
  27.0 3.2 %collective-permute-start.3 = (bf16[1,320,128]{2,1,0:T(8,128)(2,1)S(1)}, bf16[1,320,128]{2,1,0:T(8,128)(2,1)S(1)}, u32[]{:S(2)}, u32[]{:S(2)}) collective-permute-start(bf16[1,320,128]{2,1,0:T(8,128)(2,1)S(1)} %get-tuple-element.37), channel_id=1, source_target_pairs={{0,8},{1,9},{2,10},{3,11},{4,12},{5,13},{6,14},{7,15},{8,0},{9,1},... | collective-permute-start | bytes 245768 | tf_op jit(solution)/shard_map/ppermute | solution.py:203
  30.2 0.0 collective-permute-start.4
  30.2 1.7 %collective-permute-start.5 = (bf16[1,320,128]{2,1,0:T(8,128)(2,1)S(1)}, bf16[1,320,128]{2,1,0:T(8,128)(2,1)S(1)}, u32[]{:S(2)}, u32[]{:S(2)}) collective-permute-start(bf16[1,320,128]{2,1,0:T(8,128)(2,1)S(1)} %get-tuple-element.39), channel_id=1, source_target_pairs={{0,12},{1,13},{2,14},{3,15},{4,8},{5,9},{6,10},{7,11},{8,4},{9,5},... | collective-permute-start | bytes 245768 | tf_op jit(solution)/shard_map/ppermute | solution.py:203
  31.9 5.7 %collective-permute-done.3.refs_1_ = bf16[1,320,128]{2,1,0:T(8,128)(2,1)S(1)} collective-permute-done((bf16[1,320,128]{2,1,0:T(8,128)(2,1)S(1)}, bf16[1,320,128]{2,1,0:T(8,128)(2,1)S(1)}, u32[]{:S(2)}, u32[]{:S(2)}) %collective-permute-start.3) | collective-permute-done | bytes 81952 | tf_op jit(solution)/shard_map/ppermute | solution.py:203
  37.7 3.0 %collective-permute-start.7 = (bf16[1,320,128]{2,1,0:T(8,128)(2,1)S(1)}, bf16[1,320,128]{2,1,0:T(8,128)(2,1)S(1)}, u32[]{:S(2)}, u32[]{:S(2)}) collective-permute-start(bf16[1,320,128]{2,1,0:T(8,128)(2,1)S(1)} %total.2.refs_0_), channel_id=1, source_target_pairs={{0,8},{1,9},{2,10},{3,11},{4,12},{5,13},{6,14},{7,15},{8,0},{9,1},... | collective-permute-start | bytes 245768 | tf_op jit(solution)/shard_map/ppermute | solution.py:203
  40.7 0.1 collective-permute-start.8
  40.8 2.0 %collective-permute-start.9 = (bf16[1,320,128]{2,1,0:T(8,128)(2,1)S(1)}, bf16[1,320,128]{2,1,0:T(8,128)(2,1)S(1)}, u32[]{:S(2)}, u32[]{:S(2)}) collective-permute-start(bf16[1,320,128]{2,1,0:T(8,128)(2,1)S(1)} %total.2.refs_0_), channel_id=1, source_target_pairs={{0,12},{1,13},{2,14},{3,15},{4,8},{5,9},{6,10},{7,11},{8,4},{9,5},... | collective-permute-start | bytes 245768 | tf_op jit(solution)/shard_map/ppermute | solution.py:203
  42.8 1.5 %pad_maximum_fusion = bf16[16,8,64,128]{3,2,1,0:T(8,128)(2,1)} fusion(bf16[16,4,64,128]{3,2,1,0:T(8,128)(2,1)S(1)} %bitcast.9, bf16[16,4,64,128]{3,2,1,0:T(8,128)(2,1)S(1)} %bitcast.10), kind=kLoop, calls=%fused_computation | loop fusion | flops 1048576 | bytes 4194304 | tf_op jit(solution)/shard_map/concatenate | solution.py:288
  44.3 3.3 %collective-permute-done.9.refs_3_ = bf16[1,320,128]{2,1,0:T(8,128)(2,1)S(1)} collective-permute-done((bf16[1,320,128]{2,1,0:T(8,128)(2,1)S(1)}, bf16[1,320,128]{2,1,0:T(8,128)(2,1)S(1)}, u32[]{:S(2)}, u32[]{:S(2)}) %collective-permute-start.9) | collective-permute-done | bytes 81952 | tf_op jit(solution)/shard_map/ppermute | solution.py:203
  47.7 5.9 %all-to-all-start.1 = ((bf16[16,8,64,128]{3,2,1,0:T(8,128)(2,1)}), bf16[16,8,64,128]{3,2,1,0:T(8,128)(2,1)S(1)}, u32[]{:S(2)}, u32[]{:S(2)}) async-start(bf16[16,8,64,128]{3,2,1,0:T(8,128)(2,1)} %pad_maximum_fusion), calls=%async_computation.1 | async-start | bytes 4194304 | tf_op jit(solution)/shard_map/all_to_all | solution.py:206
  53.5 1.5 collective-permute-start.10
  55.0 24.3 %collective-permute-done.10.refs_1_ = bf16[4,320,128]{2,1,0:T(8,128)(2,1)S(1)} collective-permute-done((bf16[4,320,128]{2,1,0:T(8,128)(2,1)S(1)}, bf16[4,320,128]{2,1,0:T(8,128)(2,1)S(1)}, u32[]{:S(2)}, u32[]{:S(2)}) %collective-permute-start.10) | collective-permute-done | bytes 327712 | tf_op jit(solution)/shard_map/ppermute | solution.py:203
  79.3 1.3 collective-permute-start.11
  80.6 1.7 %collective-permute-done.11.refs_1_ = bf16[8,320,128]{2,1,0:T(8,128)(2,1)S(1)} collective-permute-done((bf16[8,320,128]{2,1,0:T(8,128)(2,1)S(1)}, bf16[8,320,128]{2,1,0:T(8,128)(2,1)S(1)}, u32[]{:S(2)}, u32[]{:S(2)}) %collective-permute-start.11) | collective-permute-done | bytes 655392 | tf_op jit(solution)/shard_map/ppermute | solution.py:203
  82.4 0.9 low_rank.1.refs_0_
  83.2 0.4 collective-permute-start.12
  83.6 1.8 %collective-permute-start.14 = (bf16[2,32,128]{2,1,0:T(8,128)(2,1)S(1)}, bf16[2,32,128]{2,1,0:T(8,128)(2,1)S(1)}, u32[]{:S(2)}, u32[]{:S(2)}) collective-permute-start(bf16[2,32,128]{2,1,0:T(8,128)(2,1)S(1)} %low_rank.1.refs_0_), channel_id=1, source_target_pairs={{0,3},{1,2},{2,1},{3,0},{4,7},{5,6},{6,5},{7,4},{8,11},{9,10},{10,... | collective-permute-start | bytes 49160 | tf_op jit(solution)/shard_map/ppermute | solution.py:203
  85.4 0.8 collective-permute-done.13.refs_2_
  86.2 0.9 collective-permute-done.14.refs_3_
  87.2 0.6 copy-done.11
  87.8 1.4 choose.1
  89.2 0.1 split.4
  89.3 0.1 collective-permute-start.15
  89.3 10.0 %collective-permute-done.15.refs_1_ = bf16[2,256,128]{2,1,0:T(8,128)(2,1)S(1)} collective-permute-done((bf16[2,256,128]{2,1,0:T(8,128)(2,1)S(1)}, bf16[2,256,128]{2,1,0:T(8,128)(2,1)S(1)}, u32[]{:S(2)}, u32[]{:S(2)}) %collective-permute-start.15) | collective-permute-done | bytes 131104 | tf_op jit(solution)/shard_map/ppermute | solution.py:203
  99.4 0.1 collective-permute-start.16
  99.5 0.1 collective-permute-start.17
  99.6 2.3 %collective-permute-start.18 = (bf16[4,32,128]{2,1,0:T(8,128)(2,1)}, bf16[4,32,128]{2,1,0:T(8,128)(2,1)S(1)}, u32[]{:S(2)}, u32[]{:S(2)}) collective-permute-start(bf16[4,32,128]{2,1,0:T(8,128)(2,1)} %get-tuple-element.51), channel_id=1, source_target_pairs={{0,8},{1,9},{2,10},{3,11},{4,12},{5,13},{6,14},{7,15},{8,0},{9,1},... | collective-permute-start | bytes 98312 | tf_op jit(solution)/shard_map/ppermute | solution.py:203
  101.9 1.3 collective-permute-start.19
  103.1 0.4 collective-permute-done.16.refs_1_
  103.5 0.3 collective-permute-done.18.refs_2_
  103.9 2.8 %collective-permute-done.19.refs_3_ = bf16[4,32,128]{2,1,0:T(8,128)(2,1)S(1)} collective-permute-done((bf16[4,32,128]{2,1,0:T(8,128)(2,1)}, bf16[4,32,128]{2,1,0:T(8,128)(2,1)S(1)}, u32[]{:S(2)}, u32[]{:S(2)}) %collective-permute-start.19) | collective-permute-done | bytes 32800 | tf_op jit(solution)/shard_map/ppermute | solution.py:203
  106.6 0.8 copy-done.6
  107.4 8.1 %attend.1 = bf16[16,4,64,128]{3,2,1,0:T(8,128)(2,1)S(1)} custom-call(s32[1]{0:T(128)} %bitcast.me_ref, bf16[4,64,128]{2,1,0:T(8,128)(2,1)S(1)} %bitcast.6, bf16[16,8,64,128]{3,2,1,0:T(8,128)(2,1)S(1)} %all-to-all-done.1.q_ref.v_ref, bf16[16,4,64,128]{3,2,1,0:T(8,128)(2,1)} %all-to-all-done.k_ref, bf16[16,8,64,128]{3,2,1,0:T(8,128)(2,1)S(1)} %all-to-all-done.1.q_ref.v_ref, ...), custom_call_target="tpu_custom_call" | custom-call | flops 2147483648 | bytes 4194304 | tf_op jit(solution)/shard_map/attend/pallas_call | solution.py:345
  115.5 34.9 %all_to_all.15 = bf16[16,4,64,128]{3,2,1,0:T(8,128)(2,1)S(1)} all-to-all(bf16[16,4,64,128]{3,2,1,0:T(8,128)(2,1)S(1)} %attend.1), channel_id=1, replica_groups=mesh['grp'=2,'seq'=16] {'seq'}, dimensions={0} | all-to-all | bytes 2097152 | tf_op jit(solution)/shard_map/all_to_all | solution.py:206
  150.3 1.0 copy.10
  (36 shorter events, 0.2 us)
Async XLA Ops:
  0.0 7.5 %copy-start.1 = (bf16[4,64,4096]{2,1,0:T(8,128)(2,1)S(1)}, bf16[4,64,4096]{2,1,0:T(8,128)(2,1)}, u32[]{:S(2)}) copy-start(bf16[4,64,4096]{2,1,0:T(8,128)(2,1)} %up_ref.1) | copy-start | bytes 6291460
  0.0 7.5 %copy-start.4 = (s32[64]{0:T(128)S(1)}, s32[64]{0:T(128)}, u32[]{:S(2)}) copy-start(s32[64]{0:T(128)} %row_ref.1) | copy-start | bytes 772
  0.0 7.5 %copy-start.5 = (s32[2]{0:T(128)S(1)}, s32[2]{0:T(128)}, u32[]{:S(2)}) copy-start(s32[2]{0:T(128)} %req_ref.1) | copy-start | bytes 28
  0.0 37.7 %all-to-all-start = ((bf16[16,4,64,128]{3,2,1,0:T(8,128)(2,1)}), bf16[16,4,64,128]{3,2,1,0:T(8,128)(2,1)}, u32[]{:S(2)}, u32[]{:S(2)}) async-start(bf16[16,4,64,128]{3,2,1,0:T(8,128)(2,1)} %bitcast.8), calls=%async_computation | async-start | bytes 2097152 | tf_op jit(solution)/shard_map/all_to_all | solution.py:206
  7.5 1.7 %copy-start = (bf16[4,64,5120]{2,1,0:T(8,128)(2,1)S(1)}, bf16[4,64,5120]{2,1,0:T(8,128)(2,1)}, u32[]{:S(2)}) copy-start(bf16[4,64,5120]{2,1,0:T(8,128)(2,1)} %down_ref.1) | copy-start | bytes 7864324
  10.8 32.0 %copy-start.7 = (bf16[2,32,64,128]{3,2,1,0:T(8,128)(2,1)S(1)}, bf16[2,32,64,128]{3,2,1,0:T(8,128)(2,1)}, u32[]{:S(2)}) copy-start(bf16[2,32,64,128]{3,2,1,0:T(8,128)(2,1)} %param.9) | copy-start | bytes 3145732
  10.8 32.0 %copy-start.8 = (bf16[2,32,64,128]{3,2,1,0:T(8,128)(2,1)S(1)}, bf16[2,32,64,128]{3,2,1,0:T(8,128)(2,1)}, u32[]{:S(2)}) copy-start(bf16[2,32,64,128]{3,2,1,0:T(8,128)(2,1)} %param.11) | copy-start | bytes 3145732
  10.8 2.2 %collective-permute-start = (bf16[8,320,128]{2,1,0:T(8,128)(2,1)S(1)}, bf16[8,320,128]{2,1,0:T(8,128)(2,1)S(1)}, u32[]{:S(2)}, u32[]{:S(2)}) collective-permute-start(bf16[8,320,128]{2,1,0:T(8,128)(2,1)S(1)} %get-tuple-element.33), channel_id=1, source_target_pairs={{0,1},{1,0},{2,3},{3,2},{4,5},{5,4},{6,7},{7,6},{8,9},{9,8},{10,11... | collective-permute-start | bytes 1966088 | tf_op jit(solution)/shard_map/ppermute | solution.py:203
  13.1 2.0 %collective-permute-start.1 = (bf16[8,256,128]{2,1,0:T(8,128)(2,1)S(1)}, bf16[8,256,128]{2,1,0:T(8,128)(2,1)S(1)}, u32[]{:S(2)}, u32[]{:S(2)}) collective-permute-start(bf16[8,256,128]{2,1,0:T(8,128)(2,1)S(1)} %get-tuple-element.34), channel_id=1, source_target_pairs={{0,1},{1,0},{2,3},{3,2},{4,5},{5,4},{6,7},{7,6},{8,9},{9,8},{10,11... | collective-permute-start | bytes 1572872 | tf_op jit(solution)/shard_map/ppermute | solution.py:203
  13.3 13.6 %collective-permute-start.2 = (bf16[4,320,128]{2,1,0:T(8,128)(2,1)S(1)}, bf16[4,320,128]{2,1,0:T(8,128)(2,1)S(1)}, u32[]{:S(2)}, u32[]{:S(2)}) collective-permute-start(bf16[4,320,128]{2,1,0:T(8,128)(2,1)S(1)} %halve.2), channel_id=1, source_target_pairs={{0,2},{1,3},{2,0},{3,1},{4,6},{5,7},{6,4},{7,5},{8,10},{9,11},{10,... | collective-permute-start | bytes 983048 | tf_op jit(solution)/shard_map/ppermute | solution.py:203
  15.1 22.6 %collective-permute-start.6 = (bf16[4,256,128]{2,1,0:T(8,128)(2,1)S(1)}, bf16[4,256,128]{2,1,0:T(8,128)(2,1)S(1)}, u32[]{:S(2)}, u32[]{:S(2)}) collective-permute-start(bf16[4,256,128]{2,1,0:T(8,128)(2,1)S(1)} %halve.3), channel_id=1, source_target_pairs={{0,2},{1,3},{2,0},{3,1},{4,6},{5,7},{6,4},{7,5},{8,10},{9,11},{10,... | collective-permute-start | bytes 786440 | tf_op jit(solution)/shard_map/ppermute | solution.py:203
  27.0 10.7 %collective-permute-start.3 = (bf16[1,320,128]{2,1,0:T(8,128)(2,1)S(1)}, bf16[1,320,128]{2,1,0:T(8,128)(2,1)S(1)}, u32[]{:S(2)}, u32[]{:S(2)}) collective-permute-start(bf16[1,320,128]{2,1,0:T(8,128)(2,1)S(1)} %get-tuple-element.37), channel_id=1, source_target_pairs={{0,8},{1,9},{2,10},{3,11},{4,12},{5,13},{6,14},{7,15},{8,0},{9,1},... | collective-permute-start | bytes 245768 | tf_op jit(solution)/shard_map/ppermute | solution.py:203
  30.2 7.5 %collective-permute-start.4 = (bf16[1,320,128]{2,1,0:T(8,128)(2,1)S(1)}, bf16[1,320,128]{2,1,0:T(8,128)(2,1)S(1)}, u32[]{:S(2)}, u32[]{:S(2)}) collective-permute-start(bf16[1,320,128]{2,1,0:T(8,128)(2,1)S(1)} %get-tuple-element.38), channel_id=1, source_target_pairs={{0,4},{1,5},{2,6},{3,7},{4,0},{5,1},{6,2},{7,3},{8,12},{9,13},{10,... | collective-permute-start | bytes 245768 | tf_op jit(solution)/shard_map/ppermute | solution.py:203
  30.2 7.4 %collective-permute-start.5 = (bf16[1,320,128]{2,1,0:T(8,128)(2,1)S(1)}, bf16[1,320,128]{2,1,0:T(8,128)(2,1)S(1)}, u32[]{:S(2)}, u32[]{:S(2)}) collective-permute-start(bf16[1,320,128]{2,1,0:T(8,128)(2,1)S(1)} %get-tuple-element.39), channel_id=1, source_target_pairs={{0,12},{1,13},{2,14},{3,15},{4,8},{5,9},{6,10},{7,11},{8,4},{9,5},... | collective-permute-start | bytes 245768 | tf_op jit(solution)/shard_map/ppermute | solution.py:203
  37.7 6.6 %collective-permute-start.7 = (bf16[1,320,128]{2,1,0:T(8,128)(2,1)S(1)}, bf16[1,320,128]{2,1,0:T(8,128)(2,1)S(1)}, u32[]{:S(2)}, u32[]{:S(2)}) collective-permute-start(bf16[1,320,128]{2,1,0:T(8,128)(2,1)S(1)} %total.2.refs_0_), channel_id=1, source_target_pairs={{0,8},{1,9},{2,10},{3,11},{4,12},{5,13},{6,14},{7,15},{8,0},{9,1},... | collective-permute-start | bytes 245768 | tf_op jit(solution)/shard_map/ppermute | solution.py:203
  40.7 3.6 %collective-permute-start.8 = (bf16[1,320,128]{2,1,0:T(8,128)(2,1)S(1)}, bf16[1,320,128]{2,1,0:T(8,128)(2,1)S(1)}, u32[]{:S(2)}, u32[]{:S(2)}) collective-permute-start(bf16[1,320,128]{2,1,0:T(8,128)(2,1)S(1)} %total.2.refs_0_), channel_id=1, source_target_pairs={{0,4},{1,5},{2,6},{3,7},{4,0},{5,1},{6,2},{7,3},{8,12},{9,13},{10,... | collective-permute-start | bytes 245768 | tf_op jit(solution)/shard_map/ppermute | solution.py:203
  40.8 6.8 %collective-permute-start.9 = (bf16[1,320,128]{2,1,0:T(8,128)(2,1)S(1)}, bf16[1,320,128]{2,1,0:T(8,128)(2,1)S(1)}, u32[]{:S(2)}, u32[]{:S(2)}) collective-permute-start(bf16[1,320,128]{2,1,0:T(8,128)(2,1)S(1)} %total.2.refs_0_), channel_id=1, source_target_pairs={{0,12},{1,13},{2,14},{3,15},{4,8},{5,9},{6,10},{7,11},{8,4},{9,5},... | collective-permute-start | bytes 245768 | tf_op jit(solution)/shard_map/ppermute | solution.py:203
  47.7 59.0 %all-to-all-start.1 = ((bf16[16,8,64,128]{3,2,1,0:T(8,128)(2,1)}), bf16[16,8,64,128]{3,2,1,0:T(8,128)(2,1)S(1)}, u32[]{:S(2)}, u32[]{:S(2)}) async-start(bf16[16,8,64,128]{3,2,1,0:T(8,128)(2,1)} %pad_maximum_fusion), calls=%async_computation.1 | async-start | bytes 4194304 | tf_op jit(solution)/shard_map/all_to_all | solution.py:206
  53.5 28.8 %copy-start.2 = (bf16[2,64,5120]{2,1,0:T(8,128)(2,1)S(1)}, bf16[2,64,5120]{2,1,0:T(8,128)(2,1)}, u32[]{:S(2)}) copy-start(bf16[2,64,5120]{2,1,0:T(8,128)(2,1)} %x_ref.1) | copy-start | bytes 3932164
  53.5 25.8 %collective-permute-start.10 = (bf16[4,320,128]{2,1,0:T(8,128)(2,1)S(1)}, bf16[4,320,128]{2,1,0:T(8,128)(2,1)S(1)}, u32[]{:S(2)}, u32[]{:S(2)}) collective-permute-start(bf16[4,320,128]{2,1,0:T(8,128)(2,1)S(1)} %join.2.refs_0_), channel_id=1, source_target_pairs={{0,2},{1,3},{2,0},{3,1},{4,6},{5,7},{6,4},{7,5},{8,10},{9,11},{10,... | collective-permute-start | bytes 983048 | tf_op jit(solution)/shard_map/ppermute | solution.py:203
  79.3 3.0 %collective-permute-start.11 = (bf16[8,320,128]{2,1,0:T(8,128)(2,1)S(1)}, bf16[8,320,128]{2,1,0:T(8,128)(2,1)S(1)}, u32[]{:S(2)}, u32[]{:S(2)}) collective-permute-start(bf16[8,320,128]{2,1,0:T(8,128)(2,1)S(1)} %join.3.refs_0_), channel_id=1, source_target_pairs={{0,1},{1,0},{2,3},{3,2},{4,5},{5,4},{6,7},{7,6},{8,9},{9,8},{10,11... | collective-permute-start | bytes 1966088 | tf_op jit(solution)/shard_map/ppermute | solution.py:203
  83.2 3.9 %copy-start.3 = (bf16[2,32,128]{2,1,0:T(8,128)(2,1)}, bf16[2,32,128]{2,1,0:T(8,128)(2,1)S(1)}, u32[]{:S(2)}) copy-start(bf16[2,32,128]{2,1,0:T(8,128)(2,1)S(1)} %low_rank.1.refs_0_) | copy-start | bytes 49156
  83.2 2.2 %collective-permute-start.12 = (bf16[2,32,128]{2,1,0:T(8,128)(2,1)S(1)}, bf16[2,32,128]{2,1,0:T(8,128)(2,1)S(1)}, u32[]{:S(2)}, u32[]{:S(2)}) collective-permute-start(bf16[2,32,128]{2,1,0:T(8,128)(2,1)S(1)} %low_rank.1.refs_0_), channel_id=1, source_target_pairs={{0,1},{1,0},{2,3},{3,2},{4,5},{5,4},{6,7},{7,6},{8,9},{9,8},{10,11... | collective-permute-start | bytes 49160 | tf_op jit(solution)/shard_map/ppermute | solution.py:203
  83.6 2.6 %collective-permute-start.13 = (bf16[2,32,128]{2,1,0:T(8,128)(2,1)S(1)}, bf16[2,32,128]{2,1,0:T(8,128)(2,1)S(1)}, u32[]{:S(2)}, u32[]{:S(2)}) collective-permute-start(bf16[2,32,128]{2,1,0:T(8,128)(2,1)S(1)} %low_rank.1.refs_0_), channel_id=1, source_target_pairs={{0,2},{1,3},{2,0},{3,1},{4,6},{5,7},{6,4},{7,5},{8,10},{9,11},{10,... | collective-permute-start | bytes 49160 | tf_op jit(solution)/shard_map/ppermute | solution.py:203
  83.6 3.5 %collective-permute-start.14 = (bf16[2,32,128]{2,1,0:T(8,128)(2,1)S(1)}, bf16[2,32,128]{2,1,0:T(8,128)(2,1)S(1)}, u32[]{:S(2)}, u32[]{:S(2)}) collective-permute-start(bf16[2,32,128]{2,1,0:T(8,128)(2,1)S(1)} %low_rank.1.refs_0_), channel_id=1, source_target_pairs={{0,3},{1,2},{2,1},{3,0},{4,7},{5,6},{6,5},{7,4},{8,11},{9,10},{10,... | collective-permute-start | bytes 49160 | tf_op jit(solution)/shard_map/ppermute | solution.py:203
  85.4 1.7 %copy-start.9 = (bf16[2,32,128]{2,1,0:T(8,128)(2,1)}, bf16[2,32,128]{2,1,0:T(8,128)(2,1)S(1)}, u32[]{:S(2)}) copy-start(bf16[2,32,128]{2,1,0:T(8,128)(2,1)S(1)} %collective-permute-done.12.refs_1_) | copy-start | bytes 49156
  86.2 0.9 copy-start.10
  87.2 0.6 copy-start.11
  89.3 10.1 %collective-permute-start.15 = (bf16[2,256,128]{2,1,0:T(8,128)(2,1)S(1)}, bf16[2,256,128]{2,1,0:T(8,128)(2,1)S(1)}, u32[]{:S(2)}, u32[]{:S(2)}) collective-permute-start(bf16[2,256,128]{2,1,0:T(8,128)(2,1)S(1)} %get-tuple-element.46), channel_id=1, source_target_pairs={{0,4},{1,5},{2,6},{3,7},{4,0},{5,1},{6,2},{7,3},{8,12},{9,13},{10,... | collective-permute-start | bytes 393224 | tf_op jit(solution)/shard_map/ppermute | solution.py:203
  99.4 4.1 %collective-permute-start.16 = (bf16[1,256,128]{2,1,0:T(8,128)(2,1)S(1)}, bf16[1,256,128]{2,1,0:T(8,128)(2,1)S(1)}, u32[]{:S(2)}, u32[]{:S(2)}) collective-permute-start(bf16[1,256,128]{2,1,0:T(8,128)(2,1)S(1)} %get-tuple-element.48), channel_id=1, source_target_pairs={{0,8},{1,9},{2,10},{3,11},{4,12},{5,13},{6,14},{7,15},{8,0},{9,1},... | collective-permute-start | bytes 196616 | tf_op jit(solution)/shard_map/ppermute | solution.py:203
  99.5 4.0 %collective-permute-start.17 = (bf16[4,32,128]{2,1,0:T(8,128)(2,1)}, bf16[4,32,128]{2,1,0:T(8,128)(2,1)S(1)}, u32[]{:S(2)}, u32[]{:S(2)}) collective-permute-start(bf16[4,32,128]{2,1,0:T(8,128)(2,1)} %get-tuple-element.50), channel_id=1, source_target_pairs={{0,4},{1,5},{2,6},{3,7},{4,0},{5,1},{6,2},{7,3},{8,12},{9,13},{10,... | collective-permute-start | bytes 98312 | tf_op jit(solution)/shard_map/ppermute | solution.py:203
  99.6 4.3 %collective-permute-start.18 = (bf16[4,32,128]{2,1,0:T(8,128)(2,1)}, bf16[4,32,128]{2,1,0:T(8,128)(2,1)S(1)}, u32[]{:S(2)}, u32[]{:S(2)}) collective-permute-start(bf16[4,32,128]{2,1,0:T(8,128)(2,1)} %get-tuple-element.51), channel_id=1, source_target_pairs={{0,8},{1,9},{2,10},{3,11},{4,12},{5,13},{6,14},{7,15},{8,0},{9,1},... | collective-permute-start | bytes 98312 | tf_op jit(solution)/shard_map/ppermute | solution.py:203
  101.9 4.8 %collective-permute-start.19 = (bf16[4,32,128]{2,1,0:T(8,128)(2,1)}, bf16[4,32,128]{2,1,0:T(8,128)(2,1)S(1)}, u32[]{:S(2)}, u32[]{:S(2)}) collective-permute-start(bf16[4,32,128]{2,1,0:T(8,128)(2,1)} %get-tuple-element.52), channel_id=1, source_target_pairs={{0,12},{1,13},{2,14},{3,15},{4,8},{5,9},{6,10},{7,11},{8,4},{9,5},... | collective-permute-start | bytes 98312 | tf_op jit(solution)/shard_map/ppermute | solution.py:203
  106.6 0.8 copy-start.6

commit v26 on v22

--- a/solution.py
+++ b/solution.py
@@ -156,7 +156,7 @@
     vals = add_delta(v_ref[...], low, up, 1)
     vals = jnp.concatenate([vals, jnp.ones_like(vals)], axis=1)
     q_mix[...] = add_delta(q_ref[...], low, up, 0)
-    scale = math.log2(math.e) / math.sqrt(width)
+    scale = 1 / math.sqrt(width)
 
     def score(b):
         q = q_mix[b * toks : (b + block) * toks, :]
@@ -168,7 +168,7 @@
         if b + block < devs:
             coming = score(b + block)
         top = jnp.max(scores, axis=1, keepdims=True)
-        weights = jnp.exp2((scores - top) * scale).astype(jnp.bfloat16)
+        weights = jnp.exp((scores - top) * scale).astype(jnp.bfloat16)
         mixed = jnp.dot(weights, vals, preferred_element_type=jnp.float32)
         out = mixed[:, :width] / mixed[:, width:]
         out_ref[b : b + block] = out.astype(jnp.bfloat16).reshape(block, toks, width)

time: 149 us -> 149 us (level)
  no operation moved by 1% of the time
where the time goes in v26:
time: 149 us
  waiting for transfers between devices  57.6 us (39%)
  starting transfers between devices  39.3 us (26%)
  blocking collectives  29.8 us (20%)
  Pallas kernels  11.7 us (8%)
  local copies, waits for them, and re-layouts  7.2 us (5%)
  other arithmetic  2.77 us (2%)
    ppermute x20, waiting for transfers between devices, swap(): return lax.ppermute(tensor, 'seq', [(i, i ^ k) for i in range(devs)])  57.6 us
    all_to_all x1, blocking collectives, exchange(): lax.all_to_all(tensor, 'seq', split_axis=0, concat_axis=0, tiled=True)  29.8 us
    ppermute x20, starting transfers between devices, swap(): return lax.ppermute(tensor, 'seq', [(i, i ^ k) for i in range(devs)])  26.3 us
    all_to_all x2, starting transfers between devices, exchange(): lax.all_to_all(tensor, 'seq', split_axis=0, concat_axis=0, tiled=True)  13 us
    pallas_call x1, Pallas kernels, body(): pl.pallas_call(functools.partial(attend_kernel, math.gcd(devs, max(1, 256...  7.41 us
    unnamed x31, local copies, waits for them, and re-layouts  7.2 us
  transfers between devices with their start and end apart: 22, of which 11 were waited for; matrix products, arithmetic and copies ran while one was open for 2% of the time, Pallas kernels for 3%

profile of v26, /device:TPU:1, one launch (start us, length us, event | category | flops | bytes accessed | tf_op | source)
XLA Modules:
  0.0 148.5 jit_solution(15102390680916697631)
XLA Ops:
  0.0 7.5 %all-to-all-start = ((bf16[16,4,64,128]{3,2,1,0:T(8,128)(2,1)}), bf16[16,4,64,128]{3,2,1,0:T(8,128)(2,1)S(1)}, u32[]{:S(2)}, u32[]{:S(2)}) async-start(bf16[16,4,64,128]{3,2,1,0:T(8,128)(2,1)} %bitcast.8), calls=%async_computation | async-start | bytes 2097152 | tf_op jit(solution)/shard_map/all_to_all | solution.py:206
  7.5 1.7 %copy-done = bf16[4,64,5120]{2,1,0:T(8,128)(2,1)S(1)} copy-done((bf16[4,64,5120]{2,1,0:T(8,128)(2,1)S(1)}, bf16[4,64,5120]{2,1,0:T(8,128)(2,1)}, u32[]{:S(2)}) %copy-start) | copy-done | bytes 2621464
  9.3 1.5 %pick_factors.1 = (bf16[8,320,128]{2,1,0:T(8,128)(2,1)S(1)}, bf16[4,320,128]{2,1,0:T(8,128)(2,1)S(1)}, bf16[4,320,128]{2,1,0:T(8,128)(2,1)S(1)}, bf16[8,256,128]...) custom-call(s32[1]{0:T(128)} %bitcast.me_ref, s32[64]{0:T(128)S(1)} %copy-done.8, ...), custom_call_target="tpu_custom_call" | custom-call | bytes 4718592 | tf_op jit(solution)/shard_map/pick_factors/pallas_call | solution.py:250
  10.8 0.2 collective-permute-start
  11.0 2.0 %collective-permute-done.refs_1_ = bf16[8,320,128]{2,1,0:T(8,128)(2,1)S(1)} collective-permute-done((bf16[8,320,128]{2,1,0:T(8,128)(2,1)S(1)}, bf16[8,320,128]{2,1,0:T(8,128)(2,1)S(1)}, u32[]{:S(2)}, u32[]{:S(2)}) %collective-permute-start) | collective-permute-done | bytes 655392 | tf_op jit(solution)/shard_map/ppermute | solution.py:203
  13.0 0.1 halve.2
  13.0 0.2 collective-permute-start.1
  13.2 1.6 %collective-permute-start.2 = (bf16[4,320,128]{2,1,0:T(8,128)(2,1)S(1)}, bf16[4,320,128]{2,1,0:T(8,128)(2,1)S(1)}, u32[]{:S(2)}, u32[]{:S(2)}) collective-permute-start(bf16[4,320,128]{2,1,0:T(8,128)(2,1)S(1)} %halve.2), channel_id=1, source_target_pairs={{0,2},{1,3},{2,0},{3,1},{4,6},{5,7},{6,4},{7,5},{8,10},{9,11},{10,... | collective-permute-start | bytes 983048 | tf_op jit(solution)/shard_map/ppermute | solution.py:203
  14.9 0.2 collective-permute-done.1.refs_1_
  15.0 0.1 halve.3
  15.1 1.5 collective-permute-start.6
  16.5 10.4 %collective-permute-done.2.refs_2_ = bf16[4,320,128]{2,1,0:T(8,128)(2,1)S(1)} collective-permute-done((bf16[4,320,128]{2,1,0:T(8,128)(2,1)S(1)}, bf16[4,320,128]{2,1,0:T(8,128)(2,1)S(1)}, u32[]{:S(2)}, u32[]{:S(2)}) %collective-permute-start.2) | collective-permute-done | bytes 327712 | tf_op jit(solution)/shard_map/ppermute | solution.py:203
  26.9 0.1 split.3
  27.0 3.2 %collective-permute-start.3 = (bf16[1,320,128]{2,1,0:T(8,128)(2,1)S(1)}, bf16[1,320,128]{2,1,0:T(8,128)(2,1)S(1)}, u32[]{:S(2)}, u32[]{:S(2)}) collective-permute-start(bf16[1,320,128]{2,1,0:T(8,128)(2,1)S(1)} %get-tuple-element.37), channel_id=1, source_target_pairs={{0,8},{1,9},{2,10},{3,11},{4,12},{5,13},{6,14},{7,15},{8,0},{9,1},... | collective-permute-start | bytes 245768 | tf_op jit(solution)/shard_map/ppermute | solution.py:203
  30.2 1.7 %collective-permute-start.5 = (bf16[1,320,128]{2,1,0:T(8,128)(2,1)S(1)}, bf16[1,320,128]{2,1,0:T(8,128)(2,1)S(1)}, u32[]{:S(2)}, u32[]{:S(2)}) collective-permute-start(bf16[1,320,128]{2,1,0:T(8,128)(2,1)S(1)} %get-tuple-element.39), channel_id=1, source_target_pairs={{0,12},{1,13},{2,14},{3,15},{4,8},{5,9},{6,10},{7,11},{8,4},{9,5},... | collective-permute-start | bytes 245768 | tf_op jit(solution)/shard_map/ppermute | solution.py:203
  31.9 5.8 %collective-permute-done.3.refs_1_ = bf16[1,320,128]{2,1,0:T(8,128)(2,1)S(1)} collective-permute-done((bf16[1,320,128]{2,1,0:T(8,128)(2,1)S(1)}, bf16[1,320,128]{2,1,0:T(8,128)(2,1)S(1)}, u32[]{:S(2)}, u32[]{:S(2)}) %collective-permute-start.3) | collective-permute-done | bytes 81952 | tf_op jit(solution)/shard_map/ppermute | solution.py:203
  37.7 3.0 %collective-permute-start.9 = (bf16[1,320,128]{2,1,0:T(8,128)(2,1)S(1)}, bf16[1,320,128]{2,1,0:T(8,128)(2,1)S(1)}, u32[]{:S(2)}, u32[]{:S(2)}) collective-permute-start(bf16[1,320,128]{2,1,0:T(8,128)(2,1)S(1)} %total.2.refs_0_), channel_id=1, source_target_pairs={{0,8},{1,9},{2,10},{3,11},{4,12},{5,13},{6,14},{7,15},{8,0},{9,1},... | collective-permute-start | bytes 245768 | tf_op jit(solution)/shard_map/ppermute | solution.py:203
  40.7 0.1 collective-permute-start.10
  40.8 2.0 %collective-permute-start.11 = (bf16[1,320,128]{2,1,0:T(8,128)(2,1)S(1)}, bf16[1,320,128]{2,1,0:T(8,128)(2,1)S(1)}, u32[]{:S(2)}, u32[]{:S(2)}) collective-permute-start(bf16[1,320,128]{2,1,0:T(8,128)(2,1)S(1)} %total.2.refs_0_), channel_id=1, source_target_pairs={{0,12},{1,13},{2,14},{3,15},{4,8},{5,9},{6,10},{7,11},{8,4},{9,5},... | collective-permute-start | bytes 245768 | tf_op jit(solution)/shard_map/ppermute | solution.py:203
  42.8 0.1 split.4
  42.9 0.6 copy-done.3
  43.5 0.6 collective-permute-start.7
  44.1 2.8 %pad_maximum_fusion = bf16[16,8,64,128]{3,2,1,0:T(8,128)(2,1)} fusion(bf16[16,4,64,128]{3,2,1,0:T(8,128)(2,1)S(1)} %bitcast.9, bf16[16,4,64,128]{3,2,1,0:T(8,128)(2,1)} %bitcast.10), kind=kLoop, calls=%fused_computation | loop fusion | flops 1048576 | bytes 4194304 | tf_op jit(solution)/shard_map/concatenate | solution.py:296
  46.9 0.8 collective-permute-done.11.refs_3_
  47.7 2.5 %collective-permute-done.7.refs_1_ = bf16[2,256,128]{2,1,0:T(8,128)(2,1)S(1)} collective-permute-done((bf16[2,256,128]{2,1,0:T(8,128)(2,1)S(1)}, bf16[2,256,128]{2,1,0:T(8,128)(2,1)S(1)}, u32[]{:S(2)}, u32[]{:S(2)}) %collective-permute-start.7) | collective-permute-done | bytes 131104 | tf_op jit(solution)/shard_map/ppermute | solution.py:203
  50.2 0.7 copy-done.5
  50.8 5.5 %all-to-all-start.1 = ((bf16[16,8,64,128]{3,2,1,0:T(8,128)(2,1)}), bf16[16,8,64,128]{3,2,1,0:T(8,128)(2,1)S(1)}, u32[]{:S(2)}, u32[]{:S(2)}) async-start(bf16[16,8,64,128]{3,2,1,0:T(8,128)(2,1)} %pad_maximum_fusion), calls=%async_computation.1 | async-start | bytes 4194304 | tf_op jit(solution)/shard_map/all_to_all | solution.py:206
  56.3 1.5 collective-permute-start.12
  57.8 24.3 %collective-permute-done.12.refs_1_ = bf16[4,320,128]{2,1,0:T(8,128)(2,1)S(1)} collective-permute-done((bf16[4,320,128]{2,1,0:T(8,128)(2,1)S(1)}, bf16[4,320,128]{2,1,0:T(8,128)(2,1)S(1)}, u32[]{:S(2)}, u32[]{:S(2)}) %collective-permute-start.12) | collective-permute-done | bytes 327712 | tf_op jit(solution)/shard_map/ppermute | solution.py:203
  82.1 1.3 collective-permute-start.13
  83.4 0.9 copy-done.4
  84.3 0.9 copy-done.6
  85.3 0.1 collective-permute-start.8
  85.4 0.9 low_rank.1.refs_0_
  86.2 0.2 collective-permute-start.14
  86.4 2.0 %collective-permute-start.16 = (bf16[2,32,128]{2,1,0:T(8,128)(2,1)S(1)}, bf16[2,32,128]{2,1,0:T(8,128)(2,1)S(1)}, u32[]{:S(2)}, u32[]{:S(2)}) collective-permute-start(bf16[2,32,128]{2,1,0:T(8,128)(2,1)S(1)} %low_rank.1.refs_0_), channel_id=1, source_target_pairs={{0,3},{1,2},{2,1},{3,0},{4,7},{5,6},{6,5},{7,4},{8,11},{9,10},{10,... | collective-permute-start | bytes 49160 | tf_op jit(solution)/shard_map/ppermute | solution.py:203
  88.4 0.6 collective-permute-done.15.refs_2_
  89.0 1.1 collective-permute-done.16.refs_3_
  90.1 0.6 copy-done.14
  90.7 1.4 choose.1
  92.1 5.2 %collective-permute-start.17 = (bf16[4,32,128]{2,1,0:T(8,128)(2,1)}, bf16[4,32,128]{2,1,0:T(8,128)(2,1)S(1)}, u32[]{:S(2)}, u32[]{:S(2)}) collective-permute-start(bf16[4,32,128]{2,1,0:T(8,128)(2,1)} %get-tuple-element.50), channel_id=1, source_target_pairs={{0,4},{1,5},{2,6},{3,7},{4,0},{5,1},{6,2},{7,3},{8,12},{9,13},{10,... | collective-permute-start | bytes 98312 | tf_op jit(solution)/shard_map/ppermute | solution.py:203
  97.3 2.1 %collective-permute-start.19 = (bf16[4,32,128]{2,1,0:T(8,128)(2,1)}, bf16[4,32,128]{2,1,0:T(8,128)(2,1)S(1)}, u32[]{:S(2)}, u32[]{:S(2)}) collective-permute-start(bf16[4,32,128]{2,1,0:T(8,128)(2,1)} %get-tuple-element.52), channel_id=1, source_target_pairs={{0,12},{1,13},{2,14},{3,15},{4,8},{5,9},{6,10},{7,11},{8,4},{9,5},... | collective-permute-start | bytes 98312 | tf_op jit(solution)/shard_map/ppermute | solution.py:203
  99.5 9.4 %collective-permute-done.8.refs_1_ = bf16[1,256,128]{2,1,0:T(8,128)(2,1)S(1)} collective-permute-done((bf16[1,256,128]{2,1,0:T(8,128)(2,1)S(1)}, bf16[1,256,128]{2,1,0:T(8,128)(2,1)S(1)}, u32[]{:S(2)}, u32[]{:S(2)}) %collective-permute-start.8) | collective-permute-done | bytes 65568 | tf_op jit(solution)/shard_map/ppermute | solution.py:203
  108.9 0.7 collective-permute-done.18.refs_2_
  109.5 0.8 copy-done.10
  110.3 7.4 %attend.1 = bf16[16,4,64,128]{3,2,1,0:T(8,128)(2,1)S(1)} custom-call(s32[1]{0:T(128)} %bitcast.me_ref, bf16[4,64,128]{2,1,0:T(8,128)(2,1)S(1)} %bitcast.6, bf16[16,8,64,128]{3,2,1,0:T(8,128)(2,1)S(1)} %all-to-all-done.1.q_ref.v_ref, bf16[16,4,64,128]{3,2,1,0:T(8,128)(2,1)S(1)} %all-to-all-done.k_ref, ...), custom_call_target="tpu_custom_call" | custom-call | flops 2147483648 | bytes 4194304 | tf_op jit(solution)/shard_map/attend/pallas_call | solution.py:345
  117.7 29.8 %all_to_all.15 = bf16[16,4,64,128]{3,2,1,0:T(8,128)(2,1)S(1)} all-to-all(bf16[16,4,64,128]{3,2,1,0:T(8,128)(2,1)S(1)} %attend.1), channel_id=1, replica_groups=mesh['grp'=2,'seq'=16] {'seq'}, dimensions={0} | all-to-all | bytes 2097152 | tf_op jit(solution)/shard_map/all_to_all | solution.py:206
  147.6 1.0 copy.10
  (42 shorter events, 0.2 us)
Async XLA Ops:
  0.0 7.5 %copy-start.8 = (s32[64]{0:T(128)S(1)}, s32[64]{0:T(128)}, u32[]{:S(2)}) copy-start(s32[64]{0:T(128)} %row_ref.1) | copy-start | bytes 772
  0.0 7.5 %copy-start.9 = (s32[2]{0:T(128)S(1)}, s32[2]{0:T(128)}, u32[]{:S(2)}) copy-start(s32[2]{0:T(128)} %req_ref.1) | copy-start | bytes 28
  0.0 7.5 %copy-start.1 = (bf16[4,64,4096]{2,1,0:T(8,128)(2,1)S(1)}, bf16[4,64,4096]{2,1,0:T(8,128)(2,1)}, u32[]{:S(2)}) copy-start(bf16[4,64,4096]{2,1,0:T(8,128)(2,1)} %up_ref.1) | copy-start | bytes 6291460
  0.0 37.7 %all-to-all-start = ((bf16[16,4,64,128]{3,2,1,0:T(8,128)(2,1)}), bf16[16,4,64,128]{3,2,1,0:T(8,128)(2,1)S(1)}, u32[]{:S(2)}, u32[]{:S(2)}) async-start(bf16[16,4,64,128]{3,2,1,0:T(8,128)(2,1)} %bitcast.8), calls=%async_computation | async-start | bytes 2097152 | tf_op jit(solution)/shard_map/all_to_all | solution.py:206
  7.5 1.7 %copy-start = (bf16[4,64,5120]{2,1,0:T(8,128)(2,1)S(1)}, bf16[4,64,5120]{2,1,0:T(8,128)(2,1)}, u32[]{:S(2)}) copy-start(bf16[4,64,5120]{2,1,0:T(8,128)(2,1)} %down_ref.1) | copy-start | bytes 7864324
  10.8 2.2 %collective-permute-start = (bf16[8,320,128]{2,1,0:T(8,128)(2,1)S(1)}, bf16[8,320,128]{2,1,0:T(8,128)(2,1)S(1)}, u32[]{:S(2)}, u32[]{:S(2)}) collective-permute-start(bf16[8,320,128]{2,1,0:T(8,128)(2,1)S(1)} %get-tuple-element.33), channel_id=1, source_target_pairs={{0,1},{1,0},{2,3},{3,2},{4,5},{5,4},{6,7},{7,6},{8,9},{9,8},{10,11... | collective-permute-start | bytes 1966088 | tf_op jit(solution)/shard_map/ppermute | solution.py:203
  13.0 31.1 %copy-start.11 = (bf16[2,32,64,128]{3,2,1,0:T(8,128)(2,1)S(1)}, bf16[2,32,64,128]{3,2,1,0:T(8,128)(2,1)}, u32[]{:S(2)}) copy-start(bf16[2,32,64,128]{3,2,1,0:T(8,128)(2,1)} %param.9) | copy-start | bytes 3145732
  13.0 2.0 %collective-permute-start.1 = (bf16[8,256,128]{2,1,0:T(8,128)(2,1)S(1)}, bf16[8,256,128]{2,1,0:T(8,128)(2,1)S(1)}, u32[]{:S(2)}, u32[]{:S(2)}) collective-permute-start(bf16[8,256,128]{2,1,0:T(8,128)(2,1)S(1)} %get-tuple-element.34), channel_id=1, source_target_pairs={{0,1},{1,0},{2,3},{3,2},{4,5},{5,4},{6,7},{7,6},{8,9},{9,8},{10,11... | collective-permute-start | bytes 1572872 | tf_op jit(solution)/shard_map/ppermute | solution.py:203
  13.2 13.6 %collective-permute-start.2 = (bf16[4,320,128]{2,1,0:T(8,128)(2,1)S(1)}, bf16[4,320,128]{2,1,0:T(8,128)(2,1)S(1)}, u32[]{:S(2)}, u32[]{:S(2)}) collective-permute-start(bf16[4,320,128]{2,1,0:T(8,128)(2,1)S(1)} %halve.2), channel_id=1, source_target_pairs={{0,2},{1,3},{2,0},{3,1},{4,6},{5,7},{6,4},{7,5},{8,10},{9,11},{10,... | collective-permute-start | bytes 983048 | tf_op jit(solution)/shard_map/ppermute | solution.py:203
  15.1 22.7 %collective-permute-start.6 = (bf16[4,256,128]{2,1,0:T(8,128)(2,1)S(1)}, bf16[4,256,128]{2,1,0:T(8,128)(2,1)S(1)}, u32[]{:S(2)}, u32[]{:S(2)}) collective-permute-start(bf16[4,256,128]{2,1,0:T(8,128)(2,1)S(1)} %halve.3), channel_id=1, source_target_pairs={{0,2},{1,3},{2,0},{3,1},{4,6},{5,7},{6,4},{7,5},{8,10},{9,11},{10,... | collective-permute-start | bytes 786440 | tf_op jit(solution)/shard_map/ppermute | solution.py:203
  27.0 10.7 %collective-permute-start.3 = (bf16[1,320,128]{2,1,0:T(8,128)(2,1)S(1)}, bf16[1,320,128]{2,1,0:T(8,128)(2,1)S(1)}, u32[]{:S(2)}, u32[]{:S(2)}) collective-permute-start(bf16[1,320,128]{2,1,0:T(8,128)(2,1)S(1)} %get-tuple-element.37), channel_id=1, source_target_pairs={{0,8},{1,9},{2,10},{3,11},{4,12},{5,13},{6,14},{7,15},{8,0},{9,1},... | collective-permute-start | bytes 245768 | tf_op jit(solution)/shard_map/ppermute | solution.py:203
  30.2 7.5 %collective-permute-start.4 = (bf16[1,320,128]{2,1,0:T(8,128)(2,1)S(1)}, bf16[1,320,128]{2,1,0:T(8,128)(2,1)S(1)}, u32[]{:S(2)}, u32[]{:S(2)}) collective-permute-start(bf16[1,320,128]{2,1,0:T(8,128)(2,1)S(1)} %get-tuple-element.38), channel_id=1, source_target_pairs={{0,4},{1,5},{2,6},{3,7},{4,0},{5,1},{6,2},{7,3},{8,12},{9,13},{10,... | collective-permute-start | bytes 245768 | tf_op jit(solution)/shard_map/ppermute | solution.py:203
  30.2 7.5 %collective-permute-start.5 = (bf16[1,320,128]{2,1,0:T(8,128)(2,1)S(1)}, bf16[1,320,128]{2,1,0:T(8,128)(2,1)S(1)}, u32[]{:S(2)}, u32[]{:S(2)}) collective-permute-start(bf16[1,320,128]{2,1,0:T(8,128)(2,1)S(1)} %get-tuple-element.39), channel_id=1, source_target_pairs={{0,12},{1,13},{2,14},{3,15},{4,8},{5,9},{6,10},{7,11},{8,4},{9,5},... | collective-permute-start | bytes 245768 | tf_op jit(solution)/shard_map/ppermute | solution.py:203
  37.7 9.1 %collective-permute-start.9 = (bf16[1,320,128]{2,1,0:T(8,128)(2,1)S(1)}, bf16[1,320,128]{2,1,0:T(8,128)(2,1)S(1)}, u32[]{:S(2)}, u32[]{:S(2)}) collective-permute-start(bf16[1,320,128]{2,1,0:T(8,128)(2,1)S(1)} %total.2.refs_0_), channel_id=1, source_target_pairs={{0,8},{1,9},{2,10},{3,11},{4,12},{5,13},{6,14},{7,15},{8,0},{9,1},... | collective-permute-start | bytes 245768 | tf_op jit(solution)/shard_map/ppermute | solution.py:203
  40.7 6.2 %collective-permute-start.10 = (bf16[1,320,128]{2,1,0:T(8,128)(2,1)S(1)}, bf16[1,320,128]{2,1,0:T(8,128)(2,1)S(1)}, u32[]{:S(2)}, u32[]{:S(2)}) collective-permute-start(bf16[1,320,128]{2,1,0:T(8,128)(2,1)S(1)} %total.2.refs_0_), channel_id=1, source_target_pairs={{0,4},{1,5},{2,6},{3,7},{4,0},{5,1},{6,2},{7,3},{8,12},{9,13},{10,... | collective-permute-start | bytes 245768 | tf_op jit(solution)/shard_map/ppermute | solution.py:203
  40.8 6.8 %collective-permute-start.11 = (bf16[1,320,128]{2,1,0:T(8,128)(2,1)S(1)}, bf16[1,320,128]{2,1,0:T(8,128)(2,1)S(1)}, u32[]{:S(2)}, u32[]{:S(2)}) collective-permute-start(bf16[1,320,128]{2,1,0:T(8,128)(2,1)S(1)} %total.2.refs_0_), channel_id=1, source_target_pairs={{0,12},{1,13},{2,14},{3,15},{4,8},{5,9},{6,10},{7,11},{8,4},{9,5},... | collective-permute-start | bytes 245768 | tf_op jit(solution)/shard_map/ppermute | solution.py:203
  42.9 0.7 copy-start.3
  43.5 6.6 %collective-permute-start.7 = (bf16[2,256,128]{2,1,0:T(8,128)(2,1)S(1)}, bf16[2,256,128]{2,1,0:T(8,128)(2,1)S(1)}, u32[]{:S(2)}, u32[]{:S(2)}) collective-permute-start(bf16[2,256,128]{2,1,0:T(8,128)(2,1)S(1)} %get-tuple-element.45), channel_id=1, source_target_pairs={{0,4},{1,5},{2,6},{3,7},{4,0},{5,1},{6,2},{7,3},{8,12},{9,13},{10,... | collective-permute-start | bytes 393224 | tf_op jit(solution)/shard_map/ppermute | solution.py:203
  50.2 0.7 copy-start.5
  50.8 58.7 %all-to-all-start.1 = ((bf16[16,8,64,128]{3,2,1,0:T(8,128)(2,1)}), bf16[16,8,64,128]{3,2,1,0:T(8,128)(2,1)S(1)}, u32[]{:S(2)}, u32[]{:S(2)}) async-start(bf16[16,8,64,128]{3,2,1,0:T(8,128)(2,1)} %pad_maximum_fusion), calls=%async_computation.1 | async-start | bytes 4194304 | tf_op jit(solution)/shard_map/all_to_all | solution.py:206
  56.3 29.0 %copy-start.2 = (bf16[2,64,5120]{2,1,0:T(8,128)(2,1)S(1)}, bf16[2,64,5120]{2,1,0:T(8,128)(2,1)}, u32[]{:S(2)}) copy-start(bf16[2,64,5120]{2,1,0:T(8,128)(2,1)} %x_ref.1) | copy-start | bytes 3932164
  56.3 25.8 %collective-permute-start.12 = (bf16[4,320,128]{2,1,0:T(8,128)(2,1)S(1)}, bf16[4,320,128]{2,1,0:T(8,128)(2,1)S(1)}, u32[]{:S(2)}, u32[]{:S(2)}) collective-permute-start(bf16[4,320,128]{2,1,0:T(8,128)(2,1)S(1)} %join.2.refs_0_), channel_id=1, source_target_pairs={{0,2},{1,3},{2,0},{3,1},{4,6},{5,7},{6,4},{7,5},{8,10},{9,11},{10,... | collective-permute-start | bytes 983048 | tf_op jit(solution)/shard_map/ppermute | solution.py:203
  82.1 3.2 %collective-permute-start.13 = (bf16[8,320,128]{2,1,0:T(8,128)(2,1)S(1)}, bf16[8,320,128]{2,1,0:T(8,128)(2,1)S(1)}, u32[]{:S(2)}, u32[]{:S(2)}) collective-permute-start(bf16[8,320,128]{2,1,0:T(8,128)(2,1)S(1)} %join.3.refs_0_), channel_id=1, source_target_pairs={{0,1},{1,0},{2,3},{3,2},{4,5},{5,4},{6,7},{7,6},{8,9},{9,8},{10,11... | collective-permute-start | bytes 1966088 | tf_op jit(solution)/shard_map/ppermute | solution.py:203
  83.4 0.9 copy-start.4
  84.3 0.9 copy-start.6
  85.3 23.6 %collective-permute-start.8 = (bf16[1,256,128]{2,1,0:T(8,128)(2,1)S(1)}, bf16[1,256,128]{2,1,0:T(8,128)(2,1)S(1)}, u32[]{:S(2)}, u32[]{:S(2)}) collective-permute-start(bf16[1,256,128]{2,1,0:T(8,128)(2,1)S(1)} %get-tuple-element.47), channel_id=1, source_target_pairs={{0,8},{1,9},{2,10},{3,11},{4,12},{5,13},{6,14},{7,15},{8,0},{9,1},... | collective-permute-start | bytes 196616 | tf_op jit(solution)/shard_map/ppermute | solution.py:203
  86.2 3.9 %copy-start.7 = (bf16[2,32,128]{2,1,0:T(8,128)(2,1)}, bf16[2,32,128]{2,1,0:T(8,128)(2,1)S(1)}, u32[]{:S(2)}) copy-start(bf16[2,32,128]{2,1,0:T(8,128)(2,1)S(1)} %low_rank.1.refs_0_) | copy-start | bytes 49156
  86.2 2.2 %collective-permute-start.14 = (bf16[2,32,128]{2,1,0:T(8,128)(2,1)S(1)}, bf16[2,32,128]{2,1,0:T(8,128)(2,1)S(1)}, u32[]{:S(2)}, u32[]{:S(2)}) collective-permute-start(bf16[2,32,128]{2,1,0:T(8,128)(2,1)S(1)} %low_rank.1.refs_0_), channel_id=1, source_target_pairs={{0,1},{1,0},{2,3},{3,2},{4,5},{5,4},{6,7},{7,6},{8,9},{9,8},{10,11... | collective-permute-start | bytes 49160 | tf_op jit(solution)/shard_map/ppermute | solution.py:203
  86.4 2.6 %collective-permute-start.15 = (bf16[2,32,128]{2,1,0:T(8,128)(2,1)S(1)}, bf16[2,32,128]{2,1,0:T(8,128)(2,1)S(1)}, u32[]{:S(2)}, u32[]{:S(2)}) collective-permute-start(bf16[2,32,128]{2,1,0:T(8,128)(2,1)S(1)} %low_rank.1.refs_0_), channel_id=1, source_target_pairs={{0,2},{1,3},{2,0},{3,1},{4,6},{5,7},{6,4},{7,5},{8,10},{9,11},{10,... | collective-permute-start | bytes 49160 | tf_op jit(solution)/shard_map/ppermute | solution.py:203
  86.4 3.7 %collective-permute-start.16 = (bf16[2,32,128]{2,1,0:T(8,128)(2,1)S(1)}, bf16[2,32,128]{2,1,0:T(8,128)(2,1)S(1)}, u32[]{:S(2)}, u32[]{:S(2)}) collective-permute-start(bf16[2,32,128]{2,1,0:T(8,128)(2,1)S(1)} %low_rank.1.refs_0_), channel_id=1, source_target_pairs={{0,3},{1,2},{2,1},{3,0},{4,7},{5,6},{6,5},{7,4},{8,11},{9,10},{10,... | collective-permute-start | bytes 49160 | tf_op jit(solution)/shard_map/ppermute | solution.py:203
  88.4 1.7 %copy-start.12 = (bf16[2,32,128]{2,1,0:T(8,128)(2,1)}, bf16[2,32,128]{2,1,0:T(8,128)(2,1)S(1)}, u32[]{:S(2)}) copy-start(bf16[2,32,128]{2,1,0:T(8,128)(2,1)S(1)} %collective-permute-done.14.refs_1_) | copy-start | bytes 49156
  89.0 1.1 copy-start.13
  90.1 0.6 copy-start.14
  92.1 16.7 %collective-permute-start.17 = (bf16[4,32,128]{2,1,0:T(8,128)(2,1)}, bf16[4,32,128]{2,1,0:T(8,128)(2,1)S(1)}, u32[]{:S(2)}, u32[]{:S(2)}) collective-permute-start(bf16[4,32,128]{2,1,0:T(8,128)(2,1)} %get-tuple-element.50), channel_id=1, source_target_pairs={{0,4},{1,5},{2,6},{3,7},{4,0},{5,1},{6,2},{7,3},{8,12},{9,13},{10,... | collective-permute-start | bytes 98312 | tf_op jit(solution)/shard_map/ppermute | solution.py:203
  97.3 12.2 %collective-permute-start.18 = (bf16[4,32,128]{2,1,0:T(8,128)(2,1)}, bf16[4,32,128]{2,1,0:T(8,128)(2,1)S(1)}, u32[]{:S(2)}, u32[]{:S(2)}) collective-permute-start(bf16[4,32,128]{2,1,0:T(8,128)(2,1)} %get-tuple-element.51), channel_id=1, source_target_pairs={{0,8},{1,9},{2,10},{3,11},{4,12},{5,13},{6,14},{7,15},{8,0},{9,1},... | collective-permute-start | bytes 98312 | tf_op jit(solution)/shard_map/ppermute | solution.py:203
  97.3 12.2 %collective-permute-start.19 = (bf16[4,32,128]{2,1,0:T(8,128)(2,1)}, bf16[4,32,128]{2,1,0:T(8,128)(2,1)S(1)}, u32[]{:S(2)}, u32[]{:S(2)}) collective-permute-start(bf16[4,32,128]{2,1,0:T(8,128)(2,1)} %get-tuple-element.52), channel_id=1, source_target_pairs={{0,12},{1,13},{2,14},{3,15},{4,8},{5,9},{6,10},{7,11},{8,4},{9,5},... | collective-permute-start | bytes 98312 | tf_op jit(solution)/shard_map/ppermute | solution.py:203
  109.5 0.8 copy-start.10

commit v27 on v22

--- a/solution.py
+++ b/solution.py
@@ -334,6 +334,7 @@
         in_specs=[SMEM] + [VMEM] * LOW,
         out_specs=[VMEM] * quarter,
         out_shape=[jax.ShapeDtypeStruct((LOW,) + low_shape[1:], jnp.bfloat16)] * quarter,
+        compiler_params=pltpu.CompilerParams(vmem_limit_bytes=16 << 20),
         cost_estimate=pl.CostEstimate(flops=0, bytes_accessed=8 * low.size, transcendentals=0),
         name="choose",
     )(me, *nearby)

time: 149 us -> 148 us (level)
    unnamed x31 -> x21, local copies, waits for them, and re-layouts: 7.2 us -> 5.85 us
  transfers between devices with their start and end apart: 22 -> 22, of which waited for: 11 -> 11; matrix products, arithmetic and copies ran while one was open for 2% -> 2% of each run, Pallas kernels for 3% -> 2%
where the time goes in v27:
time: 148 us
  waiting for transfers between devices  59.6 us (40%)
  starting transfers between devices  39.3 us (27%)
  blocking collectives  29.8 us (20%)
  Pallas kernels  10.1 us (7%)
  local copies, waits for them, and re-layouts  5.85 us (4%)
  other arithmetic  2.77 us (2%)
    ppermute x20, waiting for transfers between devices, swap(): return lax.ppermute(tensor, 'seq', [(i, i ^ k) for i in range(devs)])  59.6 us
    all_to_all x1, blocking collectives, exchange(): lax.all_to_all(tensor, 'seq', split_axis=0, concat_axis=0, tiled=True)  29.8 us
    ppermute x20, starting transfers between devices, swap(): return lax.ppermute(tensor, 'seq', [(i, i ^ k) for i in range(devs)])  26.4 us
    all_to_all x2, starting transfers between devices, exchange(): lax.all_to_all(tensor, 'seq', split_axis=0, concat_axis=0, tiled=True)  13 us
    pallas_call x1, Pallas kernels, body(): pl.pallas_call(functools.partial(attend_kernel, math.gcd(devs, max(1, 256...  7.24 us
    unnamed x21, local copies, waits for them, and re-layouts  5.85 us
  transfers between devices with their start and end apart: 22, of which 11 were waited for; matrix products, arithmetic and copies ran while one was open for 2% of the time, Pallas kernels for 2%

profile of v27, /device:TPU:1, one launch (start us, length us, event | category | flops | bytes accessed | tf_op | source)
XLA Modules:
  0.0 147.6 jit_solution(3802955982482413708)
XLA Ops:
  0.0 7.5 %all-to-all-start = ((bf16[16,4,64,128]{3,2,1,0:T(8,128)(2,1)}), bf16[16,4,64,128]{3,2,1,0:T(8,128)(2,1)S(1)}, u32[]{:S(2)}, u32[]{:S(2)}) async-start(bf16[16,4,64,128]{3,2,1,0:T(8,128)(2,1)} %bitcast.8), calls=%async_computation | async-start | bytes 2097152 | tf_op jit(solution)/shard_map/all_to_all | solution.py:206
  7.5 0.0 copy-start
  7.5 1.7 %copy-done = bf16[4,64,5120]{2,1,0:T(8,128)(2,1)S(1)} copy-done((bf16[4,64,5120]{2,1,0:T(8,128)(2,1)S(1)}, bf16[4,64,5120]{2,1,0:T(8,128)(2,1)}, u32[]{:S(2)}) %copy-start) | copy-done | bytes 2621464
  9.3 1.5 %pick_factors.1 = (bf16[8,320,128]{2,1,0:T(8,128)(2,1)S(1)}, bf16[4,320,128]{2,1,0:T(8,128)(2,1)S(1)}, bf16[4,320,128]{2,1,0:T(8,128)(2,1)S(1)}, bf16[8,256,128]...) custom-call(s32[1]{0:T(128)} %bitcast.me_ref, s32[64]{0:T(128)S(1)} %copy-done.7, ...), custom_call_target="tpu_custom_call" | custom-call | bytes 4718592 | tf_op jit(solution)/shard_map/pick_factors/pallas_call | solution.py:250
  10.8 0.2 collective-permute-start
  11.0 2.0 %collective-permute-done.refs_1_ = bf16[8,320,128]{2,1,0:T(8,128)(2,1)S(1)} collective-permute-done((bf16[8,320,128]{2,1,0:T(8,128)(2,1)S(1)}, bf16[8,320,128]{2,1,0:T(8,128)(2,1)S(1)}, u32[]{:S(2)}, u32[]{:S(2)}) %collective-permute-start) | collective-permute-done | bytes 655392 | tf_op jit(solution)/shard_map/ppermute | solution.py:203
  13.0 0.1 halve.2
  13.0 0.0 copy-start.9
  13.0 0.2 collective-permute-start.1
  13.2 1.6 %collective-permute-start.2 = (bf16[4,320,128]{2,1,0:T(8,128)(2,1)S(1)}, bf16[4,320,128]{2,1,0:T(8,128)(2,1)S(1)}, u32[]{:S(2)}, u32[]{:S(2)}) collective-permute-start(bf16[4,320,128]{2,1,0:T(8,128)(2,1)S(1)} %halve.2), channel_id=1, source_target_pairs={{0,2},{1,3},{2,0},{3,1},{4,6},{5,7},{6,4},{7,5},{8,10},{9,11},{10,... | collective-permute-start | bytes 983048 | tf_op jit(solution)/shard_map/ppermute | solution.py:203
  14.9 0.2 collective-permute-done.1.refs_1_
  15.0 0.1 halve.3
  15.1 1.5 collective-permute-start.6
  16.5 10.4 %collective-permute-done.2.refs_2_ = bf16[4,320,128]{2,1,0:T(8,128)(2,1)S(1)} collective-permute-done((bf16[4,320,128]{2,1,0:T(8,128)(2,1)S(1)}, bf16[4,320,128]{2,1,0:T(8,128)(2,1)S(1)}, u32[]{:S(2)}, u32[]{:S(2)}) %collective-permute-start.2) | collective-permute-done | bytes 327712 | tf_op jit(solution)/shard_map/ppermute | solution.py:203
  26.9 0.1 split.3
  27.0 3.2 %collective-permute-start.3 = (bf16[1,320,128]{2,1,0:T(8,128)(2,1)S(1)}, bf16[1,320,128]{2,1,0:T(8,128)(2,1)S(1)}, u32[]{:S(2)}, u32[]{:S(2)}) collective-permute-start(bf16[1,320,128]{2,1,0:T(8,128)(2,1)S(1)} %get-tuple-element.37), channel_id=1, source_target_pairs={{0,8},{1,9},{2,10},{3,11},{4,12},{5,13},{6,14},{7,15},{8,0},{9,1},... | collective-permute-start | bytes 245768 | tf_op jit(solution)/shard_map/ppermute | solution.py:203
  30.2 0.0 collective-permute-start.4
  30.2 1.7 %collective-permute-start.5 = (bf16[1,320,128]{2,1,0:T(8,128)(2,1)S(1)}, bf16[1,320,128]{2,1,0:T(8,128)(2,1)S(1)}, u32[]{:S(2)}, u32[]{:S(2)}) collective-permute-start(bf16[1,320,128]{2,1,0:T(8,128)(2,1)S(1)} %get-tuple-element.39), channel_id=1, source_target_pairs={{0,12},{1,13},{2,14},{3,15},{4,8},{5,9},{6,10},{7,11},{8,4},{9,5},... | collective-permute-start | bytes 245768 | tf_op jit(solution)/shard_map/ppermute | solution.py:203
  31.9 5.8 %collective-permute-done.3.refs_1_ = bf16[1,320,128]{2,1,0:T(8,128)(2,1)S(1)} collective-permute-done((bf16[1,320,128]{2,1,0:T(8,128)(2,1)S(1)}, bf16[1,320,128]{2,1,0:T(8,128)(2,1)S(1)}, u32[]{:S(2)}, u32[]{:S(2)}) %collective-permute-start.3) | collective-permute-done | bytes 81952 | tf_op jit(solution)/shard_map/ppermute | solution.py:203
  37.7 3.0 %collective-permute-start.9 = (bf16[1,320,128]{2,1,0:T(8,128)(2,1)S(1)}, bf16[1,320,128]{2,1,0:T(8,128)(2,1)S(1)}, u32[]{:S(2)}, u32[]{:S(2)}) collective-permute-start(bf16[1,320,128]{2,1,0:T(8,128)(2,1)S(1)} %total.2.refs_0_), channel_id=1, source_target_pairs={{0,8},{1,9},{2,10},{3,11},{4,12},{5,13},{6,14},{7,15},{8,0},{9,1},... | collective-permute-start | bytes 245768 | tf_op jit(solution)/shard_map/ppermute | solution.py:203
  40.7 0.1 collective-permute-start.10
  40.8 2.0 %collective-permute-start.11 = (bf16[1,320,128]{2,1,0:T(8,128)(2,1)S(1)}, bf16[1,320,128]{2,1,0:T(8,128)(2,1)S(1)}, u32[]{:S(2)}, u32[]{:S(2)}) collective-permute-start(bf16[1,320,128]{2,1,0:T(8,128)(2,1)S(1)} %total.2.refs_0_), channel_id=1, source_target_pairs={{0,12},{1,13},{2,14},{3,15},{4,8},{5,9},{6,10},{7,11},{8,4},{9,5},... | collective-permute-start | bytes 245768 | tf_op jit(solution)/shard_map/ppermute | solution.py:203
  42.8 0.1 split.4
  42.9 0.6 copy-done.3
  43.5 0.6 collective-permute-start.7
  44.1 2.8 %pad_maximum_fusion = bf16[16,8,64,128]{3,2,1,0:T(8,128)(2,1)} fusion(bf16[16,4,64,128]{3,2,1,0:T(8,128)(2,1)S(1)} %bitcast.9, bf16[16,4,64,128]{3,2,1,0:T(8,128)(2,1)} %bitcast.10), kind=kLoop, calls=%fused_computation | loop fusion | flops 1048576 | bytes 4194304 | tf_op jit(solution)/shard_map/concatenate | solution.py:296
  46.9 0.7 collective-permute-done.11.refs_3_
  47.7 2.5 %collective-permute-done.7.refs_1_ = bf16[2,256,128]{2,1,0:T(8,128)(2,1)S(1)} collective-permute-done((bf16[2,256,128]{2,1,0:T(8,128)(2,1)S(1)}, bf16[2,256,128]{2,1,0:T(8,128)(2,1)S(1)}, u32[]{:S(2)}, u32[]{:S(2)}) %collective-permute-start.7) | collective-permute-done | bytes 131104 | tf_op jit(solution)/shard_map/ppermute | solution.py:203
  50.2 0.7 copy-done.5
  50.8 5.5 %all-to-all-start.1 = ((bf16[16,8,64,128]{3,2,1,0:T(8,128)(2,1)}), bf16[16,8,64,128]{3,2,1,0:T(8,128)(2,1)S(1)}, u32[]{:S(2)}, u32[]{:S(2)}) async-start(bf16[16,8,64,128]{3,2,1,0:T(8,128)(2,1)} %pad_maximum_fusion), calls=%async_computation.1 | async-start | bytes 4194304 | tf_op jit(solution)/shard_map/all_to_all | solution.py:206
  56.3 1.5 collective-permute-start.12
  57.8 24.3 %collective-permute-done.12.refs_1_ = bf16[4,320,128]{2,1,0:T(8,128)(2,1)S(1)} collective-permute-done((bf16[4,320,128]{2,1,0:T(8,128)(2,1)S(1)}, bf16[4,320,128]{2,1,0:T(8,128)(2,1)S(1)}, u32[]{:S(2)}, u32[]{:S(2)}) %collective-permute-start.12) | collective-permute-done | bytes 327712 | tf_op jit(solution)/shard_map/ppermute | solution.py:203
  82.1 1.3 collective-permute-start.13
  83.4 0.9 copy-done.4
  84.3 0.9 copy-done.6
  85.3 0.1 collective-permute-start.8
  85.4 0.9 low_rank.1.refs_0_
  86.2 0.2 collective-permute-start.14
  86.4 2.0 %collective-permute-start.16 = (bf16[2,32,128]{2,1,0:T(8,128)(2,1)S(1)}, bf16[2,32,128]{2,1,0:T(8,128)(2,1)S(1)}, u32[]{:S(2)}, u32[]{:S(2)}) collective-permute-start(bf16[2,32,128]{2,1,0:T(8,128)(2,1)S(1)} %low_rank.1.refs_0_), channel_id=1, source_target_pairs={{0,3},{1,2},{2,1},{3,0},{4,7},{5,6},{6,5},{7,4},{8,11},{9,10},{10,... | collective-permute-start | bytes 49160 | tf_op jit(solution)/shard_map/ppermute | solution.py:203
  88.4 0.6 collective-permute-done.15.refs_2_
  89.0 1.1 collective-permute-done.16.refs_3_
  90.1 5.2 %collective-permute-start.17 = (bf16[4,32,128]{2,1,0:T(8,128)(2,1)S(1)}, bf16[4,32,128]{2,1,0:T(8,128)(2,1)S(1)}, u32[]{:S(2)}, u32[]{:S(2)}) collective-permute-start(bf16[4,32,128]{2,1,0:T(8,128)(2,1)S(1)} %get-tuple-element.50), channel_id=1, source_target_pairs={{0,4},{1,5},{2,6},{3,7},{4,0},{5,1},{6,2},{7,3},{8,12},{9,13},{10,... | collective-permute-start | bytes 98312 | tf_op jit(solution)/shard_map/ppermute | solution.py:203
  95.4 2.2 %collective-permute-start.19 = (bf16[4,32,128]{2,1,0:T(8,128)(2,1)S(1)}, bf16[4,32,128]{2,1,0:T(8,128)(2,1)S(1)}, u32[]{:S(2)}, u32[]{:S(2)}) collective-permute-start(bf16[4,32,128]{2,1,0:T(8,128)(2,1)S(1)} %get-tuple-element.52), channel_id=1, source_target_pairs={{0,12},{1,13},{2,14},{3,15},{4,8},{5,9},{6,10},{7,11},{8,4},{9,5},... | collective-permute-start | bytes 98312 | tf_op jit(solution)/shard_map/ppermute | solution.py:203
  97.5 11.3 %collective-permute-done.8.refs_1_ = bf16[1,256,128]{2,1,0:T(8,128)(2,1)S(1)} collective-permute-done((bf16[1,256,128]{2,1,0:T(8,128)(2,1)S(1)}, bf16[1,256,128]{2,1,0:T(8,128)(2,1)S(1)}, u32[]{:S(2)}, u32[]{:S(2)}) %collective-permute-start.8) | collective-permute-done | bytes 65568 | tf_op jit(solution)/shard_map/ppermute | solution.py:203
  108.9 0.7 collective-permute-done.18.refs_2_
  109.6 7.2 %attend.1 = bf16[16,4,64,128]{3,2,1,0:T(8,128)(2,1)S(1)} custom-call(s32[1]{0:T(128)} %bitcast.me_ref, bf16[4,64,128]{2,1,0:T(8,128)(2,1)S(1)} %bitcast.6, bf16[16,8,64,128]{3,2,1,0:T(8,128)(2,1)S(1)} %all-to-all-done.1.q_ref.v_ref, bf16[16,4,64,128]{3,2,1,0:T(8,128)(2,1)S(1)} %all-to-all-done.k_ref, ...), custom_call_target="tpu_custom_call" | custom-call | flops 2147483648 | bytes 4194304 | tf_op jit(solution)/shard_map/attend/pallas_call | solution.py:346
  116.8 29.8 %all_to_all.15 = bf16[16,4,64,128]{3,2,1,0:T(8,128)(2,1)S(1)} all-to-all(bf16[16,4,64,128]{3,2,1,0:T(8,128)(2,1)S(1)} %attend.1), channel_id=1, replica_groups=mesh['grp'=2,'seq'=16] {'seq'}, dimensions={0} | all-to-all | bytes 2097152 | tf_op jit(solution)/shard_map/all_to_all | solution.py:206
  146.6 1.0 copy.10
  (32 shorter events, 0.2 us)
Async XLA Ops:
  0.0 7.5 %copy-start.7 = (s32[64]{0:T(128)S(1)}, s32[64]{0:T(128)}, u32[]{:S(2)}) copy-start(s32[64]{0:T(128)} %row_ref.1) | copy-start | bytes 772
  0.0 7.5 %copy-start.8 = (s32[2]{0:T(128)S(1)}, s32[2]{0:T(128)}, u32[]{:S(2)}) copy-start(s32[2]{0:T(128)} %req_ref.1) | copy-start | bytes 28
  0.0 7.5 %copy-start.1 = (bf16[4,64,4096]{2,1,0:T(8,128)(2,1)S(1)}, bf16[4,64,4096]{2,1,0:T(8,128)(2,1)}, u32[]{:S(2)}) copy-start(bf16[4,64,4096]{2,1,0:T(8,128)(2,1)} %up_ref.1) | copy-start | bytes 6291460
  0.0 37.7 %all-to-all-start = ((bf16[16,4,64,128]{3,2,1,0:T(8,128)(2,1)}), bf16[16,4,64,128]{3,2,1,0:T(8,128)(2,1)S(1)}, u32[]{:S(2)}, u32[]{:S(2)}) async-start(bf16[16,4,64,128]{3,2,1,0:T(8,128)(2,1)} %bitcast.8), calls=%async_computation | async-start | bytes 2097152 | tf_op jit(solution)/shard_map/all_to_all | solution.py:206
  7.5 1.7 %copy-start = (bf16[4,64,5120]{2,1,0:T(8,128)(2,1)S(1)}, bf16[4,64,5120]{2,1,0:T(8,128)(2,1)}, u32[]{:S(2)}) copy-start(bf16[4,64,5120]{2,1,0:T(8,128)(2,1)} %down_ref.1) | copy-start | bytes 7864324
  10.8 2.2 %collective-permute-start = (bf16[8,320,128]{2,1,0:T(8,128)(2,1)S(1)}, bf16[8,320,128]{2,1,0:T(8,128)(2,1)S(1)}, u32[]{:S(2)}, u32[]{:S(2)}) collective-permute-start(bf16[8,320,128]{2,1,0:T(8,128)(2,1)S(1)} %get-tuple-element.33), channel_id=1, source_target_pairs={{0,1},{1,0},{2,3},{3,2},{4,5},{5,4},{6,7},{7,6},{8,9},{9,8},{10,11... | collective-permute-start | bytes 1966088 | tf_op jit(solution)/shard_map/ppermute | solution.py:203
  13.0 31.1 %copy-start.9 = (bf16[2,32,64,128]{3,2,1,0:T(8,128)(2,1)S(1)}, bf16[2,32,64,128]{3,2,1,0:T(8,128)(2,1)}, u32[]{:S(2)}) copy-start(bf16[2,32,64,128]{3,2,1,0:T(8,128)(2,1)} %param.9) | copy-start | bytes 3145732
  13.0 2.0 %collective-permute-start.1 = (bf16[8,256,128]{2,1,0:T(8,128)(2,1)S(1)}, bf16[8,256,128]{2,1,0:T(8,128)(2,1)S(1)}, u32[]{:S(2)}, u32[]{:S(2)}) collective-permute-start(bf16[8,256,128]{2,1,0:T(8,128)(2,1)S(1)} %get-tuple-element.34), channel_id=1, source_target_pairs={{0,1},{1,0},{2,3},{3,2},{4,5},{5,4},{6,7},{7,6},{8,9},{9,8},{10,11... | collective-permute-start | bytes 1572872 | tf_op jit(solution)/shard_map/ppermute | solution.py:203
  13.2 13.6 %collective-permute-start.2 = (bf16[4,320,128]{2,1,0:T(8,128)(2,1)S(1)}, bf16[4,320,128]{2,1,0:T(8,128)(2,1)S(1)}, u32[]{:S(2)}, u32[]{:S(2)}) collective-permute-start(bf16[4,320,128]{2,1,0:T(8,128)(2,1)S(1)} %halve.2), channel_id=1, source_target_pairs={{0,2},{1,3},{2,0},{3,1},{4,6},{5,7},{6,4},{7,5},{8,10},{9,11},{10,... | collective-permute-start | bytes 983048 | tf_op jit(solution)/shard_map/ppermute | solution.py:203
  15.1 22.7 %collective-permute-start.6 = (bf16[4,256,128]{2,1,0:T(8,128)(2,1)S(1)}, bf16[4,256,128]{2,1,0:T(8,128)(2,1)S(1)}, u32[]{:S(2)}, u32[]{:S(2)}) collective-permute-start(bf16[4,256,128]{2,1,0:T(8,128)(2,1)S(1)} %halve.3), channel_id=1, source_target_pairs={{0,2},{1,3},{2,0},{3,1},{4,6},{5,7},{6,4},{7,5},{8,10},{9,11},{10,... | collective-permute-start | bytes 786440 | tf_op jit(solution)/shard_map/ppermute | solution.py:203
  27.0 10.7 %collective-permute-start.3 = (bf16[1,320,128]{2,1,0:T(8,128)(2,1)S(1)}, bf16[1,320,128]{2,1,0:T(8,128)(2,1)S(1)}, u32[]{:S(2)}, u32[]{:S(2)}) collective-permute-start(bf16[1,320,128]{2,1,0:T(8,128)(2,1)S(1)} %get-tuple-element.37), channel_id=1, source_target_pairs={{0,8},{1,9},{2,10},{3,11},{4,12},{5,13},{6,14},{7,15},{8,0},{9,1},... | collective-permute-start | bytes 245768 | tf_op jit(solution)/shard_map/ppermute | solution.py:203
  30.2 7.5 %collective-permute-start.4 = (bf16[1,320,128]{2,1,0:T(8,128)(2,1)S(1)}, bf16[1,320,128]{2,1,0:T(8,128)(2,1)S(1)}, u32[]{:S(2)}, u32[]{:S(2)}) collective-permute-start(bf16[1,320,128]{2,1,0:T(8,128)(2,1)S(1)} %get-tuple-element.38), channel_id=1, source_target_pairs={{0,4},{1,5},{2,6},{3,7},{4,0},{5,1},{6,2},{7,3},{8,12},{9,13},{10,... | collective-permute-start | bytes 245768 | tf_op jit(solution)/shard_map/ppermute | solution.py:203
  30.2 7.4 %collective-permute-start.5 = (bf16[1,320,128]{2,1,0:T(8,128)(2,1)S(1)}, bf16[1,320,128]{2,1,0:T(8,128)(2,1)S(1)}, u32[]{:S(2)}, u32[]{:S(2)}) collective-permute-start(bf16[1,320,128]{2,1,0:T(8,128)(2,1)S(1)} %get-tuple-element.39), channel_id=1, source_target_pairs={{0,12},{1,13},{2,14},{3,15},{4,8},{5,9},{6,10},{7,11},{8,4},{9,5},... | collective-permute-start | bytes 245768 | tf_op jit(solution)/shard_map/ppermute | solution.py:203
  37.7 9.1 %collective-permute-start.9 = (bf16[1,320,128]{2,1,0:T(8,128)(2,1)S(1)}, bf16[1,320,128]{2,1,0:T(8,128)(2,1)S(1)}, u32[]{:S(2)}, u32[]{:S(2)}) collective-permute-start(bf16[1,320,128]{2,1,0:T(8,128)(2,1)S(1)} %total.2.refs_0_), channel_id=1, source_target_pairs={{0,8},{1,9},{2,10},{3,11},{4,12},{5,13},{6,14},{7,15},{8,0},{9,1},... | collective-permute-start | bytes 245768 | tf_op jit(solution)/shard_map/ppermute | solution.py:203
  40.7 6.2 %collective-permute-start.10 = (bf16[1,320,128]{2,1,0:T(8,128)(2,1)S(1)}, bf16[1,320,128]{2,1,0:T(8,128)(2,1)S(1)}, u32[]{:S(2)}, u32[]{:S(2)}) collective-permute-start(bf16[1,320,128]{2,1,0:T(8,128)(2,1)S(1)} %total.2.refs_0_), channel_id=1, source_target_pairs={{0,4},{1,5},{2,6},{3,7},{4,0},{5,1},{6,2},{7,3},{8,12},{9,13},{10,... | collective-permute-start | bytes 245768 | tf_op jit(solution)/shard_map/ppermute | solution.py:203
  40.8 6.8 %collective-permute-start.11 = (bf16[1,320,128]{2,1,0:T(8,128)(2,1)S(1)}, bf16[1,320,128]{2,1,0:T(8,128)(2,1)S(1)}, u32[]{:S(2)}, u32[]{:S(2)}) collective-permute-start(bf16[1,320,128]{2,1,0:T(8,128)(2,1)S(1)} %total.2.refs_0_), channel_id=1, source_target_pairs={{0,12},{1,13},{2,14},{3,15},{4,8},{5,9},{6,10},{7,11},{8,4},{9,5},... | collective-permute-start | bytes 245768 | tf_op jit(solution)/shard_map/ppermute | solution.py:203
  42.9 0.7 copy-start.3
  43.5 6.6 %collective-permute-start.7 = (bf16[2,256,128]{2,1,0:T(8,128)(2,1)S(1)}, bf16[2,256,128]{2,1,0:T(8,128)(2,1)S(1)}, u32[]{:S(2)}, u32[]{:S(2)}) collective-permute-start(bf16[2,256,128]{2,1,0:T(8,128)(2,1)S(1)} %get-tuple-element.45), channel_id=1, source_target_pairs={{0,4},{1,5},{2,6},{3,7},{4,0},{5,1},{6,2},{7,3},{8,12},{9,13},{10,... | collective-permute-start | bytes 393224 | tf_op jit(solution)/shard_map/ppermute | solution.py:203
  50.2 0.7 copy-start.5
  50.8 58.7 %all-to-all-start.1 = ((bf16[16,8,64,128]{3,2,1,0:T(8,128)(2,1)}), bf16[16,8,64,128]{3,2,1,0:T(8,128)(2,1)S(1)}, u32[]{:S(2)}, u32[]{:S(2)}) async-start(bf16[16,8,64,128]{3,2,1,0:T(8,128)(2,1)} %pad_maximum_fusion), calls=%async_computation.1 | async-start | bytes 4194304 | tf_op jit(solution)/shard_map/all_to_all | solution.py:206
  56.3 29.0 %copy-start.2 = (bf16[2,64,5120]{2,1,0:T(8,128)(2,1)S(1)}, bf16[2,64,5120]{2,1,0:T(8,128)(2,1)}, u32[]{:S(2)}) copy-start(bf16[2,64,5120]{2,1,0:T(8,128)(2,1)} %x_ref.1) | copy-start | bytes 3932164
  56.3 25.8 %collective-permute-start.12 = (bf16[4,320,128]{2,1,0:T(8,128)(2,1)S(1)}, bf16[4,320,128]{2,1,0:T(8,128)(2,1)S(1)}, u32[]{:S(2)}, u32[]{:S(2)}) collective-permute-start(bf16[4,320,128]{2,1,0:T(8,128)(2,1)S(1)} %join.2.refs_0_), channel_id=1, source_target_pairs={{0,2},{1,3},{2,0},{3,1},{4,6},{5,7},{6,4},{7,5},{8,10},{9,11},{10,... | collective-permute-start | bytes 983048 | tf_op jit(solution)/shard_map/ppermute | solution.py:203
  82.1 3.2 %collective-permute-start.13 = (bf16[8,320,128]{2,1,0:T(8,128)(2,1)S(1)}, bf16[8,320,128]{2,1,0:T(8,128)(2,1)S(1)}, u32[]{:S(2)}, u32[]{:S(2)}) collective-permute-start(bf16[8,320,128]{2,1,0:T(8,128)(2,1)S(1)} %join.3.refs_0_), channel_id=1, source_target_pairs={{0,1},{1,0},{2,3},{3,2},{4,5},{5,4},{6,7},{7,6},{8,9},{9,8},{10,11... | collective-permute-start | bytes 1966088 | tf_op jit(solution)/shard_map/ppermute | solution.py:203
  83.4 0.9 copy-start.4
  84.3 0.9 copy-start.6
  85.3 23.6 %collective-permute-start.8 = (bf16[1,256,128]{2,1,0:T(8,128)(2,1)S(1)}, bf16[1,256,128]{2,1,0:T(8,128)(2,1)S(1)}, u32[]{:S(2)}, u32[]{:S(2)}) collective-permute-start(bf16[1,256,128]{2,1,0:T(8,128)(2,1)S(1)} %get-tuple-element.47), channel_id=1, source_target_pairs={{0,8},{1,9},{2,10},{3,11},{4,12},{5,13},{6,14},{7,15},{8,0},{9,1},... | collective-permute-start | bytes 196616 | tf_op jit(solution)/shard_map/ppermute | solution.py:203
  86.2 2.2 %collective-permute-start.14 = (bf16[2,32,128]{2,1,0:T(8,128)(2,1)S(1)}, bf16[2,32,128]{2,1,0:T(8,128)(2,1)S(1)}, u32[]{:S(2)}, u32[]{:S(2)}) collective-permute-start(bf16[2,32,128]{2,1,0:T(8,128)(2,1)S(1)} %low_rank.1.refs_0_), channel_id=1, source_target_pairs={{0,1},{1,0},{2,3},{3,2},{4,5},{5,4},{6,7},{7,6},{8,9},{9,8},{10,11... | collective-permute-start | bytes 49160 | tf_op jit(solution)/shard_map/ppermute | solution.py:203
  86.4 2.6 %collective-permute-start.15 = (bf16[2,32,128]{2,1,0:T(8,128)(2,1)S(1)}, bf16[2,32,128]{2,1,0:T(8,128)(2,1)S(1)}, u32[]{:S(2)}, u32[]{:S(2)}) collective-permute-start(bf16[2,32,128]{2,1,0:T(8,128)(2,1)S(1)} %low_rank.1.refs_0_), channel_id=1, source_target_pairs={{0,2},{1,3},{2,0},{3,1},{4,6},{5,7},{6,4},{7,5},{8,10},{9,11},{10,... | collective-permute-start | bytes 49160 | tf_op jit(solution)/shard_map/ppermute | solution.py:203
  86.4 3.7 %collective-permute-start.16 = (bf16[2,32,128]{2,1,0:T(8,128)(2,1)S(1)}, bf16[2,32,128]{2,1,0:T(8,128)(2,1)S(1)}, u32[]{:S(2)}, u32[]{:S(2)}) collective-permute-start(bf16[2,32,128]{2,1,0:T(8,128)(2,1)S(1)} %low_rank.1.refs_0_), channel_id=1, source_target_pairs={{0,3},{1,2},{2,1},{3,0},{4,7},{5,6},{6,5},{7,4},{8,11},{9,10},{10,... | collective-permute-start | bytes 49160 | tf_op jit(solution)/shard_map/ppermute | solution.py:203
  90.1 18.8 %collective-permute-start.17 = (bf16[4,32,128]{2,1,0:T(8,128)(2,1)S(1)}, bf16[4,32,128]{2,1,0:T(8,128)(2,1)S(1)}, u32[]{:S(2)}, u32[]{:S(2)}) collective-permute-start(bf16[4,32,128]{2,1,0:T(8,128)(2,1)S(1)} %get-tuple-element.50), channel_id=1, source_target_pairs={{0,4},{1,5},{2,6},{3,7},{4,0},{5,1},{6,2},{7,3},{8,12},{9,13},{10,... | collective-permute-start | bytes 98312 | tf_op jit(solution)/shard_map/ppermute | solution.py:203
  95.4 14.2 %collective-permute-start.18 = (bf16[4,32,128]{2,1,0:T(8,128)(2,1)S(1)}, bf16[4,32,128]{2,1,0:T(8,128)(2,1)S(1)}, u32[]{:S(2)}, u32[]{:S(2)}) collective-permute-start(bf16[4,32,128]{2,1,0:T(8,128)(2,1)S(1)} %get-tuple-element.51), channel_id=1, source_target_pairs={{0,8},{1,9},{2,10},{3,11},{4,12},{5,13},{6,14},{7,15},{8,0},{9,1},... | collective-permute-start | bytes 98312 | tf_op jit(solution)/shard_map/ppermute | solution.py:203
  95.4 14.2 %collective-permute-start.19 = (bf16[4,32,128]{2,1,0:T(8,128)(2,1)S(1)}, bf16[4,32,128]{2,1,0:T(8,128)(2,1)S(1)}, u32[]{:S(2)}, u32[]{:S(2)}) collective-permute-start(bf16[4,32,128]{2,1,0:T(8,128)(2,1)S(1)} %get-tuple-element.52), channel_id=1, source_target_pairs={{0,12},{1,13},{2,14},{3,15},{4,8},{5,9},{6,10},{7,11},{8,4},{9,5},... | collective-permute-start | bytes 98312 | tf_op jit(solution)/shard_map/ppermute | solution.py:203

commit v28 on v24

--- a/solution.py
+++ b/solution.py
@@ -334,6 +334,7 @@
         in_specs=[SMEM] + [VMEM] * LOW,
         out_specs=[VMEM] * quarter,
         out_shape=[jax.ShapeDtypeStruct((LOW,) + low_shape[1:], jnp.bfloat16)] * quarter,
+        compiler_params=pltpu.CompilerParams(vmem_limit_bytes=16 << 20),
         cost_estimate=pl.CostEstimate(flops=0, bytes_accessed=8 * low.size, transcendentals=0),
         name="choose",
     )(me, *nearby)

time: 150 us -> 147 us (0.980)
    unnamed x21 -> x11, local copies, waits for them, and re-layouts: 4.08 us -> 2.72 us
  transfers between devices with their start and end apart: 22 -> 22, of which waited for: 12 -> 12; matrix products, arithmetic and copies ran while one was open for 2% -> 2% of each run, Pallas kernels for 3% -> 2%
where the time goes in v28:
time: 147 us; the launch traced here: 146 us
  waiting for transfers between devices  58.3 us (40%)
  starting transfers between devices  40.3 us (27%)
  blocking collectives  30.8 us (21%)
  Pallas kernels  10.9 us (7%)
  other arithmetic  3.08 us (2%)
  local copies, waits for them, and re-layouts  2.72 us (2%)
    ppermute x20, waiting for transfers between devices, swap(): return lax.ppermute(tensor, 'seq', [(i, i ^ k) for i in range(devs)])  58.3 us
    all_to_all x1, blocking collectives, exchange(): lax.all_to_all(tensor, 'seq', split_axis=0, concat_axis=0, tiled=True)  30.8 us
    ppermute x20, starting transfers between devices, swap(): return lax.ppermute(tensor, 'seq', [(i, i ^ k) for i in range(devs)])  26.9 us
    all_to_all x2, starting transfers between devices, exchange(): lax.all_to_all(tensor, 'seq', split_axis=0, concat_axis=0, tiled=True)  13.4 us
    pallas_call x1, Pallas kernels, body(): pl.pallas_call(functools.partial(attend_kernel, math.gcd(devs, max(1, 256...  8.06 us
    concatenate x1, other arithmetic, body(): asked = jnp.concatenate([by_pairs(values), by_pairs(queries)], axis=1)  3.08 us
  transfers between devices with their start and end apart: 22, of which 12 were waited for; matrix products, arithmetic and copies ran while one was open for 2% of the time, Pallas kernels for 2%

profile of v28, /device:TPU:1, one launch (start us, length us, event | category | flops | bytes accessed | tf_op | source)
XLA Modules:
  0.0 146.3 jit_solution(17561672131400425676)
XLA Ops:
  0.0 7.5 %all-to-all-start = ((bf16[16,4,64,128]{3,2,1,0:T(8,128)(2,1)}), bf16[16,4,64,128]{3,2,1,0:T(8,128)(2,1)}, u32[]{:S(2)}, u32[]{:S(2)}) async-start(bf16[16,4,64,128]{3,2,1,0:T(8,128)(2,1)} %bitcast.8), calls=%async_computation | async-start | bytes 2097152 | tf_op jit(solution)/shard_map/all_to_all | solution.py:206
  7.5 0.0 copy-start
  7.5 1.7 %copy-done = bf16[4,64,5120]{2,1,0:T(8,128)(2,1)S(1)} copy-done((bf16[4,64,5120]{2,1,0:T(8,128)(2,1)S(1)}, bf16[4,64,5120]{2,1,0:T(8,128)(2,1)}, u32[]{:S(2)}) %copy-start) | copy-done | bytes 2621464
  9.3 1.5 %pick_factors.1 = (bf16[8,320,128]{2,1,0:T(8,128)(2,1)S(1)}, bf16[4,320,128]{2,1,0:T(8,128)(2,1)S(1)}, bf16[4,320,128]{2,1,0:T(8,128)(2,1)S(1)}, bf16[8,256,128]...) custom-call(s32[1]{0:T(128)} %bitcast.me_ref, s32[64]{0:T(128)S(1)} %copy-done.3, ...), custom_call_target="tpu_custom_call" | custom-call | bytes 4718592 | tf_op jit(solution)/shard_map/pick_factors/pallas_call | solution.py:250
  10.8 0.2 collective-permute-start
  11.0 1.9 %collective-permute-done.refs_1_ = bf16[8,320,128]{2,1,0:T(8,128)(2,1)S(1)} collective-permute-done((bf16[8,320,128]{2,1,0:T(8,128)(2,1)S(1)}, bf16[8,320,128]{2,1,0:T(8,128)(2,1)S(1)}, u32[]{:S(2)}, u32[]{:S(2)}) %collective-permute-start) | collective-permute-done | bytes 655392 | tf_op jit(solution)/shard_map/ppermute | solution.py:203
  13.0 0.1 halve.2
  13.0 0.2 collective-permute-start.1
  13.3 1.8 %collective-permute-start.2 = (bf16[4,320,128]{2,1,0:T(8,128)(2,1)S(1)}, bf16[4,320,128]{2,1,0:T(8,128)(2,1)S(1)}, u32[]{:S(2)}, u32[]{:S(2)}) collective-permute-start(bf16[4,320,128]{2,1,0:T(8,128)(2,1)S(1)} %halve.2), channel_id=1, source_target_pairs={{0,2},{1,3},{2,0},{3,1},{4,6},{5,7},{6,4},{7,5},{8,10},{9,11},{10,... | collective-permute-start | bytes 983048 | tf_op jit(solution)/shard_map/ppermute | solution.py:203
  15.0 0.0 collective-permute-done.1.refs_1_
  15.0 0.1 halve.3
  15.1 1.6 %collective-permute-start.6 = (bf16[4,256,128]{2,1,0:T(8,128)(2,1)S(1)}, bf16[4,256,128]{2,1,0:T(8,128)(2,1)S(1)}, u32[]{:S(2)}, u32[]{:S(2)}) collective-permute-start(bf16[4,256,128]{2,1,0:T(8,128)(2,1)S(1)} %halve.3), channel_id=1, source_target_pairs={{0,2},{1,3},{2,0},{3,1},{4,6},{5,7},{6,4},{7,5},{8,10},{9,11},{10,... | collective-permute-start | bytes 786440 | tf_op jit(solution)/shard_map/ppermute | solution.py:203
  16.7 10.2 %collective-permute-done.2.refs_2_ = bf16[4,320,128]{2,1,0:T(8,128)(2,1)S(1)} collective-permute-done((bf16[4,320,128]{2,1,0:T(8,128)(2,1)S(1)}, bf16[4,320,128]{2,1,0:T(8,128)(2,1)S(1)}, u32[]{:S(2)}, u32[]{:S(2)}) %collective-permute-start.2) | collective-permute-done | bytes 327712 | tf_op jit(solution)/shard_map/ppermute | solution.py:203
  26.9 0.1 split.3
  27.0 3.3 %collective-permute-start.3 = (bf16[1,320,128]{2,1,0:T(8,128)(2,1)S(1)}, bf16[1,320,128]{2,1,0:T(8,128)(2,1)S(1)}, u32[]{:S(2)}, u32[]{:S(2)}) collective-permute-start(bf16[1,320,128]{2,1,0:T(8,128)(2,1)S(1)} %get-tuple-element.37), channel_id=1, source_target_pairs={{0,8},{1,9},{2,10},{3,11},{4,12},{5,13},{6,14},{7,15},{8,0},{9,1},... | collective-permute-start | bytes 245768 | tf_op jit(solution)/shard_map/ppermute | solution.py:203
  30.2 0.0 collective-permute-start.4
  30.2 1.7 %collective-permute-start.5 = (bf16[1,320,128]{2,1,0:T(8,128)(2,1)S(1)}, bf16[1,320,128]{2,1,0:T(8,128)(2,1)S(1)}, u32[]{:S(2)}, u32[]{:S(2)}) collective-permute-start(bf16[1,320,128]{2,1,0:T(8,128)(2,1)S(1)} %get-tuple-element.39), channel_id=1, source_target_pairs={{0,12},{1,13},{2,14},{3,15},{4,8},{5,9},{6,10},{7,11},{8,4},{9,5},... | collective-permute-start | bytes 245768 | tf_op jit(solution)/shard_map/ppermute | solution.py:203
  31.9 5.8 %collective-permute-done.3.refs_1_ = bf16[1,320,128]{2,1,0:T(8,128)(2,1)S(1)} collective-permute-done((bf16[1,320,128]{2,1,0:T(8,128)(2,1)S(1)}, bf16[1,320,128]{2,1,0:T(8,128)(2,1)S(1)}, u32[]{:S(2)}, u32[]{:S(2)}) %collective-permute-start.3) | collective-permute-done | bytes 81952 | tf_op jit(solution)/shard_map/ppermute | solution.py:203
  37.7 0.0 collective-permute-done.5.refs_3_
  37.7 3.0 %collective-permute-start.7 = (bf16[1,320,128]{2,1,0:T(8,128)(2,1)S(1)}, bf16[1,320,128]{2,1,0:T(8,128)(2,1)S(1)}, u32[]{:S(2)}, u32[]{:S(2)}) collective-permute-start(bf16[1,320,128]{2,1,0:T(8,128)(2,1)S(1)} %total.2.refs_0_), channel_id=1, source_target_pairs={{0,8},{1,9},{2,10},{3,11},{4,12},{5,13},{6,14},{7,15},{8,0},{9,1},... | collective-permute-start | bytes 245768 | tf_op jit(solution)/shard_map/ppermute | solution.py:203
  40.7 0.1 collective-permute-start.8
  40.8 2.0 %collective-permute-start.9 = (bf16[1,320,128]{2,1,0:T(8,128)(2,1)S(1)}, bf16[1,320,128]{2,1,0:T(8,128)(2,1)S(1)}, u32[]{:S(2)}, u32[]{:S(2)}) collective-permute-start(bf16[1,320,128]{2,1,0:T(8,128)(2,1)S(1)} %total.2.refs_0_), channel_id=1, source_target_pairs={{0,12},{1,13},{2,14},{3,15},{4,8},{5,9},{6,10},{7,11},{8,4},{9,5},... | collective-permute-start | bytes 245768 | tf_op jit(solution)/shard_map/ppermute | solution.py:203
  42.8 3.1 %pad_maximum_fusion = bf16[16,8,64,128]{3,2,1,0:T(8,128)(2,1)} fusion(bf16[16,4,64,128]{3,2,1,0:T(8,128)(2,1)} %bitcast.9, bf16[16,4,64,128]{3,2,1,0:T(8,128)(2,1)} %bitcast.10), kind=kLoop, calls=%fused_computation | loop fusion | flops 1048576 | bytes 4194304 | tf_op jit(solution)/shard_map/concatenate | solution.py:288
  45.9 1.7 %collective-permute-done.9.refs_3_ = bf16[1,320,128]{2,1,0:T(8,128)(2,1)S(1)} collective-permute-done((bf16[1,320,128]{2,1,0:T(8,128)(2,1)S(1)}, bf16[1,320,128]{2,1,0:T(8,128)(2,1)S(1)}, u32[]{:S(2)}, u32[]{:S(2)}) %collective-permute-start.9) | collective-permute-done | bytes 81952 | tf_op jit(solution)/shard_map/ppermute | solution.py:203
  47.7 5.9 %all-to-all-start.1 = ((bf16[16,8,64,128]{3,2,1,0:T(8,128)(2,1)}), bf16[16,8,64,128]{3,2,1,0:T(8,128)(2,1)S(1)}, u32[]{:S(2)}, u32[]{:S(2)}) async-start(bf16[16,8,64,128]{3,2,1,0:T(8,128)(2,1)} %pad_maximum_fusion), calls=%async_computation.1 | async-start | bytes 4194304 | tf_op jit(solution)/shard_map/all_to_all | solution.py:206
  53.5 1.5 collective-permute-start.10
  55.0 24.3 %collective-permute-done.10.refs_1_ = bf16[4,320,128]{2,1,0:T(8,128)(2,1)S(1)} collective-permute-done((bf16[4,320,128]{2,1,0:T(8,128)(2,1)S(1)}, bf16[4,320,128]{2,1,0:T(8,128)(2,1)S(1)}, u32[]{:S(2)}, u32[]{:S(2)}) %collective-permute-start.10) | collective-permute-done | bytes 327712 | tf_op jit(solution)/shard_map/ppermute | solution.py:203
  79.3 1.3 collective-permute-start.11
  80.6 1.7 %collective-permute-done.11.refs_1_ = bf16[8,320,128]{2,1,0:T(8,128)(2,1)S(1)} collective-permute-done((bf16[8,320,128]{2,1,0:T(8,128)(2,1)S(1)}, bf16[8,320,128]{2,1,0:T(8,128)(2,1)S(1)}, u32[]{:S(2)}, u32[]{:S(2)}) %collective-permute-start.11) | collective-permute-done | bytes 655392 | tf_op jit(solution)/shard_map/ppermute | solution.py:203
  82.4 0.9 low_rank.1.refs_0_
  83.2 0.1 split.4
  83.3 0.1 collective-permute-start.12
  83.4 7.4 %collective-permute-done.12.refs_1_ = bf16[2,256,128]{2,1,0:T(8,128)(2,1)S(1)} collective-permute-done((bf16[2,256,128]{2,1,0:T(8,128)(2,1)S(1)}, bf16[2,256,128]{2,1,0:T(8,128)(2,1)S(1)}, u32[]{:S(2)}, u32[]{:S(2)}) %collective-permute-start.12) | collective-permute-done | bytes 131104 | tf_op jit(solution)/shard_map/ppermute | solution.py:203
  90.9 3.9 %collective-permute-start.13 = (bf16[1,256,128]{2,1,0:T(8,128)(2,1)S(1)}, bf16[1,256,128]{2,1,0:T(8,128)(2,1)S(1)}, u32[]{:S(2)}, u32[]{:S(2)}) collective-permute-start(bf16[1,256,128]{2,1,0:T(8,128)(2,1)S(1)} %get-tuple-element.47), channel_id=1, source_target_pairs={{0,8},{1,9},{2,10},{3,11},{4,12},{5,13},{6,14},{7,15},{8,0},{9,1},... | collective-permute-start | bytes 196616 | tf_op jit(solution)/shard_map/ppermute | solution.py:203
  94.8 1.2 collective-permute-start.14
  95.9 1.3 collective-permute-start.15
  97.2 0.3 collective-permute-start.16
  97.6 1.0 collective-permute-done.15.refs_2_
  98.5 1.9 %collective-permute-done.16.refs_3_ = bf16[2,32,128]{2,1,0:T(8,128)(2,1)S(1)} collective-permute-done((bf16[2,32,128]{2,1,0:T(8,128)(2,1)S(1)}, bf16[2,32,128]{2,1,0:T(8,128)(2,1)S(1)}, u32[]{:S(2)}, u32[]{:S(2)}) %collective-permute-start.16) | collective-permute-done | bytes 16416 | tf_op jit(solution)/shard_map/ppermute | solution.py:203
  100.4 0.1 collective-permute-start.17
  100.5 1.1 collective-permute-start.18
  101.6 2.4 %collective-permute-start.19 = (bf16[4,32,128]{2,1,0:T(8,128)(2,1)S(1)}, bf16[4,32,128]{2,1,0:T(8,128)(2,1)S(1)}, u32[]{:S(2)}, u32[]{:S(2)}) collective-permute-start(bf16[4,32,128]{2,1,0:T(8,128)(2,1)S(1)} %get-tuple-element.52), channel_id=1, source_target_pairs={{0,12},{1,13},{2,14},{3,15},{4,8},{5,9},{6,10},{7,11},{8,4},{9,5},... | collective-permute-start | bytes 98312 | tf_op jit(solution)/shard_map/ppermute | solution.py:203
  104.0 0.6 collective-permute-done.13.refs_1_
  104.7 0.7 collective-permute-done.18.refs_2_
  105.4 1.0 collective-permute-done.19.refs_3_
  106.4 8.1 %attend.1 = bf16[16,4,64,128]{3,2,1,0:T(8,128)(2,1)S(1)} custom-call(s32[1]{0:T(128)} %bitcast.me_ref, bf16[4,64,128]{2,1,0:T(8,128)(2,1)S(1)} %bitcast.6, bf16[16,8,64,128]{3,2,1,0:T(8,128)(2,1)S(1)} %all-to-all-done.1.q_ref.v_ref, bf16[16,4,64,128]{3,2,1,0:T(8,128)(2,1)} %all-to-all-done.k_ref, bf16[16,8,64,128]{3,2,1,0:T(8,128)(2,1)S(1)} %all-to-all-done.1.q_ref.v_ref, ...), custom_call_target="tpu_custom_call" | custom-call | flops 2147483648 | bytes 4194304 | tf_op jit(solution)/shard_map/attend/pallas_call | solution.py:346
  114.5 30.8 %all_to_all.15 = bf16[16,4,64,128]{3,2,1,0:T(8,128)(2,1)S(1)} all-to-all(bf16[16,4,64,128]{3,2,1,0:T(8,128)(2,1)S(1)} %attend.1), channel_id=1, replica_groups=mesh['grp'=2,'seq'=16] {'seq'}, dimensions={0} | all-to-all | bytes 2097152 | tf_op jit(solution)/shard_map/all_to_all | solution.py:206
  145.3 1.0 copy.10
  (22 shorter events, 0.2 us)
Async XLA Ops:
  0.0 7.5 %copy-start.3 = (s32[64]{0:T(128)S(1)}, s32[64]{0:T(128)}, u32[]{:S(2)}) copy-start(s32[64]{0:T(128)} %row_ref.1) | copy-start | bytes 772
  0.0 7.5 %copy-start.4 = (s32[2]{0:T(128)S(1)}, s32[2]{0:T(128)}, u32[]{:S(2)}) copy-start(s32[2]{0:T(128)} %req_ref.1) | copy-start | bytes 28
  0.0 7.5 %copy-start.1 = (bf16[4,64,4096]{2,1,0:T(8,128)(2,1)S(1)}, bf16[4,64,4096]{2,1,0:T(8,128)(2,1)}, u32[]{:S(2)}) copy-start(bf16[4,64,4096]{2,1,0:T(8,128)(2,1)} %up_ref.1) | copy-start | bytes 6291460
  0.0 37.7 %all-to-all-start = ((bf16[16,4,64,128]{3,2,1,0:T(8,128)(2,1)}), bf16[16,4,64,128]{3,2,1,0:T(8,128)(2,1)}, u32[]{:S(2)}, u32[]{:S(2)}) async-start(bf16[16,4,64,128]{3,2,1,0:T(8,128)(2,1)} %bitcast.8), calls=%async_computation | async-start | bytes 2097152 | tf_op jit(solution)/shard_map/all_to_all | solution.py:206
  7.5 1.7 %copy-start = (bf16[4,64,5120]{2,1,0:T(8,128)(2,1)S(1)}, bf16[4,64,5120]{2,1,0:T(8,128)(2,1)}, u32[]{:S(2)}) copy-start(bf16[4,64,5120]{2,1,0:T(8,128)(2,1)} %down_ref.1) | copy-start | bytes 7864324
  10.8 2.2 %collective-permute-start = (bf16[8,320,128]{2,1,0:T(8,128)(2,1)S(1)}, bf16[8,320,128]{2,1,0:T(8,128)(2,1)S(1)}, u32[]{:S(2)}, u32[]{:S(2)}) collective-permute-start(bf16[8,320,128]{2,1,0:T(8,128)(2,1)S(1)} %get-tuple-element.33), channel_id=1, source_target_pairs={{0,1},{1,0},{2,3},{3,2},{4,5},{5,4},{6,7},{7,6},{8,9},{9,8},{10,11... | collective-permute-start | bytes 1966088 | tf_op jit(solution)/shard_map/ppermute | solution.py:203
  13.0 2.0 %collective-permute-start.1 = (bf16[8,256,128]{2,1,0:T(8,128)(2,1)S(1)}, bf16[8,256,128]{2,1,0:T(8,128)(2,1)S(1)}, u32[]{:S(2)}, u32[]{:S(2)}) collective-permute-start(bf16[8,256,128]{2,1,0:T(8,128)(2,1)S(1)} %get-tuple-element.34), channel_id=1, source_target_pairs={{0,1},{1,0},{2,3},{3,2},{4,5},{5,4},{6,7},{7,6},{8,9},{9,8},{10,11... | collective-permute-start | bytes 1572872 | tf_op jit(solution)/shard_map/ppermute | solution.py:203
  13.3 13.6 %collective-permute-start.2 = (bf16[4,320,128]{2,1,0:T(8,128)(2,1)S(1)}, bf16[4,320,128]{2,1,0:T(8,128)(2,1)S(1)}, u32[]{:S(2)}, u32[]{:S(2)}) collective-permute-start(bf16[4,320,128]{2,1,0:T(8,128)(2,1)S(1)} %halve.2), channel_id=1, source_target_pairs={{0,2},{1,3},{2,0},{3,1},{4,6},{5,7},{6,4},{7,5},{8,10},{9,11},{10,... | collective-permute-start | bytes 983048 | tf_op jit(solution)/shard_map/ppermute | solution.py:203
  15.1 22.7 %collective-permute-start.6 = (bf16[4,256,128]{2,1,0:T(8,128)(2,1)S(1)}, bf16[4,256,128]{2,1,0:T(8,128)(2,1)S(1)}, u32[]{:S(2)}, u32[]{:S(2)}) collective-permute-start(bf16[4,256,128]{2,1,0:T(8,128)(2,1)S(1)} %halve.3), channel_id=1, source_target_pairs={{0,2},{1,3},{2,0},{3,1},{4,6},{5,7},{6,4},{7,5},{8,10},{9,11},{10,... | collective-permute-start | bytes 786440 | tf_op jit(solution)/shard_map/ppermute | solution.py:203
  27.0 10.7 %collective-permute-start.3 = (bf16[1,320,128]{2,1,0:T(8,128)(2,1)S(1)}, bf16[1,320,128]{2,1,0:T(8,128)(2,1)S(1)}, u32[]{:S(2)}, u32[]{:S(2)}) collective-permute-start(bf16[1,320,128]{2,1,0:T(8,128)(2,1)S(1)} %get-tuple-element.37), channel_id=1, source_target_pairs={{0,8},{1,9},{2,10},{3,11},{4,12},{5,13},{6,14},{7,15},{8,0},{9,1},... | collective-permute-start | bytes 245768 | tf_op jit(solution)/shard_map/ppermute | solution.py:203
  30.2 7.5 %collective-permute-start.4 = (bf16[1,320,128]{2,1,0:T(8,128)(2,1)S(1)}, bf16[1,320,128]{2,1,0:T(8,128)(2,1)S(1)}, u32[]{:S(2)}, u32[]{:S(2)}) collective-permute-start(bf16[1,320,128]{2,1,0:T(8,128)(2,1)S(1)} %get-tuple-element.38), channel_id=1, source_target_pairs={{0,4},{1,5},{2,6},{3,7},{4,0},{5,1},{6,2},{7,3},{8,12},{9,13},{10,... | collective-permute-start | bytes 245768 | tf_op jit(solution)/shard_map/ppermute | solution.py:203
  30.2 7.5 %collective-permute-start.5 = (bf16[1,320,128]{2,1,0:T(8,128)(2,1)S(1)}, bf16[1,320,128]{2,1,0:T(8,128)(2,1)S(1)}, u32[]{:S(2)}, u32[]{:S(2)}) collective-permute-start(bf16[1,320,128]{2,1,0:T(8,128)(2,1)S(1)} %get-tuple-element.39), channel_id=1, source_target_pairs={{0,12},{1,13},{2,14},{3,15},{4,8},{5,9},{6,10},{7,11},{8,4},{9,5},... | collective-permute-start | bytes 245768 | tf_op jit(solution)/shard_map/ppermute | solution.py:203
  37.7 8.1 %collective-permute-start.7 = (bf16[1,320,128]{2,1,0:T(8,128)(2,1)S(1)}, bf16[1,320,128]{2,1,0:T(8,128)(2,1)S(1)}, u32[]{:S(2)}, u32[]{:S(2)}) collective-permute-start(bf16[1,320,128]{2,1,0:T(8,128)(2,1)S(1)} %total.2.refs_0_), channel_id=1, source_target_pairs={{0,8},{1,9},{2,10},{3,11},{4,12},{5,13},{6,14},{7,15},{8,0},{9,1},... | collective-permute-start | bytes 245768 | tf_op jit(solution)/shard_map/ppermute | solution.py:203
  40.7 5.2 %collective-permute-start.8 = (bf16[1,320,128]{2,1,0:T(8,128)(2,1)S(1)}, bf16[1,320,128]{2,1,0:T(8,128)(2,1)S(1)}, u32[]{:S(2)}, u32[]{:S(2)}) collective-permute-start(bf16[1,320,128]{2,1,0:T(8,128)(2,1)S(1)} %total.2.refs_0_), channel_id=1, source_target_pairs={{0,4},{1,5},{2,6},{3,7},{4,0},{5,1},{6,2},{7,3},{8,12},{9,13},{10,... | collective-permute-start | bytes 245768 | tf_op jit(solution)/shard_map/ppermute | solution.py:203
  40.8 6.8 %collective-permute-start.9 = (bf16[1,320,128]{2,1,0:T(8,128)(2,1)S(1)}, bf16[1,320,128]{2,1,0:T(8,128)(2,1)S(1)}, u32[]{:S(2)}, u32[]{:S(2)}) collective-permute-start(bf16[1,320,128]{2,1,0:T(8,128)(2,1)S(1)} %total.2.refs_0_), channel_id=1, source_target_pairs={{0,12},{1,13},{2,14},{3,15},{4,8},{5,9},{6,10},{7,11},{8,4},{9,5},... | collective-permute-start | bytes 245768 | tf_op jit(solution)/shard_map/ppermute | solution.py:203
  47.7 58.7 %all-to-all-start.1 = ((bf16[16,8,64,128]{3,2,1,0:T(8,128)(2,1)}), bf16[16,8,64,128]{3,2,1,0:T(8,128)(2,1)S(1)}, u32[]{:S(2)}, u32[]{:S(2)}) async-start(bf16[16,8,64,128]{3,2,1,0:T(8,128)(2,1)} %pad_maximum_fusion), calls=%async_computation.1 | async-start | bytes 4194304 | tf_op jit(solution)/shard_map/all_to_all | solution.py:206
  53.5 28.8 %copy-start.2 = (bf16[2,64,5120]{2,1,0:T(8,128)(2,1)S(1)}, bf16[2,64,5120]{2,1,0:T(8,128)(2,1)}, u32[]{:S(2)}) copy-start(bf16[2,64,5120]{2,1,0:T(8,128)(2,1)} %x_ref.1) | copy-start | bytes 3932164
  53.5 25.8 %collective-permute-start.10 = (bf16[4,320,128]{2,1,0:T(8,128)(2,1)S(1)}, bf16[4,320,128]{2,1,0:T(8,128)(2,1)S(1)}, u32[]{:S(2)}, u32[]{:S(2)}) collective-permute-start(bf16[4,320,128]{2,1,0:T(8,128)(2,1)S(1)} %join.2.refs_0_), channel_id=1, source_target_pairs={{0,2},{1,3},{2,0},{3,1},{4,6},{5,7},{6,4},{7,5},{8,10},{9,11},{10,... | collective-permute-start | bytes 983048 | tf_op jit(solution)/shard_map/ppermute | solution.py:203
  79.3 3.0 %collective-permute-start.11 = (bf16[8,320,128]{2,1,0:T(8,128)(2,1)S(1)}, bf16[8,320,128]{2,1,0:T(8,128)(2,1)S(1)}, u32[]{:S(2)}, u32[]{:S(2)}) collective-permute-start(bf16[8,320,128]{2,1,0:T(8,128)(2,1)S(1)} %join.3.refs_0_), channel_id=1, source_target_pairs={{0,1},{1,0},{2,3},{3,2},{4,5},{5,4},{6,7},{7,6},{8,9},{9,8},{10,11... | collective-permute-start | bytes 1966088 | tf_op jit(solution)/shard_map/ppermute | solution.py:203
  83.3 7.5 %collective-permute-start.12 = (bf16[2,256,128]{2,1,0:T(8,128)(2,1)S(1)}, bf16[2,256,128]{2,1,0:T(8,128)(2,1)S(1)}, u32[]{:S(2)}, u32[]{:S(2)}) collective-permute-start(bf16[2,256,128]{2,1,0:T(8,128)(2,1)S(1)} %get-tuple-element.45), channel_id=1, source_target_pairs={{0,4},{1,5},{2,6},{3,7},{4,0},{5,1},{6,2},{7,3},{8,12},{9,13},{10,... | collective-permute-start | bytes 393224 | tf_op jit(solution)/shard_map/ppermute | solution.py:203
  90.9 13.8 %collective-permute-start.13 = (bf16[1,256,128]{2,1,0:T(8,128)(2,1)S(1)}, bf16[1,256,128]{2,1,0:T(8,128)(2,1)S(1)}, u32[]{:S(2)}, u32[]{:S(2)}) collective-permute-start(bf16[1,256,128]{2,1,0:T(8,128)(2,1)S(1)} %get-tuple-element.47), channel_id=1, source_target_pairs={{0,8},{1,9},{2,10},{3,11},{4,12},{5,13},{6,14},{7,15},{8,0},{9,1},... | collective-permute-start | bytes 196616 | tf_op jit(solution)/shard_map/ppermute | solution.py:203
  94.8 2.8 %collective-permute-start.14 = (bf16[2,32,128]{2,1,0:T(8,128)(2,1)S(1)}, bf16[2,32,128]{2,1,0:T(8,128)(2,1)S(1)}, u32[]{:S(2)}, u32[]{:S(2)}) collective-permute-start(bf16[2,32,128]{2,1,0:T(8,128)(2,1)S(1)} %low_rank.1.refs_0_), channel_id=1, source_target_pairs={{0,1},{1,0},{2,3},{3,2},{4,5},{5,4},{6,7},{7,6},{8,9},{9,8},{10,11... | collective-permute-start | bytes 49160 | tf_op jit(solution)/shard_map/ppermute | solution.py:203
  95.9 2.6 %collective-permute-start.15 = (bf16[2,32,128]{2,1,0:T(8,128)(2,1)S(1)}, bf16[2,32,128]{2,1,0:T(8,128)(2,1)S(1)}, u32[]{:S(2)}, u32[]{:S(2)}) collective-permute-start(bf16[2,32,128]{2,1,0:T(8,128)(2,1)S(1)} %low_rank.1.refs_0_), channel_id=1, source_target_pairs={{0,2},{1,3},{2,0},{3,1},{4,6},{5,7},{6,4},{7,5},{8,10},{9,11},{10,... | collective-permute-start | bytes 49160 | tf_op jit(solution)/shard_map/ppermute | solution.py:203
  97.2 3.2 %collective-permute-start.16 = (bf16[2,32,128]{2,1,0:T(8,128)(2,1)S(1)}, bf16[2,32,128]{2,1,0:T(8,128)(2,1)S(1)}, u32[]{:S(2)}, u32[]{:S(2)}) collective-permute-start(bf16[2,32,128]{2,1,0:T(8,128)(2,1)S(1)} %low_rank.1.refs_0_), channel_id=1, source_target_pairs={{0,3},{1,2},{2,1},{3,0},{4,7},{5,6},{6,5},{7,4},{8,11},{9,10},{10,... | collective-permute-start | bytes 49160 | tf_op jit(solution)/shard_map/ppermute | solution.py:203
  100.4 4.2 %collective-permute-start.17 = (bf16[4,32,128]{2,1,0:T(8,128)(2,1)S(1)}, bf16[4,32,128]{2,1,0:T(8,128)(2,1)S(1)}, u32[]{:S(2)}, u32[]{:S(2)}) collective-permute-start(bf16[4,32,128]{2,1,0:T(8,128)(2,1)S(1)} %get-tuple-element.50), channel_id=1, source_target_pairs={{0,4},{1,5},{2,6},{3,7},{4,0},{5,1},{6,2},{7,3},{8,12},{9,13},{10,... | collective-permute-start | bytes 98312 | tf_op jit(solution)/shard_map/ppermute | solution.py:203
  100.5 4.9 %collective-permute-start.18 = (bf16[4,32,128]{2,1,0:T(8,128)(2,1)S(1)}, bf16[4,32,128]{2,1,0:T(8,128)(2,1)S(1)}, u32[]{:S(2)}, u32[]{:S(2)}) collective-permute-start(bf16[4,32,128]{2,1,0:T(8,128)(2,1)S(1)} %get-tuple-element.51), channel_id=1, source_target_pairs={{0,8},{1,9},{2,10},{3,11},{4,12},{5,13},{6,14},{7,15},{8,0},{9,1},... | collective-permute-start | bytes 98312 | tf_op jit(solution)/shard_map/ppermute | solution.py:203
  101.6 4.7 %collective-permute-start.19 = (bf16[4,32,128]{2,1,0:T(8,128)(2,1)S(1)}, bf16[4,32,128]{2,1,0:T(8,128)(2,1)S(1)}, u32[]{:S(2)}, u32[]{:S(2)}) collective-permute-start(bf16[4,32,128]{2,1,0:T(8,128)(2,1)S(1)} %get-tuple-element.52), channel_id=1, source_target_pairs={{0,12},{1,13},{2,14},{3,15},{4,8},{5,9},{6,10},{7,11},{8,4},{9,5},... | collective-permute-start | bytes 98312 | tf_op jit(solution)/shard_map/ppermute | solution.py:203

commit v29 on v24

--- a/solution.py
+++ b/solution.py
@@ -94,7 +94,7 @@
         in_specs=[VMEM] * len(arrays),
         out_specs=[VMEM] * len(shapes),
         out_shape=[jax.ShapeDtypeStruct(s, arrays[0].dtype) for s in shapes],
-        compiler_params=pltpu.CompilerParams(vmem_limit_bytes=16 << 20),
+        compiler_params=pltpu.CompilerParams(vmem_limit_bytes=8 << 20),
         cost_estimate=pl.CostEstimate(
             flops=0, bytes_accessed=2 * sum(a.size for a in arrays), transcendentals=0
         ),
@@ -257,7 +257,7 @@
             pltpu.VMEM((videos, ranks, up_width), jnp.bfloat16),
             pltpu.SemaphoreType.DMA((2 * videos,)),
         ],
-        compiler_params=pltpu.CompilerParams(vmem_limit_bytes=24 << 20),
+        compiler_params=pltpu.CompilerParams(vmem_limit_bytes=12 << 20),
         cost_estimate=pl.CostEstimate(
             flops=0,
             bytes_accessed=4 * videos * ranks * (model_width + up_width),
@@ -299,7 +299,7 @@
         out_specs=VMEM,
         scratch_shapes=[pltpu.VMEM((videos, ranks, model_width), jnp.bfloat16)],
         out_shape=jax.ShapeDtypeStruct(low_shape, jnp.bfloat16),
-        compiler_params=pltpu.CompilerParams(vmem_limit_bytes=24 << 20),
+        compiler_params=pltpu.CompilerParams(vmem_limit_bytes=12 << 20),
         cost_estimate=pl.CostEstimate(
             flops=2 * videos * toks * ranks * model_width,
             bytes_accessed=2 * videos * (toks + ranks) * model_width,
@@ -334,6 +334,7 @@
         in_specs=[SMEM] + [VMEM] * LOW,
         out_specs=[VMEM] * quarter,
         out_shape=[jax.ShapeDtypeStruct((LOW,) + low_shape[1:], jnp.bfloat16)] * quarter,
+        compiler_params=pltpu.CompilerParams(vmem_limit_bytes=8 << 20),
         cost_estimate=pl.CostEstimate(flops=0, bytes_accessed=8 * low.size, transcendentals=0),
         name="choose",
     )(me, *nearby)
@@ -354,7 +355,7 @@
             pltpu.VMEM((devs,) + low_shape[1:], jnp.bfloat16),
             pltpu.VMEM((length, width), jnp.bfloat16),
         ],
-        compiler_params=pltpu.CompilerParams(vmem_limit_bytes=48 << 20),
+        compiler_params=pltpu.CompilerParams(vmem_limit_bytes=40 << 20),
         cost_estimate=pl.CostEstimate(
             flops=4 * pairs * length * length * width,
             bytes_accessed=8 * pairs * length * width,

time: 150 us -> 147 us (0.980)
    unnamed x21 -> x11, local copies, waits for them, and re-layouts: 4.08 us -> 2.72 us
  transfers between devices with their start and end apart: 22 -> 22, of which waited for: 12 -> 13; matrix products, arithmetic and copies ran while one was open for 2% -> 2% of each run, Pallas kernels for 3% -> 2%
where the time goes in v29:
time: 147 us; the launch traced here: 146 us
  waiting for transfers between devices  58.4 us (40%)
  starting transfers between devices  40.2 us (27%)
  blocking collectives  30.8 us (21%)
  Pallas kernels  10.9 us (7%)
  other arithmetic  3.08 us (2%)
  local copies, waits for them, and re-layouts  2.72 us (2%)
    ppermute x20, waiting for transfers between devices, swap(): return lax.ppermute(tensor, 'seq', [(i, i ^ k) for i in range(devs)])  58.4 us
    all_to_all x1, blocking collectives, exchange(): lax.all_to_all(tensor, 'seq', split_axis=0, concat_axis=0, tiled=True)  30.8 us
    ppermute x20, starting transfers between devices, swap(): return lax.ppermute(tensor, 'seq', [(i, i ^ k) for i in range(devs)])  26.8 us
    all_to_all x2, starting transfers between devices, exchange(): lax.all_to_all(tensor, 'seq', split_axis=0, concat_axis=0, tiled=True)  13.4 us
    pallas_call x1, Pallas kernels, body(): pl.pallas_call(functools.partial(attend_kernel, math.gcd(devs, max(1, 256...  8.06 us
    concatenate x1, other arithmetic, body(): asked = jnp.concatenate([by_pairs(values), by_pairs(queries)], axis=1)  3.08 us
  transfers between devices with their start and end apart: 22, of which 13 were waited for; matrix products, arithmetic and copies ran while one was open for 2% of the time, Pallas kernels for 2%

profile of v29, /device:TPU:1, one launch (start us, length us, event | category | flops | bytes accessed | tf_op | source)
XLA Modules:
  0.0 146.3 jit_solution(11092062946431302797)
XLA Ops:
  0.0 7.5 %all-to-all-start = ((bf16[16,4,64,128]{3,2,1,0:T(8,128)(2,1)}), bf16[16,4,64,128]{3,2,1,0:T(8,128)(2,1)}, u32[]{:S(2)}, u32[]{:S(2)}) async-start(bf16[16,4,64,128]{3,2,1,0:T(8,128)(2,1)} %bitcast.8), calls=%async_computation | async-start | bytes 2097152 | tf_op jit(solution)/shard_map/all_to_all | solution.py:206
  7.5 0.0 copy-start
  7.5 1.7 %copy-done = bf16[4,64,5120]{2,1,0:T(8,128)(2,1)S(1)} copy-done((bf16[4,64,5120]{2,1,0:T(8,128)(2,1)S(1)}, bf16[4,64,5120]{2,1,0:T(8,128)(2,1)}, u32[]{:S(2)}) %copy-start) | copy-done | bytes 2621464
  9.3 1.5 %pick_factors.1 = (bf16[8,320,128]{2,1,0:T(8,128)(2,1)S(1)}, bf16[4,320,128]{2,1,0:T(8,128)(2,1)S(1)}, bf16[4,320,128]{2,1,0:T(8,128)(2,1)S(1)}, bf16[8,256,128]...) custom-call(s32[1]{0:T(128)} %bitcast.me_ref, s32[64]{0:T(128)S(1)} %copy-done.3, ...), custom_call_target="tpu_custom_call" | custom-call | bytes 4718592 | tf_op jit(solution)/shard_map/pick_factors/pallas_call | solution.py:250
  10.8 0.2 collective-permute-start
  11.0 1.9 %collective-permute-done.refs_1_ = bf16[8,320,128]{2,1,0:T(8,128)(2,1)S(1)} collective-permute-done((bf16[8,320,128]{2,1,0:T(8,128)(2,1)S(1)}, bf16[8,320,128]{2,1,0:T(8,128)(2,1)S(1)}, u32[]{:S(2)}, u32[]{:S(2)}) %collective-permute-start) | collective-permute-done | bytes 655392 | tf_op jit(solution)/shard_map/ppermute | solution.py:203
  13.0 0.1 halve.2
  13.0 0.2 collective-permute-start.1
  13.3 1.6 %collective-permute-start.2 = (bf16[4,320,128]{2,1,0:T(8,128)(2,1)S(1)}, bf16[4,320,128]{2,1,0:T(8,128)(2,1)S(1)}, u32[]{:S(2)}, u32[]{:S(2)}) collective-permute-start(bf16[4,320,128]{2,1,0:T(8,128)(2,1)S(1)} %halve.2), channel_id=1, source_target_pairs={{0,2},{1,3},{2,0},{3,1},{4,6},{5,7},{6,4},{7,5},{8,10},{9,11},{10,... | collective-permute-start | bytes 983048 | tf_op jit(solution)/shard_map/ppermute | solution.py:203
  14.8 0.2 collective-permute-done.1.refs_1_
  15.0 0.1 halve.3
  15.1 1.6 %collective-permute-start.6 = (bf16[4,256,128]{2,1,0:T(8,128)(2,1)S(1)}, bf16[4,256,128]{2,1,0:T(8,128)(2,1)S(1)}, u32[]{:S(2)}, u32[]{:S(2)}) collective-permute-start(bf16[4,256,128]{2,1,0:T(8,128)(2,1)S(1)} %halve.3), channel_id=1, source_target_pairs={{0,2},{1,3},{2,0},{3,1},{4,6},{5,7},{6,4},{7,5},{8,10},{9,11},{10,... | collective-permute-start | bytes 786440 | tf_op jit(solution)/shard_map/ppermute | solution.py:203
  16.7 10.1 %collective-permute-done.2.refs_2_ = bf16[4,320,128]{2,1,0:T(8,128)(2,1)S(1)} collective-permute-done((bf16[4,320,128]{2,1,0:T(8,128)(2,1)S(1)}, bf16[4,320,128]{2,1,0:T(8,128)(2,1)S(1)}, u32[]{:S(2)}, u32[]{:S(2)}) %collective-permute-start.2) | collective-permute-done | bytes 327712 | tf_op jit(solution)/shard_map/ppermute | solution.py:203
  26.8 0.1 split.3
  26.9 3.3 %collective-permute-start.3 = (bf16[1,320,128]{2,1,0:T(8,128)(2,1)S(1)}, bf16[1,320,128]{2,1,0:T(8,128)(2,1)S(1)}, u32[]{:S(2)}, u32[]{:S(2)}) collective-permute-start(bf16[1,320,128]{2,1,0:T(8,128)(2,1)S(1)} %get-tuple-element.37), channel_id=1, source_target_pairs={{0,8},{1,9},{2,10},{3,11},{4,12},{5,13},{6,14},{7,15},{8,0},{9,1},... | collective-permute-start | bytes 245768 | tf_op jit(solution)/shard_map/ppermute | solution.py:203
  30.2 0.0 collective-permute-start.4
  30.2 1.7 %collective-permute-start.5 = (bf16[1,320,128]{2,1,0:T(8,128)(2,1)S(1)}, bf16[1,320,128]{2,1,0:T(8,128)(2,1)S(1)}, u32[]{:S(2)}, u32[]{:S(2)}) collective-permute-start(bf16[1,320,128]{2,1,0:T(8,128)(2,1)S(1)} %get-tuple-element.39), channel_id=1, source_target_pairs={{0,12},{1,13},{2,14},{3,15},{4,8},{5,9},{6,10},{7,11},{8,4},{9,5},... | collective-permute-start | bytes 245768 | tf_op jit(solution)/shard_map/ppermute | solution.py:203
  31.9 5.8 %collective-permute-done.3.refs_1_ = bf16[1,320,128]{2,1,0:T(8,128)(2,1)S(1)} collective-permute-done((bf16[1,320,128]{2,1,0:T(8,128)(2,1)S(1)}, bf16[1,320,128]{2,1,0:T(8,128)(2,1)S(1)}, u32[]{:S(2)}, u32[]{:S(2)}) %collective-permute-start.3) | collective-permute-done | bytes 81952 | tf_op jit(solution)/shard_map/ppermute | solution.py:203
  37.7 0.0 collective-permute-done.5.refs_3_
  37.7 3.0 %collective-permute-start.7 = (bf16[1,320,128]{2,1,0:T(8,128)(2,1)S(1)}, bf16[1,320,128]{2,1,0:T(8,128)(2,1)S(1)}, u32[]{:S(2)}, u32[]{:S(2)}) collective-permute-start(bf16[1,320,128]{2,1,0:T(8,128)(2,1)S(1)} %total.2.refs_0_), channel_id=1, source_target_pairs={{0,8},{1,9},{2,10},{3,11},{4,12},{5,13},{6,14},{7,15},{8,0},{9,1},... | collective-permute-start | bytes 245768 | tf_op jit(solution)/shard_map/ppermute | solution.py:203
  40.7 0.1 collective-permute-start.8
  40.8 2.0 %collective-permute-start.9 = (bf16[1,320,128]{2,1,0:T(8,128)(2,1)S(1)}, bf16[1,320,128]{2,1,0:T(8,128)(2,1)S(1)}, u32[]{:S(2)}, u32[]{:S(2)}) collective-permute-start(bf16[1,320,128]{2,1,0:T(8,128)(2,1)S(1)} %total.2.refs_0_), channel_id=1, source_target_pairs={{0,12},{1,13},{2,14},{3,15},{4,8},{5,9},{6,10},{7,11},{8,4},{9,5},... | collective-permute-start | bytes 245768 | tf_op jit(solution)/shard_map/ppermute | solution.py:203
  42.8 3.1 %pad_maximum_fusion = bf16[16,8,64,128]{3,2,1,0:T(8,128)(2,1)} fusion(bf16[16,4,64,128]{3,2,1,0:T(8,128)(2,1)} %bitcast.9, bf16[16,4,64,128]{3,2,1,0:T(8,128)(2,1)} %bitcast.10), kind=kLoop, calls=%fused_computation | loop fusion | flops 1048576 | bytes 4194304 | tf_op jit(solution)/shard_map/concatenate | solution.py:288
  45.9 1.7 %collective-permute-done.9.refs_3_ = bf16[1,320,128]{2,1,0:T(8,128)(2,1)S(1)} collective-permute-done((bf16[1,320,128]{2,1,0:T(8,128)(2,1)S(1)}, bf16[1,320,128]{2,1,0:T(8,128)(2,1)S(1)}, u32[]{:S(2)}, u32[]{:S(2)}) %collective-permute-start.9) | collective-permute-done | bytes 81952 | tf_op jit(solution)/shard_map/ppermute | solution.py:203
  47.7 5.9 %all-to-all-start.1 = ((bf16[16,8,64,128]{3,2,1,0:T(8,128)(2,1)}), bf16[16,8,64,128]{3,2,1,0:T(8,128)(2,1)S(1)}, u32[]{:S(2)}, u32[]{:S(2)}) async-start(bf16[16,8,64,128]{3,2,1,0:T(8,128)(2,1)} %pad_maximum_fusion), calls=%async_computation.1 | async-start | bytes 4194304 | tf_op jit(solution)/shard_map/all_to_all | solution.py:206
  53.5 1.5 collective-permute-start.10
  55.0 24.3 %collective-permute-done.10.refs_1_ = bf16[4,320,128]{2,1,0:T(8,128)(2,1)S(1)} collective-permute-done((bf16[4,320,128]{2,1,0:T(8,128)(2,1)S(1)}, bf16[4,320,128]{2,1,0:T(8,128)(2,1)S(1)}, u32[]{:S(2)}, u32[]{:S(2)}) %collective-permute-start.10) | collective-permute-done | bytes 327712 | tf_op jit(solution)/shard_map/ppermute | solution.py:203
  79.3 1.3 collective-permute-start.11
  80.6 1.7 %collective-permute-done.11.refs_1_ = bf16[8,320,128]{2,1,0:T(8,128)(2,1)S(1)} collective-permute-done((bf16[8,320,128]{2,1,0:T(8,128)(2,1)S(1)}, bf16[8,320,128]{2,1,0:T(8,128)(2,1)S(1)}, u32[]{:S(2)}, u32[]{:S(2)}) %collective-permute-start.11) | collective-permute-done | bytes 655392 | tf_op jit(solution)/shard_map/ppermute | solution.py:203
  82.4 0.9 low_rank.1.refs_0_
  83.2 0.1 split.4
  83.3 0.1 collective-permute-start.12
  83.4 7.4 %collective-permute-done.12.refs_1_ = bf16[2,256,128]{2,1,0:T(8,128)(2,1)S(1)} collective-permute-done((bf16[2,256,128]{2,1,0:T(8,128)(2,1)S(1)}, bf16[2,256,128]{2,1,0:T(8,128)(2,1)S(1)}, u32[]{:S(2)}, u32[]{:S(2)}) %collective-permute-start.12) | collective-permute-done | bytes 131104 | tf_op jit(solution)/shard_map/ppermute | solution.py:203
  90.9 3.9 %collective-permute-start.13 = (bf16[1,256,128]{2,1,0:T(8,128)(2,1)S(1)}, bf16[1,256,128]{2,1,0:T(8,128)(2,1)S(1)}, u32[]{:S(2)}, u32[]{:S(2)}) collective-permute-start(bf16[1,256,128]{2,1,0:T(8,128)(2,1)S(1)} %get-tuple-element.47), channel_id=1, source_target_pairs={{0,8},{1,9},{2,10},{3,11},{4,12},{5,13},{6,14},{7,15},{8,0},{9,1},... | collective-permute-start | bytes 196616 | tf_op jit(solution)/shard_map/ppermute | solution.py:203
  94.8 1.2 collective-permute-start.14
  95.9 1.3 collective-permute-start.15
  97.2 0.3 collective-permute-start.16
  97.6 1.0 collective-permute-done.15.refs_2_
  98.5 1.9 %collective-permute-done.16.refs_3_ = bf16[2,32,128]{2,1,0:T(8,128)(2,1)S(1)} collective-permute-done((bf16[2,32,128]{2,1,0:T(8,128)(2,1)S(1)}, bf16[2,32,128]{2,1,0:T(8,128)(2,1)S(1)}, u32[]{:S(2)}, u32[]{:S(2)}) %collective-permute-start.16) | collective-permute-done | bytes 16416 | tf_op jit(solution)/shard_map/ppermute | solution.py:203
  100.4 0.1 collective-permute-start.17
  100.5 1.1 collective-permute-start.18
  101.6 2.4 %collective-permute-start.19 = (bf16[4,32,128]{2,1,0:T(8,128)(2,1)S(1)}, bf16[4,32,128]{2,1,0:T(8,128)(2,1)S(1)}, u32[]{:S(2)}, u32[]{:S(2)}) collective-permute-start(bf16[4,32,128]{2,1,0:T(8,128)(2,1)S(1)} %get-tuple-element.52), channel_id=1, source_target_pairs={{0,12},{1,13},{2,14},{3,15},{4,8},{5,9},{6,10},{7,11},{8,4},{9,5},... | collective-permute-start | bytes 98312 | tf_op jit(solution)/shard_map/ppermute | solution.py:203
  104.0 0.6 collective-permute-done.13.refs_1_
  104.7 0.7 collective-permute-done.18.refs_2_
  105.4 1.0 collective-permute-done.19.refs_3_
  106.4 8.1 %attend.1 = bf16[16,4,64,128]{3,2,1,0:T(8,128)(2,1)S(1)} custom-call(s32[1]{0:T(128)} %bitcast.me_ref, bf16[4,64,128]{2,1,0:T(8,128)(2,1)S(1)} %bitcast.6, bf16[16,8,64,128]{3,2,1,0:T(8,128)(2,1)S(1)} %all-to-all-done.1.q_ref.v_ref, bf16[16,4,64,128]{3,2,1,0:T(8,128)(2,1)} %all-to-all-done.k_ref, bf16[16,8,64,128]{3,2,1,0:T(8,128)(2,1)S(1)} %all-to-all-done.1.q_ref.v_ref, ...), custom_call_target="tpu_custom_call" | custom-call | flops 2147483648 | bytes 4194304 | tf_op jit(solution)/shard_map/attend/pallas_call | solution.py:346
  114.5 30.8 %all_to_all.15 = bf16[16,4,64,128]{3,2,1,0:T(8,128)(2,1)S(1)} all-to-all(bf16[16,4,64,128]{3,2,1,0:T(8,128)(2,1)S(1)} %attend.1), channel_id=1, replica_groups=mesh['grp'=2,'seq'=16] {'seq'}, dimensions={0} | all-to-all | bytes 2097152 | tf_op jit(solution)/shard_map/all_to_all | solution.py:206
  145.3 1.0 copy.10
  (22 shorter events, 0.2 us)
Async XLA Ops:
  0.0 7.5 %copy-start.3 = (s32[64]{0:T(128)S(1)}, s32[64]{0:T(128)}, u32[]{:S(2)}) copy-start(s32[64]{0:T(128)} %row_ref.1) | copy-start | bytes 772
  0.0 7.5 %copy-start.4 = (s32[2]{0:T(128)S(1)}, s32[2]{0:T(128)}, u32[]{:S(2)}) copy-start(s32[2]{0:T(128)} %req_ref.1) | copy-start | bytes 28
  0.0 7.5 %copy-start.1 = (bf16[4,64,4096]{2,1,0:T(8,128)(2,1)S(1)}, bf16[4,64,4096]{2,1,0:T(8,128)(2,1)}, u32[]{:S(2)}) copy-start(bf16[4,64,4096]{2,1,0:T(8,128)(2,1)} %up_ref.1) | copy-start | bytes 6291460
  0.0 37.7 %all-to-all-start = ((bf16[16,4,64,128]{3,2,1,0:T(8,128)(2,1)}), bf16[16,4,64,128]{3,2,1,0:T(8,128)(2,1)}, u32[]{:S(2)}, u32[]{:S(2)}) async-start(bf16[16,4,64,128]{3,2,1,0:T(8,128)(2,1)} %bitcast.8), calls=%async_computation | async-start | bytes 2097152 | tf_op jit(solution)/shard_map/all_to_all | solution.py:206
  7.5 1.7 %copy-start = (bf16[4,64,5120]{2,1,0:T(8,128)(2,1)S(1)}, bf16[4,64,5120]{2,1,0:T(8,128)(2,1)}, u32[]{:S(2)}) copy-start(bf16[4,64,5120]{2,1,0:T(8,128)(2,1)} %down_ref.1) | copy-start | bytes 7864324
  10.8 2.2 %collective-permute-start = (bf16[8,320,128]{2,1,0:T(8,128)(2,1)S(1)}, bf16[8,320,128]{2,1,0:T(8,128)(2,1)S(1)}, u32[]{:S(2)}, u32[]{:S(2)}) collective-permute-start(bf16[8,320,128]{2,1,0:T(8,128)(2,1)S(1)} %get-tuple-element.33), channel_id=1, source_target_pairs={{0,1},{1,0},{2,3},{3,2},{4,5},{5,4},{6,7},{7,6},{8,9},{9,8},{10,11... | collective-permute-start | bytes 1966088 | tf_op jit(solution)/shard_map/ppermute | solution.py:203
  13.0 2.0 %collective-permute-start.1 = (bf16[8,256,128]{2,1,0:T(8,128)(2,1)S(1)}, bf16[8,256,128]{2,1,0:T(8,128)(2,1)S(1)}, u32[]{:S(2)}, u32[]{:S(2)}) collective-permute-start(bf16[8,256,128]{2,1,0:T(8,128)(2,1)S(1)} %get-tuple-element.34), channel_id=1, source_target_pairs={{0,1},{1,0},{2,3},{3,2},{4,5},{5,4},{6,7},{7,6},{8,9},{9,8},{10,11... | collective-permute-start | bytes 1572872 | tf_op jit(solution)/shard_map/ppermute | solution.py:203
  13.3 13.6 %collective-permute-start.2 = (bf16[4,320,128]{2,1,0:T(8,128)(2,1)S(1)}, bf16[4,320,128]{2,1,0:T(8,128)(2,1)S(1)}, u32[]{:S(2)}, u32[]{:S(2)}) collective-permute-start(bf16[4,320,128]{2,1,0:T(8,128)(2,1)S(1)} %halve.2), channel_id=1, source_target_pairs={{0,2},{1,3},{2,0},{3,1},{4,6},{5,7},{6,4},{7,5},{8,10},{9,11},{10,... | collective-permute-start | bytes 983048 | tf_op jit(solution)/shard_map/ppermute | solution.py:203
  15.1 22.7 %collective-permute-start.6 = (bf16[4,256,128]{2,1,0:T(8,128)(2,1)S(1)}, bf16[4,256,128]{2,1,0:T(8,128)(2,1)S(1)}, u32[]{:S(2)}, u32[]{:S(2)}) collective-permute-start(bf16[4,256,128]{2,1,0:T(8,128)(2,1)S(1)} %halve.3), channel_id=1, source_target_pairs={{0,2},{1,3},{2,0},{3,1},{4,6},{5,7},{6,4},{7,5},{8,10},{9,11},{10,... | collective-permute-start | bytes 786440 | tf_op jit(solution)/shard_map/ppermute | solution.py:203
  26.9 10.8 %collective-permute-start.3 = (bf16[1,320,128]{2,1,0:T(8,128)(2,1)S(1)}, bf16[1,320,128]{2,1,0:T(8,128)(2,1)S(1)}, u32[]{:S(2)}, u32[]{:S(2)}) collective-permute-start(bf16[1,320,128]{2,1,0:T(8,128)(2,1)S(1)} %get-tuple-element.37), channel_id=1, source_target_pairs={{0,8},{1,9},{2,10},{3,11},{4,12},{5,13},{6,14},{7,15},{8,0},{9,1},... | collective-permute-start | bytes 245768 | tf_op jit(solution)/shard_map/ppermute | solution.py:203
  30.2 7.5 %collective-permute-start.4 = (bf16[1,320,128]{2,1,0:T(8,128)(2,1)S(1)}, bf16[1,320,128]{2,1,0:T(8,128)(2,1)S(1)}, u32[]{:S(2)}, u32[]{:S(2)}) collective-permute-start(bf16[1,320,128]{2,1,0:T(8,128)(2,1)S(1)} %get-tuple-element.38), channel_id=1, source_target_pairs={{0,4},{1,5},{2,6},{3,7},{4,0},{5,1},{6,2},{7,3},{8,12},{9,13},{10,... | collective-permute-start | bytes 245768 | tf_op jit(solution)/shard_map/ppermute | solution.py:203
  30.2 7.4 %collective-permute-start.5 = (bf16[1,320,128]{2,1,0:T(8,128)(2,1)S(1)}, bf16[1,320,128]{2,1,0:T(8,128)(2,1)S(1)}, u32[]{:S(2)}, u32[]{:S(2)}) collective-permute-start(bf16[1,320,128]{2,1,0:T(8,128)(2,1)S(1)} %get-tuple-element.39), channel_id=1, source_target_pairs={{0,12},{1,13},{2,14},{3,15},{4,8},{5,9},{6,10},{7,11},{8,4},{9,5},... | collective-permute-start | bytes 245768 | tf_op jit(solution)/shard_map/ppermute | solution.py:203
  37.7 8.1 %collective-permute-start.7 = (bf16[1,320,128]{2,1,0:T(8,128)(2,1)S(1)}, bf16[1,320,128]{2,1,0:T(8,128)(2,1)S(1)}, u32[]{:S(2)}, u32[]{:S(2)}) collective-permute-start(bf16[1,320,128]{2,1,0:T(8,128)(2,1)S(1)} %total.2.refs_0_), channel_id=1, source_target_pairs={{0,8},{1,9},{2,10},{3,11},{4,12},{5,13},{6,14},{7,15},{8,0},{9,1},... | collective-permute-start | bytes 245768 | tf_op jit(solution)/shard_map/ppermute | solution.py:203
  40.7 5.2 %collective-permute-start.8 = (bf16[1,320,128]{2,1,0:T(8,128)(2,1)S(1)}, bf16[1,320,128]{2,1,0:T(8,128)(2,1)S(1)}, u32[]{:S(2)}, u32[]{:S(2)}) collective-permute-start(bf16[1,320,128]{2,1,0:T(8,128)(2,1)S(1)} %total.2.refs_0_), channel_id=1, source_target_pairs={{0,4},{1,5},{2,6},{3,7},{4,0},{5,1},{6,2},{7,3},{8,12},{9,13},{10,... | collective-permute-start | bytes 245768 | tf_op jit(solution)/shard_map/ppermute | solution.py:203
  40.8 6.8 %collective-permute-start.9 = (bf16[1,320,128]{2,1,0:T(8,128)(2,1)S(1)}, bf16[1,320,128]{2,1,0:T(8,128)(2,1)S(1)}, u32[]{:S(2)}, u32[]{:S(2)}) collective-permute-start(bf16[1,320,128]{2,1,0:T(8,128)(2,1)S(1)} %total.2.refs_0_), channel_id=1, source_target_pairs={{0,12},{1,13},{2,14},{3,15},{4,8},{5,9},{6,10},{7,11},{8,4},{9,5},... | collective-permute-start | bytes 245768 | tf_op jit(solution)/shard_map/ppermute | solution.py:203
  47.7 58.7 %all-to-all-start.1 = ((bf16[16,8,64,128]{3,2,1,0:T(8,128)(2,1)}), bf16[16,8,64,128]{3,2,1,0:T(8,128)(2,1)S(1)}, u32[]{:S(2)}, u32[]{:S(2)}) async-start(bf16[16,8,64,128]{3,2,1,0:T(8,128)(2,1)} %pad_maximum_fusion), calls=%async_computation.1 | async-start | bytes 4194304 | tf_op jit(solution)/shard_map/all_to_all | solution.py:206
  53.5 28.8 %copy-start.2 = (bf16[2,64,5120]{2,1,0:T(8,128)(2,1)S(1)}, bf16[2,64,5120]{2,1,0:T(8,128)(2,1)}, u32[]{:S(2)}) copy-start(bf16[2,64,5120]{2,1,0:T(8,128)(2,1)} %x_ref.1) | copy-start | bytes 3932164
  53.5 25.8 %collective-permute-start.10 = (bf16[4,320,128]{2,1,0:T(8,128)(2,1)S(1)}, bf16[4,320,128]{2,1,0:T(8,128)(2,1)S(1)}, u32[]{:S(2)}, u32[]{:S(2)}) collective-permute-start(bf16[4,320,128]{2,1,0:T(8,128)(2,1)S(1)} %join.2.refs_0_), channel_id=1, source_target_pairs={{0,2},{1,3},{2,0},{3,1},{4,6},{5,7},{6,4},{7,5},{8,10},{9,11},{10,... | collective-permute-start | bytes 983048 | tf_op jit(solution)/shard_map/ppermute | solution.py:203
  79.3 3.0 %collective-permute-start.11 = (bf16[8,320,128]{2,1,0:T(8,128)(2,1)S(1)}, bf16[8,320,128]{2,1,0:T(8,128)(2,1)S(1)}, u32[]{:S(2)}, u32[]{:S(2)}) collective-permute-start(bf16[8,320,128]{2,1,0:T(8,128)(2,1)S(1)} %join.3.refs_0_), channel_id=1, source_target_pairs={{0,1},{1,0},{2,3},{3,2},{4,5},{5,4},{6,7},{7,6},{8,9},{9,8},{10,11... | collective-permute-start | bytes 1966088 | tf_op jit(solution)/shard_map/ppermute | solution.py:203
  83.3 7.5 %collective-permute-start.12 = (bf16[2,256,128]{2,1,0:T(8,128)(2,1)S(1)}, bf16[2,256,128]{2,1,0:T(8,128)(2,1)S(1)}, u32[]{:S(2)}, u32[]{:S(2)}) collective-permute-start(bf16[2,256,128]{2,1,0:T(8,128)(2,1)S(1)} %get-tuple-element.45), channel_id=1, source_target_pairs={{0,4},{1,5},{2,6},{3,7},{4,0},{5,1},{6,2},{7,3},{8,12},{9,13},{10,... | collective-permute-start | bytes 393224 | tf_op jit(solution)/shard_map/ppermute | solution.py:203
  90.9 13.8 %collective-permute-start.13 = (bf16[1,256,128]{2,1,0:T(8,128)(2,1)S(1)}, bf16[1,256,128]{2,1,0:T(8,128)(2,1)S(1)}, u32[]{:S(2)}, u32[]{:S(2)}) collective-permute-start(bf16[1,256,128]{2,1,0:T(8,128)(2,1)S(1)} %get-tuple-element.47), channel_id=1, source_target_pairs={{0,8},{1,9},{2,10},{3,11},{4,12},{5,13},{6,14},{7,15},{8,0},{9,1},... | collective-permute-start | bytes 196616 | tf_op jit(solution)/shard_map/ppermute | solution.py:203
  94.8 2.8 %collective-permute-start.14 = (bf16[2,32,128]{2,1,0:T(8,128)(2,1)S(1)}, bf16[2,32,128]{2,1,0:T(8,128)(2,1)S(1)}, u32[]{:S(2)}, u32[]{:S(2)}) collective-permute-start(bf16[2,32,128]{2,1,0:T(8,128)(2,1)S(1)} %low_rank.1.refs_0_), channel_id=1, source_target_pairs={{0,1},{1,0},{2,3},{3,2},{4,5},{5,4},{6,7},{7,6},{8,9},{9,8},{10,11... | collective-permute-start | bytes 49160 | tf_op jit(solution)/shard_map/ppermute | solution.py:203
  95.9 2.6 %collective-permute-start.15 = (bf16[2,32,128]{2,1,0:T(8,128)(2,1)S(1)}, bf16[2,32,128]{2,1,0:T(8,128)(2,1)S(1)}, u32[]{:S(2)}, u32[]{:S(2)}) collective-permute-start(bf16[2,32,128]{2,1,0:T(8,128)(2,1)S(1)} %low_rank.1.refs_0_), channel_id=1, source_target_pairs={{0,2},{1,3},{2,0},{3,1},{4,6},{5,7},{6,4},{7,5},{8,10},{9,11},{10,... | collective-permute-start | bytes 49160 | tf_op jit(solution)/shard_map/ppermute | solution.py:203
  97.2 3.2 %collective-permute-start.16 = (bf16[2,32,128]{2,1,0:T(8,128)(2,1)S(1)}, bf16[2,32,128]{2,1,0:T(8,128)(2,1)S(1)}, u32[]{:S(2)}, u32[]{:S(2)}) collective-permute-start(bf16[2,32,128]{2,1,0:T(8,128)(2,1)S(1)} %low_rank.1.refs_0_), channel_id=1, source_target_pairs={{0,3},{1,2},{2,1},{3,0},{4,7},{5,6},{6,5},{7,4},{8,11},{9,10},{10,... | collective-permute-start | bytes 49160 | tf_op jit(solution)/shard_map/ppermute | solution.py:203
  100.4 4.2 %collective-permute-start.17 = (bf16[4,32,128]{2,1,0:T(8,128)(2,1)S(1)}, bf16[4,32,128]{2,1,0:T(8,128)(2,1)S(1)}, u32[]{:S(2)}, u32[]{:S(2)}) collective-permute-start(bf16[4,32,128]{2,1,0:T(8,128)(2,1)S(1)} %get-tuple-element.50), channel_id=1, source_target_pairs={{0,4},{1,5},{2,6},{3,7},{4,0},{5,1},{6,2},{7,3},{8,12},{9,13},{10,... | collective-permute-start | bytes 98312 | tf_op jit(solution)/shard_map/ppermute | solution.py:203
  100.5 4.9 %collective-permute-start.18 = (bf16[4,32,128]{2,1,0:T(8,128)(2,1)S(1)}, bf16[4,32,128]{2,1,0:T(8,128)(2,1)S(1)}, u32[]{:S(2)}, u32[]{:S(2)}) collective-permute-start(bf16[4,32,128]{2,1,0:T(8,128)(2,1)S(1)} %get-tuple-element.51), channel_id=1, source_target_pairs={{0,8},{1,9},{2,10},{3,11},{4,12},{5,13},{6,14},{7,15},{8,0},{9,1},... | collective-permute-start | bytes 98312 | tf_op jit(solution)/shard_map/ppermute | solution.py:203
  101.6 4.7 %collective-permute-start.19 = (bf16[4,32,128]{2,1,0:T(8,128)(2,1)S(1)}, bf16[4,32,128]{2,1,0:T(8,128)(2,1)S(1)}, u32[]{:S(2)}, u32[]{:S(2)}) collective-permute-start(bf16[4,32,128]{2,1,0:T(8,128)(2,1)S(1)} %get-tuple-element.52), channel_id=1, source_target_pairs={{0,12},{1,13},{2,14},{3,15},{4,8},{5,9},{6,10},{7,11},{8,4},{9,5},... | collective-permute-start | bytes 98312 | tf_op jit(solution)/shard_map/ppermute | solution.py:203

commit v30 on v29

--- a/solution.py
+++ b/solution.py
@@ -287,10 +287,19 @@
     joined = join(gathered)
     asked = jnp.concatenate([by_pairs(values), by_pairs(queries)], axis=1)
     asked = exchange(after(asked, joined))
+    up_part = after(up_pieces[-1], joined)
+    near_pair, far_pair = on_vmem(
+        functools.partial(sum_kernel, [[(n, 2 * h) for n in range(1 + len(up_got))] for h in (0, 1)]),
+        [(2,) + up_part.shape[1:]] * 2,
+        "split",
+        up_part,
+        *up_got,
+    )
+    came = swap(far_pair, quarter)
     for i in reversed(range(bits - 2)):
         gathered = [joined, swap(joined, 1 << i)]
         if i > 0:
-            joined = join(gathered)
+            joined = after(join(gathered), came)
 
     low_shape = (videos, toks // 2, 2 * ranks)
     low = pl.pallas_call(
@@ -307,15 +316,6 @@
         ),
         name="low_rank",
     )(me, normed_token_features, *gathered)
-    up_part = after(up_pieces[-1], low)
-    near_pair, far_pair = on_vmem(
-        functools.partial(sum_kernel, [[(n, 2 * h) for n in range(1 + len(up_got))] for h in (0, 1)]),
-        [(2,) + up_part.shape[1:]] * 2,
-        "split",
-        up_part,
-        *up_got,
-    )
-    came = swap(far_pair, quarter)
     one_shape = (1,) + up_part.shape[1:]
     kept, sent = on_vmem(
         functools.partial(sum_kernel, [[(n, h) for n in range(2)] for h in (0, 1)]),

time: 147 us -> 149 us (1.014)
  waiting for transfers between devices: 58.4 us -> 60.1 us
  starting transfers between devices: 40.2 us -> 41.9 us
    ppermute x20, starting transfers between devices: 26.8 us -> 28.5 us  [swap(): return lax.ppermute(tensor, 'seq', [(i, i ^ k) for i in range(devs)])]
    ppermute x20, waiting for transfers between devices: 58.4 us -> 60.1 us  [swap(): return lax.ppermute(tensor, 'seq', [(i, i ^ k) for i in range(devs)])]
  transfers between devices with their start and end apart: 22 -> 22, of which waited for: 13 -> 10; matrix products, arithmetic and copies ran while one was open for 2% -> 2% of each run, Pallas kernels for 2% -> 2%
where the time goes in v30:
time: 149 us; the launch traced here: 148 us
  waiting for transfers between devices  60.1 us (40%)
  starting transfers between devices  41.9 us (28%)
  blocking collectives  29.6 us (20%)
  Pallas kernels  10.9 us (7%)
  other arithmetic  3.08 us (2%)
  local copies, waits for them, and re-layouts  2.72 us (2%)
    ppermute x20, waiting for transfers between devices, swap(): return lax.ppermute(tensor, 'seq', [(i, i ^ k) for i in range(devs)])  60.1 us
    all_to_all x1, blocking collectives, exchange(): lax.all_to_all(tensor, 'seq', split_axis=0, concat_axis=0, tiled=True)  29.6 us
    ppermute x20, starting transfers between devices, swap(): return lax.ppermute(tensor, 'seq', [(i, i ^ k) for i in range(devs)])  28.5 us
    all_to_all x2, starting transfers between devices, exchange(): lax.all_to_all(tensor, 'seq', split_axis=0, concat_axis=0, tiled=True)  13.4 us
    pallas_call x1, Pallas kernels, body(): pl.pallas_call(functools.partial(attend_kernel, math.gcd(devs, max(1, 256...  8.07 us
    concatenate x1, other arithmetic, body(): asked = jnp.concatenate([by_pairs(values), by_pairs(queries)], axis=1)  3.08 us
  transfers between devices with their start and end apart: 22, of which 10 were waited for; matrix products, arithmetic and copies ran while one was open for 2% of the time, Pallas kernels for 2%

profile of v30, /device:TPU:1, one launch (start us, length us, event | category | flops | bytes accessed | tf_op | source)
XLA Modules:
  0.0 148.4 jit_solution(14384427816203657103)
XLA Ops:
  0.0 7.5 %all-to-all-start = ((bf16[16,4,64,128]{3,2,1,0:T(8,128)(2,1)}), bf16[16,4,64,128]{3,2,1,0:T(8,128)(2,1)}, u32[]{:S(2)}, u32[]{:S(2)}) async-start(bf16[16,4,64,128]{3,2,1,0:T(8,128)(2,1)} %bitcast.8), calls=%async_computation | async-start | bytes 2097152 | tf_op jit(solution)/shard_map/all_to_all | solution.py:206
  7.5 0.0 copy-start
  7.5 1.7 %copy-done = bf16[4,64,5120]{2,1,0:T(8,128)(2,1)S(1)} copy-done((bf16[4,64,5120]{2,1,0:T(8,128)(2,1)S(1)}, bf16[4,64,5120]{2,1,0:T(8,128)(2,1)}, u32[]{:S(2)}) %copy-start) | copy-done | bytes 2621464
  9.3 1.5 %pick_factors.1 = (bf16[8,320,128]{2,1,0:T(8,128)(2,1)S(1)}, bf16[4,320,128]{2,1,0:T(8,128)(2,1)S(1)}, bf16[4,320,128]{2,1,0:T(8,128)(2,1)S(1)}, bf16[8,256,128]...) custom-call(s32[1]{0:T(128)} %bitcast.me_ref, s32[64]{0:T(128)S(1)} %copy-done.3, ...), custom_call_target="tpu_custom_call" | custom-call | bytes 4718592 | tf_op jit(solution)/shard_map/pick_factors/pallas_call | solution.py:250
  10.8 0.4 collective-permute-start
  11.2 1.8 %collective-permute-done.refs_1_ = bf16[8,320,128]{2,1,0:T(8,128)(2,1)S(1)} collective-permute-done((bf16[8,320,128]{2,1,0:T(8,128)(2,1)S(1)}, bf16[8,320,128]{2,1,0:T(8,128)(2,1)S(1)}, u32[]{:S(2)}, u32[]{:S(2)}) %collective-permute-start) | collective-permute-done | bytes 655392 | tf_op jit(solution)/shard_map/ppermute | solution.py:203
  13.0 0.1 halve.2
  13.0 0.4 collective-permute-start.1
  13.4 1.6 %collective-permute-start.2 = (bf16[4,320,128]{2,1,0:T(8,128)(2,1)S(1)}, bf16[4,320,128]{2,1,0:T(8,128)(2,1)S(1)}, u32[]{:S(2)}, u32[]{:S(2)}) collective-permute-start(bf16[4,320,128]{2,1,0:T(8,128)(2,1)S(1)} %halve.2), channel_id=1, source_target_pairs={{0,2},{1,3},{2,0},{3,1},{4,6},{5,7},{6,4},{7,5},{8,10},{9,11},{10,... | collective-permute-start | bytes 983048 | tf_op jit(solution)/shard_map/ppermute | solution.py:203
  15.0 0.0 collective-permute-done.1.refs_1_
  15.0 0.1 halve.3
  15.1 1.6 %collective-permute-start.6 = (bf16[4,256,128]{2,1,0:T(8,128)(2,1)S(1)}, bf16[4,256,128]{2,1,0:T(8,128)(2,1)S(1)}, u32[]{:S(2)}, u32[]{:S(2)}) collective-permute-start(bf16[4,256,128]{2,1,0:T(8,128)(2,1)S(1)} %halve.3), channel_id=1, source_target_pairs={{0,2},{1,3},{2,0},{3,1},{4,6},{5,7},{6,4},{7,5},{8,10},{9,11},{10,... | collective-permute-start | bytes 786440 | tf_op jit(solution)/shard_map/ppermute | solution.py:203
  16.7 10.2 %collective-permute-done.2.refs_2_ = bf16[4,320,128]{2,1,0:T(8,128)(2,1)S(1)} collective-permute-done((bf16[4,320,128]{2,1,0:T(8,128)(2,1)S(1)}, bf16[4,320,128]{2,1,0:T(8,128)(2,1)S(1)}, u32[]{:S(2)}, u32[]{:S(2)}) %collective-permute-start.2) | collective-permute-done | bytes 327712 | tf_op jit(solution)/shard_map/ppermute | solution.py:203
  26.9 0.1 split.3
  27.0 3.3 %collective-permute-start.3 = (bf16[1,320,128]{2,1,0:T(8,128)(2,1)S(1)}, bf16[1,320,128]{2,1,0:T(8,128)(2,1)S(1)}, u32[]{:S(2)}, u32[]{:S(2)}) collective-permute-start(bf16[1,320,128]{2,1,0:T(8,128)(2,1)S(1)} %get-tuple-element.38), channel_id=1, source_target_pairs={{0,8},{1,9},{2,10},{3,11},{4,12},{5,13},{6,14},{7,15},{8,0},{9,1},... | collective-permute-start | bytes 245768 | tf_op jit(solution)/shard_map/ppermute | solution.py:203
  30.2 0.0 collective-permute-start.4
  30.2 1.7 %collective-permute-start.5 = (bf16[1,320,128]{2,1,0:T(8,128)(2,1)S(1)}, bf16[1,320,128]{2,1,0:T(8,128)(2,1)S(1)}, u32[]{:S(2)}, u32[]{:S(2)}) collective-permute-start(bf16[1,320,128]{2,1,0:T(8,128)(2,1)S(1)} %get-tuple-element.40), channel_id=1, source_target_pairs={{0,12},{1,13},{2,14},{3,15},{4,8},{5,9},{6,10},{7,11},{8,4},{9,5},... | collective-permute-start | bytes 245768 | tf_op jit(solution)/shard_map/ppermute | solution.py:203
  31.9 5.8 %collective-permute-done.3.refs_1_ = bf16[1,320,128]{2,1,0:T(8,128)(2,1)S(1)} collective-permute-done((bf16[1,320,128]{2,1,0:T(8,128)(2,1)S(1)}, bf16[1,320,128]{2,1,0:T(8,128)(2,1)S(1)}, u32[]{:S(2)}, u32[]{:S(2)}) %collective-permute-start.3) | collective-permute-done | bytes 81952 | tf_op jit(solution)/shard_map/ppermute | solution.py:203
  37.7 0.0 collective-permute-done.4.refs_2_
  37.7 0.0 collective-permute-done.5.refs_3_
  37.7 3.0 %collective-permute-start.7 = (bf16[1,320,128]{2,1,0:T(8,128)(2,1)S(1)}, bf16[1,320,128]{2,1,0:T(8,128)(2,1)S(1)}, u32[]{:S(2)}, u32[]{:S(2)}) collective-permute-start(bf16[1,320,128]{2,1,0:T(8,128)(2,1)S(1)} %total.2.refs_0_), channel_id=1, source_target_pairs={{0,8},{1,9},{2,10},{3,11},{4,12},{5,13},{6,14},{7,15},{8,0},{9,1},... | collective-permute-start | bytes 245768 | tf_op jit(solution)/shard_map/ppermute | solution.py:203
  40.7 0.1 collective-permute-start.8
  40.8 2.0 %collective-permute-start.9 = (bf16[1,320,128]{2,1,0:T(8,128)(2,1)S(1)}, bf16[1,320,128]{2,1,0:T(8,128)(2,1)S(1)}, u32[]{:S(2)}, u32[]{:S(2)}) collective-permute-start(bf16[1,320,128]{2,1,0:T(8,128)(2,1)S(1)} %total.2.refs_0_), channel_id=1, source_target_pairs={{0,12},{1,13},{2,14},{3,15},{4,8},{5,9},{6,10},{7,11},{8,4},{9,5},... | collective-permute-start | bytes 245768 | tf_op jit(solution)/shard_map/ppermute | solution.py:203
  42.8 3.1 %pad_maximum_fusion = bf16[16,8,64,128]{3,2,1,0:T(8,128)(2,1)} fusion(bf16[16,4,64,128]{3,2,1,0:T(8,128)(2,1)} %bitcast.9, bf16[16,4,64,128]{3,2,1,0:T(8,128)(2,1)} %bitcast.10), kind=kLoop, calls=%fused_computation | loop fusion | flops 1048576 | bytes 4194304 | tf_op jit(solution)/shard_map/concatenate | solution.py:288
  45.9 1.7 %collective-permute-done.9.refs_3_ = bf16[1,320,128]{2,1,0:T(8,128)(2,1)S(1)} collective-permute-done((bf16[1,320,128]{2,1,0:T(8,128)(2,1)S(1)}, bf16[1,320,128]{2,1,0:T(8,128)(2,1)S(1)}, u32[]{:S(2)}, u32[]{:S(2)}) %collective-permute-start.9) | collective-permute-done | bytes 81952 | tf_op jit(solution)/shard_map/ppermute | solution.py:203
  47.7 5.9 %all-to-all-start.1 = ((bf16[16,8,64,128]{3,2,1,0:T(8,128)(2,1)}), bf16[16,8,64,128]{3,2,1,0:T(8,128)(2,1)S(1)}, u32[]{:S(2)}, u32[]{:S(2)}) async-start(bf16[16,8,64,128]{3,2,1,0:T(8,128)(2,1)} %pad_maximum_fusion), calls=%async_computation.1 | async-start | bytes 4194304 | tf_op jit(solution)/shard_map/all_to_all | solution.py:206
  53.5 1.5 collective-permute-start.12
  55.0 0.1 split.4
  55.1 1.2 collective-permute-start.10
  56.3 23.0 %collective-permute-done.12.refs_1_ = bf16[4,320,128]{2,1,0:T(8,128)(2,1)S(1)} collective-permute-done((bf16[4,320,128]{2,1,0:T(8,128)(2,1)S(1)}, bf16[4,320,128]{2,1,0:T(8,128)(2,1)S(1)}, u32[]{:S(2)}, u32[]{:S(2)}) %collective-permute-start.12) | collective-permute-done | bytes 327712 | tf_op jit(solution)/shard_map/ppermute | solution.py:203
  79.3 11.4 %collective-permute-done.10.refs_1_ = bf16[2,256,128]{2,1,0:T(8,128)(2,1)S(1)} collective-permute-done((bf16[2,256,128]{2,1,0:T(8,128)(2,1)S(1)}, bf16[2,256,128]{2,1,0:T(8,128)(2,1)S(1)}, u32[]{:S(2)}, u32[]{:S(2)}) %collective-permute-start.10) | collective-permute-done | bytes 131104 | tf_op jit(solution)/shard_map/ppermute | solution.py:203
  90.8 0.6 collective-permute-start.13
  91.4 4.2 %collective-permute-start.11 = (bf16[1,256,128]{2,1,0:T(8,128)(2,1)S(1)}, bf16[1,256,128]{2,1,0:T(8,128)(2,1)S(1)}, u32[]{:S(2)}, u32[]{:S(2)}) collective-permute-start(bf16[1,256,128]{2,1,0:T(8,128)(2,1)S(1)} %get-tuple-element.48), channel_id=1, source_target_pairs={{0,8},{1,9},{2,10},{3,11},{4,12},{5,13},{6,14},{7,15},{8,0},{9,1},... | collective-permute-start | bytes 196616 | tf_op jit(solution)/shard_map/ppermute | solution.py:203
  95.6 0.0 collective-permute-done.13.refs_1_
  95.6 0.9 low_rank.1.refs_0_
  96.5 0.3 collective-permute-start.14
  96.8 1.3 collective-permute-start.15
  98.1 0.5 collective-permute-start.16
  98.7 0.7 collective-permute-done.15.refs_2_
  99.4 2.0 %collective-permute-done.16.refs_3_ = bf16[2,32,128]{2,1,0:T(8,128)(2,1)S(1)} collective-permute-done((bf16[2,32,128]{2,1,0:T(8,128)(2,1)S(1)}, bf16[2,32,128]{2,1,0:T(8,128)(2,1)S(1)}, u32[]{:S(2)}, u32[]{:S(2)}) %collective-permute-start.16) | collective-permute-done | bytes 16416 | tf_op jit(solution)/shard_map/ppermute | solution.py:203
  101.4 1.0 collective-permute-start.17
  102.4 2.8 %collective-permute-start.18 = (bf16[4,32,128]{2,1,0:T(8,128)(2,1)S(1)}, bf16[4,32,128]{2,1,0:T(8,128)(2,1)S(1)}, u32[]{:S(2)}, u32[]{:S(2)}) collective-permute-start(bf16[4,32,128]{2,1,0:T(8,128)(2,1)S(1)} %get-tuple-element.53), channel_id=1, source_target_pairs={{0,8},{1,9},{2,10},{3,11},{4,12},{5,13},{6,14},{7,15},{8,0},{9,1},... | collective-permute-start | bytes 98312 | tf_op jit(solution)/shard_map/ppermute | solution.py:203
  105.2 1.1 collective-permute-start.19
  106.4 0.2 collective-permute-done.18.refs_2_
  106.5 3.3 %collective-permute-done.19.refs_3_ = bf16[4,32,128]{2,1,0:T(8,128)(2,1)S(1)} collective-permute-done((bf16[4,32,128]{2,1,0:T(8,128)(2,1)S(1)}, bf16[4,32,128]{2,1,0:T(8,128)(2,1)S(1)}, u32[]{:S(2)}, u32[]{:S(2)}) %collective-permute-start.19) | collective-permute-done | bytes 32800 | tf_op jit(solution)/shard_map/ppermute | solution.py:203
  109.8 8.1 %attend.1 = bf16[16,4,64,128]{3,2,1,0:T(8,128)(2,1)S(1)} custom-call(s32[1]{0:T(128)} %bitcast.me_ref, bf16[4,64,128]{2,1,0:T(8,128)(2,1)S(1)} %bitcast.6, bf16[16,8,64,128]{3,2,1,0:T(8,128)(2,1)S(1)} %all-to-all-done.1.q_ref.v_ref, bf16[16,4,64,128]{3,2,1,0:T(8,128)(2,1)} %all-to-all-done.k_ref, bf16[16,8,64,128]{3,2,1,0:T(8,128)(2,1)S(1)} %all-to-all-done.1.q_ref.v_ref, ...), custom_call_target="tpu_custom_call" | custom-call | flops 2147483648 | bytes 4194304 | tf_op jit(solution)/shard_map/attend/pallas_call | solution.py:346
  117.9 29.6 %all_to_all.15 = bf16[16,4,64,128]{3,2,1,0:T(8,128)(2,1)S(1)} all-to-all(bf16[16,4,64,128]{3,2,1,0:T(8,128)(2,1)S(1)} %attend.1), channel_id=1, replica_groups=mesh['grp'=2,'seq'=16] {'seq'}, dimensions={0} | all-to-all | bytes 2097152 | tf_op jit(solution)/shard_map/all_to_all | solution.py:206
  147.4 1.0 copy.10
  (22 shorter events, 0.2 us)
Async XLA Ops:
  0.0 7.5 %copy-start.1 = (bf16[4,64,4096]{2,1,0:T(8,128)(2,1)S(1)}, bf16[4,64,4096]{2,1,0:T(8,128)(2,1)}, u32[]{:S(2)}) copy-start(bf16[4,64,4096]{2,1,0:T(8,128)(2,1)} %up_ref.1) | copy-start | bytes 6291460
  0.0 7.5 %copy-start.3 = (s32[64]{0:T(128)S(1)}, s32[64]{0:T(128)}, u32[]{:S(2)}) copy-start(s32[64]{0:T(128)} %row_ref.1) | copy-start | bytes 772
  0.0 7.5 %copy-start.4 = (s32[2]{0:T(128)S(1)}, s32[2]{0:T(128)}, u32[]{:S(2)}) copy-start(s32[2]{0:T(128)} %req_ref.1) | copy-start | bytes 28
  0.0 37.7 %all-to-all-start = ((bf16[16,4,64,128]{3,2,1,0:T(8,128)(2,1)}), bf16[16,4,64,128]{3,2,1,0:T(8,128)(2,1)}, u32[]{:S(2)}, u32[]{:S(2)}) async-start(bf16[16,4,64,128]{3,2,1,0:T(8,128)(2,1)} %bitcast.8), calls=%async_computation | async-start | bytes 2097152 | tf_op jit(solution)/shard_map/all_to_all | solution.py:206
  7.5 1.7 %copy-start = (bf16[4,64,5120]{2,1,0:T(8,128)(2,1)S(1)}, bf16[4,64,5120]{2,1,0:T(8,128)(2,1)}, u32[]{:S(2)}) copy-start(bf16[4,64,5120]{2,1,0:T(8,128)(2,1)} %down_ref.1) | copy-start | bytes 7864324
  10.8 2.2 %collective-permute-start = (bf16[8,320,128]{2,1,0:T(8,128)(2,1)S(1)}, bf16[8,320,128]{2,1,0:T(8,128)(2,1)S(1)}, u32[]{:S(2)}, u32[]{:S(2)}) collective-permute-start(bf16[8,320,128]{2,1,0:T(8,128)(2,1)S(1)} %get-tuple-element.34), channel_id=1, source_target_pairs={{0,1},{1,0},{2,3},{3,2},{4,5},{5,4},{6,7},{7,6},{8,9},{9,8},{10,11... | collective-permute-start | bytes 1966088 | tf_op jit(solution)/shard_map/ppermute | solution.py:203
  13.0 2.0 %collective-permute-start.1 = (bf16[8,256,128]{2,1,0:T(8,128)(2,1)S(1)}, bf16[8,256,128]{2,1,0:T(8,128)(2,1)S(1)}, u32[]{:S(2)}, u32[]{:S(2)}) collective-permute-start(bf16[8,256,128]{2,1,0:T(8,128)(2,1)S(1)} %get-tuple-element.35), channel_id=1, source_target_pairs={{0,1},{1,0},{2,3},{3,2},{4,5},{5,4},{6,7},{7,6},{8,9},{9,8},{10,11... | collective-permute-start | bytes 1572872 | tf_op jit(solution)/shard_map/ppermute | solution.py:203
  13.4 13.4 %collective-permute-start.2 = (bf16[4,320,128]{2,1,0:T(8,128)(2,1)S(1)}, bf16[4,320,128]{2,1,0:T(8,128)(2,1)S(1)}, u32[]{:S(2)}, u32[]{:S(2)}) collective-permute-start(bf16[4,320,128]{2,1,0:T(8,128)(2,1)S(1)} %halve.2), channel_id=1, source_target_pairs={{0,2},{1,3},{2,0},{3,1},{4,6},{5,7},{6,4},{7,5},{8,10},{9,11},{10,... | collective-permute-start | bytes 983048 | tf_op jit(solution)/shard_map/ppermute | solution.py:203
  15.1 22.7 %collective-permute-start.6 = (bf16[4,256,128]{2,1,0:T(8,128)(2,1)S(1)}, bf16[4,256,128]{2,1,0:T(8,128)(2,1)S(1)}, u32[]{:S(2)}, u32[]{:S(2)}) collective-permute-start(bf16[4,256,128]{2,1,0:T(8,128)(2,1)S(1)} %halve.3), channel_id=1, source_target_pairs={{0,2},{1,3},{2,0},{3,1},{4,6},{5,7},{6,4},{7,5},{8,10},{9,11},{10,... | collective-permute-start | bytes 786440 | tf_op jit(solution)/shard_map/ppermute | solution.py:203
  27.0 10.7 %collective-permute-start.3 = (bf16[1,320,128]{2,1,0:T(8,128)(2,1)S(1)}, bf16[1,320,128]{2,1,0:T(8,128)(2,1)S(1)}, u32[]{:S(2)}, u32[]{:S(2)}) collective-permute-start(bf16[1,320,128]{2,1,0:T(8,128)(2,1)S(1)} %get-tuple-element.38), channel_id=1, source_target_pairs={{0,8},{1,9},{2,10},{3,11},{4,12},{5,13},{6,14},{7,15},{8,0},{9,1},... | collective-permute-start | bytes 245768 | tf_op jit(solution)/shard_map/ppermute | solution.py:203
  30.2 7.5 %collective-permute-start.4 = (bf16[1,320,128]{2,1,0:T(8,128)(2,1)S(1)}, bf16[1,320,128]{2,1,0:T(8,128)(2,1)S(1)}, u32[]{:S(2)}, u32[]{:S(2)}) collective-permute-start(bf16[1,320,128]{2,1,0:T(8,128)(2,1)S(1)} %get-tuple-element.39), channel_id=1, source_target_pairs={{0,4},{1,5},{2,6},{3,7},{4,0},{5,1},{6,2},{7,3},{8,12},{9,13},{10,... | collective-permute-start | bytes 245768 | tf_op jit(solution)/shard_map/ppermute | solution.py:203
  30.2 7.4 %collective-permute-start.5 = (bf16[1,320,128]{2,1,0:T(8,128)(2,1)S(1)}, bf16[1,320,128]{2,1,0:T(8,128)(2,1)S(1)}, u32[]{:S(2)}, u32[]{:S(2)}) collective-permute-start(bf16[1,320,128]{2,1,0:T(8,128)(2,1)S(1)} %get-tuple-element.40), channel_id=1, source_target_pairs={{0,12},{1,13},{2,14},{3,15},{4,8},{5,9},{6,10},{7,11},{8,4},{9,5},... | collective-permute-start | bytes 245768 | tf_op jit(solution)/shard_map/ppermute | solution.py:203
  37.7 8.1 %collective-permute-start.7 = (bf16[1,320,128]{2,1,0:T(8,128)(2,1)S(1)}, bf16[1,320,128]{2,1,0:T(8,128)(2,1)S(1)}, u32[]{:S(2)}, u32[]{:S(2)}) collective-permute-start(bf16[1,320,128]{2,1,0:T(8,128)(2,1)S(1)} %total.2.refs_0_), channel_id=1, source_target_pairs={{0,8},{1,9},{2,10},{3,11},{4,12},{5,13},{6,14},{7,15},{8,0},{9,1},... | collective-permute-start | bytes 245768 | tf_op jit(solution)/shard_map/ppermute | solution.py:203
  40.7 5.2 %collective-permute-start.8 = (bf16[1,320,128]{2,1,0:T(8,128)(2,1)S(1)}, bf16[1,320,128]{2,1,0:T(8,128)(2,1)S(1)}, u32[]{:S(2)}, u32[]{:S(2)}) collective-permute-start(bf16[1,320,128]{2,1,0:T(8,128)(2,1)S(1)} %total.2.refs_0_), channel_id=1, source_target_pairs={{0,4},{1,5},{2,6},{3,7},{4,0},{5,1},{6,2},{7,3},{8,12},{9,13},{10,... | collective-permute-start | bytes 245768 | tf_op jit(solution)/shard_map/ppermute | solution.py:203
  40.8 6.8 %collective-permute-start.9 = (bf16[1,320,128]{2,1,0:T(8,128)(2,1)S(1)}, bf16[1,320,128]{2,1,0:T(8,128)(2,1)S(1)}, u32[]{:S(2)}, u32[]{:S(2)}) collective-permute-start(bf16[1,320,128]{2,1,0:T(8,128)(2,1)S(1)} %total.2.refs_0_), channel_id=1, source_target_pairs={{0,12},{1,13},{2,14},{3,15},{4,8},{5,9},{6,10},{7,11},{8,4},{9,5},... | collective-permute-start | bytes 245768 | tf_op jit(solution)/shard_map/ppermute | solution.py:203
  47.7 62.1 %all-to-all-start.1 = ((bf16[16,8,64,128]{3,2,1,0:T(8,128)(2,1)}), bf16[16,8,64,128]{3,2,1,0:T(8,128)(2,1)S(1)}, u32[]{:S(2)}, u32[]{:S(2)}) async-start(bf16[16,8,64,128]{3,2,1,0:T(8,128)(2,1)} %pad_maximum_fusion), calls=%async_computation.1 | async-start | bytes 4194304 | tf_op jit(solution)/shard_map/all_to_all | solution.py:206
  53.5 42.1 %copy-start.2 = (bf16[2,64,5120]{2,1,0:T(8,128)(2,1)S(1)}, bf16[2,64,5120]{2,1,0:T(8,128)(2,1)}, u32[]{:S(2)}) copy-start(bf16[2,64,5120]{2,1,0:T(8,128)(2,1)} %x_ref.1) | copy-start | bytes 3932164
  53.5 25.8 %collective-permute-start.12 = (bf16[4,320,128]{2,1,0:T(8,128)(2,1)S(1)}, bf16[4,320,128]{2,1,0:T(8,128)(2,1)S(1)}, u32[]{:S(2)}, u32[]{:S(2)}) collective-permute-start(bf16[4,320,128]{2,1,0:T(8,128)(2,1)S(1)} %join.2.refs_0_), channel_id=1, source_target_pairs={{0,2},{1,3},{2,0},{3,1},{4,6},{5,7},{6,4},{7,5},{8,10},{9,11},{10,... | collective-permute-start | bytes 983048 | tf_op jit(solution)/shard_map/ppermute | solution.py:203
  55.1 35.7 %collective-permute-start.10 = (bf16[2,256,128]{2,1,0:T(8,128)(2,1)S(1)}, bf16[2,256,128]{2,1,0:T(8,128)(2,1)S(1)}, u32[]{:S(2)}, u32[]{:S(2)}) collective-permute-start(bf16[2,256,128]{2,1,0:T(8,128)(2,1)S(1)} %get-tuple-element.46), channel_id=1, source_target_pairs={{0,4},{1,5},{2,6},{3,7},{4,0},{5,1},{6,2},{7,3},{8,12},{9,13},{10,... | collective-permute-start | bytes 393224 | tf_op jit(solution)/shard_map/ppermute | solution.py:203
  90.8 4.9 %collective-permute-start.13 = (bf16[8,320,128]{2,1,0:T(8,128)(2,1)S(1)}, bf16[8,320,128]{2,1,0:T(8,128)(2,1)S(1)}, u32[]{:S(2)}, u32[]{:S(2)}) collective-permute-start(bf16[8,320,128]{2,1,0:T(8,128)(2,1)S(1)} %join.3.refs_0_), channel_id=1, source_target_pairs={{0,1},{1,0},{2,3},{3,2},{4,5},{5,4},{6,7},{7,6},{8,9},{9,8},{10,11... | collective-permute-start | bytes 1966088 | tf_op jit(solution)/shard_map/ppermute | solution.py:203
  91.4 14.9 %collective-permute-start.11 = (bf16[1,256,128]{2,1,0:T(8,128)(2,1)S(1)}, bf16[1,256,128]{2,1,0:T(8,128)(2,1)S(1)}, u32[]{:S(2)}, u32[]{:S(2)}) collective-permute-start(bf16[1,256,128]{2,1,0:T(8,128)(2,1)S(1)} %get-tuple-element.48), channel_id=1, source_target_pairs={{0,8},{1,9},{2,10},{3,11},{4,12},{5,13},{6,14},{7,15},{8,0},{9,1},... | collective-permute-start | bytes 196616 | tf_op jit(solution)/shard_map/ppermute | solution.py:203
  96.5 2.2 %collective-permute-start.14 = (bf16[2,32,128]{2,1,0:T(8,128)(2,1)S(1)}, bf16[2,32,128]{2,1,0:T(8,128)(2,1)S(1)}, u32[]{:S(2)}, u32[]{:S(2)}) collective-permute-start(bf16[2,32,128]{2,1,0:T(8,128)(2,1)S(1)} %low_rank.1.refs_0_), channel_id=1, source_target_pairs={{0,1},{1,0},{2,3},{3,2},{4,5},{5,4},{6,7},{7,6},{8,9},{9,8},{10,11... | collective-permute-start | bytes 49160 | tf_op jit(solution)/shard_map/ppermute | solution.py:203
  96.8 2.6 %collective-permute-start.15 = (bf16[2,32,128]{2,1,0:T(8,128)(2,1)S(1)}, bf16[2,32,128]{2,1,0:T(8,128)(2,1)S(1)}, u32[]{:S(2)}, u32[]{:S(2)}) collective-permute-start(bf16[2,32,128]{2,1,0:T(8,128)(2,1)S(1)} %low_rank.1.refs_0_), channel_id=1, source_target_pairs={{0,2},{1,3},{2,0},{3,1},{4,6},{5,7},{6,4},{7,5},{8,10},{9,11},{10,... | collective-permute-start | bytes 49160 | tf_op jit(solution)/shard_map/ppermute | solution.py:203
  98.1 3.3 %collective-permute-start.16 = (bf16[2,32,128]{2,1,0:T(8,128)(2,1)S(1)}, bf16[2,32,128]{2,1,0:T(8,128)(2,1)S(1)}, u32[]{:S(2)}, u32[]{:S(2)}) collective-permute-start(bf16[2,32,128]{2,1,0:T(8,128)(2,1)S(1)} %low_rank.1.refs_0_), channel_id=1, source_target_pairs={{0,3},{1,2},{2,1},{3,0},{4,7},{5,6},{6,5},{7,4},{8,11},{9,10},{10,... | collective-permute-start | bytes 49160 | tf_op jit(solution)/shard_map/ppermute | solution.py:203
  101.4 4.9 %collective-permute-start.17 = (bf16[4,32,128]{2,1,0:T(8,128)(2,1)S(1)}, bf16[4,32,128]{2,1,0:T(8,128)(2,1)S(1)}, u32[]{:S(2)}, u32[]{:S(2)}) collective-permute-start(bf16[4,32,128]{2,1,0:T(8,128)(2,1)S(1)} %get-tuple-element.52), channel_id=1, source_target_pairs={{0,4},{1,5},{2,6},{3,7},{4,0},{5,1},{6,2},{7,3},{8,12},{9,13},{10,... | collective-permute-start | bytes 98312 | tf_op jit(solution)/shard_map/ppermute | solution.py:203
  102.4 4.1 %collective-permute-start.18 = (bf16[4,32,128]{2,1,0:T(8,128)(2,1)S(1)}, bf16[4,32,128]{2,1,0:T(8,128)(2,1)S(1)}, u32[]{:S(2)}, u32[]{:S(2)}) collective-permute-start(bf16[4,32,128]{2,1,0:T(8,128)(2,1)S(1)} %get-tuple-element.53), channel_id=1, source_target_pairs={{0,8},{1,9},{2,10},{3,11},{4,12},{5,13},{6,14},{7,15},{8,0},{9,1},... | collective-permute-start | bytes 98312 | tf_op jit(solution)/shard_map/ppermute | solution.py:203
  105.2 4.6 %collective-permute-start.19 = (bf16[4,32,128]{2,1,0:T(8,128)(2,1)S(1)}, bf16[4,32,128]{2,1,0:T(8,128)(2,1)S(1)}, u32[]{:S(2)}, u32[]{:S(2)}) collective-permute-start(bf16[4,32,128]{2,1,0:T(8,128)(2,1)S(1)} %get-tuple-element.54), channel_id=1, source_target_pairs={{0,12},{1,13},{2,14},{3,15},{4,8},{5,9},{6,10},{7,11},{8,4},{9,5},... | collective-permute-start | bytes 98312 | tf_op jit(solution)/shard_map/ppermute | solution.py:203
